TPU v7x, 32 devices: a whole 2x2x4 slice. The times are simulated.
32 devices in a mesh: groups: 2 (over y), graph: 4 (over x, core), mp: 4 (over z).
Axes of the slice: x: 2, y: 2, z: 4, core: 2. Of those that a mesh axis runs over, the one named last changes fastest.
Arguments:
- grid_lat: bfloat16 [16384, 512], P(('groups', 'graph', 'mp')), parts along dimension 0, may hold values from -6 to 6
- mesh_lat: bfloat16 [8192, 512], P(('groups', 'graph', 'mp')), parts along dimension 0, may hold values from -6 to 6
- cotangent: bfloat16 [8192, 512], P(('groups', 'graph', 'mp')), parts along dimension 0, may hold values from -6 to 6
- grid_send: int32 [512, 4], P(('groups', 'graph', 'mp')), parts along dimension 0, may hold values from 0 to 511
- g2m_slot: int32 [16384], P(('groups', 'graph', 'mp')), parts along dimension 0, may hold values from 0 to 63, as said below
- g2m_receiver: int32 [16384], P(('groups', 'graph', 'mp')), parts along dimension 0, may hold values from 0 to 255, as said below
- halo_send: int32 [512, 2], P(('groups', 'graph', 'mp')), parts along dimension 0, may hold values from 0 to 255
- mesh_sender: int32 [16384], P(('groups', 'graph', 'mp')), parts along dimension 0, may hold values from 0 to 287
- mesh_receiver: int32 [16384], P(('groups', 'graph', 'mp')), parts along dimension 0, may hold values from 0 to 255, as said below
- enc_edge_in: bfloat16 [1024, 512], P(None, 'mp'), may hold values from -0.1875 to 0.1875
- enc_edge_out: bfloat16 [512, 512], P('mp'), may hold values from -0.25 to 0.25
- enc_node_in: bfloat16 [1024, 512], P(None, 'mp'), may hold values from -0.1875 to 0.1875
- enc_node_out: bfloat16 [512, 512], P('mp'), may hold values from -0.25 to 0.25
- proc_edge_in: bfloat16 [1024, 512], P(None, 'mp'), may hold values from -0.1875 to 0.1875
- proc_edge_out: bfloat16 [512, 512], P('mp'), may hold values from -0.25 to 0.25
- proc_node_in: bfloat16 [1024, 512], P(None, 'mp'), may hold values from -0.1875 to 0.1875
- proc_node_out: bfloat16 [512, 512], P('mp'), may hold values from -0.25 to 0.25
Outputs:
- mesh_two: bfloat16 [8192, 512], P(('groups', 'graph', 'mp')), parts along dimension 0
- grid_grad: float32 [16384, 512], P(('groups', 'graph', 'mp')), parts along dimension 0
- mesh_grad: float32 [8192, 512], P(('groups', 'graph', 'mp')), parts along dimension 0
There are 2 independent parts, one for each index of `groups`. A program takes and returns all parts, laid end to end along the dimension named above; an argument that names none is the same for every part. Nothing has to cross between parts.
Inputs may be any that keep to these rules, and one draw needn't show every extreme that they name: `g2m_slot`: an edge names only slots of a pair that hold a grid row its receiver's partition needs; slots of a pair that no edge names still hold valid rows. `g2m_receiver`: every mesh node of a device receives at least one grid-to-mesh edge. `mesh_receiver`: every mesh node of a device receives at least one mesh edge.
All inputs are finite; a program needn't handle non-finite values.
Results may differ from a plain program's by a relative error of at most 0.017.
Values may be sent and summed in bfloat16 or wider, within the bound.
No kernel may reach another device: no remote copies, remote signals or barrier semaphores. Data moves between devices by JAX's collectives and lax.ppermute only.
A program may use at most 64 MiB of HBM per device.

v0:
```python
import jax
import jax.numpy as jnp
from jax import lax
from jax.sharding import PartitionSpec as P


def dense_trans(left, right):
    return lax.dot_general(
        left, right, (((1,), (1,)), ((), ())), preferred_element_type=jnp.float32
    )


def onehot_table(index, count):
    position = jnp.arange(count, dtype=jnp.int32)[:, None]
    return (position == index[None, :]).astype(jnp.float32)


def table_sum(table, values):
    return jnp.dot(
        table, values, precision=lax.Precision.HIGHEST, preferred_element_type=jnp.float32
    )


def mlp_forward(inputs, w_first, w_second):
    before = jnp.dot(inputs, w_first, preferred_element_type=jnp.float32)
    hidden = jax.nn.silu(before).astype(jnp.bfloat16)
    summed = jnp.dot(hidden, w_second, preferred_element_type=jnp.float32)
    average = jnp.mean(summed, axis=-1, keepdims=True)
    centered = summed - average
    rescale = lax.rsqrt(jnp.mean(centered * centered, axis=-1, keepdims=True) + 1e-05)
    normed = centered * rescale
    return (normed, (before, normed, rescale))


def mlp_backward(incoming, saved, w_first, w_second):
    before, normed, rescale = saved
    g_out = (
        incoming
        - jnp.mean(incoming, axis=-1, keepdims=True)
        - normed * jnp.mean(incoming * normed, axis=-1, keepdims=True)
    ) * rescale
    g_round = g_out.astype(jnp.bfloat16)
    g_hidden = dense_trans(g_round, w_second)
    logistic = jax.nn.sigmoid(before)
    g_before = (g_hidden * logistic * (1.0 + before * (1.0 - logistic))).astype(jnp.bfloat16)
    partial_in = dense_trans(g_before, w_first)
    return partial_in


def local(
    grid_lat,
    mesh_lat,
    cotangent,
    grid_send,
    g2m_slot,
    g2m_receiver,
    halo_send,
    mesh_sender,
    mesh_receiver,
    enc_edge_in,
    enc_edge_out,
    enc_node_in,
    enc_node_out,
    proc_edge_in,
    proc_edge_out,
    proc_node_in,
    proc_node_out,
):
    features = mesh_lat.shape[1]
    mesh_rows = mesh_lat.shape[0]
    grid_rows = grid_lat.shape[0]
    peer_count = grid_send.shape[0]
    capacity = grid_send.shape[1]
    halo_capacity = halo_send.shape[1]
    weight_set = (
        lax.all_gather(enc_edge_in, "mp", axis=1, tiled=True),
        lax.all_gather(enc_edge_out, "mp", axis=0, tiled=True),
        lax.all_gather(enc_node_in, "mp", axis=1, tiled=True),
        lax.all_gather(enc_node_out, "mp", axis=0, tiled=True),
        lax.all_gather(proc_edge_in, "mp", axis=1, tiled=True),
        lax.all_gather(proc_edge_out, "mp", axis=0, tiled=True),
        lax.all_gather(proc_node_in, "mp", axis=1, tiled=True),
        lax.all_gather(proc_node_out, "mp", axis=0, tiled=True),
    )
    outgoing = jnp.take(grid_lat, grid_send, axis=0)
    arrived = lax.all_to_all(outgoing, ("graph", "mp"), split_axis=0, concat_axis=0, tiled=True)
    arrived = arrived.reshape(peer_count * capacity, features)
    edge_in = jnp.concatenate(
        [jnp.take(arrived, g2m_slot, axis=0), jnp.take(mesh_lat, g2m_receiver, axis=0)], axis=1
    )
    normed_e, saved_e = mlp_forward(edge_in, weight_set[0], weight_set[1])
    edge_latent = normed_e.astype(jnp.bfloat16)
    position = jnp.arange(mesh_rows, dtype=jnp.int32)[:, None]
    onehot_enc = (position == g2m_receiver[None, :]).astype(jnp.bfloat16)
    aggregate = jnp.dot(onehot_enc, edge_latent, preferred_element_type=jnp.float32).astype(
        jnp.bfloat16
    )
    node_in = jnp.concatenate([mesh_lat, aggregate], axis=1)
    normed_n, saved_n = mlp_forward(node_in, weight_set[2], weight_set[3])
    mesh_one = (mesh_lat.astype(jnp.float32) + normed_n).astype(jnp.bfloat16)
    halo_out = jnp.take(mesh_one, halo_send, axis=0)
    halo_in = lax.all_to_all(halo_out, ("graph", "mp"), split_axis=0, concat_axis=0, tiled=True)
    lookup = jnp.concatenate(
        [mesh_one, halo_in.reshape(peer_count * halo_capacity, features)], axis=0
    )
    proc_in = jnp.concatenate(
        [jnp.take(lookup, mesh_sender, axis=0), jnp.take(mesh_one, mesh_receiver, axis=0)], axis=1
    )
    normed_p, saved_p = mlp_forward(proc_in, weight_set[4], weight_set[5])
    message = normed_p.astype(jnp.bfloat16)
    onehot_proc = (position == mesh_receiver[None, :]).astype(jnp.bfloat16)
    aggregate_two = jnp.dot(onehot_proc, message, preferred_element_type=jnp.float32).astype(
        jnp.bfloat16
    )
    node_two = jnp.concatenate([mesh_one, aggregate_two], axis=1)
    normed_q, saved_q = mlp_forward(node_two, weight_set[6], weight_set[7])
    mesh_two = (mesh_one.astype(jnp.float32) + normed_q).astype(jnp.bfloat16)
    recv_proc = onehot_proc.astype(jnp.float32)
    recv_enc = onehot_enc.astype(jnp.float32)
    grad_two = cotangent.astype(jnp.float32)
    g_q = mlp_backward(grad_two, saved_q, weight_set[6], weight_set[7])
    grad_one = grad_two + g_q[:, :features]
    grad_msg = jnp.take(g_q[:, features:], mesh_receiver, axis=0)
    g_p = mlp_backward(grad_msg, saved_p, weight_set[4], weight_set[5])
    grad_one = grad_one + table_sum(recv_proc, g_p[:, features:])
    sender_table = onehot_table(mesh_sender, mesh_rows + peer_count * halo_capacity)
    grad_lookup = table_sum(sender_table, g_p[:, :features])
    grad_one = grad_one + grad_lookup[:mesh_rows]
    grad_halo = grad_lookup[mesh_rows:].reshape(peer_count, halo_capacity, features)
    halo_back = lax.all_to_all(
        grad_halo.astype(jnp.bfloat16), ("graph", "mp"), split_axis=0, concat_axis=0, tiled=True
    ).astype(grad_halo.dtype)
    halo_table = onehot_table(halo_send.reshape(-1), mesh_rows)
    grad_one = grad_one + table_sum(halo_table, halo_back.reshape(-1, features))
    g_n = mlp_backward(grad_one, saved_n, weight_set[2], weight_set[3])
    mesh_grad = grad_one + g_n[:, :features]
    grad_edge = jnp.take(g_n[:, features:], g2m_receiver, axis=0)
    g_e = mlp_backward(grad_edge, saved_e, weight_set[0], weight_set[1])
    mesh_grad = mesh_grad + table_sum(recv_enc, g_e[:, features:])
    slot_table = onehot_table(g2m_slot, peer_count * capacity)
    grad_slots = table_sum(slot_table, g_e[:, :features])
    returned = lax.all_to_all(
        grad_slots.reshape(peer_count, capacity, features).astype(jnp.bfloat16),
        ("graph", "mp"),
        split_axis=0,
        concat_axis=0,
        tiled=True,
    ).astype(jnp.float32)
    grid_table = onehot_table(grid_send.reshape(-1), grid_rows)
    grid_grad = table_sum(grid_table, returned.reshape(-1, features))
    return (mesh_two, grid_grad, mesh_grad)


def solution(mesh):
    in_specs = (
        P(("groups", "graph", "mp"), None),
        P(("groups", "graph", "mp"), None),
        P(("groups", "graph", "mp"), None),
        P(("groups", "graph", "mp"), None),
        P(("groups", "graph", "mp")),
        P(("groups", "graph", "mp")),
        P(("groups", "graph", "mp"), None),
        P(("groups", "graph", "mp")),
        P(("groups", "graph", "mp")),
        P(None, "mp"),
        P("mp", None),
        P(None, "mp"),
        P("mp", None),
        P(None, "mp"),
        P("mp", None),
        P(None, "mp"),
        P("mp", None),
    )
    out_specs = (
        P(("groups", "graph", "mp"), None),
        P(("groups", "graph", "mp"), None),
        P(("groups", "graph", "mp"), None),
    )
    return jax.shard_map(local, mesh=mesh, in_specs=in_specs, out_specs=out_specs, check_vma=False)
```

profile of v0, /device:TPU:0, one launch (start us, length us, event | category | flops | bytes accessed | tf_op | source)
XLA Modules:
  0.0 222.1 jit_solution(15565954836555797936)
XLA Ops:
  12.6 7.4 %all-to-all-start = ((bf16[16,4,512]{2,1,0:T(4,128)(2,1)}), bf16[16,4,512]{2,1,0:T(4,128)(2,1)S(1)}, u32[]{:S(2)}, u32[]{:S(2)}) async-start(bf16[16,4,512]{2,1,0:T(4,128)(2,1)} %broadcast_select_fusion.5), calls=%async_computation | async-start | bytes 131072 | tf_op jit(solution)/shard_map/all_to_all | solution.py:86
  26.1 23.1 %all_gather.31 = bf16[512,512]{1,0:T(8,128)(2,1)} all-gather(bf16[128,512]{1,0:T(8,128)(2,1)S(1)} %copy-done.13), channel_id=1, replica_groups=mesh['groups'=2,'graph'=4,'mp'=4] {'mp'}, dimensions={0}, use_global_device_ids=true | all-gather | bytes 655360 | tf_op jit(solution)/shard_map/all_gather | solution.py:83
  49.1 18.1 %all_gather.29 = bf16[512,512]{1,0:T(8,128)(2,1)} all-gather(bf16[128,512]{1,0:T(8,128)(2,1)S(1)} %copy-done.14), channel_id=1, replica_groups=mesh['groups'=2,'graph'=4,'mp'=4] {'mp'}, dimensions={0}, use_global_device_ids=true | all-gather | bytes 655360 | tf_op jit(solution)/shard_map/all_gather | solution.py:81
  67.3 20.7 %all_gather.27 = bf16[512,512]{1,0:T(8,128)(2,1)S(1)} all-gather(bf16[128,512]{1,0:T(8,128)(2,1)S(1)} %copy-done.15), channel_id=1, replica_groups=mesh['groups'=2,'graph'=4,'mp'=4] {'mp'}, dimensions={0}, use_global_device_ids=true | all-gather | bytes 655360 | tf_op jit(solution)/shard_map/all_gather | solution.py:79
  88.0 15.4 %all_gather.25 = bf16[512,512]{1,0:T(8,128)(2,1)S(1)} all-gather(bf16[128,512]{1,0:T(8,128)(2,1)S(1)} %copy-done.16), channel_id=1, replica_groups=mesh['groups'=2,'graph'=4,'mp'=4] {'mp'}, dimensions={0}, use_global_device_ids=true | all-gather | bytes 655360 | tf_op jit(solution)/shard_map/all_gather | solution.py:77
  105.7 2.0 gather_fusion.1
  108.8 2.3 %fusion.19 = f32[512,512]{1,0:T(8,128)S(1)} fusion(bf16[1024,512]{1,0:T(8,128)(2,1)} %all-gather.5.cloned.1.call-done, bf16[512,512]{1,0:T(8,128)(2,1)} %get-tuple-element.23, bf16[512,512]{1,0:T(8,128)(2,1)} %get-tuple-element.24), kind=kOutput, calls=%fused_computation.36 | convolution fusion | flops 538968064 | bytes 3145728 | tf_op jit(solution)/shard_map/dot_general | solution.py:25
  119.1 5.7 %all-to-all-start.1 = ((bf16[16,2,512]{2,1,0:T(2,128)(2,1)}), bf16[16,2,512]{2,1,0:T(2,128)(2,1)S(1)}, u32[]{:S(2)}, u32[]{:S(2)}) async-start(bf16[16,2,512]{2,1,0:T(2,128)(2,1)} %broadcast_select_fusion.4), calls=%async_computation.1 | async-start | bytes 65536 | tf_op jit(solution)/shard_map/all_to_all | solution.py:102
  124.9 6.3 %all-to-all-done.1 = bf16[16,2,512]{2,1,0:T(2,128)(2,1)S(1)} async-done(((bf16[16,2,512]{2,1,0:T(2,128)(2,1)}), bf16[16,2,512]{2,1,0:T(2,128)(2,1)S(1)}, u32[]{:S(2)}, u32[]{:S(2)}) %all-to-all-start.1) | async-done | bytes 32800 | tf_op jit(solution)/shard_map/all_to_all | solution.py:102
  134.2 2.1 fusion.23
  137.9 14.1 %all-gather.11.cloned.1.call-done = bf16[1024,512]{1,0:T(8,128)(2,1)} async-done(((bf16[1024,128]{1,0:T(8,128)(2,1)}), bf16[1024,512]{1,0:T(8,128)(2,1)}) %all-gather.11.cloned.1.call-update) | async-done | bytes 1048592 | tf_op jit(solution)/shard_map/all_gather | solution.py:82
  156.5 3.6 %fusion.13 = f32[256,1024]{1,0:T(8,128)} fusion(bf16[1024,512]{1,0:T(8,128)(2,1)} %all-gather.11.cloned.1.call-done, bf16[512,512]{1,0:T(8,128)(2,1)} %all_gather.31, f32[256,512]{1,0:T(8,128)} %copy-done.24, bf16[256,512]{1,0:T(8,128)(2,1)S(1)} %copy-done.8, f32[256,512]{1,0:T(8,128)} %copy-done.7, f32[256]{0:T(256)S(1)} %broadcast_multiply_fusion.8, ...), kind=kOutput, calls=%fused_computation.29 | convolution fusion | flops 404881408 | bytes 3936256 | tf_op jit(solution)/shard_map/dot_general | solution.py:8
  161.1 2.3 %gather_fusion.6 = f32[512,512]{1,0:T(8,128)} fusion(f32[256,512]{1,0:T(8,128)S(1)} %slice.58, s32[1024]{0:T(1024)S(1)} %pad_clamp_fusion), kind=kCustom, calls=%fused_computation.1.clone | custom fusion | bytes 2099200 | tf_op jit(solution)/shard_map/jit(_take)/gather | solution.py:123
  163.5 2.6 %copy.33 = f32[512,512]{0,1:T(8,128)} copy(f32[512,512]{1,0:T(8,128)} %gather_fusion.6) | data formatting | bytes 2097152 | tf_op jit(solution)/shard_map/jit(_take)/gather | solution.py:123
  167.6 4.5 %fusion.5 = f32[512,1024]{1,0:T(8,128)} fusion(bf16[1024,512]{1,0:T(8,128)(2,1)} %all-gather.9.cloned.1.call-done, bf16[512,512]{1,0:T(8,128)(2,1)S(1)} %copy-done.12, f32[512,512]{1,0:T(8,128)} %copy-done.26, f32[512,512]{0,1:T(8,128)} %copy.33, f32[512,512]{0,1:T(8,128)S(1)} %get-tuple-element.19, f32[512]{0:T(512)S(1)} %broadcast_multiply_fusion.2, ...), kind=kOutput, calls=%fused_computation.15 | convolution fusion | flops 809762816 | bytes 6824448 | tf_op jit(solution)/shard_map/dot_general | solution.py:8
  172.1 2.0 fusion.16
  174.8 3.9 %all-to-all-start.2 = ((bf16[16,2,512]{2,1,0:T(2,128)(2,1)}), bf16[16,2,512]{2,1,0:T(2,128)(2,1)S(1)}, u32[]{:S(2)}, u32[]{:S(2)}) async-start(bf16[16,2,512]{2,1,0:T(2,128)(2,1)} %convert_element_type.100), calls=%async_computation.2 | async-start | bytes 65536 | tf_op jit(solution)/shard_map/all_to_all | solution.py:130
  179.0 6.1 %all-to-all-done.2 = bf16[16,2,512]{2,1,0:T(2,128)(2,1)S(1)} async-done(((bf16[16,2,512]{2,1,0:T(2,128)(2,1)}), bf16[16,2,512]{2,1,0:T(2,128)(2,1)S(1)}, u32[]{:S(2)}, u32[]{:S(2)}) %all-to-all-start.2) | async-done | bytes 32800 | tf_op jit(solution)/shard_map/all_to_all | solution.py:130
  185.4 2.3 %fusion.137 = (f32[256]{0:T(256)S(1)}, f32[256]{0:T(256)S(1)}, f32[256,512]{1,0:T(8,128)S(1)}) fusion(f32[256]{0:T(256)S(1)} %add_rsqrt_fusion.3, f32[256,512]{1,0:T(8,128)S(1)} %copy-done.3, f32[256]{0:T(256)S(1)} %broadcast_multiply_fusion.11, f32[256,512]{1,0:T(8,128)S(1)} %fusion.118, f32[288,512]{1,0:T(8,128)S(1)} %fusion.16, f32[512,1024]{1,0:T(8,128)} %fusion.5, ...), kind=kOutput, calls=%fused_computation.207 | convolution fusion | flops 806747648 | bytes 3938304 | tf_op jit(solution)/shard_map/dot_general | solution.py:19
  188.5 3.3 %fusion.12 = f32[256,1024]{1,0:T(8,128)} fusion(bf16[1024,512]{1,0:T(8,128)(2,1)} %all-gather.7.cloned.1.call-done, bf16[512,512]{1,0:T(8,128)(2,1)} %copy-done.10, f32[256,512]{1,0:T(8,128)} %copy-done.23, f32[256,512]{1,0:T(8,128)S(1)} %get-tuple-element.22, f32[256,512]{1,0:T(8,128)S(1)} %copy-done.3, f32[256]{0:T(256)S(1)} %broadcast_multiply_fusion.6, ...), kind=kOutput, calls=%fused_computation.28 | convolution fusion | flops 404750336 | bytes 4198400 | tf_op jit(solution)/shard_map/dot_general | solution.py:8
  197.4 4.4 %fusion.4 = f32[512,1024]{1,0:T(8,128)} fusion(bf16[1024,512]{1,0:T(8,128)(2,1)} %all-gather.5.cloned.1.call-done, bf16[512,512]{1,0:T(8,128)(2,1)} %copy-done.9, f32[512,512]{1,0:T(8,128)} %copy-done.25, f32[512,512]{0,1:T(8,128)S(1)} %copy-done.4, f32[512,512]{0,1:T(8,128)S(1)} %get-tuple-element.15, f32[512]{0:T(512)S(1)} %broadcast_multiply_fusion, ...), kind=kOutput, calls=%fused_computation.14 | convolution fusion | flops 809762816 | bytes 6824448 | tf_op jit(solution)/shard_map/dot_general | solution.py:8
  204.2 3.5 %all-to-all-start.3 = ((bf16[16,4,512]{2,1,0:T(4,128)(2,1)}), bf16[16,4,512]{2,1,0:T(4,128)(2,1)S(1)}, u32[]{:S(2)}, u32[]{:S(2)}) async-start(bf16[16,4,512]{2,1,0:T(4,128)(2,1)} %convert_element_type.106), calls=%async_computation.3 | async-start | bytes 131072 | tf_op jit(solution)/shard_map/all_to_all | solution.py:142
  207.7 2.9 %convolution_add_fusion = f32[256,512]{1,0:T(8,128)} fusion(f32[512,1024]{1,0:T(8,128)} %fusion.4, f32[256,512]{1,0:T(8,128)S(1)} %copy-done.6, f32[256,1024]{1,0:T(8,128)} %fusion.12, s32[512]{0:T(512)S(1)} %copy-done.18), kind=kOutput, calls=%fused_computation.16 | convolution fusion | flops 805699584 | bytes 2623488 | tf_op jit(solution)/shard_map/dot_general | solution.py:19
  210.6 3.7 %all-to-all-done.3 = bf16[16,4,512]{2,1,0:T(4,128)(2,1)S(1)} async-done(((bf16[16,4,512]{2,1,0:T(4,128)(2,1)}), bf16[16,4,512]{2,1,0:T(4,128)(2,1)S(1)}, u32[]{:S(2)}, u32[]{:S(2)}) %all-to-all-start.3) | async-done | bytes 65568 | tf_op jit(solution)/shard_map/all_to_all | solution.py:142
  (153 shorter events, 45.6 us)
Async XLA Ops:
  7.2 3.2 %copy-start = (bf16[512,512]{1,0:T(8,128)(2,1)S(1)}, bf16[512,512]{1,0:T(8,128)(2,1)}, u32[]{:S(2)}) copy-start(bf16[512,512]{1,0:T(8,128)(2,1)} %param.21) | copy-start | bytes 1572868
  7.2 18.9 %copy-start.19 = (s32[512]{0:T(512)S(1)}, s32[512]{0:T(512)}, u32[]{:S(2)}) copy-start(s32[512]{0:T(512)} %param.28) | copy-start | bytes 6148
  7.2 18.9 %copy-start.13 = (bf16[128,512]{1,0:T(8,128)(2,1)S(1)}, bf16[128,512]{1,0:T(8,128)(2,1)}, u32[]{:S(2)}) copy-start(bf16[128,512]{1,0:T(8,128)(2,1)} %param.37) | copy-start | bytes 393220
  7.2 41.9 %copy-start.14 = (bf16[128,512]{1,0:T(8,128)(2,1)S(1)}, bf16[128,512]{1,0:T(8,128)(2,1)}, u32[]{:S(2)}) copy-start(bf16[128,512]{1,0:T(8,128)(2,1)} %param.35) | copy-start | bytes 393220
  7.2 60.1 %copy-start.15 = (bf16[128,512]{1,0:T(8,128)(2,1)S(1)}, bf16[128,512]{1,0:T(8,128)(2,1)}, u32[]{:S(2)}) copy-start(bf16[128,512]{1,0:T(8,128)(2,1)} %param.33) | copy-start | bytes 393220
  7.2 80.7 %copy-start.16 = (bf16[128,512]{1,0:T(8,128)(2,1)S(1)}, bf16[128,512]{1,0:T(8,128)(2,1)}, u32[]{:S(2)}) copy-start(bf16[128,512]{1,0:T(8,128)(2,1)} %param.31) | copy-start | bytes 393220
  7.2 101.6 %all-gather.5.cloned.1.call-start = ((), (), s32[]{:S(2)}) async-start(), calls=%async_computation.4 | async-start | bytes 1310720 | tf_op jit(solution)/shard_map/all_gather | solution.py:76
  8.0 104.7 %all-gather.7.cloned.1.call-start = ((), (), s32[]{:S(2)}) async-start(), calls=%async_computation.5 | async-start | bytes 1310720 | tf_op jit(solution)/shard_map/all_gather | solution.py:78
  8.7 94.9 %copy-start.1 = (bf16[256,512]{1,0:T(8,128)(2,1)S(1)}, bf16[256,512]{1,0:T(8,128)(2,1)}, u32[]{:S(2)}) copy-start(bf16[256,512]{1,0:T(8,128)(2,1)} %param.22) | copy-start | bytes 786436
  8.7 125.5 %all-gather.9.cloned.1.call-start = ((), (), s32[]{:S(2)}) async-start(), calls=%async_computation.6 | async-start | bytes 1310720 | tf_op jit(solution)/shard_map/all_gather | solution.py:80
  12.6 93.0 %all-to-all-start = ((bf16[16,4,512]{2,1,0:T(4,128)(2,1)}), bf16[16,4,512]{2,1,0:T(4,128)(2,1)S(1)}, u32[]{:S(2)}, u32[]{:S(2)}) async-start(bf16[16,4,512]{2,1,0:T(4,128)(2,1)} %broadcast_select_fusion.5), calls=%async_computation | async-start | bytes 131072 | tf_op jit(solution)/shard_map/all_to_all | solution.py:86
  20.0 132.0 %all-gather.11.cloned.1.call-start = ((), (), s32[]{:S(2)}) async-start(), calls=%async_computation.7 | async-start | bytes 1310720 | tf_op jit(solution)/shard_map/all_gather | solution.py:82
  88.0 26.3 %copy-start.10 = (bf16[512,512]{1,0:T(8,128)(2,1)}, bf16[512,512]{1,0:T(8,128)(2,1)S(1)}, u32[]{:S(2)}) copy-start(bf16[512,512]{1,0:T(8,128)(2,1)S(1)} %all_gather.27) | copy-start | bytes 1572868
  103.3 7.8 %copy-start.9 = (bf16[512,512]{1,0:T(8,128)(2,1)}, bf16[512,512]{1,0:T(8,128)(2,1)S(1)}, u32[]{:S(2)}) copy-start(bf16[512,512]{1,0:T(8,128)(2,1)S(1)} %all_gather.25) | copy-start | bytes 1572868
  119.1 12.2 %all-to-all-start.1 = ((bf16[16,2,512]{2,1,0:T(2,128)(2,1)}), bf16[16,2,512]{2,1,0:T(2,128)(2,1)S(1)}, u32[]{:S(2)}, u32[]{:S(2)}) async-start(bf16[16,2,512]{2,1,0:T(2,128)(2,1)} %broadcast_select_fusion.4), calls=%async_computation.1 | async-start | bytes 65536 | tf_op jit(solution)/shard_map/all_to_all | solution.py:102
  134.2 2.2 copy-start.11
  163.5 4.1 %copy-start.12 = (bf16[512,512]{1,0:T(8,128)(2,1)S(1)}, bf16[512,512]{1,0:T(8,128)(2,1)}, u32[]{:S(2)}) copy-start(bf16[512,512]{1,0:T(8,128)(2,1)} %all_gather.29) | copy-start | bytes 1572868
  167.6 11.1 %copy-start.22 = (s32[16,2]{0,1:T(2,128)S(1)}, s32[16,2]{0,1:T(2,128)}, u32[]{:S(2)}) copy-start(s32[16,2]{0,1:T(2,128)} %param.27) | copy-start | bytes 388
  167.6 11.2 %copy-start.21 = (s32[16,4]{0,1:T(4,128)S(1)}, s32[16,4]{0,1:T(4,128)}, u32[]{:S(2)}) copy-start(s32[16,4]{0,1:T(4,128)} %param.24) | copy-start | bytes 772
  172.1 13.3 %copy-start.3 = (f32[256,512]{1,0:T(8,128)S(1)}, f32[256,512]{1,0:T(8,128)}, u32[]{:S(2)}) copy-start(f32[256,512]{1,0:T(8,128)} %copy-done.2) | copy-start | bytes 1572868
  174.8 10.4 %all-to-all-start.2 = ((bf16[16,2,512]{2,1,0:T(2,128)(2,1)}), bf16[16,2,512]{2,1,0:T(2,128)(2,1)S(1)}, u32[]{:S(2)}, u32[]{:S(2)}) async-start(bf16[16,2,512]{2,1,0:T(2,128)(2,1)} %convert_element_type.100), calls=%async_computation.2 | async-start | bytes 65536 | tf_op jit(solution)/shard_map/all_to_all | solution.py:130
  197.4 4.4 %copy-start.20 = (s32[512]{0:T(512)S(1)}, s32[512]{0:T(512)}, u32[]{:S(2)}) copy-start(s32[512]{0:T(512)} %param.25) | copy-start | bytes 6148
  197.4 10.3 %copy-start.6 = (f32[256,512]{1,0:T(8,128)S(1)}, f32[256,512]{1,0:T(8,128)}, u32[]{:S(2)}) copy-start(f32[256,512]{1,0:T(8,128)} %copy-done.5) | copy-start | bytes 1572868
  204.2 10.1 %all-to-all-start.3 = ((bf16[16,4,512]{2,1,0:T(4,128)(2,1)}), bf16[16,4,512]{2,1,0:T(4,128)(2,1)S(1)}, u32[]{:S(2)}, u32[]{:S(2)}) async-start(bf16[16,4,512]{2,1,0:T(4,128)(2,1)} %convert_element_type.106), calls=%async_computation.3 | async-start | bytes 131072 | tf_op jit(solution)/shard_map/all_to_all | solution.py:142
  (11 other events, 13.3 us)
Sparse Core Ops, SparseCore 0:
  9.6 41.3 all-gather.4
  52.5 39.4 all-gather.6
  93.6 27.9 all-gather.8
  123.0 28.8 all-gather.10
where the time goes:
time: 223 us; the launch traced here: 222 us
  blocking collectives  77.2 us (35%)
  matrix products  37.7 us (17%)
  waiting for transfers between devices  32.9 us (15%)
  local copies, waits for them, and re-layouts  23.8 us (11%)
  starting transfers between devices  20.6 us (9%)
  other arithmetic  15.5 us (7%)
  between operations  14.4 us (6%)
    all_gather x1, blocking collectives, local(): lax.all_gather(proc_node_out, 'mp', axis=0, tiled=True)  23.1 us
    all_gather x1, blocking collectives, local(): lax.all_gather(enc_node_out, 'mp', axis=0, tiled=True)  20.7 us
    all_gather x1, blocking collectives, local(): lax.all_gather(proc_edge_out, 'mp', axis=0, tiled=True)  18.1 us
    dot_general x4, matrix products, dense_trans(): lax.dot_general(left, right, (((1,), (1,)), ((), ())), preferred_element_...  15.7 us
    all_gather x1, blocking collectives, local(): lax.all_gather(enc_edge_out, 'mp', axis=0, tiled=True)  15.4 us
    all_gather x1, waiting for transfers between devices, local(): lax.all_gather(proc_node_in, 'mp', axis=1, tiled=True)  14.1 us
    dot_general x6, matrix products, table_sum(): jnp.dot(table, values, precision=lax.Precision.HIGHEST, preferred_element...  10.3 us
    dot_general x4, matrix products, mlp_forward(): before = jnp.dot(inputs, w_first, preferred_element_type=jnp.float32)  7.7 us
  transfers between devices with their start and end apart: 8, of which 4 were waited for; matrix products, arithmetic and copies ran while one was open for 15% of the time, Pallas kernels for 0%

commit v1 on v0

v1 whole, which is shorter than its diff:
```python
import functools

import jax
import jax.numpy as jnp
from jax import lax
from jax.experimental import pallas as pl
from jax.experimental.pallas import tpu as pltpu
from jax.sharding import PartitionSpec as P

F32 = jnp.float32
BF16 = jnp.bfloat16
LANES = 128
ROWS = 256
AXES = ("groups", "graph", "mp")
PEERS = ("graph", "mp")


def dot(left, right):
    return jnp.dot(left, right, preferred_element_type=F32)


def dot_trans(left, right):
    return lax.dot_general(left, right, (((1,), (1,)), ((), ())), preferred_element_type=F32)


def call(kernel, out_shape, *args):
    flops = 0
    return pl.pallas_call(
        kernel,
        out_shape=out_shape,
        in_specs=[pl.BlockSpec(memory_space=pltpu.VMEM)] * len(args),
        out_specs=[pl.BlockSpec(memory_space=pltpu.VMEM)] * len(out_shape),
        compiler_params=pltpu.CompilerParams(vmem_limit_bytes=40 * 1024 * 1024),
    )(*args)


def shape(rows, columns, dtype):
    return jax.ShapeDtypeStruct((rows, columns), dtype)


def weight_pair(ref, which, features):
    columns = features // LANES
    blocks = 2 * columns
    low = which * 192
    first = [
        jnp.concatenate([ref[p * columns + m, low : low + 128, :] for p in range(blocks)], axis=0)
        for m in range(columns)
    ]
    second = []
    for q in range(columns):
        parts = []
        for m in range(columns):
            for half in range(2):
                parts.append(ref[(half * columns + q) * columns + m, low + 128 : low + 192, :])
        second.append(jnp.concatenate(parts, axis=0))
    return jnp.concatenate(first, axis=1), jnp.concatenate(second, axis=1)


def pack_kernel(*refs):
    shards, (enc, proc), sem = refs[:8], refs[8:10], refs[10]
    plane = lax.axis_index("groups") * lax.axis_size("graph") + lax.axis_index("graph")
    half, quarter = plane // 4, plane % 4
    copies = []
    for i in range(4):
        out, low = (enc, proc)[i // 2], (i % 2) * 192
        row = pl.multiple_of(plane * 128, 128)
        copies.append(
            pltpu.make_async_copy(
                shards[2 * i].at[pl.ds(row, 128), :], out.at[pl.ds(low, 128), :], sem.at[2 * i]
            )
        )
        copies.append(
            pltpu.make_async_copy(
                shards[2 * i + 1].at[
                    pl.ds(pl.multiple_of(half * 64, 64), 64),
                    pl.ds(pl.multiple_of(quarter * 128, 128), 128),
                ],
                out.at[pl.ds(low + 128, 64), :],
                sem.at[2 * i + 1],
            )
        )
    for copy in copies:
        copy.start()
    for copy in copies:
        copy.wait()


def pack_whole(first, second):
    features = second.shape[1]
    columns = features // LANES
    blocks = 2 * columns
    one = first.reshape(blocks, 128, columns, 128).transpose(0, 2, 1, 3)
    two = second.reshape(columns, 2, 64, columns, 128).transpose(1, 3, 0, 2, 4)
    return jnp.concatenate(
        [one.reshape(blocks * columns, 128, 128), two.reshape(blocks * columns, 64, 128)], axis=1
    )


def gather_weights(shards):
    features = shards[1].shape[1]
    planes = lax.axis_size("groups") * lax.axis_size("graph")
    if features == 512 and planes == 8 and lax.axis_size("mp") == 4:
        enc, proc = pl.pallas_call(
            pack_kernel,
            out_shape=[shape(384, 128, BF16)] * 2,
            in_specs=[pl.BlockSpec(memory_space=pl.ANY)] * 8,
            out_specs=[pl.BlockSpec(memory_space=pl.ANY)] * 2,
            scratch_shapes=[pltpu.SemaphoreType.DMA((8,))],
            name="pack",
        )(*shards)
        return lax.all_gather(enc, AXES), lax.all_gather(proc, AXES)
    whole = [lax.all_gather(w, "mp", axis=1 - i % 2, tiled=True) for i, w in enumerate(shards)]
    packed = [pack_whole(whole[2 * i], whole[2 * i + 1]) for i in range(4)]
    return jnp.concatenate(packed[:2], axis=1), jnp.concatenate(packed[2:], axis=1)


def forward(inputs, first, second):
    before = dot(inputs, first)
    logistic = jax.nn.sigmoid(before)
    hidden = (before * logistic).astype(BF16)
    slope = logistic * (1.0 + before * (1.0 - logistic))
    summed = dot(hidden, second)
    centered = summed - jnp.mean(summed, axis=-1, keepdims=True)
    rescale = lax.rsqrt(jnp.mean(centered * centered, axis=-1, keepdims=True) + 1e-05)
    normed = centered * rescale
    return normed, slope.astype(BF16), normed.astype(BF16), rescale


def backward_hidden(incoming, slope, normed, rescale, second):
    normed = normed.astype(F32)
    g_out = (
        incoming
        - jnp.mean(incoming, axis=-1, keepdims=True)
        - normed * jnp.mean(incoming * normed, axis=-1, keepdims=True)
    ) * rescale
    return (dot_trans(g_out.astype(BF16), second) * slope.astype(F32)).astype(BF16)


def table(index_row, count):
    n = index_row.shape[1]
    return jnp.where(lax.broadcasted_iota(jnp.int32, (count, n), 0) == index_row, 1.0, 0.0)


def send_kernel(grid_ref, send_ref, outgoing_ref, table_ref):
    one = table(send_ref[...], grid_ref.shape[0])
    table_ref[...] = one.astype(BF16)
    outgoing_ref[...] = dot(one.T.astype(BF16), grid_ref[...]).astype(BF16)


def tables_kernel(
    mesh_ref,
    slot_ref,
    recv_e_ref,
    halo_ref,
    sender_ref,
    recv_p_ref,
    slot_t,
    slot_g,
    enc_t,
    enc_g,
    halo_t,
    halo_g,
    sender_t,
    sender_g,
    proc_t,
    proc_g,
    recv_rows,
):
    for index, scatter, gather in (
        (slot_ref, slot_t, slot_g),
        (recv_e_ref, enc_t, enc_g),
        (halo_ref, halo_t, halo_g),
        (sender_ref, sender_t, sender_g),
        (recv_p_ref, proc_t, proc_g),
    ):
        one = table(index[...], scatter.shape[0])
        scatter[...] = one.astype(BF16)
        gather[...] = one.T.astype(BF16)
    recv_rows[...] = dot(enc_g[...], mesh_ref[...]).astype(BF16)


def encode_kernel(
    mesh_ref,
    arrived_ref,
    slot_g,
    recv_rows,
    enc_t,
    halo_g,
    weights,
    one_ref,
    halo_ref,
    slope_e,
    normed_e,
    scale_e,
    slope_n,
    normed_n,
    scale_n,
):
    features = mesh_ref.shape[1]
    first, second = weight_pair(weights, 0, features)
    edges = slot_g.shape[0]
    for low in range(0, edges, ROWS):
        rows = pl.ds(low, ROWS)
        sent = dot(slot_g[rows, :], arrived_ref[...]).astype(BF16)
        inputs = jnp.concatenate([sent, recv_rows[rows, :]], axis=1)
        _, slope, normed, rescale = forward(inputs, first, second)
        slope_e[rows, :] = slope
        normed_e[rows, :] = normed
        scale_e[rows, :] = jnp.broadcast_to(rescale, (ROWS, LANES))
    aggregate = dot(enc_t[...], normed_e[...]).astype(BF16)
    first, second = weight_pair(weights, 1, features)
    mesh = mesh_ref[...]
    normed, slope, rounded, rescale = forward(
        jnp.concatenate([mesh, aggregate], axis=1), first, second
    )
    slope_n[...] = slope
    normed_n[...] = rounded
    scale_n[...] = jnp.broadcast_to(rescale, scale_n.shape)
    one_ref[...] = (mesh.astype(F32) + normed).astype(BF16)
    halo_ref[...] = dot(halo_g[...], one_ref[...]).astype(BF16)


def process_kernel(
    one_ref,
    halo_ref,
    cotangent_ref,
    sender_t,
    sender_g,
    proc_t,
    proc_g,
    weights,
    two_ref,
    grad_one_ref,
    grad_halo_ref,
    slope_p,
    normed_p,
    scale_p,
    ga_p,
):
    features = one_ref.shape[1]
    mesh_rows = one_ref.shape[0]
    edges = sender_g.shape[0]
    first, second = weight_pair(weights, 0, features)
    lookup = jnp.concatenate([one_ref[...], halo_ref[...]], axis=0)
    for low in range(0, edges, ROWS):
        rows = pl.ds(low, ROWS)
        sent = dot(sender_g[rows, :], lookup).astype(BF16)
        got = dot(proc_g[rows, :], one_ref[...]).astype(BF16)
        _, slope, normed, rescale = forward(jnp.concatenate([sent, got], axis=1), first, second)
        slope_p[rows, :] = slope
        normed_p[rows, :] = normed
        scale_p[rows, :] = jnp.broadcast_to(rescale, (ROWS, LANES))
    aggregate = dot(proc_t[...], normed_p[...]).astype(BF16)
    first_n, second_n = weight_pair(weights, 1, features)
    one = one_ref[...]
    normed, slope, rounded, rescale = forward(
        jnp.concatenate([one, aggregate], axis=1), first_n, second_n
    )
    two_ref[...] = (one.astype(F32) + normed).astype(BF16)
    cotangent = cotangent_ref[...].astype(F32)
    ga = backward_hidden(cotangent, slope, rounded, rescale, second_n)
    g_q = dot_trans(ga, first_n)
    g_msg = g_q[:, features:].astype(BF16)
    for low in range(0, edges, ROWS):
        rows = pl.ds(low, ROWS)
        incoming = dot(proc_g[rows, :], g_msg)
        ga_p[rows, :] = backward_hidden(
            incoming, slope_p[rows, :], normed_p[rows, :], scale_p[rows, 0:1], second
        )
    by_recv = dot(proc_t[...], ga_p[...]).astype(BF16)
    by_send = dot(sender_t[...], ga_p[...]).astype(BF16)
    g_send = dot_trans(by_send, first[:features, :])
    g_recv = dot_trans(by_recv, first[features:, :])
    grad_one_ref[...] = cotangent + g_q[:, :features] + g_recv + g_send[:mesh_rows, :]
    grad_halo_ref[...] = g_send[mesh_rows:, :].astype(BF16)


def decode_kernel(
    grad_one_ref,
    back_ref,
    halo_t,
    slope_e,
    normed_e,
    scale_e,
    slope_n,
    normed_n,
    scale_n,
    enc_t,
    enc_g,
    slot_t,
    weights,
    mesh_grad_ref,
    grad_slots_ref,
    ga_e,
):
    features = grad_one_ref.shape[1]
    edges = enc_g.shape[0]
    grad_one = grad_one_ref[...] + dot(halo_t[...], back_ref[...])
    first_n, second_n = weight_pair(weights, 1, features)
    ga = backward_hidden(grad_one, slope_n[...], normed_n[...], scale_n[:, 0:1], second_n)
    g_n = dot_trans(ga, first_n)
    g_edge = g_n[:, features:].astype(BF16)
    first, second = weight_pair(weights, 0, features)
    for low in range(0, edges, ROWS):
        rows = pl.ds(low, ROWS)
        incoming = dot(enc_g[rows, :], g_edge)
        ga_e[rows, :] = backward_hidden(
            incoming, slope_e[rows, :], normed_e[rows, :], scale_e[rows, 0:1], second
        )
    by_recv = dot(enc_t[...], ga_e[...]).astype(BF16)
    by_slot = dot(slot_t[...], ga_e[...]).astype(BF16)
    mesh_grad_ref[...] = grad_one + g_n[:, :features] + dot_trans(by_recv, first[features:, :])
    grad_slots_ref[...] = dot_trans(by_slot, first[:features, :]).astype(BF16)


def grid_kernel(table_ref, back_ref, out_ref):
    out_ref[...] = dot(table_ref[...], back_ref[...])


def exchange(rows, capacity):
    features = rows.shape[1]
    parts = rows.reshape(-1, capacity, features)
    return lax.all_to_all(parts, PEERS, split_axis=0, concat_axis=0, tiled=True).reshape(rows.shape)


def local(
    grid_lat,
    mesh_lat,
    cotangent,
    grid_send,
    g2m_slot,
    g2m_receiver,
    halo_send,
    mesh_sender,
    mesh_receiver,
    *shards,
):
    grid_rows, features = grid_lat.shape
    mesh_rows = mesh_lat.shape[0]
    edges = g2m_slot.shape[0]
    mesh_edges = mesh_sender.shape[0]
    slots, halos = grid_send.size, halo_send.size
    capacity, halo_capacity = grid_send.shape[1], halo_send.shape[1]
    enc_weights, proc_weights = gather_weights(shards)

    outgoing, grid_t = call(
        send_kernel,
        [shape(slots, features, BF16), shape(grid_rows, slots, BF16)],
        grid_lat,
        grid_send.reshape(1, slots),
    )
    arrived = exchange(outgoing, capacity)
    slot_t, slot_g, enc_t, enc_g, halo_t, halo_g, sender_t, sender_g, proc_t, proc_g, recv_rows = call(
        tables_kernel,
        [
            shape(slots, edges, BF16),
            shape(edges, slots, BF16),
            shape(mesh_rows, edges, BF16),
            shape(edges, mesh_rows, BF16),
            shape(mesh_rows, halos, BF16),
            shape(halos, mesh_rows, BF16),
            shape(mesh_rows + halos, mesh_edges, BF16),
            shape(mesh_edges, mesh_rows + halos, BF16),
            shape(mesh_rows, mesh_edges, BF16),
            shape(mesh_edges, mesh_rows, BF16),
            shape(edges, features, BF16),
        ],
        mesh_lat,
        g2m_slot.reshape(1, edges),
        g2m_receiver.reshape(1, edges),
        halo_send.reshape(1, halos),
        mesh_sender.reshape(1, mesh_edges),
        mesh_receiver.reshape(1, mesh_edges),
    )
    saved = [
        shape(edges, features, BF16),
        shape(edges, features, BF16),
        shape(edges, LANES, F32),
        shape(mesh_rows, features, BF16),
        shape(mesh_rows, features, BF16),
        shape(mesh_rows, LANES, F32),
    ]
    mesh_one, halo_out, *kept = call(
        encode_kernel,
        [shape(mesh_rows, features, BF16), shape(halos, features, BF16)] + saved,
        mesh_lat,
        arrived,
        slot_g,
        recv_rows,
        enc_t,
        halo_g,
        enc_weights,
    )
    halo_in = exchange(halo_out, halo_capacity)
    mesh_two, grad_one, grad_halo = pl.pallas_call(
        process_kernel,
        out_shape=[
            shape(mesh_rows, features, BF16),
            shape(mesh_rows, features, F32),
            shape(halos, features, BF16),
        ],
        in_specs=[pl.BlockSpec(memory_space=pltpu.VMEM)] * 8,
        out_specs=[pl.BlockSpec(memory_space=pltpu.VMEM)] * 3,
        scratch_shapes=[
            pltpu.VMEM((mesh_edges, features), BF16),
            pltpu.VMEM((mesh_edges, features), BF16),
            pltpu.VMEM((mesh_edges, LANES), F32),
            pltpu.VMEM((mesh_edges, features), BF16),
        ],
        compiler_params=pltpu.CompilerParams(vmem_limit_bytes=40 * 1024 * 1024),
    )(mesh_one, halo_in, cotangent, sender_t, sender_g, proc_t, proc_g, proc_weights)
    halo_back = exchange(grad_halo, halo_capacity)
    mesh_grad, grad_slots = pl.pallas_call(
        decode_kernel,
        out_shape=[shape(mesh_rows, features, F32), shape(slots, features, BF16)],
        in_specs=[pl.BlockSpec(memory_space=pltpu.VMEM)] * 13,
        out_specs=[pl.BlockSpec(memory_space=pltpu.VMEM)] * 2,
        scratch_shapes=[pltpu.VMEM((edges, features), BF16)],
        compiler_params=pltpu.CompilerParams(vmem_limit_bytes=40 * 1024 * 1024),
    )(grad_one, halo_back, halo_t, *kept, enc_t, enc_g, slot_t, enc_weights)
    returned = exchange(grad_slots, capacity)
    (grid_grad,) = call(grid_kernel, [shape(grid_rows, features, F32)], grid_t, returned)
    return (mesh_two, grid_grad, mesh_grad)


def solution(mesh):
    rows = P(AXES, None)
    flat = P(AXES)
    in_specs = (rows,) * 4 + (flat,) * 2 + (rows,) + (flat,) * 2 + (P(None, "mp"), P("mp", None)) * 4
    return jax.shard_map(
        local, mesh=mesh, in_specs=in_specs, out_specs=(rows,) * 3, check_vma=False
    )
```

time: 223 us -> 195 us (0.87)
  waiting for transfers between devices: 32.9 us -> 81.3 us
  blocking collectives: 77.2 us -> 30.9 us
  matrix products: 37.7 us -> 0 us
  Pallas kernels: 0 us -> 20.7 us
  other arithmetic: 15.5 us -> 0 us
  local copies, waits for them, and re-layouts: 23.8 us -> 39.3 us
  starting transfers between devices: 20.6 us -> 7.44 us
    all_gather x4 -> x0, blocking collectives: 77.2 us -> none  [the longest x1 23.1 us: local(): lax.all_gather(proc_node_out, 'mp', axis=0, tiled=True)]
    all_gather x4 -> x2, waiting for transfers between devices: 14.1 us -> 80.6 us  [gather_weights(): return (lax.all_gather(enc, AXES), lax.all_gather(proc, AXES))]
    dot_general x20 -> x0, matrix products: 37.7 us -> none  [the longest x4 15.7 us: dense_trans(): lax.dot_general(left, right, (((1,), (1,)), ((), ())), preferred_element_...]
    unnamed x56 -> x86, local copies, waits for them, and re-layouts: 2.37 us -> 36.7 us
    all_to_all x0 -> x3, blocking collectives: none -> 30.9 us  [exchange(): lax.all_to_all(parts, PEERS, split_axis=0, concat_axis=0, tiled=True)]
    pallas_call x0 -> x7, Pallas kernels: none -> 20.7 us  [the longest x1 7.14 us: gather_weights(): pl.pallas_call(pack_kernel, out_shape=[shape(384, 128, BF16)] * 2, in_spe...]
    gather x12 -> x0, local copies, waits for them, and re-layouts: 17.2 us -> none  [the longest x2 4.96 us: local(): grad_msg = jnp.take(g_q[:, features:], mesh_receiver, axis=0)]
    all_to_all x4 -> x1, waiting for transfers between devices: 16.2 us -> 0.01 us  [exchange(): lax.all_to_all(parts, PEERS, split_axis=0, concat_axis=0, tiled=True)]
  transfers between devices with their start and end apart: 8 -> 3, of which waited for: 4 -> 2; matrix products, arithmetic and copies ran while one was open for 15% -> 2% of each run, Pallas kernels for 0% -> 2%
where the time goes in v1:
time: 195 us; the launch traced here: 194 us
  waiting for transfers between devices  81.3 us (42%)
  local copies, waits for them, and re-layouts  39.3 us (20%)
  blocking collectives  30.9 us (16%)
  Pallas kernels  20.7 us (11%)
  between operations  14.2 us (7%)
  starting transfers between devices  7.44 us (4%)
    all_gather x2, waiting for transfers between devices, gather_weights(): return (lax.all_gather(enc, AXES), lax.all_gather(proc, AXES))  80.6 us
    unnamed x86, local copies, waits for them, and re-layouts  36.7 us
    all_to_all x3, blocking collectives, exchange(): lax.all_to_all(parts, PEERS, split_axis=0, concat_axis=0, tiled=True)  30.9 us
    all_to_all x1, starting transfers between devices, exchange(): lax.all_to_all(parts, PEERS, split_axis=0, concat_axis=0, tiled=True)  7.36 us
    pallas_call x1, Pallas kernels, gather_weights(): pl.pallas_call(pack_kernel, out_shape=[shape(384, 128, BF16)] * 2, in_spe...  7.14 us
    pallas_call x1, Pallas kernels, local(): pl.pallas_call(process_kernel, out_shape=[shape(mesh_rows, features, BF16...  5.67 us
    pallas_call x4, Pallas kernels, call(): pl.pallas_call(kernel, out_shape=out_shape, in_specs=[pl.BlockSpec(memory...  4.7 us
  transfers between devices with their start and end apart: 3, of which 2 were waited for; matrix products, arithmetic and copies ran while one was open for 2% of the time, Pallas kernels for 2%

profile of v1, /device:TPU:0, one launch (start us, length us, event | category | flops | bytes accessed | tf_op | source)
XLA Modules:
  0.0 193.8 jit_solution(2594284663302021089)
XLA Ops:
  7.2 7.1 %pack.1 = (bf16[384,128]{1,0:T(8,128)(2,1)}, bf16[384,128]{1,0:T(8,128)(2,1)}) custom-call(bf16[1024,128]{1,0:T(8,128)(2,1)} %refs_0_.1, bf16[128,512]{1,0:T(8,128)(2,1)} %refs_1_.1, bf16[1024,128]{1,0:T(8,128)(2,1)} %refs_2_.1, bf16[128,512]{1,0:T(8,128)(2,1)} %refs_3_.1, bf16[1024,128]{1,0:T(8,128)(2,1)} %refs_4_.1, bf16[128,512]{1,0:T(8,128)(2,1)} %refs_5_.1, ...), custom_call_target="tpu_custom_call" | custom-call | tf_op jit(solution)/shard_map/pack/pallas_call | solution.py:103
  16.0 1.0 copy-done.11
  18.6 7.4 %all-to-all-start = ((bf16[16,4,512]{2,1,0:T(4,128)(2,1)}), bf16[16,4,512]{2,1,0:T(4,128)(2,1)S(1)}, u32[]{:S(2)}, u32[]{:S(2)}) async-start(bf16[16,4,512]{2,1,0:T(4,128)(2,1)} %reshape.49), calls=%async_computation | async-start | bytes 131072 | tf_op jit(solution)/shard_map/all_to_all | solution.py:323
  35.2 41.4 %all-gather.5.cloned.1.call-done = bf16[12288,128]{1,0:T(8,128)(2,1)} async-done(((bf16[384,128]{1,0:T(8,128)(2,1)}), bf16[12288,128]{1,0:T(8,128)(2,1)}) %all-gather.5.cloned.1.call-update) | async-done | bytes 3145744 | tf_op jit(solution)/shard_map/all_gather | solution.py:111
  76.6 1.9 copy-done
  78.4 2.8 %shard_map.186 = (bf16[256,512]{1,0:T(8,128)(2,1)S(1)}, bf16[32,512]{1,0:T(8,128)(2,1)S(1)}, bf16[512,512]{1,0:T(8,128)(2,1)S(1)}, bf16[512,512]{1,0:T(8,128)(2,...) custom-call(bf16[256,512]{1,0:T(8,128)(2,1)S(1)} %copy-done.4, ...), custom_call_target="tpu_custom_call" | custom-call | tf_op jit(solution)/shard_map/pallas_call | solution.py:28
  86.4 11.1 %all_to_all.20 = bf16[16,2,512]{2,1,0:T(2,128)(2,1)} all-to-all(bf16[16,2,512]{2,1,0:T(2,128)(2,1)S(1)} %reshape.56), channel_id=1, replica_groups=mesh['groups'=2,'graph'=4,'mp'=4] {'graph','mp'}, dimensions={0} | all-to-all | bytes 65536 | tf_op jit(solution)/shard_map/all_to_all | solution.py:323
  98.2 39.2 %all-gather.7.cloned.1.call-done = bf16[12288,128]{1,0:T(8,128)(2,1)} async-done(((bf16[384,128]{1,0:T(8,128)(2,1)}), bf16[12288,128]{1,0:T(8,128)(2,1)}) %all-gather.7.cloned.1.call-update) | async-done | bytes 3145744 | tf_op jit(solution)/shard_map/all_gather | solution.py:111
  137.4 1.9 copy-done.2
  139.3 1.0 copy-done.13
  140.3 1.0 copy-done.15
  141.2 0.9 copy-done.16
  142.2 0.9 copy-done.20
  144.1 0.9 copy-done.30
  145.0 5.7 %shard_map.187 = (bf16[256,512]{1,0:T(8,128)(2,1)}, f32[256,512]{1,0:T(8,128)S(1)}, bf16[32,512]{1,0:T(8,128)(2,1)S(1)}) custom-call(bf16[256,512]{1,0:T(8,128)(2,1)S(1)} %copy-done.30, bf16[32,512]{1,0:T(8,128)(2,1)S(1)} %reshape.57.halo_ref, bf16[256,512]{1,0:T(8,128)(2,1)S(1)} %copy-done.16, bf16[288,512]{1,0:T(8,128)(2,1)S(1)} %copy-done.15, ...), custom_call_target="tpu_custom_call" | custom-call | tf_op jit(solution)/shard_map/pallas_call | solution.py:395
  151.5 10.7 %all_to_all.21 = bf16[16,2,512]{2,1,0:T(2,128)(2,1)S(1)} all-to-all(bf16[16,2,512]{2,1,0:T(2,128)(2,1)S(1)} %reshape.58), channel_id=1, replica_groups=mesh['groups'=2,'graph'=4,'mp'=4] {'graph','mp'}, dimensions={0} | all-to-all | bytes 65536 | tf_op jit(solution)/shard_map/all_to_all | solution.py:323
  162.3 1.0 copy-done.6
  163.3 1.0 copy-done.8
  164.3 1.0 copy-done.10
  165.4 0.9 copy-done.18
  166.3 0.9 copy-done.24
  170.9 3.2 %shard_map.188 = (f32[256,512]{1,0:T(8,128)}, bf16[64,512]{1,0:T(8,128)(2,1)S(1)}) custom-call(f32[256,512]{1,0:T(8,128)S(1)} %copy-done.10, bf16[32,512]{1,0:T(8,128)(2,1)S(1)} %reshape.59.back_ref, bf16[256,32]{1,0:T(8,128)(2,1)S(1)} %copy-done.36, bf16[512,512]{1,0:T(8,128)(2,1)S(1)} %copy-done.6, bf16[512,512]{1,0:T(8,128)(2,1)S(1)} %copy-done.8, ...), custom_call_target="tpu_custom_call" | custom-call | tf_op jit(solution)/shard_map/pallas_call | solution.py:413
  175.6 9.2 %all_to_all.22 = bf16[16,4,512]{2,1,0:T(4,128)(2,1)S(1)} all-to-all(bf16[16,4,512]{2,1,0:T(4,128)(2,1)S(1)} %reshape.60), channel_id=1, replica_groups=mesh['groups'=2,'graph'=4,'mp'=4] {'graph','mp'}, dimensions={0} | all-to-all | bytes 131072 | tf_op jit(solution)/shard_map/all_to_all | solution.py:323
  185.7 1.2 shard_map.189
  (90 shorter events, 26.1 us)
Async XLA Ops:
  7.2 69.4 %copy-start.4 = (bf16[256,512]{1,0:T(8,128)(2,1)S(1)}, bf16[256,512]{1,0:T(8,128)(2,1)}, u32[]{:S(2)}) copy-start(bf16[256,512]{1,0:T(8,128)(2,1)} %mesh_ref.3) | copy-start | bytes 786436
  7.2 69.4 %all-gather.5.cloned.1.call-start = ((), (), s32[]{:S(2)}) async-start(), calls=%async_computation.4 | async-start | bytes 3244032 | tf_op jit(solution)/shard_map/all_gather | solution.py:111
  14.4 123.0 %all-gather.7.cloned.1.call-start = ((), (), s32[]{:S(2)}) async-start(), calls=%async_computation.5 | async-start | bytes 3244032 | tf_op jit(solution)/shard_map/all_gather | solution.py:111
  16.0 1.0 copy-start.11
  18.6 16.5 %all-to-all-start = ((bf16[16,4,512]{2,1,0:T(4,128)(2,1)}), bf16[16,4,512]{2,1,0:T(4,128)(2,1)S(1)}, u32[]{:S(2)}, u32[]{:S(2)}) async-start(bf16[16,4,512]{2,1,0:T(4,128)(2,1)} %reshape.49), calls=%async_computation | async-start | bytes 131072 | tf_op jit(solution)/shard_map/all_to_all | solution.py:323
  26.8 1.0 copy-start.3
  76.6 1.9 copy-start
  86.4 75.9 %copy-start.1 = (bf16[12288,128]{1,0:T(8,128)(2,1)S(1)}, bf16[12288,128]{1,0:T(8,128)(2,1)}, u32[]{:S(2)}) copy-start(bf16[12288,128]{1,0:T(8,128)(2,1)} %all-gather.5.cloned.1.call-done) | copy-start | bytes 9437188
  137.4 1.9 copy-start.2
  139.3 1.0 copy-start.13
  140.3 1.0 copy-start.15
  141.2 0.9 copy-start.16
  142.2 0.9 copy-start.20
  143.1 0.9 copy-start.22
  144.1 0.9 copy-start.30
  162.2 1.0 copy-start.6
  163.3 1.0 copy-start.8
  164.3 1.0 copy-start.10
  165.4 0.9 copy-start.18
  166.3 0.9 copy-start.24
  167.3 0.9 copy-start.26
  168.2 0.9 copy-start.28
  169.2 0.9 copy-start.34
  184.8 0.9 copy-start.32
  (21 other events, 15.0 us)
Sparse Core Ops, SparseCore 0:
  14.5 61.9 all-gather.4
  79.4 57.9 all-gather.6

commit v2 on v1

--- a/solution.py
+++ b/solution.py
@@ -11,6 +11,7 @@
 BF16 = jnp.bfloat16
 LANES = 128
 ROWS = 256
+FEATURES = 512
 AXES = ("groups", "graph", "mp")
 PEERS = ("graph", "mp")
 
@@ -23,59 +24,80 @@
     return lax.dot_general(left, right, (((1,), (1,)), ((), ())), preferred_element_type=F32)
 
 
-def call(kernel, out_shape, *args):
-    flops = 0
+def call(kernel, out_shape, *args, weights=None, scratch=()):
+    scratch = list(scratch)
+    in_specs = [pl.BlockSpec(a.shape, functools.partial(origin, a.ndim)) for a in args]
+    extra = []
+    if weights is not None:
+        place, sets = weights
+        sizes = [len(arrays) for arrays in sets]
+        extra = [a for arrays in sets for a in arrays]
+        for arrays in sets:
+            in_specs += [pl.BlockSpec(memory_space=pltpu.HBM)] * 2
+            in_specs += [pl.BlockSpec(memory_space=pl.ANY)] * (len(arrays) - 2)
+        for arrays in sets:
+            scratch.append(pltpu.VMEM((2 * FEATURES, FEATURES), BF16))
+            scratch.append(pltpu.VMEM((FEATURES, FEATURES), BF16))
+        scratch.append(pltpu.SemaphoreType.DMA((len(sets), 2)))
+
+    def body(*refs):
+        if weights is None:
+            return kernel(*refs)
+        ins, refs = refs[: len(args)], refs[len(args) :]
+        sources, refs = refs[: len(extra)], refs[len(extra) :]
+        outs, refs = refs[: len(out_shape)], refs[len(out_shape) :]
+        own, refs = refs[: len(scratch) - 2 * len(sets) - 1], refs[len(scratch) - 2 * len(sets) - 1 :]
+        sem = refs[-1]
+        held, low = [], 0
+        for i, size in enumerate(sizes):
+            one = (sources[low : low + size], refs[2 * i], refs[2 * i + 1], sem.at[i])
+            low += size
+            place(*one)
+            held.append(one)
+        kernel(held, *ins, *outs, *own)
+
     return pl.pallas_call(
-        kernel,
+        body,
+        grid=(1,),
         out_shape=out_shape,
-        in_specs=[pl.BlockSpec(memory_space=pltpu.VMEM)] * len(args),
-        out_specs=[pl.BlockSpec(memory_space=pltpu.VMEM)] * len(out_shape),
+        in_specs=in_specs,
+        out_specs=[pl.BlockSpec(s.shape, functools.partial(origin, len(s.shape))) for s in out_shape],
+        scratch_shapes=scratch,
+        name=kernel.__name__,
         compiler_params=pltpu.CompilerParams(vmem_limit_bytes=40 * 1024 * 1024),
-    )(*args)
+    )(*args, *extra)
+
+
+def origin(rank, step):
+    return (0,) * rank
+
+
+def taken(one):
+    wait_weights(*one)
+    return one[1][...], one[2][...]
 
 
 def shape(rows, columns, dtype):
     return jax.ShapeDtypeStruct((rows, columns), dtype)
 
 
-def weight_pair(ref, which, features):
-    columns = features // LANES
-    blocks = 2 * columns
-    low = which * 192
-    first = [
-        jnp.concatenate([ref[p * columns + m, low : low + 128, :] for p in range(blocks)], axis=0)
-        for m in range(columns)
-    ]
-    second = []
-    for q in range(columns):
-        parts = []
-        for m in range(columns):
-            for half in range(2):
-                parts.append(ref[(half * columns + q) * columns + m, low + 128 : low + 192, :])
-        second.append(jnp.concatenate(parts, axis=0))
-    return jnp.concatenate(first, axis=1), jnp.concatenate(second, axis=1)
-
-
 def pack_kernel(*refs):
-    shards, (enc, proc), sem = refs[:8], refs[8:10], refs[10]
+    shards, outs, sem = refs[:8], refs[8:12], refs[12]
     plane = lax.axis_index("groups") * lax.axis_size("graph") + lax.axis_index("graph")
-    half, quarter = plane // 4, plane % 4
     copies = []
-    for i in range(4):
-        out, low = (enc, proc)[i // 2], (i % 2) * 192
+    for i, out in enumerate(outs):
         row = pl.multiple_of(plane * 128, 128)
+        low = pl.multiple_of(plane // 4 * 64, 64)
+        column = pl.multiple_of(plane % 4 * 128, 128)
         copies.append(
             pltpu.make_async_copy(
-                shards[2 * i].at[pl.ds(row, 128), :], out.at[pl.ds(low, 128), :], sem.at[2 * i]
+                shards[2 * i].at[pl.ds(row, 128), :], out.at[pl.ds(0, 128), :], sem.at[2 * i]
             )
         )
         copies.append(
             pltpu.make_async_copy(
-                shards[2 * i + 1].at[
-                    pl.ds(pl.multiple_of(half * 64, 64), 64),
-                    pl.ds(pl.multiple_of(quarter * 128, 128), 128),
-                ],
-                out.at[pl.ds(low + 128, 64), :],
+                shards[2 * i + 1].at[pl.ds(low, 64), pl.ds(column, 128)],
+                out.at[pl.ds(128, 64), :],
                 sem.at[2 * i + 1],
             )
         )
@@ -85,33 +107,81 @@
         copy.wait()
 
 
-def pack_whole(first, second):
-    features = second.shape[1]
-    columns = features // LANES
-    blocks = 2 * columns
-    one = first.reshape(blocks, 128, columns, 128).transpose(0, 2, 1, 3)
-    two = second.reshape(columns, 2, 64, columns, 128).transpose(1, 3, 0, 2, 4)
-    return jnp.concatenate(
-        [one.reshape(blocks * columns, 128, 128), two.reshape(blocks * columns, 64, 128)], axis=1
-    )
+def place_pieces(refs, first, second, sem):
+    (own_first, own_second), pieces = refs[:2], refs[2:]
+    sem, sem_second = sem.at[0], sem.at[1]
+    me = lax.axis_index("mp")
+    plane = lax.axis_index("groups") * lax.axis_size("graph") + lax.axis_index("graph")
+    column = pl.multiple_of(me * 128, 128)
+    copies = [
+        pltpu.make_async_copy(own_first, first.at[:, pl.ds(column, 128)], sem),
+        pltpu.make_async_copy(own_second, second.at[pl.ds(column, 128), :], sem_second),
+    ]
+    for d, piece in enumerate(pieces):
+        source = plane ^ d
+        for step in range(3):
+            m = (me + 3 - step) % 4
+            copies.append(
+                pltpu.make_async_copy(
+                    piece.at[step, pl.ds(0, 128), :],
+                    first.at[
+                        pl.ds(pl.multiple_of(source * 128, 128), 128),
+                        pl.ds(pl.multiple_of(m * 128, 128), 128),
+                    ],
+                    sem,
+                )
+            )
+            copies.append(
+                pltpu.make_async_copy(
+                    piece.at[step, pl.ds(128, 64), :],
+                    second.at[
+                        pl.ds(pl.multiple_of(m * 128 + source // 4 * 64, 64), 64),
+                        pl.ds(pl.multiple_of(source % 4 * 128, 128), 128),
+                    ],
+                    sem_second,
+                )
+            )
+    for copy in copies:
+        copy.start()
+
+
+def place_whole(refs, first, second, sem):
+    pltpu.make_async_copy(refs[0], first, sem.at[0]).start()
+    pltpu.make_async_copy(refs[1], second, sem.at[1]).start()
+
+
+def wait_weights(refs, first, second, sem):
+    pltpu.make_async_copy(first, first, sem.at[0]).wait()
+    pltpu.make_async_copy(second, second, sem.at[1]).wait()
 
 
 def gather_weights(shards):
-    features = shards[1].shape[1]
     planes = lax.axis_size("groups") * lax.axis_size("graph")
-    if features == 512 and planes == 8 and lax.axis_size("mp") == 4:
-        enc, proc = pl.pallas_call(
-            pack_kernel,
-            out_shape=[shape(384, 128, BF16)] * 2,
-            in_specs=[pl.BlockSpec(memory_space=pl.ANY)] * 8,
-            out_specs=[pl.BlockSpec(memory_space=pl.ANY)] * 2,
-            scratch_shapes=[pltpu.SemaphoreType.DMA((8,))],
-            name="pack",
-        )(*shards)
-        return lax.all_gather(enc, AXES), lax.all_gather(proc, AXES)
-    whole = [lax.all_gather(w, "mp", axis=1 - i % 2, tiled=True) for i, w in enumerate(shards)]
-    packed = [pack_whole(whole[2 * i], whole[2 * i + 1]) for i in range(4)]
-    return jnp.concatenate(packed[:2], axis=1), jnp.concatenate(packed[2:], axis=1)
+    if shards[1].shape[1] != 512 or planes != 8 or lax.axis_size("mp") != 4:
+        whole = [lax.all_gather(w, "mp", axis=1 - i % 2, tiled=True) for i, w in enumerate(shards)]
+        return place_whole, [whole[2 * i : 2 * i + 2] for i in range(4)]
+    pieces = pl.pallas_call(
+        pack_kernel,
+        out_shape=[shape(192, 128, BF16)] * 4,
+        in_specs=[pl.BlockSpec(memory_space=pltpu.HBM)] * 8,
+        out_specs=[pl.BlockSpec(memory_space=pl.ANY)] * 4,
+        scratch_shapes=[pltpu.SemaphoreType.DMA((8,))],
+        name="pack",
+    )(*shards)
+
+    def across(x, flip):
+        return lax.ppermute(x, ("groups", "graph"), [(p, p ^ flip) for p in range(8)])
+
+    sets = []
+    for i, piece in enumerate(pieces):
+        along = [lax.ppermute(piece, "mp", [(m, (m + s) % 4) for m in range(4)]) for s in (1, 2, 3)]
+        held = {0: jnp.stack(along)}
+        for flip in (2, 4, 6):
+            held[flip] = across(held[0], flip)
+        for flip in (0, 2, 4, 6):
+            held[flip + 1] = across(held[flip], 1)
+        sets.append([shards[2 * i], shards[2 * i + 1]] + [held[d] for d in range(8)])
+    return place_pieces, sets
 
 
 def forward(inputs, first, second):
@@ -141,8 +211,18 @@
     return jnp.where(lax.broadcasted_iota(jnp.int32, (count, n), 0) == index_row, 1.0, 0.0)
 
 
+def flat_row(index):
+    count, width = index.shape
+    at = lax.broadcasted_iota(jnp.int32, (count, count * width), 1)
+    row = lax.broadcasted_iota(jnp.int32, (count, count * width), 0)
+    spread = jnp.zeros_like(at)
+    for c in range(width):
+        spread = jnp.where(at % width == c, index[:, c : c + 1], spread)
+    return jnp.sum(jnp.where(at // width == row, spread, 0), axis=0, keepdims=True)
+
+
 def send_kernel(grid_ref, send_ref, outgoing_ref, table_ref):
-    one = table(send_ref[...], grid_ref.shape[0])
+    one = table(flat_row(send_ref[...]), grid_ref.shape[0])
     table_ref[...] = one.astype(BF16)
     outgoing_ref[...] = dot(one.T.astype(BF16), grid_ref[...]).astype(BF16)
 
@@ -173,20 +253,21 @@
         (sender_ref, sender_t, sender_g),
         (recv_p_ref, proc_t, proc_g),
     ):
-        one = table(index[...], scatter.shape[0])
+        row = flat_row(index[...]) if index is halo_ref else index[...]
+        one = table(row, scatter.shape[0])
         scatter[...] = one.astype(BF16)
         gather[...] = one.T.astype(BF16)
     recv_rows[...] = dot(enc_g[...], mesh_ref[...]).astype(BF16)
 
 
 def encode_kernel(
+    held,
     mesh_ref,
     arrived_ref,
     slot_g,
     recv_rows,
     enc_t,
     halo_g,
-    weights,
     one_ref,
     halo_ref,
     slope_e,
@@ -197,7 +278,7 @@
     scale_n,
 ):
     features = mesh_ref.shape[1]
-    first, second = weight_pair(weights, 0, features)
+    first, second = taken(held[0])
     edges = slot_g.shape[0]
     for low in range(0, edges, ROWS):
         rows = pl.ds(low, ROWS)
@@ -208,7 +289,7 @@
         normed_e[rows, :] = normed
         scale_e[rows, :] = jnp.broadcast_to(rescale, (ROWS, LANES))
     aggregate = dot(enc_t[...], normed_e[...]).astype(BF16)
-    first, second = weight_pair(weights, 1, features)
+    first, second = taken(held[1])
     mesh = mesh_ref[...]
     normed, slope, rounded, rescale = forward(
         jnp.concatenate([mesh, aggregate], axis=1), first, second
@@ -221,6 +302,7 @@
 
 
 def process_kernel(
+    held,
     one_ref,
     halo_ref,
     cotangent_ref,
@@ -228,7 +310,6 @@
     sender_g,
     proc_t,
     proc_g,
-    weights,
     two_ref,
     grad_one_ref,
     grad_halo_ref,
@@ -240,7 +321,7 @@
     features = one_ref.shape[1]
     mesh_rows = one_ref.shape[0]
     edges = sender_g.shape[0]
-    first, second = weight_pair(weights, 0, features)
+    first, second = taken(held[0])
     lookup = jnp.concatenate([one_ref[...], halo_ref[...]], axis=0)
     for low in range(0, edges, ROWS):
         rows = pl.ds(low, ROWS)
@@ -251,7 +332,7 @@
         normed_p[rows, :] = normed
         scale_p[rows, :] = jnp.broadcast_to(rescale, (ROWS, LANES))
     aggregate = dot(proc_t[...], normed_p[...]).astype(BF16)
-    first_n, second_n = weight_pair(weights, 1, features)
+    first_n, second_n = taken(held[1])
     one = one_ref[...]
     normed, slope, rounded, rescale = forward(
         jnp.concatenate([one, aggregate], axis=1), first_n, second_n
@@ -276,6 +357,7 @@
 
 
 def decode_kernel(
+    held,
     grad_one_ref,
     back_ref,
     halo_t,
@@ -288,7 +370,6 @@
     enc_t,
     enc_g,
     slot_t,
-    weights,
     mesh_grad_ref,
     grad_slots_ref,
     ga_e,
@@ -296,11 +377,11 @@
     features = grad_one_ref.shape[1]
     edges = enc_g.shape[0]
     grad_one = grad_one_ref[...] + dot(halo_t[...], back_ref[...])
-    first_n, second_n = weight_pair(weights, 1, features)
+    first_n, second_n = taken(held[1])
     ga = backward_hidden(grad_one, slope_n[...], normed_n[...], scale_n[:, 0:1], second_n)
     g_n = dot_trans(ga, first_n)
     g_edge = g_n[:, features:].astype(BF16)
-    first, second = weight_pair(weights, 0, features)
+    first, second = taken(held[0])
     for low in range(0, edges, ROWS):
         rows = pl.ds(low, ROWS)
         incoming = dot(enc_g[rows, :], g_edge)
@@ -341,13 +422,13 @@
     mesh_edges = mesh_sender.shape[0]
     slots, halos = grid_send.size, halo_send.size
     capacity, halo_capacity = grid_send.shape[1], halo_send.shape[1]
-    enc_weights, proc_weights = gather_weights(shards)
+    place, sets = gather_weights(shards)
 
     outgoing, grid_t = call(
         send_kernel,
         [shape(slots, features, BF16), shape(grid_rows, slots, BF16)],
         grid_lat,
-        grid_send.reshape(1, slots),
+        grid_send,
     )
     arrived = exchange(outgoing, capacity)
     slot_t, slot_g, enc_t, enc_g, halo_t, halo_g, sender_t, sender_g, proc_t, proc_g, recv_rows = call(
@@ -368,7 +449,7 @@
         mesh_lat,
         g2m_slot.reshape(1, edges),
         g2m_receiver.reshape(1, edges),
-        halo_send.reshape(1, halos),
+        halo_send,
         mesh_sender.reshape(1, mesh_edges),
         mesh_receiver.reshape(1, mesh_edges),
     )
@@ -389,35 +470,45 @@
         recv_rows,
         enc_t,
         halo_g,
-        enc_weights,
+        weights=(place, sets[:2]),
     )
     halo_in = exchange(halo_out, halo_capacity)
-    mesh_two, grad_one, grad_halo = pl.pallas_call(
+    mesh_two, grad_one, grad_halo = call(
         process_kernel,
-        out_shape=[
+        [
             shape(mesh_rows, features, BF16),
             shape(mesh_rows, features, F32),
             shape(halos, features, BF16),
         ],
-        in_specs=[pl.BlockSpec(memory_space=pltpu.VMEM)] * 8,
-        out_specs=[pl.BlockSpec(memory_space=pltpu.VMEM)] * 3,
-        scratch_shapes=[
+        mesh_one,
+        halo_in,
+        cotangent,
+        sender_t,
+        sender_g,
+        proc_t,
+        proc_g,
+        weights=(place, sets[2:]),
+        scratch=[
             pltpu.VMEM((mesh_edges, features), BF16),
             pltpu.VMEM((mesh_edges, features), BF16),
             pltpu.VMEM((mesh_edges, LANES), F32),
             pltpu.VMEM((mesh_edges, features), BF16),
         ],
-        compiler_params=pltpu.CompilerParams(vmem_limit_bytes=40 * 1024 * 1024),
-    )(mesh_one, halo_in, cotangent, sender_t, sender_g, proc_t, proc_g, proc_weights)
+    )
     halo_back = exchange(grad_halo, halo_capacity)
-    mesh_grad, grad_slots = pl.pallas_call(
+    mesh_grad, grad_slots = call(
         decode_kernel,
-        out_shape=[shape(mesh_rows, features, F32), shape(slots, features, BF16)],
-        in_specs=[pl.BlockSpec(memory_space=pltpu.VMEM)] * 13,
-        out_specs=[pl.BlockSpec(memory_space=pltpu.VMEM)] * 2,
-        scratch_shapes=[pltpu.VMEM((edges, features), BF16)],
-        compiler_params=pltpu.CompilerParams(vmem_limit_bytes=40 * 1024 * 1024),
-    )(grad_one, halo_back, halo_t, *kept, enc_t, enc_g, slot_t, enc_weights)
+        [shape(mesh_rows, features, F32), shape(slots, features, BF16)],
+        grad_one,
+        halo_back,
+        halo_t,
+        *kept,
+        enc_t,
+        enc_g,
+        slot_t,
+        weights=(place, sets[:2]),
+        scratch=[pltpu.VMEM((edges, features), BF16)],
+    )
     returned = exchange(grad_slots, capacity)
     (grid_grad,) = call(grid_kernel, [shape(grid_rows, features, F32)], grid_t, returned)
     return (mesh_two, grid_grad, mesh_grad)

time: 195 us -> 164 us (0.84)
  waiting for transfers between devices: 81.3 us -> 12.7 us
  starting transfers between devices: 7.44 us -> 45.5 us
  between operations: 14.2 us -> 1.19 us
  local copies, waits for them, and re-layouts: 39.3 us -> 47.9 us
  Pallas kernels: 20.7 us -> 24.7 us
    all_gather x2 -> x0, waiting for transfers between devices: 80.6 us -> none  [gather_weights(): return (lax.all_gather(enc, AXES), lax.all_gather(proc, AXES))]
    ppermute x0 -> x40, starting transfers between devices: none -> 39.7 us  [the longest x12 22.3 us: gather_weights(): lax.ppermute(piece, 'mp', [(m, (m + s) % 4) for m in range(4)])]
    ppermute x0 -> x40, waiting for transfers between devices: none -> 12.7 us  [the longest x28 9.31 us: across(): lax.ppermute(x, ('groups', 'graph'), [(p, p ^ flip) for p in range(8)])]
    unnamed x86 -> x166, local copies, waits for them, and re-layouts: 36.7 us -> 46.2 us
    pallas_call x7, Pallas kernels: 20.7 us -> 24.7 us  [the longest x6 17.6 us: call(): pl.pallas_call(body, grid=(1,), out_shape=out_shape, in_specs=in_specs, o...]
  transfers between devices with their start and end apart: 3 -> 41, of which waited for: 2 -> 9; matrix products, arithmetic and copies ran while one was open for 2% -> 1% of each run, Pallas kernels for 2% -> 3%
where the time goes in v2:
time: 164 us; the launch traced here: 163 us
  local copies, waits for them, and re-layouts  47.9 us (29%)
  starting transfers between devices  45.5 us (28%)
  blocking collectives  30.7 us (19%)
  Pallas kernels  24.7 us (15%)
  waiting for transfers between devices  12.7 us (8%)
    unnamed x166, local copies, waits for them, and re-layouts  46.2 us
    all_to_all x3, blocking collectives, exchange(): lax.all_to_all(parts, PEERS, split_axis=0, concat_axis=0, tiled=True)  30.7 us
    ppermute x12, starting transfers between devices, gather_weights(): lax.ppermute(piece, 'mp', [(m, (m + s) % 4) for m in range(4)])  22.3 us
    pallas_call x6, Pallas kernels, call(): pl.pallas_call(body, grid=(1,), out_shape=out_shape, in_specs=in_specs, o...  17.6 us
    ppermute x28, starting transfers between devices, across(): lax.ppermute(x, ('groups', 'graph'), [(p, p ^ flip) for p in range(8)])  17.4 us
    ppermute x28, waiting for transfers between devices, across(): lax.ppermute(x, ('groups', 'graph'), [(p, p ^ flip) for p in range(8)])  9.31 us
    pallas_call x1, Pallas kernels, gather_weights(): pl.pallas_call(pack_kernel, out_shape=[shape(192, 128, BF16)] * 4, in_spe...  7.15 us
    all_to_all x1, starting transfers between devices, exchange(): lax.all_to_all(parts, PEERS, split_axis=0, concat_axis=0, tiled=True)  5.8 us
  transfers between devices with their start and end apart: 41, of which 9 were waited for; matrix products, arithmetic and copies ran while one was open for 1% of the time, Pallas kernels for 3%

profile of v2, /device:TPU:0, one launch (start us, length us, event | category | flops | bytes accessed | tf_op | source)
XLA Modules:
  0.0 162.7 jit_solution(1381129592826832464)
XLA Ops:
  0.6 7.1 %pack.1 = (bf16[192,128]{1,0:T(8,128)(2,1)}, bf16[192,128]{1,0:T(8,128)(2,1)}, bf16[192,128]{1,0:T(8,128)(2,1)}, bf16[192,128]{1,0:T(8,128)(2,1)}) custom-call(bf16[1024,128]{1,0:T(8,128)(2,1)} %refs_12_.1, bf16[128,512]{1,0:T(8,128)(2,1)} %refs_13_.1, bf16[1024,128]{1,0:T(8,128)(2,1)} %refs_22_.1, bf16[128,512]{1,0:T(8,128)(2,1)} %refs_23_.1, ...), custom_call_target="tpu_custom_call" | custom-call | tf_op jit(solution)/shard_map/pack/pallas_call | solution.py:163
  7.8 5.1 %collective-permute-start.2 = (bf16[192,128]{1,0:T(8,128)(2,1)}, bf16[192,128]{1,0:T(8,128)(2,1)S(1)}, u32[]{:S(2)}, u32[]{:S(2)}) collective-permute-start(bf16[192,128]{1,0:T(8,128)(2,1)} %get-tuple-element.38), channel_id=1, source_target_pairs={{0,3},{1,0},{2,1},{3,2},{4,7},{5,4},{6,5},{7,6},{8,11},{9,8},{10,9... | collective-permute-start | bytes 147464 | tf_op jit(solution)/shard_map/ppermute | solution.py:177
  13.3 2.5 %collective-permute-start.31 = (bf16[192,128]{1,0:T(8,128)(2,1)}, bf16[192,128]{1,0:T(8,128)(2,1)S(1)}, u32[]{:S(2)}, u32[]{:S(2)}) collective-permute-start(bf16[192,128]{1,0:T(8,128)(2,1)} %get-tuple-element.47), channel_id=1, source_target_pairs={{0,2},{1,3},{2,0},{3,1},{4,6},{5,7},{6,4},{7,5},{8,10},{9,11},{10,... | collective-permute-start | bytes 147464 | tf_op jit(solution)/shard_map/ppermute | solution.py:177
  15.8 2.0 %collective-permute-start.30 = (bf16[192,128]{1,0:T(8,128)(2,1)}, bf16[192,128]{1,0:T(8,128)(2,1)S(1)}, u32[]{:S(2)}, u32[]{:S(2)}) collective-permute-start(bf16[192,128]{1,0:T(8,128)(2,1)} %get-tuple-element.47), channel_id=1, source_target_pairs={{0,1},{1,2},{2,3},{3,0},{4,5},{5,6},{6,7},{7,4},{8,9},{9,10},{10,1... | collective-permute-start | bytes 147464 | tf_op jit(solution)/shard_map/ppermute | solution.py:177
  18.8 3.7 %collective-permute-start.22 = (bf16[192,128]{1,0:T(8,128)(2,1)}, bf16[192,128]{1,0:T(8,128)(2,1)S(1)}, u32[]{:S(2)}, u32[]{:S(2)}) collective-permute-start(bf16[192,128]{1,0:T(8,128)(2,1)} %get-tuple-element.46), channel_id=1, source_target_pairs={{0,3},{1,0},{2,1},{3,2},{4,7},{5,4},{6,5},{7,6},{8,11},{9,8},{10,9... | collective-permute-start | bytes 147464 | tf_op jit(solution)/shard_map/ppermute | solution.py:177
  23.1 3.3 %collective-permute-start.12 = (bf16[192,128]{1,0:T(8,128)(2,1)}, bf16[192,128]{1,0:T(8,128)(2,1)S(1)}, u32[]{:S(2)}, u32[]{:S(2)}) collective-permute-start(bf16[192,128]{1,0:T(8,128)(2,1)} %get-tuple-element.39), channel_id=1, source_target_pairs={{0,3},{1,0},{2,1},{3,2},{4,7},{5,4},{6,5},{7,6},{8,11},{9,8},{10,9... | collective-permute-start | bytes 147464 | tf_op jit(solution)/shard_map/ppermute | solution.py:177
  26.4 2.5 %collective-permute-start.38 = (bf16[3,192,128]{2,1,0:T(8,128)(2,1)S(1)}, bf16[3,192,128]{2,1,0:T(8,128)(2,1)S(1)}, u32[]{:S(2)}, u32[]{:S(2)}) collective-permute-start(bf16[3,192,128]{2,1,0:T(8,128)(2,1)S(1)} %pad_maximum_fusion.3.refs_19_), channel_id=1, source_target_pairs={{0,24},{4,28},{8,16},{12,20},{16,8},{20,12},{24,0},{28,4},{1,25},{... | collective-permute-start | bytes 442376 | tf_op jit(solution)/shard_map/ppermute | solution.py:173
  30.3 1.5 collective-permute-start.34
  33.0 3.4 %collective-permute-start.10 = (bf16[192,128]{1,0:T(8,128)(2,1)S(1)}, bf16[192,128]{1,0:T(8,128)(2,1)S(1)}, u32[]{:S(2)}, u32[]{:S(2)}) collective-permute-start(bf16[192,128]{1,0:T(8,128)(2,1)S(1)} %copy-done.81), channel_id=1, source_target_pairs={{0,1},{1,2},{2,3},{3,0},{4,5},{5,6},{6,7},{7,4},{8,9},{9,10},{10,1... | collective-permute-start | bytes 147464 | tf_op jit(solution)/shard_map/ppermute | solution.py:177
  36.8 2.1 %collective-permute-done.10 = bf16[192,128]{1,0:T(8,128)(2,1)S(1)} collective-permute-done((bf16[192,128]{1,0:T(8,128)(2,1)S(1)}, bf16[192,128]{1,0:T(8,128)(2,1)S(1)}, u32[]{:S(2)}, u32[]{:S(2)}) %collective-permute-start.10) | collective-permute-done | bytes 49184 | tf_op jit(solution)/shard_map/ppermute | solution.py:177
  40.7 1.7 %collective-permute-start.24 = (bf16[3,192,128]{2,1,0:T(8,128)(2,1)S(1)}, bf16[3,192,128]{2,1,0:T(8,128)(2,1)S(1)}, u32[]{:S(2)}, u32[]{:S(2)}) collective-permute-start(bf16[3,192,128]{2,1,0:T(8,128)(2,1)S(1)} %pad_maximum_fusion.2.refs_9_), channel_id=1, source_target_pairs={{0,8},{4,12},{8,0},{12,4},{16,24},{20,28},{24,16},{28,20},{1,9},{5... | collective-permute-start | bytes 442376 | tf_op jit(solution)/shard_map/ppermute | solution.py:173
  43.7 2.1 %collective-permute-done.28.refs_15_ = bf16[3,192,128]{2,1,0:T(8,128)(2,1)} collective-permute-done((bf16[3,192,128]{2,1,0:T(8,128)(2,1)S(1)}, bf16[3,192,128]{2,1,0:T(8,128)(2,1)}, u32[]{:S(2)}, u32[]{:S(2)}) %collective-permute-start.28) | collective-permute-done | bytes 147488 | tf_op jit(solution)/shard_map/ppermute | solution.py:173
  48.6 1.4 collective-permute-start.8
  51.1 1.8 %collective-permute-done.16.refs_22_.refs_28_ = bf16[3,192,128]{2,1,0:T(8,128)(2,1)S(1)} collective-permute-done((bf16[3,192,128]{2,1,0:T(8,128)(2,1)S(1)}, bf16[3,192,128]{2,1,0:T(8,128)(2,1)S(1)}, u32[]{:S(2)}, u32[]{:S(2)}) %collective-permute-start.16) | collective-permute-done | bytes 147488 | tf_op jit(solution)/shard_map/ppermute | solution.py:173
  52.9 1.7 %collective-permute-start.4 = (bf16[3,192,128]{2,1,0:T(8,128)(2,1)S(1)}, bf16[3,192,128]{2,1,0:T(8,128)(2,1)S(1)}, u32[]{:S(2)}, u32[]{:S(2)}) collective-permute-start(bf16[3,192,128]{2,1,0:T(8,128)(2,1)S(1)} %pad_maximum_fusion.refs_8_.refs_14_), channel_id=1, source_target_pairs={{0,8},{4,12},{8,0},{12,4},{16,24},{20,28},{24,16},{28,20},{1,9},{5... | collective-permute-start | bytes 442376 | tf_op jit(solution)/shard_map/ppermute | solution.py:173
  55.1 1.8 %collective-permute-done.8.refs_14_.refs_20_ = bf16[3,192,128]{2,1,0:T(8,128)(2,1)S(1)} collective-permute-done((bf16[3,192,128]{2,1,0:T(8,128)(2,1)S(1)}, bf16[3,192,128]{2,1,0:T(8,128)(2,1)S(1)}, u32[]{:S(2)}, u32[]{:S(2)}) %collective-permute-start.8) | collective-permute-done | bytes 147488 | tf_op jit(solution)/shard_map/ppermute | solution.py:173
  57.0 2.3 %collective-permute-done.6.refs_12_.refs_18_ = bf16[3,192,128]{2,1,0:T(8,128)(2,1)S(1)} collective-permute-done((bf16[3,192,128]{2,1,0:T(8,128)(2,1)S(1)}, bf16[3,192,128]{2,1,0:T(8,128)(2,1)S(1)}, u32[]{:S(2)}, u32[]{:S(2)}) %collective-permute-start.6) | collective-permute-done | bytes 147488 | tf_op jit(solution)/shard_map/ppermute | solution.py:173
  62.8 5.8 %all-to-all-start = ((bf16[16,4,512]{2,1,0:T(4,128)(2,1)}), bf16[16,4,512]{2,1,0:T(4,128)(2,1)}, u32[]{:S(2)}, u32[]{:S(2)}) async-start(bf16[16,4,512]{2,1,0:T(4,128)(2,1)} %reshape.42), calls=%async_computation | async-start | bytes 131072 | tf_op jit(solution)/shard_map/all_to_all | solution.py:404
  85.6 4.2 %encode_kernel.1 = (bf16[256,512]{1,0:T(8,128)(2,1)S(1)}, bf16[32,512]{1,0:T(8,128)(2,1)S(1)}, bf16[512,512]{1,0:T(8,128)(2,1)S(1)}, bf16[512,512]{1,0:T(8,128)(...) custom-call(bf16[256,512]{1,0:T(8,128)(2,1)S(1)} %copy-done.4, ...), custom_call_target="tpu_custom_call" | custom-call | tf_op jit(solution)/shard_map/encode_kernel/pallas_call | solution.py:59
  94.9 12.2 %all_to_all.20 = bf16[16,2,512]{2,1,0:T(2,128)(2,1)S(1)} all-to-all(bf16[16,2,512]{2,1,0:T(2,128)(2,1)S(1)} %reshape.48), channel_id=1, replica_groups=mesh['groups'=2,'graph'=4,'mp'=4] {'graph','mp'}, dimensions={0} | all-to-all | bytes 65536 | tf_op jit(solution)/shard_map/all_to_all | solution.py:404
  120.2 6.8 %process_kernel.1 = (bf16[256,512]{1,0:T(8,128)(2,1)}, f32[256,512]{1,0:T(8,128)S(1)}, bf16[32,512]{1,0:T(8,128)(2,1)S(1)}) custom-call(bf16[256,512]{1,0:T(8,128)(2,1)S(1)} %copy-done.52, bf16[32,512]{1,0:T(8,128)(2,1)S(1)} %reshape.49.refs_1_, bf16[256,512]{1,0:T(8,128)(2,1)S(1)} %copy-done.38, bf16[288,512]{1,0:T(8,128)(2,1)S(1)} %copy-done.37, ...), custom_call_target="tpu_custom_call" | custom-call | tf_op jit(solution)/shard_map/process_kernel/pallas_call | solution.py:59
  127.8 9.2 %all_to_all.21 = bf16[16,2,512]{2,1,0:T(2,128)(2,1)S(1)} all-to-all(bf16[16,2,512]{2,1,0:T(2,128)(2,1)S(1)} %reshape.50), channel_id=1, replica_groups=mesh['groups'=2,'graph'=4,'mp'=4] {'graph','mp'}, dimensions={0} | all-to-all | bytes 65536 | tf_op jit(solution)/shard_map/all_to_all | solution.py:404
  147.6 4.5 %decode_kernel.1 = (f32[256,512]{1,0:T(8,128)}, bf16[64,512]{1,0:T(8,128)(2,1)S(1)}) custom-call(f32[256,512]{1,0:T(8,128)S(1)} %copy-done.28, bf16[32,512]{1,0:T(8,128)(2,1)S(1)} %reshape.51.refs_1_, bf16[256,32]{1,0:T(8,128)(2,1)S(1)} %copy-done.72, bf16[512,512]{1,0:T(8,128)(2,1)S(1)} %copy-done.24, bf16[512,512]{1,0:T(8,128)(2,1)S(1)} %copy-done.26, ...), custom_call_target="tpu_custom_call" | custom-call | tf_op jit(solution)/shard_map/decode_kernel/pallas_call | solution.py:59
  152.1 9.3 %all_to_all.22 = bf16[16,4,512]{2,1,0:T(4,128)(2,1)S(1)} all-to-all(bf16[16,4,512]{2,1,0:T(4,128)(2,1)S(1)} %reshape.52), channel_id=1, replica_groups=mesh['groups'=2,'graph'=4,'mp'=4] {'graph','mp'}, dimensions={0} | all-to-all | bytes 131072 | tf_op jit(solution)/shard_map/all_to_all | solution.py:404
  (246 shorter events, 63.4 us)
Async XLA Ops:
  7.8 10.1 %collective-permute-start.2 = (bf16[192,128]{1,0:T(8,128)(2,1)}, bf16[192,128]{1,0:T(8,128)(2,1)S(1)}, u32[]{:S(2)}, u32[]{:S(2)}) collective-permute-start(bf16[192,128]{1,0:T(8,128)(2,1)} %get-tuple-element.38), channel_id=1, source_target_pairs={{0,3},{1,0},{2,1},{3,2},{4,7},{5,4},{6,5},{7,6},{8,11},{9,8},{10,9... | collective-permute-start | bytes 147464 | tf_op jit(solution)/shard_map/ppermute | solution.py:177
  12.9 9.6 %collective-permute-start.32 = (bf16[192,128]{1,0:T(8,128)(2,1)}, bf16[192,128]{1,0:T(8,128)(2,1)S(1)}, u32[]{:S(2)}, u32[]{:S(2)}) collective-permute-start(bf16[192,128]{1,0:T(8,128)(2,1)} %get-tuple-element.47), channel_id=1, source_target_pairs={{0,3},{1,0},{2,1},{3,2},{4,7},{5,4},{6,5},{7,6},{8,11},{9,8},{10,9... | collective-permute-start | bytes 147464 | tf_op jit(solution)/shard_map/ppermute | solution.py:177
  13.3 9.2 %collective-permute-start.31 = (bf16[192,128]{1,0:T(8,128)(2,1)}, bf16[192,128]{1,0:T(8,128)(2,1)S(1)}, u32[]{:S(2)}, u32[]{:S(2)}) collective-permute-start(bf16[192,128]{1,0:T(8,128)(2,1)} %get-tuple-element.47), channel_id=1, source_target_pairs={{0,2},{1,3},{2,0},{3,1},{4,6},{5,7},{6,4},{7,5},{8,10},{9,11},{10,... | collective-permute-start | bytes 147464 | tf_op jit(solution)/shard_map/ppermute | solution.py:177
  17.8 8.6 %collective-permute-start = (bf16[192,128]{1,0:T(8,128)(2,1)}, bf16[192,128]{1,0:T(8,128)(2,1)S(1)}, u32[]{:S(2)}, u32[]{:S(2)}) collective-permute-start(bf16[192,128]{1,0:T(8,128)(2,1)} %get-tuple-element.38), channel_id=1, source_target_pairs={{0,1},{1,2},{2,3},{3,0},{4,5},{5,6},{6,7},{7,4},{8,9},{9,10},{10,1... | collective-permute-start | bytes 147464 | tf_op jit(solution)/shard_map/ppermute | solution.py:177
  18.8 11.5 %collective-permute-start.22 = (bf16[192,128]{1,0:T(8,128)(2,1)}, bf16[192,128]{1,0:T(8,128)(2,1)S(1)}, u32[]{:S(2)}, u32[]{:S(2)}) collective-permute-start(bf16[192,128]{1,0:T(8,128)(2,1)} %get-tuple-element.46), channel_id=1, source_target_pairs={{0,3},{1,0},{2,1},{3,2},{4,7},{5,4},{6,5},{7,6},{8,11},{9,8},{10,9... | collective-permute-start | bytes 147464 | tf_op jit(solution)/shard_map/ppermute | solution.py:177
  22.5 9.3 %collective-permute-start.21 = (bf16[192,128]{1,0:T(8,128)(2,1)}, bf16[192,128]{1,0:T(8,128)(2,1)S(1)}, u32[]{:S(2)}, u32[]{:S(2)}) collective-permute-start(bf16[192,128]{1,0:T(8,128)(2,1)} %get-tuple-element.46), channel_id=1, source_target_pairs={{0,2},{1,3},{2,0},{3,1},{4,6},{5,7},{6,4},{7,5},{8,10},{9,11},{10,... | collective-permute-start | bytes 147464 | tf_op jit(solution)/shard_map/ppermute | solution.py:177
  22.5 10.5 %collective-permute-start.20 = (bf16[192,128]{1,0:T(8,128)(2,1)}, bf16[192,128]{1,0:T(8,128)(2,1)S(1)}, u32[]{:S(2)}, u32[]{:S(2)}) collective-permute-start(bf16[192,128]{1,0:T(8,128)(2,1)} %get-tuple-element.46), channel_id=1, source_target_pairs={{0,1},{1,2},{2,3},{3,0},{4,5},{5,6},{6,7},{7,4},{8,9},{9,10},{10,1... | collective-permute-start | bytes 147464 | tf_op jit(solution)/shard_map/ppermute | solution.py:177
  26.4 13.0 %collective-permute-start.38 = (bf16[3,192,128]{2,1,0:T(8,128)(2,1)S(1)}, bf16[3,192,128]{2,1,0:T(8,128)(2,1)S(1)}, u32[]{:S(2)}, u32[]{:S(2)}) collective-permute-start(bf16[3,192,128]{2,1,0:T(8,128)(2,1)S(1)} %pad_maximum_fusion.3.refs_19_), channel_id=1, source_target_pairs={{0,24},{4,28},{8,16},{12,20},{16,8},{20,12},{24,0},{28,4},{1,25},{... | collective-permute-start | bytes 442376 | tf_op jit(solution)/shard_map/ppermute | solution.py:173
  29.0 11.8 %collective-permute-start.36 = (bf16[3,192,128]{2,1,0:T(8,128)(2,1)S(1)}, bf16[3,192,128]{2,1,0:T(8,128)(2,1)}, u32[]{:S(2)}, u32[]{:S(2)}) collective-permute-start(bf16[3,192,128]{2,1,0:T(8,128)(2,1)S(1)} %pad_maximum_fusion.3.refs_19_), channel_id=1, source_target_pairs={{0,16},{4,20},{8,24},{12,28},{16,0},{20,4},{24,8},{28,12},{1,17},{... | collective-permute-start | bytes 442376 | tf_op jit(solution)/shard_map/ppermute | solution.py:173
  30.3 12.1 %collective-permute-start.34 = (bf16[3,192,128]{2,1,0:T(8,128)(2,1)S(1)}, bf16[3,192,128]{2,1,0:T(8,128)(2,1)}, u32[]{:S(2)}, u32[]{:S(2)}) collective-permute-start(bf16[3,192,128]{2,1,0:T(8,128)(2,1)S(1)} %pad_maximum_fusion.3.refs_19_), channel_id=1, source_target_pairs={{0,8},{4,12},{8,0},{12,4},{16,24},{20,28},{24,16},{28,20},{1,9},{5... | collective-permute-start | bytes 442376 | tf_op jit(solution)/shard_map/ppermute | solution.py:173
  46.8 7.9 %collective-permute-start.14 = (bf16[3,192,128]{2,1,0:T(8,128)(2,1)S(1)}, bf16[3,192,128]{2,1,0:T(8,128)(2,1)S(1)}, u32[]{:S(2)}, u32[]{:S(2)}) collective-permute-start(bf16[3,192,128]{2,1,0:T(8,128)(2,1)S(1)} %pad_maximum_fusion.1.refs_18_.refs_24_), channel_id=1, source_target_pairs={{0,8},{4,12},{8,0},{12,4},{16,24},{20,28},{24,16},{28,20},{1,9},{5... | collective-permute-start | bytes 442376 | tf_op jit(solution)/shard_map/ppermute | solution.py:173
  48.6 8.3 %collective-permute-start.8 = (bf16[3,192,128]{2,1,0:T(8,128)(2,1)S(1)}, bf16[3,192,128]{2,1,0:T(8,128)(2,1)S(1)}, u32[]{:S(2)}, u32[]{:S(2)}) collective-permute-start(bf16[3,192,128]{2,1,0:T(8,128)(2,1)S(1)} %pad_maximum_fusion.refs_8_.refs_14_), channel_id=1, source_target_pairs={{0,24},{4,28},{8,16},{12,20},{16,8},{20,12},{24,0},{28,4},{1,25},{... | collective-permute-start | bytes 442376 | tf_op jit(solution)/shard_map/ppermute | solution.py:173
  50.8 8.5 %collective-permute-start.6 = (bf16[3,192,128]{2,1,0:T(8,128)(2,1)S(1)}, bf16[3,192,128]{2,1,0:T(8,128)(2,1)S(1)}, u32[]{:S(2)}, u32[]{:S(2)}) collective-permute-start(bf16[3,192,128]{2,1,0:T(8,128)(2,1)S(1)} %pad_maximum_fusion.refs_8_.refs_14_), channel_id=1, source_target_pairs={{0,16},{4,20},{8,24},{12,28},{16,0},{20,4},{24,8},{28,12},{1,17},{... | collective-permute-start | bytes 442376 | tf_op jit(solution)/shard_map/ppermute | solution.py:173
  59.2 9.4 %collective-permute-start.17 = (bf16[3,192,128]{2,1,0:T(8,128)(2,1)S(1)}, bf16[3,192,128]{2,1,0:T(8,128)(2,1)S(1)}, u32[]{:S(2)}, u32[]{:S(2)}) collective-permute-start(bf16[3,192,128]{2,1,0:T(8,128)(2,1)S(1)} %collective-permute-done.16.refs_22_.refs_28_), channel_id=1, source_target_pairs={{0,4},{4,0},{8,12},{12,8},{16,20},{20,16},{24,28},{28,24},{1,5},{5... | collective-permute-start | bytes 442376 | tf_op jit(solution)/shard_map/ppermute | solution.py:173
  59.2 10.4 %collective-permute-start.15 = (bf16[3,192,128]{2,1,0:T(8,128)(2,1)S(1)}, bf16[3,192,128]{2,1,0:T(8,128)(2,1)S(1)}, u32[]{:S(2)}, u32[]{:S(2)}) collective-permute-start(bf16[3,192,128]{2,1,0:T(8,128)(2,1)S(1)} %collective-permute-done.14.refs_20_.refs_26_), channel_id=1, source_target_pairs={{0,4},{4,0},{8,12},{12,8},{16,20},{20,16},{24,28},{28,24},{1,5},{5... | collective-permute-start | bytes 442376 | tf_op jit(solution)/shard_map/ppermute | solution.py:173
  59.8 10.0 %collective-permute-start.9 = (bf16[3,192,128]{2,1,0:T(8,128)(2,1)S(1)}, bf16[3,192,128]{2,1,0:T(8,128)(2,1)S(1)}, u32[]{:S(2)}, u32[]{:S(2)}) collective-permute-start(bf16[3,192,128]{2,1,0:T(8,128)(2,1)S(1)} %collective-permute-done.8.refs_14_.refs_20_), channel_id=1, source_target_pairs={{0,4},{4,0},{8,12},{12,8},{16,20},{20,16},{24,28},{28,24},{1,5},{5... | collective-permute-start | bytes 442376 | tf_op jit(solution)/shard_map/ppermute | solution.py:173
  60.5 9.7 %collective-permute-start.7 = (bf16[3,192,128]{2,1,0:T(8,128)(2,1)S(1)}, bf16[3,192,128]{2,1,0:T(8,128)(2,1)S(1)}, u32[]{:S(2)}, u32[]{:S(2)}) collective-permute-start(bf16[3,192,128]{2,1,0:T(8,128)(2,1)S(1)} %collective-permute-done.6.refs_12_.refs_18_), channel_id=1, source_target_pairs={{0,4},{4,0},{8,12},{12,8},{16,20},{20,16},{24,28},{28,24},{1,5},{5... | collective-permute-start | bytes 442376 | tf_op jit(solution)/shard_map/ppermute | solution.py:173
  60.9 10.1 %collective-permute-start.5 = (bf16[3,192,128]{2,1,0:T(8,128)(2,1)S(1)}, bf16[3,192,128]{2,1,0:T(8,128)(2,1)}, u32[]{:S(2)}, u32[]{:S(2)}) collective-permute-start(bf16[3,192,128]{2,1,0:T(8,128)(2,1)S(1)} %collective-permute-done.4.refs_10_.refs_16_), channel_id=1, source_target_pairs={{0,4},{4,0},{8,12},{12,8},{16,20},{20,16},{24,28},{28,24},{1,5},{5... | collective-permute-start | bytes 442376 | tf_op jit(solution)/shard_map/ppermute | solution.py:173
  62.8 15.5 %all-to-all-start = ((bf16[16,4,512]{2,1,0:T(4,128)(2,1)}), bf16[16,4,512]{2,1,0:T(4,128)(2,1)}, u32[]{:S(2)}, u32[]{:S(2)}) async-start(bf16[16,4,512]{2,1,0:T(4,128)(2,1)} %reshape.42), calls=%async_computation | async-start | bytes 131072 | tf_op jit(solution)/shard_map/all_to_all | solution.py:404
  69.3 37.8 %collective-permute-start.37 = (bf16[3,192,128]{2,1,0:T(8,128)(2,1)}, bf16[3,192,128]{2,1,0:T(8,128)(2,1)}, u32[]{:S(2)}, u32[]{:S(2)}) collective-permute-start(bf16[3,192,128]{2,1,0:T(8,128)(2,1)} %collective-permute-done.36.refs_23_), channel_id=1, source_target_pairs={{0,4},{4,0},{8,12},{12,8},{16,20},{20,16},{24,28},{28,24},{1,5},{5... | collective-permute-start | bytes 442376 | tf_op jit(solution)/shard_map/ppermute | solution.py:173
  69.7 37.4 %collective-permute-start.35 = (bf16[3,192,128]{2,1,0:T(8,128)(2,1)}, bf16[3,192,128]{2,1,0:T(8,128)(2,1)}, u32[]{:S(2)}, u32[]{:S(2)}) collective-permute-start(bf16[3,192,128]{2,1,0:T(8,128)(2,1)} %collective-permute-done.34.refs_21_), channel_id=1, source_target_pairs={{0,4},{4,0},{8,12},{12,8},{16,20},{20,16},{24,28},{28,24},{1,5},{5... | collective-permute-start | bytes 442376 | tf_op jit(solution)/shard_map/ppermute | solution.py:173
  69.8 37.3 %collective-permute-start.29 = (bf16[3,192,128]{2,1,0:T(8,128)(2,1)}, bf16[3,192,128]{2,1,0:T(8,128)(2,1)}, u32[]{:S(2)}, u32[]{:S(2)}) collective-permute-start(bf16[3,192,128]{2,1,0:T(8,128)(2,1)} %collective-permute-done.28.refs_15_), channel_id=1, source_target_pairs={{0,4},{4,0},{8,12},{12,8},{16,20},{20,16},{24,28},{28,24},{1,5},{5... | collective-permute-start | bytes 442376 | tf_op jit(solution)/shard_map/ppermute | solution.py:173
  70.8 36.3 %collective-permute-start.27 = (bf16[3,192,128]{2,1,0:T(8,128)(2,1)}, bf16[3,192,128]{2,1,0:T(8,128)(2,1)}, u32[]{:S(2)}, u32[]{:S(2)}) collective-permute-start(bf16[3,192,128]{2,1,0:T(8,128)(2,1)} %collective-permute-done.26.refs_13_), channel_id=1, source_target_pairs={{0,4},{4,0},{8,12},{12,8},{16,20},{20,16},{24,28},{28,24},{1,5},{5... | collective-permute-start | bytes 442376 | tf_op jit(solution)/shard_map/ppermute | solution.py:173
  71.0 36.1 %collective-permute-start.25 = (bf16[3,192,128]{2,1,0:T(8,128)(2,1)}, bf16[3,192,128]{2,1,0:T(8,128)(2,1)}, u32[]{:S(2)}, u32[]{:S(2)}) collective-permute-start(bf16[3,192,128]{2,1,0:T(8,128)(2,1)} %copy-done.57), channel_id=1, source_target_pairs={{0,4},{4,0},{8,12},{12,8},{16,20},{20,16},{24,28},{28,24},{1,5},{5... | collective-permute-start | bytes 442376 | tf_op jit(solution)/shard_map/ppermute | solution.py:173
  (99 other events, 480.6 us)

commit v3 on v2

v3 whole, which is shorter than its diff:
```python
import functools

import jax
import jax.numpy as jnp
from jax import lax
from jax.experimental import pallas as pl
from jax.experimental.pallas import tpu as pltpu
from jax.sharding import PartitionSpec as P

F32 = jnp.float32
BF16 = jnp.bfloat16
LANES = 128
ROWS = 256
FEATURES = 512
AXES = ("groups", "graph", "mp")
PEERS = ("graph", "mp")


def dot(left, right):
    return jnp.dot(left, right, preferred_element_type=F32)


def dot_trans(left, right):
    return lax.dot_general(left, right, (((1,), (1,)), ((), ())), preferred_element_type=F32)


def shape(rows, columns, dtype):
    return pltpu.HBM((rows, columns), dtype)


def origin(rank, step):
    return (0,) * rank


def call(kernel, out_shape, *args, weights=(), scratch=()):
    scratch = list(scratch)
    in_specs = [pl.BlockSpec(a.shape, functools.partial(origin, a.ndim)) for a in args]
    in_specs += [pl.BlockSpec(memory_space=pl.ANY)] * len(weights)
    if weights:
        scratch.append(pltpu.VMEM((FEATURES, weights[0].shape[1]), BF16))
        scratch.append(pltpu.SemaphoreType.DMA)

    def body(*refs):
        if not weights:
            return kernel(*refs)
        ins, refs = refs[: len(args)], refs[len(args) :]
        sources, refs = refs[: len(weights)], refs[len(weights) :]
        held, sem = refs[-2:]
        low = 0
        for source in sources:
            rows = source.shape[0]
            pltpu.make_async_copy(source, held.at[pl.ds(low, rows), :], sem).start()
            low += rows
        kernel((held, sem), *ins, *refs[:-2])

    operands = [pltpu.with_memory_space_constraint(a, pltpu.HBM) for a in args] + list(weights)
    return pl.pallas_call(
        body,
        grid=(1,),
        out_shape=out_shape,
        in_specs=in_specs,
        out_specs=[pl.BlockSpec(s.shape, functools.partial(origin, len(s.shape))) for s in out_shape],
        scratch_shapes=scratch,
        name=kernel.__name__,
        compiler_params=pltpu.CompilerParams(vmem_limit_bytes=40 * 1024 * 1024),
    )(*operands)


def wait_weights(weights):
    held, sem = weights
    pltpu.make_async_copy(held, held, sem).wait()


def layers(weights, which):
    low = which * 3 * FEATURES
    held = weights[0]
    return (
        held[:, low : low + 2 * FEATURES],
        held[:, low + 2 * FEATURES : low + 3 * FEATURES],
    )


def prepare_kernel(*refs):
    shards, refs = refs[:8], refs[8:]
    grid_ref, send_ref, enc_own, proc_own, enc_piece, proc_piece, outgoing_ref, table_ref = refs
    plane = lax.axis_index("groups") * lax.axis_size("graph") + lax.axis_index("graph")
    for i in range(4):
        own, low = (enc_own, proc_own)[i // 2], i % 2 * 3 * FEATURES
        own[:, low : low + 2 * FEATURES] = shards[2 * i][...].astype(F32).T.astype(BF16)
        own[:, low + 2 * FEATURES : low + 3 * FEATURES] = shards[2 * i + 1][...]
    rows = enc_piece.shape[0]
    low = pl.multiple_of(plane * rows, rows)
    enc_piece[...] = enc_own[pl.ds(low, rows), :]
    proc_piece[...] = proc_own[pl.ds(low, rows), :]
    send_kernel(grid_ref, send_ref, outgoing_ref, table_ref)


def across(x, flip):
    planes = lax.axis_size("groups") * lax.axis_size("graph")
    return lax.ppermute(x, ("groups", "graph"), [(p, p ^ flip) for p in range(planes)])


def spread_along(piece):
    size = lax.axis_size("mp")
    return jnp.concatenate(
        [lax.ppermute(piece, "mp", [(m, (m + s) % size) for m in range(size)]) for s in range(1, size)]
    )


def spread_plane(own, first, second):
    blocks = [own, first, second]
    for flip in (2, 4, 6):
        block = across(first, flip)
        blocks += [block, across(block, 1)]
    return blocks


def start(grid_lat, grid_send, shards):
    grid_rows, features = grid_lat.shape
    slots, capacity = grid_send.size, grid_send.shape[1]
    sent = [shape(slots, features, BF16), shape(grid_rows, slots, BF16)]
    planes = lax.axis_size("groups") * lax.axis_size("graph")
    hidden = shards[1].shape[0]
    if planes != 8 or lax.axis_size("mp") != 4 or hidden != 128 or features != FEATURES:
        outgoing, grid_t = call(send_kernel, sent, grid_lat, grid_send)
        rows = []
        for i in range(4):
            rows.append(lax.all_gather(shards[2 * i], "mp", axis=1, tiled=True).T)
            rows.append(lax.all_gather(shards[2 * i + 1], "mp", axis=0, tiled=True))
        sets = [[jnp.concatenate(rows[:4], axis=1)], [jnp.concatenate(rows[4:], axis=1)]]
        return sets[0], sets[1], exchange(outgoing, capacity), grid_t
    enc_own, proc_own, enc_piece, proc_piece, outgoing, grid_t = call(
        prepare_kernel,
        [shape(hidden, 6 * features, BF16)] * 2
        + [shape(hidden // planes, 6 * features, BF16)] * 2
        + sent,
        *shards,
        grid_lat,
        grid_send,
    )
    first = spread_along(enc_piece)
    second = across(first, 1)
    outgoing, proc_piece, second = lax.optimization_barrier((outgoing, proc_piece, second))
    enc = spread_plane(enc_own, first, second)
    arrived = exchange(outgoing, capacity)
    first = spread_along(proc_piece)
    proc = spread_plane(proc_own, first, across(first, 1))
    return enc, proc, arrived, grid_t


def forward(inputs, first, second):
    before = dot_trans(inputs, first)
    logistic = jax.nn.sigmoid(before)
    hidden = (before * logistic).astype(BF16)
    slope = logistic * (1.0 + before * (1.0 - logistic))
    summed = dot(hidden, second)
    centered = summed - jnp.mean(summed, axis=-1, keepdims=True)
    rescale = lax.rsqrt(jnp.mean(centered * centered, axis=-1, keepdims=True) + 1e-05)
    normed = centered * rescale
    return normed, slope.astype(BF16), normed.astype(BF16), rescale


def backward_hidden(incoming, slope, normed, rescale, second):
    normed = normed.astype(F32)
    g_out = (
        incoming
        - jnp.mean(incoming, axis=-1, keepdims=True)
        - normed * jnp.mean(incoming * normed, axis=-1, keepdims=True)
    ) * rescale
    return (dot_trans(g_out.astype(BF16), second) * slope.astype(F32)).astype(BF16)


def table(index_row, count):
    n = index_row.shape[1]
    return jnp.where(lax.broadcasted_iota(jnp.int32, (count, n), 0) == index_row, 1.0, 0.0)


def flat_row(index):
    count, width = index.shape
    at = lax.broadcasted_iota(jnp.int32, (count, count * width), 1)
    row = lax.broadcasted_iota(jnp.int32, (count, count * width), 0)
    spread = jnp.zeros_like(at)
    for c in range(width):
        spread = jnp.where(at % width == c, index[:, c : c + 1], spread)
    return jnp.sum(jnp.where(at // width == row, spread, 0), axis=0, keepdims=True)


def send_kernel(grid_ref, send_ref, outgoing_ref, table_ref):
    one = table(flat_row(send_ref[...]), grid_ref.shape[0])
    table_ref[...] = one.astype(BF16)
    outgoing_ref[...] = dot(one.T.astype(BF16), grid_ref[...]).astype(BF16)


def tables_kernel(
    mesh_ref,
    slot_ref,
    recv_e_ref,
    halo_ref,
    sender_ref,
    recv_p_ref,
    slot_t,
    slot_g,
    enc_t,
    enc_g,
    halo_t,
    halo_g,
    sender_t,
    sender_g,
    proc_t,
    proc_g,
    recv_rows,
):
    for index, scatter, gather in (
        (slot_ref, slot_t, slot_g),
        (recv_e_ref, enc_t, enc_g),
        (halo_ref, halo_t, halo_g),
        (sender_ref, sender_t, sender_g),
        (recv_p_ref, proc_t, proc_g),
    ):
        row = flat_row(index[...]) if index is halo_ref else index[...]
        one = table(row, scatter.shape[0])
        scatter[...] = one.astype(BF16)
        gather[...] = one.T.astype(BF16)
    recv_rows[...] = dot(enc_g[...], mesh_ref[...]).astype(BF16)


def encode_kernel(
    weights,
    mesh_ref,
    arrived_ref,
    slot_g,
    recv_rows,
    enc_t,
    halo_g,
    one_ref,
    halo_ref,
    slope_e,
    normed_e,
    scale_e,
    slope_n,
    normed_n,
    scale_n,
):
    edges = slot_g.shape[0]
    wait_weights(weights)
    first, second = layers(weights, 0)
    for low in range(0, edges, ROWS):
        rows = pl.ds(low, ROWS)
        sent = dot(slot_g[rows, :], arrived_ref[...]).astype(BF16)
        inputs = jnp.concatenate([sent, recv_rows[rows, :]], axis=1)
        _, slope, normed, rescale = forward(inputs, first, second)
        slope_e[rows, :] = slope
        normed_e[rows, :] = normed
        scale_e[rows, :] = jnp.broadcast_to(rescale, (ROWS, LANES))
    aggregate = dot(enc_t[...], normed_e[...]).astype(BF16)
    first, second = layers(weights, 1)
    mesh = mesh_ref[...]
    normed, slope, rounded, rescale = forward(
        jnp.concatenate([mesh, aggregate], axis=1), first, second
    )
    slope_n[...] = slope
    normed_n[...] = rounded
    scale_n[...] = jnp.broadcast_to(rescale, scale_n.shape)
    one_ref[...] = (mesh.astype(F32) + normed).astype(BF16)
    halo_ref[...] = dot(halo_g[...], one_ref[...]).astype(BF16)


def process_kernel(
    weights,
    one_ref,
    halo_ref,
    cotangent_ref,
    sender_t,
    sender_g,
    proc_t,
    proc_g,
    two_ref,
    grad_one_ref,
    grad_halo_ref,
    slope_p,
    normed_p,
    scale_p,
    ga_p,
):
    features = one_ref.shape[1]
    mesh_rows = one_ref.shape[0]
    edges = sender_g.shape[0]
    wait_weights(weights)
    first, second = layers(weights, 0)
    lookup = jnp.concatenate([one_ref[...], halo_ref[...]], axis=0)
    for low in range(0, edges, ROWS):
        rows = pl.ds(low, ROWS)
        sent = dot(sender_g[rows, :], lookup).astype(BF16)
        got = dot(proc_g[rows, :], one_ref[...]).astype(BF16)
        _, slope, normed, rescale = forward(jnp.concatenate([sent, got], axis=1), first, second)
        slope_p[rows, :] = slope
        normed_p[rows, :] = normed
        scale_p[rows, :] = jnp.broadcast_to(rescale, (ROWS, LANES))
    aggregate = dot(proc_t[...], normed_p[...]).astype(BF16)
    first_n, second_n = layers(weights, 1)
    one = one_ref[...]
    normed, slope, rounded, rescale = forward(
        jnp.concatenate([one, aggregate], axis=1), first_n, second_n
    )
    two_ref[...] = (one.astype(F32) + normed).astype(BF16)
    cotangent = cotangent_ref[...].astype(F32)
    ga = backward_hidden(cotangent, slope, rounded, rescale, second_n)
    g_q = dot(ga, first_n)
    g_msg = g_q[:, features:].astype(BF16)
    for low in range(0, edges, ROWS):
        rows = pl.ds(low, ROWS)
        incoming = dot(proc_g[rows, :], g_msg)
        ga_p[rows, :] = backward_hidden(
            incoming, slope_p[rows, :], normed_p[rows, :], scale_p[rows, 0:1], second
        )
    by_recv = dot(proc_t[...], ga_p[...]).astype(BF16)
    by_send = dot(sender_t[...], ga_p[...]).astype(BF16)
    g_send = dot(by_send, first[:, :features])
    g_recv = dot(by_recv, first[:, features:])
    grad_one_ref[...] = cotangent + g_q[:, :features] + g_recv + g_send[:mesh_rows, :]
    grad_halo_ref[...] = g_send[mesh_rows:, :].astype(BF16)


def decode_kernel(
    weights,
    grad_one_ref,
    back_ref,
    halo_t,
    slope_e,
    normed_e,
    scale_e,
    slope_n,
    normed_n,
    scale_n,
    enc_t,
    enc_g,
    slot_t,
    mesh_grad_ref,
    grad_slots_ref,
    ga_e,
):
    features = grad_one_ref.shape[1]
    edges = enc_g.shape[0]
    grad_one = grad_one_ref[...] + dot(halo_t[...], back_ref[...])
    wait_weights(weights)
    first_n, second_n = layers(weights, 1)
    ga = backward_hidden(grad_one, slope_n[...], normed_n[...], scale_n[:, 0:1], second_n)
    g_n = dot(ga, first_n)
    g_edge = g_n[:, features:].astype(BF16)
    first, second = layers(weights, 0)
    for low in range(0, edges, ROWS):
        rows = pl.ds(low, ROWS)
        incoming = dot(enc_g[rows, :], g_edge)
        ga_e[rows, :] = backward_hidden(
            incoming, slope_e[rows, :], normed_e[rows, :], scale_e[rows, 0:1], second
        )
    by_recv = dot(enc_t[...], ga_e[...]).astype(BF16)
    by_slot = dot(slot_t[...], ga_e[...]).astype(BF16)
    mesh_grad_ref[...] = grad_one + g_n[:, :features] + dot(by_recv, first[:, features:])
    grad_slots_ref[...] = dot(by_slot, first[:, :features]).astype(BF16)


def grid_kernel(table_ref, back_ref, out_ref):
    out_ref[...] = dot(table_ref[...], back_ref[...])


def exchange(rows, capacity):
    features = rows.shape[1]
    parts = rows.reshape(-1, capacity, features)
    return lax.all_to_all(parts, PEERS, split_axis=0, concat_axis=0, tiled=True).reshape(rows.shape)


def local(
    grid_lat,
    mesh_lat,
    cotangent,
    grid_send,
    g2m_slot,
    g2m_receiver,
    halo_send,
    mesh_sender,
    mesh_receiver,
    *shards,
):
    grid_rows, features = grid_lat.shape
    mesh_rows = mesh_lat.shape[0]
    edges = g2m_slot.shape[0]
    mesh_edges = mesh_sender.shape[0]
    slots, halos = grid_send.size, halo_send.size
    capacity, halo_capacity = grid_send.shape[1], halo_send.shape[1]
    enc, proc, arrived, grid_t = start(grid_lat, grid_send, shards)
    slot_t, slot_g, enc_t, enc_g, halo_t, halo_g, sender_t, sender_g, proc_t, proc_g, recv_rows = call(
        tables_kernel,
        [
            shape(slots, edges, BF16),
            shape(edges, slots, BF16),
            shape(mesh_rows, edges, BF16),
            shape(edges, mesh_rows, BF16),
            shape(mesh_rows, halos, BF16),
            shape(halos, mesh_rows, BF16),
            shape(mesh_rows + halos, mesh_edges, BF16),
            shape(mesh_edges, mesh_rows + halos, BF16),
            shape(mesh_rows, mesh_edges, BF16),
            shape(mesh_edges, mesh_rows, BF16),
            shape(edges, features, BF16),
        ],
        mesh_lat,
        g2m_slot.reshape(1, edges),
        g2m_receiver.reshape(1, edges),
        halo_send,
        mesh_sender.reshape(1, mesh_edges),
        mesh_receiver.reshape(1, mesh_edges),
    )
    saved = [
        shape(edges, features, BF16),
        shape(edges, features, BF16),
        shape(edges, LANES, F32),
        shape(mesh_rows, features, BF16),
        shape(mesh_rows, features, BF16),
        shape(mesh_rows, LANES, F32),
    ]
    mesh_one, halo_out, *kept = call(
        encode_kernel,
        [shape(mesh_rows, features, BF16), shape(halos, features, BF16)] + saved,
        mesh_lat,
        arrived,
        slot_g,
        recv_rows,
        enc_t,
        halo_g,
        weights=enc,
    )
    halo_in = exchange(halo_out, halo_capacity)
    mesh_two, grad_one, grad_halo = call(
        process_kernel,
        [
            shape(mesh_rows, features, BF16),
            shape(mesh_rows, features, F32),
            shape(halos, features, BF16),
        ],
        mesh_one,
        halo_in,
        cotangent,
        sender_t,
        sender_g,
        proc_t,
        proc_g,
        weights=proc,
        scratch=[
            pltpu.VMEM((mesh_edges, features), BF16),
            pltpu.VMEM((mesh_edges, features), BF16),
            pltpu.VMEM((mesh_edges, LANES), F32),
            pltpu.VMEM((mesh_edges, features), BF16),
        ],
    )
    halo_back = exchange(grad_halo, halo_capacity)
    mesh_grad, grad_slots = call(
        decode_kernel,
        [shape(mesh_rows, features, F32), shape(slots, features, BF16)],
        grad_one,
        halo_back,
        halo_t,
        *kept,
        enc_t,
        enc_g,
        slot_t,
        weights=enc,
        scratch=[pltpu.VMEM((edges, features), BF16)],
    )
    returned = exchange(grad_slots, capacity)
    (grid_grad,) = call(grid_kernel, [shape(grid_rows, features, F32)], grid_t, returned)
    return (mesh_two, grid_grad, mesh_grad)


def solution(mesh):
    rows = P(AXES, None)
    flat = P(AXES)
    in_specs = (rows,) * 4 + (flat,) * 2 + (rows,) + (flat,) * 2 + (P(None, "mp"), P("mp", None)) * 4
    return jax.shard_map(
        local, mesh=mesh, in_specs=in_specs, out_specs=(rows,) * 3, check_vma=False
    )
```

time: 164 us -> 121 us (0.74)
  local copies, waits for them, and re-layouts: 47.9 us -> 8.79 us
  starting transfers between devices: 45.5 us -> 22.7 us
  waiting for transfers between devices: 12.7 us -> 33.2 us
  blocking collectives: 30.7 us -> 27.3 us
  Pallas kernels: 24.7 us -> 27.9 us
    unnamed x166 -> x16, local copies, waits for them, and re-layouts: 46.2 us -> 3.2 us
    ppermute x40 -> x20, starting transfers between devices: 39.7 us -> 18.5 us  [the longest x6 9.82 us: spread_along(): lax.ppermute(piece, 'mp', [(m, (m + s) % size) for m in range(size)])]
    ppermute x40 -> x20, waiting for transfers between devices: 12.7 us -> 29.9 us  [the longest x14 21.6 us: across(): lax.ppermute(x, ('groups', 'graph'), [(p, p ^ flip) for p in range(planes)])]
    pallas_call x6, Pallas kernels: 17.6 us -> 27.9 us  [call(): pl.pallas_call(body, grid=(1,), out_shape=out_shape, in_specs=in_specs, o...]
    pallas_call x1 -> x0, Pallas kernels: 7.15 us -> none  [gather_weights(): pl.pallas_call(pack_kernel, out_shape=[shape(192, 128, BF16)] * 4, in_spe...]
    all_to_all x3, blocking collectives: 30.7 us -> 27.3 us  [exchange(): lax.all_to_all(parts, PEERS, split_axis=0, concat_axis=0, tiled=True)]
    all_to_all x1, waiting for transfers between devices: 0.01 us -> 3.3 us  [exchange(): lax.all_to_all(parts, PEERS, split_axis=0, concat_axis=0, tiled=True)]
    reshape x4, local copies, waits for them, and re-layouts: 0.71 us -> 3.05 us  [exchange(): parts = rows.reshape(-1, capacity, features)]
  transfers between devices with their start and end apart: 41 -> 21, of which waited for: 9 -> 8; matrix products, arithmetic and copies ran while one was open for 1% -> 3% of each run, Pallas kernels for 3% -> 7%
where the time goes in v3:
time: 121 us
  waiting for transfers between devices  33.2 us (27%)
  Pallas kernels  27.9 us (23%)
  blocking collectives  27.3 us (23%)
  starting transfers between devices  22.7 us (19%)
  local copies, waits for them, and re-layouts  8.79 us (7%)
    pallas_call x6, Pallas kernels, call(): pl.pallas_call(body, grid=(1,), out_shape=out_shape, in_specs=in_specs, o...  27.9 us
    all_to_all x3, blocking collectives, exchange(): lax.all_to_all(parts, PEERS, split_axis=0, concat_axis=0, tiled=True)  27.3 us
    ppermute x14, waiting for transfers between devices, across(): lax.ppermute(x, ('groups', 'graph'), [(p, p ^ flip) for p in range(planes)])  21.6 us
    ppermute x6, starting transfers between devices, spread_along(): lax.ppermute(piece, 'mp', [(m, (m + s) % size) for m in range(size)])  9.82 us
    ppermute x14, starting transfers between devices, across(): lax.ppermute(x, ('groups', 'graph'), [(p, p ^ flip) for p in range(planes)])  8.7 us
    ppermute x6, waiting for transfers between devices, spread_along(): lax.ppermute(piece, 'mp', [(m, (m + s) % size) for m in range(size)])  8.31 us
    all_to_all x1, starting transfers between devices, exchange(): lax.all_to_all(parts, PEERS, split_axis=0, concat_axis=0, tiled=True)  4.15 us
    all_to_all x1, waiting for transfers between devices, exchange(): lax.all_to_all(parts, PEERS, split_axis=0, concat_axis=0, tiled=True)  3.3 us
  transfers between devices with their start and end apart: 21, of which 8 were waited for; matrix products, arithmetic and copies ran while one was open for 3% of the time, Pallas kernels for 7%

profile of v3, /device:TPU:0, one launch (start us, length us, event | category | flops | bytes accessed | tf_op | source)
XLA Modules:
  0.0 120.7 jit_solution(16031831429273453497)
XLA Ops:
  0.6 1.3 %copy.20.refs_9_ = s32[16,4]{1,0:T(8,128)} copy(s32[16,4]{0,1:T(4,128)} %param.20) | data formatting | bytes 512 | tf_op args[3]
  2.0 3.1 %prepare_kernel.1 = (bf16[128,3072]{1,0:T(8,128)(2,1)}, bf16[128,3072]{1,0:T(8,128)(2,1)}, bf16[16,3072]{1,0:T(8,128)(2,1)}, bf16[16,3072]{1,0:T(8,128)(2,1)}, b...) custom-call(bf16[1024,128]{1,0:T(8,128)(2,1)} %refs_0_.3, bf16[128,512]{1,0:T(8,128)(2,1)} %refs_1_.1, ...), custom_call_target="tpu_custom_call" | custom-call | tf_op jit(solution)/shard_map/prepare_kernel/pallas_call | solution.py:57
  5.1 3.0 %collective-permute-start = (bf16[16,3072]{1,0:T(8,128)(2,1)}, bf16[16,3072]{1,0:T(8,128)(2,1)S(1)}, u32[]{:S(2)}, u32[]{:S(2)}) collective-permute-start(bf16[16,3072]{1,0:T(8,128)(2,1)} %get-tuple-element.38), channel_id=1, source_target_pairs={{0,1},{1,2},{2,3},{3,0},{4,5},{5,6},{6,7},{7,4},{8,9},{9,10},{10,1... | collective-permute-start | bytes 294920 | tf_op jit(solution)/shard_map/ppermute | solution.py:106
  8.1 2.1 %collective-permute-start.2 = (bf16[16,3072]{1,0:T(8,128)(2,1)}, bf16[16,3072]{1,0:T(8,128)(2,1)S(1)}, u32[]{:S(2)}, u32[]{:S(2)}) collective-permute-start(bf16[16,3072]{1,0:T(8,128)(2,1)} %get-tuple-element.38), channel_id=1, source_target_pairs={{0,3},{1,0},{2,1},{3,2},{4,7},{5,4},{6,5},{7,6},{8,11},{9,8},{10,9... | collective-permute-start | bytes 294920 | tf_op jit(solution)/shard_map/ppermute | solution.py:106
  11.1 2.7 %collective-permute-done = bf16[16,3072]{1,0:T(8,128)(2,1)S(1)} collective-permute-done((bf16[16,3072]{1,0:T(8,128)(2,1)}, bf16[16,3072]{1,0:T(8,128)(2,1)S(1)}, u32[]{:S(2)}, u32[]{:S(2)}) %collective-permute-start) | collective-permute-done | bytes 98336 | tf_op jit(solution)/shard_map/ppermute | solution.py:106
  13.8 5.6 %collective-permute-done.1 = bf16[16,3072]{1,0:T(8,128)(2,1)S(1)} collective-permute-done((bf16[16,3072]{1,0:T(8,128)(2,1)}, bf16[16,3072]{1,0:T(8,128)(2,1)S(1)}, u32[]{:S(2)}, u32[]{:S(2)}) %collective-permute-start.1) | collective-permute-done | bytes 98336 | tf_op jit(solution)/shard_map/ppermute | solution.py:106
  19.6 2.5 %collective-permute-start.8 = (bf16[48,3072]{1,0:T(8,128)(2,1)S(1)}, bf16[48,3072]{1,0:T(8,128)(2,1)S(1)}, u32[]{:S(2)}, u32[]{:S(2)}) collective-permute-start(bf16[48,3072]{1,0:T(8,128)(2,1)S(1)} %constant_dynamic-update-slice_fusion.refs_7_.refs_13_), channel_id=1, source_target_pairs={{0,24},{4,28},{8,16},{12,20},{16,8},{20,12},{24,0},{28,4},{1,25},{... | collective-permute-start | bytes 884744 | tf_op jit(solution)/shard_map/ppermute | solution.py:100
  23.2 3.8 %collective-permute-start.12 = (bf16[16,3072]{1,0:T(8,128)(2,1)S(1)}, bf16[16,3072]{1,0:T(8,128)(2,1)S(1)}, u32[]{:S(2)}, u32[]{:S(2)}) collective-permute-start(bf16[16,3072]{1,0:T(8,128)(2,1)S(1)} %copy-done.4), channel_id=1, source_target_pairs={{0,3},{1,0},{2,1},{3,2},{4,7},{5,4},{6,5},{7,6},{8,11},{9,8},{10,9... | collective-permute-start | bytes 294920 | tf_op jit(solution)/shard_map/ppermute | solution.py:106
  27.0 3.4 %collective-permute-done.8.refs_13_.refs_19_ = bf16[48,3072]{1,0:T(8,128)(2,1)S(1)} collective-permute-done((bf16[48,3072]{1,0:T(8,128)(2,1)S(1)}, bf16[48,3072]{1,0:T(8,128)(2,1)S(1)}, u32[]{:S(2)}, u32[]{:S(2)}) %collective-permute-start.8) | collective-permute-done | bytes 294944 | tf_op jit(solution)/shard_map/ppermute | solution.py:100
  30.4 5.8 %collective-permute-done.6.refs_11_.refs_17_ = bf16[48,3072]{1,0:T(8,128)(2,1)S(1)} collective-permute-done((bf16[48,3072]{1,0:T(8,128)(2,1)S(1)}, bf16[48,3072]{1,0:T(8,128)(2,1)S(1)}, u32[]{:S(2)}, u32[]{:S(2)}) %collective-permute-start.6) | collective-permute-done | bytes 294944 | tf_op jit(solution)/shard_map/ppermute | solution.py:100
  36.8 2.1 %collective-permute-start.18 = (bf16[48,3072]{1,0:T(8,128)(2,1)S(1)}, bf16[48,3072]{1,0:T(8,128)(2,1)}, u32[]{:S(2)}, u32[]{:S(2)}) collective-permute-start(bf16[48,3072]{1,0:T(8,128)(2,1)S(1)} %constant_dynamic-update-slice_fusion.3.refs_8_), channel_id=1, source_target_pairs={{0,24},{4,28},{8,16},{12,20},{16,8},{20,12},{24,0},{28,4},{1,25},{... | collective-permute-start | bytes 884744 | tf_op jit(solution)/shard_map/ppermute | solution.py:100
  40.9 6.9 %collective-permute-done.18.refs_14_ = bf16[48,3072]{1,0:T(8,128)(2,1)} collective-permute-done((bf16[48,3072]{1,0:T(8,128)(2,1)S(1)}, bf16[48,3072]{1,0:T(8,128)(2,1)}, u32[]{:S(2)}, u32[]{:S(2)}) %collective-permute-start.18) | collective-permute-done | bytes 294944 | tf_op jit(solution)/shard_map/ppermute | solution.py:100
  47.8 5.4 %collective-permute-done.16.refs_12_ = bf16[48,3072]{1,0:T(8,128)(2,1)} collective-permute-done((bf16[48,3072]{1,0:T(8,128)(2,1)S(1)}, bf16[48,3072]{1,0:T(8,128)(2,1)}, u32[]{:S(2)}, u32[]{:S(2)}) %collective-permute-start.16) | collective-permute-done | bytes 294944 | tf_op jit(solution)/shard_map/ppermute | solution.py:100
  54.3 4.2 %all-to-all-start = ((bf16[16,4,512]{2,1,0:T(4,128)(2,1)}), bf16[16,4,512]{2,1,0:T(4,128)(2,1)S(1)}, u32[]{:S(2)}, u32[]{:S(2)}) async-start(bf16[16,4,512]{2,1,0:T(4,128)(2,1)} %reshape.42), calls=%async_computation | async-start | bytes 131072 | tf_op jit(solution)/shard_map/all_to_all | solution.py:370
  59.1 2.6 %tables_kernel.1 = (bf16[64,512]{1,0:T(8,128)(2,1)}, bf16[512,64]{1,0:T(8,128)(2,1)}, bf16[256,512]{1,0:T(8,128)(2,1)}, bf16[512,256]{1,0:T(8,128)(2,1)}, bf16[2...) custom-call(bf16[256,512]{1,0:T(8,128)(2,1)} %refs_0_.5, ...), custom_call_target="tpu_custom_call" | custom-call | tf_op jit(solution)/shard_map/tables_kernel/pallas_call | solution.py:57
  61.8 3.3 %all-to-all-done = bf16[16,4,512]{2,1,0:T(4,128)(2,1)S(1)} async-done(((bf16[16,4,512]{2,1,0:T(4,128)(2,1)}), bf16[16,4,512]{2,1,0:T(4,128)(2,1)S(1)}, u32[]{:S(2)}, u32[]{:S(2)}) %all-to-all-start) | async-done | bytes 65568 | tf_op jit(solution)/shard_map/all_to_all | solution.py:370
  65.7 5.5 %encode_kernel.1 = (bf16[256,512]{1,0:T(8,128)(2,1)}, bf16[32,512]{1,0:T(8,128)(2,1)}, bf16[512,512]{1,0:T(8,128)(2,1)}, bf16[512,512]{1,0:T(8,128)(2,1)}, f32[5...) custom-call(bf16[256,512]{1,0:T(8,128)(2,1)} %refs_0_.5, ...), custom_call_target="tpu_custom_call" | custom-call | tf_op jit(solution)/shard_map/encode_kernel/pallas_call | solution.py:57
  72.0 9.1 %all_to_all.20 = bf16[16,2,512]{2,1,0:T(2,128)(2,1)S(1)} all-to-all(bf16[16,2,512]{2,1,0:T(2,128)(2,1)S(1)} %reshape.48), channel_id=1, replica_groups=mesh['groups'=2,'graph'=4,'mp'=4] {'graph','mp'}, dimensions={0} | all-to-all | bytes 65536 | tf_op jit(solution)/shard_map/all_to_all | solution.py:370
  81.7 1.1 copy-done.1
  82.8 8.9 %process_kernel.1 = (bf16[256,512]{1,0:T(8,128)(2,1)}, f32[256,512]{1,0:T(8,128)}, bf16[32,512]{1,0:T(8,128)(2,1)}) custom-call(bf16[256,512]{1,0:T(8,128)(2,1)} %get-tuple-element.46.refs_0_, bf16[32,512]{1,0:T(8,128)(2,1)} %reshape.49.refs_1_, bf16[256,512]{1,0:T(8,128)(2,1)} %refs_2_.3, bf16[288,512]{1,0:T(8,128)(2,1)} %get-tuple-element.48.refs_3_, ...), custom_call_target="tpu_custom_call" | custom-call | tf_op jit(solution)/shard_map/process_kernel/pallas_call | solution.py:57
  92.5 9.1 %all_to_all.21 = bf16[16,2,512]{2,1,0:T(2,128)(2,1)S(1)} all-to-all(bf16[16,2,512]{2,1,0:T(2,128)(2,1)S(1)} %reshape.50), channel_id=1, replica_groups=mesh['groups'=2,'graph'=4,'mp'=4] {'graph','mp'}, dimensions={0} | all-to-all | bytes 65536 | tf_op jit(solution)/shard_map/all_to_all | solution.py:370
  102.2 5.6 %decode_kernel.1 = (f32[256,512]{1,0:T(8,128)}, bf16[64,512]{1,0:T(8,128)(2,1)}) custom-call(f32[256,512]{1,0:T(8,128)} %get-tuple-element.56.refs_0_, bf16[32,512]{1,0:T(8,128)(2,1)} %reshape.51.refs_1_, bf16[256,32]{1,0:T(8,128)(2,1)} %get-tuple-element.58.refs_2_, bf16[512,512]{1,0:T(8,128)(2,1)} %get-tuple-element.59.refs_3_, ...), custom_call_target="tpu_custom_call" | custom-call | tf_op jit(solution)/shard_map/decode_kernel/pallas_call | solution.py:57
  108.7 9.2 %all_to_all.22 = bf16[16,4,512]{2,1,0:T(4,128)(2,1)S(1)} all-to-all(bf16[16,4,512]{2,1,0:T(4,128)(2,1)S(1)} %reshape.52), channel_id=1, replica_groups=mesh['groups'=2,'graph'=4,'mp'=4] {'graph','mp'}, dimensions={0} | all-to-all | bytes 131072 | tf_op jit(solution)/shard_map/all_to_all | solution.py:370
  118.6 2.1 %grid_kernel.1 = f32[512,512]{1,0:T(8,128)} custom-call(bf16[512,64]{1,0:T(8,128)(2,1)} %get-tuple-element.55.refs_0_, bf16[64,512]{1,0:T(8,128)(2,1)} %reshape.53.refs_1_), custom_call_target="tpu_custom_call" | custom-call | tf_op jit(solution)/shard_map/grid_kernel/pallas_call | solution.py:57
  (53 shorter events, 11.4 us)
Async XLA Ops:
  5.1 8.8 %collective-permute-start = (bf16[16,3072]{1,0:T(8,128)(2,1)}, bf16[16,3072]{1,0:T(8,128)(2,1)S(1)}, u32[]{:S(2)}, u32[]{:S(2)}) collective-permute-start(bf16[16,3072]{1,0:T(8,128)(2,1)} %get-tuple-element.38), channel_id=1, source_target_pairs={{0,1},{1,2},{2,3},{3,0},{4,5},{5,6},{6,7},{7,4},{8,9},{9,10},{10,1... | collective-permute-start | bytes 294920 | tf_op jit(solution)/shard_map/ppermute | solution.py:106
  8.1 11.4 %collective-permute-start.2 = (bf16[16,3072]{1,0:T(8,128)(2,1)}, bf16[16,3072]{1,0:T(8,128)(2,1)S(1)}, u32[]{:S(2)}, u32[]{:S(2)}) collective-permute-start(bf16[16,3072]{1,0:T(8,128)(2,1)} %get-tuple-element.38), channel_id=1, source_target_pairs={{0,3},{1,0},{2,1},{3,2},{4,7},{5,4},{6,5},{7,6},{8,11},{9,8},{10,9... | collective-permute-start | bytes 294920 | tf_op jit(solution)/shard_map/ppermute | solution.py:106
  10.2 9.3 %collective-permute-start.1 = (bf16[16,3072]{1,0:T(8,128)(2,1)}, bf16[16,3072]{1,0:T(8,128)(2,1)S(1)}, u32[]{:S(2)}, u32[]{:S(2)}) collective-permute-start(bf16[16,3072]{1,0:T(8,128)(2,1)} %get-tuple-element.38), channel_id=1, source_target_pairs={{0,2},{1,3},{2,0},{3,1},{4,6},{5,7},{6,4},{7,5},{8,10},{9,11},{10,... | collective-permute-start | bytes 294920 | tf_op jit(solution)/shard_map/ppermute | solution.py:106
  19.5 34.2 %copy-start.2 = (bf16[64,512]{1,0:T(8,128)(2,1)S(1)}, bf16[64,512]{1,0:T(8,128)(2,1)}, u32[]{:S(2)}) copy-start(bf16[64,512]{1,0:T(8,128)(2,1)} %get-tuple-element.39) | copy-start | bytes 196612
  19.5 46.3 %copy-start = (bf16[128,3072]{1,0:T(8,128)(2,1)S(1)}, bf16[128,3072]{1,0:T(8,128)(2,1)}, u32[]{:S(2)}) copy-start(bf16[128,3072]{1,0:T(8,128)(2,1)} %get-tuple-element.44.refs_6_.refs_12_) | copy-start | bytes 2359300
  19.5 3.1 %collective-permute-start.3 = (bf16[48,3072]{1,0:T(8,128)(2,1)S(1)}, bf16[48,3072]{1,0:T(8,128)(2,1)S(1)}, u32[]{:S(2)}, u32[]{:S(2)}) collective-permute-start(bf16[48,3072]{1,0:T(8,128)(2,1)S(1)} %constant_dynamic-update-slice_fusion.refs_7_.refs_13_), channel_id=1, source_target_pairs={{0,4},{4,0},{8,12},{12,8},{16,20},{20,16},{24,28},{28,24},{1,5},{5... | collective-permute-start | bytes 884744 | tf_op jit(solution)/shard_map/ppermute | solution.py:100
  19.6 10.8 %collective-permute-start.8 = (bf16[48,3072]{1,0:T(8,128)(2,1)S(1)}, bf16[48,3072]{1,0:T(8,128)(2,1)S(1)}, u32[]{:S(2)}, u32[]{:S(2)}) collective-permute-start(bf16[48,3072]{1,0:T(8,128)(2,1)S(1)} %constant_dynamic-update-slice_fusion.refs_7_.refs_13_), channel_id=1, source_target_pairs={{0,24},{4,28},{8,16},{12,20},{16,8},{20,12},{24,0},{28,4},{1,25},{... | collective-permute-start | bytes 884744 | tf_op jit(solution)/shard_map/ppermute | solution.py:100
  22.1 14.1 %collective-permute-start.6 = (bf16[48,3072]{1,0:T(8,128)(2,1)S(1)}, bf16[48,3072]{1,0:T(8,128)(2,1)S(1)}, u32[]{:S(2)}, u32[]{:S(2)}) collective-permute-start(bf16[48,3072]{1,0:T(8,128)(2,1)S(1)} %constant_dynamic-update-slice_fusion.refs_7_.refs_13_), channel_id=1, source_target_pairs={{0,16},{4,20},{8,24},{12,28},{16,0},{20,4},{24,8},{28,12},{1,17},{... | collective-permute-start | bytes 884744 | tf_op jit(solution)/shard_map/ppermute | solution.py:100
  22.6 13.7 %collective-permute-start.10 = (bf16[16,3072]{1,0:T(8,128)(2,1)S(1)}, bf16[16,3072]{1,0:T(8,128)(2,1)S(1)}, u32[]{:S(2)}, u32[]{:S(2)}) collective-permute-start(bf16[16,3072]{1,0:T(8,128)(2,1)S(1)} %copy-done.4), channel_id=1, source_target_pairs={{0,1},{1,2},{2,3},{3,0},{4,5},{5,6},{6,7},{7,4},{8,9},{9,10},{10,1... | collective-permute-start | bytes 294920 | tf_op jit(solution)/shard_map/ppermute | solution.py:106
  22.6 17.2 %collective-permute-start.4 = (bf16[48,3072]{1,0:T(8,128)(2,1)S(1)}, bf16[48,3072]{1,0:T(8,128)(2,1)S(1)}, u32[]{:S(2)}, u32[]{:S(2)}) collective-permute-start(bf16[48,3072]{1,0:T(8,128)(2,1)S(1)} %constant_dynamic-update-slice_fusion.refs_7_.refs_13_), channel_id=1, source_target_pairs={{0,8},{4,12},{8,0},{12,4},{16,24},{20,28},{24,16},{28,20},{1,9},{5... | collective-permute-start | bytes 884744 | tf_op jit(solution)/shard_map/ppermute | solution.py:100
  23.2 13.6 %collective-permute-start.12 = (bf16[16,3072]{1,0:T(8,128)(2,1)S(1)}, bf16[16,3072]{1,0:T(8,128)(2,1)S(1)}, u32[]{:S(2)}, u32[]{:S(2)}) collective-permute-start(bf16[16,3072]{1,0:T(8,128)(2,1)S(1)} %copy-done.4), channel_id=1, source_target_pairs={{0,3},{1,0},{2,1},{3,2},{4,7},{5,4},{6,5},{7,6},{8,11},{9,8},{10,9... | collective-permute-start | bytes 294920 | tf_op jit(solution)/shard_map/ppermute | solution.py:106
  30.4 6.4 %collective-permute-start.11 = (bf16[16,3072]{1,0:T(8,128)(2,1)S(1)}, bf16[16,3072]{1,0:T(8,128)(2,1)S(1)}, u32[]{:S(2)}, u32[]{:S(2)}) collective-permute-start(bf16[16,3072]{1,0:T(8,128)(2,1)S(1)} %copy-done.4), channel_id=1, source_target_pairs={{0,2},{1,3},{2,0},{3,1},{4,6},{5,7},{6,4},{7,5},{8,10},{9,11},{10,... | collective-permute-start | bytes 294920 | tf_op jit(solution)/shard_map/ppermute | solution.py:106
  36.2 4.1 %collective-permute-start.9 = (bf16[48,3072]{1,0:T(8,128)(2,1)S(1)}, bf16[48,3072]{1,0:T(8,128)(2,1)S(1)}, u32[]{:S(2)}, u32[]{:S(2)}) collective-permute-start(bf16[48,3072]{1,0:T(8,128)(2,1)S(1)} %collective-permute-done.8.refs_13_.refs_19_), channel_id=1, source_target_pairs={{0,4},{4,0},{8,12},{12,8},{16,20},{20,16},{24,28},{28,24},{1,5},{5... | collective-permute-start | bytes 884744 | tf_op jit(solution)/shard_map/ppermute | solution.py:100
  36.3 4.1 %collective-permute-start.7 = (bf16[48,3072]{1,0:T(8,128)(2,1)S(1)}, bf16[48,3072]{1,0:T(8,128)(2,1)S(1)}, u32[]{:S(2)}, u32[]{:S(2)}) collective-permute-start(bf16[48,3072]{1,0:T(8,128)(2,1)S(1)} %collective-permute-done.6.refs_11_.refs_17_), channel_id=1, source_target_pairs={{0,4},{4,0},{8,12},{12,8},{16,20},{20,16},{24,28},{28,24},{1,5},{5... | collective-permute-start | bytes 884744 | tf_op jit(solution)/shard_map/ppermute | solution.py:100
  36.8 11.0 %collective-permute-start.18 = (bf16[48,3072]{1,0:T(8,128)(2,1)S(1)}, bf16[48,3072]{1,0:T(8,128)(2,1)}, u32[]{:S(2)}, u32[]{:S(2)}) collective-permute-start(bf16[48,3072]{1,0:T(8,128)(2,1)S(1)} %constant_dynamic-update-slice_fusion.3.refs_8_), channel_id=1, source_target_pairs={{0,24},{4,28},{8,16},{12,20},{16,8},{20,12},{24,0},{28,4},{1,25},{... | collective-permute-start | bytes 884744 | tf_op jit(solution)/shard_map/ppermute | solution.py:100
  38.9 14.2 %collective-permute-start.16 = (bf16[48,3072]{1,0:T(8,128)(2,1)S(1)}, bf16[48,3072]{1,0:T(8,128)(2,1)}, u32[]{:S(2)}, u32[]{:S(2)}) collective-permute-start(bf16[48,3072]{1,0:T(8,128)(2,1)S(1)} %constant_dynamic-update-slice_fusion.3.refs_8_), channel_id=1, source_target_pairs={{0,16},{4,20},{8,24},{12,28},{16,0},{20,4},{24,8},{28,12},{1,17},{... | collective-permute-start | bytes 884744 | tf_op jit(solution)/shard_map/ppermute | solution.py:100
  39.8 13.4 %collective-permute-start.14 = (bf16[48,3072]{1,0:T(8,128)(2,1)S(1)}, bf16[48,3072]{1,0:T(8,128)(2,1)}, u32[]{:S(2)}, u32[]{:S(2)}) collective-permute-start(bf16[48,3072]{1,0:T(8,128)(2,1)S(1)} %constant_dynamic-update-slice_fusion.3.refs_8_), channel_id=1, source_target_pairs={{0,8},{4,12},{8,0},{12,4},{16,24},{20,28},{24,16},{28,20},{1,9},{5... | collective-permute-start | bytes 884744 | tf_op jit(solution)/shard_map/ppermute | solution.py:100
  40.4 25.4 %collective-permute-start.5 = (bf16[48,3072]{1,0:T(8,128)(2,1)S(1)}, bf16[48,3072]{1,0:T(8,128)(2,1)S(1)}, u32[]{:S(2)}, u32[]{:S(2)}) collective-permute-start(bf16[48,3072]{1,0:T(8,128)(2,1)S(1)} %collective-permute-done.4.refs_9_.refs_15_), channel_id=1, source_target_pairs={{0,4},{4,0},{8,12},{12,8},{16,20},{20,16},{24,28},{28,24},{1,5},{5... | collective-permute-start | bytes 884744 | tf_op jit(solution)/shard_map/ppermute | solution.py:100
  40.4 41.3 %collective-permute-start.13 = (bf16[48,3072]{1,0:T(8,128)(2,1)S(1)}, bf16[48,3072]{1,0:T(8,128)(2,1)}, u32[]{:S(2)}, u32[]{:S(2)}) collective-permute-start(bf16[48,3072]{1,0:T(8,128)(2,1)S(1)} %constant_dynamic-update-slice_fusion.3.refs_8_), channel_id=1, source_target_pairs={{0,4},{4,0},{8,12},{12,8},{16,20},{20,16},{24,28},{28,24},{1,5},{5... | collective-permute-start | bytes 884744 | tf_op jit(solution)/shard_map/ppermute | solution.py:100
  47.8 33.9 %collective-permute-start.19 = (bf16[48,3072]{1,0:T(8,128)(2,1)}, bf16[48,3072]{1,0:T(8,128)(2,1)}, u32[]{:S(2)}, u32[]{:S(2)}) collective-permute-start(bf16[48,3072]{1,0:T(8,128)(2,1)} %collective-permute-done.18.refs_14_), channel_id=1, source_target_pairs={{0,4},{4,0},{8,12},{12,8},{16,20},{20,16},{24,28},{28,24},{1,5},{5... | collective-permute-start | bytes 884744 | tf_op jit(solution)/shard_map/ppermute | solution.py:100
  53.1 28.5 %collective-permute-start.17 = (bf16[48,3072]{1,0:T(8,128)(2,1)}, bf16[48,3072]{1,0:T(8,128)(2,1)}, u32[]{:S(2)}, u32[]{:S(2)}) collective-permute-start(bf16[48,3072]{1,0:T(8,128)(2,1)} %collective-permute-done.16.refs_12_), channel_id=1, source_target_pairs={{0,4},{4,0},{8,12},{12,8},{16,20},{20,16},{24,28},{28,24},{1,5},{5... | collective-permute-start | bytes 884744 | tf_op jit(solution)/shard_map/ppermute | solution.py:100
  53.2 28.4 %collective-permute-start.15 = (bf16[48,3072]{1,0:T(8,128)(2,1)}, bf16[48,3072]{1,0:T(8,128)(2,1)}, u32[]{:S(2)}, u32[]{:S(2)}) collective-permute-start(bf16[48,3072]{1,0:T(8,128)(2,1)} %collective-permute-done.14.refs_10_), channel_id=1, source_target_pairs={{0,4},{4,0},{8,12},{12,8},{16,20},{20,16},{24,28},{28,24},{1,5},{5... | collective-permute-start | bytes 884744 | tf_op jit(solution)/shard_map/ppermute | solution.py:100
  54.3 4.2 %copy-start.3 = (s32[16,2]{0,1:T(2,128)S(1)}, s32[16,2]{0,1:T(2,128)}, u32[]{:S(2)}) copy-start(s32[16,2]{0,1:T(2,128)} %param.23) | copy-start | bytes 388
  54.3 10.8 %all-to-all-start = ((bf16[16,4,512]{2,1,0:T(4,128)(2,1)}), bf16[16,4,512]{2,1,0:T(4,128)(2,1)S(1)}, u32[]{:S(2)}, u32[]{:S(2)}) async-start(bf16[16,4,512]{2,1,0:T(4,128)(2,1)} %reshape.42), calls=%async_computation | async-start | bytes 131072 | tf_op jit(solution)/shard_map/all_to_all | solution.py:370
  (2 other events, 4.3 us)

commit v4 on v3

v4 whole, which is shorter than its diff:
```python
import jax
import jax.numpy as jnp
from jax import lax
from jax.experimental import pallas as pl
from jax.experimental.pallas import tpu as pltpu
from jax.sharding import PartitionSpec as P

F32 = jnp.float32
BF16 = jnp.bfloat16
LANES = 128
ROWS = 256
FEATURES = 512
AXES = ("groups", "graph", "mp")
PEERS = ("graph", "mp")


def dot(left, right):
    return jnp.dot(left, right, preferred_element_type=F32)


def dot_trans(left, right):
    return lax.dot_general(left, right, (((1,), (1,)), ((), ())), preferred_element_type=F32)


def shape(rows, columns, dtype):
    return pltpu.HBM((rows, columns), dtype)


def free(rows, columns, dtype):
    return jax.ShapeDtypeStruct((rows, columns), dtype)


def held(array):
    return pltpu.with_memory_space_constraint(array, pltpu.HBM)


class Input:
    def __init__(self, copies, ref, sem):
        self.copies, self.ref, self.sem = copies, ref, sem

    def __call__(self):
        if self.copies:
            pltpu.make_async_copy(self.ref, self.ref, self.sem).wait()
            self.copies = None
        return self.ref


class Output:
    def __init__(self, ref, copy):
        self.ref, self.copy = ref, copy

    def send(self, value=None):
        if value is not None:
            self.ref[...] = value
        self.copy.start()


WEIGHTS = object()


def call(kernel, out_shape, *args, weights=(), first=0, scratch=(), flops=0):
    packed = lambda a: a.dtype == BF16 and a.shape[-1] == LANES
    args = [a if a is WEIGHTS or packed(a) else held(a) for a in args]
    arrays = [a for a in args if a is not WEIGHTS]
    width = 3 * FEATURES
    count, outs = len(args), len(out_shape)

    def body(*refs):
        sources, refs = list(refs[: len(arrays)]), refs[len(arrays) :]
        blocks, refs = refs[: len(weights)], refs[len(weights) :]
        out_refs, refs = refs[:outs], refs[outs:]
        places, refs = refs[:count], refs[count:]
        results, refs = refs[:outs], refs[outs:]
        sem_in, sem_out, refs = refs[0], refs[1], refs[2:]
        which, inputs = first, []
        for i, (arg, place) in enumerate(zip(args, places)):
            if arg is WEIGHTS:
                copies, low = [], 0
                for block in blocks:
                    n = block.shape[0]
                    copies.append(
                        pltpu.make_async_copy(
                            block.at[:, pl.ds(which * width, width)],
                            place.at[pl.ds(low, n), :],
                            sem_in.at[i],
                        )
                    )
                    low += n
                which = 1 - which
            else:
                copies = [pltpu.make_async_copy(sources.pop(0), place, sem_in.at[i])]
            for copy in copies:
                copy.start()
            inputs.append(Input(copies, place, sem_in.at[i]))
        outputs = [
            Output(ref, pltpu.make_async_copy(ref, out, sem_out.at[i]))
            for i, (ref, out) in enumerate(zip(results, out_refs))
        ]
        kernel(*inputs, *outputs, *refs)
        for output in outputs:
            output.copy.wait()

    places = [
        pltpu.VMEM((FEATURES, width), BF16) if a is WEIGHTS else pltpu.VMEM(a.shape, a.dtype)
        for a in args
    ]
    total = sum(a.size * a.dtype.itemsize for a in (*arrays, *weights))
    return pl.pallas_call(
        body,
        out_shape=out_shape,
        in_specs=[pl.BlockSpec(memory_space=pl.ANY)] * (len(arrays) + len(weights)),
        out_specs=[pl.BlockSpec(memory_space=pl.ANY)] * outs,
        scratch_shapes=places
        + [pltpu.VMEM(s.shape, s.dtype) for s in out_shape]
        + [pltpu.SemaphoreType.DMA((count,)), pltpu.SemaphoreType.DMA((outs,))]
        + list(scratch),
        name=kernel.__name__,
        cost_estimate=pl.CostEstimate(flops=flops, bytes_accessed=total, transcendentals=0),
        compiler_params=pltpu.CompilerParams(vmem_limit_bytes=40 * 1024 * 1024),
    )(*arrays, *weights)


def layers(ref):
    return ref[:, : 2 * FEATURES], ref[:, 2 * FEATURES :]


def turned(first, select):
    return dot_trans(select, first).astype(BF16)


def prepare_kernel(grid, send, *refs):
    shards, (outgoing, table_out, *pieces) = refs[:8], refs[8:]
    plane = lax.axis_index("groups") * lax.axis_size("graph") + lax.axis_index("graph")
    width = 3 * FEATURES
    for i, out in ((0, pieces[0]), (1, pieces[0]), (2, pieces[1]), (3, pieces[1])):
        rows = out.ref.shape[0]
        base = plane * rows
        one, two = shards[2 * i](), shards[2 * i + 1]()
        hidden = one.shape[1]
        select = jnp.where(
            lax.broadcasted_iota(jnp.int32, (rows, hidden), 0) + base
            == lax.broadcasted_iota(jnp.int32, (rows, hidden), 1),
            1.0,
            0.0,
        ).astype(BF16)
        low = i % 2 * width
        out.ref[:, low : low + 2 * FEATURES] = turned(one[...], select)
        out.ref[:, low + 2 * FEATURES : low + width] = two[pl.ds(pl.multiple_of(base, rows), rows), :]
        if i % 2:
            out.send()
    send_kernel(grid, send, outgoing, table_out)


def own_kernel(*refs):
    shards, outs = refs[:8], refs[8:]
    width = 3 * FEATURES
    for i in range(4):
        one, two = shards[2 * i](), shards[2 * i + 1]()
        hidden = one.shape[1]
        select = jnp.where(
            lax.broadcasted_iota(jnp.int32, (hidden, hidden), 0)
            == lax.broadcasted_iota(jnp.int32, (hidden, hidden), 1),
            1.0,
            0.0,
        ).astype(BF16)
        out, low = outs[i // 2], i % 2 * width
        out.ref[:, low : low + 2 * FEATURES] = turned(one[...], select)
        out.ref[:, low + 2 * FEATURES : low + width] = two[...]
        if i % 2:
            out.send()


def across(x, flip):
    planes = lax.axis_size("groups") * lax.axis_size("graph")
    return lax.ppermute(x, ("groups", "graph"), [(p, p ^ flip) for p in range(planes)])


def spread_along(piece):
    size = lax.axis_size("mp")
    return jnp.concatenate(
        [lax.ppermute(piece, "mp", [(m, (m + s) % size) for m in range(size)]) for s in range(1, size)]
    )


def start(grid_lat, grid_send, shards):
    grid_rows, features = grid_lat.shape
    slots, capacity = grid_send.size, grid_send.shape[1]
    sent = [free(slots * features // LANES, LANES, BF16), shape(grid_rows, slots, BF16)]
    planes = lax.axis_size("groups") * lax.axis_size("graph")
    hidden = shards[1].shape[0]
    grid_send = grid_send.T
    if planes != 8 or lax.axis_size("mp") != 4 or hidden != 128 or features != FEATURES:
        outgoing, grid_t = call(send_kernel, sent, grid_lat, grid_send)
        rows = []
        for i in range(4):
            rows.append(lax.all_gather(shards[2 * i], "mp", axis=1, tiled=True).T)
            rows.append(lax.all_gather(shards[2 * i + 1], "mp", axis=0, tiled=True))
        enc, proc = jnp.concatenate(rows[:4], axis=1), jnp.concatenate(rows[4:], axis=1)
        return [enc], lambda after: ([proc], after), exchange(outgoing, capacity), grid_t
    outgoing, grid_t, enc_piece, proc_piece = call(
        prepare_kernel,
        sent + [free(hidden // planes, 6 * features, BF16)] * 2,
        grid_lat,
        grid_send,
        *shards,
    )
    first = spread_along(enc_piece)
    second = across(first, 1)
    outgoing, proc_piece, second = lax.optimization_barrier((outgoing, proc_piece, second))
    enc_own, proc_own = call(own_kernel, [shape(hidden, 6 * features, BF16)] * 2, *shards)
    enc_own, proc_own = held(enc_own), held(proc_own)
    enc = [enc_own, first, second]
    for flip in (2, 4, 6):
        block = across(first, flip)
        enc += [block, across(block, 1)]
    arrived = exchange(outgoing, capacity)
    first = spread_along(proc_piece)
    first, arrived = lax.optimization_barrier((first, arrived))
    blocks = [first] + [across(first, flip) for flip in (2, 4, 6)]

    def finish(after):
        *tied, after = lax.optimization_barrier((*blocks, after))
        return [proc_own] + tied + [across(block, 1) for block in tied], after

    return enc, finish, arrived, grid_t


def forward(inputs, first, second):
    before = dot_trans(inputs, first)
    logistic = jax.nn.sigmoid(before)
    hidden = (before * logistic).astype(BF16)
    slope = logistic * (1.0 + before * (1.0 - logistic))
    summed = dot(hidden, second)
    centered = summed - jnp.mean(summed, axis=-1, keepdims=True)
    rescale = lax.rsqrt(jnp.mean(centered * centered, axis=-1, keepdims=True) + 1e-05)
    normed = centered * rescale
    return normed, slope.astype(BF16), normed.astype(BF16), rescale


def backward_hidden(incoming, slope, normed, rescale, second):
    normed = normed.astype(F32)
    g_out = (
        incoming
        - jnp.mean(incoming, axis=-1, keepdims=True)
        - normed * jnp.mean(incoming * normed, axis=-1, keepdims=True)
    ) * rescale
    return (dot_trans(g_out.astype(BF16), second) * slope.astype(F32)).astype(BF16)


def table(index_row, count):
    n = index_row.shape[1]
    return jnp.where(lax.broadcasted_iota(jnp.int32, (count, n), 0) == index_row, 1.0, 0.0)


def flat_row(index):
    width, count = index.shape
    index = index.astype(F32).T
    at = lax.broadcasted_iota(jnp.int32, (count, count * width), 1)
    row = lax.broadcasted_iota(jnp.int32, (count, count * width), 0)
    spread = jnp.zeros(at.shape, F32)
    for c in range(width):
        spread = jnp.where(at % width == c, index[:, c : c + 1], spread)
    return jnp.sum(jnp.where(at // width == row, spread, 0.0), axis=0, keepdims=True).astype(jnp.int32)


def lane_table(n, blocks, block, tall):
    sizes = (n * blocks, n) if tall else (n, n * blocks)
    long = lax.broadcasted_iota(jnp.int32, sizes, 0 if tall else 1)
    short = lax.broadcasted_iota(jnp.int32, sizes, 1 if tall else 0)
    return jnp.where(long == short * blocks + block, 1.0, 0.0).astype(BF16)


def pack_rows(rows):
    n, blocks = rows.shape[0], rows.shape[1] // LANES
    return sum(
        dot(lane_table(n, blocks, k, True), rows[:, k * LANES : (k + 1) * LANES])
        for k in range(blocks)
    ).astype(BF16)


def unpack_rows(packed, features):
    blocks = features // LANES
    n = packed.shape[0] // blocks
    return jnp.concatenate(
        [dot(lane_table(n, blocks, k, False), packed).astype(BF16) for k in range(blocks)], axis=1
    )


def send_kernel(grid, send, outgoing, table_out):
    one = table(flat_row(send()[...]), grid().shape[0])
    rows = dot(one.T.astype(BF16), grid()[...]).astype(BF16)
    outgoing.send(pack_rows(rows))
    table_out.send(one.astype(BF16))


def tables_kernel(mesh, slot, recv_e, halo, sender, recv_p, *outs):
    for i, index in enumerate((slot, recv_e, halo, sender, recv_p)):
        scatter, gather = outs[2 * i : 2 * i + 2]
        row = flat_row(index()[...]) if index is halo else index()[...]
        one = table(row, scatter.ref.shape[0])
        scatter.send(one.astype(BF16))
        gather.send(one.T.astype(BF16))
    outs[10].send(dot(outs[3].ref[...], mesh()[...]).astype(BF16))


def encode_kernel(
    recv_rows, arrived, slot_g, weights_e, enc_t, mesh, weights_n, halo_g,
    one_out, halo_out, slope_e, normed_e, scale_e, slope_n, normed_n, scale_n,
):
    rows_in = unpack_rows(arrived()[...], FEATURES)
    edges = slot_g().shape[0]
    first, second = layers(weights_e())
    for low in range(0, edges, ROWS):
        rows = pl.ds(low, ROWS)
        sent = dot(slot_g()[rows, :], rows_in).astype(BF16)
        inputs = jnp.concatenate([sent, recv_rows()[rows, :]], axis=1)
        _, slope, normed, rescale = forward(inputs, first, second)
        slope_e.ref[rows, :] = slope
        normed_e.ref[rows, :] = normed
        scale_e.ref[rows, :] = jnp.broadcast_to(rescale, (ROWS, LANES))
    for out in (slope_e, normed_e, scale_e):
        out.send()
    aggregate = dot(enc_t()[...], normed_e.ref[...]).astype(BF16)
    first, second = layers(weights_n())
    own = mesh()[...]
    normed, slope, rounded, rescale = forward(
        jnp.concatenate([own, aggregate], axis=1), first, second
    )
    one = (own.astype(F32) + normed).astype(BF16)
    one_out.send(one)
    halo_out.send(pack_rows(dot(halo_g()[...], one).astype(BF16)))
    slope_n.send(slope)
    normed_n.send(rounded)
    scale_n.send(jnp.broadcast_to(rescale, scale_n.ref.shape))


def process_kernel(
    one_in, halo, sender_g, proc_g, weights_p, proc_t, weights_n, cotangent_in, sender_t,
    two, grad_one, grad_halo, slope_p, normed_p, scale_p, ga_p,
):
    features = FEATURES
    one = one_in()[...]
    mesh_rows = one.shape[0]
    lookup = jnp.concatenate([one, unpack_rows(halo()[...], features)], axis=0)
    edges = sender_g().shape[0]
    first, second = layers(weights_p())
    for low in range(0, edges, ROWS):
        rows = pl.ds(low, ROWS)
        sent = dot(sender_g()[rows, :], lookup).astype(BF16)
        got = dot(proc_g()[rows, :], one).astype(BF16)
        _, slope, normed, rescale = forward(jnp.concatenate([sent, got], axis=1), first, second)
        slope_p[rows, :] = slope
        normed_p[rows, :] = normed
        scale_p[rows, :] = jnp.broadcast_to(rescale, (ROWS, LANES))
    aggregate = dot(proc_t()[...], normed_p[...]).astype(BF16)
    first_n, second_n = layers(weights_n())
    normed, slope, rounded, rescale = forward(
        jnp.concatenate([one, aggregate], axis=1), first_n, second_n
    )
    two.send((one.astype(F32) + normed).astype(BF16))
    cotangent = cotangent_in()[...].astype(F32)
    ga = backward_hidden(cotangent, slope, rounded, rescale, second_n)
    g_q = dot(ga, first_n)
    g_msg = g_q[:, features:].astype(BF16)
    for low in range(0, edges, ROWS):
        rows = pl.ds(low, ROWS)
        incoming = dot(proc_g()[rows, :], g_msg)
        ga_p[rows, :] = backward_hidden(
            incoming, slope_p[rows, :], normed_p[rows, :], scale_p[rows, 0:1], second
        )
    by_send = dot(sender_t()[...], ga_p[...]).astype(BF16)
    g_send = dot(by_send, first[:, :features])
    grad_halo.send(pack_rows(g_send[mesh_rows:, :].astype(BF16)))
    by_recv = dot(proc_t()[...], ga_p[...]).astype(BF16)
    g_recv = dot(by_recv, first[:, features:])
    grad_one.send(cotangent + g_q[:, :features] + g_recv + g_send[:mesh_rows, :])


def decode_kernel(
    back, halo_t, grad_in, slope_n, normed_n, scale_n, weights_n, enc_g, slope_e, normed_e, scale_e,
    weights_e, slot_t, enc_t, mesh_grad, grad_slots, ga_e,
):
    features = FEATURES
    edges = enc_g().shape[0]
    grad_one = grad_in()[...] + dot(halo_t()[...], unpack_rows(back()[...], features))
    first_n, second_n = layers(weights_n())
    ga = backward_hidden(grad_one, slope_n()[...], normed_n()[...], scale_n()[:, 0:1], second_n)
    g_n = dot(ga, first_n)
    g_edge = g_n[:, features:].astype(BF16)
    first, second = layers(weights_e())
    for low in range(0, edges, ROWS):
        rows = pl.ds(low, ROWS)
        incoming = dot(enc_g()[rows, :], g_edge)
        ga_e[rows, :] = backward_hidden(
            incoming, slope_e()[rows, :], normed_e()[rows, :], scale_e()[rows, 0:1], second
        )
    by_slot = dot(slot_t()[...], ga_e[...]).astype(BF16)
    grad_slots.send(pack_rows(dot(by_slot, first[:, :features]).astype(BF16)))
    by_recv = dot(enc_t()[...], ga_e[...]).astype(BF16)
    mesh_grad.send(grad_one + g_n[:, :features] + dot(by_recv, first[:, features:]))


def grid_kernel(back, table_in, out):
    rows = unpack_rows(back()[...], FEATURES)
    out.send(dot(table_in()[...], rows))


def exchange(packed, capacity):
    peers = lax.axis_size("graph") * lax.axis_size("mp")
    parts = packed.reshape(peers, -1, LANES)
    return lax.all_to_all(parts, PEERS, split_axis=0, concat_axis=0, tiled=True).reshape(packed.shape)


def local(
    grid_lat,
    mesh_lat,
    cotangent,
    grid_send,
    g2m_slot,
    g2m_receiver,
    halo_send,
    mesh_sender,
    mesh_receiver,
    *shards,
):
    grid_rows, features = grid_lat.shape
    mesh_rows = mesh_lat.shape[0]
    edges = g2m_slot.shape[0]
    mesh_edges = mesh_sender.shape[0]
    slots, halos = grid_send.size, halo_send.size
    capacity, halo_capacity = grid_send.shape[1], halo_send.shape[1]
    blocks = features // LANES
    enc, finish, arrived, grid_t = start(grid_lat, grid_send, shards)
    slot_t, slot_g, enc_t, enc_g, halo_t, halo_g, sender_t, sender_g, proc_t, proc_g, recv_rows = call(
        tables_kernel,
        [
            shape(slots, edges, BF16),
            shape(edges, slots, BF16),
            shape(mesh_rows, edges, BF16),
            shape(edges, mesh_rows, BF16),
            shape(mesh_rows, halos, BF16),
            shape(halos, mesh_rows, BF16),
            shape(mesh_rows + halos, mesh_edges, BF16),
            shape(mesh_edges, mesh_rows + halos, BF16),
            shape(mesh_rows, mesh_edges, BF16),
            shape(mesh_edges, mesh_rows, BF16),
            shape(edges, features, BF16),
        ],
        mesh_lat,
        g2m_slot.reshape(1, edges),
        g2m_receiver.reshape(1, edges),
        halo_send.T,
        mesh_sender.reshape(1, mesh_edges),
        mesh_receiver.reshape(1, mesh_edges),
    )
    saved = [
        shape(edges, features, BF16),
        shape(edges, features, BF16),
        shape(edges, LANES, F32),
        shape(mesh_rows, features, BF16),
        shape(mesh_rows, features, BF16),
        shape(mesh_rows, LANES, F32),
    ]
    mesh_one, halo_out, slope_e, normed_e, scale_e, slope_n, normed_n, scale_n = call(
        encode_kernel,
        [shape(mesh_rows, features, BF16), free(halos * blocks, LANES, BF16)] + saved,
        recv_rows,
        arrived,
        slot_g,
        WEIGHTS,
        enc_t,
        mesh_lat,
        WEIGHTS,
        halo_g,
        weights=enc,
        flops=3 * 10**9,
    )
    proc, mesh_one = finish(mesh_one)
    halo_in = exchange(halo_out, halo_capacity)
    mesh_two, grad_one, grad_halo = call(
        process_kernel,
        [
            shape(mesh_rows, features, BF16),
            shape(mesh_rows, features, F32),
            free(halos * blocks, LANES, BF16),
        ],
        mesh_one,
        halo_in,
        sender_g,
        proc_g,
        WEIGHTS,
        proc_t,
        WEIGHTS,
        cotangent,
        sender_t,
        weights=proc,
        flops=5 * 10**9,
        scratch=[
            pltpu.VMEM((mesh_edges, features), BF16),
            pltpu.VMEM((mesh_edges, features), BF16),
            pltpu.VMEM((mesh_edges, LANES), F32),
            pltpu.VMEM((mesh_edges, features), BF16),
        ],
    )
    halo_back = exchange(grad_halo, halo_capacity)
    mesh_grad, grad_slots = call(
        decode_kernel,
        [shape(mesh_rows, features, F32), free(slots * blocks, LANES, BF16)],
        halo_back,
        halo_t,
        grad_one,
        slope_n,
        normed_n,
        scale_n,
        WEIGHTS,
        enc_g,
        slope_e,
        normed_e,
        scale_e,
        WEIGHTS,
        slot_t,
        enc_t,
        weights=enc,
        first=1,
        flops=3 * 10**9,
        scratch=[pltpu.VMEM((edges, features), BF16)],
    )
    returned = exchange(grad_slots, capacity)
    (grid_grad,) = call(grid_kernel, [shape(grid_rows, features, F32)], returned, grid_t)
    return (mesh_two, grid_grad, mesh_grad)


def solution(mesh):
    rows = P(AXES, None)
    flat = P(AXES)
    in_specs = (rows,) * 4 + (flat,) * 2 + (rows,) + (flat,) * 2 + (P(None, "mp"), P("mp", None)) * 4
    return jax.shard_map(
        local, mesh=mesh, in_specs=in_specs, out_specs=(rows,) * 3, check_vma=False
    )
```

time: 121 us -> 109 us (0.901)
  waiting for transfers between devices: 33.2 us -> 18.5 us
  Pallas kernels: 27.9 us -> 32.3 us
  local copies, waits for them, and re-layouts: 8.79 us -> 4.71 us
    ppermute x14, waiting for transfers between devices: 21.6 us -> 6.71 us  [across(): lax.ppermute(x, ('groups', 'graph'), [(p, p ^ flip) for p in range(planes)])]
    reshape x8 -> x0, local copies, waits for them, and re-layouts: 5.58 us -> none  [the longest x4 3.05 us: exchange(): parts = rows.reshape(-1, capacity, features)]
    pallas_call x6 -> x7, Pallas kernels: 27.9 us -> 32.3 us  [call(): pl.pallas_call(body, out_shape=out_shape, in_specs=[pl.BlockSpec(memory_s...]
    ppermute x6, starting transfers between devices: 9.82 us -> 7.84 us  [spread_along(): lax.ppermute(piece, 'mp', [(m, (m + s) % size) for m in range(size)])]
    all_to_all x1, starting transfers between devices: 4.15 us -> 6.13 us  [exchange(): lax.all_to_all(parts, PEERS, split_axis=0, concat_axis=0, tiled=True)]
    unnamed x16 -> x22, local copies, waits for them, and re-layouts: 3.2 us -> 4.7 us
  transfers between devices with their start and end apart: 21 -> 21, of which waited for: 8 -> 6; matrix products, arithmetic and copies ran while one was open for 3% -> 1% of each run, Pallas kernels for 7% -> 11%
where the time goes in v4:
time: 109 us; the launch traced here: 108 us
  Pallas kernels  32.3 us (30%)
  blocking collectives  27.3 us (25%)
  starting transfers between devices  23.1 us (21%)
  waiting for transfers between devices  18.5 us (17%)
  local copies, waits for them, and re-layouts  4.71 us (4%)
    pallas_call x7, Pallas kernels, call(): pl.pallas_call(body, out_shape=out_shape, in_specs=[pl.BlockSpec(memory_s...  32.3 us
    all_to_all x3, blocking collectives, exchange(): lax.all_to_all(parts, PEERS, split_axis=0, concat_axis=0, tiled=True)  27.3 us
    ppermute x14, starting transfers between devices, across(): lax.ppermute(x, ('groups', 'graph'), [(p, p ^ flip) for p in range(planes)])  9.12 us
    ppermute x6, waiting for transfers between devices, spread_along(): lax.ppermute(piece, 'mp', [(m, (m + s) % size) for m in range(size)])  8.1 us
    ppermute x6, starting transfers between devices, spread_along(): lax.ppermute(piece, 'mp', [(m, (m + s) % size) for m in range(size)])  7.84 us
    ppermute x14, waiting for transfers between devices, across(): lax.ppermute(x, ('groups', 'graph'), [(p, p ^ flip) for p in range(planes)])  6.71 us
    all_to_all x1, starting transfers between devices, exchange(): lax.all_to_all(parts, PEERS, split_axis=0, concat_axis=0, tiled=True)  6.13 us
    unnamed x22, local copies, waits for them, and re-layouts  4.7 us
  transfers between devices with their start and end apart: 21, of which 6 were waited for; matrix products, arithmetic and copies ran while one was open for 1% of the time, Pallas kernels for 11%

profile of v4, /device:TPU:0, one launch (start us, length us, event | category | flops | bytes accessed | tf_op | source)
XLA Modules:
  0.0 108.0 jit_solution(3179327748951527683)
XLA Ops:
  1.6 0.9 copy-done.2
  4.4 3.6 %prepare_kernel.1 = (bf16[256,128]{1,0:T(8,128)(2,1)}, bf16[512,64]{1,0:T(8,128)(2,1)}, bf16[16,3072]{1,0:T(8,128)(2,1)S(1)}, bf16[16,3072]{1,0:T(8,128)(2,1)S(1)}) custom-call(bf16[512,512]{1,0:T(8,128)(2,1)} %refs_0_.3, s32[4,16]{1,0:T(4,128)} %bitcast.21, bf16[1024,128]{1,0:T(8,128)(2,1)S(1)} %copy-done, bf16[128,512]{1,0:T(8,128)(2,1)} %refs_1_.1, ...), custom_call_target="tpu_custom_call" | custom-call | bytes 2097408 | tf_op jit(solution)/shard_map/prepare_kernel/pallas_call | solution.py:108
  8.0 3.1 %collective-permute-start = (bf16[16,3072]{1,0:T(8,128)(2,1)S(1)}, bf16[16,3072]{1,0:T(8,128)(2,1)S(1)}, u32[]{:S(2)}, u32[]{:S(2)}) collective-permute-start(bf16[16,3072]{1,0:T(8,128)(2,1)S(1)} %get-tuple-element.45), channel_id=1, source_target_pairs={{0,1},{1,2},{2,3},{3,0},{4,5},{5,6},{6,7},{7,4},{8,9},{9,10},{10,1... | collective-permute-start | bytes 294920 | tf_op jit(solution)/shard_map/ppermute | solution.py:181
  11.1 2.1 %collective-permute-start.2 = (bf16[16,3072]{1,0:T(8,128)(2,1)S(1)}, bf16[16,3072]{1,0:T(8,128)(2,1)S(1)}, u32[]{:S(2)}, u32[]{:S(2)}) collective-permute-start(bf16[16,3072]{1,0:T(8,128)(2,1)S(1)} %get-tuple-element.45), channel_id=1, source_target_pairs={{0,3},{1,0},{2,1},{3,2},{4,7},{5,4},{6,5},{7,6},{8,11},{9,8},{10,9... | collective-permute-start | bytes 294920 | tf_op jit(solution)/shard_map/ppermute | solution.py:181
  14.1 2.5 %collective-permute-done = bf16[16,3072]{1,0:T(8,128)(2,1)S(1)} collective-permute-done((bf16[16,3072]{1,0:T(8,128)(2,1)S(1)}, bf16[16,3072]{1,0:T(8,128)(2,1)S(1)}, u32[]{:S(2)}, u32[]{:S(2)}) %collective-permute-start) | collective-permute-done | bytes 98336 | tf_op jit(solution)/shard_map/ppermute | solution.py:181
  16.6 5.6 %collective-permute-done.1 = bf16[16,3072]{1,0:T(8,128)(2,1)S(1)} collective-permute-done((bf16[16,3072]{1,0:T(8,128)(2,1)S(1)}, bf16[16,3072]{1,0:T(8,128)(2,1)S(1)}, u32[]{:S(2)}, u32[]{:S(2)}) %collective-permute-start.1) | collective-permute-done | bytes 98336 | tf_op jit(solution)/shard_map/ppermute | solution.py:181
  22.4 2.5 %collective-permute-start.14 = (bf16[48,3072]{1,0:T(8,128)(2,1)S(1)}, bf16[48,3072]{1,0:T(8,128)(2,1)S(1)}, u32[]{:S(2)}, u32[]{:S(2)}) collective-permute-start(bf16[48,3072]{1,0:T(8,128)(2,1)S(1)} %constant_dynamic-update-slice_fusion.refs_7_.refs_13_), channel_id=1, source_target_pairs={{0,24},{4,28},{8,16},{12,20},{16,8},{20,12},{24,0},{28,4},{1,25},{... | collective-permute-start | bytes 884744 | tf_op jit(solution)/shard_map/ppermute | solution.py:175
  25.9 1.7 %collective-permute-start.6 = (bf16[16,3072]{1,0:T(8,128)(2,1)S(1)}, bf16[16,3072]{1,0:T(8,128)(2,1)S(1)}, u32[]{:S(2)}, u32[]{:S(2)}) collective-permute-start(bf16[16,3072]{1,0:T(8,128)(2,1)S(1)} %get-tuple-element.46), channel_id=1, source_target_pairs={{0,3},{1,0},{2,1},{3,2},{4,7},{5,4},{6,5},{7,6},{8,11},{9,8},{10,9... | collective-permute-start | bytes 294920 | tf_op jit(solution)/shard_map/ppermute | solution.py:181
  27.6 5.5 %collective-permute-done.14.refs_13_.refs_19_ = bf16[48,3072]{1,0:T(8,128)(2,1)S(1)} collective-permute-done((bf16[48,3072]{1,0:T(8,128)(2,1)S(1)}, bf16[48,3072]{1,0:T(8,128)(2,1)S(1)}, u32[]{:S(2)}, u32[]{:S(2)}) %collective-permute-start.14) | collective-permute-done | bytes 294944 | tf_op jit(solution)/shard_map/ppermute | solution.py:175
  33.2 6.1 %all-to-all-start = ((bf16[16,16,128]{2,1,0:T(8,128)(2,1)}), bf16[16,16,128]{2,1,0:T(8,128)(2,1)S(1)}, u32[]{:S(2)}, u32[]{:S(2)}) async-start(bf16[16,16,128]{2,1,0:T(8,128)(2,1)} %bitcast.1), calls=%async_computation | async-start | bytes 131072 | tf_op jit(solution)/shard_map/all_to_all | solution.py:411
  41.2 1.0 pad_maximum_fusion.refs_8_
  42.2 3.7 %all-to-all-done = bf16[16,16,128]{2,1,0:T(8,128)(2,1)S(1)} async-done(((bf16[16,16,128]{2,1,0:T(8,128)(2,1)}), bf16[16,16,128]{2,1,0:T(8,128)(2,1)S(1)}, u32[]{:S(2)}, u32[]{:S(2)}) %all-to-all-start) | async-done | bytes 65568 | tf_op jit(solution)/shard_map/all_to_all | solution.py:411
  45.9 1.7 %collective-permute-start.9 = (bf16[48,3072]{1,0:T(8,128)(2,1)S(1)}, bf16[48,3072]{1,0:T(8,128)(2,1)S(1)}, u32[]{:S(2)}, u32[]{:S(2)}) collective-permute-start(bf16[48,3072]{1,0:T(8,128)(2,1)S(1)} %pad_maximum_fusion.refs_8_), channel_id=1, source_target_pairs={{0,24},{4,28},{8,16},{12,20},{16,8},{20,12},{24,0},{28,4},{1,25},{... | collective-permute-start | bytes 884744 | tf_op jit(solution)/shard_map/ppermute | solution.py:175
  48.2 1.3 %collective-permute-start.7 = (bf16[48,3072]{1,0:T(8,128)(2,1)S(1)}, bf16[48,3072]{1,0:T(8,128)(2,1)S(1)}, u32[]{:S(2)}, u32[]{:S(2)}) collective-permute-start(bf16[48,3072]{1,0:T(8,128)(2,1)S(1)} %pad_maximum_fusion.refs_8_), channel_id=1, source_target_pairs={{0,8},{4,12},{8,0},{12,4},{16,24},{20,28},{24,16},{28,20},{1,9},{5... | collective-permute-start | bytes 884744 | tf_op jit(solution)/shard_map/ppermute | solution.py:175
  49.5 2.9 %own_kernel.1 = (bf16[128,3072]{1,0:T(8,128)(2,1)}, bf16[128,3072]{1,0:T(8,128)(2,1)}) custom-call(bf16[1024,128]{1,0:T(8,128)(2,1)S(1)} %copy-done.1, bf16[128,512]{1,0:T(8,128)(2,1)} %refs_1_.1, bf16[1024,128]{1,0:T(8,128)(2,1)S(1)} %copy-done.3, bf16[128,512]{1,0:T(8,128)(2,1)} %refs_3_.3, bf16[1024,128]{1,0:T(8,128)(2,1)S(1)} %copy-done.5, ...), custom_call_target="tpu_custom_call" | custom-call | bytes 1572864 | tf_op jit(solution)/shard_map/own_kernel/pallas_call | solution.py:108
  52.3 2.9 %tables_kernel.1 = (bf16[64,512]{1,0:T(8,128)(2,1)}, bf16[512,64]{1,0:T(8,128)(2,1)}, bf16[256,512]{1,0:T(8,128)(2,1)}, bf16[512,256]{1,0:T(8,128)(2,1)}, bf16[2...) custom-call(bf16[256,512]{1,0:T(8,128)(2,1)} %refs_4_.5, ...), custom_call_target="tpu_custom_call" | custom-call | bytes 270464 | tf_op jit(solution)/shard_map/tables_kernel/pallas_call | solution.py:108
  55.2 5.9 %encode_kernel.1 = (bf16[256,512]{1,0:T(8,128)(2,1)}, bf16[128,128]{1,0:T(8,128)(2,1)S(1)}, bf16[512,512]{1,0:T(8,128)(2,1)}, bf16[512,512]{1,0:T(8,128)(2,1)}, ...) custom-call(bf16[512,512]{1,0:T(8,128)(2,1)} %get-tuple-element.49.refs_0_, ...), custom_call_target="tpu_custom_call" | custom-call | flops 3000000000 | bytes 4341760 | tf_op jit(solution)/shard_map/encode_kernel/pallas_call | solution.py:108
  61.2 1.0 collective-permute-done.8.refs_10_
  63.3 9.0 %all_to_all.20 = bf16[16,8,128]{2,1,0:T(8,128)(2,1)S(1)} all-to-all(bf16[16,8,128]{2,1,0:T(8,128)(2,1)S(1)} %bitcast.17), channel_id=1, replica_groups=mesh['groups'=2,'graph'=4,'mp'=4] {'graph','mp'}, dimensions={0} | all-to-all | bytes 65536 | tf_op jit(solution)/shard_map/all_to_all | solution.py:411
  72.4 8.5 %process_kernel.1 = (bf16[256,512]{1,0:T(8,128)(2,1)}, f32[256,512]{1,0:T(8,128)}, bf16[128,128]{1,0:T(8,128)(2,1)S(1)}) custom-call(bf16[256,512]{1,0:T(8,128)(2,1)} %get-tuple-element.57.refs_0_, bf16[128,128]{1,0:T(8,128)(2,1)S(1)} %bitcast.18, bf16[512,288]{1,0:T(8,128)(2,1)} %get-tuple-element.59.refs_2_, bf16[512,256]{1,0:T(8,128)(2,1)} %get-tuple-element.60.refs_3_, ...), custom_call_target="tpu_custom_call" | custom-call | flops 5000000000 | bytes 4816896 | tf_op jit(solution)/shard_map/process_kernel/pallas_call | solution.py:108
  80.9 9.1 %all_to_all.21 = bf16[16,8,128]{2,1,0:T(8,128)(2,1)S(1)} all-to-all(bf16[16,8,128]{2,1,0:T(8,128)(2,1)S(1)} %bitcast.20), channel_id=1, replica_groups=mesh['groups'=2,'graph'=4,'mp'=4] {'graph','mp'}, dimensions={0} | all-to-all | bytes 65536 | tf_op jit(solution)/shard_map/all_to_all | solution.py:411
  90.0 6.4 %decode_kernel.1 = (f32[256,512]{1,0:T(8,128)}, bf16[256,128]{1,0:T(8,128)(2,1)S(1)}) custom-call(bf16[128,128]{1,0:T(8,128)(2,1)S(1)} %bitcast.19, bf16[256,32]{1,0:T(8,128)(2,1)} %get-tuple-element.70.refs_1_, f32[256,512]{1,0:T(8,128)} %get-tuple-element.71.refs_2_, bf16[256,512]{1,0:T(8,128)(2,1)} %get-tuple-element.72.refs_3_, ...), custom_call_target="tpu_custom_call" | custom-call | flops 3000000000 | bytes 6275072 | tf_op jit(solution)/shard_map/decode_kernel/pallas_call | solution.py:108
  96.4 9.2 %all_to_all.22 = bf16[16,16,128]{2,1,0:T(8,128)(2,1)S(1)} all-to-all(bf16[16,16,128]{2,1,0:T(8,128)(2,1)S(1)} %bitcast.16), channel_id=1, replica_groups=mesh['groups'=2,'graph'=4,'mp'=4] {'graph','mp'}, dimensions={0} | all-to-all | bytes 131072 | tf_op jit(solution)/shard_map/all_to_all | solution.py:411
  105.6 2.2 %grid_kernel.1 = f32[512,512]{1,0:T(8,128)} custom-call(bf16[256,128]{1,0:T(8,128)(2,1)S(1)} %bitcast.14, bf16[512,64]{1,0:T(8,128)(2,1)} %get-tuple-element.81.refs_1_), custom_call_target="tpu_custom_call" | custom-call | bytes 131072 | tf_op jit(solution)/shard_map/grid_kernel/pallas_call | solution.py:108
  (52 shorter events, 8.5 us)
Async XLA Ops:
  8.0 8.6 %collective-permute-start = (bf16[16,3072]{1,0:T(8,128)(2,1)S(1)}, bf16[16,3072]{1,0:T(8,128)(2,1)S(1)}, u32[]{:S(2)}, u32[]{:S(2)}) collective-permute-start(bf16[16,3072]{1,0:T(8,128)(2,1)S(1)} %get-tuple-element.45), channel_id=1, source_target_pairs={{0,1},{1,2},{2,3},{3,0},{4,5},{5,6},{6,7},{7,4},{8,9},{9,10},{10,1... | collective-permute-start | bytes 294920 | tf_op jit(solution)/shard_map/ppermute | solution.py:181
  11.1 11.2 %collective-permute-start.2 = (bf16[16,3072]{1,0:T(8,128)(2,1)S(1)}, bf16[16,3072]{1,0:T(8,128)(2,1)S(1)}, u32[]{:S(2)}, u32[]{:S(2)}) collective-permute-start(bf16[16,3072]{1,0:T(8,128)(2,1)S(1)} %get-tuple-element.45), channel_id=1, source_target_pairs={{0,3},{1,0},{2,1},{3,2},{4,7},{5,4},{6,5},{7,6},{8,11},{9,8},{10,9... | collective-permute-start | bytes 294920 | tf_op jit(solution)/shard_map/ppermute | solution.py:181
  13.2 9.0 %collective-permute-start.1 = (bf16[16,3072]{1,0:T(8,128)(2,1)S(1)}, bf16[16,3072]{1,0:T(8,128)(2,1)S(1)}, u32[]{:S(2)}, u32[]{:S(2)}) collective-permute-start(bf16[16,3072]{1,0:T(8,128)(2,1)S(1)} %get-tuple-element.45), channel_id=1, source_target_pairs={{0,2},{1,3},{2,0},{3,1},{4,6},{5,7},{6,4},{7,5},{8,10},{9,11},{10,... | collective-permute-start | bytes 294920 | tf_op jit(solution)/shard_map/ppermute | solution.py:181
  22.2 27.2 %copy-start.7 = (bf16[1024,128]{1,0:T(8,128)(2,1)S(1)}, bf16[1024,128]{1,0:T(8,128)(2,1)}, u32[]{:S(2)}) copy-start(bf16[1024,128]{1,0:T(8,128)(2,1)} %refs_6_.3) | copy-start | bytes 786436
  22.2 27.2 %copy-start.5 = (bf16[1024,128]{1,0:T(8,128)(2,1)S(1)}, bf16[1024,128]{1,0:T(8,128)(2,1)}, u32[]{:S(2)}) copy-start(bf16[1024,128]{1,0:T(8,128)(2,1)} %refs_4_.4) | copy-start | bytes 786436
  22.3 3.6 %collective-permute-start.3 = (bf16[48,3072]{1,0:T(8,128)(2,1)S(1)}, bf16[48,3072]{1,0:T(8,128)(2,1)S(1)}, u32[]{:S(2)}, u32[]{:S(2)}) collective-permute-start(bf16[48,3072]{1,0:T(8,128)(2,1)S(1)} %constant_dynamic-update-slice_fusion.refs_7_.refs_13_), channel_id=1, source_target_pairs={{0,4},{4,0},{8,12},{12,8},{16,20},{20,16},{24,28},{28,24},{1,5},{5... | collective-permute-start | bytes 884744 | tf_op jit(solution)/shard_map/ppermute | solution.py:175
  22.4 10.8 %collective-permute-start.14 = (bf16[48,3072]{1,0:T(8,128)(2,1)S(1)}, bf16[48,3072]{1,0:T(8,128)(2,1)S(1)}, u32[]{:S(2)}, u32[]{:S(2)}) collective-permute-start(bf16[48,3072]{1,0:T(8,128)(2,1)S(1)} %constant_dynamic-update-slice_fusion.refs_7_.refs_13_), channel_id=1, source_target_pairs={{0,24},{4,28},{8,16},{12,20},{16,8},{20,12},{24,0},{28,4},{1,25},{... | collective-permute-start | bytes 884744 | tf_op jit(solution)/shard_map/ppermute | solution.py:175
  24.9 14.5 %collective-permute-start.12 = (bf16[48,3072]{1,0:T(8,128)(2,1)S(1)}, bf16[48,3072]{1,0:T(8,128)(2,1)S(1)}, u32[]{:S(2)}, u32[]{:S(2)}) collective-permute-start(bf16[48,3072]{1,0:T(8,128)(2,1)S(1)} %constant_dynamic-update-slice_fusion.refs_7_.refs_13_), channel_id=1, source_target_pairs={{0,16},{4,20},{8,24},{12,28},{16,0},{20,4},{24,8},{28,12},{1,17},{... | collective-permute-start | bytes 884744 | tf_op jit(solution)/shard_map/ppermute | solution.py:175
  25.4 14.4 %collective-permute-start.10 = (bf16[48,3072]{1,0:T(8,128)(2,1)S(1)}, bf16[48,3072]{1,0:T(8,128)(2,1)S(1)}, u32[]{:S(2)}, u32[]{:S(2)}) collective-permute-start(bf16[48,3072]{1,0:T(8,128)(2,1)S(1)} %constant_dynamic-update-slice_fusion.refs_7_.refs_13_), channel_id=1, source_target_pairs={{0,8},{4,12},{8,0},{12,4},{16,24},{20,28},{24,16},{28,20},{1,9},{5... | collective-permute-start | bytes 884744 | tf_op jit(solution)/shard_map/ppermute | solution.py:175
  25.9 14.0 %collective-permute-start.6 = (bf16[16,3072]{1,0:T(8,128)(2,1)S(1)}, bf16[16,3072]{1,0:T(8,128)(2,1)S(1)}, u32[]{:S(2)}, u32[]{:S(2)}) collective-permute-start(bf16[16,3072]{1,0:T(8,128)(2,1)S(1)} %get-tuple-element.46), channel_id=1, source_target_pairs={{0,3},{1,0},{2,1},{3,2},{4,7},{5,4},{6,5},{7,6},{8,11},{9,8},{10,9... | collective-permute-start | bytes 294920 | tf_op jit(solution)/shard_map/ppermute | solution.py:181
  27.6 12.7 %collective-permute-start.5 = (bf16[16,3072]{1,0:T(8,128)(2,1)S(1)}, bf16[16,3072]{1,0:T(8,128)(2,1)S(1)}, u32[]{:S(2)}, u32[]{:S(2)}) collective-permute-start(bf16[16,3072]{1,0:T(8,128)(2,1)S(1)} %get-tuple-element.46), channel_id=1, source_target_pairs={{0,2},{1,3},{2,0},{3,1},{4,6},{5,7},{6,4},{7,5},{8,10},{9,11},{10,... | collective-permute-start | bytes 294920 | tf_op jit(solution)/shard_map/ppermute | solution.py:181
  33.2 8.0 %collective-permute-start.4 = (bf16[16,3072]{1,0:T(8,128)(2,1)S(1)}, bf16[16,3072]{1,0:T(8,128)(2,1)}, u32[]{:S(2)}, u32[]{:S(2)}) collective-permute-start(bf16[16,3072]{1,0:T(8,128)(2,1)S(1)} %get-tuple-element.46), channel_id=1, source_target_pairs={{0,1},{1,2},{2,3},{3,0},{4,5},{5,6},{6,7},{7,4},{8,9},{9,10},{10,1... | collective-permute-start | bytes 294920 | tf_op jit(solution)/shard_map/ppermute | solution.py:181
  33.2 12.8 %all-to-all-start = ((bf16[16,16,128]{2,1,0:T(8,128)(2,1)}), bf16[16,16,128]{2,1,0:T(8,128)(2,1)S(1)}, u32[]{:S(2)}, u32[]{:S(2)}) async-start(bf16[16,16,128]{2,1,0:T(8,128)(2,1)} %bitcast.1), calls=%async_computation | async-start | bytes 131072 | tf_op jit(solution)/shard_map/all_to_all | solution.py:411
  39.3 10.1 %copy-start.1 = (bf16[1024,128]{1,0:T(8,128)(2,1)S(1)}, bf16[1024,128]{1,0:T(8,128)(2,1)}, u32[]{:S(2)}) copy-start(bf16[1024,128]{1,0:T(8,128)(2,1)} %refs_0_.5) | copy-start | bytes 786436
  39.3 8.8 %collective-permute-start.15 = (bf16[48,3072]{1,0:T(8,128)(2,1)S(1)}, bf16[48,3072]{1,0:T(8,128)(2,1)S(1)}, u32[]{:S(2)}, u32[]{:S(2)}) collective-permute-start(bf16[48,3072]{1,0:T(8,128)(2,1)S(1)} %collective-permute-done.14.refs_13_.refs_19_), channel_id=1, source_target_pairs={{0,4},{4,0},{8,12},{12,8},{16,20},{20,16},{24,28},{28,24},{1,5},{5... | collective-permute-start | bytes 884744 | tf_op jit(solution)/shard_map/ppermute | solution.py:175
  39.8 15.4 %collective-permute-start.13 = (bf16[48,3072]{1,0:T(8,128)(2,1)S(1)}, bf16[48,3072]{1,0:T(8,128)(2,1)S(1)}, u32[]{:S(2)}, u32[]{:S(2)}) collective-permute-start(bf16[48,3072]{1,0:T(8,128)(2,1)S(1)} %collective-permute-done.12.refs_11_.refs_17_), channel_id=1, source_target_pairs={{0,4},{4,0},{8,12},{12,8},{16,20},{20,16},{24,28},{28,24},{1,5},{5... | collective-permute-start | bytes 884744 | tf_op jit(solution)/shard_map/ppermute | solution.py:175
  39.9 15.3 %collective-permute-start.11 = (bf16[48,3072]{1,0:T(8,128)(2,1)S(1)}, bf16[48,3072]{1,0:T(8,128)(2,1)}, u32[]{:S(2)}, u32[]{:S(2)}) collective-permute-start(bf16[48,3072]{1,0:T(8,128)(2,1)S(1)} %collective-permute-done.10.refs_9_.refs_15_), channel_id=1, source_target_pairs={{0,4},{4,0},{8,12},{12,8},{16,20},{20,16},{24,28},{28,24},{1,5},{5... | collective-permute-start | bytes 884744 | tf_op jit(solution)/shard_map/ppermute | solution.py:175
  45.9 15.2 %collective-permute-start.9 = (bf16[48,3072]{1,0:T(8,128)(2,1)S(1)}, bf16[48,3072]{1,0:T(8,128)(2,1)S(1)}, u32[]{:S(2)}, u32[]{:S(2)}) collective-permute-start(bf16[48,3072]{1,0:T(8,128)(2,1)S(1)} %pad_maximum_fusion.refs_8_), channel_id=1, source_target_pairs={{0,24},{4,28},{8,16},{12,20},{16,8},{20,12},{24,0},{28,4},{1,25},{... | collective-permute-start | bytes 884744 | tf_op jit(solution)/shard_map/ppermute | solution.py:175
  47.6 14.6 %collective-permute-start.8 = (bf16[48,3072]{1,0:T(8,128)(2,1)S(1)}, bf16[48,3072]{1,0:T(8,128)(2,1)S(1)}, u32[]{:S(2)}, u32[]{:S(2)}) collective-permute-start(bf16[48,3072]{1,0:T(8,128)(2,1)S(1)} %pad_maximum_fusion.refs_8_), channel_id=1, source_target_pairs={{0,16},{4,20},{8,24},{12,28},{16,0},{20,4},{24,8},{28,12},{1,17},{... | collective-permute-start | bytes 884744 | tf_op jit(solution)/shard_map/ppermute | solution.py:175
  48.2 14.1 %collective-permute-start.7 = (bf16[48,3072]{1,0:T(8,128)(2,1)S(1)}, bf16[48,3072]{1,0:T(8,128)(2,1)S(1)}, u32[]{:S(2)}, u32[]{:S(2)}) collective-permute-start(bf16[48,3072]{1,0:T(8,128)(2,1)S(1)} %pad_maximum_fusion.refs_8_), channel_id=1, source_target_pairs={{0,8},{4,12},{8,0},{12,4},{16,24},{20,28},{24,16},{28,20},{1,9},{5... | collective-permute-start | bytes 884744 | tf_op jit(solution)/shard_map/ppermute | solution.py:175
  62.3 10.1 %collective-permute-start.16 = (bf16[48,3072]{1,0:T(8,128)(2,1)S(1)}, bf16[48,3072]{1,0:T(8,128)(2,1)S(1)}, u32[]{:S(2)}, u32[]{:S(2)}) collective-permute-start(bf16[48,3072]{1,0:T(8,128)(2,1)S(1)} %pad_maximum_fusion.refs_8_), channel_id=1, source_target_pairs={{0,4},{4,0},{8,12},{12,8},{16,20},{20,16},{24,28},{28,24},{1,5},{5... | collective-permute-start | bytes 884744 | tf_op jit(solution)/shard_map/ppermute | solution.py:175
  62.3 10.1 %collective-permute-start.17 = (bf16[48,3072]{1,0:T(8,128)(2,1)S(1)}, bf16[48,3072]{1,0:T(8,128)(2,1)S(1)}, u32[]{:S(2)}, u32[]{:S(2)}) collective-permute-start(bf16[48,3072]{1,0:T(8,128)(2,1)S(1)} %collective-permute-done.7.refs_9_), channel_id=1, source_target_pairs={{0,4},{4,0},{8,12},{12,8},{16,20},{20,16},{24,28},{28,24},{1,5},{5... | collective-permute-start | bytes 884744 | tf_op jit(solution)/shard_map/ppermute | solution.py:175
  62.8 9.6 %collective-permute-start.18 = (bf16[48,3072]{1,0:T(8,128)(2,1)S(1)}, bf16[48,3072]{1,0:T(8,128)(2,1)S(1)}, u32[]{:S(2)}, u32[]{:S(2)}) collective-permute-start(bf16[48,3072]{1,0:T(8,128)(2,1)S(1)} %collective-permute-done.8.refs_10_), channel_id=1, source_target_pairs={{0,4},{4,0},{8,12},{12,8},{16,20},{20,16},{24,28},{28,24},{1,5},{5... | collective-permute-start | bytes 884744 | tf_op jit(solution)/shard_map/ppermute | solution.py:175
  62.8 9.6 %collective-permute-start.19 = (bf16[48,3072]{1,0:T(8,128)(2,1)S(1)}, bf16[48,3072]{1,0:T(8,128)(2,1)S(1)}, u32[]{:S(2)}, u32[]{:S(2)}) collective-permute-start(bf16[48,3072]{1,0:T(8,128)(2,1)S(1)} %collective-permute-done.9.refs_11_), channel_id=1, source_target_pairs={{0,4},{4,0},{8,12},{12,8},{16,20},{20,16},{24,28},{28,24},{1,5},{5... | collective-permute-start | bytes 884744 | tf_op jit(solution)/shard_map/ppermute | solution.py:175
  (7 other events, 15.2 us)

commit v5 on v4

v5 whole, which is shorter than its diff:
```python
import jax
import jax.numpy as jnp
from jax import lax
from jax.experimental import pallas as pl
from jax.experimental.pallas import tpu as pltpu
from jax.sharding import PartitionSpec as P

F32 = jnp.float32
BF16 = jnp.bfloat16
LANES = 128
ROWS = 256
FEATURES = 512
AXES = ("groups", "graph", "mp")


def dot(left, right):
    return jnp.dot(left, right, preferred_element_type=F32)


def dot_trans(left, right):
    return lax.dot_general(left, right, (((1,), (1,)), ((), ())), preferred_element_type=F32)


def shape(rows, columns, dtype):
    return jax.ShapeDtypeStruct((rows, columns), dtype)


class Far:
    def __init__(self, array):
        self.array = pltpu.with_memory_space_constraint(array, pltpu.HBM)


class Input:
    def __init__(self, copy, ref):
        self.copy, self.ref = copy, ref

    def __call__(self):
        if self.copy is not None:
            self.copy.wait()
            self.copy = None
        return self.ref


class Output:
    def __init__(self, ref, copy):
        self.ref, self.copy = ref, copy

    def send(self, value=None):
        if value is not None:
            self.ref[...] = value
        if self.copy is not None:
            self.copy.start()


def call(kernel, out_shape, *args, last=(), scratch=(), flops=0):
    groups = [a if isinstance(a, list) else [a] for a in args]
    flat = [a for group in groups for a in group]
    far = [isinstance(a, Far) for a in flat]
    arrays = [a.array if isinstance(a, Far) else a for a in flat]
    count, outs = len(arrays), len(out_shape)

    def body(*refs):
        ins, refs = refs[:count], refs[count:]
        out_refs, refs = refs[:outs], refs[outs:]
        places, refs = list(refs[: sum(far)]), refs[sum(far) :]
        results, refs = list(refs[: len(last)]), refs[len(last) :]
        sem_in, sem_out, refs = refs[0], refs[1], refs[2:]
        inputs = []
        for ref, away in zip(ins, far):
            copy = None
            if away:
                place = places.pop(0)
                copy = pltpu.make_async_copy(ref, place, sem_in.at[len(places)])
                copy.start()
                ref = place
            inputs.append(Input(copy, ref))
        outputs = []
        for i, ref in enumerate(out_refs):
            copy = None
            if i in last:
                place = results.pop(0)
                copy = pltpu.make_async_copy(place, ref, sem_out.at[len(results)])
                ref = place
            outputs.append(Output(ref, copy))
        given = []
        for arg, group in zip(args, groups):
            part, inputs = inputs[: len(group)], inputs[len(group) :]
            given.append(part if isinstance(arg, list) else part[0])
        kernel(*given, *outputs, *refs)
        for output in outputs:
            if output.copy is not None:
                output.copy.wait()

    vmem, hbm = pl.BlockSpec(memory_space=pltpu.VMEM), pl.BlockSpec(memory_space=pl.ANY)
    total = sum(a.size * a.dtype.itemsize for a in arrays)
    return pl.pallas_call(
        body,
        out_shape=out_shape,
        in_specs=[hbm if away else vmem for away in far],
        out_specs=[hbm if i in last else vmem for i in range(outs)],
        scratch_shapes=[pltpu.VMEM(a.shape, a.dtype) for a, away in zip(arrays, far) if away]
        + [pltpu.VMEM(out_shape[i].shape, out_shape[i].dtype) for i in last]
        + [pltpu.SemaphoreType.DMA((max(sum(far), 1),)), pltpu.SemaphoreType.DMA((max(len(last), 1),))]
        + list(scratch),
        name=kernel.__name__,
        cost_estimate=pl.CostEstimate(flops=flops, bytes_accessed=total, transcendentals=0),
        compiler_params=pltpu.CompilerParams(vmem_limit_bytes=24 * 1024 * 1024),
    )(*arrays)


def layers(blocks, which):
    low = which * 3 * FEATURES
    middle = low + 2 * FEATURES
    return (
        jnp.concatenate([block()[:, low:middle] for block in blocks], axis=0),
        jnp.concatenate([block()[:, middle : middle + FEATURES] for block in blocks], axis=0),
    )


def turned(first, select):
    return dot_trans(select, first).astype(BF16)


def prepare_kernel(grid, send, shards, *outs):
    pieces, outs = outs[:2], outs[2:]
    plane = lax.axis_index("groups") * lax.axis_size("graph") + lax.axis_index("graph")
    width = 3 * FEATURES
    for i in range(4):
        out, low = pieces[i // 2], i % 2 * width
        rows = out.ref.shape[0]
        base = plane * rows
        one, two = shards[2 * i](), shards[2 * i + 1]()
        hidden = one.shape[1]
        select = jnp.where(
            lax.broadcasted_iota(jnp.int32, (rows, hidden), 0) + base
            == lax.broadcasted_iota(jnp.int32, (rows, hidden), 1),
            1.0,
            0.0,
        ).astype(BF16)
        out.ref[:, low : low + 2 * FEATURES] = turned(one[...], select)
        out.ref[:, low + 2 * FEATURES : low + width] = two[pl.ds(pl.multiple_of(base, rows), rows), :]
    send_kernel(grid, send, *outs)


def own_kernel(shards, *outs):
    width = 3 * FEATURES
    for i in range(4):
        one, two = shards[2 * i](), shards[2 * i + 1]()
        hidden = one.shape[1]
        select = jnp.where(
            lax.broadcasted_iota(jnp.int32, (hidden, hidden), 0)
            == lax.broadcasted_iota(jnp.int32, (hidden, hidden), 1),
            1.0,
            0.0,
        ).astype(BF16)
        out, low = outs[i // 2], i % 2 * width
        out.ref[:, low : low + 2 * FEATURES] = turned(one[...], select)
        out.ref[:, low + 2 * FEATURES : low + width] = two[...]


def across(x, flip):
    planes = lax.axis_size("groups") * lax.axis_size("graph")
    return lax.ppermute(x, ("groups", "graph"), [(p, p ^ flip) for p in range(planes)])


def spread_along(piece):
    size = lax.axis_size("mp")
    return jnp.concatenate(
        [lax.ppermute(piece, "mp", [(m, (m + s) % size) for m in range(size)]) for s in range(1, size)]
    )


def start(grid_lat, grid_send, shards, tables):
    grid_rows, features = grid_lat.shape
    mp, graph = lax.axis_size("mp"), lax.axis_size("graph")
    step = stride(grid_send.shape[1])
    sent = [shape(grid_rows, mp * graph * step, BF16)] + [shape(graph * step, features, BF16)] * mp
    planes = lax.axis_size("groups") * graph
    hidden = shards[1].shape[0]
    if planes != 8 or mp != 4 or hidden != 128 or features != FEATURES:
        grid_t, *outgoing = call(send_kernel, sent, Far(grid_lat), Far(grid_send.T))
        rows = []
        for i in range(4):
            rows.append(lax.all_gather(shards[2 * i], "mp", axis=1, tiled=True).T)
            rows.append(lax.all_gather(shards[2 * i + 1], "mp", axis=0, tiled=True))
        enc, proc = jnp.concatenate(rows[:4], axis=1), jnp.concatenate(rows[4:], axis=1)
        return [enc], lambda after: ([proc], after), exchange(outgoing, step), grid_t, tables
    far = [Far(s) for s in shards]
    enc_piece, proc_piece, grid_t, *outgoing = call(
        prepare_kernel,
        [shape(hidden // planes, 6 * features, BF16)] * 2 + sent,
        Far(grid_lat),
        Far(grid_send.T),
        far,
    )
    enc_own, proc_own = call(own_kernel, [shape(hidden, 6 * features, BF16)] * 2, far)
    first = spread_along(enc_piece)
    first, enc_own, *tables = lax.optimization_barrier((first, enc_own, *tables))
    second = across(first, 1)
    proc_piece, second = lax.optimization_barrier((proc_piece, second))
    plane = [across(first, flip) for flip in (2, 4, 6)]
    enc = [enc_own, first, second] + plane + [across(block, 1) for block in plane]
    arrived = exchange(outgoing, step)
    first = spread_along(proc_piece)
    first, *plane = lax.optimization_barrier((first, *plane))
    enc[3:6] = plane
    blocks = [first] + [across(first, flip) for flip in (2, 4, 6)]

    def finish(after):
        *tied, after = lax.optimization_barrier((*blocks, after))
        return [proc_own] + tied + [across(block, 1) for block in tied], after

    return enc, finish, arrived, grid_t, tables


def forward(inputs, first, second):
    before = dot_trans(inputs, first)
    logistic = jax.nn.sigmoid(before)
    hidden = (before * logistic).astype(BF16)
    slope = logistic * (1.0 + before * (1.0 - logistic))
    summed = dot(hidden, second)
    centered = summed - jnp.mean(summed, axis=-1, keepdims=True)
    rescale = lax.rsqrt(jnp.mean(centered * centered, axis=-1, keepdims=True) + 1e-05)
    normed = centered * rescale
    return normed, slope.astype(BF16), normed.astype(BF16), rescale


def backward_hidden(incoming, slope, normed, rescale, second):
    normed = normed.astype(F32)
    g_out = (
        incoming
        - jnp.mean(incoming, axis=-1, keepdims=True)
        - normed * jnp.mean(incoming * normed, axis=-1, keepdims=True)
    ) * rescale
    return (dot_trans(g_out.astype(BF16), second) * slope.astype(F32)).astype(BF16)


def table(index_row, count):
    n = index_row.shape[1]
    return jnp.where(lax.broadcasted_iota(jnp.int32, (count, n), 0) == index_row, 1.0, 0.0)


def stride(capacity):
    return max(capacity, 16 // min(lax.axis_size("mp"), lax.axis_size("graph")))


def sent_at(peer, slot, step):
    mp, graph = lax.axis_size("mp"), lax.axis_size("graph")
    shift = (peer % mp + mp - lax.axis_index("mp")) % mp
    return (shift * graph + (peer // mp ^ lax.axis_index("graph"))) * step + slot


def arrived_at(peer, slot, step):
    mp = lax.axis_size("mp")
    shift = (lax.axis_index("mp") + mp - peer % mp) % mp
    return ((peer // mp ^ lax.axis_index("graph")) * mp + shift) * step + slot


def sent_row(index, step):
    width, count = index.shape
    index = index.astype(F32).T
    at = lax.broadcasted_iota(jnp.int32, (count, count * step), 1)
    peer = lax.broadcasted_iota(jnp.int32, (count, count * step), 0)
    row = jnp.zeros(at.shape, F32)
    for slot in range(width):
        row = jnp.where(sent_at(peer, slot, step) == at, index[:, slot : slot + 1] + 1.0, row)
    return jnp.sum(row, axis=0, keepdims=True).astype(jnp.int32) - 1


def stacked(blocks):
    return jnp.concatenate([block()[...] for block in blocks], axis=0)


def split(rows, outs):
    size = rows.shape[0] // len(outs)
    for i, out in enumerate(outs):
        out.ref[...] = rows[i * size : (i + 1) * size, :].astype(BF16)


def send_kernel(grid, send, table_out, *outgoing):
    count = table_out.ref.shape[1]
    one = table(sent_row(send()[...], count // send().shape[1]), grid().shape[0])
    split(dot(one.T.astype(BF16), grid()[...]), outgoing)
    table_out.ref[...] = one.astype(BF16)


def turn_kernel(blocks, *outs):
    rows = stacked(blocks)
    step = rows.shape[0] // (len(blocks) * len(outs))
    for j, out in enumerate(outs):
        row = lax.broadcasted_iota(jnp.int32, (out.ref.shape[0], rows.shape[0]), 0)
        at = lax.broadcasted_iota(jnp.int32, row.shape, 1)
        source = (row // step * len(outs) + j) * step + row % step
        out.ref[...] = dot(jnp.where(at == source, 1.0, 0.0).astype(BF16), rows).astype(BF16)


def tables_kernel(mesh, slot, recv_e, halo, sender, recv_p, *outs):
    mesh_rows = mesh().shape[0]
    peers = halo().shape[1]
    slot_step, halo_step = outs[0].ref.shape[0] // peers, outs[4].ref.shape[1] // peers
    capacity, halo_capacity = slot_step, halo().shape[0]
    slots = slot()[...]
    slots = arrived_at(slots // capacity, slots % capacity, slot_step)
    senders = sender()[...]
    remote = jnp.maximum(senders - mesh_rows, 0)
    remote = arrived_at(remote // halo_capacity, remote % halo_capacity, halo_step)
    senders = jnp.where(senders < mesh_rows, senders, mesh_rows + remote)
    rows = (slots, recv_e()[...], sent_row(halo()[...], halo_step), senders, recv_p()[...])
    for i, row in enumerate(rows):
        scatter, gather = outs[2 * i : 2 * i + 2]
        one = table(row, scatter.ref.shape[0])
        scatter.ref[...] = one.astype(BF16)
        gather.ref[...] = one.T.astype(BF16)
    outs[10].ref[...] = dot(outs[3].ref[...], mesh()[...]).astype(BF16)


def encode_kernel(
    recv_rows, arrived, slot_g, enc_t, mesh, weights, halo_g,
    one_out, slope_e, normed_e, scale_e, slope_n, normed_n, scale_n, *halo_out,
):
    rows_in = stacked(arrived)
    edges = slot_g().shape[0]
    first, second = layers(weights, 0)
    for low in range(0, edges, ROWS):
        rows = pl.ds(low, ROWS)
        sent = dot(slot_g()[rows, :], rows_in).astype(BF16)
        inputs = jnp.concatenate([sent, recv_rows()[rows, :]], axis=1)
        _, slope, normed, rescale = forward(inputs, first, second)
        slope_e.ref[rows, :] = slope
        normed_e.ref[rows, :] = normed
        scale_e.ref[rows, :] = jnp.broadcast_to(rescale, (ROWS, LANES))
    aggregate = dot(enc_t()[...], normed_e.ref[...]).astype(BF16)
    first, second = layers(weights, 1)
    own = mesh()[...]
    normed, slope, rounded, rescale = forward(
        jnp.concatenate([own, aggregate], axis=1), first, second
    )
    one = (own.astype(F32) + normed).astype(BF16)
    one_out.ref[...] = one
    split(dot(halo_g()[...], one), halo_out)
    slope_n.ref[...] = slope
    normed_n.ref[...] = rounded
    scale_n.ref[...] = jnp.broadcast_to(rescale, scale_n.ref.shape)


def process_kernel(
    cotangent_in, one_in, halo, sender_g, proc_g, weights, proc_t, sender_t, two, grad_one, *refs
):
    grad_halo, (slope_p, normed_p, scale_p, ga_p) = refs[:-4], refs[-4:]
    features = FEATURES
    one = one_in()[...]
    mesh_rows = one.shape[0]
    lookup = jnp.concatenate([one, stacked(halo)], axis=0)
    edges = sender_g().shape[0]
    first, second = layers(weights, 0)
    for low in range(0, edges, ROWS):
        rows = pl.ds(low, ROWS)
        sent = dot(sender_g()[rows, :], lookup).astype(BF16)
        got = dot(proc_g()[rows, :], one).astype(BF16)
        _, slope, normed, rescale = forward(jnp.concatenate([sent, got], axis=1), first, second)
        slope_p[rows, :] = slope
        normed_p[rows, :] = normed
        scale_p[rows, :] = jnp.broadcast_to(rescale, (ROWS, LANES))
    aggregate = dot(proc_t()[...], normed_p[...]).astype(BF16)
    first_n, second_n = layers(weights, 1)
    normed, slope, rounded, rescale = forward(
        jnp.concatenate([one, aggregate], axis=1), first_n, second_n
    )
    two.send((one.astype(F32) + normed).astype(BF16))
    cotangent = cotangent_in()[...].astype(F32)
    ga = backward_hidden(cotangent, slope, rounded, rescale, second_n)
    g_q = dot(ga, first_n)
    g_msg = g_q[:, features:].astype(BF16)
    for low in range(0, edges, ROWS):
        rows = pl.ds(low, ROWS)
        incoming = dot(proc_g()[rows, :], g_msg)
        ga_p[rows, :] = backward_hidden(
            incoming, slope_p[rows, :], normed_p[rows, :], scale_p[rows, 0:1], second
        )
    by_send = dot(sender_t()[...], ga_p[...]).astype(BF16)
    g_send = dot(by_send, first[:, :features])
    split(g_send[mesh_rows:, :], grad_halo)
    by_recv = dot(proc_t()[...], ga_p[...]).astype(BF16)
    g_recv = dot(by_recv, first[:, features:])
    grad_one.ref[...] = cotangent + g_q[:, :features] + g_recv + g_send[:mesh_rows, :]


def decode_kernel(
    back, halo_t, grad_in, slope_n, normed_n, scale_n, enc_g, slope_e, normed_e, scale_e,
    weights, slot_t, enc_t, mesh_grad, *refs
):
    grad_slots, ga_e = refs[:-1], refs[-1]
    features = FEATURES
    edges = enc_g().shape[0]
    grad_one = grad_in()[...] + dot(halo_t()[...], stacked(back))
    first_n, second_n = layers(weights, 1)
    ga = backward_hidden(grad_one, slope_n()[...], normed_n()[...], scale_n()[:, 0:1], second_n)
    g_n = dot(ga, first_n)
    g_edge = g_n[:, features:].astype(BF16)
    first, second = layers(weights, 0)
    for low in range(0, edges, ROWS):
        rows = pl.ds(low, ROWS)
        incoming = dot(enc_g()[rows, :], g_edge)
        ga_e[rows, :] = backward_hidden(
            incoming, slope_e()[rows, :], normed_e()[rows, :], scale_e()[rows, 0:1], second
        )
    by_recv = dot(enc_t()[...], ga_e[...]).astype(BF16)
    mesh_grad.send(grad_one + g_n[:, :features] + dot(by_recv, first[:, features:]))
    by_slot = dot(slot_t()[...], ga_e[...]).astype(BF16)
    split(dot(by_slot, first[:, :features]), grad_slots)


def grid_kernel(back, table_in, out):
    out.send(dot(table_in()[...], stacked(back)))


def along(block, shift):
    size = lax.axis_size("mp")
    if shift % size == 0:
        return block
    return lax.ppermute(block, "mp", [(m, (m + shift) % size) for m in range(size)])


def beside(block, flip):
    if flip == 0:
        return block
    return lax.ppermute(block, "graph", [(g, g ^ flip) for g in range(lax.axis_size("graph"))])


def turn(blocks, count, step):
    out = shape(len(blocks) * step, blocks[0].shape[1], BF16)
    return call(turn_kernel, [out] * count, list(blocks))


def exchange(blocks, step):
    blocks = turn([along(b, s) for s, b in enumerate(blocks)], lax.axis_size("graph"), step)
    return [beside(b, t) for t, b in enumerate(blocks)]


def exchange_back(blocks, step):
    blocks = turn([beside(b, t) for t, b in enumerate(blocks)], lax.axis_size("mp"), step)
    return [along(b, -s) for s, b in enumerate(blocks)]


def local(
    grid_lat,
    mesh_lat,
    cotangent,
    grid_send,
    g2m_slot,
    g2m_receiver,
    halo_send,
    mesh_sender,
    mesh_receiver,
    *shards,
):
    grid_rows, features = grid_lat.shape
    mesh_rows = mesh_lat.shape[0]
    edges = g2m_slot.shape[0]
    mesh_edges = mesh_sender.shape[0]
    mp, graph = lax.axis_size("mp"), lax.axis_size("graph")
    step, halo_step = stride(grid_send.shape[1]), stride(halo_send.shape[1])
    slots, halos = mp * graph * step, mp * graph * halo_step
    tables = call(
        tables_kernel,
        [
            shape(slots, edges, BF16),
            shape(edges, slots, BF16),
            shape(mesh_rows, edges, BF16),
            shape(edges, mesh_rows, BF16),
            shape(mesh_rows, halos, BF16),
            shape(halos, mesh_rows, BF16),
            shape(mesh_rows + halos, mesh_edges, BF16),
            shape(mesh_edges, mesh_rows + halos, BF16),
            shape(mesh_rows, mesh_edges, BF16),
            shape(mesh_edges, mesh_rows, BF16),
            shape(edges, features, BF16),
        ],
        Far(mesh_lat),
        Far(g2m_slot.reshape(1, edges)),
        Far(g2m_receiver.reshape(1, edges)),
        Far(halo_send.T),
        Far(mesh_sender.reshape(1, mesh_edges)),
        Far(mesh_receiver.reshape(1, mesh_edges)),
    )
    enc, finish, arrived, grid_t, tables = start(grid_lat, grid_send, shards, tables)
    slot_t, slot_g, enc_t, enc_g, halo_t, halo_g, sender_t, sender_g, proc_t, proc_g, recv_rows = tables
    saved = [
        shape(edges, features, BF16),
        shape(edges, features, BF16),
        shape(edges, LANES, F32),
        shape(mesh_rows, features, BF16),
        shape(mesh_rows, features, BF16),
        shape(mesh_rows, LANES, F32),
    ]
    mesh_one, slope_e, normed_e, scale_e, slope_n, normed_n, scale_n, *halo_out = call(
        encode_kernel,
        [shape(mesh_rows, features, BF16)] + saved + [shape(graph * halo_step, features, BF16)] * mp,
        recv_rows,
        arrived,
        slot_g,
        enc_t,
        Far(mesh_lat),
        enc,
        halo_g,
        flops=3 * 10**9,
    )
    proc, mesh_one = finish(mesh_one)
    halo_in = exchange(halo_out, halo_step)
    mesh_two, grad_one, *grad_halo = call(
        process_kernel,
        [shape(mesh_rows, features, BF16), shape(mesh_rows, features, F32)]
        + [shape(mp * halo_step, features, BF16)] * graph,
        Far(cotangent),
        mesh_one,
        halo_in,
        sender_g,
        proc_g,
        proc,
        proc_t,
        sender_t,
        last=(0,),
        flops=5 * 10**9,
        scratch=[
            pltpu.VMEM((mesh_edges, features), BF16),
            pltpu.VMEM((mesh_edges, features), BF16),
            pltpu.VMEM((mesh_edges, LANES), F32),
            pltpu.VMEM((mesh_edges, features), BF16),
        ],
    )
    halo_back = exchange_back(grad_halo, halo_step)
    mesh_grad, *grad_slots = call(
        decode_kernel,
        [shape(mesh_rows, features, F32)] + [shape(mp * step, features, BF16)] * graph,
        halo_back,
        halo_t,
        grad_one,
        slope_n,
        normed_n,
        scale_n,
        enc_g,
        slope_e,
        normed_e,
        scale_e,
        enc,
        slot_t,
        enc_t,
        last=(0,),
        flops=3 * 10**9,
        scratch=[pltpu.VMEM((edges, features), BF16)],
    )
    returned = exchange_back(grad_slots, step)
    (grid_grad,) = call(
        grid_kernel, [shape(grid_rows, features, F32)], returned, grid_t, last=(0,)
    )
    return (mesh_two, grid_grad, mesh_grad)


def solution(mesh):
    rows = P(AXES, None)
    flat = P(AXES)
    in_specs = (rows,) * 4 + (flat,) * 2 + (rows,) + (flat,) * 2 + (P(None, "mp"), P("mp", None)) * 4
    return jax.shard_map(
        local, mesh=mesh, in_specs=in_specs, out_specs=(rows,) * 3, check_vma=False
    )
```

time: 109 us -> 120 us (1.10)
  waiting for transfers between devices: 18.5 us -> 64.7 us
  blocking collectives: 27.3 us -> 0 us
  Pallas kernels: 32.3 us -> 19.7 us
  starting transfers between devices: 23.1 us -> 34.8 us
  local copies, waits for them, and re-layouts: 4.71 us -> 0 us
    ppermute x0 -> x24, waiting for transfers between devices: none -> 45.1 us  [the longest x12 33.7 us: along(): lax.ppermute(block, 'mp', [(m, (m + shift) % size) for m in range(size)])]
    all_to_all x3 -> x0, blocking collectives: 27.3 us -> none  [exchange(): lax.all_to_all(parts, PEERS, split_axis=0, concat_axis=0, tiled=True)]
    ppermute x0 -> x24, starting transfers between devices: none -> 15.7 us  [the longest x12 8.52 us: along(): lax.ppermute(block, 'mp', [(m, (m + shift) % size) for m in range(size)])]
    pallas_call x7 -> x11, Pallas kernels: 32.3 us -> 19.7 us  [call(): pl.pallas_call(body, out_shape=out_shape, in_specs=[hbm if away else vmem...]
    all_to_all x1 -> x0, starting transfers between devices: 6.13 us -> none  [exchange(): lax.all_to_all(parts, PEERS, split_axis=0, concat_axis=0, tiled=True)]
    unnamed x22 -> x0, local copies, waits for them, and re-layouts: 4.7 us -> none
    all_to_all x1 -> x0, waiting for transfers between devices: 3.72 us -> none  [exchange(): lax.all_to_all(parts, PEERS, split_axis=0, concat_axis=0, tiled=True)]
    ppermute x14, waiting for transfers between devices: 6.71 us -> 9.75 us  [across(): lax.ppermute(x, ('groups', 'graph'), [(p, p ^ flip) for p in range(planes)])]
  transfers between devices with their start and end apart: 21 -> 44, of which waited for: 6 -> 24; matrix products, arithmetic and copies ran while one was open for 1% -> 0% of each run, Pallas kernels for 11% -> 6%
where the time goes in v5:
time: 120 us
  waiting for transfers between devices  64.7 us (54%)
  starting transfers between devices  34.8 us (29%)
  Pallas kernels  19.7 us (16%)
    ppermute x12, waiting for transfers between devices, along(): lax.ppermute(block, 'mp', [(m, (m + shift) % size) for m in range(size)])  33.7 us
    pallas_call x11, Pallas kernels, call(): pl.pallas_call(body, out_shape=out_shape, in_specs=[hbm if away else vmem...  19.7 us
    ppermute x12, waiting for transfers between devices, beside(): lax.ppermute(block, 'graph', [(g, g ^ flip) for g in range(lax.axis_size(...  11.4 us
    ppermute x6, waiting for transfers between devices, spread_along(): lax.ppermute(piece, 'mp', [(m, (m + s) % size) for m in range(size)])  9.89 us
    ppermute x6, starting transfers between devices, spread_along(): lax.ppermute(piece, 'mp', [(m, (m + s) % size) for m in range(size)])  9.77 us
    ppermute x14, waiting for transfers between devices, across(): lax.ppermute(x, ('groups', 'graph'), [(p, p ^ flip) for p in range(planes)])  9.75 us
    ppermute x14, starting transfers between devices, across(): lax.ppermute(x, ('groups', 'graph'), [(p, p ^ flip) for p in range(planes)])  9.34 us
    ppermute x12, starting transfers between devices, along(): lax.ppermute(block, 'mp', [(m, (m + shift) % size) for m in range(size)])  8.52 us
  transfers between devices with their start and end apart: 44, of which 24 were waited for; matrix products, arithmetic and copies ran while one was open for 0% of the time, Pallas kernels for 6%

profile of v5, /device:TPU:0, one launch (start us, length us, event | category | flops | bytes accessed | tf_op | source)
XLA Modules:
  0.0 120.0 jit_solution(9563126463321828763)
XLA Ops:
  0.6 2.4 %prepare_kernel.1 = (bf16[16,3072]{1,0:T(8,128)(2,1)S(1)}, bf16[16,3072]{1,0:T(8,128)(2,1)S(1)}, bf16[512,64]{1,0:T(8,128)(2,1)S(1)}, bf16[16,512]{1,0:T(8,128)(...) custom-call(bf16[512,512]{1,0:T(8,128)(2,1)} %refs_0_.4, ...), custom_call_target="tpu_custom_call" | custom-call | bytes 2097408 | tf_op jit(solution)/shard_map/prepare_kernel/pallas_call | solution.py:96
  3.1 5.1 %collective-permute-start.2 = (bf16[16,3072]{1,0:T(8,128)(2,1)S(1)}, bf16[16,3072]{1,0:T(8,128)(2,1)S(1)}, u32[]{:S(2)}, u32[]{:S(2)}) collective-permute-start(bf16[16,3072]{1,0:T(8,128)(2,1)S(1)} %get-tuple-element.86), channel_id=1, source_target_pairs={{0,3},{1,0},{2,1},{3,2},{4,7},{5,4},{6,5},{7,6},{8,11},{9,8},{10,9... | collective-permute-start | bytes 294920 | tf_op jit(solution)/shard_map/ppermute | solution.py:169
  9.2 2.0 %own_kernel.1 = (bf16[128,3072]{1,0:T(8,128)(2,1)S(1)}, bf16[128,3072]{1,0:T(8,128)(2,1)S(1)}) custom-call(bf16[1024,128]{1,0:T(8,128)(2,1)} %refs_0_.5, bf16[128,512]{1,0:T(8,128)(2,1)} %refs_1_.1, bf16[1024,128]{1,0:T(8,128)(2,1)} %refs_2_.3, bf16[128,512]{1,0:T(8,128)(2,1)} %refs_3_.3, bf16[1024,128]{1,0:T(8,128)(2,1)} %refs_4_.3, ...), custom_call_target="tpu_custom_call" | custom-call | bytes 1572864 | tf_op jit(solution)/shard_map/own_kernel/pallas_call | solution.py:96
  12.9 4.0 %collective-permute-done.1 = bf16[16,3072]{1,0:T(8,128)(2,1)S(1)} collective-permute-done((bf16[16,3072]{1,0:T(8,128)(2,1)S(1)}, bf16[16,3072]{1,0:T(8,128)(2,1)S(1)}, u32[]{:S(2)}, u32[]{:S(2)}) %collective-permute-start.1) | collective-permute-done | bytes 98336 | tf_op jit(solution)/shard_map/ppermute | solution.py:169
  17.0 2.5 %collective-permute-start.9 = (bf16[48,3072]{1,0:T(8,128)(2,1)S(1)}, bf16[48,3072]{1,0:T(8,128)(2,1)S(1)}, u32[]{:S(2)}, u32[]{:S(2)}) collective-permute-start(bf16[48,3072]{1,0:T(8,128)(2,1)S(1)} %pad_maximum_fusion.refs_9_.refs_14_), channel_id=1, source_target_pairs={{0,24},{4,28},{8,16},{12,20},{16,8},{20,12},{24,0},{28,4},{1,25},{... | collective-permute-start | bytes 884744 | tf_op jit(solution)/shard_map/ppermute | solution.py:163
  20.9 5.2 %collective-permute-done.13.refs_1_ = bf16[16,512]{1,0:T(8,128)(2,1)S(1)} collective-permute-done((bf16[16,512]{1,0:T(8,128)(2,1)S(1)}, bf16[16,512]{1,0:T(8,128)(2,1)S(1)}, u32[]{:S(2)}, u32[]{:S(2)}) %collective-permute-start.13) | collective-permute-done | bytes 16416 | tf_op jit(solution)/shard_map/ppermute | solution.py:421
  26.6 4.2 %collective-permute-done.14.refs_2_ = bf16[16,512]{1,0:T(8,128)(2,1)S(1)} collective-permute-done((bf16[16,512]{1,0:T(8,128)(2,1)S(1)}, bf16[16,512]{1,0:T(8,128)(2,1)S(1)}, u32[]{:S(2)}, u32[]{:S(2)}) %collective-permute-start.14) | collective-permute-done | bytes 16416 | tf_op jit(solution)/shard_map/ppermute | solution.py:421
  30.9 3.6 %collective-permute-done.15.refs_3_ = bf16[16,512]{1,0:T(8,128)(2,1)S(1)} collective-permute-done((bf16[16,512]{1,0:T(8,128)(2,1)S(1)}, bf16[16,512]{1,0:T(8,128)(2,1)S(1)}, u32[]{:S(2)}, u32[]{:S(2)}) %collective-permute-start.15) | collective-permute-done | bytes 16416 | tf_op jit(solution)/shard_map/ppermute | solution.py:421
  34.8 2.0 %collective-permute-start.6 = (bf16[16,3072]{1,0:T(8,128)(2,1)S(1)}, bf16[16,3072]{1,0:T(8,128)(2,1)S(1)}, u32[]{:S(2)}, u32[]{:S(2)}) collective-permute-start(bf16[16,3072]{1,0:T(8,128)(2,1)S(1)} %get-tuple-element.100), channel_id=1, source_target_pairs={{0,3},{1,0},{2,1},{3,2},{4,7},{5,4},{6,5},{7,6},{8,11},{9,8},{10,9... | collective-permute-start | bytes 294920 | tf_op jit(solution)/shard_map/ppermute | solution.py:169
  40.6 5.9 %collective-permute-done.5 = bf16[16,3072]{1,0:T(8,128)(2,1)S(1)} collective-permute-done((bf16[16,3072]{1,0:T(8,128)(2,1)S(1)}, bf16[16,3072]{1,0:T(8,128)(2,1)S(1)}, u32[]{:S(2)}, u32[]{:S(2)}) %collective-permute-start.5) | collective-permute-done | bytes 98336 | tf_op jit(solution)/shard_map/ppermute | solution.py:169
  47.0 2.5 %collective-permute-start.12 = (bf16[48,3072]{1,0:T(8,128)(2,1)S(1)}, bf16[48,3072]{1,0:T(8,128)(2,1)S(1)}, u32[]{:S(2)}, u32[]{:S(2)}) collective-permute-start(bf16[48,3072]{1,0:T(8,128)(2,1)S(1)} %pad_maximum_fusion.1.refs_9_), channel_id=1, source_target_pairs={{0,24},{4,28},{8,16},{12,20},{16,8},{20,12},{24,0},{28,4},{1,25},{... | collective-permute-start | bytes 884744 | tf_op jit(solution)/shard_map/ppermute | solution.py:163
  50.6 3.0 %encode_kernel.1 = (bf16[256,512]{1,0:T(8,128)(2,1)S(1)}, bf16[512,512]{1,0:T(8,128)(2,1)S(1)}, bf16[512,512]{1,0:T(8,128)(2,1)S(1)}, f32[512,128]{1,0:T(8,128)S...) custom-call(bf16[512,512]{1,0:T(8,128)(2,1)S(1)} %get-tuple-element., ...), custom_call_target="tpu_custom_call" | custom-call | flops 3000000000 | bytes 4358144 | tf_op jit(solution)/shard_map/encode_kernel/pallas_call | solution.py:96
  53.6 4.3 %collective-permute-done.12.refs_12_ = bf16[48,3072]{1,0:T(8,128)(2,1)S(1)} collective-permute-done((bf16[48,3072]{1,0:T(8,128)(2,1)S(1)}, bf16[48,3072]{1,0:T(8,128)(2,1)S(1)}, u32[]{:S(2)}, u32[]{:S(2)}) %collective-permute-start.12) | collective-permute-done | bytes 294944 | tf_op jit(solution)/shard_map/ppermute | solution.py:163
  57.9 5.4 %collective-permute-done.11.refs_11_ = bf16[48,3072]{1,0:T(8,128)(2,1)S(1)} collective-permute-done((bf16[48,3072]{1,0:T(8,128)(2,1)S(1)}, bf16[48,3072]{1,0:T(8,128)(2,1)S(1)}, u32[]{:S(2)}, u32[]{:S(2)}) %collective-permute-start.11) | collective-permute-done | bytes 294944 | tf_op jit(solution)/shard_map/ppermute | solution.py:163
  65.0 4.9 %collective-permute-done.22.refs_1_ = bf16[16,512]{1,0:T(8,128)(2,1)S(1)} collective-permute-done((bf16[16,512]{1,0:T(8,128)(2,1)S(1)}, bf16[16,512]{1,0:T(8,128)(2,1)S(1)}, u32[]{:S(2)}, u32[]{:S(2)}) %collective-permute-start.22) | collective-permute-done | bytes 16416 | tf_op jit(solution)/shard_map/ppermute | solution.py:421
  70.7 3.9 %collective-permute-done.23.refs_2_ = bf16[16,512]{1,0:T(8,128)(2,1)S(1)} collective-permute-done((bf16[16,512]{1,0:T(8,128)(2,1)S(1)}, bf16[16,512]{1,0:T(8,128)(2,1)S(1)}, u32[]{:S(2)}, u32[]{:S(2)}) %collective-permute-start.23) | collective-permute-done | bytes 16416 | tf_op jit(solution)/shard_map/ppermute | solution.py:421
  74.7 3.6 %collective-permute-done.24.refs_3_ = bf16[16,512]{1,0:T(8,128)(2,1)S(1)} collective-permute-done((bf16[16,512]{1,0:T(8,128)(2,1)S(1)}, bf16[16,512]{1,0:T(8,128)(2,1)S(1)}, u32[]{:S(2)}, u32[]{:S(2)}) %collective-permute-start.24) | collective-permute-done | bytes 16416 | tf_op jit(solution)/shard_map/ppermute | solution.py:421
  81.2 2.2 %collective-permute-done.26.refs_4_ = bf16[16,512]{1,0:T(8,128)(2,1)S(1)} collective-permute-done((bf16[16,512]{1,0:T(8,128)(2,1)S(1)}, bf16[16,512]{1,0:T(8,128)(2,1)S(1)}, u32[]{:S(2)}, u32[]{:S(2)}) %collective-permute-start.26) | collective-permute-done | bytes 16416 | tf_op jit(solution)/shard_map/ppermute | solution.py:427
  83.6 3.2 %collective-permute-done.27.refs_5_ = bf16[16,512]{1,0:T(8,128)(2,1)S(1)} collective-permute-done((bf16[16,512]{1,0:T(8,128)(2,1)S(1)}, bf16[16,512]{1,0:T(8,128)(2,1)S(1)}, u32[]{:S(2)}, u32[]{:S(2)}) %collective-permute-start.27) | collective-permute-done | bytes 16416 | tf_op jit(solution)/shard_map/ppermute | solution.py:427
  86.8 5.3 %process_kernel.1 = (bf16[256,512]{1,0:T(8,128)(2,1)}, f32[256,512]{1,0:T(8,128)S(1)}, bf16[16,512]{1,0:T(8,128)(2,1)S(1)}, bf16[16,512]{1,0:T(8,128)(2,1)S(1)},...) custom-call(bf16[256,512]{1,0:T(8,128)(2,1)} %refs_0_.7, bf16[256,512]{1,0:T(8,128)(2,1)S(1)} %get-tuple-element.120.refs_1_, ...), custom_call_target="tpu_custom_call" | custom-call | flops 5000000000 | bytes 4915200 | tf_op jit(solution)/shard_map/process_kernel/pallas_call | solution.py:96
  94.1 2.0 %collective-permute-done.33.refs_2_ = bf16[16,512]{1,0:T(8,128)(2,1)S(1)} collective-permute-done((bf16[16,512]{1,0:T(8,128)(2,1)S(1)}, bf16[16,512]{1,0:T(8,128)(2,1)S(1)}, u32[]{:S(2)}, u32[]{:S(2)}) %collective-permute-start.33) | collective-permute-done | bytes 16416 | tf_op jit(solution)/shard_map/ppermute | solution.py:427
  97.0 2.0 %collective-permute-start.35 = (bf16[16,512]{1,0:T(8,128)(2,1)S(1)}, bf16[16,512]{1,0:T(8,128)(2,1)S(1)}, u32[]{:S(2)}, u32[]{:S(2)}) collective-permute-start(bf16[16,512]{1,0:T(8,128)(2,1)S(1)} %get-tuple-element.144), channel_id=1, source_target_pairs={{0,3},{1,0},{2,1},{3,2},{4,7},{5,4},{6,5},{7,6},{8,11},{9,8},{10,9... | collective-permute-start | bytes 49160 | tf_op jit(solution)/shard_map/ppermute | solution.py:421
  100.7 2.9 %collective-permute-done.36.refs_2_ = bf16[16,512]{1,0:T(8,128)(2,1)S(1)} collective-permute-done((bf16[16,512]{1,0:T(8,128)(2,1)S(1)}, bf16[16,512]{1,0:T(8,128)(2,1)S(1)}, u32[]{:S(2)}, u32[]{:S(2)}) %collective-permute-start.36) | collective-permute-done | bytes 16416 | tf_op jit(solution)/shard_map/ppermute | solution.py:421
  104.5 3.2 %decode_kernel.1 = (f32[256,512]{1,0:T(8,128)}, bf16[16,512]{1,0:T(8,128)(2,1)S(1)}, bf16[16,512]{1,0:T(8,128)(2,1)S(1)}, bf16[16,512]{1,0:T(8,128)(2,1)S(1)}, bf16[16,512]{1,0:T(8,128)(2,1)S(1)}) custom-call(bf16[16,512]{1,0:T(8,128)(2,1)S(1)} %get-tuple-element.143.refs_0_, bf16[16,512]{1,0:T(8,128)(2,1)S(1)} %collective-permute-done.35.refs_1_, ...), custom_call_target="tpu_custom_call" | custom-call | flops 3000000000 | bytes 6324224 | tf_op jit(solution)/shard_map/decode_kernel/pallas_call | solution.py:96
  (77 shorter events, 34.0 us)
Async XLA Ops:
  3.1 9.9 %collective-permute-start.2 = (bf16[16,3072]{1,0:T(8,128)(2,1)S(1)}, bf16[16,3072]{1,0:T(8,128)(2,1)S(1)}, u32[]{:S(2)}, u32[]{:S(2)}) collective-permute-start(bf16[16,3072]{1,0:T(8,128)(2,1)S(1)} %get-tuple-element.86), channel_id=1, source_target_pairs={{0,3},{1,0},{2,1},{3,2},{4,7},{5,4},{6,5},{7,6},{8,11},{9,8},{10,9... | collective-permute-start | bytes 294920 | tf_op jit(solution)/shard_map/ppermute | solution.py:169
  8.2 8.7 %collective-permute-start.1 = (bf16[16,3072]{1,0:T(8,128)(2,1)S(1)}, bf16[16,3072]{1,0:T(8,128)(2,1)S(1)}, u32[]{:S(2)}, u32[]{:S(2)}) collective-permute-start(bf16[16,3072]{1,0:T(8,128)(2,1)S(1)} %get-tuple-element.86), channel_id=1, source_target_pairs={{0,2},{1,3},{2,0},{3,1},{4,6},{5,7},{6,4},{7,5},{8,10},{9,11},{10,... | collective-permute-start | bytes 294920 | tf_op jit(solution)/shard_map/ppermute | solution.py:169
  8.2 8.7 %collective-permute-start = (bf16[16,3072]{1,0:T(8,128)(2,1)S(1)}, bf16[16,3072]{1,0:T(8,128)(2,1)S(1)}, u32[]{:S(2)}, u32[]{:S(2)}) collective-permute-start(bf16[16,3072]{1,0:T(8,128)(2,1)S(1)} %get-tuple-element.86), channel_id=1, source_target_pairs={{0,1},{1,2},{2,3},{3,0},{4,5},{5,6},{6,7},{7,4},{8,9},{9,10},{10,1... | collective-permute-start | bytes 294920 | tf_op jit(solution)/shard_map/ppermute | solution.py:169
  16.9 17.8 %collective-permute-start.3 = (bf16[48,3072]{1,0:T(8,128)(2,1)S(1)}, bf16[48,3072]{1,0:T(8,128)(2,1)S(1)}, u32[]{:S(2)}, u32[]{:S(2)}) collective-permute-start(bf16[48,3072]{1,0:T(8,128)(2,1)S(1)} %pad_maximum_fusion.refs_9_.refs_14_), channel_id=1, source_target_pairs={{0,4},{4,0},{8,12},{12,8},{16,20},{20,16},{24,28},{28,24},{1,5},{5... | collective-permute-start | bytes 884744 | tf_op jit(solution)/shard_map/ppermute | solution.py:163
  17.0 19.8 %collective-permute-start.9 = (bf16[48,3072]{1,0:T(8,128)(2,1)S(1)}, bf16[48,3072]{1,0:T(8,128)(2,1)S(1)}, u32[]{:S(2)}, u32[]{:S(2)}) collective-permute-start(bf16[48,3072]{1,0:T(8,128)(2,1)S(1)} %pad_maximum_fusion.refs_9_.refs_14_), channel_id=1, source_target_pairs={{0,24},{4,28},{8,16},{12,20},{16,8},{20,12},{24,0},{28,4},{1,25},{... | collective-permute-start | bytes 884744 | tf_op jit(solution)/shard_map/ppermute | solution.py:163
  19.5 18.9 %collective-permute-start.8 = (bf16[48,3072]{1,0:T(8,128)(2,1)S(1)}, bf16[48,3072]{1,0:T(8,128)(2,1)S(1)}, u32[]{:S(2)}, u32[]{:S(2)}) collective-permute-start(bf16[48,3072]{1,0:T(8,128)(2,1)S(1)} %pad_maximum_fusion.refs_9_.refs_14_), channel_id=1, source_target_pairs={{0,16},{4,20},{8,24},{12,28},{16,0},{20,4},{24,8},{28,12},{1,17},{... | collective-permute-start | bytes 884744 | tf_op jit(solution)/shard_map/ppermute | solution.py:163
  20.0 19.9 %collective-permute-start.7 = (bf16[48,3072]{1,0:T(8,128)(2,1)S(1)}, bf16[48,3072]{1,0:T(8,128)(2,1)S(1)}, u32[]{:S(2)}, u32[]{:S(2)}) collective-permute-start(bf16[48,3072]{1,0:T(8,128)(2,1)S(1)} %pad_maximum_fusion.refs_9_.refs_14_), channel_id=1, source_target_pairs={{0,8},{4,12},{8,0},{12,4},{16,24},{20,28},{24,16},{28,20},{1,9},{5... | collective-permute-start | bytes 884744 | tf_op jit(solution)/shard_map/ppermute | solution.py:163
  20.6 5.5 %collective-permute-start.13 = (bf16[16,512]{1,0:T(8,128)(2,1)S(1)}, bf16[16,512]{1,0:T(8,128)(2,1)S(1)}, u32[]{:S(2)}, u32[]{:S(2)}) collective-permute-start(bf16[16,512]{1,0:T(8,128)(2,1)S(1)} %get-tuple-element.104), channel_id=1, source_target_pairs={{0,1},{1,2},{2,3},{3,0},{4,5},{5,6},{6,7},{7,4},{8,9},{9,10},{10,1... | collective-permute-start | bytes 49160 | tf_op jit(solution)/shard_map/ppermute | solution.py:421
  34.8 5.2 %collective-permute-start.6 = (bf16[16,3072]{1,0:T(8,128)(2,1)S(1)}, bf16[16,3072]{1,0:T(8,128)(2,1)S(1)}, u32[]{:S(2)}, u32[]{:S(2)}) collective-permute-start(bf16[16,3072]{1,0:T(8,128)(2,1)S(1)} %get-tuple-element.100), channel_id=1, source_target_pairs={{0,3},{1,0},{2,1},{3,2},{4,7},{5,4},{6,5},{7,6},{8,11},{9,8},{10,9... | collective-permute-start | bytes 294920 | tf_op jit(solution)/shard_map/ppermute | solution.py:169
  36.8 9.7 %collective-permute-start.5 = (bf16[16,3072]{1,0:T(8,128)(2,1)S(1)}, bf16[16,3072]{1,0:T(8,128)(2,1)S(1)}, u32[]{:S(2)}, u32[]{:S(2)}) collective-permute-start(bf16[16,3072]{1,0:T(8,128)(2,1)S(1)} %get-tuple-element.100), channel_id=1, source_target_pairs={{0,2},{1,3},{2,0},{3,1},{4,6},{5,7},{6,4},{7,5},{8,10},{9,11},{10,... | collective-permute-start | bytes 294920 | tf_op jit(solution)/shard_map/ppermute | solution.py:169
  36.8 9.7 %collective-permute-start.4 = (bf16[16,3072]{1,0:T(8,128)(2,1)S(1)}, bf16[16,3072]{1,0:T(8,128)(2,1)S(1)}, u32[]{:S(2)}, u32[]{:S(2)}) collective-permute-start(bf16[16,3072]{1,0:T(8,128)(2,1)S(1)} %get-tuple-element.100), channel_id=1, source_target_pairs={{0,1},{1,2},{2,3},{3,0},{4,5},{5,6},{6,7},{7,4},{8,9},{9,10},{10,1... | collective-permute-start | bytes 294920 | tf_op jit(solution)/shard_map/ppermute | solution.py:169
  38.5 8.6 %collective-permute-start.17 = (bf16[16,512]{1,0:T(8,128)(2,1)S(1)}, bf16[16,512]{1,0:T(8,128)(2,1)S(1)}, u32[]{:S(2)}, u32[]{:S(2)}) collective-permute-start(bf16[16,512]{1,0:T(8,128)(2,1)S(1)} %get-tuple-element.109), channel_id=1, source_target_pairs={{0,8},{4,12},{8,0},{12,4},{1,9},{5,13},{9,1},{13,5},{2,10},{6,14},... | collective-permute-start | bytes 49160 | tf_op jit(solution)/shard_map/ppermute | solution.py:427
  39.9 9.6 %collective-permute-start.18 = (bf16[16,512]{1,0:T(8,128)(2,1)S(1)}, bf16[16,512]{1,0:T(8,128)(2,1)S(1)}, u32[]{:S(2)}, u32[]{:S(2)}) collective-permute-start(bf16[16,512]{1,0:T(8,128)(2,1)S(1)} %get-tuple-element.110), channel_id=1, source_target_pairs={{0,12},{4,8},{8,4},{12,0},{1,13},{5,9},{9,5},{13,1},{2,14},{6,10},... | collective-permute-start | bytes 49160 | tf_op jit(solution)/shard_map/ppermute | solution.py:427
  40.0 10.1 %collective-permute-start.21 = (bf16[48,3072]{1,0:T(8,128)(2,1)S(1)}, bf16[48,3072]{1,0:T(8,128)(2,1)S(1)}, u32[]{:S(2)}, u32[]{:S(2)}) collective-permute-start(bf16[48,3072]{1,0:T(8,128)(2,1)S(1)} %collective-permute-done.9.refs_13_.refs_18_), channel_id=1, source_target_pairs={{0,4},{4,0},{8,12},{12,8},{16,20},{20,16},{24,28},{28,24},{1,5},{5... | collective-permute-start | bytes 884744 | tf_op jit(solution)/shard_map/ppermute | solution.py:163
  47.0 10.9 %collective-permute-start.12 = (bf16[48,3072]{1,0:T(8,128)(2,1)S(1)}, bf16[48,3072]{1,0:T(8,128)(2,1)S(1)}, u32[]{:S(2)}, u32[]{:S(2)}) collective-permute-start(bf16[48,3072]{1,0:T(8,128)(2,1)S(1)} %pad_maximum_fusion.1.refs_9_), channel_id=1, source_target_pairs={{0,24},{4,28},{8,16},{12,20},{16,8},{20,12},{24,0},{28,4},{1,25},{... | collective-permute-start | bytes 884744 | tf_op jit(solution)/shard_map/ppermute | solution.py:163
  49.6 13.7 %collective-permute-start.11 = (bf16[48,3072]{1,0:T(8,128)(2,1)S(1)}, bf16[48,3072]{1,0:T(8,128)(2,1)S(1)}, u32[]{:S(2)}, u32[]{:S(2)}) collective-permute-start(bf16[48,3072]{1,0:T(8,128)(2,1)S(1)} %pad_maximum_fusion.1.refs_9_), channel_id=1, source_target_pairs={{0,16},{4,20},{8,24},{12,28},{16,0},{20,4},{24,8},{28,12},{1,17},{... | collective-permute-start | bytes 884744 | tf_op jit(solution)/shard_map/ppermute | solution.py:163
  50.1 13.3 %collective-permute-start.10 = (bf16[48,3072]{1,0:T(8,128)(2,1)S(1)}, bf16[48,3072]{1,0:T(8,128)(2,1)S(1)}, u32[]{:S(2)}, u32[]{:S(2)}) collective-permute-start(bf16[48,3072]{1,0:T(8,128)(2,1)S(1)} %pad_maximum_fusion.1.refs_9_), channel_id=1, source_target_pairs={{0,8},{4,12},{8,0},{12,4},{16,24},{20,28},{24,16},{28,20},{1,9},{5... | collective-permute-start | bytes 884744 | tf_op jit(solution)/shard_map/ppermute | solution.py:163
  63.4 23.4 %collective-permute-start.28 = (bf16[48,3072]{1,0:T(8,128)(2,1)S(1)}, bf16[48,3072]{1,0:T(8,128)(2,1)S(1)}, u32[]{:S(2)}, u32[]{:S(2)}) collective-permute-start(bf16[48,3072]{1,0:T(8,128)(2,1)S(1)} %pad_maximum_fusion.1.refs_9_), channel_id=1, source_target_pairs={{0,4},{4,0},{8,12},{12,8},{16,20},{20,16},{24,28},{28,24},{1,5},{5... | collective-permute-start | bytes 884744 | tf_op jit(solution)/shard_map/ppermute | solution.py:163
  63.4 23.4 %collective-permute-start.29 = (bf16[48,3072]{1,0:T(8,128)(2,1)S(1)}, bf16[48,3072]{1,0:T(8,128)(2,1)S(1)}, u32[]{:S(2)}, u32[]{:S(2)}) collective-permute-start(bf16[48,3072]{1,0:T(8,128)(2,1)S(1)} %collective-permute-done.10.refs_10_), channel_id=1, source_target_pairs={{0,4},{4,0},{8,12},{12,8},{16,20},{20,16},{24,28},{28,24},{1,5},{5... | collective-permute-start | bytes 884744 | tf_op jit(solution)/shard_map/ppermute | solution.py:163
  63.9 22.9 %collective-permute-start.30 = (bf16[48,3072]{1,0:T(8,128)(2,1)S(1)}, bf16[48,3072]{1,0:T(8,128)(2,1)S(1)}, u32[]{:S(2)}, u32[]{:S(2)}) collective-permute-start(bf16[48,3072]{1,0:T(8,128)(2,1)S(1)} %collective-permute-done.11.refs_11_), channel_id=1, source_target_pairs={{0,4},{4,0},{8,12},{12,8},{16,20},{20,16},{24,28},{28,24},{1,5},{5... | collective-permute-start | bytes 884744 | tf_op jit(solution)/shard_map/ppermute | solution.py:163
  63.9 22.9 %collective-permute-start.31 = (bf16[48,3072]{1,0:T(8,128)(2,1)S(1)}, bf16[48,3072]{1,0:T(8,128)(2,1)S(1)}, u32[]{:S(2)}, u32[]{:S(2)}) collective-permute-start(bf16[48,3072]{1,0:T(8,128)(2,1)S(1)} %collective-permute-done.12.refs_12_), channel_id=1, source_target_pairs={{0,4},{4,0},{8,12},{12,8},{16,20},{20,16},{24,28},{28,24},{1,5},{5... | collective-permute-start | bytes 884744 | tf_op jit(solution)/shard_map/ppermute | solution.py:163
  64.4 5.5 %collective-permute-start.22 = (bf16[16,512]{1,0:T(8,128)(2,1)S(1)}, bf16[16,512]{1,0:T(8,128)(2,1)S(1)}, u32[]{:S(2)}, u32[]{:S(2)}) collective-permute-start(bf16[16,512]{1,0:T(8,128)(2,1)S(1)} %get-tuple-element.122), channel_id=1, source_target_pairs={{0,1},{1,2},{2,3},{3,0},{4,5},{5,6},{6,7},{7,4},{8,9},{9,10},{10,1... | collective-permute-start | bytes 49160 | tf_op jit(solution)/shard_map/ppermute | solution.py:421
  99.0 5.5 %collective-permute-start.37 = (bf16[16,512]{1,0:T(8,128)(2,1)S(1)}, bf16[16,512]{1,0:T(8,128)(2,1)S(1)}, u32[]{:S(2)}, u32[]{:S(2)}) collective-permute-start(bf16[16,512]{1,0:T(8,128)(2,1)S(1)} %get-tuple-element.146), channel_id=1, source_target_pairs={{0,1},{1,2},{2,3},{3,0},{4,5},{5,6},{6,7},{7,4},{8,9},{9,10},{10,1... | collective-permute-start | bytes 49160 | tf_op jit(solution)/shard_map/ppermute | solution.py:421
  113.2 5.5 %collective-permute-start.43 = (bf16[16,512]{1,0:T(8,128)(2,1)S(1)}, bf16[16,512]{1,0:T(8,128)(2,1)S(1)}, u32[]{:S(2)}, u32[]{:S(2)}) collective-permute-start(bf16[16,512]{1,0:T(8,128)(2,1)S(1)} %get-tuple-element.164), channel_id=1, source_target_pairs={{0,1},{1,2},{2,3},{3,0},{4,5},{5,6},{6,7},{7,4},{8,9},{9,10},{10,1... | collective-permute-start | bytes 49160 | tf_op jit(solution)/shard_map/ppermute | solution.py:421
  (20 other events, 70.0 us)

commit v6 on v5

--- a/solution.py
+++ b/solution.py
@@ -121,14 +121,12 @@
     return dot_trans(select, first).astype(BF16)
 
 
-def prepare_kernel(grid, send, shards, *outs):
-    pieces, outs = outs[:2], outs[2:]
+def prepare_kernel(grid, send, shards, proc_piece, table_out, kept, *messages):
     plane = lax.axis_index("groups") * lax.axis_size("graph") + lax.axis_index("graph")
     width = 3 * FEATURES
+    rows = proc_piece.ref.shape[0]
+    base = plane * rows
     for i in range(4):
-        out, low = pieces[i // 2], i % 2 * width
-        rows = out.ref.shape[0]
-        base = plane * rows
         one, two = shards[2 * i](), shards[2 * i + 1]()
         hidden = one.shape[1]
         select = jnp.where(
@@ -137,9 +135,33 @@
             1.0,
             0.0,
         ).astype(BF16)
-        out.ref[:, low : low + 2 * FEATURES] = turned(one[...], select)
-        out.ref[:, low + 2 * FEATURES : low + width] = two[pl.ds(pl.multiple_of(base, rows), rows), :]
-    send_kernel(grid, send, *outs)
+        low = i % 2 * width
+        first = turned(one[...], select)
+        second = two[pl.ds(pl.multiple_of(base, rows), rows), :]
+        for out in (proc_piece,) if i // 2 else messages:
+            out.ref[:, low : low + 2 * FEATURES] = first
+            out.ref[:, low + 2 * FEATURES : low + width] = second
+    outgoing = send_rows(grid, send, table_out)
+    size = kept.ref.shape[0]
+    kept.ref[...] = outgoing[:size, :].astype(BF16)
+    for i, out in enumerate(messages):
+        out.ref[:, 2 * width :] = outgoing[(i + 1) * size : (i + 2) * size, :].astype(BF16)
+
+
+def join_kernel(kept, messages, near, block, both):
+    width = 6 * FEATURES
+    weights = jnp.concatenate([m()[:, :width] for m in messages], axis=0)
+    rows = jnp.concatenate([kept()[...]] + [m()[:, width:] for m in messages], axis=0)
+    step = rows.shape[0] // 16
+    block.ref[...] = weights
+    both.ref[:, :width] = weights
+    size = near.ref.shape[0]
+    for j in range(4):
+        moved = dot(turn_table(4, 4, step, j), rows).astype(BF16)
+        if j == 0:
+            near.ref[...] = moved
+        else:
+            both.ref[(j - 1) * size : j * size, width:] = moved
 
 
 def own_kernel(shards, *outs):
@@ -163,13 +185,6 @@
     return lax.ppermute(x, ("groups", "graph"), [(p, p ^ flip) for p in range(planes)])
 
 
-def spread_along(piece):
-    size = lax.axis_size("mp")
-    return jnp.concatenate(
-        [lax.ppermute(piece, "mp", [(m, (m + s) % size) for m in range(size)]) for s in range(1, size)]
-    )
-
-
 def start(grid_lat, grid_send, shards, tables):
     grid_rows, features = grid_lat.shape
     mp, graph = lax.axis_size("mp"), lax.axis_size("graph")
@@ -184,33 +199,54 @@
             rows.append(lax.all_gather(shards[2 * i], "mp", axis=1, tiled=True).T)
             rows.append(lax.all_gather(shards[2 * i + 1], "mp", axis=0, tiled=True))
         enc, proc = jnp.concatenate(rows[:4], axis=1), jnp.concatenate(rows[4:], axis=1)
-        return [enc], lambda after: ([proc], after), exchange(outgoing, step), grid_t, tables
+        arrived = exchange(outgoing, step)
+        return [enc], lambda one, moved: [proc], arrived, grid_t, tables
     far = [Far(s) for s in shards]
-    enc_piece, proc_piece, grid_t, *outgoing = call(
+    piece = hidden // planes
+    width = 6 * features
+    proc_piece, grid_t, kept, *messages = call(
         prepare_kernel,
-        [shape(hidden // planes, 6 * features, BF16)] * 2 + sent,
+        [shape(piece, width, BF16)] + sent[:2] + [shape(piece, width + features, BF16)] * 3,
         Far(grid_lat),
         Far(grid_send.T),
         far,
     )
-    enc_own, proc_own = call(own_kernel, [shape(hidden, 6 * features, BF16)] * 2, far)
-    first = spread_along(enc_piece)
-    first, enc_own, *tables = lax.optimization_barrier((first, enc_own, *tables))
-    second = across(first, 1)
-    proc_piece, second = lax.optimization_barrier((proc_piece, second))
-    plane = [across(first, flip) for flip in (2, 4, 6)]
-    enc = [enc_own, first, second] + plane + [across(block, 1) for block in plane]
-    arrived = exchange(outgoing, step)
-    first = spread_along(proc_piece)
-    first, *plane = lax.optimization_barrier((first, *plane))
-    enc[3:6] = plane
-    blocks = [first] + [across(first, flip) for flip in (2, 4, 6)]
-
-    def finish(after):
-        *tied, after = lax.optimization_barrier((*blocks, after))
-        return [proc_own] + tied + [across(block, 1) for block in tied], after
+    enc_own, proc_own = call(own_kernel, [shape(hidden, width, BF16)] * 2, far)
+    messages = [along(m, i + 1) for i, m in enumerate(messages)]
+    kept, enc_own, *tables = lax.optimization_barrier((kept, enc_own, *tables))
+    rows = mp * step
+    near, first, both = call(
+        join_kernel,
+        [shape(rows, features, BF16), shape(3 * piece, width, BF16), shape(3 * rows, width + features, BF16)],
+        kept,
+        messages,
+    )
+    core, x, y = across(both, 1), across(both, 2), across(first, 4)
+    proc_piece, _ = lax.optimization_barrier((proc_piece, core))
+    low, high = relay(x, y)
+    x_core, y_core = across(x, 1), across(y, 1)
+    parts = [along(proc_piece, s) for s in (1, 2, 3)]
+    *parts, _, _ = lax.optimization_barrier((*parts, low, high))
+    far_corner = jnp.concatenate([low, high], axis=1)
+    enc = [enc_own, first, core, x, y, x_core, y_core, far_corner, across(far_corner, 1)]
+    arrived = [near, core, x, x_core]
+    proc_first = jnp.concatenate(parts)
+    proc_core, proc_x, proc_y = [across(proc_first, flip) for flip in (1, 2, 4)]
+
+    def finish(one, moved):
+        x, y, _ = lax.optimization_barrier((proc_x, proc_y, one))
+        low, high = relay(x, y)
+        x, y, *_ = lax.optimization_barrier((x, y, *moved))
+        corner = jnp.concatenate([low, high], axis=1)
+        blocks = [proc_own, proc_first, proc_core, x, y, across(x, 1), across(y, 1)]
+        return blocks + [corner, across(corner, 1)]
 
     return enc, finish, arrived, grid_t, tables
+
+
+def relay(x, y):
+    half = 3 * FEATURES
+    return across(x[:, :half], 4), across(y[:, half : 2 * half], 2)
 
 
 def forward(inputs, first, second):
@@ -277,21 +313,29 @@
         out.ref[...] = rows[i * size : (i + 1) * size, :].astype(BF16)
 
 
-def send_kernel(grid, send, table_out, *outgoing):
+def send_rows(grid, send, table_out):
     count = table_out.ref.shape[1]
     one = table(sent_row(send()[...], count // send().shape[1]), grid().shape[0])
-    split(dot(one.T.astype(BF16), grid()[...]), outgoing)
     table_out.ref[...] = one.astype(BF16)
+    return dot(one.T.astype(BF16), grid()[...])
+
+
+def send_kernel(grid, send, table_out, *outgoing):
+    split(send_rows(grid, send, table_out), outgoing)
+
+
+def turn_table(sources, targets, step, j):
+    row = lax.broadcasted_iota(jnp.int32, (sources * step, sources * targets * step), 0)
+    at = lax.broadcasted_iota(jnp.int32, row.shape, 1)
+    source = (row // step * targets + j) * step + row % step
+    return jnp.where(at == source, 1.0, 0.0).astype(BF16)
 
 
 def turn_kernel(blocks, *outs):
     rows = stacked(blocks)
     step = rows.shape[0] // (len(blocks) * len(outs))
     for j, out in enumerate(outs):
-        row = lax.broadcasted_iota(jnp.int32, (out.ref.shape[0], rows.shape[0]), 0)
-        at = lax.broadcasted_iota(jnp.int32, row.shape, 1)
-        source = (row // step * len(outs) + j) * step + row % step
-        out.ref[...] = dot(jnp.where(at == source, 1.0, 0.0).astype(BF16), rows).astype(BF16)
+        out.ref[...] = dot(turn_table(len(blocks), len(outs), step, j), rows).astype(BF16)
 
 
 def tables_kernel(mesh, slot, recv_e, halo, sender, recv_p, *outs):
@@ -314,11 +358,22 @@
     outs[10].ref[...] = dot(outs[3].ref[...], mesh()[...]).astype(BF16)
 
 
+def arrived_rows(blocks):
+    size = blocks[0]().shape[0]
+    rows = [blocks[0]()[...]]
+    for t, block in enumerate(blocks[1:]):
+        if block().shape[1] == FEATURES:
+            rows.append(block()[...])
+        else:
+            rows.append(block()[t * size : (t + 1) * size, 6 * FEATURES :])
+    return jnp.concatenate(rows, axis=0)
+
+
 def encode_kernel(
     recv_rows, arrived, slot_g, enc_t, mesh, weights, halo_g,
     one_out, slope_e, normed_e, scale_e, slope_n, normed_n, scale_n, *halo_out,
 ):
-    rows_in = stacked(arrived)
+    rows_in = arrived_rows(arrived)
     edges = slot_g().shape[0]
     first, second = layers(weights, 0)
     for low in range(0, edges, ROWS):
@@ -433,7 +488,14 @@
 
 
 def exchange(blocks, step):
-    blocks = turn([along(b, s) for s, b in enumerate(blocks)], lax.axis_size("graph"), step)
+    return second_level(first_level(blocks, step))
+
+
+def first_level(blocks, step):
+    return turn([along(b, s) for s, b in enumerate(blocks)], lax.axis_size("graph"), step)
+
+
+def second_level(blocks):
     return [beside(b, t) for t, b in enumerate(blocks)]
 
 
@@ -505,8 +567,9 @@
         halo_g,
         flops=3 * 10**9,
     )
-    proc, mesh_one = finish(mesh_one)
-    halo_in = exchange(halo_out, halo_step)
+    moved = first_level(halo_out, halo_step)
+    proc = finish(mesh_one, moved)
+    halo_in = second_level(moved)
     mesh_two, grad_one, *grad_halo = call(
         process_kernel,
         [shape(mesh_rows, features, BF16), shape(mesh_rows, features, F32)]

time: 120 us -> 103 us (0.86)
  waiting for transfers between devices: 64.7 us -> 44 us
  starting transfers between devices: 34.8 us -> 37.7 us
    ppermute x12 -> x15, starting transfers between devices: 8.52 us -> 21.5 us  [along(): lax.ppermute(block, 'mp', [(m, (m + shift) % size) for m in range(size)])]
    ppermute x12 -> x15, waiting for transfers between devices: 33.7 us -> 21.7 us  [along(): lax.ppermute(block, 'mp', [(m, (m + shift) % size) for m in range(size)])]
    ppermute x6 -> x0, waiting for transfers between devices: 9.89 us -> none  [spread_along(): lax.ppermute(piece, 'mp', [(m, (m + s) % size) for m in range(size)])]
    ppermute x6 -> x0, starting transfers between devices: 9.77 us -> none  [spread_along(): lax.ppermute(piece, 'mp', [(m, (m + s) % size) for m in range(size)])]
    ppermute x14 -> x16, waiting for transfers between devices: 9.75 us -> 14.1 us  [across(): lax.ppermute(x, ('groups', 'graph'), [(p, p ^ flip) for p in range(planes)])]
    ppermute x12 -> x9, waiting for transfers between devices: 11.4 us -> 8.15 us  [beside(): lax.ppermute(block, 'graph', [(g, g ^ flip) for g in range(lax.axis_size(...]
    ppermute x12 -> x9, starting transfers between devices: 7.14 us -> 5.3 us  [beside(): lax.ppermute(block, 'graph', [(g, g ^ flip) for g in range(lax.axis_size(...]
    ppermute x14 -> x16, starting transfers between devices: 9.34 us -> 10.9 us  [across(): lax.ppermute(x, ('groups', 'graph'), [(p, p ^ flip) for p in range(planes)])]
  transfers between devices with their start and end apart: 44 -> 40, of which waited for: 24 -> 21; matrix products, arithmetic and copies ran while one was open for 0% -> 0% of each run, Pallas kernels for 6% -> 7%
where the time goes in v6:
time: 103 us
  waiting for transfers between devices  44 us (43%)
  starting transfers between devices  37.7 us (37%)
  Pallas kernels  20.4 us (20%)
    ppermute x15, waiting for transfers between devices, along(): lax.ppermute(block, 'mp', [(m, (m + shift) % size) for m in range(size)])  21.7 us
    ppermute x15, starting transfers between devices, along(): lax.ppermute(block, 'mp', [(m, (m + shift) % size) for m in range(size)])  21.5 us
    pallas_call x11, Pallas kernels, call(): pl.pallas_call(body, out_shape=out_shape, in_specs=[hbm if away else vmem...  20.4 us
    ppermute x16, waiting for transfers between devices, across(): lax.ppermute(x, ('groups', 'graph'), [(p, p ^ flip) for p in range(planes)])  14.1 us
    ppermute x16, starting transfers between devices, across(): lax.ppermute(x, ('groups', 'graph'), [(p, p ^ flip) for p in range(planes)])  10.9 us
    ppermute x9, waiting for transfers between devices, beside(): lax.ppermute(block, 'graph', [(g, g ^ flip) for g in range(lax.axis_size(...  8.15 us
    ppermute x9, starting transfers between devices, beside(): lax.ppermute(block, 'graph', [(g, g ^ flip) for g in range(lax.axis_size(...  5.3 us
  transfers between devices with their start and end apart: 40, of which 21 were waited for; matrix products, arithmetic and copies ran while one was open for 0% of the time, Pallas kernels for 7%

profile of v6, /device:TPU:0, one launch (start us, length us, event | category | flops | bytes accessed | tf_op | source)
XLA Modules:
  0.0 103.0 jit_solution(15445094730361801122)
XLA Ops:
  0.6 2.4 %prepare_kernel.1 = (bf16[16,3072]{1,0:T(8,128)(2,1)S(1)}, bf16[512,64]{1,0:T(8,128)(2,1)S(1)}, bf16[16,512]{1,0:T(8,128)(2,1)S(1)}, bf16[16,3584]{1,0:T(8,128)(...) custom-call(bf16[512,512]{1,0:T(8,128)(2,1)} %refs_0_.4, s32[4,16]{1,0:T(4,128)} %bitcast.6, ...), custom_call_target="tpu_custom_call" | custom-call | bytes 2097408 | tf_op jit(solution)/shard_map/prepare_kernel/pallas_call | solution.py:96
  3.1 3.1 %collective-permute-start = (bf16[16,3584]{1,0:T(8,128)(2,1)S(1)}, bf16[16,3584]{1,0:T(8,128)(2,1)S(1)}, u32[]{:S(2)}, u32[]{:S(2)}) collective-permute-start(bf16[16,3584]{1,0:T(8,128)(2,1)S(1)} %get-tuple-element.95), channel_id=1, source_target_pairs={{0,1},{1,2},{2,3},{3,0},{4,5},{5,6},{6,7},{7,4},{8,9},{9,10},{10,1... | collective-permute-start | bytes 344072 | tf_op jit(solution)/shard_map/ppermute | solution.py:476
  6.1 2.6 %collective-permute-start.1 = (bf16[16,3584]{1,0:T(8,128)(2,1)S(1)}, bf16[16,3584]{1,0:T(8,128)(2,1)S(1)}, u32[]{:S(2)}, u32[]{:S(2)}) collective-permute-start(bf16[16,3584]{1,0:T(8,128)(2,1)S(1)} %get-tuple-element.96), channel_id=1, source_target_pairs={{0,2},{1,3},{2,0},{3,1},{4,6},{5,7},{6,4},{7,5},{8,10},{9,11},{10,... | collective-permute-start | bytes 344072 | tf_op jit(solution)/shard_map/ppermute | solution.py:476
  10.1 2.0 %own_kernel.1 = (bf16[128,3072]{1,0:T(8,128)(2,1)S(1)}, bf16[128,3072]{1,0:T(8,128)(2,1)S(1)}) custom-call(bf16[1024,128]{1,0:T(8,128)(2,1)} %refs_0_.5, bf16[128,512]{1,0:T(8,128)(2,1)} %refs_1_.1, bf16[1024,128]{1,0:T(8,128)(2,1)} %refs_2_.3, bf16[128,512]{1,0:T(8,128)(2,1)} %refs_3_.3, bf16[1024,128]{1,0:T(8,128)(2,1)} %refs_4_.3, ...), custom_call_target="tpu_custom_call" | custom-call | bytes 1572864 | tf_op jit(solution)/shard_map/own_kernel/pallas_call | solution.py:96
  12.1 1.7 %tables_kernel.1 = (bf16[64,512]{1,0:T(8,128)(2,1)S(1)}, bf16[512,64]{1,0:T(8,128)(2,1)S(1)}, bf16[256,512]{1,0:T(8,128)(2,1)S(1)}, bf16[512,256]{1,0:T(8,128)(2...) custom-call(bf16[256,512]{1,0:T(8,128)(2,1)} %refs_7_.5, ...), custom_call_target="tpu_custom_call" | custom-call | bytes 270464 | tf_op jit(solution)/shard_map/tables_kernel/pallas_call | solution.py:96
  13.8 2.5 %collective-permute-done.1.refs_2_ = bf16[16,3584]{1,0:T(8,128)(2,1)S(1)} collective-permute-done((bf16[16,3584]{1,0:T(8,128)(2,1)S(1)}, bf16[16,3584]{1,0:T(8,128)(2,1)S(1)}, u32[]{:S(2)}, u32[]{:S(2)}) %collective-permute-start.1) | collective-permute-done | bytes 114720 | tf_op jit(solution)/shard_map/ppermute | solution.py:476
  19.7 6.8 %collective-permute-done.4.refs_3_.refs_11_.refs_16_ = bf16[48,3584]{1,0:T(8,128)(2,1)S(1)} collective-permute-done((bf16[48,3584]{1,0:T(8,128)(2,1)S(1)}, bf16[48,3584]{1,0:T(8,128)(2,1)S(1)}, u32[]{:S(2)}, u32[]{:S(2)}) %collective-permute-start.4) | collective-permute-done | bytes 344096 | tf_op jit(solution)/shard_map/ppermute | solution.py:185
  26.5 1.6 %collective-permute-start.8 = (bf16[48,1536]{1,0:T(8,128)(2,1)S(1)}, bf16[48,1536]{1,0:T(8,128)(2,1)S(1)}, u32[]{:S(2)}, u32[]{:S(2)}) collective-permute-start(bf16[48,1536]{1,0:T(8,128)(2,1)S(1)} %slice.16), channel_id=1, source_target_pairs={{0,16},{4,20},{8,24},{12,28},{16,0},{20,4},{24,8},{28,12},{1,17},{... | collective-permute-start | bytes 442376 | tf_op jit(solution)/shard_map/ppermute | solution.py:185
  29.7 3.0 %collective-permute-start.19 = (bf16[16,3072]{1,0:T(8,128)(2,1)S(1)}, bf16[16,3072]{1,0:T(8,128)(2,1)S(1)}, u32[]{:S(2)}, u32[]{:S(2)}) collective-permute-start(bf16[16,3072]{1,0:T(8,128)(2,1)S(1)} %get-tuple-element.118), channel_id=1, source_target_pairs={{0,3},{1,0},{2,1},{3,2},{4,7},{5,4},{6,5},{7,6},{8,11},{9,8},{10,9... | collective-permute-start | bytes 294920 | tf_op jit(solution)/shard_map/ppermute | solution.py:476
  36.2 7.5 %collective-permute-done.18 = bf16[16,3072]{1,0:T(8,128)(2,1)S(1)} collective-permute-done((bf16[16,3072]{1,0:T(8,128)(2,1)S(1)}, bf16[16,3072]{1,0:T(8,128)(2,1)S(1)}, u32[]{:S(2)}, u32[]{:S(2)}) %collective-permute-start.18) | collective-permute-done | bytes 98336 | tf_op jit(solution)/shard_map/ppermute | solution.py:476
  45.4 3.8 %encode_kernel.1 = (bf16[256,512]{1,0:T(8,128)(2,1)S(1)}, bf16[512,512]{1,0:T(8,128)(2,1)S(1)}, bf16[512,512]{1,0:T(8,128)(2,1)S(1)}, f32[512,128]{1,0:T(8,128)S...) custom-call(bf16[512,512]{1,0:T(8,128)(2,1)S(1)} %get-tuple-element., ...), custom_call_target="tpu_custom_call" | custom-call | flops 3000000000 | bytes 5488640 | tf_op jit(solution)/shard_map/encode_kernel/pallas_call | solution.py:96
  49.2 3.2 %collective-permute-done.22.refs_12_ = bf16[48,3072]{1,0:T(8,128)(2,1)S(1)} collective-permute-done((bf16[48,3072]{1,0:T(8,128)(2,1)S(1)}, bf16[48,3072]{1,0:T(8,128)(2,1)S(1)}, u32[]{:S(2)}, u32[]{:S(2)}) %collective-permute-start.22) | collective-permute-done | bytes 294944 | tf_op jit(solution)/shard_map/ppermute | solution.py:185
  54.7 3.4 %collective-permute-start.13 = (bf16[16,512]{1,0:T(8,128)(2,1)S(1)}, bf16[16,512]{1,0:T(8,128)(2,1)S(1)}, u32[]{:S(2)}, u32[]{:S(2)}) collective-permute-start(bf16[16,512]{1,0:T(8,128)(2,1)S(1)} %get-tuple-element.109), channel_id=1, source_target_pairs={{0,3},{1,0},{2,1},{3,2},{4,7},{5,4},{6,5},{7,6},{8,11},{9,8},{10,9... | collective-permute-start | bytes 49160 | tf_op jit(solution)/shard_map/ppermute | solution.py:476
  58.1 1.7 %collective-permute-done.11.refs_1_ = bf16[16,512]{1,0:T(8,128)(2,1)S(1)} collective-permute-done((bf16[16,512]{1,0:T(8,128)(2,1)S(1)}, bf16[16,512]{1,0:T(8,128)(2,1)S(1)}, u32[]{:S(2)}, u32[]{:S(2)}) %collective-permute-start.11) | collective-permute-done | bytes 16416 | tf_op jit(solution)/shard_map/ppermute | solution.py:476
  61.2 3.8 %collective-permute-done.26 = bf16[48,1536]{1,0:T(8,128)(2,1)S(1)} collective-permute-done((bf16[48,1536]{1,0:T(8,128)(2,1)S(1)}, bf16[48,1536]{1,0:T(8,128)(2,1)S(1)}, u32[]{:S(2)}, u32[]{:S(2)}) %collective-permute-start.26) | collective-permute-done | bytes 147488 | tf_op jit(solution)/shard_map/ppermute | solution.py:185
  67.0 2.3 %collective-permute-done.15.refs_4_ = bf16[16,512]{1,0:T(8,128)(2,1)S(1)} collective-permute-done((bf16[16,512]{1,0:T(8,128)(2,1)S(1)}, bf16[16,512]{1,0:T(8,128)(2,1)S(1)}, u32[]{:S(2)}, u32[]{:S(2)}) %collective-permute-start.15) | collective-permute-done | bytes 16416 | tf_op jit(solution)/shard_map/ppermute | solution.py:482
  69.8 5.3 %process_kernel.1 = (bf16[256,512]{1,0:T(8,128)(2,1)}, f32[256,512]{1,0:T(8,128)S(1)}, bf16[16,512]{1,0:T(8,128)(2,1)S(1)}, bf16[16,512]{1,0:T(8,128)(2,1)S(1)},...) custom-call(bf16[256,512]{1,0:T(8,128)(2,1)} %refs_0_.7, bf16[256,512]{1,0:T(8,128)(2,1)S(1)} %get-tuple-element.105.refs_1_, ...), custom_call_target="tpu_custom_call" | custom-call | flops 5000000000 | bytes 4915200 | tf_op jit(solution)/shard_map/process_kernel/pallas_call | solution.py:96
  77.0 2.0 %collective-permute-done.29.refs_2_ = bf16[16,512]{1,0:T(8,128)(2,1)S(1)} collective-permute-done((bf16[16,512]{1,0:T(8,128)(2,1)S(1)}, bf16[16,512]{1,0:T(8,128)(2,1)S(1)}, u32[]{:S(2)}, u32[]{:S(2)}) %collective-permute-start.29) | collective-permute-done | bytes 16416 | tf_op jit(solution)/shard_map/ppermute | solution.py:482
  81.4 1.9 %collective-permute-start.33 = (bf16[16,512]{1,0:T(8,128)(2,1)S(1)}, bf16[16,512]{1,0:T(8,128)(2,1)S(1)}, u32[]{:S(2)}, u32[]{:S(2)}) collective-permute-start(bf16[16,512]{1,0:T(8,128)(2,1)S(1)} %get-tuple-element.136), channel_id=1, source_target_pairs={{0,1},{1,2},{2,3},{3,0},{4,5},{5,6},{6,7},{7,4},{8,9},{9,10},{10,1... | collective-permute-start | bytes 49160 | tf_op jit(solution)/shard_map/ppermute | solution.py:476
  84.5 2.4 %collective-permute-done.33.refs_3_ = bf16[16,512]{1,0:T(8,128)(2,1)S(1)} collective-permute-done((bf16[16,512]{1,0:T(8,128)(2,1)S(1)}, bf16[16,512]{1,0:T(8,128)(2,1)S(1)}, u32[]{:S(2)}, u32[]{:S(2)}) %collective-permute-start.33) | collective-permute-done | bytes 16416 | tf_op jit(solution)/shard_map/ppermute | solution.py:476
  86.9 3.2 %decode_kernel.1 = (f32[256,512]{1,0:T(8,128)}, bf16[16,512]{1,0:T(8,128)(2,1)S(1)}, bf16[16,512]{1,0:T(8,128)(2,1)S(1)}, bf16[16,512]{1,0:T(8,128)(2,1)S(1)}, bf16[16,512]{1,0:T(8,128)(2,1)S(1)}) custom-call(bf16[16,512]{1,0:T(8,128)(2,1)S(1)} %get-tuple-element.133.refs_0_, bf16[16,512]{1,0:T(8,128)(2,1)S(1)} %collective-permute-done.31.refs_1_, ...), custom_call_target="tpu_custom_call" | custom-call | flops 3000000000 | bytes 6471680 | tf_op jit(solution)/shard_map/decode_kernel/pallas_call | solution.py:96
  92.0 1.9 %collective-permute-done.35.refs_2_ = bf16[16,512]{1,0:T(8,128)(2,1)S(1)} collective-permute-done((bf16[16,512]{1,0:T(8,128)(2,1)S(1)}, bf16[16,512]{1,0:T(8,128)(2,1)S(1)}, u32[]{:S(2)}, u32[]{:S(2)}) %collective-permute-start.35) | collective-permute-done | bytes 16416 | tf_op jit(solution)/shard_map/ppermute | solution.py:482
  96.7 1.7 %collective-permute-done.37.refs_1_ = bf16[16,512]{1,0:T(8,128)(2,1)S(1)} collective-permute-done((bf16[16,512]{1,0:T(8,128)(2,1)S(1)}, bf16[16,512]{1,0:T(8,128)(2,1)S(1)}, u32[]{:S(2)}, u32[]{:S(2)}) %collective-permute-start.37) | collective-permute-done | bytes 16416 | tf_op jit(solution)/shard_map/ppermute | solution.py:476
  98.4 1.9 %collective-permute-done.38.refs_2_ = bf16[16,512]{1,0:T(8,128)(2,1)S(1)} collective-permute-done((bf16[16,512]{1,0:T(8,128)(2,1)S(1)}, bf16[16,512]{1,0:T(8,128)(2,1)S(1)}, u32[]{:S(2)}, u32[]{:S(2)}) %collective-permute-start.38) | collective-permute-done | bytes 16416 | tf_op jit(solution)/shard_map/ppermute | solution.py:476
  (78 shorter events, 30.4 us)
Async XLA Ops:
  3.1 10.8 %collective-permute-start = (bf16[16,3584]{1,0:T(8,128)(2,1)S(1)}, bf16[16,3584]{1,0:T(8,128)(2,1)S(1)}, u32[]{:S(2)}, u32[]{:S(2)}) collective-permute-start(bf16[16,3584]{1,0:T(8,128)(2,1)S(1)} %get-tuple-element.95), channel_id=1, source_target_pairs={{0,1},{1,2},{2,3},{3,0},{4,5},{5,6},{6,7},{7,4},{8,9},{9,10},{10,1... | collective-permute-start | bytes 344072 | tf_op jit(solution)/shard_map/ppermute | solution.py:476
  6.1 10.2 %collective-permute-start.1 = (bf16[16,3584]{1,0:T(8,128)(2,1)S(1)}, bf16[16,3584]{1,0:T(8,128)(2,1)S(1)}, u32[]{:S(2)}, u32[]{:S(2)}) collective-permute-start(bf16[16,3584]{1,0:T(8,128)(2,1)S(1)} %get-tuple-element.96), channel_id=1, source_target_pairs={{0,2},{1,3},{2,0},{3,1},{4,6},{5,7},{6,4},{7,5},{8,10},{9,11},{10,... | collective-permute-start | bytes 344072 | tf_op jit(solution)/shard_map/ppermute | solution.py:476
  8.7 7.6 %collective-permute-start.2 = (bf16[16,3584]{1,0:T(8,128)(2,1)S(1)}, bf16[16,3584]{1,0:T(8,128)(2,1)S(1)}, u32[]{:S(2)}, u32[]{:S(2)}) collective-permute-start(bf16[16,3584]{1,0:T(8,128)(2,1)S(1)} %get-tuple-element.97), channel_id=1, source_target_pairs={{0,3},{1,0},{2,1},{3,2},{4,7},{5,4},{6,5},{7,6},{8,11},{9,8},{10,9... | collective-permute-start | bytes 344072 | tf_op jit(solution)/shard_map/ppermute | solution.py:476
  16.5 10.0 %collective-permute-start.4 = (bf16[48,3584]{1,0:T(8,128)(2,1)S(1)}, bf16[48,3584]{1,0:T(8,128)(2,1)S(1)}, u32[]{:S(2)}, u32[]{:S(2)}) collective-permute-start(bf16[48,3584]{1,0:T(8,128)(2,1)S(1)} %get-tuple-element.99), channel_id=1, source_target_pairs={{0,8},{4,12},{8,0},{12,4},{16,24},{20,28},{24,16},{28,20},{1,9},{5... | collective-permute-start | bytes 1032200 | tf_op jit(solution)/shard_map/ppermute | solution.py:185
  18.1 11.6 %collective-permute-start.3 = (bf16[48,3584]{1,0:T(8,128)(2,1)S(1)}, bf16[48,3584]{1,0:T(8,128)(2,1)S(1)}, u32[]{:S(2)}, u32[]{:S(2)}) collective-permute-start(bf16[48,3584]{1,0:T(8,128)(2,1)S(1)} %get-tuple-element.99), channel_id=1, source_target_pairs={{0,4},{4,0},{8,12},{12,8},{16,20},{20,16},{24,28},{28,24},{1,5},{5... | collective-permute-start | bytes 1032200 | tf_op jit(solution)/shard_map/ppermute | solution.py:185
  18.1 10.0 %collective-permute-start.6 = (bf16[48,3072]{1,0:T(8,128)(2,1)S(1)}, bf16[48,3072]{1,0:T(8,128)(2,1)S(1)}, u32[]{:S(2)}, u32[]{:S(2)}) collective-permute-start(bf16[48,3072]{1,0:T(8,128)(2,1)S(1)} %get-tuple-element.103.refs_9_.refs_14_), channel_id=1, source_target_pairs={{0,16},{4,20},{8,24},{12,28},{16,0},{20,4},{24,8},{28,12},{1,17},{... | collective-permute-start | bytes 884744 | tf_op jit(solution)/shard_map/ppermute | solution.py:185
  26.5 7.7 %collective-permute-start.8 = (bf16[48,1536]{1,0:T(8,128)(2,1)S(1)}, bf16[48,1536]{1,0:T(8,128)(2,1)S(1)}, u32[]{:S(2)}, u32[]{:S(2)}) collective-permute-start(bf16[48,1536]{1,0:T(8,128)(2,1)S(1)} %slice.16), channel_id=1, source_target_pairs={{0,16},{4,20},{8,24},{12,28},{16,0},{20,4},{24,8},{28,12},{1,17},{... | collective-permute-start | bytes 442376 | tf_op jit(solution)/shard_map/ppermute | solution.py:185
  28.1 6.6 %collective-permute-start.9 = (bf16[48,1536]{1,0:T(8,128)(2,1)S(1)}, bf16[48,1536]{1,0:T(8,128)(2,1)S(1)}, u32[]{:S(2)}, u32[]{:S(2)}) collective-permute-start(bf16[48,1536]{1,0:T(8,128)(2,1)S(1)} %slice.17), channel_id=1, source_target_pairs={{0,8},{4,12},{8,0},{12,4},{16,24},{20,28},{24,16},{28,20},{1,9},{5... | collective-permute-start | bytes 442376 | tf_op jit(solution)/shard_map/ppermute | solution.py:185
  29.7 15.7 %collective-permute-start.7 = (bf16[48,3072]{1,0:T(8,128)(2,1)S(1)}, bf16[48,3072]{1,0:T(8,128)(2,1)S(1)}, u32[]{:S(2)}, u32[]{:S(2)}) collective-permute-start(bf16[48,3072]{1,0:T(8,128)(2,1)S(1)} %collective-permute-done.6.refs_12_.refs_17_), channel_id=1, source_target_pairs={{0,4},{4,0},{8,12},{12,8},{16,20},{20,16},{24,28},{28,24},{1,5},{5... | collective-permute-start | bytes 884744 | tf_op jit(solution)/shard_map/ppermute | solution.py:185
  29.7 6.5 %collective-permute-start.19 = (bf16[16,3072]{1,0:T(8,128)(2,1)S(1)}, bf16[16,3072]{1,0:T(8,128)(2,1)S(1)}, u32[]{:S(2)}, u32[]{:S(2)}) collective-permute-start(bf16[16,3072]{1,0:T(8,128)(2,1)S(1)} %get-tuple-element.118), channel_id=1, source_target_pairs={{0,3},{1,0},{2,1},{3,2},{4,7},{5,4},{6,5},{7,6},{8,11},{9,8},{10,9... | collective-permute-start | bytes 294920 | tf_op jit(solution)/shard_map/ppermute | solution.py:476
  32.7 11.0 %collective-permute-start.18 = (bf16[16,3072]{1,0:T(8,128)(2,1)S(1)}, bf16[16,3072]{1,0:T(8,128)(2,1)S(1)}, u32[]{:S(2)}, u32[]{:S(2)}) collective-permute-start(bf16[16,3072]{1,0:T(8,128)(2,1)S(1)} %get-tuple-element.118), channel_id=1, source_target_pairs={{0,2},{1,3},{2,0},{3,1},{4,6},{5,7},{6,4},{7,5},{8,10},{9,11},{10,... | collective-permute-start | bytes 294920 | tf_op jit(solution)/shard_map/ppermute | solution.py:476
  34.2 9.5 %collective-permute-start.17 = (bf16[16,3072]{1,0:T(8,128)(2,1)S(1)}, bf16[16,3072]{1,0:T(8,128)(2,1)S(1)}, u32[]{:S(2)}, u32[]{:S(2)}) collective-permute-start(bf16[16,3072]{1,0:T(8,128)(2,1)S(1)} %get-tuple-element.118), channel_id=1, source_target_pairs={{0,1},{1,2},{2,3},{3,0},{4,5},{5,6},{6,7},{7,4},{8,9},{9,10},{10,1... | collective-permute-start | bytes 294920 | tf_op jit(solution)/shard_map/ppermute | solution.py:476
  34.8 10.7 %collective-permute-start.5 = (bf16[48,3584]{1,0:T(8,128)(2,1)S(1)}, bf16[48,3584]{1,0:T(8,128)(2,1)S(1)}, u32[]{:S(2)}, u32[]{:S(2)}) collective-permute-start(bf16[48,3584]{1,0:T(8,128)(2,1)S(1)} %collective-permute-done.4.refs_3_.refs_11_.refs_16_), channel_id=1, source_target_pairs={{0,4},{4,0},{8,12},{12,8},{16,20},{20,16},{24,28},{28,24},{1,5},{5... | collective-permute-start | bytes 1032200 | tf_op jit(solution)/shard_map/ppermute | solution.py:185
  36.2 9.2 %collective-permute-start.10 = (bf16[48,3072]{1,0:T(8,128)(2,1)S(1)}, bf16[48,3072]{1,0:T(8,128)(2,1)S(1)}, u32[]{:S(2)}, u32[]{:S(2)}) collective-permute-start(bf16[48,3072]{1,0:T(8,128)(2,1)S(1)} %constant_dynamic-update-slice_fusion.refs_15_.refs_20_), channel_id=1, source_target_pairs={{0,4},{4,0},{8,12},{12,8},{16,20},{20,16},{24,28},{28,24},{1,5},{5... | collective-permute-start | bytes 884744 | tf_op jit(solution)/shard_map/ppermute | solution.py:185
  43.7 8.7 %collective-permute-start.22 = (bf16[48,3072]{1,0:T(8,128)(2,1)S(1)}, bf16[48,3072]{1,0:T(8,128)(2,1)S(1)}, u32[]{:S(2)}, u32[]{:S(2)}) collective-permute-start(bf16[48,3072]{1,0:T(8,128)(2,1)S(1)} %constant_dynamic-update-slice_fusion.2.refs_9_), channel_id=1, source_target_pairs={{0,16},{4,20},{8,24},{12,28},{16,0},{20,4},{24,8},{28,12},{1,17},{... | collective-permute-start | bytes 884744 | tf_op jit(solution)/shard_map/ppermute | solution.py:185
  44.3 8.4 %collective-permute-start.21 = (bf16[48,3072]{1,0:T(8,128)(2,1)S(1)}, bf16[48,3072]{1,0:T(8,128)(2,1)S(1)}, u32[]{:S(2)}, u32[]{:S(2)}) collective-permute-start(bf16[48,3072]{1,0:T(8,128)(2,1)S(1)} %constant_dynamic-update-slice_fusion.2.refs_9_), channel_id=1, source_target_pairs={{0,8},{4,12},{8,0},{12,4},{16,24},{20,28},{24,16},{28,20},{1,9},{5... | collective-permute-start | bytes 884744 | tf_op jit(solution)/shard_map/ppermute | solution.py:185
  52.7 8.5 %collective-permute-start.25 = (bf16[48,1536]{1,0:T(8,128)(2,1)S(1)}, bf16[48,1536]{1,0:T(8,128)(2,1)S(1)}, u32[]{:S(2)}, u32[]{:S(2)}) collective-permute-start(bf16[48,1536]{1,0:T(8,128)(2,1)S(1)} %slice.14), channel_id=1, source_target_pairs={{0,16},{4,20},{8,24},{12,28},{16,0},{20,4},{24,8},{28,12},{1,17},{... | collective-permute-start | bytes 442376 | tf_op jit(solution)/shard_map/ppermute | solution.py:185
  54.3 5.5 %collective-permute-start.11 = (bf16[16,512]{1,0:T(8,128)(2,1)S(1)}, bf16[16,512]{1,0:T(8,128)(2,1)S(1)}, u32[]{:S(2)}, u32[]{:S(2)}) collective-permute-start(bf16[16,512]{1,0:T(8,128)(2,1)S(1)} %get-tuple-element.107), channel_id=1, source_target_pairs={{0,1},{1,2},{2,3},{3,0},{4,5},{5,6},{6,7},{7,4},{8,9},{9,10},{10,1... | collective-permute-start | bytes 49160 | tf_op jit(solution)/shard_map/ppermute | solution.py:476
  54.3 6.1 %collective-permute-start.12 = (bf16[16,512]{1,0:T(8,128)(2,1)S(1)}, bf16[16,512]{1,0:T(8,128)(2,1)S(1)}, u32[]{:S(2)}, u32[]{:S(2)}) collective-permute-start(bf16[16,512]{1,0:T(8,128)(2,1)S(1)} %get-tuple-element.108), channel_id=1, source_target_pairs={{0,2},{1,3},{2,0},{3,1},{4,6},{5,7},{6,4},{7,5},{8,10},{9,11},{10,... | collective-permute-start | bytes 49160 | tf_op jit(solution)/shard_map/ppermute | solution.py:476
  54.7 5.7 %collective-permute-start.13 = (bf16[16,512]{1,0:T(8,128)(2,1)S(1)}, bf16[16,512]{1,0:T(8,128)(2,1)S(1)}, u32[]{:S(2)}, u32[]{:S(2)}) collective-permute-start(bf16[16,512]{1,0:T(8,128)(2,1)S(1)} %get-tuple-element.109), channel_id=1, source_target_pairs={{0,3},{1,0},{2,1},{3,2},{4,7},{5,4},{6,5},{7,6},{8,11},{9,8},{10,9... | collective-permute-start | bytes 49160 | tf_op jit(solution)/shard_map/ppermute | solution.py:476
  58.1 7.4 %collective-permute-start.20 = (bf16[48,3072]{1,0:T(8,128)(2,1)S(1)}, bf16[48,3072]{1,0:T(8,128)(2,1)S(1)}, u32[]{:S(2)}, u32[]{:S(2)}) collective-permute-start(bf16[48,3072]{1,0:T(8,128)(2,1)S(1)} %constant_dynamic-update-slice_fusion.2.refs_9_), channel_id=1, source_target_pairs={{0,4},{4,0},{8,12},{12,8},{16,20},{20,16},{24,28},{28,24},{1,5},{5... | collective-permute-start | bytes 884744 | tf_op jit(solution)/shard_map/ppermute | solution.py:185
  60.6 9.2 %collective-permute-start.23 = (bf16[48,3072]{1,0:T(8,128)(2,1)S(1)}, bf16[48,3072]{1,0:T(8,128)(2,1)S(1)}, u32[]{:S(2)}, u32[]{:S(2)}) collective-permute-start(bf16[48,3072]{1,0:T(8,128)(2,1)S(1)} %collective-permute-done.21.refs_11_), channel_id=1, source_target_pairs={{0,4},{4,0},{8,12},{12,8},{16,20},{20,16},{24,28},{28,24},{1,5},{5... | collective-permute-start | bytes 884744 | tf_op jit(solution)/shard_map/ppermute | solution.py:185
  60.7 9.1 %collective-permute-start.24 = (bf16[48,3072]{1,0:T(8,128)(2,1)S(1)}, bf16[48,3072]{1,0:T(8,128)(2,1)S(1)}, u32[]{:S(2)}, u32[]{:S(2)}) collective-permute-start(bf16[48,3072]{1,0:T(8,128)(2,1)S(1)} %collective-permute-done.22.refs_12_), channel_id=1, source_target_pairs={{0,4},{4,0},{8,12},{12,8},{16,20},{20,16},{24,28},{28,24},{1,5},{5... | collective-permute-start | bytes 884744 | tf_op jit(solution)/shard_map/ppermute | solution.py:185
  81.4 5.5 %collective-permute-start.33 = (bf16[16,512]{1,0:T(8,128)(2,1)S(1)}, bf16[16,512]{1,0:T(8,128)(2,1)S(1)}, u32[]{:S(2)}, u32[]{:S(2)}) collective-permute-start(bf16[16,512]{1,0:T(8,128)(2,1)S(1)} %get-tuple-element.136), channel_id=1, source_target_pairs={{0,1},{1,2},{2,3},{3,0},{4,5},{5,6},{6,7},{7,4},{8,9},{9,10},{10,1... | collective-permute-start | bytes 49160 | tf_op jit(solution)/shard_map/ppermute | solution.py:476
  (16 other events, 58.7 us)

commit v7 on v6

--- a/solution.py
+++ b/solution.py
@@ -200,7 +200,7 @@
             rows.append(lax.all_gather(shards[2 * i + 1], "mp", axis=0, tiled=True))
         enc, proc = jnp.concatenate(rows[:4], axis=1), jnp.concatenate(rows[4:], axis=1)
         arrived = exchange(outgoing, step)
-        return [enc], lambda one, moved: [proc], arrived, grid_t, tables
+        return [enc], lambda moved: [proc], arrived, grid_t, tables
     far = [Far(s) for s in shards]
     piece = hidden // planes
     width = 6 * features
@@ -221,32 +221,24 @@
         kept,
         messages,
     )
-    core, x, y = across(both, 1), across(both, 2), across(first, 4)
+    x, y, corner, core = across(both, 2), across(first, 4), across(first, 6), across(both, 1)
     proc_piece, _ = lax.optimization_barrier((proc_piece, core))
-    low, high = relay(x, y)
-    x_core, y_core = across(x, 1), across(y, 1)
-    parts = [along(proc_piece, s) for s in (1, 2, 3)]
-    *parts, _, _ = lax.optimization_barrier((*parts, low, high))
-    far_corner = jnp.concatenate([low, high], axis=1)
-    enc = [enc_own, first, core, x, y, x_core, y_core, far_corner, across(far_corner, 1)]
+    x_core = across(x, 1)
+    enc = [enc_own, first, core, x, y, corner, x_core, across(y, 1), across(corner, 1)]
     arrived = [near, core, x, x_core]
-    proc_first = jnp.concatenate(parts)
-    proc_core, proc_x, proc_y = [across(proc_first, flip) for flip in (1, 2, 4)]
-
-    def finish(one, moved):
-        x, y, _ = lax.optimization_barrier((proc_x, proc_y, one))
-        low, high = relay(x, y)
-        x, y, *_ = lax.optimization_barrier((x, y, *moved))
-        corner = jnp.concatenate([low, high], axis=1)
-        blocks = [proc_own, proc_first, proc_core, x, y, across(x, 1), across(y, 1)]
-        return blocks + [corner, across(corner, 1)]
+    beside_me = lax.ppermute(proc_piece, "mp", [(m, m ^ 1) for m in range(mp)])
+    pair = jnp.concatenate([proc_piece, beside_me])
+    others = lax.ppermute(pair, "mp", [(m, m ^ 2) for m in range(mp)])
+    proc_first = jnp.concatenate([beside_me, others])
+    proc_first, *_ = lax.optimization_barrier((proc_first, x, y, corner))
+    plane = [across(proc_first, flip) for flip in (2, 4, 6)]
+    proc = [proc_own, proc_first, across(proc_first, 1)] + plane
+
+    def finish(moved):
+        tied, *_ = lax.optimization_barrier((jnp.concatenate(plane), *moved))
+        return proc + [across(tied, 1)]
 
     return enc, finish, arrived, grid_t, tables
-
-
-def relay(x, y):
-    half = 3 * FEATURES
-    return across(x[:, :half], 4), across(y[:, half : 2 * half], 2)
 
 
 def forward(inputs, first, second):
@@ -568,7 +560,7 @@
         flops=3 * 10**9,
     )
     moved = first_level(halo_out, halo_step)
-    proc = finish(mesh_one, moved)
+    proc = finish(moved)
     halo_in = second_level(moved)
     mesh_two, grad_one, *grad_halo = call(
         process_kernel,

time: 103 us -> 94.8 us (0.920)
  waiting for transfers between devices: 44 us -> 39.3 us
  starting transfers between devices: 37.7 us -> 33.8 us
    ppermute x15 -> x12, starting transfers between devices: 21.5 us -> 15.3 us  [along(): lax.ppermute(block, 'mp', [(m, (m + shift) % size) for m in range(size)])]
    ppermute x0 -> x2, starting transfers between devices: none -> 4.62 us  [the longest x1 2.92 us: start(): beside_me = lax.ppermute(proc_piece, 'mp', [(m, m ^ 1) for m in range(mp)])]
    ppermute x15 -> x12, waiting for transfers between devices: 21.7 us -> 17.7 us  [along(): lax.ppermute(block, 'mp', [(m, (m + shift) % size) for m in range(size)])]
    ppermute x16 -> x12, starting transfers between devices: 10.9 us -> 8.19 us  [across(): lax.ppermute(x, ('groups', 'graph'), [(p, p ^ flip) for p in range(planes)])]
    ppermute x16 -> x12, waiting for transfers between devices: 14.1 us -> 13.8 us  [across(): lax.ppermute(x, ('groups', 'graph'), [(p, p ^ flip) for p in range(planes)])]
  transfers between devices with their start and end apart: 40 -> 35, of which waited for: 21 -> 18; matrix products, arithmetic and copies ran while one was open for 0% -> 0% of each run, Pallas kernels for 7% -> 8%
where the time goes in v7:
time: 94.8 us; the launch traced here: 94.6 us
  waiting for transfers between devices  39.3 us (41%)
  starting transfers between devices  33.8 us (36%)
  Pallas kernels  20.3 us (21%)
  between operations  0.97 us (1%)
    pallas_call x11, Pallas kernels, call(): pl.pallas_call(body, out_shape=out_shape, in_specs=[hbm if away else vmem...  20.3 us
    ppermute x12, waiting for transfers between devices, along(): lax.ppermute(block, 'mp', [(m, (m + shift) % size) for m in range(size)])  17.7 us
    ppermute x12, starting transfers between devices, along(): lax.ppermute(block, 'mp', [(m, (m + shift) % size) for m in range(size)])  15.3 us
    ppermute x12, waiting for transfers between devices, across(): lax.ppermute(x, ('groups', 'graph'), [(p, p ^ flip) for p in range(planes)])  13.8 us
    ppermute x12, starting transfers between devices, across(): lax.ppermute(x, ('groups', 'graph'), [(p, p ^ flip) for p in range(planes)])  8.19 us
    ppermute x9, waiting for transfers between devices, beside(): lax.ppermute(block, 'graph', [(g, g ^ flip) for g in range(lax.axis_size(...  7.76 us
    ppermute x9, starting transfers between devices, beside(): lax.ppermute(block, 'graph', [(g, g ^ flip) for g in range(lax.axis_size(...  5.73 us
    ppermute x1, starting transfers between devices, start(): beside_me = lax.ppermute(proc_piece, 'mp', [(m, m ^ 1) for m in range(mp)])  2.92 us
  transfers between devices with their start and end apart: 35, of which 18 were waited for; matrix products, arithmetic and copies ran while one was open for 0% of the time, Pallas kernels for 8%

profile of v7, /device:TPU:0, one launch (start us, length us, event | category | flops | bytes accessed | tf_op | source)
XLA Modules:
  0.0 94.6 jit_solution(17037232918281351986)
XLA Ops:
  0.6 2.4 %prepare_kernel.1 = (bf16[16,3072]{1,0:T(8,128)(2,1)S(1)}, bf16[512,64]{1,0:T(8,128)(2,1)S(1)}, bf16[16,512]{1,0:T(8,128)(2,1)S(1)}, bf16[16,3584]{1,0:T(8,128)(...) custom-call(bf16[512,512]{1,0:T(8,128)(2,1)} %refs_0_.4, s32[4,16]{1,0:T(4,128)} %bitcast.6, ...), custom_call_target="tpu_custom_call" | custom-call | bytes 2097408 | tf_op jit(solution)/shard_map/prepare_kernel/pallas_call | solution.py:96
  3.1 3.1 %collective-permute-start = (bf16[16,3584]{1,0:T(8,128)(2,1)S(1)}, bf16[16,3584]{1,0:T(8,128)(2,1)S(1)}, u32[]{:S(2)}, u32[]{:S(2)}) collective-permute-start(bf16[16,3584]{1,0:T(8,128)(2,1)S(1)} %get-tuple-element.90), channel_id=1, source_target_pairs={{0,1},{1,2},{2,3},{3,0},{4,5},{5,6},{6,7},{7,4},{8,9},{9,10},{10,1... | collective-permute-start | bytes 344072 | tf_op jit(solution)/shard_map/ppermute | solution.py:468
  6.1 2.6 %collective-permute-start.1 = (bf16[16,3584]{1,0:T(8,128)(2,1)S(1)}, bf16[16,3584]{1,0:T(8,128)(2,1)S(1)}, u32[]{:S(2)}, u32[]{:S(2)}) collective-permute-start(bf16[16,3584]{1,0:T(8,128)(2,1)S(1)} %get-tuple-element.91), channel_id=1, source_target_pairs={{0,2},{1,3},{2,0},{3,1},{4,6},{5,7},{6,4},{7,5},{8,10},{9,11},{10,... | collective-permute-start | bytes 344072 | tf_op jit(solution)/shard_map/ppermute | solution.py:468
  10.1 2.0 %own_kernel.1 = (bf16[128,3072]{1,0:T(8,128)(2,1)S(1)}, bf16[128,3072]{1,0:T(8,128)(2,1)S(1)}) custom-call(bf16[1024,128]{1,0:T(8,128)(2,1)} %refs_0_.5, bf16[128,512]{1,0:T(8,128)(2,1)} %refs_1_.1, bf16[1024,128]{1,0:T(8,128)(2,1)} %refs_2_.3, bf16[128,512]{1,0:T(8,128)(2,1)} %refs_3_.3, bf16[1024,128]{1,0:T(8,128)(2,1)} %refs_4_.3, ...), custom_call_target="tpu_custom_call" | custom-call | bytes 1572864 | tf_op jit(solution)/shard_map/own_kernel/pallas_call | solution.py:96
  12.1 1.7 %tables_kernel.1 = (bf16[64,512]{1,0:T(8,128)(2,1)S(1)}, bf16[512,64]{1,0:T(8,128)(2,1)S(1)}, bf16[256,512]{1,0:T(8,128)(2,1)S(1)}, bf16[512,256]{1,0:T(8,128)(2...) custom-call(bf16[256,512]{1,0:T(8,128)(2,1)} %refs_7_.5, ...), custom_call_target="tpu_custom_call" | custom-call | bytes 270464 | tf_op jit(solution)/shard_map/tables_kernel/pallas_call | solution.py:96
  13.8 2.5 %collective-permute-done.1.refs_2_ = bf16[16,3584]{1,0:T(8,128)(2,1)S(1)} collective-permute-done((bf16[16,3584]{1,0:T(8,128)(2,1)S(1)}, bf16[16,3584]{1,0:T(8,128)(2,1)S(1)}, u32[]{:S(2)}, u32[]{:S(2)}) %collective-permute-start.1) | collective-permute-done | bytes 114720 | tf_op jit(solution)/shard_map/ppermute | solution.py:468
  16.6 1.6 %collective-permute-done.3.refs_2_.refs_10_.refs_15_ = bf16[48,3584]{1,0:T(8,128)(2,1)S(1)} collective-permute-done((bf16[48,3584]{1,0:T(8,128)(2,1)S(1)}, bf16[48,3584]{1,0:T(8,128)(2,1)S(1)}, u32[]{:S(2)}, u32[]{:S(2)}) %collective-permute-start.3) | collective-permute-done | bytes 344096 | tf_op jit(solution)/shard_map/ppermute | solution.py:185
  18.2 2.9 %collective-permute-start.16 = (bf16[16,3072]{1,0:T(8,128)(2,1)S(1)}, bf16[16,3072]{1,0:T(8,128)(2,1)S(1)}, u32[]{:S(2)}, u32[]{:S(2)}) collective-permute-start(bf16[16,3072]{1,0:T(8,128)(2,1)S(1)} %get-tuple-element.113), channel_id=1, source_target_pairs={{0,1},{1,0},{2,3},{3,2},{4,5},{5,4},{6,7},{7,6},{8,9},{9,8},{10,11... | collective-permute-start | bytes 294920 | tf_op jit(solution)/shard_map/ppermute | solution.py:229
  24.7 1.7 %collective-permute-start.17 = (bf16[32,3072]{1,0:T(8,128)(2,1)S(1)}, bf16[32,3072]{1,0:T(8,128)(2,1)S(1)}, u32[]{:S(2)}, u32[]{:S(2)}) collective-permute-start(bf16[32,3072]{1,0:T(8,128)(2,1)S(1)} %pad_maximum_fusion.2), channel_id=1, source_target_pairs={{0,2},{1,3},{2,0},{3,1},{4,6},{5,7},{6,4},{7,5},{8,10},{9,11},{10,... | collective-permute-start | bytes 589832 | tf_op jit(solution)/shard_map/ppermute | solution.py:231
  26.4 9.9 %collective-permute-done.6.refs_12_.refs_17_ = bf16[48,3072]{1,0:T(8,128)(2,1)S(1)} collective-permute-done((bf16[48,3072]{1,0:T(8,128)(2,1)S(1)}, bf16[48,3072]{1,0:T(8,128)(2,1)S(1)}, u32[]{:S(2)}, u32[]{:S(2)}) %collective-permute-start.6) | collective-permute-done | bytes 294944 | tf_op jit(solution)/shard_map/ppermute | solution.py:185
  36.3 2.3 %collective-permute-done.4.refs_3_.refs_11_.refs_16_ = bf16[48,3584]{1,0:T(8,128)(2,1)S(1)} collective-permute-done((bf16[48,3584]{1,0:T(8,128)(2,1)S(1)}, bf16[48,3584]{1,0:T(8,128)(2,1)S(1)}, u32[]{:S(2)}, u32[]{:S(2)}) %collective-permute-start.4) | collective-permute-done | bytes 344096 | tf_op jit(solution)/shard_map/ppermute | solution.py:185
  39.1 1.6 %collective-permute-start.19 = (bf16[48,3072]{1,0:T(8,128)(2,1)S(1)}, bf16[48,3072]{1,0:T(8,128)(2,1)S(1)}, u32[]{:S(2)}, u32[]{:S(2)}) collective-permute-start(bf16[48,3072]{1,0:T(8,128)(2,1)S(1)} %pad_maximum_fusion.1.refs_9_), channel_id=1, source_target_pairs={{0,8},{4,12},{8,0},{12,4},{16,24},{20,28},{24,16},{28,20},{1,9},{5... | collective-permute-start | bytes 884744 | tf_op jit(solution)/shard_map/ppermute | solution.py:185
  42.7 3.8 %encode_kernel.1 = (bf16[256,512]{1,0:T(8,128)(2,1)S(1)}, bf16[512,512]{1,0:T(8,128)(2,1)S(1)}, bf16[512,512]{1,0:T(8,128)(2,1)S(1)}, f32[512,128]{1,0:T(8,128)S...) custom-call(bf16[512,512]{1,0:T(8,128)(2,1)S(1)} %get-tuple-element., ...), custom_call_target="tpu_custom_call" | custom-call | flops 3000000000 | bytes 5488640 | tf_op jit(solution)/shard_map/encode_kernel/pallas_call | solution.py:96
  46.8 1.6 %collective-permute-start.11 = (bf16[16,512]{1,0:T(8,128)(2,1)S(1)}, bf16[16,512]{1,0:T(8,128)(2,1)S(1)}, u32[]{:S(2)}, u32[]{:S(2)}) collective-permute-start(bf16[16,512]{1,0:T(8,128)(2,1)S(1)} %get-tuple-element.103), channel_id=1, source_target_pairs={{0,2},{1,3},{2,0},{3,1},{4,6},{5,7},{6,4},{7,5},{8,10},{9,11},{10,... | collective-permute-start | bytes 49160 | tf_op jit(solution)/shard_map/ppermute | solution.py:468
  48.4 3.6 %collective-permute-done.10.refs_1_ = bf16[16,512]{1,0:T(8,128)(2,1)S(1)} collective-permute-done((bf16[16,512]{1,0:T(8,128)(2,1)S(1)}, bf16[16,512]{1,0:T(8,128)(2,1)S(1)}, u32[]{:S(2)}, u32[]{:S(2)}) %collective-permute-start.10) | collective-permute-done | bytes 16416 | tf_op jit(solution)/shard_map/ppermute | solution.py:468
  52.0 3.7 %collective-permute-done.12.refs_3_ = bf16[16,512]{1,0:T(8,128)(2,1)S(1)} collective-permute-done((bf16[16,512]{1,0:T(8,128)(2,1)S(1)}, bf16[16,512]{1,0:T(8,128)(2,1)S(1)}, u32[]{:S(2)}, u32[]{:S(2)}) %collective-permute-start.12) | collective-permute-done | bytes 16416 | tf_op jit(solution)/shard_map/ppermute | solution.py:468
  61.4 5.3 %process_kernel.1 = (bf16[256,512]{1,0:T(8,128)(2,1)}, f32[256,512]{1,0:T(8,128)S(1)}, bf16[16,512]{1,0:T(8,128)(2,1)S(1)}, bf16[16,512]{1,0:T(8,128)(2,1)S(1)},...) custom-call(bf16[256,512]{1,0:T(8,128)(2,1)} %refs_0_.7, bf16[256,512]{1,0:T(8,128)(2,1)S(1)} %get-tuple-element.100.refs_1_, ...), custom_call_target="tpu_custom_call" | custom-call | flops 5000000000 | bytes 4915200 | tf_op jit(solution)/shard_map/process_kernel/pallas_call | solution.py:96
  68.6 2.2 %collective-permute-done.24.refs_2_ = bf16[16,512]{1,0:T(8,128)(2,1)S(1)} collective-permute-done((bf16[16,512]{1,0:T(8,128)(2,1)S(1)}, bf16[16,512]{1,0:T(8,128)(2,1)S(1)}, u32[]{:S(2)}, u32[]{:S(2)}) %collective-permute-start.24) | collective-permute-done | bytes 16416 | tf_op jit(solution)/shard_map/ppermute | solution.py:474
  71.0 1.9 %collective-permute-start.26 = (bf16[16,512]{1,0:T(8,128)(2,1)S(1)}, bf16[16,512]{1,0:T(8,128)(2,1)S(1)}, u32[]{:S(2)}, u32[]{:S(2)}) collective-permute-start(bf16[16,512]{1,0:T(8,128)(2,1)S(1)} %get-tuple-element.124), channel_id=1, source_target_pairs={{0,3},{1,0},{2,1},{3,2},{4,7},{5,4},{6,5},{7,6},{8,11},{9,8},{10,9... | collective-permute-start | bytes 49160 | tf_op jit(solution)/shard_map/ppermute | solution.py:468
  74.8 2.7 %collective-permute-done.27.refs_2_ = bf16[16,512]{1,0:T(8,128)(2,1)S(1)} collective-permute-done((bf16[16,512]{1,0:T(8,128)(2,1)S(1)}, bf16[16,512]{1,0:T(8,128)(2,1)S(1)}, u32[]{:S(2)}, u32[]{:S(2)}) %collective-permute-start.27) | collective-permute-done | bytes 16416 | tf_op jit(solution)/shard_map/ppermute | solution.py:468
  78.4 3.2 %decode_kernel.1 = (f32[256,512]{1,0:T(8,128)}, bf16[16,512]{1,0:T(8,128)(2,1)S(1)}, bf16[16,512]{1,0:T(8,128)(2,1)S(1)}, bf16[16,512]{1,0:T(8,128)(2,1)S(1)}, bf16[16,512]{1,0:T(8,128)(2,1)S(1)}) custom-call(bf16[16,512]{1,0:T(8,128)(2,1)S(1)} %get-tuple-element.123.refs_0_, bf16[16,512]{1,0:T(8,128)(2,1)S(1)} %collective-permute-done.26.refs_1_, ...), custom_call_target="tpu_custom_call" | custom-call | flops 3000000000 | bytes 6471680 | tf_op jit(solution)/shard_map/decode_kernel/pallas_call | solution.py:96
  83.5 1.9 %collective-permute-done.30.refs_2_ = bf16[16,512]{1,0:T(8,128)(2,1)S(1)} collective-permute-done((bf16[16,512]{1,0:T(8,128)(2,1)S(1)}, bf16[16,512]{1,0:T(8,128)(2,1)S(1)}, u32[]{:S(2)}, u32[]{:S(2)}) %collective-permute-start.30) | collective-permute-done | bytes 16416 | tf_op jit(solution)/shard_map/ppermute | solution.py:474
  87.6 1.9 %collective-permute-start.34 = (bf16[16,512]{1,0:T(8,128)(2,1)S(1)}, bf16[16,512]{1,0:T(8,128)(2,1)S(1)}, u32[]{:S(2)}, u32[]{:S(2)}) collective-permute-start(bf16[16,512]{1,0:T(8,128)(2,1)S(1)} %get-tuple-element.144), channel_id=1, source_target_pairs={{0,1},{1,2},{2,3},{3,0},{4,5},{5,6},{6,7},{7,4},{8,9},{9,10},{10,1... | collective-permute-start | bytes 49160 | tf_op jit(solution)/shard_map/ppermute | solution.py:468
  90.1 1.7 %collective-permute-done.33.refs_2_ = bf16[16,512]{1,0:T(8,128)(2,1)S(1)} collective-permute-done((bf16[16,512]{1,0:T(8,128)(2,1)S(1)}, bf16[16,512]{1,0:T(8,128)(2,1)S(1)}, u32[]{:S(2)}, u32[]{:S(2)}) %collective-permute-start.33) | collective-permute-done | bytes 16416 | tf_op jit(solution)/shard_map/ppermute | solution.py:468
  (60 shorter events, 25.8 us)
Async XLA Ops:
  3.1 10.8 %collective-permute-start = (bf16[16,3584]{1,0:T(8,128)(2,1)S(1)}, bf16[16,3584]{1,0:T(8,128)(2,1)S(1)}, u32[]{:S(2)}, u32[]{:S(2)}) collective-permute-start(bf16[16,3584]{1,0:T(8,128)(2,1)S(1)} %get-tuple-element.90), channel_id=1, source_target_pairs={{0,1},{1,2},{2,3},{3,0},{4,5},{5,6},{6,7},{7,4},{8,9},{9,10},{10,1... | collective-permute-start | bytes 344072 | tf_op jit(solution)/shard_map/ppermute | solution.py:468
  6.1 10.2 %collective-permute-start.1 = (bf16[16,3584]{1,0:T(8,128)(2,1)S(1)}, bf16[16,3584]{1,0:T(8,128)(2,1)S(1)}, u32[]{:S(2)}, u32[]{:S(2)}) collective-permute-start(bf16[16,3584]{1,0:T(8,128)(2,1)S(1)} %get-tuple-element.91), channel_id=1, source_target_pairs={{0,2},{1,3},{2,0},{3,1},{4,6},{5,7},{6,4},{7,5},{8,10},{9,11},{10,... | collective-permute-start | bytes 344072 | tf_op jit(solution)/shard_map/ppermute | solution.py:468
  8.7 7.6 %collective-permute-start.2 = (bf16[16,3584]{1,0:T(8,128)(2,1)S(1)}, bf16[16,3584]{1,0:T(8,128)(2,1)S(1)}, u32[]{:S(2)}, u32[]{:S(2)}) collective-permute-start(bf16[16,3584]{1,0:T(8,128)(2,1)S(1)} %get-tuple-element.92), channel_id=1, source_target_pairs={{0,3},{1,0},{2,1},{3,2},{4,7},{5,4},{6,5},{7,6},{8,11},{9,8},{10,9... | collective-permute-start | bytes 344072 | tf_op jit(solution)/shard_map/ppermute | solution.py:468
  18.2 6.4 %collective-permute-start.16 = (bf16[16,3072]{1,0:T(8,128)(2,1)S(1)}, bf16[16,3072]{1,0:T(8,128)(2,1)S(1)}, u32[]{:S(2)}, u32[]{:S(2)}) collective-permute-start(bf16[16,3072]{1,0:T(8,128)(2,1)S(1)} %get-tuple-element.113), channel_id=1, source_target_pairs={{0,1},{1,0},{2,3},{3,2},{4,5},{5,4},{6,7},{7,6},{8,9},{9,8},{10,11... | collective-permute-start | bytes 294920 | tf_op jit(solution)/shard_map/ppermute | solution.py:229
  21.2 15.1 %collective-permute-start.6 = (bf16[48,3072]{1,0:T(8,128)(2,1)S(1)}, bf16[48,3072]{1,0:T(8,128)(2,1)S(1)}, u32[]{:S(2)}, u32[]{:S(2)}) collective-permute-start(bf16[48,3072]{1,0:T(8,128)(2,1)S(1)} %get-tuple-element.98.refs_9_.refs_14_), channel_id=1, source_target_pairs={{0,16},{4,20},{8,24},{12,28},{16,0},{20,4},{24,8},{28,12},{1,17},{... | collective-permute-start | bytes 884744 | tf_op jit(solution)/shard_map/ppermute | solution.py:185
  22.7 15.8 %collective-permute-start.7 = (bf16[48,3072]{1,0:T(8,128)(2,1)S(1)}, bf16[48,3072]{1,0:T(8,128)(2,1)S(1)}, u32[]{:S(2)}, u32[]{:S(2)}) collective-permute-start(bf16[48,3072]{1,0:T(8,128)(2,1)S(1)} %get-tuple-element.98.refs_9_.refs_14_), channel_id=1, source_target_pairs={{0,24},{4,28},{8,16},{12,20},{16,8},{20,12},{24,0},{28,4},{1,25},{... | collective-permute-start | bytes 884744 | tf_op jit(solution)/shard_map/ppermute | solution.py:185
  24.2 14.4 %collective-permute-start.4 = (bf16[48,3584]{1,0:T(8,128)(2,1)S(1)}, bf16[48,3584]{1,0:T(8,128)(2,1)S(1)}, u32[]{:S(2)}, u32[]{:S(2)}) collective-permute-start(bf16[48,3584]{1,0:T(8,128)(2,1)S(1)} %get-tuple-element.94), channel_id=1, source_target_pairs={{0,8},{4,12},{8,0},{12,4},{16,24},{20,28},{24,16},{28,20},{1,9},{5... | collective-permute-start | bytes 1032200 | tf_op jit(solution)/shard_map/ppermute | solution.py:185
  24.7 14.4 %collective-permute-start.17 = (bf16[32,3072]{1,0:T(8,128)(2,1)S(1)}, bf16[32,3072]{1,0:T(8,128)(2,1)S(1)}, u32[]{:S(2)}, u32[]{:S(2)}) collective-permute-start(bf16[32,3072]{1,0:T(8,128)(2,1)S(1)} %pad_maximum_fusion.2), channel_id=1, source_target_pairs={{0,2},{1,3},{2,0},{3,1},{4,6},{5,7},{6,4},{7,5},{8,10},{9,11},{10,... | collective-permute-start | bytes 589832 | tf_op jit(solution)/shard_map/ppermute | solution.py:231
  36.3 5.9 %collective-permute-start.8 = (bf16[48,3072]{1,0:T(8,128)(2,1)S(1)}, bf16[48,3072]{1,0:T(8,128)(2,1)S(1)}, u32[]{:S(2)}, u32[]{:S(2)}) collective-permute-start(bf16[48,3072]{1,0:T(8,128)(2,1)S(1)} %collective-permute-done.6.refs_12_.refs_17_), channel_id=1, source_target_pairs={{0,4},{4,0},{8,12},{12,8},{16,20},{20,16},{24,28},{28,24},{1,5},{5... | collective-permute-start | bytes 884744 | tf_op jit(solution)/shard_map/ppermute | solution.py:185
  38.5 4.1 %collective-permute-start.5 = (bf16[48,3584]{1,0:T(8,128)(2,1)S(1)}, bf16[48,3584]{1,0:T(8,128)(2,1)S(1)}, u32[]{:S(2)}, u32[]{:S(2)}) collective-permute-start(bf16[48,3584]{1,0:T(8,128)(2,1)S(1)} %collective-permute-done.4.refs_3_.refs_11_.refs_16_), channel_id=1, source_target_pairs={{0,4},{4,0},{8,12},{12,8},{16,20},{20,16},{24,28},{28,24},{1,5},{5... | collective-permute-start | bytes 1032200 | tf_op jit(solution)/shard_map/ppermute | solution.py:185
  38.6 4.1 %collective-permute-start.9 = (bf16[48,3072]{1,0:T(8,128)(2,1)S(1)}, bf16[48,3072]{1,0:T(8,128)(2,1)S(1)}, u32[]{:S(2)}, u32[]{:S(2)}) collective-permute-start(bf16[48,3072]{1,0:T(8,128)(2,1)S(1)} %collective-permute-done.7.refs_13_.refs_18_), channel_id=1, source_target_pairs={{0,4},{4,0},{8,12},{12,8},{16,20},{20,16},{24,28},{28,24},{1,5},{5... | collective-permute-start | bytes 884744 | tf_op jit(solution)/shard_map/ppermute | solution.py:185
  39.1 16.8 %collective-permute-start.19 = (bf16[48,3072]{1,0:T(8,128)(2,1)S(1)}, bf16[48,3072]{1,0:T(8,128)(2,1)S(1)}, u32[]{:S(2)}, u32[]{:S(2)}) collective-permute-start(bf16[48,3072]{1,0:T(8,128)(2,1)S(1)} %pad_maximum_fusion.1.refs_9_), channel_id=1, source_target_pairs={{0,8},{4,12},{8,0},{12,4},{16,24},{20,28},{24,16},{28,20},{1,9},{5... | collective-permute-start | bytes 884744 | tf_op jit(solution)/shard_map/ppermute | solution.py:185
  40.7 15.3 %collective-permute-start.20 = (bf16[48,3072]{1,0:T(8,128)(2,1)S(1)}, bf16[48,3072]{1,0:T(8,128)(2,1)S(1)}, u32[]{:S(2)}, u32[]{:S(2)}) collective-permute-start(bf16[48,3072]{1,0:T(8,128)(2,1)S(1)} %pad_maximum_fusion.1.refs_9_), channel_id=1, source_target_pairs={{0,16},{4,20},{8,24},{12,28},{16,0},{20,4},{24,8},{28,12},{1,17},{... | collective-permute-start | bytes 884744 | tf_op jit(solution)/shard_map/ppermute | solution.py:185
  42.2 13.7 %collective-permute-start.21 = (bf16[48,3072]{1,0:T(8,128)(2,1)S(1)}, bf16[48,3072]{1,0:T(8,128)(2,1)S(1)}, u32[]{:S(2)}, u32[]{:S(2)}) collective-permute-start(bf16[48,3072]{1,0:T(8,128)(2,1)S(1)} %pad_maximum_fusion.1.refs_9_), channel_id=1, source_target_pairs={{0,24},{4,28},{8,16},{12,20},{16,8},{20,12},{24,0},{28,4},{1,25},{... | collective-permute-start | bytes 884744 | tf_op jit(solution)/shard_map/ppermute | solution.py:185
  46.4 5.6 %collective-permute-start.10 = (bf16[16,512]{1,0:T(8,128)(2,1)S(1)}, bf16[16,512]{1,0:T(8,128)(2,1)S(1)}, u32[]{:S(2)}, u32[]{:S(2)}) collective-permute-start(bf16[16,512]{1,0:T(8,128)(2,1)S(1)} %get-tuple-element.102), channel_id=1, source_target_pairs={{0,1},{1,2},{2,3},{3,0},{4,5},{5,6},{6,7},{7,4},{8,9},{9,10},{10,1... | collective-permute-start | bytes 49160 | tf_op jit(solution)/shard_map/ppermute | solution.py:468
  46.8 5.3 %collective-permute-start.11 = (bf16[16,512]{1,0:T(8,128)(2,1)S(1)}, bf16[16,512]{1,0:T(8,128)(2,1)S(1)}, u32[]{:S(2)}, u32[]{:S(2)}) collective-permute-start(bf16[16,512]{1,0:T(8,128)(2,1)S(1)} %get-tuple-element.103), channel_id=1, source_target_pairs={{0,2},{1,3},{2,0},{3,1},{4,6},{5,7},{6,4},{7,5},{8,10},{9,11},{10,... | collective-permute-start | bytes 49160 | tf_op jit(solution)/shard_map/ppermute | solution.py:468
  56.0 5.4 %collective-permute-start.22 = (bf16[144,3072]{1,0:T(8,128)(2,1)S(1)}, bf16[144,3072]{1,0:T(8,128)(2,1)S(1)}, u32[]{:S(2)}, u32[]{:S(2)}) collective-permute-start(bf16[144,3072]{1,0:T(8,128)(2,1)S(1)} %pad_maximum_fusion), channel_id=1, source_target_pairs={{0,4},{4,0},{8,12},{12,8},{16,20},{20,16},{24,28},{28,24},{1,5},{5... | collective-permute-start | bytes 2654216 | tf_op jit(solution)/shard_map/ppermute | solution.py:185
  56.1 5.3 %collective-permute-start.18 = (bf16[48,3072]{1,0:T(8,128)(2,1)S(1)}, bf16[48,3072]{1,0:T(8,128)(2,1)S(1)}, u32[]{:S(2)}, u32[]{:S(2)}) collective-permute-start(bf16[48,3072]{1,0:T(8,128)(2,1)S(1)} %pad_maximum_fusion.1.refs_9_), channel_id=1, source_target_pairs={{0,4},{4,0},{8,12},{12,8},{16,20},{20,16},{24,28},{28,24},{1,5},{5... | collective-permute-start | bytes 884744 | tf_op jit(solution)/shard_map/ppermute | solution.py:185
  66.9 3.9 %collective-permute-start.24 = (bf16[16,512]{1,0:T(8,128)(2,1)S(1)}, bf16[16,512]{1,0:T(8,128)(2,1)S(1)}, u32[]{:S(2)}, u32[]{:S(2)}) collective-permute-start(bf16[16,512]{1,0:T(8,128)(2,1)S(1)} %get-tuple-element.121), channel_id=1, source_target_pairs={{0,8},{4,12},{8,0},{12,4},{1,9},{5,13},{9,1},{13,5},{2,10},{6,14},... | collective-permute-start | bytes 49160 | tf_op jit(solution)/shard_map/ppermute | solution.py:474
  72.9 4.6 %collective-permute-start.27 = (bf16[16,512]{1,0:T(8,128)(2,1)S(1)}, bf16[16,512]{1,0:T(8,128)(2,1)S(1)}, u32[]{:S(2)}, u32[]{:S(2)}) collective-permute-start(bf16[16,512]{1,0:T(8,128)(2,1)S(1)} %get-tuple-element.125), channel_id=1, source_target_pairs={{0,2},{1,3},{2,0},{3,1},{4,6},{5,7},{6,4},{7,5},{8,10},{9,11},{10,... | collective-permute-start | bytes 49160 | tf_op jit(solution)/shard_map/ppermute | solution.py:468
  72.9 5.5 %collective-permute-start.28 = (bf16[16,512]{1,0:T(8,128)(2,1)S(1)}, bf16[16,512]{1,0:T(8,128)(2,1)S(1)}, u32[]{:S(2)}, u32[]{:S(2)}) collective-permute-start(bf16[16,512]{1,0:T(8,128)(2,1)S(1)} %get-tuple-element.126), channel_id=1, source_target_pairs={{0,1},{1,2},{2,3},{3,0},{4,5},{5,6},{6,7},{7,4},{8,9},{9,10},{10,1... | collective-permute-start | bytes 49160 | tf_op jit(solution)/shard_map/ppermute | solution.py:468
  81.7 3.8 %collective-permute-start.30 = (bf16[16,512]{1,0:T(8,128)(2,1)S(1)}, bf16[16,512]{1,0:T(8,128)(2,1)S(1)}, u32[]{:S(2)}, u32[]{:S(2)}) collective-permute-start(bf16[16,512]{1,0:T(8,128)(2,1)S(1)} %get-tuple-element.139), channel_id=1, source_target_pairs={{0,8},{4,12},{8,0},{12,4},{1,9},{5,13},{9,1},{13,5},{2,10},{6,14},... | collective-permute-start | bytes 49160 | tf_op jit(solution)/shard_map/ppermute | solution.py:474
  87.2 4.6 %collective-permute-start.33 = (bf16[16,512]{1,0:T(8,128)(2,1)S(1)}, bf16[16,512]{1,0:T(8,128)(2,1)S(1)}, u32[]{:S(2)}, u32[]{:S(2)}) collective-permute-start(bf16[16,512]{1,0:T(8,128)(2,1)S(1)} %get-tuple-element.143), channel_id=1, source_target_pairs={{0,2},{1,3},{2,0},{3,1},{4,6},{5,7},{6,4},{7,5},{8,10},{9,11},{10,... | collective-permute-start | bytes 49160 | tf_op jit(solution)/shard_map/ppermute | solution.py:468
  87.6 5.5 %collective-permute-start.34 = (bf16[16,512]{1,0:T(8,128)(2,1)S(1)}, bf16[16,512]{1,0:T(8,128)(2,1)S(1)}, u32[]{:S(2)}, u32[]{:S(2)}) collective-permute-start(bf16[16,512]{1,0:T(8,128)(2,1)S(1)} %get-tuple-element.144), channel_id=1, source_target_pairs={{0,1},{1,2},{2,3},{3,0},{4,5},{5,6},{6,7},{7,4},{8,9},{9,10},{10,1... | collective-permute-start | bytes 49160 | tf_op jit(solution)/shard_map/ppermute | solution.py:468
  (11 other events, 32.6 us)

commit v8 on v7

--- a/solution.py
+++ b/solution.py
@@ -1,3 +1,5 @@
+import functools
+
 import jax
 import jax.numpy as jnp
 from jax import lax
@@ -102,7 +104,7 @@
         + [pltpu.VMEM(out_shape[i].shape, out_shape[i].dtype) for i in last]
         + [pltpu.SemaphoreType.DMA((max(sum(far), 1),)), pltpu.SemaphoreType.DMA((max(len(last), 1),))]
         + list(scratch),
-        name=kernel.__name__,
+        name=getattr(kernel, "func", kernel).__name__,
         cost_estimate=pl.CostEstimate(flops=flops, bytes_accessed=total, transcendentals=0),
         compiler_params=pltpu.CompilerParams(vmem_limit_bytes=24 * 1024 * 1024),
     )(*arrays)
@@ -185,11 +187,12 @@
     return lax.ppermute(x, ("groups", "graph"), [(p, p ^ flip) for p in range(planes)])
 
 
-def start(grid_lat, grid_send, shards, tables):
+def start(grid_lat, grid_send, shards, make_tables):
     grid_rows, features = grid_lat.shape
     mp, graph = lax.axis_size("mp"), lax.axis_size("graph")
     step = stride(grid_send.shape[1])
-    sent = [shape(grid_rows, mp * graph * step, BF16)] + [shape(graph * step, features, BF16)] * mp
+    table_shape = shape(grid_rows, grid_send.size, BF16)
+    sent = [table_shape] + [shape(graph * step, features, BF16)] * mp
     planes = lax.axis_size("groups") * graph
     hidden = shards[1].shape[0]
     if planes != 8 or mp != 4 or hidden != 128 or features != FEATURES:
@@ -199,8 +202,8 @@
             rows.append(lax.all_gather(shards[2 * i], "mp", axis=1, tiled=True).T)
             rows.append(lax.all_gather(shards[2 * i + 1], "mp", axis=0, tiled=True))
         enc, proc = jnp.concatenate(rows[:4], axis=1), jnp.concatenate(rows[4:], axis=1)
-        arrived = exchange(outgoing, step)
-        return [enc], lambda moved: [proc], arrived, grid_t, tables
+        arrived = exchange_levels(outgoing, step)
+        return [enc], lambda after: [proc], arrived, grid_t, make_tables(outgoing[0])
     far = [Far(s) for s in shards]
     piece = hidden // planes
     width = 6 * features
@@ -213,7 +216,9 @@
     )
     enc_own, proc_own = call(own_kernel, [shape(hidden, width, BF16)] * 2, far)
     messages = [along(m, i + 1) for i, m in enumerate(messages)]
-    kept, enc_own, *tables = lax.optimization_barrier((kept, enc_own, *tables))
+    kept, proc_piece, enc_own = lax.optimization_barrier((kept, proc_piece, enc_own))
+    beside_me = lax.ppermute(proc_piece, "mp", [(m, m ^ 1) for m in range(mp)])
+    kept, beside_me = lax.optimization_barrier((kept, beside_me))
     rows = mp * step
     near, first, both = call(
         join_kernel,
@@ -221,21 +226,21 @@
         kept,
         messages,
     )
-    x, y, corner, core = across(both, 2), across(first, 4), across(first, 6), across(both, 1)
-    proc_piece, _ = lax.optimization_barrier((proc_piece, core))
-    x_core = across(x, 1)
-    enc = [enc_own, first, core, x, y, corner, x_core, across(y, 1), across(corner, 1)]
+    x, y, corner = across(both, 2), across(first, 4), across(first, 6)
+    pair = jnp.concatenate([proc_piece, beside_me])
+    pairs = lax.ppermute(pair, "mp", [(m, m ^ 2) for m in range(mp)])
+    proc_first = jnp.concatenate([beside_me, pairs])
+    tables = make_tables(pairs)
+    both, x, y, corner, _ = lax.optimization_barrier((both, x, y, corner, tables[0]))
+    core, x_core, others = across(both, 1), across(x, 1), across(jnp.concatenate([y, corner]), 1)
+    enc = [enc_own, first, core, x, y, corner, x_core, others]
     arrived = [near, core, x, x_core]
-    beside_me = lax.ppermute(proc_piece, "mp", [(m, m ^ 1) for m in range(mp)])
-    pair = jnp.concatenate([proc_piece, beside_me])
-    others = lax.ppermute(pair, "mp", [(m, m ^ 2) for m in range(mp)])
-    proc_first = jnp.concatenate([beside_me, others])
     proc_first, *_ = lax.optimization_barrier((proc_first, x, y, corner))
     plane = [across(proc_first, flip) for flip in (2, 4, 6)]
     proc = [proc_own, proc_first, across(proc_first, 1)] + plane
 
-    def finish(moved):
-        tied, *_ = lax.optimization_barrier((jnp.concatenate(plane), *moved))
+    def finish(after):
+        tied, *_ = lax.optimization_barrier((jnp.concatenate(plane), after))
         return proc + [across(tied, 1)]
 
     return enc, finish, arrived, grid_t, tables
@@ -243,9 +248,10 @@
 
 def forward(inputs, first, second):
     before = dot_trans(inputs, first)
-    logistic = jax.nn.sigmoid(before)
-    hidden = (before * logistic).astype(BF16)
-    slope = logistic * (1.0 + before * (1.0 - logistic))
+    logistic = 0.5 + 0.5 * jnp.tanh(0.5 * before)
+    wide = before * logistic
+    hidden = wide.astype(BF16)
+    slope = logistic + wide * (1.0 - logistic)
     summed = dot(hidden, second)
     centered = summed - jnp.mean(summed, axis=-1, keepdims=True)
     rescale = lax.rsqrt(jnp.mean(centered * centered, axis=-1, keepdims=True) + 1e-05)
@@ -284,14 +290,19 @@
     return ((peer // mp ^ lax.axis_index("graph")) * mp + shift) * step + slot
 
 
-def sent_row(index, step):
+def apart_at(peer, slot, step):
+    rank = lax.axis_index("graph") * lax.axis_size("mp") + lax.axis_index("mp")
+    return (peer ^ rank) * step + slot
+
+
+def sent_row(index, step, order):
     width, count = index.shape
     index = index.astype(F32).T
     at = lax.broadcasted_iota(jnp.int32, (count, count * step), 1)
     peer = lax.broadcasted_iota(jnp.int32, (count, count * step), 0)
     row = jnp.zeros(at.shape, F32)
     for slot in range(width):
-        row = jnp.where(sent_at(peer, slot, step) == at, index[:, slot : slot + 1] + 1.0, row)
+        row = jnp.where(order(peer, slot, step) == at, index[:, slot : slot + 1] + 1.0, row)
     return jnp.sum(row, axis=0, keepdims=True).astype(jnp.int32) - 1
 
 
@@ -306,9 +317,10 @@
 
 
 def send_rows(grid, send, table_out):
-    count = table_out.ref.shape[1]
-    one = table(sent_row(send()[...], count // send().shape[1]), grid().shape[0])
-    table_out.ref[...] = one.astype(BF16)
+    index, count = send()[...], grid().shape[0]
+    back = table(sent_row(index, index.shape[0], apart_at), count)
+    table_out.ref[...] = back.astype(BF16)
+    one = table(sent_row(index, stride(index.shape[0]), sent_at), count)
     return dot(one.T.astype(BF16), grid()[...])
 
 
@@ -330,24 +342,55 @@
         out.ref[...] = dot(turn_table(len(blocks), len(outs), step, j), rows).astype(BF16)
 
 
-def tables_kernel(mesh, slot, recv_e, halo, sender, recv_p, *outs):
+def swap_table(kept, bit, last):
+    rows, total, step = kept.rows, kept.total, kept.step
+    row = lax.broadcasted_iota(jnp.int32, (rows, total), 0)
+    at = lax.broadcasted_iota(jnp.int32, (rows, total), 1)
+    block = row // step
+    peer = block // bit * (2 * bit) + block % bit + (bit if kept.sent else 0)
+    if last:
+        source = peer // (2 * last) * last + peer % last + peer // last % 2 * (total // step // 2)
+    else:
+        source = peer
+    return jnp.where(at == source * step + row % step, 1.0, 0.0).astype(BF16)
+
+
+class Pick:
+    def __init__(self, total, step, sent):
+        self.rows, self.total, self.step, self.sent = total // 2, total, step, sent
+
+
+def swap(rows, step, bit, last, keep_out, send_out):
+    total = rows.shape[0]
+    for out, sent in ((keep_out, False), (send_out, True)):
+        picks = swap_table(Pick(total, step, sent), bit, last)
+        out.ref[...] = dot(picks, rows).astype(BF16)
+
+
+def tables_kernel(after, mesh, slot, recv_e, halo, sender, recv_p, *outs):
+    slot_t, slot_g, enc_t, enc_g, halo_t, halo_g, sender_t, sender_g, proc_t, proc_g, recv_rows = outs
     mesh_rows = mesh().shape[0]
-    peers = halo().shape[1]
-    slot_step, halo_step = outs[0].ref.shape[0] // peers, outs[4].ref.shape[1] // peers
-    capacity, halo_capacity = slot_step, halo().shape[0]
+    peers, halo_capacity = halo().shape[1], halo().shape[0]
+    capacity = slot_t.ref.shape[0] // peers
     slots = slot()[...]
-    slots = arrived_at(slots // capacity, slots % capacity, slot_step)
+    peer, place = slots // capacity, slots % capacity
+    slot_t.ref[...] = table(apart_at(peer, place, capacity), slot_t.ref.shape[0]).astype(BF16)
+    slots = arrived_at(peer, place, slot_g.ref.shape[1] // peers)
+    slot_g.ref[...] = table(slots, slot_g.ref.shape[1]).T.astype(BF16)
     senders = sender()[...]
     remote = jnp.maximum(senders - mesh_rows, 0)
-    remote = arrived_at(remote // halo_capacity, remote % halo_capacity, halo_step)
+    remote = apart_at(remote // halo_capacity, remote % halo_capacity, halo_capacity)
     senders = jnp.where(senders < mesh_rows, senders, mesh_rows + remote)
-    rows = (slots, recv_e()[...], sent_row(halo()[...], halo_step), senders, recv_p()[...])
-    for i, row in enumerate(rows):
-        scatter, gather = outs[2 * i : 2 * i + 2]
+    for row, scatter, gather in (
+        (recv_e()[...], enc_t, enc_g),
+        (sent_row(halo()[...], halo_capacity, apart_at), halo_t, halo_g),
+        (senders, sender_t, sender_g),
+        (recv_p()[...], proc_t, proc_g),
+    ):
         one = table(row, scatter.ref.shape[0])
         scatter.ref[...] = one.astype(BF16)
         gather.ref[...] = one.T.astype(BF16)
-    outs[10].ref[...] = dot(outs[3].ref[...], mesh()[...]).astype(BF16)
+    recv_rows.ref[...] = dot(enc_g.ref[...], mesh()[...]).astype(BF16)
 
 
 def arrived_rows(blocks):
@@ -362,7 +405,7 @@
 
 
 def encode_kernel(
-    recv_rows, arrived, slot_g, enc_t, mesh, weights, halo_g,
+    halo_step, recv_rows, arrived, slot_g, enc_t, mesh, weights, halo_g,
     one_out, slope_e, normed_e, scale_e, slope_n, normed_n, scale_n, *halo_out,
 ):
     rows_in = arrived_rows(arrived)
@@ -384,14 +427,14 @@
     )
     one = (own.astype(F32) + normed).astype(BF16)
     one_out.ref[...] = one
-    split(dot(halo_g()[...], one), halo_out)
+    swap(dot(halo_g()[...], one).astype(BF16), halo_step, 1, 0, *halo_out)
     slope_n.ref[...] = slope
     normed_n.ref[...] = rounded
     scale_n.ref[...] = jnp.broadcast_to(rescale, scale_n.ref.shape)
 
 
 def process_kernel(
-    cotangent_in, one_in, halo, sender_g, proc_g, weights, proc_t, sender_t, two, grad_one, *refs
+    halo_step, cotangent_in, one_in, halo, sender_g, proc_g, weights, proc_t, sender_t, two, grad_one, *refs
 ):
     grad_halo, (slope_p, normed_p, scale_p, ga_p) = refs[:-4], refs[-4:]
     features = FEATURES
@@ -426,14 +469,14 @@
         )
     by_send = dot(sender_t()[...], ga_p[...]).astype(BF16)
     g_send = dot(by_send, first[:, :features])
-    split(g_send[mesh_rows:, :], grad_halo)
+    swap(g_send[mesh_rows:, :].astype(BF16), halo_step, 1, 0, *grad_halo)
     by_recv = dot(proc_t()[...], ga_p[...]).astype(BF16)
     g_recv = dot(by_recv, first[:, features:])
     grad_one.ref[...] = cotangent + g_q[:, :features] + g_recv + g_send[:mesh_rows, :]
 
 
 def decode_kernel(
-    back, halo_t, grad_in, slope_n, normed_n, scale_n, enc_g, slope_e, normed_e, scale_e,
+    step, back, halo_t, grad_in, slope_n, normed_n, scale_n, enc_g, slope_e, normed_e, scale_e,
     weights, slot_t, enc_t, mesh_grad, *refs
 ):
     grad_slots, ga_e = refs[:-1], refs[-1]
@@ -454,7 +497,7 @@
     by_recv = dot(enc_t()[...], ga_e[...]).astype(BF16)
     mesh_grad.send(grad_one + g_n[:, :features] + dot(by_recv, first[:, features:]))
     by_slot = dot(slot_t()[...], ga_e[...]).astype(BF16)
-    split(dot(by_slot, first[:, :features]), grad_slots)
+    swap(dot(by_slot, first[:, :features]).astype(BF16), step, 1, 0, *grad_slots)
 
 
 def grid_kernel(back, table_in, out):
@@ -479,21 +522,31 @@
     return call(turn_kernel, [out] * count, list(blocks))
 
 
-def exchange(blocks, step):
-    return second_level(first_level(blocks, step))
-
-
-def first_level(blocks, step):
-    return turn([along(b, s) for s, b in enumerate(blocks)], lax.axis_size("graph"), step)
-
-
-def second_level(blocks):
+def exchange_levels(blocks, step):
+    blocks = turn([along(b, s) for s, b in enumerate(blocks)], lax.axis_size("graph"), step)
     return [beside(b, t) for t, b in enumerate(blocks)]
 
 
-def exchange_back(blocks, step):
-    blocks = turn([beside(b, t) for t, b in enumerate(blocks)], lax.axis_size("mp"), step)
-    return [along(b, -s) for s, b in enumerate(blocks)]
+def swap_kernel(step, bit, blocks, keep_out, send_out):
+    swap(stacked(blocks), step, bit, bit // 2, keep_out, send_out)
+
+
+def exchange(halves, step, before_last=None):
+    mp, graph = lax.axis_size("mp"), lax.axis_size("graph")
+    keep, send = halves
+    bit = 1
+    while True:
+        if 2 * bit == mp * graph and before_last is not None:
+            before_last(keep)
+        if bit < mp:
+            got = lax.ppermute(send, "mp", [(m, m ^ bit) for m in range(mp)])
+        else:
+            got = lax.ppermute(send, "graph", [(g, g ^ bit // mp) for g in range(graph)])
+        bit *= 2
+        if bit == mp * graph:
+            return [keep, got]
+        half = shape(*keep.shape, BF16)
+        keep, send = call(functools.partial(swap_kernel, step, bit), [half] * 2, [keep, got])
 
 
 def local(
@@ -512,14 +565,14 @@
     mesh_rows = mesh_lat.shape[0]
     edges = g2m_slot.shape[0]
     mesh_edges = mesh_sender.shape[0]
-    mp, graph = lax.axis_size("mp"), lax.axis_size("graph")
-    step, halo_step = stride(grid_send.shape[1]), stride(halo_send.shape[1])
-    slots, halos = mp * graph * step, mp * graph * halo_step
-    tables = call(
+    peers = lax.axis_size("mp") * lax.axis_size("graph")
+    step, halo_step = grid_send.shape[1], halo_send.shape[1]
+    slots, halos, spread = grid_send.size, halo_send.size, peers * stride(step)
+    make_tables = lambda after: call(
         tables_kernel,
         [
             shape(slots, edges, BF16),
-            shape(edges, slots, BF16),
+            shape(edges, spread, BF16),
             shape(mesh_rows, edges, BF16),
             shape(edges, mesh_rows, BF16),
             shape(mesh_rows, halos, BF16),
@@ -530,6 +583,7 @@
             shape(mesh_edges, mesh_rows, BF16),
             shape(edges, features, BF16),
         ],
+        after,
         Far(mesh_lat),
         Far(g2m_slot.reshape(1, edges)),
         Far(g2m_receiver.reshape(1, edges)),
@@ -537,7 +591,7 @@
         Far(mesh_sender.reshape(1, mesh_edges)),
         Far(mesh_receiver.reshape(1, mesh_edges)),
     )
-    enc, finish, arrived, grid_t, tables = start(grid_lat, grid_send, shards, tables)
+    enc, finish, arrived, grid_t, tables = start(grid_lat, grid_send, shards, make_tables)
     slot_t, slot_g, enc_t, enc_g, halo_t, halo_g, sender_t, sender_g, proc_t, proc_g, recv_rows = tables
     saved = [
         shape(edges, features, BF16),
@@ -547,9 +601,10 @@
         shape(mesh_rows, features, BF16),
         shape(mesh_rows, LANES, F32),
     ]
+    half, grid_half = shape(halos // 2, features, BF16), shape(slots // 2, features, BF16)
     mesh_one, slope_e, normed_e, scale_e, slope_n, normed_n, scale_n, *halo_out = call(
-        encode_kernel,
-        [shape(mesh_rows, features, BF16)] + saved + [shape(graph * halo_step, features, BF16)] * mp,
+        functools.partial(encode_kernel, halo_step),
+        [shape(mesh_rows, features, BF16)] + saved + [half] * 2,
         recv_rows,
         arrived,
         slot_g,
@@ -559,13 +614,11 @@
         halo_g,
         flops=3 * 10**9,
     )
-    moved = first_level(halo_out, halo_step)
-    proc = finish(moved)
-    halo_in = second_level(moved)
+    proc = []
+    halo_in = exchange(halo_out, halo_step, lambda kept: proc.extend(finish(kept)))
     mesh_two, grad_one, *grad_halo = call(
-        process_kernel,
-        [shape(mesh_rows, features, BF16), shape(mesh_rows, features, F32)]
-        + [shape(mp * halo_step, features, BF16)] * graph,
+        functools.partial(process_kernel, halo_step),
+        [shape(mesh_rows, features, BF16), shape(mesh_rows, features, F32)] + [half] * 2,
         Far(cotangent),
         mesh_one,
         halo_in,
@@ -583,10 +636,10 @@
             pltpu.VMEM((mesh_edges, features), BF16),
         ],
     )
-    halo_back = exchange_back(grad_halo, halo_step)
+    halo_back = exchange(grad_halo, halo_step)
     mesh_grad, *grad_slots = call(
-        decode_kernel,
-        [shape(mesh_rows, features, F32)] + [shape(mp * step, features, BF16)] * graph,
+        functools.partial(decode_kernel, step),
+        [shape(mesh_rows, features, F32)] + [grid_half] * 2,
         halo_back,
         halo_t,
         grad_one,
@@ -604,7 +657,7 @@
         flops=3 * 10**9,
         scratch=[pltpu.VMEM((edges, features), BF16)],
     )
-    returned = exchange_back(grad_slots, step)
+    returned = exchange(grad_slots, step)
     (grid_grad,) = call(
         grid_kernel, [shape(grid_rows, features, F32)], returned, grid_t, last=(0,)
     )

time: 94.8 us -> 98.4 us (1.038)
  waiting for transfers between devices: 39.3 us -> 50 us
  starting transfers between devices: 33.8 us -> 25.3 us
  Pallas kernels: 20.3 us -> 21.9 us
    ppermute x10 -> x13, waiting for transfers between devices: 7.77 us -> 41.7 us  [the longest x6 20.5 us: exchange(): got = lax.ppermute(send, 'mp', [(m, m ^ bit) for m in range(mp)])]
    ppermute x12 -> x3, waiting for transfers between devices: 17.7 us -> 0.01 us  [along(): lax.ppermute(block, 'mp', [(m, (m + shift) % size) for m in range(size)])]
    ppermute x12 -> x11, waiting for transfers between devices: 13.8 us -> 2.75 us  [across(): lax.ppermute(x, ('groups', 'graph'), [(p, p ^ flip) for p in range(planes)])]
    ppermute x12 -> x3, starting transfers between devices: 15.3 us -> 7.01 us  [along(): lax.ppermute(block, 'mp', [(m, (m + shift) % size) for m in range(size)])]
    ppermute x1, waiting for transfers between devices: 0.01 us -> 5.48 us  [start(): beside_me = lax.ppermute(proc_piece, 'mp', [(m, m ^ 1) for m in range(mp)])]
    ppermute x1, starting transfers between devices: 2.92 us -> 0.75 us  [start(): beside_me = lax.ppermute(proc_piece, 'mp', [(m, m ^ 1) for m in range(mp)])]
    pallas_call x11 -> x17, Pallas kernels: 20.3 us -> 21.9 us  [call(): pl.pallas_call(body, out_shape=out_shape, in_specs=[hbm if away else vmem...]
    ppermute x10 -> x13, starting transfers between devices: 7.43 us -> 8.55 us  [the longest x6 5.4 us: exchange(): got = lax.ppermute(send, 'mp', [(m, m ^ bit) for m in range(mp)])]
  transfers between devices with their start and end apart: 35 -> 28, of which waited for: 18 -> 16; matrix products, arithmetic and copies ran while one was open for 0% -> 0% of each run, Pallas kernels for 8% -> 8%
where the time goes in v8:
time: 98.4 us; the launch traced here: 98.2 us
  waiting for transfers between devices  50 us (51%)
  starting transfers between devices  25.3 us (26%)
  Pallas kernels  21.9 us (22%)
    pallas_call x17, Pallas kernels, call(): pl.pallas_call(body, out_shape=out_shape, in_specs=[hbm if away else vmem...  21.9 us
    ppermute x6, waiting for transfers between devices, exchange(): got = lax.ppermute(send, 'mp', [(m, m ^ bit) for m in range(mp)])  20.5 us
    ppermute x6, waiting for transfers between devices, exchange(): lax.ppermute(send, 'graph', [(g, g ^ bit // mp) for g in range(graph)])  11.1 us
    ppermute x1, waiting for transfers between devices, start(): pairs = lax.ppermute(pair, 'mp', [(m, m ^ 2) for m in range(mp)])  10.2 us
    ppermute x11, starting transfers between devices, across(): lax.ppermute(x, ('groups', 'graph'), [(p, p ^ flip) for p in range(planes)])  8.97 us
    ppermute x3, starting transfers between devices, along(): lax.ppermute(block, 'mp', [(m, (m + shift) % size) for m in range(size)])  7.01 us
    ppermute x1, waiting for transfers between devices, start(): beside_me = lax.ppermute(proc_piece, 'mp', [(m, m ^ 1) for m in range(mp)])  5.48 us
    ppermute x6, starting transfers between devices, exchange(): got = lax.ppermute(send, 'mp', [(m, m ^ bit) for m in range(mp)])  5.4 us
  transfers between devices with their start and end apart: 28, of which 16 were waited for; matrix products, arithmetic and copies ran while one was open for 0% of the time, Pallas kernels for 8%

profile of v8, /device:TPU:0, one launch (start us, length us, event | category | flops | bytes accessed | tf_op | source)
XLA Modules:
  0.0 98.2 jit_solution(8683606641623271499)
XLA Ops:
  0.6 2.4 %prepare_kernel.1 = (bf16[16,3072]{1,0:T(8,128)(2,1)S(1)}, bf16[512,64]{1,0:T(8,128)(2,1)S(1)}, bf16[16,512]{1,0:T(8,128)(2,1)S(1)}, bf16[16,3584]{1,0:T(8,128)(...) custom-call(bf16[512,512]{1,0:T(8,128)(2,1)} %refs_0_.3, s32[4,16]{1,0:T(4,128)} %bitcast.6, ...), custom_call_target="tpu_custom_call" | custom-call | bytes 2097408 | tf_op jit(solution)/shard_map/prepare_kernel/pallas_call | solution.py:98
  3.1 3.1 %collective-permute-start.2 = (bf16[16,3584]{1,0:T(8,128)(2,1)S(1)}, bf16[16,3584]{1,0:T(8,128)(2,1)S(1)}, u32[]{:S(2)}, u32[]{:S(2)}) collective-permute-start(bf16[16,3584]{1,0:T(8,128)(2,1)S(1)} %get-tuple-element.78), channel_id=1, source_target_pairs={{0,1},{1,2},{2,3},{3,0},{4,5},{5,6},{6,7},{7,4},{8,9},{9,10},{10,1... | collective-permute-start | bytes 344072 | tf_op jit(solution)/shard_map/ppermute | solution.py:511
  6.2 2.6 %collective-permute-start.3 = (bf16[16,3584]{1,0:T(8,128)(2,1)S(1)}, bf16[16,3584]{1,0:T(8,128)(2,1)S(1)}, u32[]{:S(2)}, u32[]{:S(2)}) collective-permute-start(bf16[16,3584]{1,0:T(8,128)(2,1)S(1)} %get-tuple-element.79), channel_id=1, source_target_pairs={{0,2},{1,3},{2,0},{3,1},{4,6},{5,7},{6,4},{7,5},{8,10},{9,11},{10,... | collective-permute-start | bytes 344072 | tf_op jit(solution)/shard_map/ppermute | solution.py:511
  10.1 2.0 %own_kernel.1 = (bf16[128,3072]{1,0:T(8,128)(2,1)S(1)}, bf16[128,3072]{1,0:T(8,128)(2,1)S(1)}) custom-call(bf16[1024,128]{1,0:T(8,128)(2,1)} %refs_0_.4, bf16[128,512]{1,0:T(8,128)(2,1)} %refs_1_.2, bf16[1024,128]{1,0:T(8,128)(2,1)} %refs_2_.3, bf16[128,512]{1,0:T(8,128)(2,1)} %refs_3_.3, bf16[1024,128]{1,0:T(8,128)(2,1)} %refs_4_.3, ...), custom_call_target="tpu_custom_call" | custom-call | bytes 1572864 | tf_op jit(solution)/shard_map/own_kernel/pallas_call | solution.py:98
  12.9 5.5 %collective-permute-done = bf16[16,3072]{1,0:T(8,128)(2,1)S(1)} collective-permute-done((bf16[16,3072]{1,0:T(8,128)(2,1)S(1)}, bf16[16,3072]{1,0:T(8,128)(2,1)S(1)}, u32[]{:S(2)}, u32[]{:S(2)}) %collective-permute-start) | collective-permute-done | bytes 98336 | tf_op jit(solution)/shard_map/ppermute | solution.py:220
  18.6 1.7 %collective-permute-start.6 = (bf16[48,3072]{1,0:T(8,128)(2,1)S(1)}, bf16[48,3072]{1,0:T(8,128)(2,1)S(1)}, u32[]{:S(2)}, u32[]{:S(2)}) collective-permute-start(bf16[48,3072]{1,0:T(8,128)(2,1)S(1)} %get-tuple-element.83.refs_9_.refs_12_), channel_id=1, source_target_pairs={{0,16},{4,20},{8,24},{12,28},{16,0},{20,4},{24,8},{28,12},{1,17},{... | collective-permute-start | bytes 884744 | tf_op jit(solution)/shard_map/ppermute | solution.py:187
  20.3 1.4 %collective-permute-start.7 = (bf16[48,3072]{1,0:T(8,128)(2,1)S(1)}, bf16[48,3072]{1,0:T(8,128)(2,1)S(1)}, u32[]{:S(2)}, u32[]{:S(2)}) collective-permute-start(bf16[48,3072]{1,0:T(8,128)(2,1)S(1)} %get-tuple-element.83.refs_9_.refs_12_), channel_id=1, source_target_pairs={{0,24},{4,28},{8,16},{12,20},{16,8},{20,12},{24,0},{28,4},{1,25},{... | collective-permute-start | bytes 884744 | tf_op jit(solution)/shard_map/ppermute | solution.py:187
  22.8 10.2 %collective-permute-done.1.refs_0_ = bf16[32,3072]{1,0:T(8,128)(2,1)S(1)} collective-permute-done((bf16[32,3072]{1,0:T(8,128)(2,1)S(1)}, bf16[32,3072]{1,0:T(8,128)(2,1)S(1)}, u32[]{:S(2)}, u32[]{:S(2)}) %collective-permute-start.1) | collective-permute-done | bytes 196640 | tf_op jit(solution)/shard_map/ppermute | solution.py:231
  33.0 1.7 %tables_kernel.1 = (bf16[64,512]{1,0:T(8,128)(2,1)S(1)}, bf16[512,64]{1,0:T(8,128)(2,1)S(1)}, bf16[256,512]{1,0:T(8,128)(2,1)S(1)}, bf16[512,256]{1,0:T(8,128)(2...) custom-call(bf16[32,3072]{1,0:T(8,128)(2,1)S(1)} %collective-permute, ...), custom_call_target="tpu_custom_call" | custom-call | bytes 467072 | tf_op jit(solution)/shard_map/tables_kernel/pallas_call | solution.py:98
  36.6 1.4 %collective-permute-start.16 = (bf16[48,3072]{1,0:T(8,128)(2,1)S(1)}, bf16[48,3072]{1,0:T(8,128)(2,1)S(1)}, u32[]{:S(2)}, u32[]{:S(2)}) collective-permute-start(bf16[48,3072]{1,0:T(8,128)(2,1)S(1)} %pad_maximum_fusion.2.refs_7_), channel_id=1, source_target_pairs={{0,8},{4,12},{8,0},{12,4},{16,24},{20,28},{24,16},{28,20},{1,9},{5... | collective-permute-start | bytes 884744 | tf_op jit(solution)/shard_map/ppermute | solution.py:187
  38.0 1.5 %collective-permute-start.17 = (bf16[48,3072]{1,0:T(8,128)(2,1)S(1)}, bf16[48,3072]{1,0:T(8,128)(2,1)S(1)}, u32[]{:S(2)}, u32[]{:S(2)}) collective-permute-start(bf16[48,3072]{1,0:T(8,128)(2,1)S(1)} %pad_maximum_fusion.2.refs_7_), channel_id=1, source_target_pairs={{0,16},{4,20},{8,24},{12,28},{16,0},{20,4},{24,8},{28,12},{1,17},{... | collective-permute-start | bytes 884744 | tf_op jit(solution)/shard_map/ppermute | solution.py:187
  40.8 3.9 %encode_kernel.1 = (bf16[256,512]{1,0:T(8,128)(2,1)S(1)}, bf16[512,512]{1,0:T(8,128)(2,1)S(1)}, bf16[512,512]{1,0:T(8,128)(2,1)S(1)}, f32[512,128]{1,0:T(8,128)S...) custom-call(bf16[512,512]{1,0:T(8,128)(2,1)S(1)} %get-tuple-element., ...), custom_call_target="tpu_custom_call" | custom-call | flops 3000000000 | bytes 5472256 | tf_op jit(solution)/shard_map/encode_kernel/pallas_call | solution.py:98
  46.2 2.4 %collective-permute-done.11.refs_1_ = bf16[16,512]{1,0:T(8,128)(2,1)S(1)} collective-permute-done((bf16[16,512]{1,0:T(8,128)(2,1)S(1)}, bf16[16,512]{1,0:T(8,128)(2,1)S(1)}, u32[]{:S(2)}, u32[]{:S(2)}) %collective-permute-start.11) | collective-permute-done | bytes 16416 | tf_op jit(solution)/shard_map/ppermute | solution.py:542
  49.1 4.3 %collective-permute-done.12.refs_1_ = bf16[16,512]{1,0:T(8,128)(2,1)S(1)} collective-permute-done((bf16[16,512]{1,0:T(8,128)(2,1)S(1)}, bf16[16,512]{1,0:T(8,128)(2,1)S(1)}, u32[]{:S(2)}, u32[]{:S(2)}) %collective-permute-start.12) | collective-permute-done | bytes 16416 | tf_op jit(solution)/shard_map/ppermute | solution.py:542
  56.4 1.6 %collective-permute-done.15.refs_8_ = bf16[48,3072]{1,0:T(8,128)(2,1)S(1)} collective-permute-done((bf16[48,3072]{1,0:T(8,128)(2,1)S(1)}, bf16[48,3072]{1,0:T(8,128)(2,1)S(1)}, u32[]{:S(2)}, u32[]{:S(2)}) %collective-permute-start.15) | collective-permute-done | bytes 294944 | tf_op jit(solution)/shard_map/ppermute | solution.py:187
  59.4 5.5 %process_kernel.1 = (bf16[256,512]{1,0:T(8,128)(2,1)}, f32[256,512]{1,0:T(8,128)S(1)}, bf16[16,512]{1,0:T(8,128)(2,1)S(1)}, bf16[16,512]{1,0:T(8,128)(2,1)S(1)}) custom-call(bf16[256,512]{1,0:T(8,128)(2,1)} %refs_0_.5, bf16[256,512]{1,0:T(8,128)(2,1)S(1)} %get-tuple-element.93.refs_1_, bf16[16,512]{1,0:T(8,128)(2,1)S(1)} %get-tuple-element.100.refs_2_, ...), custom_call_target="tpu_custom_call" | custom-call | flops 5000000000 | bytes 4816896 | tf_op jit(solution)/shard_map/process_kernel/pallas_call | solution.py:98
  66.3 2.4 %collective-permute-done.20.refs_1_ = bf16[16,512]{1,0:T(8,128)(2,1)S(1)} collective-permute-done((bf16[16,512]{1,0:T(8,128)(2,1)S(1)}, bf16[16,512]{1,0:T(8,128)(2,1)S(1)}, u32[]{:S(2)}, u32[]{:S(2)}) %collective-permute-start.20) | collective-permute-done | bytes 16416 | tf_op jit(solution)/shard_map/ppermute | solution.py:542
  69.2 4.3 %collective-permute-done.21.refs_1_ = bf16[16,512]{1,0:T(8,128)(2,1)S(1)} collective-permute-done((bf16[16,512]{1,0:T(8,128)(2,1)S(1)}, bf16[16,512]{1,0:T(8,128)(2,1)S(1)}, u32[]{:S(2)}, u32[]{:S(2)}) %collective-permute-start.21) | collective-permute-done | bytes 16416 | tf_op jit(solution)/shard_map/ppermute | solution.py:542
  76.0 3.0 %collective-permute-done.23.refs_1_ = bf16[16,512]{1,0:T(8,128)(2,1)S(1)} collective-permute-done((bf16[16,512]{1,0:T(8,128)(2,1)S(1)}, bf16[16,512]{1,0:T(8,128)(2,1)S(1)}, u32[]{:S(2)}, u32[]{:S(2)}) %collective-permute-start.23) | collective-permute-done | bytes 16416 | tf_op jit(solution)/shard_map/ppermute | solution.py:544
  79.0 3.2 %decode_kernel.1 = (f32[256,512]{1,0:T(8,128)}, bf16[32,512]{1,0:T(8,128)(2,1)S(1)}, bf16[32,512]{1,0:T(8,128)(2,1)S(1)}) custom-call(bf16[16,512]{1,0:T(8,128)(2,1)S(1)} %get-tuple-element.116.refs_0_, bf16[16,512]{1,0:T(8,128)(2,1)S(1)} %collective-permute-done.23.refs_1_, bf16[256,32]{1,0:T(8,128)(2,1)S(1)} %get-tuple-element.118.refs_2_, ...), custom_call_target="tpu_custom_call" | custom-call | flops 3000000000 | bytes 6422528 | tf_op jit(solution)/shard_map/decode_kernel/pallas_call | solution.py:98
  82.2 1.4 %collective-permute-start.24 = (bf16[32,512]{1,0:T(8,128)(2,1)S(1)}, bf16[32,512]{1,0:T(8,128)(2,1)S(1)}, u32[]{:S(2)}, u32[]{:S(2)}) collective-permute-start(bf16[32,512]{1,0:T(8,128)(2,1)S(1)} %get-tuple-element.128), channel_id=1, source_target_pairs={{0,1},{1,0},{2,3},{3,2},{4,5},{5,4},{6,7},{7,6},{8,9},{9,8},{10,11... | collective-permute-start | bytes 98312 | tf_op jit(solution)/shard_map/ppermute | solution.py:542
  83.6 2.5 %collective-permute-done.24.refs_1_ = bf16[32,512]{1,0:T(8,128)(2,1)S(1)} collective-permute-done((bf16[32,512]{1,0:T(8,128)(2,1)S(1)}, bf16[32,512]{1,0:T(8,128)(2,1)S(1)}, u32[]{:S(2)}, u32[]{:S(2)}) %collective-permute-start.24) | collective-permute-done | bytes 32800 | tf_op jit(solution)/shard_map/ppermute | solution.py:542
  86.7 4.5 %collective-permute-done.25.refs_1_ = bf16[32,512]{1,0:T(8,128)(2,1)S(1)} collective-permute-done((bf16[32,512]{1,0:T(8,128)(2,1)S(1)}, bf16[32,512]{1,0:T(8,128)(2,1)S(1)}, u32[]{:S(2)}, u32[]{:S(2)}) %collective-permute-start.25) | collective-permute-done | bytes 32800 | tf_op jit(solution)/shard_map/ppermute | solution.py:542
  93.7 3.2 %collective-permute-done.27.refs_1_ = bf16[32,512]{1,0:T(8,128)(2,1)S(1)} collective-permute-done((bf16[32,512]{1,0:T(8,128)(2,1)S(1)}, bf16[32,512]{1,0:T(8,128)(2,1)S(1)}, u32[]{:S(2)}, u32[]{:S(2)}) %collective-permute-start.27) | collective-permute-done | bytes 32800 | tf_op jit(solution)/shard_map/ppermute | solution.py:544
  (53 shorter events, 21.3 us)
Async XLA Ops:
  3.1 15.3 %collective-permute-start.2 = (bf16[16,3584]{1,0:T(8,128)(2,1)S(1)}, bf16[16,3584]{1,0:T(8,128)(2,1)S(1)}, u32[]{:S(2)}, u32[]{:S(2)}) collective-permute-start(bf16[16,3584]{1,0:T(8,128)(2,1)S(1)} %get-tuple-element.78), channel_id=1, source_target_pairs={{0,1},{1,2},{2,3},{3,0},{4,5},{5,6},{6,7},{7,4},{8,9},{9,10},{10,1... | collective-permute-start | bytes 344072 | tf_op jit(solution)/shard_map/ppermute | solution.py:511
  6.2 12.2 %collective-permute-start.3 = (bf16[16,3584]{1,0:T(8,128)(2,1)S(1)}, bf16[16,3584]{1,0:T(8,128)(2,1)S(1)}, u32[]{:S(2)}, u32[]{:S(2)}) collective-permute-start(bf16[16,3584]{1,0:T(8,128)(2,1)S(1)} %get-tuple-element.79), channel_id=1, source_target_pairs={{0,2},{1,3},{2,0},{3,1},{4,6},{5,7},{6,4},{7,5},{8,10},{9,11},{10,... | collective-permute-start | bytes 344072 | tf_op jit(solution)/shard_map/ppermute | solution.py:511
  8.8 9.6 %collective-permute-start.4 = (bf16[16,3584]{1,0:T(8,128)(2,1)S(1)}, bf16[16,3584]{1,0:T(8,128)(2,1)S(1)}, u32[]{:S(2)}, u32[]{:S(2)}) collective-permute-start(bf16[16,3584]{1,0:T(8,128)(2,1)S(1)} %get-tuple-element.80), channel_id=1, source_target_pairs={{0,3},{1,0},{2,1},{3,2},{4,7},{5,4},{6,5},{7,6},{8,11},{9,8},{10,9... | collective-permute-start | bytes 344072 | tf_op jit(solution)/shard_map/ppermute | solution.py:511
  12.1 6.2 %collective-permute-start = (bf16[16,3072]{1,0:T(8,128)(2,1)S(1)}, bf16[16,3072]{1,0:T(8,128)(2,1)S(1)}, u32[]{:S(2)}, u32[]{:S(2)}) collective-permute-start(bf16[16,3072]{1,0:T(8,128)(2,1)S(1)} %get-tuple-element.73), channel_id=1, source_target_pairs={{0,1},{1,0},{2,3},{3,2},{4,5},{5,4},{6,7},{7,6},{8,9},{9,8},{10,11... | collective-permute-start | bytes 294920 | tf_op jit(solution)/shard_map/ppermute | solution.py:220
  18.6 16.2 %collective-permute-start.6 = (bf16[48,3072]{1,0:T(8,128)(2,1)S(1)}, bf16[48,3072]{1,0:T(8,128)(2,1)S(1)}, u32[]{:S(2)}, u32[]{:S(2)}) collective-permute-start(bf16[48,3072]{1,0:T(8,128)(2,1)S(1)} %get-tuple-element.83.refs_9_.refs_12_), channel_id=1, source_target_pairs={{0,16},{4,20},{8,24},{12,28},{16,0},{20,4},{24,8},{28,12},{1,17},{... | collective-permute-start | bytes 884744 | tf_op jit(solution)/shard_map/ppermute | solution.py:187
  20.3 14.5 %collective-permute-start.7 = (bf16[48,3072]{1,0:T(8,128)(2,1)S(1)}, bf16[48,3072]{1,0:T(8,128)(2,1)S(1)}, u32[]{:S(2)}, u32[]{:S(2)}) collective-permute-start(bf16[48,3072]{1,0:T(8,128)(2,1)S(1)} %get-tuple-element.83.refs_9_.refs_12_), channel_id=1, source_target_pairs={{0,24},{4,28},{8,16},{12,20},{16,8},{20,12},{24,0},{28,4},{1,25},{... | collective-permute-start | bytes 884744 | tf_op jit(solution)/shard_map/ppermute | solution.py:187
  21.7 14.2 %collective-permute-start.5 = (bf16[48,3584]{1,0:T(8,128)(2,1)S(1)}, bf16[48,3584]{1,0:T(8,128)(2,1)S(1)}, u32[]{:S(2)}, u32[]{:S(2)}) collective-permute-start(bf16[48,3584]{1,0:T(8,128)(2,1)S(1)} %get-tuple-element.85), channel_id=1, source_target_pairs={{0,8},{4,12},{8,0},{12,4},{16,24},{20,28},{24,16},{28,20},{1,9},{5... | collective-permute-start | bytes 1032200 | tf_op jit(solution)/shard_map/ppermute | solution.py:187
  22.2 10.9 %collective-permute-start.1 = (bf16[32,3072]{1,0:T(8,128)(2,1)S(1)}, bf16[32,3072]{1,0:T(8,128)(2,1)S(1)}, u32[]{:S(2)}, u32[]{:S(2)}) collective-permute-start(bf16[32,3072]{1,0:T(8,128)(2,1)S(1)} %pad_maximum_fusion.3), channel_id=1, source_target_pairs={{0,2},{1,3},{2,0},{3,1},{4,6},{5,7},{6,4},{7,5},{8,10},{9,11},{10,... | collective-permute-start | bytes 589832 | tf_op jit(solution)/shard_map/ppermute | solution.py:231
  35.9 4.9 %collective-permute-start.10 = (bf16[96,3072]{1,0:T(8,128)(2,1)S(1)}, bf16[96,3072]{1,0:T(8,128)(2,1)S(1)}, u32[]{:S(2)}, u32[]{:S(2)}) collective-permute-start(bf16[96,3072]{1,0:T(8,128)(2,1)S(1)} %pad_maximum_fusion.1), channel_id=1, source_target_pairs={{0,4},{4,0},{8,12},{12,8},{16,20},{20,16},{24,28},{28,24},{1,5},{5... | collective-permute-start | bytes 1769480 | tf_op jit(solution)/shard_map/ppermute | solution.py:187
  36.0 3.5 %collective-permute-start.8 = (bf16[48,3584]{1,0:T(8,128)(2,1)S(1)}, bf16[48,3584]{1,0:T(8,128)(2,1)S(1)}, u32[]{:S(2)}, u32[]{:S(2)}) collective-permute-start(bf16[48,3584]{1,0:T(8,128)(2,1)S(1)} %get-tuple-element.85), channel_id=1, source_target_pairs={{0,4},{4,0},{8,12},{12,8},{16,20},{20,16},{24,28},{28,24},{1,5},{5... | collective-permute-start | bytes 1032200 | tf_op jit(solution)/shard_map/ppermute | solution.py:187
  36.5 4.3 %collective-permute-start.9 = (bf16[48,3584]{1,0:T(8,128)(2,1)S(1)}, bf16[48,3584]{1,0:T(8,128)(2,1)S(1)}, u32[]{:S(2)}, u32[]{:S(2)}) collective-permute-start(bf16[48,3584]{1,0:T(8,128)(2,1)S(1)} %collective-permute-done.5.refs_3_.refs_11_.refs_14_), channel_id=1, source_target_pairs={{0,4},{4,0},{8,12},{12,8},{16,20},{20,16},{24,28},{28,24},{1,5},{5... | collective-permute-start | bytes 1032200 | tf_op jit(solution)/shard_map/ppermute | solution.py:187
  36.6 17.1 %collective-permute-start.16 = (bf16[48,3072]{1,0:T(8,128)(2,1)S(1)}, bf16[48,3072]{1,0:T(8,128)(2,1)S(1)}, u32[]{:S(2)}, u32[]{:S(2)}) collective-permute-start(bf16[48,3072]{1,0:T(8,128)(2,1)S(1)} %pad_maximum_fusion.2.refs_7_), channel_id=1, source_target_pairs={{0,8},{4,12},{8,0},{12,4},{16,24},{20,28},{24,16},{28,20},{1,9},{5... | collective-permute-start | bytes 884744 | tf_op jit(solution)/shard_map/ppermute | solution.py:187
  38.0 15.7 %collective-permute-start.17 = (bf16[48,3072]{1,0:T(8,128)(2,1)S(1)}, bf16[48,3072]{1,0:T(8,128)(2,1)S(1)}, u32[]{:S(2)}, u32[]{:S(2)}) collective-permute-start(bf16[48,3072]{1,0:T(8,128)(2,1)S(1)} %pad_maximum_fusion.2.refs_7_), channel_id=1, source_target_pairs={{0,16},{4,20},{8,24},{12,28},{16,0},{20,4},{24,8},{28,12},{1,17},{... | collective-permute-start | bytes 884744 | tf_op jit(solution)/shard_map/ppermute | solution.py:187
  39.6 14.2 %collective-permute-start.18 = (bf16[48,3072]{1,0:T(8,128)(2,1)S(1)}, bf16[48,3072]{1,0:T(8,128)(2,1)S(1)}, u32[]{:S(2)}, u32[]{:S(2)}) collective-permute-start(bf16[48,3072]{1,0:T(8,128)(2,1)S(1)} %pad_maximum_fusion.2.refs_7_), channel_id=1, source_target_pairs={{0,24},{4,28},{8,16},{12,20},{16,8},{20,12},{24,0},{28,4},{1,25},{... | collective-permute-start | bytes 884744 | tf_op jit(solution)/shard_map/ppermute | solution.py:187
  44.8 3.8 %collective-permute-start.11 = (bf16[16,512]{1,0:T(8,128)(2,1)S(1)}, bf16[16,512]{1,0:T(8,128)(2,1)S(1)}, u32[]{:S(2)}, u32[]{:S(2)}) collective-permute-start(bf16[16,512]{1,0:T(8,128)(2,1)S(1)} %get-tuple-element.95), channel_id=1, source_target_pairs={{0,1},{1,0},{2,3},{3,2},{4,5},{5,4},{6,7},{7,6},{8,9},{9,8},{10,11... | collective-permute-start | bytes 49160 | tf_op jit(solution)/shard_map/ppermute | solution.py:542
  48.7 4.7 %collective-permute-start.12 = (bf16[16,512]{1,0:T(8,128)(2,1)S(1)}, bf16[16,512]{1,0:T(8,128)(2,1)S(1)}, u32[]{:S(2)}, u32[]{:S(2)}) collective-permute-start(bf16[16,512]{1,0:T(8,128)(2,1)S(1)} %get-tuple-element.97), channel_id=1, source_target_pairs={{0,2},{1,3},{2,0},{3,1},{4,6},{5,7},{6,4},{7,5},{8,10},{9,11},{10,... | collective-permute-start | bytes 49160 | tf_op jit(solution)/shard_map/ppermute | solution.py:542
  55.1 4.3 %collective-permute-start.19 = (bf16[144,3072]{1,0:T(8,128)(2,1)S(1)}, bf16[144,3072]{1,0:T(8,128)(2,1)S(1)}, u32[]{:S(2)}, u32[]{:S(2)}) collective-permute-start(bf16[144,3072]{1,0:T(8,128)(2,1)S(1)} %pad_maximum_fusion), channel_id=1, source_target_pairs={{0,4},{4,0},{8,12},{12,8},{16,20},{20,16},{24,28},{28,24},{1,5},{5... | collective-permute-start | bytes 2654216 | tf_op jit(solution)/shard_map/ppermute | solution.py:187
  55.6 3.7 %collective-permute-start.14 = (bf16[16,512]{1,0:T(8,128)(2,1)S(1)}, bf16[16,512]{1,0:T(8,128)(2,1)S(1)}, u32[]{:S(2)}, u32[]{:S(2)}) collective-permute-start(bf16[16,512]{1,0:T(8,128)(2,1)S(1)} %get-tuple-element.101), channel_id=1, source_target_pairs={{0,8},{4,12},{8,0},{12,4},{1,9},{5,13},{9,1},{13,5},{2,10},{6,14},... | collective-permute-start | bytes 49160 | tf_op jit(solution)/shard_map/ppermute | solution.py:544
  64.9 3.8 %collective-permute-start.20 = (bf16[16,512]{1,0:T(8,128)(2,1)S(1)}, bf16[16,512]{1,0:T(8,128)(2,1)S(1)}, u32[]{:S(2)}, u32[]{:S(2)}) collective-permute-start(bf16[16,512]{1,0:T(8,128)(2,1)S(1)} %get-tuple-element.111), channel_id=1, source_target_pairs={{0,1},{1,0},{2,3},{3,2},{4,5},{5,4},{6,7},{7,6},{8,9},{9,8},{10,11... | collective-permute-start | bytes 49160 | tf_op jit(solution)/shard_map/ppermute | solution.py:542
  68.8 4.7 %collective-permute-start.21 = (bf16[16,512]{1,0:T(8,128)(2,1)S(1)}, bf16[16,512]{1,0:T(8,128)(2,1)S(1)}, u32[]{:S(2)}, u32[]{:S(2)}) collective-permute-start(bf16[16,512]{1,0:T(8,128)(2,1)S(1)} %get-tuple-element.113), channel_id=1, source_target_pairs={{0,2},{1,3},{2,0},{3,1},{4,6},{5,7},{6,4},{7,5},{8,10},{9,11},{10,... | collective-permute-start | bytes 49160 | tf_op jit(solution)/shard_map/ppermute | solution.py:542
  75.2 3.8 %collective-permute-start.23 = (bf16[16,512]{1,0:T(8,128)(2,1)S(1)}, bf16[16,512]{1,0:T(8,128)(2,1)S(1)}, u32[]{:S(2)}, u32[]{:S(2)}) collective-permute-start(bf16[16,512]{1,0:T(8,128)(2,1)S(1)} %get-tuple-element.117), channel_id=1, source_target_pairs={{0,8},{4,12},{8,0},{12,4},{1,9},{5,13},{9,1},{13,5},{2,10},{6,14},... | collective-permute-start | bytes 49160 | tf_op jit(solution)/shard_map/ppermute | solution.py:544
  82.2 4.0 %collective-permute-start.24 = (bf16[32,512]{1,0:T(8,128)(2,1)S(1)}, bf16[32,512]{1,0:T(8,128)(2,1)S(1)}, u32[]{:S(2)}, u32[]{:S(2)}) collective-permute-start(bf16[32,512]{1,0:T(8,128)(2,1)S(1)} %get-tuple-element.128), channel_id=1, source_target_pairs={{0,1},{1,0},{2,3},{3,2},{4,5},{5,4},{6,7},{7,6},{8,9},{9,8},{10,11... | collective-permute-start | bytes 98312 | tf_op jit(solution)/shard_map/ppermute | solution.py:542
  86.3 4.9 %collective-permute-start.25 = (bf16[32,512]{1,0:T(8,128)(2,1)S(1)}, bf16[32,512]{1,0:T(8,128)(2,1)S(1)}, u32[]{:S(2)}, u32[]{:S(2)}) collective-permute-start(bf16[32,512]{1,0:T(8,128)(2,1)S(1)} %get-tuple-element.130), channel_id=1, source_target_pairs={{0,2},{1,3},{2,0},{3,1},{4,6},{5,7},{6,4},{7,5},{8,10},{9,11},{10,... | collective-permute-start | bytes 98312 | tf_op jit(solution)/shard_map/ppermute | solution.py:542
  92.9 4.0 %collective-permute-start.27 = (bf16[32,512]{1,0:T(8,128)(2,1)S(1)}, bf16[32,512]{1,0:T(8,128)(2,1)S(1)}, u32[]{:S(2)}, u32[]{:S(2)}) collective-permute-start(bf16[32,512]{1,0:T(8,128)(2,1)S(1)} %get-tuple-element.134), channel_id=1, source_target_pairs={{0,8},{4,12},{8,0},{12,4},{1,9},{5,13},{9,1},{13,5},{2,10},{6,14},... | collective-permute-start | bytes 98312 | tf_op jit(solution)/shard_map/ppermute | solution.py:544
  (4 other events, 6.5 us)

commit v9 on v7

--- a/solution.py
+++ b/solution.py
@@ -1,3 +1,5 @@
+import functools
+
 import jax
 import jax.numpy as jnp
 from jax import lax
@@ -102,7 +104,7 @@
         + [pltpu.VMEM(out_shape[i].shape, out_shape[i].dtype) for i in last]
         + [pltpu.SemaphoreType.DMA((max(sum(far), 1),)), pltpu.SemaphoreType.DMA((max(len(last), 1),))]
         + list(scratch),
-        name=kernel.__name__,
+        name=getattr(kernel, "func", kernel).__name__,
         cost_estimate=pl.CostEstimate(flops=flops, bytes_accessed=total, transcendentals=0),
         compiler_params=pltpu.CompilerParams(vmem_limit_bytes=24 * 1024 * 1024),
     )(*arrays)
@@ -141,7 +143,7 @@
         for out in (proc_piece,) if i // 2 else messages:
             out.ref[:, low : low + 2 * FEATURES] = first
             out.ref[:, low + 2 * FEATURES : low + width] = second
-    outgoing = send_rows(grid, send, table_out)
+    outgoing = send_rows(grid, send, table_out, sent_at, stride(send().shape[0]))
     size = kept.ref.shape[0]
     kept.ref[...] = outgoing[:size, :].astype(BF16)
     for i, out in enumerate(messages):
@@ -185,22 +187,24 @@
     return lax.ppermute(x, ("groups", "graph"), [(p, p ^ flip) for p in range(planes)])
 
 
-def start(grid_lat, grid_send, shards, tables):
+def start(grid_lat, grid_send, shards, make_tables):
     grid_rows, features = grid_lat.shape
     mp, graph = lax.axis_size("mp"), lax.axis_size("graph")
     step = stride(grid_send.shape[1])
-    sent = [shape(grid_rows, mp * graph * step, BF16)] + [shape(graph * step, features, BF16)] * mp
+    table_shape = pltpu.HBM((grid_rows, grid_send.size), BF16)
+    sent = [table_shape] + [shape(graph * step, features, BF16)] * mp
     planes = lax.axis_size("groups") * graph
     hidden = shards[1].shape[0]
     if planes != 8 or mp != 4 or hidden != 128 or features != FEATURES:
-        grid_t, *outgoing = call(send_kernel, sent, Far(grid_lat), Far(grid_send.T))
+        packed = shape(grid_send.size * features // LANES, LANES, BF16)
+        grid_t, *outgoing = call(send_kernel, [table_shape, packed], Far(grid_lat), Far(grid_send.T), last=(0,))
         rows = []
         for i in range(4):
             rows.append(lax.all_gather(shards[2 * i], "mp", axis=1, tiled=True).T)
             rows.append(lax.all_gather(shards[2 * i + 1], "mp", axis=0, tiled=True))
         enc, proc = jnp.concatenate(rows[:4], axis=1), jnp.concatenate(rows[4:], axis=1)
-        arrived = exchange(outgoing, step)
-        return [enc], lambda moved: [proc], arrived, grid_t, tables
+        arrived = [exchange_all(outgoing[0])]
+        return [enc], lambda one, moved: [proc], arrived, grid_t, make_tables()
     far = [Far(s) for s in shards]
     piece = hidden // planes
     width = 6 * features
@@ -210,10 +214,12 @@
         Far(grid_lat),
         Far(grid_send.T),
         far,
+        last=(1,),
     )
     enc_own, proc_own = call(own_kernel, [shape(hidden, width, BF16)] * 2, far)
     messages = [along(m, i + 1) for i, m in enumerate(messages)]
-    kept, enc_own, *tables = lax.optimization_barrier((kept, enc_own, *tables))
+    tables = make_tables()
+    kept, enc_own, _ = lax.optimization_barrier((kept, enc_own, tables[0]))
     rows = mp * step
     near, first, both = call(
         join_kernel,
@@ -221,31 +227,34 @@
         kept,
         messages,
     )
-    x, y, corner, core = across(both, 2), across(first, 4), across(first, 6), across(both, 1)
-    proc_piece, _ = lax.optimization_barrier((proc_piece, core))
-    x_core = across(x, 1)
-    enc = [enc_own, first, core, x, y, corner, x_core, across(y, 1), across(corner, 1)]
-    arrived = [near, core, x, x_core]
+    x, y, corner = across(both, 2), across(first, 4), across(first, 6)
+    proc_piece, _ = lax.optimization_barrier((proc_piece, near))
     beside_me = lax.ppermute(proc_piece, "mp", [(m, m ^ 1) for m in range(mp)])
     pair = jnp.concatenate([proc_piece, beside_me])
-    others = lax.ppermute(pair, "mp", [(m, m ^ 2) for m in range(mp)])
-    proc_first = jnp.concatenate([beside_me, others])
+    pairs = lax.ppermute(pair, "mp", [(m, m ^ 2) for m in range(mp)])
+    proc_first = jnp.concatenate([beside_me, pairs])
+    both, x, y, corner, _ = lax.optimization_barrier((both, x, y, corner, pairs))
+    core, x_core, others = across(both, 1), across(x, 1), across(jnp.concatenate([y, corner]), 1)
+    enc = [enc_own, first, core, x, y, corner, x_core, others]
+    arrived = [near, core, x, x_core]
     proc_first, *_ = lax.optimization_barrier((proc_first, x, y, corner))
-    plane = [across(proc_first, flip) for flip in (2, 4, 6)]
-    proc = [proc_own, proc_first, across(proc_first, 1)] + plane
-
-    def finish(moved):
-        tied, *_ = lax.optimization_barrier((jnp.concatenate(plane), *moved))
-        return proc + [across(tied, 1)]
+    proc_x, proc_y, proc_core = [across(proc_first, flip) for flip in (2, 4, 1)]
+
+    def finish(one, moved):
+        late, _ = lax.optimization_barrier((proc_x, one))
+        blocks = [proc_x, proc_y, across(late, 4)]
+        tied, *_ = lax.optimization_barrier((jnp.concatenate(blocks), *moved))
+        return [proc_own, proc_first, proc_core] + blocks + [across(tied, 1)]
 
     return enc, finish, arrived, grid_t, tables
 
 
 def forward(inputs, first, second):
     before = dot_trans(inputs, first)
-    logistic = jax.nn.sigmoid(before)
-    hidden = (before * logistic).astype(BF16)
-    slope = logistic * (1.0 + before * (1.0 - logistic))
+    logistic = 0.5 + 0.5 * jnp.tanh(0.5 * before)
+    wide = before * logistic
+    hidden = wide.astype(BF16)
+    slope = logistic + wide * (1.0 - logistic)
     summed = dot(hidden, second)
     centered = summed - jnp.mean(summed, axis=-1, keepdims=True)
     rescale = lax.rsqrt(jnp.mean(centered * centered, axis=-1, keepdims=True) + 1e-05)
@@ -284,14 +293,46 @@
     return ((peer // mp ^ lax.axis_index("graph")) * mp + shift) * step + slot
 
 
-def sent_row(index, step):
+def small():
+    return lax.axis_size("mp") == 4 and lax.axis_size("graph") == 4
+
+
+def plain_at(peer, slot, step):
+    return peer * step + slot
+
+
+def apart(peer):
+    rank = lax.axis_index("graph") * 4 + lax.axis_index("mp")
+    differs = peer ^ rank
+    return differs // 4 % 2, differs // 8 * 4 + differs % 4
+
+
+def out_at(peer, slot, step):
+    if not small():
+        return plain_at(peer, slot, step)
+    core, chip = apart(peer)
+    return (core * 8 + chip) * step + slot
+
+
+def in_at(peer, slot, step):
+    if not small():
+        return plain_at(peer, slot, step)
+    core, chip = apart(peer)
+    return chip * 16 + core * step + slot
+
+
+def in_rows(count, step):
+    return 128 if small() else count * step
+
+
+def sent_row(index, step, order):
     width, count = index.shape
     index = index.astype(F32).T
     at = lax.broadcasted_iota(jnp.int32, (count, count * step), 1)
     peer = lax.broadcasted_iota(jnp.int32, (count, count * step), 0)
     row = jnp.zeros(at.shape, F32)
     for slot in range(width):
-        row = jnp.where(sent_at(peer, slot, step) == at, index[:, slot : slot + 1] + 1.0, row)
+        row = jnp.where(order(peer, slot, step) == at, index[:, slot : slot + 1] + 1.0, row)
     return jnp.sum(row, axis=0, keepdims=True).astype(jnp.int32) - 1
 
 
@@ -305,15 +346,16 @@
         out.ref[...] = rows[i * size : (i + 1) * size, :].astype(BF16)
 
 
-def send_rows(grid, send, table_out):
-    count = table_out.ref.shape[1]
-    one = table(sent_row(send()[...], count // send().shape[1]), grid().shape[0])
-    table_out.ref[...] = one.astype(BF16)
+def send_rows(grid, send, table_out, order, step):
+    index, count = send()[...], grid().shape[0]
+    table_out.send(table(sent_row(index, index.shape[0], plain_at), count).astype(BF16))
+    one = table(sent_row(index, step, order), count)
     return dot(one.T.astype(BF16), grid()[...])
 
 
-def send_kernel(grid, send, table_out, *outgoing):
-    split(send_rows(grid, send, table_out), outgoing)
+def send_kernel(grid, send, table_out, outgoing):
+    rows = send_rows(grid, send, table_out, plain_at, send().shape[0])
+    outgoing.ref[...] = pack_rows(rows.astype(BF16))
 
 
 def turn_table(sources, targets, step, j):
@@ -323,35 +365,97 @@
     return jnp.where(at == source, 1.0, 0.0).astype(BF16)
 
 
-def turn_kernel(blocks, *outs):
+def lane_table(n, blocks, block, tall):
+    sizes = (n * blocks, n) if tall else (n, n * blocks)
+    long = lax.broadcasted_iota(jnp.int32, sizes, 0 if tall else 1)
+    short = lax.broadcasted_iota(jnp.int32, sizes, 1 if tall else 0)
+    return jnp.where(long == short * blocks + block, 1.0, 0.0).astype(BF16)
+
+
+def pack_rows(rows):
+    n, blocks = rows.shape[0], rows.shape[1] // LANES
+    return sum(
+        dot(lane_table(n, blocks, k, True), rows[:, k * LANES : (k + 1) * LANES])
+        for k in range(blocks)
+    ).astype(BF16)
+
+
+def unpack_rows(packed):
+    blocks = FEATURES // LANES
+    n = packed.shape[0] // blocks
+    return jnp.concatenate(
+        [dot(lane_table(n, blocks, k, False), packed).astype(BF16) for k in range(blocks)], axis=1
+    )
+
+
+def pick_rows(rows, count, source):
+    row = lax.broadcasted_iota(jnp.int32, (count, rows.shape[0]), 0)
+    at = lax.broadcasted_iota(jnp.int32, row.shape, 1)
+    return dot(jnp.where(at == source(row), 1.0, 0.0).astype(BF16), rows).astype(BF16)
+
+
+def fan_kernel(step, halves, *outs):
+    rows = stacked(halves)
+    for chip, out in enumerate(outs):
+
+        def source(row, chip=chip):
+            from_row = (row // step * 8 + chip) * step + row % step
+            return jnp.where(row < 2 * step, from_row, -1)
+
+        out.ref[...] = pick_rows(rows, 16, source)
+
+
+def fold_kernel(step, blocks, keep_out, send_out):
     rows = stacked(blocks)
-    step = rows.shape[0] // (len(blocks) * len(outs))
-    for j, out in enumerate(outs):
-        out.ref[...] = dot(turn_table(len(blocks), len(outs), step, j), rows).astype(BF16)
+    for core, out in enumerate((keep_out, send_out)):
+        out.ref[...] = pick_rows(
+            rows, 8 * step, lambda row: row // step * 16 + core * step + row % step
+        )
+
+
+def put(rows, outs):
+    rows = rows.astype(BF16)
+    if len(outs) == 1:
+        outs[0].ref[...] = pack_rows(rows)
+    else:
+        split(rows, outs)
+
+
+def joined(blocks):
+    rows = stacked(blocks)
+    return unpack_rows(rows) if rows.shape[1] == LANES else rows
 
 
 def tables_kernel(mesh, slot, recv_e, halo, sender, recv_p, *outs):
+    slot_t, slot_g, enc_t, enc_g, halo_t, halo_g, sender_t, sender_g, proc_t, proc_g, recv_rows = outs
     mesh_rows = mesh().shape[0]
-    peers = halo().shape[1]
-    slot_step, halo_step = outs[0].ref.shape[0] // peers, outs[4].ref.shape[1] // peers
-    capacity, halo_capacity = slot_step, halo().shape[0]
+    peers, halo_capacity = halo().shape[1], halo().shape[0]
+    capacity = slot_t.ref.shape[0] // peers
     slots = slot()[...]
-    slots = arrived_at(slots // capacity, slots % capacity, slot_step)
+    slot_t.ref[...] = table(slots, slot_t.ref.shape[0]).astype(BF16)
+    if small():
+        slots = arrived_at(slots // capacity, slots % capacity, slot_g.ref.shape[1] // peers)
+    slot_g.ref[...] = table(slots, slot_g.ref.shape[1]).T.astype(BF16)
     senders = sender()[...]
     remote = jnp.maximum(senders - mesh_rows, 0)
-    remote = arrived_at(remote // halo_capacity, remote % halo_capacity, halo_step)
+    remote = in_at(remote // halo_capacity, remote % halo_capacity, halo_capacity)
     senders = jnp.where(senders < mesh_rows, senders, mesh_rows + remote)
-    rows = (slots, recv_e()[...], sent_row(halo()[...], halo_step), senders, recv_p()[...])
-    for i, row in enumerate(rows):
-        scatter, gather = outs[2 * i : 2 * i + 2]
+    for row, scatter, gather in (
+        (recv_e()[...], enc_t, enc_g),
+        (sent_row(halo()[...], halo_capacity, out_at), halo_t, halo_g),
+        (senders, sender_t, sender_g),
+        (recv_p()[...], proc_t, proc_g),
+    ):
         one = table(row, scatter.ref.shape[0])
         scatter.ref[...] = one.astype(BF16)
         gather.ref[...] = one.T.astype(BF16)
-    outs[10].ref[...] = dot(outs[3].ref[...], mesh()[...]).astype(BF16)
+    recv_rows.ref[...] = dot(enc_g.ref[...], mesh()[...]).astype(BF16)
 
 
 def arrived_rows(blocks):
     size = blocks[0]().shape[0]
+    if len(blocks) == 1:
+        return joined(blocks)
     rows = [blocks[0]()[...]]
     for t, block in enumerate(blocks[1:]):
         if block().shape[1] == FEATURES:
@@ -384,7 +488,7 @@
     )
     one = (own.astype(F32) + normed).astype(BF16)
     one_out.ref[...] = one
-    split(dot(halo_g()[...], one), halo_out)
+    put(dot(halo_g()[...], one), halo_out)
     slope_n.ref[...] = slope
     normed_n.ref[...] = rounded
     scale_n.ref[...] = jnp.broadcast_to(rescale, scale_n.ref.shape)
@@ -397,7 +501,7 @@
     features = FEATURES
     one = one_in()[...]
     mesh_rows = one.shape[0]
-    lookup = jnp.concatenate([one, stacked(halo)], axis=0)
+    lookup = jnp.concatenate([one, joined(halo)], axis=0)
     edges = sender_g().shape[0]
     first, second = layers(weights, 0)
     for low in range(0, edges, ROWS):
@@ -426,7 +530,7 @@
         )
     by_send = dot(sender_t()[...], ga_p[...]).astype(BF16)
     g_send = dot(by_send, first[:, :features])
-    split(g_send[mesh_rows:, :], grad_halo)
+    put(g_send[mesh_rows:, :], grad_halo)
     by_recv = dot(proc_t()[...], ga_p[...]).astype(BF16)
     g_recv = dot(by_recv, first[:, features:])
     grad_one.ref[...] = cotangent + g_q[:, :features] + g_recv + g_send[:mesh_rows, :]
@@ -439,7 +543,7 @@
     grad_slots, ga_e = refs[:-1], refs[-1]
     features = FEATURES
     edges = enc_g().shape[0]
-    grad_one = grad_in()[...] + dot(halo_t()[...], stacked(back))
+    grad_one = grad_in()[...] + dot(halo_t()[...], joined(back))
     first_n, second_n = layers(weights, 1)
     ga = backward_hidden(grad_one, slope_n()[...], normed_n()[...], scale_n()[:, 0:1], second_n)
     g_n = dot(ga, first_n)
@@ -454,11 +558,11 @@
     by_recv = dot(enc_t()[...], ga_e[...]).astype(BF16)
     mesh_grad.send(grad_one + g_n[:, :features] + dot(by_recv, first[:, features:]))
     by_slot = dot(slot_t()[...], ga_e[...]).astype(BF16)
-    split(dot(by_slot, first[:, :features]), grad_slots)
+    put(dot(by_slot, first[:, :features]), grad_slots)
 
 
 def grid_kernel(back, table_in, out):
-    out.send(dot(table_in()[...], stacked(back)))
+    out.send(dot(table_in()[...], joined(back)))
 
 
 def along(block, shift):
@@ -468,32 +572,41 @@
     return lax.ppermute(block, "mp", [(m, (m + shift) % size) for m in range(size)])
 
 
-def beside(block, flip):
-    if flip == 0:
-        return block
-    return lax.ppermute(block, "graph", [(g, g ^ flip) for g in range(lax.axis_size("graph"))])
-
-
-def turn(blocks, count, step):
-    out = shape(len(blocks) * step, blocks[0].shape[1], BF16)
-    return call(turn_kernel, [out] * count, list(blocks))
-
-
-def exchange(blocks, step):
-    return second_level(first_level(blocks, step))
-
-
-def first_level(blocks, step):
-    return turn([along(b, s) for s, b in enumerate(blocks)], lax.axis_size("graph"), step)
-
-
-def second_level(blocks):
-    return [beside(b, t) for t, b in enumerate(blocks)]
+def chip_to_chip(blocks):
+    names = ("graph", "mp")
+    return [blocks[0]] + [
+        lax.ppermute(b, names, [(r, r ^ (c // 4 * 8 + c % 4)) for r in range(16)])
+        for c, b in enumerate(blocks)
+        if c
+    ]
+
+
+def core_to_core(block):
+    return lax.ppermute(block, "graph", [(g, g ^ 1) for g in range(4)])
+
+
+def exchange_all(packed):
+    peers = lax.axis_size("graph") * lax.axis_size("mp")
+    parts = packed.reshape(peers, -1, LANES)
+    parts = lax.all_to_all(parts, ("graph", "mp"), split_axis=0, concat_axis=0, tiled=True)
+    return parts.reshape(packed.shape)
+
+
+def exchange(halves, step):
+    if not small():
+        return [exchange_all(halves[0])]
+    keep, send = halves
+    block = shape(16, keep.shape[1], BF16)
+    blocks = call(functools.partial(fan_kernel, step), [block] * 8, [keep, core_to_core(send)])
+    return chip_to_chip(blocks)
 
 
 def exchange_back(blocks, step):
-    blocks = turn([beside(b, t) for t, b in enumerate(blocks)], lax.axis_size("mp"), step)
-    return [along(b, -s) for s, b in enumerate(blocks)]
+    if not small():
+        return [exchange_all(blocks[0])]
+    half = shape(8 * step, blocks[0].shape[1], BF16)
+    keep, send = call(functools.partial(fold_kernel, step), [half] * 2, chip_to_chip(blocks))
+    return [keep, core_to_core(send)]
 
 
 def local(
@@ -512,20 +625,21 @@
     mesh_rows = mesh_lat.shape[0]
     edges = g2m_slot.shape[0]
     mesh_edges = mesh_sender.shape[0]
-    mp, graph = lax.axis_size("mp"), lax.axis_size("graph")
-    step, halo_step = stride(grid_send.shape[1]), stride(halo_send.shape[1])
-    slots, halos = mp * graph * step, mp * graph * halo_step
-    tables = call(
+    peers = lax.axis_size("mp") * lax.axis_size("graph")
+    step, halo_step = grid_send.shape[1], halo_send.shape[1]
+    slots, halos, halos_in = grid_send.size, halo_send.size, in_rows(peers, halo_step)
+    spread = peers * stride(step) if small() else slots
+    make_tables = lambda: call(
         tables_kernel,
         [
             shape(slots, edges, BF16),
-            shape(edges, slots, BF16),
+            shape(edges, spread, BF16),
             shape(mesh_rows, edges, BF16),
             shape(edges, mesh_rows, BF16),
             shape(mesh_rows, halos, BF16),
             shape(halos, mesh_rows, BF16),
-            shape(mesh_rows + halos, mesh_edges, BF16),
-            shape(mesh_edges, mesh_rows + halos, BF16),
+            shape(mesh_rows + halos_in, mesh_edges, BF16),
+            shape(mesh_edges, mesh_rows + halos_in, BF16),
             shape(mesh_rows, mesh_edges, BF16),
             shape(mesh_edges, mesh_rows, BF16),
             shape(edges, features, BF16),
@@ -537,7 +651,7 @@
         Far(mesh_sender.reshape(1, mesh_edges)),
         Far(mesh_receiver.reshape(1, mesh_edges)),
     )
-    enc, finish, arrived, grid_t, tables = start(grid_lat, grid_send, shards, tables)
+    enc, finish, arrived, grid_t, tables = start(grid_lat, grid_send, shards, make_tables)
     slot_t, slot_g, enc_t, enc_g, halo_t, halo_g, sender_t, sender_g, proc_t, proc_g, recv_rows = tables
     saved = [
         shape(edges, features, BF16),
@@ -547,9 +661,12 @@
         shape(mesh_rows, features, BF16),
         shape(mesh_rows, LANES, F32),
     ]
+    packed = lambda rows: [shape(rows * features // LANES, LANES, BF16)]
+    halo_parts = [shape(halos // 2, features, BF16)] * 2 if small() else packed(halos)
+    back_parts = [shape(16, features, BF16)] * 8 if small() else packed(halos)
     mesh_one, slope_e, normed_e, scale_e, slope_n, normed_n, scale_n, *halo_out = call(
         encode_kernel,
-        [shape(mesh_rows, features, BF16)] + saved + [shape(graph * halo_step, features, BF16)] * mp,
+        [shape(mesh_rows, features, BF16)] + saved + halo_parts,
         recv_rows,
         arrived,
         slot_g,
@@ -559,13 +676,11 @@
         halo_g,
         flops=3 * 10**9,
     )
-    moved = first_level(halo_out, halo_step)
-    proc = finish(moved)
-    halo_in = second_level(moved)
+    halo_in = exchange(halo_out, halo_step)
+    proc = finish(mesh_one, halo_in[1:6])
     mesh_two, grad_one, *grad_halo = call(
         process_kernel,
-        [shape(mesh_rows, features, BF16), shape(mesh_rows, features, F32)]
-        + [shape(mp * halo_step, features, BF16)] * graph,
+        [shape(mesh_rows, features, BF16), shape(mesh_rows, features, F32)] + back_parts,
         Far(cotangent),
         mesh_one,
         halo_in,
@@ -586,7 +701,7 @@
     halo_back = exchange_back(grad_halo, halo_step)
     mesh_grad, *grad_slots = call(
         decode_kernel,
-        [shape(mesh_rows, features, F32)] + [shape(mp * step, features, BF16)] * graph,
+        [shape(mesh_rows, features, F32)] + packed(slots),
         halo_back,
         halo_t,
         grad_one,
@@ -604,9 +719,9 @@
         flops=3 * 10**9,
         scratch=[pltpu.VMEM((edges, features), BF16)],
     )
-    returned = exchange_back(grad_slots, step)
+    returned = exchange_all(grad_slots[0])
     (grid_grad,) = call(
-        grid_kernel, [shape(grid_rows, features, F32)], returned, grid_t, last=(0,)
+        grid_kernel, [shape(grid_rows, features, F32)], [returned], Far(grid_t), last=(0,)
     )
     return (mesh_two, grid_grad, mesh_grad)
 

time: 94.8 us -> 107 us (1.13)
  blocking collectives: 0 us -> 10.4 us
  starting transfers between devices: 33.8 us -> 41 us
  waiting for transfers between devices: 39.3 us -> 32.4 us
  Pallas kernels: 20.3 us -> 21.8 us
    ppermute x10 -> x17, starting transfers between devices: 7.43 us -> 23.9 us  [the longest x14 22.1 us: chip_to_chip(): lax.ppermute(b, names, [(r, r ^ c // 4 * 8 + c % 4) for r in range(16)])]
    ppermute x12 -> x3, waiting for transfers between devices: 17.7 us -> 2.43 us  [along(): lax.ppermute(block, 'mp', [(m, (m + shift) % size) for m in range(size)])]
    ppermute x10 -> x17, waiting for transfers between devices: 7.77 us -> 23 us  [the longest x14 11.4 us: chip_to_chip(): lax.ppermute(b, names, [(r, r ^ c // 4 * 8 + c % 4) for r in range(16)])]
    all_to_all x0 -> x1, blocking collectives: none -> 10.4 us  [exchange_all(): lax.all_to_all(parts, ('graph', 'mp'), split_axis=0, concat_axis=0, tiled...]
    ppermute x12 -> x3, starting transfers between devices: 15.3 us -> 7.01 us  [along(): lax.ppermute(block, 'mp', [(m, (m + shift) % size) for m in range(size)])]
    ppermute x12 -> x11, waiting for transfers between devices: 13.8 us -> 6.91 us  [across(): lax.ppermute(x, ('groups', 'graph'), [(p, p ^ flip) for p in range(planes)])]
    pallas_call x11 -> x10, Pallas kernels: 20.3 us -> 21.8 us  [call(): pl.pallas_call(body, out_shape=out_shape, in_specs=[hbm if away else vmem...]
    ppermute x12 -> x11, starting transfers between devices: 8.19 us -> 7.17 us  [across(): lax.ppermute(x, ('groups', 'graph'), [(p, p ^ flip) for p in range(planes)])]
  transfers between devices with their start and end apart: 35 -> 32, of which waited for: 18 -> 14; matrix products, arithmetic and copies ran while one was open for 0% -> 0% of each run, Pallas kernels for 8% -> 7%
where the time goes in v9:
time: 107 us
  starting transfers between devices  41 us (38%)
  waiting for transfers between devices  32.4 us (30%)
  Pallas kernels  21.8 us (20%)
  blocking collectives  10.4 us (10%)
    ppermute x14, starting transfers between devices, chip_to_chip(): lax.ppermute(b, names, [(r, r ^ c // 4 * 8 + c % 4) for r in range(16)])  22.1 us
    pallas_call x10, Pallas kernels, call(): pl.pallas_call(body, out_shape=out_shape, in_specs=[hbm if away else vmem...  21.8 us
    ppermute x14, waiting for transfers between devices, chip_to_chip(): lax.ppermute(b, names, [(r, r ^ c // 4 * 8 + c % 4) for r in range(16)])  11.4 us
    all_to_all x1, blocking collectives, exchange_all(): lax.all_to_all(parts, ('graph', 'mp'), split_axis=0, concat_axis=0, tiled...  10.4 us
    ppermute x1, waiting for transfers between devices, start(): pairs = lax.ppermute(pair, 'mp', [(m, m ^ 2) for m in range(mp)])  9.26 us
    ppermute x11, starting transfers between devices, across(): lax.ppermute(x, ('groups', 'graph'), [(p, p ^ flip) for p in range(planes)])  7.17 us
    ppermute x3, starting transfers between devices, along(): lax.ppermute(block, 'mp', [(m, (m + shift) % size) for m in range(size)])  7.01 us
    ppermute x11, waiting for transfers between devices, across(): lax.ppermute(x, ('groups', 'graph'), [(p, p ^ flip) for p in range(planes)])  6.91 us
  transfers between devices with their start and end apart: 32, of which 14 were waited for; matrix products, arithmetic and copies ran while one was open for 0% of the time, Pallas kernels for 7%

profile of v9, /device:TPU:0, one launch (start us, length us, event | category | flops | bytes accessed | tf_op | source)
XLA Modules:
  0.0 106.5 jit_solution(16186845292461897036)
XLA Ops:
  0.6 2.9 %prepare_kernel.1 = (bf16[16,3072]{1,0:T(8,128)(2,1)S(1)}, bf16[512,64]{1,0:T(8,128)(2,1)}, bf16[16,512]{1,0:T(8,128)(2,1)S(1)}, bf16[16,3584]{1,0:T(8,128)(2,1)...) custom-call(bf16[512,512]{1,0:T(8,128)(2,1)} %refs_0_.5, s32[4,16]{1,0:T(4,128)} %bitcast.10, ...), custom_call_target="tpu_custom_call" | custom-call | bytes 2097408 | tf_op jit(solution)/shard_map/prepare_kernel/pallas_call | solution.py:98
  3.5 3.1 %collective-permute-start = (bf16[16,3584]{1,0:T(8,128)(2,1)S(1)}, bf16[16,3584]{1,0:T(8,128)(2,1)S(1)}, u32[]{:S(2)}, u32[]{:S(2)}) collective-permute-start(bf16[16,3584]{1,0:T(8,128)(2,1)S(1)} %get-tuple-element.71), channel_id=1, source_target_pairs={{0,1},{1,2},{2,3},{3,0},{4,5},{5,6},{6,7},{7,4},{8,9},{9,10},{10,1... | collective-permute-start | bytes 344072 | tf_op jit(solution)/shard_map/ppermute | solution.py:572
  6.6 2.6 %collective-permute-start.1 = (bf16[16,3584]{1,0:T(8,128)(2,1)S(1)}, bf16[16,3584]{1,0:T(8,128)(2,1)S(1)}, u32[]{:S(2)}, u32[]{:S(2)}) collective-permute-start(bf16[16,3584]{1,0:T(8,128)(2,1)S(1)} %get-tuple-element.72), channel_id=1, source_target_pairs={{0,2},{1,3},{2,0},{3,1},{4,6},{5,7},{6,4},{7,5},{8,10},{9,11},{10,... | collective-permute-start | bytes 344072 | tf_op jit(solution)/shard_map/ppermute | solution.py:572
  10.5 2.0 %own_kernel.1 = (bf16[128,3072]{1,0:T(8,128)(2,1)S(1)}, bf16[128,3072]{1,0:T(8,128)(2,1)S(1)}) custom-call(bf16[1024,128]{1,0:T(8,128)(2,1)} %refs_0_.6, bf16[128,512]{1,0:T(8,128)(2,1)} %refs_1_.1, bf16[1024,128]{1,0:T(8,128)(2,1)} %refs_2_.3, bf16[128,512]{1,0:T(8,128)(2,1)} %refs_3_.3, bf16[1024,128]{1,0:T(8,128)(2,1)} %refs_4_.3, ...), custom_call_target="tpu_custom_call" | custom-call | bytes 1572864 | tf_op jit(solution)/shard_map/own_kernel/pallas_call | solution.py:98
  12.6 1.8 %tables_kernel.1 = (bf16[64,512]{1,0:T(8,128)(2,1)S(1)}, bf16[512,64]{1,0:T(8,128)(2,1)S(1)}, bf16[256,512]{1,0:T(8,128)(2,1)S(1)}, bf16[512,256]{1,0:T(8,128)(2...) custom-call(bf16[256,512]{1,0:T(8,128)(2,1)} %refs_7_.5, ...), custom_call_target="tpu_custom_call" | custom-call | bytes 270464 | tf_op jit(solution)/shard_map/tables_kernel/pallas_call | solution.py:98
  14.4 2.4 %collective-permute-done.1.refs_2_ = bf16[16,3584]{1,0:T(8,128)(2,1)S(1)} collective-permute-done((bf16[16,3584]{1,0:T(8,128)(2,1)S(1)}, bf16[16,3584]{1,0:T(8,128)(2,1)S(1)}, u32[]{:S(2)}, u32[]{:S(2)}) %collective-permute-start.1) | collective-permute-done | bytes 114720 | tf_op jit(solution)/shard_map/ppermute | solution.py:572
  17.0 3.0 %collective-permute-start.6 = (bf16[16,3072]{1,0:T(8,128)(2,1)S(1)}, bf16[16,3072]{1,0:T(8,128)(2,1)S(1)}, u32[]{:S(2)}, u32[]{:S(2)}) collective-permute-start(bf16[16,3072]{1,0:T(8,128)(2,1)S(1)} %get-tuple-element.78), channel_id=1, source_target_pairs={{0,1},{1,0},{2,3},{3,2},{4,5},{5,4},{6,7},{7,6},{8,9},{9,8},{10,11... | collective-permute-start | bytes 294920 | tf_op jit(solution)/shard_map/ppermute | solution.py:232
  20.0 2.5 %collective-permute-start.5 = (bf16[48,3072]{1,0:T(8,128)(2,1)S(1)}, bf16[48,3072]{1,0:T(8,128)(2,1)S(1)}, u32[]{:S(2)}, u32[]{:S(2)}) collective-permute-start(bf16[48,3072]{1,0:T(8,128)(2,1)S(1)} %get-tuple-element.76.refs_9_.refs_12_), channel_id=1, source_target_pairs={{0,24},{4,28},{8,16},{12,20},{16,8},{20,12},{24,0},{28,4},{1,25},{... | collective-permute-start | bytes 884744 | tf_op jit(solution)/shard_map/ppermute | solution.py:187
  25.2 9.3 %collective-permute-done.7 = bf16[32,3072]{1,0:T(8,128)(2,1)S(1)} collective-permute-done((bf16[32,3072]{1,0:T(8,128)(2,1)S(1)}, bf16[32,3072]{1,0:T(8,128)(2,1)S(1)}, u32[]{:S(2)}, u32[]{:S(2)}) %collective-permute-start.7) | collective-permute-done | bytes 196640 | tf_op jit(solution)/shard_map/ppermute | solution.py:234
  40.1 3.8 %encode_kernel.1 = (bf16[256,512]{1,0:T(8,128)(2,1)S(1)}, bf16[512,512]{1,0:T(8,128)(2,1)S(1)}, bf16[512,512]{1,0:T(8,128)(2,1)S(1)}, f32[512,128]{1,0:T(8,128)S...) custom-call(bf16[512,512]{1,0:T(8,128)(2,1)S(1)} %get-tuple-element., ...), custom_call_target="tpu_custom_call" | custom-call | flops 3000000000 | bytes 5472256 | tf_op jit(solution)/shard_map/encode_kernel/pallas_call | solution.py:98
  43.9 3.3 %collective-permute-done.20.refs_15_ = bf16[48,3072]{1,0:T(8,128)(2,1)S(1)} collective-permute-done((bf16[48,3072]{1,0:T(8,128)(2,1)S(1)}, bf16[48,3072]{1,0:T(8,128)(2,1)S(1)}, u32[]{:S(2)}, u32[]{:S(2)}) %collective-permute-start.20) | collective-permute-done | bytes 294944 | tf_op jit(solution)/shard_map/ppermute | solution.py:187
  50.1 3.4 %collective-permute-start.14 = (bf16[16,512]{1,0:T(8,128)(2,1)S(1)}, bf16[16,512]{1,0:T(8,128)(2,1)S(1)}, u32[]{:S(2)}, u32[]{:S(2)}) collective-permute-start(bf16[16,512]{1,0:T(8,128)(2,1)S(1)} %get-tuple-element.93), channel_id=1, source_target_pairs={{0,3},{1,2},{2,1},{3,0},{4,7},{5,6},{6,5},{7,4},{8,11},{9,10},{10,... | collective-permute-start | bytes 49160 | tf_op jit(solution)/shard_map/ppermute | solution.py:578
  57.2 3.2 %collective-permute-done.16.refs_7_ = bf16[16,512]{1,0:T(8,128)(2,1)S(1)} collective-permute-done((bf16[16,512]{1,0:T(8,128)(2,1)S(1)}, bf16[16,512]{1,0:T(8,128)(2,1)S(1)}, u32[]{:S(2)}, u32[]{:S(2)}) %collective-permute-start.16) | collective-permute-done | bytes 16416 | tf_op jit(solution)/shard_map/ppermute | solution.py:578
  62.4 2.2 %collective-permute-start.18 = (bf16[16,512]{1,0:T(8,128)(2,1)S(1)}, bf16[16,512]{1,0:T(8,128)(2,1)S(1)}, u32[]{:S(2)}, u32[]{:S(2)}) collective-permute-start(bf16[16,512]{1,0:T(8,128)(2,1)S(1)} %get-tuple-element.97), channel_id=1, source_target_pairs={{0,11},{1,10},{2,9},{3,8},{4,15},{5,14},{6,13},{7,12},{8,3},{9,2},... | collective-permute-start | bytes 49160 | tf_op jit(solution)/shard_map/ppermute | solution.py:578
  64.5 1.9 %collective-permute-done.17.refs_8_ = bf16[16,512]{1,0:T(8,128)(2,1)S(1)} collective-permute-done((bf16[16,512]{1,0:T(8,128)(2,1)S(1)}, bf16[16,512]{1,0:T(8,128)(2,1)S(1)}, u32[]{:S(2)}, u32[]{:S(2)}) %collective-permute-start.17) | collective-permute-done | bytes 16416 | tf_op jit(solution)/shard_map/ppermute | solution.py:578
  66.4 2.4 %collective-permute-done.18.refs_9_ = bf16[16,512]{1,0:T(8,128)(2,1)S(1)} collective-permute-done((bf16[16,512]{1,0:T(8,128)(2,1)S(1)}, bf16[16,512]{1,0:T(8,128)(2,1)S(1)}, u32[]{:S(2)}, u32[]{:S(2)}) %collective-permute-start.18) | collective-permute-done | bytes 16416 | tf_op jit(solution)/shard_map/ppermute | solution.py:578
  68.8 5.4 %process_kernel.1 = (bf16[256,512]{1,0:T(8,128)(2,1)}, f32[256,512]{1,0:T(8,128)S(1)}, bf16[16,512]{1,0:T(8,128)(2,1)S(1)}, bf16[16,512]{1,0:T(8,128)(2,1)S(1)},...) custom-call(bf16[256,512]{1,0:T(8,128)(2,1)} %refs_0_.7, ...), custom_call_target="tpu_custom_call" | custom-call | flops 5000000000 | bytes 5111808 | tf_op jit(solution)/shard_map/process_kernel/pallas_call | solution.py:98
  74.3 2.7 %collective-permute-start.25 = (bf16[16,512]{1,0:T(8,128)(2,1)S(1)}, bf16[16,512]{1,0:T(8,128)(2,1)S(1)}, u32[]{:S(2)}, u32[]{:S(2)}) collective-permute-start(bf16[16,512]{1,0:T(8,128)(2,1)S(1)} %get-tuple-element.109), channel_id=1, source_target_pairs={{0,2},{1,3},{2,0},{3,1},{4,6},{5,7},{6,4},{7,5},{8,10},{9,11},{10,... | collective-permute-start | bytes 49160 | tf_op jit(solution)/shard_map/ppermute | solution.py:578
  79.3 3.5 %collective-permute-start.29 = (bf16[16,512]{1,0:T(8,128)(2,1)S(1)}, bf16[16,512]{1,0:T(8,128)(2,1)S(1)}, u32[]{:S(2)}, u32[]{:S(2)}) collective-permute-start(bf16[16,512]{1,0:T(8,128)(2,1)S(1)} %get-tuple-element.113), channel_id=1, source_target_pairs={{0,10},{1,11},{2,8},{3,9},{4,14},{5,15},{6,12},{7,13},{8,2},{9,3},... | collective-permute-start | bytes 49160 | tf_op jit(solution)/shard_map/ppermute | solution.py:578
  82.8 2.6 %collective-permute-start.30 = (bf16[16,512]{1,0:T(8,128)(2,1)S(1)}, bf16[16,512]{1,0:T(8,128)(2,1)S(1)}, u32[]{:S(2)}, u32[]{:S(2)}) collective-permute-start(bf16[16,512]{1,0:T(8,128)(2,1)S(1)} %get-tuple-element.114), channel_id=1, source_target_pairs={{0,11},{1,10},{2,9},{3,8},{4,15},{5,14},{6,13},{7,12},{8,3},{9,2},... | collective-permute-start | bytes 49160 | tf_op jit(solution)/shard_map/ppermute | solution.py:578
  85.4 3.8 %collective-permute-done.30.refs_7_ = bf16[16,512]{1,0:T(8,128)(2,1)S(1)} collective-permute-done((bf16[16,512]{1,0:T(8,128)(2,1)S(1)}, bf16[16,512]{1,0:T(8,128)(2,1)S(1)}, u32[]{:S(2)}, u32[]{:S(2)}) %collective-permute-start.30) | collective-permute-done | bytes 16416 | tf_op jit(solution)/shard_map/ppermute | solution.py:578
  90.7 3.2 %decode_kernel.1 = (f32[256,512]{1,0:T(8,128)}, bf16[256,128]{1,0:T(8,128)(2,1)S(1)}) custom-call(bf16[16,512]{1,0:T(8,128)(2,1)S(1)} %get-tuple-element.115.refs_0_, bf16[16,512]{1,0:T(8,128)(2,1)S(1)} %collective-permute-done.31.refs_1_, bf16[256,32]{1,0:T(8,128)(2,1)S(1)} %get-tuple-element.117.refs_2_, f32[256,512]{1,0:T(8,128)S(1)} %get-tuple-element.118.refs_3_, ...), custom_call_target="tpu_custom_call" | custom-call | flops 3000000000 | bytes 6422528 | tf_op jit(solution)/shard_map/decode_kernel/pallas_call | solution.py:98
  93.8 10.4 %all_to_all.5 = bf16[16,16,128]{2,1,0:T(8,128)(2,1)S(1)} all-to-all(bf16[16,16,128]{2,1,0:T(8,128)(2,1)S(1)} %bitcast.9), channel_id=1, replica_groups=mesh['groups'=2,'graph'=4,'mp'=4] {'graph','mp'}, dimensions={0} | all-to-all | bytes 131072 | tf_op jit(solution)/shard_map/all_to_all | solution.py:591
  104.2 2.3 %grid_kernel.1 = f32[512,512]{1,0:T(8,128)} custom-call(bf16[256,128]{1,0:T(8,128)(2,1)S(1)} %bitcast.8, bf16[512,64]{1,0:T(8,128)(2,1)} %get-tuple-element.127.refs_1_), custom_call_target="tpu_custom_call" | custom-call | bytes 131072 | tf_op jit(solution)/shard_map/grid_kernel/pallas_call | solution.py:98
  (55 shorter events, 22.3 us)
Async XLA Ops:
  3.5 10.8 %collective-permute-start = (bf16[16,3584]{1,0:T(8,128)(2,1)S(1)}, bf16[16,3584]{1,0:T(8,128)(2,1)S(1)}, u32[]{:S(2)}, u32[]{:S(2)}) collective-permute-start(bf16[16,3584]{1,0:T(8,128)(2,1)S(1)} %get-tuple-element.71), channel_id=1, source_target_pairs={{0,1},{1,2},{2,3},{3,0},{4,5},{5,6},{6,7},{7,4},{8,9},{9,10},{10,1... | collective-permute-start | bytes 344072 | tf_op jit(solution)/shard_map/ppermute | solution.py:572
  6.6 10.2 %collective-permute-start.1 = (bf16[16,3584]{1,0:T(8,128)(2,1)S(1)}, bf16[16,3584]{1,0:T(8,128)(2,1)S(1)}, u32[]{:S(2)}, u32[]{:S(2)}) collective-permute-start(bf16[16,3584]{1,0:T(8,128)(2,1)S(1)} %get-tuple-element.72), channel_id=1, source_target_pairs={{0,2},{1,3},{2,0},{3,1},{4,6},{5,7},{6,4},{7,5},{8,10},{9,11},{10,... | collective-permute-start | bytes 344072 | tf_op jit(solution)/shard_map/ppermute | solution.py:572
  9.2 7.6 %collective-permute-start.2 = (bf16[16,3584]{1,0:T(8,128)(2,1)S(1)}, bf16[16,3584]{1,0:T(8,128)(2,1)S(1)}, u32[]{:S(2)}, u32[]{:S(2)}) collective-permute-start(bf16[16,3584]{1,0:T(8,128)(2,1)S(1)} %get-tuple-element.73), channel_id=1, source_target_pairs={{0,3},{1,0},{2,1},{3,2},{4,7},{5,4},{6,5},{7,6},{8,11},{9,8},{10,9... | collective-permute-start | bytes 344072 | tf_op jit(solution)/shard_map/ppermute | solution.py:572
  17.0 6.5 %collective-permute-start.6 = (bf16[16,3072]{1,0:T(8,128)(2,1)S(1)}, bf16[16,3072]{1,0:T(8,128)(2,1)S(1)}, u32[]{:S(2)}, u32[]{:S(2)}) collective-permute-start(bf16[16,3072]{1,0:T(8,128)(2,1)S(1)} %get-tuple-element.78), channel_id=1, source_target_pairs={{0,1},{1,0},{2,3},{3,2},{4,5},{5,4},{6,7},{7,6},{8,9},{9,8},{10,11... | collective-permute-start | bytes 294920 | tf_op jit(solution)/shard_map/ppermute | solution.py:232
  20.0 14.5 %collective-permute-start.5 = (bf16[48,3072]{1,0:T(8,128)(2,1)S(1)}, bf16[48,3072]{1,0:T(8,128)(2,1)S(1)}, u32[]{:S(2)}, u32[]{:S(2)}) collective-permute-start(bf16[48,3072]{1,0:T(8,128)(2,1)S(1)} %get-tuple-element.76.refs_9_.refs_12_), channel_id=1, source_target_pairs={{0,24},{4,28},{8,16},{12,20},{16,8},{20,12},{24,0},{28,4},{1,25},{... | collective-permute-start | bytes 884744 | tf_op jit(solution)/shard_map/ppermute | solution.py:187
  22.5 13.4 %collective-permute-start.4 = (bf16[48,3072]{1,0:T(8,128)(2,1)S(1)}, bf16[48,3072]{1,0:T(8,128)(2,1)S(1)}, u32[]{:S(2)}, u32[]{:S(2)}) collective-permute-start(bf16[48,3072]{1,0:T(8,128)(2,1)S(1)} %get-tuple-element.76.refs_9_.refs_12_), channel_id=1, source_target_pairs={{0,16},{4,20},{8,24},{12,28},{16,0},{20,4},{24,8},{28,12},{1,17},{... | collective-permute-start | bytes 884744 | tf_op jit(solution)/shard_map/ppermute | solution.py:187
  23.0 14.1 %collective-permute-start.3 = (bf16[48,3584]{1,0:T(8,128)(2,1)S(1)}, bf16[48,3584]{1,0:T(8,128)(2,1)S(1)}, u32[]{:S(2)}, u32[]{:S(2)}) collective-permute-start(bf16[48,3584]{1,0:T(8,128)(2,1)S(1)} %get-tuple-element.79), channel_id=1, source_target_pairs={{0,8},{4,12},{8,0},{12,4},{16,24},{20,28},{24,16},{28,20},{1,9},{5... | collective-permute-start | bytes 1032200 | tf_op jit(solution)/shard_map/ppermute | solution.py:187
  23.5 11.0 %collective-permute-start.7 = (bf16[32,3072]{1,0:T(8,128)(2,1)S(1)}, bf16[32,3072]{1,0:T(8,128)(2,1)S(1)}, u32[]{:S(2)}, u32[]{:S(2)}) collective-permute-start(bf16[32,3072]{1,0:T(8,128)(2,1)S(1)} %pad_maximum_fusion.3), channel_id=1, source_target_pairs={{0,2},{1,3},{2,0},{3,1},{4,6},{5,7},{6,4},{7,5},{8,10},{9,11},{10,... | collective-permute-start | bytes 589832 | tf_op jit(solution)/shard_map/ppermute | solution.py:234
  37.8 9.4 %collective-permute-start.20 = (bf16[48,3072]{1,0:T(8,128)(2,1)S(1)}, bf16[48,3072]{1,0:T(8,128)(2,1)S(1)}, u32[]{:S(2)}, u32[]{:S(2)}) collective-permute-start(bf16[48,3072]{1,0:T(8,128)(2,1)S(1)} %pad_maximum_fusion.2.refs_13_), channel_id=1, source_target_pairs={{0,8},{4,12},{8,0},{12,4},{16,24},{20,28},{24,16},{28,20},{1,9},{5... | collective-permute-start | bytes 884744 | tf_op jit(solution)/shard_map/ppermute | solution.py:187
  39.3 14.2 %collective-permute-start.21 = (bf16[48,3072]{1,0:T(8,128)(2,1)S(1)}, bf16[48,3072]{1,0:T(8,128)(2,1)S(1)}, u32[]{:S(2)}, u32[]{:S(2)}) collective-permute-start(bf16[48,3072]{1,0:T(8,128)(2,1)S(1)} %pad_maximum_fusion.2.refs_13_), channel_id=1, source_target_pairs={{0,16},{4,20},{8,24},{12,28},{16,0},{20,4},{24,8},{28,12},{1,17},{... | collective-permute-start | bytes 884744 | tf_op jit(solution)/shard_map/ppermute | solution.py:187
  47.2 8.6 %collective-permute-start.22 = (bf16[48,3072]{1,0:T(8,128)(2,1)S(1)}, bf16[48,3072]{1,0:T(8,128)(2,1)S(1)}, u32[]{:S(2)}, u32[]{:S(2)}) collective-permute-start(bf16[48,3072]{1,0:T(8,128)(2,1)S(1)} %collective-permute-done.20.refs_15_), channel_id=1, source_target_pairs={{0,16},{4,20},{8,24},{12,28},{16,0},{20,4},{24,8},{28,12},{1,17},{... | collective-permute-start | bytes 884744 | tf_op jit(solution)/shard_map/ppermute | solution.py:187
  49.0 8.1 %collective-permute-start.12 = (bf16[16,512]{1,0:T(8,128)(2,1)S(1)}, bf16[16,512]{1,0:T(8,128)(2,1)S(1)}, u32[]{:S(2)}, u32[]{:S(2)}) collective-permute-start(bf16[16,512]{1,0:T(8,128)(2,1)S(1)} %get-tuple-element.91), channel_id=1, source_target_pairs={{0,1},{1,0},{2,3},{3,2},{4,5},{5,4},{6,7},{7,6},{8,9},{9,8},{10,11... | collective-permute-start | bytes 49160 | tf_op jit(solution)/shard_map/ppermute | solution.py:578
  49.5 7.7 %collective-permute-start.13 = (bf16[16,512]{1,0:T(8,128)(2,1)S(1)}, bf16[16,512]{1,0:T(8,128)(2,1)S(1)}, u32[]{:S(2)}, u32[]{:S(2)}) collective-permute-start(bf16[16,512]{1,0:T(8,128)(2,1)S(1)} %get-tuple-element.92), channel_id=1, source_target_pairs={{0,2},{1,3},{2,0},{3,1},{4,6},{5,7},{6,4},{7,5},{8,10},{9,11},{10,... | collective-permute-start | bytes 49160 | tf_op jit(solution)/shard_map/ppermute | solution.py:578
  50.1 7.0 %collective-permute-start.14 = (bf16[16,512]{1,0:T(8,128)(2,1)S(1)}, bf16[16,512]{1,0:T(8,128)(2,1)S(1)}, u32[]{:S(2)}, u32[]{:S(2)}) collective-permute-start(bf16[16,512]{1,0:T(8,128)(2,1)S(1)} %get-tuple-element.93), channel_id=1, source_target_pairs={{0,3},{1,2},{2,1},{3,0},{4,7},{5,6},{6,5},{7,4},{8,11},{9,10},{10,... | collective-permute-start | bytes 49160 | tf_op jit(solution)/shard_map/ppermute | solution.py:578
  60.4 8.4 %collective-permute-start.23 = (bf16[144,3072]{1,0:T(8,128)(2,1)S(1)}, bf16[144,3072]{1,0:T(8,128)(2,1)S(1)}, u32[]{:S(2)}, u32[]{:S(2)}) collective-permute-start(bf16[144,3072]{1,0:T(8,128)(2,1)S(1)} %pad_maximum_fusion), channel_id=1, source_target_pairs={{0,4},{4,0},{8,12},{12,8},{16,20},{20,16},{24,28},{28,24},{1,5},{5... | collective-permute-start | bytes 2654216 | tf_op jit(solution)/shard_map/ppermute | solution.py:187
  60.9 5.5 %collective-permute-start.17 = (bf16[16,512]{1,0:T(8,128)(2,1)S(1)}, bf16[16,512]{1,0:T(8,128)(2,1)S(1)}, u32[]{:S(2)}, u32[]{:S(2)}) collective-permute-start(bf16[16,512]{1,0:T(8,128)(2,1)S(1)} %get-tuple-element.96), channel_id=1, source_target_pairs={{0,10},{1,11},{2,8},{3,9},{4,14},{5,15},{6,12},{7,13},{8,2},{9,3},... | collective-permute-start | bytes 49160 | tf_op jit(solution)/shard_map/ppermute | solution.py:578
  62.4 6.4 %collective-permute-start.18 = (bf16[16,512]{1,0:T(8,128)(2,1)S(1)}, bf16[16,512]{1,0:T(8,128)(2,1)S(1)}, u32[]{:S(2)}, u32[]{:S(2)}) collective-permute-start(bf16[16,512]{1,0:T(8,128)(2,1)S(1)} %get-tuple-element.97), channel_id=1, source_target_pairs={{0,11},{1,10},{2,9},{3,8},{4,15},{5,14},{6,13},{7,12},{8,3},{9,2},... | collective-permute-start | bytes 49160 | tf_op jit(solution)/shard_map/ppermute | solution.py:578
  74.2 5.1 %collective-permute-start.24 = (bf16[16,512]{1,0:T(8,128)(2,1)S(1)}, bf16[16,512]{1,0:T(8,128)(2,1)S(1)}, u32[]{:S(2)}, u32[]{:S(2)}) collective-permute-start(bf16[16,512]{1,0:T(8,128)(2,1)S(1)} %get-tuple-element.108), channel_id=1, source_target_pairs={{0,1},{1,0},{2,3},{3,2},{4,5},{5,4},{6,7},{7,6},{8,9},{9,8},{10,11... | collective-permute-start | bytes 49160 | tf_op jit(solution)/shard_map/ppermute | solution.py:578
  74.3 8.6 %collective-permute-start.25 = (bf16[16,512]{1,0:T(8,128)(2,1)S(1)}, bf16[16,512]{1,0:T(8,128)(2,1)S(1)}, u32[]{:S(2)}, u32[]{:S(2)}) collective-permute-start(bf16[16,512]{1,0:T(8,128)(2,1)S(1)} %get-tuple-element.109), channel_id=1, source_target_pairs={{0,2},{1,3},{2,0},{3,1},{4,6},{5,7},{6,4},{7,5},{8,10},{9,11},{10,... | collective-permute-start | bytes 49160 | tf_op jit(solution)/shard_map/ppermute | solution.py:578
  77.0 8.4 %collective-permute-start.26 = (bf16[16,512]{1,0:T(8,128)(2,1)S(1)}, bf16[16,512]{1,0:T(8,128)(2,1)S(1)}, u32[]{:S(2)}, u32[]{:S(2)}) collective-permute-start(bf16[16,512]{1,0:T(8,128)(2,1)S(1)} %get-tuple-element.110), channel_id=1, source_target_pairs={{0,3},{1,2},{2,1},{3,0},{4,7},{5,6},{6,5},{7,4},{8,11},{9,10},{10,... | collective-permute-start | bytes 49160 | tf_op jit(solution)/shard_map/ppermute | solution.py:578
  78.6 6.8 %collective-permute-start.27 = (bf16[16,512]{1,0:T(8,128)(2,1)S(1)}, bf16[16,512]{1,0:T(8,128)(2,1)S(1)}, u32[]{:S(2)}, u32[]{:S(2)}) collective-permute-start(bf16[16,512]{1,0:T(8,128)(2,1)S(1)} %get-tuple-element.111), channel_id=1, source_target_pairs={{0,8},{1,9},{2,10},{3,11},{4,12},{5,13},{6,14},{7,15},{8,0},{9,1},... | collective-permute-start | bytes 49160 | tf_op jit(solution)/shard_map/ppermute | solution.py:578
  79.2 6.2 %collective-permute-start.28 = (bf16[16,512]{1,0:T(8,128)(2,1)S(1)}, bf16[16,512]{1,0:T(8,128)(2,1)S(1)}, u32[]{:S(2)}, u32[]{:S(2)}) collective-permute-start(bf16[16,512]{1,0:T(8,128)(2,1)S(1)} %get-tuple-element.112), channel_id=1, source_target_pairs={{0,9},{1,8},{2,11},{3,10},{4,13},{5,12},{6,15},{7,14},{8,1},{9,0},... | collective-permute-start | bytes 49160 | tf_op jit(solution)/shard_map/ppermute | solution.py:578
  79.3 6.1 %collective-permute-start.29 = (bf16[16,512]{1,0:T(8,128)(2,1)S(1)}, bf16[16,512]{1,0:T(8,128)(2,1)S(1)}, u32[]{:S(2)}, u32[]{:S(2)}) collective-permute-start(bf16[16,512]{1,0:T(8,128)(2,1)S(1)} %get-tuple-element.113), channel_id=1, source_target_pairs={{0,10},{1,11},{2,8},{3,9},{4,14},{5,15},{6,12},{7,13},{8,2},{9,3},... | collective-permute-start | bytes 49160 | tf_op jit(solution)/shard_map/ppermute | solution.py:578
  82.8 6.4 %collective-permute-start.30 = (bf16[16,512]{1,0:T(8,128)(2,1)S(1)}, bf16[16,512]{1,0:T(8,128)(2,1)S(1)}, u32[]{:S(2)}, u32[]{:S(2)}) collective-permute-start(bf16[16,512]{1,0:T(8,128)(2,1)S(1)} %get-tuple-element.114), channel_id=1, source_target_pairs={{0,11},{1,10},{2,9},{3,8},{4,15},{5,14},{6,13},{7,12},{8,3},{9,2},... | collective-permute-start | bytes 49160 | tf_op jit(solution)/shard_map/ppermute | solution.py:578
  (8 other events, 23.1 us)

commit v10 on v9

--- a/solution.py
+++ b/solution.py
@@ -191,20 +191,20 @@
     grid_rows, features = grid_lat.shape
     mp, graph = lax.axis_size("mp"), lax.axis_size("graph")
     step = stride(grid_send.shape[1])
-    table_shape = pltpu.HBM((grid_rows, grid_send.size), BF16)
+    table_shape = shape(grid_rows, mp * graph * spread(grid_send.shape[1]), BF16)
     sent = [table_shape] + [shape(graph * step, features, BF16)] * mp
     planes = lax.axis_size("groups") * graph
     hidden = shards[1].shape[0]
     if planes != 8 or mp != 4 or hidden != 128 or features != FEATURES:
         packed = shape(grid_send.size * features // LANES, LANES, BF16)
-        grid_t, *outgoing = call(send_kernel, [table_shape, packed], Far(grid_lat), Far(grid_send.T), last=(0,))
+        grid_t, *outgoing = call(send_kernel, [table_shape, packed], Far(grid_lat), Far(grid_send.T))
         rows = []
         for i in range(4):
             rows.append(lax.all_gather(shards[2 * i], "mp", axis=1, tiled=True).T)
             rows.append(lax.all_gather(shards[2 * i + 1], "mp", axis=0, tiled=True))
         enc, proc = jnp.concatenate(rows[:4], axis=1), jnp.concatenate(rows[4:], axis=1)
         arrived = [exchange_all(outgoing[0])]
-        return [enc], lambda one, moved: [proc], arrived, grid_t, make_tables()
+        return [enc], lambda moved: [proc], arrived, grid_t, make_tables()
     far = [Far(s) for s in shards]
     piece = hidden // planes
     width = 6 * features
@@ -214,7 +214,6 @@
         Far(grid_lat),
         Far(grid_send.T),
         far,
-        last=(1,),
     )
     enc_own, proc_own = call(own_kernel, [shape(hidden, width, BF16)] * 2, far)
     messages = [along(m, i + 1) for i, m in enumerate(messages)]
@@ -238,13 +237,11 @@
     enc = [enc_own, first, core, x, y, corner, x_core, others]
     arrived = [near, core, x, x_core]
     proc_first, *_ = lax.optimization_barrier((proc_first, x, y, corner))
-    proc_x, proc_y, proc_core = [across(proc_first, flip) for flip in (2, 4, 1)]
-
-    def finish(one, moved):
-        late, _ = lax.optimization_barrier((proc_x, one))
-        blocks = [proc_x, proc_y, across(late, 4)]
-        tied, *_ = lax.optimization_barrier((jnp.concatenate(blocks), *moved))
-        return [proc_own, proc_first, proc_core] + blocks + [across(tied, 1)]
+    plane = [across(proc_first, flip) for flip in (2, 4, 6)]
+
+    def finish(moved):
+        tied, *_ = lax.optimization_barrier((jnp.concatenate(plane), *moved))
+        return [proc_own, proc_first, across(proc_first, 1)] + plane + [across(tied, 1)]
 
     return enc, finish, arrived, grid_t, tables
 
@@ -302,27 +299,28 @@
 
 
 def apart(peer):
-    rank = lax.axis_index("graph") * 4 + lax.axis_index("mp")
-    differs = peer ^ rank
-    return differs // 4 % 2, differs // 8 * 4 + differs % 4
+    differs = peer // 4 ^ lax.axis_index("graph")
+    return differs % 2, differs // 2
 
 
 def out_at(peer, slot, step):
     if not small():
         return plain_at(peer, slot, step)
-    core, chip = apart(peer)
-    return (core * 8 + chip) * step + slot
+    core, x = apart(peer)
+    shift = (peer % 4 + 4 - lax.axis_index("mp")) % 4
+    return ((core * 2 + x) * 4 + shift) * step + slot
 
 
 def in_at(peer, slot, step):
     if not small():
         return plain_at(peer, slot, step)
-    core, chip = apart(peer)
-    return chip * 16 + core * step + slot
-
-
-def in_rows(count, step):
-    return 128 if small() else count * step
+    core, x = apart(peer)
+    shift = (lax.axis_index("mp") + 4 - peer % 4) % 4
+    return (shift * 4 + x * 2 + core) * step + slot
+
+
+def spread(capacity):
+    return stride(capacity) if small() else capacity
 
 
 def sent_row(index, step, order):
@@ -348,7 +346,7 @@
 
 def send_rows(grid, send, table_out, order, step):
     index, count = send()[...], grid().shape[0]
-    table_out.send(table(sent_row(index, index.shape[0], plain_at), count).astype(BF16))
+    table_out.ref[...] = table(sent_row(index, spread(index.shape[0]), in_at), count).astype(BF16)
     one = table(sent_row(index, step, order), count)
     return dot(one.T.astype(BF16), grid()[...])
 
@@ -394,23 +392,16 @@
     return dot(jnp.where(at == source(row), 1.0, 0.0).astype(BF16), rows).astype(BF16)
 
 
-def fan_kernel(step, halves, *outs):
+def level_kernel(step, inner, halves, *outs):
     rows = stacked(halves)
-    for chip, out in enumerate(outs):
-
-        def source(row, chip=chip):
-            from_row = (row // step * 8 + chip) * step + row % step
-            return jnp.where(row < 2 * step, from_row, -1)
-
-        out.ref[...] = pick_rows(rows, 16, source)
-
-
-def fold_kernel(step, blocks, keep_out, send_out):
-    rows = stacked(blocks)
-    for core, out in enumerate((keep_out, send_out)):
-        out.ref[...] = pick_rows(
-            rows, 8 * step, lambda row: row // step * 16 + core * step + row % step
-        )
+    count = len(outs)
+    for value, out in enumerate(outs):
+        size = inner * step
+
+        def source(row, value=value):
+            return (row // size * count + value) * size + row % size
+
+        out.ref[...] = pick_rows(rows, out.ref.shape[0], source)
 
 
 def put(rows, outs):
@@ -426,27 +417,29 @@
     return unpack_rows(rows) if rows.shape[1] == LANES else rows
 
 
-def tables_kernel(mesh, slot, recv_e, halo, sender, recv_p, *outs):
+def tables_kernel(capacity, mesh, slot, recv_e, halo, sender, recv_p, *outs):
     slot_t, slot_g, enc_t, enc_g, halo_t, halo_g, sender_t, sender_g, proc_t, proc_g, recv_rows = outs
     mesh_rows = mesh().shape[0]
     peers, halo_capacity = halo().shape[1], halo().shape[0]
-    capacity = slot_t.ref.shape[0] // peers
     slots = slot()[...]
-    slot_t.ref[...] = table(slots, slot_t.ref.shape[0]).astype(BF16)
+    peer, place = slots // capacity, slots % capacity
+    step = spread(capacity)
+    slot_t.ref[...] = table(out_at(peer, place, step), slot_t.ref.shape[0]).astype(BF16)
     if small():
-        slots = arrived_at(slots // capacity, slots % capacity, slot_g.ref.shape[1] // peers)
+        slots = arrived_at(peer, place, step)
     slot_g.ref[...] = table(slots, slot_g.ref.shape[1]).T.astype(BF16)
-    senders = sender()[...]
+    senders, step = sender()[...], spread(halo_capacity)
     remote = jnp.maximum(senders - mesh_rows, 0)
-    remote = in_at(remote // halo_capacity, remote % halo_capacity, halo_capacity)
-    senders = jnp.where(senders < mesh_rows, senders, mesh_rows + remote)
-    for row, scatter, gather in (
-        (recv_e()[...], enc_t, enc_g),
-        (sent_row(halo()[...], halo_capacity, out_at), halo_t, halo_g),
-        (senders, sender_t, sender_g),
-        (recv_p()[...], proc_t, proc_g),
-    ):
-        one = table(row, scatter.ref.shape[0])
+    peer, place = remote // halo_capacity, remote % halo_capacity
+    own = senders < mesh_rows
+    coming = jnp.where(own, senders, mesh_rows + in_at(peer, place, step))
+    going = jnp.where(own, senders, mesh_rows + out_at(peer, place, step))
+    sender_g.ref[...] = table(coming, sender_g.ref.shape[1]).T.astype(BF16)
+    sender_t.ref[...] = table(going, sender_t.ref.shape[0]).astype(BF16)
+    halo_g.ref[...] = table(sent_row(halo()[...], step, out_at), mesh_rows).T.astype(BF16)
+    halo_t.ref[...] = table(sent_row(halo()[...], step, in_at), mesh_rows).astype(BF16)
+    for row, scatter, gather in ((recv_e()[...], enc_t, enc_g), (recv_p()[...], proc_t, proc_g)):
+        one = table(row, mesh_rows)
         scatter.ref[...] = one.astype(BF16)
         gather.ref[...] = one.T.astype(BF16)
     recv_rows.ref[...] = dot(enc_g.ref[...], mesh()[...]).astype(BF16)
@@ -572,17 +565,8 @@
     return lax.ppermute(block, "mp", [(m, (m + shift) % size) for m in range(size)])
 
 
-def chip_to_chip(blocks):
-    names = ("graph", "mp")
-    return [blocks[0]] + [
-        lax.ppermute(b, names, [(r, r ^ (c // 4 * 8 + c % 4)) for r in range(16)])
-        for c, b in enumerate(blocks)
-        if c
-    ]
-
-
-def core_to_core(block):
-    return lax.ppermute(block, "graph", [(g, g ^ 1) for g in range(4)])
+def beside(block, flip):
+    return lax.ppermute(block, "graph", [(g, g ^ flip) for g in range(4)])
 
 
 def exchange_all(packed):
@@ -592,21 +576,18 @@
     return parts.reshape(packed.shape)
 
 
-def exchange(halves, step):
+def exchange(halves, step, behind=None):
     if not small():
         return [exchange_all(halves[0])]
+    width = halves[0].shape[1]
     keep, send = halves
-    block = shape(16, keep.shape[1], BF16)
-    blocks = call(functools.partial(fan_kernel, step), [block] * 8, [keep, core_to_core(send)])
-    return chip_to_chip(blocks)
-
-
-def exchange_back(blocks, step):
-    if not small():
-        return [exchange_all(blocks[0])]
-    half = shape(8 * step, blocks[0].shape[1], BF16)
-    keep, send = call(functools.partial(fold_kernel, step), [half] * 2, chip_to_chip(blocks))
-    return [keep, core_to_core(send)]
+    half, block = shape(8 * step, width, BF16), shape(4 * step, width, BF16)
+    level = functools.partial(level_kernel, step)
+    keep, send = call(functools.partial(level, 4), [half] * 2, [keep, beside(send, 1)])
+    blocks = call(functools.partial(level, 1), [block] * 4, [keep, beside(send, 2)])
+    if behind is not None:
+        behind(blocks)
+    return [along(b, s) for s, b in enumerate(blocks)]
 
 
 def local(
@@ -626,20 +607,19 @@
     edges = g2m_slot.shape[0]
     mesh_edges = mesh_sender.shape[0]
     peers = lax.axis_size("mp") * lax.axis_size("graph")
-    step, halo_step = grid_send.shape[1], halo_send.shape[1]
-    slots, halos, halos_in = grid_send.size, halo_send.size, in_rows(peers, halo_step)
-    spread = peers * stride(step) if small() else slots
+    step, halo_step = spread(grid_send.shape[1]), spread(halo_send.shape[1])
+    slots, halos = peers * step, peers * halo_step
     make_tables = lambda: call(
-        tables_kernel,
+        functools.partial(tables_kernel, grid_send.shape[1]),
         [
             shape(slots, edges, BF16),
-            shape(edges, spread, BF16),
+            shape(edges, slots, BF16),
             shape(mesh_rows, edges, BF16),
             shape(edges, mesh_rows, BF16),
             shape(mesh_rows, halos, BF16),
             shape(halos, mesh_rows, BF16),
-            shape(mesh_rows + halos_in, mesh_edges, BF16),
-            shape(mesh_edges, mesh_rows + halos_in, BF16),
+            shape(mesh_rows + halos, mesh_edges, BF16),
+            shape(mesh_edges, mesh_rows + halos, BF16),
             shape(mesh_rows, mesh_edges, BF16),
             shape(mesh_edges, mesh_rows, BF16),
             shape(edges, features, BF16),
@@ -661,12 +641,14 @@
         shape(mesh_rows, features, BF16),
         shape(mesh_rows, LANES, F32),
     ]
-    packed = lambda rows: [shape(rows * features // LANES, LANES, BF16)]
-    halo_parts = [shape(halos // 2, features, BF16)] * 2 if small() else packed(halos)
-    back_parts = [shape(16, features, BF16)] * 8 if small() else packed(halos)
+    def leaving(rows):
+        if small():
+            return [shape(rows // 2, features, BF16)] * 2
+        return [shape(rows * features // LANES, LANES, BF16)]
+
     mesh_one, slope_e, normed_e, scale_e, slope_n, normed_n, scale_n, *halo_out = call(
         encode_kernel,
-        [shape(mesh_rows, features, BF16)] + saved + halo_parts,
+        [shape(mesh_rows, features, BF16)] + saved + leaving(halos),
         recv_rows,
         arrived,
         slot_g,
@@ -676,11 +658,12 @@
         halo_g,
         flops=3 * 10**9,
     )
-    halo_in = exchange(halo_out, halo_step)
-    proc = finish(mesh_one, halo_in[1:6])
+    proc = []
+    halo_in = exchange(halo_out, halo_step, lambda blocks: proc.extend(finish(blocks)))
+    proc = proc or finish(halo_in)
     mesh_two, grad_one, *grad_halo = call(
         process_kernel,
-        [shape(mesh_rows, features, BF16), shape(mesh_rows, features, F32)] + back_parts,
+        [shape(mesh_rows, features, BF16), shape(mesh_rows, features, F32)] + leaving(halos),
         Far(cotangent),
         mesh_one,
         halo_in,
@@ -698,10 +681,10 @@
             pltpu.VMEM((mesh_edges, features), BF16),
         ],
     )
-    halo_back = exchange_back(grad_halo, halo_step)
+    halo_back = exchange(grad_halo, halo_step)
     mesh_grad, *grad_slots = call(
         decode_kernel,
-        [shape(mesh_rows, features, F32)] + packed(slots),
+        [shape(mesh_rows, features, F32)] + leaving(slots),
         halo_back,
         halo_t,
         grad_one,
@@ -719,9 +702,9 @@
         flops=3 * 10**9,
         scratch=[pltpu.VMEM((edges, features), BF16)],
     )
-    returned = exchange_all(grad_slots[0])
+    returned = exchange(grad_slots, step)
     (grid_grad,) = call(
-        grid_kernel, [shape(grid_rows, features, F32)], [returned], Far(grid_t), last=(0,)
+        grid_kernel, [shape(grid_rows, features, F32)], returned, grid_t, last=(0,)
     )
     return (mesh_two, grid_grad, mesh_grad)
 

time: 107 us -> 97.2 us (0.908)
  blocking collectives: 10.4 us -> 0 us
  waiting for transfers between devices: 32.4 us -> 37.5 us
  starting transfers between devices: 41 us -> 37.2 us
    ppermute x16 -> x6, starting transfers between devices: 22.2 us -> 4.03 us  [beside(): return lax.ppermute(block, 'graph', [(g, g ^ flip) for g in range(4)])]
    ppermute x3 -> x12, starting transfers between devices: 7.01 us -> 19.4 us  [along(): lax.ppermute(block, 'mp', [(m, (m + shift) % size) for m in range(size)])]
    all_to_all x1 -> x0, blocking collectives: 10.4 us -> none  [exchange_all(): lax.all_to_all(parts, ('graph', 'mp'), split_axis=0, concat_axis=0, tiled...]
    ppermute x3 -> x12, waiting for transfers between devices: 2.43 us -> 10.2 us  [along(): lax.ppermute(block, 'mp', [(m, (m + shift) % size) for m in range(size)])]
    ppermute x16 -> x6, waiting for transfers between devices: 13.8 us -> 8.51 us  [beside(): return lax.ppermute(block, 'graph', [(g, g ^ flip) for g in range(4)])]
    ppermute x11, waiting for transfers between devices: 6.91 us -> 9.5 us  [across(): lax.ppermute(x, ('groups', 'graph'), [(p, p ^ flip) for p in range(planes)])]
    ppermute x11, starting transfers between devices: 7.17 us -> 9.07 us  [across(): lax.ppermute(x, ('groups', 'graph'), [(p, p ^ flip) for p in range(planes)])]
    pallas_call x10 -> x14, Pallas kernels: 21.8 us -> 21.4 us  [call(): pl.pallas_call(body, out_shape=out_shape, in_specs=[hbm if away else vmem...]
  transfers between devices with their start and end apart: 32 -> 31, of which waited for: 14 -> 18; matrix products, arithmetic and copies ran while one was open for 0% -> 0% of each run, Pallas kernels for 7% -> 8%
where the time goes in v10:
time: 97.2 us; the launch traced here: 97 us
  waiting for transfers between devices  37.5 us (39%)
  starting transfers between devices  37.2 us (38%)
  Pallas kernels  21.4 us (22%)
    pallas_call x14, Pallas kernels, call(): pl.pallas_call(body, out_shape=out_shape, in_specs=[hbm if away else vmem...  21.4 us
    ppermute x12, starting transfers between devices, along(): lax.ppermute(block, 'mp', [(m, (m + shift) % size) for m in range(size)])  19.4 us
    ppermute x12, waiting for transfers between devices, along(): lax.ppermute(block, 'mp', [(m, (m + shift) % size) for m in range(size)])  10.2 us
    ppermute x11, waiting for transfers between devices, across(): lax.ppermute(x, ('groups', 'graph'), [(p, p ^ flip) for p in range(planes)])  9.5 us
    ppermute x1, waiting for transfers between devices, start(): pairs = lax.ppermute(pair, 'mp', [(m, m ^ 2) for m in range(mp)])  9.26 us
    ppermute x11, starting transfers between devices, across(): lax.ppermute(x, ('groups', 'graph'), [(p, p ^ flip) for p in range(planes)])  9.07 us
    ppermute x6, waiting for transfers between devices, beside(): return lax.ppermute(block, 'graph', [(g, g ^ flip) for g in range(4)])  8.51 us
    ppermute x6, starting transfers between devices, beside(): return lax.ppermute(block, 'graph', [(g, g ^ flip) for g in range(4)])  4.03 us
  transfers between devices with their start and end apart: 31, of which 18 were waited for; matrix products, arithmetic and copies ran while one was open for 0% of the time, Pallas kernels for 8%

profile of v10, /device:TPU:0, one launch (start us, length us, event | category | flops | bytes accessed | tf_op | source)
XLA Modules:
  0.0 97.0 jit_solution(11029792410301658693)
XLA Ops:
  0.6 2.4 %prepare_kernel.1 = (bf16[16,3072]{1,0:T(8,128)(2,1)S(1)}, bf16[512,64]{1,0:T(8,128)(2,1)S(1)}, bf16[16,512]{1,0:T(8,128)(2,1)S(1)}, bf16[16,3584]{1,0:T(8,128)(...) custom-call(bf16[512,512]{1,0:T(8,128)(2,1)} %refs_0_.5, s32[4,16]{1,0:T(4,128)} %bitcast.6, ...), custom_call_target="tpu_custom_call" | custom-call | bytes 2097408 | tf_op jit(solution)/shard_map/prepare_kernel/pallas_call | solution.py:98
  3.1 3.1 %collective-permute-start = (bf16[16,3584]{1,0:T(8,128)(2,1)S(1)}, bf16[16,3584]{1,0:T(8,128)(2,1)S(1)}, u32[]{:S(2)}, u32[]{:S(2)}) collective-permute-start(bf16[16,3584]{1,0:T(8,128)(2,1)S(1)} %get-tuple-element.73), channel_id=1, source_target_pairs={{0,1},{1,2},{2,3},{3,0},{4,5},{5,6},{6,7},{7,4},{8,9},{9,10},{10,1... | collective-permute-start | bytes 344072 | tf_op jit(solution)/shard_map/ppermute | solution.py:565
  6.2 2.6 %collective-permute-start.1 = (bf16[16,3584]{1,0:T(8,128)(2,1)S(1)}, bf16[16,3584]{1,0:T(8,128)(2,1)S(1)}, u32[]{:S(2)}, u32[]{:S(2)}) collective-permute-start(bf16[16,3584]{1,0:T(8,128)(2,1)S(1)} %get-tuple-element.74), channel_id=1, source_target_pairs={{0,2},{1,3},{2,0},{3,1},{4,6},{5,7},{6,4},{7,5},{8,10},{9,11},{10,... | collective-permute-start | bytes 344072 | tf_op jit(solution)/shard_map/ppermute | solution.py:565
  10.1 2.0 %own_kernel.1 = (bf16[128,3072]{1,0:T(8,128)(2,1)S(1)}, bf16[128,3072]{1,0:T(8,128)(2,1)S(1)}) custom-call(bf16[1024,128]{1,0:T(8,128)(2,1)} %refs_0_.6, bf16[128,512]{1,0:T(8,128)(2,1)} %refs_1_.1, bf16[1024,128]{1,0:T(8,128)(2,1)} %refs_2_.3, bf16[128,512]{1,0:T(8,128)(2,1)} %refs_3_.3, bf16[1024,128]{1,0:T(8,128)(2,1)} %refs_4_.3, ...), custom_call_target="tpu_custom_call" | custom-call | bytes 1572864 | tf_op jit(solution)/shard_map/own_kernel/pallas_call | solution.py:98
  12.1 2.1 %tables_kernel.1 = (bf16[64,512]{1,0:T(8,128)(2,1)S(1)}, bf16[512,64]{1,0:T(8,128)(2,1)S(1)}, bf16[256,512]{1,0:T(8,128)(2,1)S(1)}, bf16[512,256]{1,0:T(8,128)(2...) custom-call(bf16[256,512]{1,0:T(8,128)(2,1)} %refs_7_.5, ...), custom_call_target="tpu_custom_call" | custom-call | bytes 270464 | tf_op jit(solution)/shard_map/tables_kernel/pallas_call | solution.py:98
  14.2 2.1 %collective-permute-done.1.refs_2_ = bf16[16,3584]{1,0:T(8,128)(2,1)S(1)} collective-permute-done((bf16[16,3584]{1,0:T(8,128)(2,1)S(1)}, bf16[16,3584]{1,0:T(8,128)(2,1)S(1)}, u32[]{:S(2)}, u32[]{:S(2)}) %collective-permute-start.1) | collective-permute-done | bytes 114720 | tf_op jit(solution)/shard_map/ppermute | solution.py:565
  16.5 3.0 %collective-permute-start.6 = (bf16[16,3072]{1,0:T(8,128)(2,1)S(1)}, bf16[16,3072]{1,0:T(8,128)(2,1)S(1)}, u32[]{:S(2)}, u32[]{:S(2)}) collective-permute-start(bf16[16,3072]{1,0:T(8,128)(2,1)S(1)} %get-tuple-element.80), channel_id=1, source_target_pairs={{0,1},{1,0},{2,3},{3,2},{4,5},{5,4},{6,7},{7,6},{8,9},{9,8},{10,11... | collective-permute-start | bytes 294920 | tf_op jit(solution)/shard_map/ppermute | solution.py:231
  19.5 1.6 %collective-permute-start.4 = (bf16[48,3072]{1,0:T(8,128)(2,1)S(1)}, bf16[48,3072]{1,0:T(8,128)(2,1)S(1)}, u32[]{:S(2)}, u32[]{:S(2)}) collective-permute-start(bf16[48,3072]{1,0:T(8,128)(2,1)S(1)} %get-tuple-element.78.refs_9_.refs_14_), channel_id=1, source_target_pairs={{0,16},{4,20},{8,24},{12,28},{16,0},{20,4},{24,8},{28,12},{1,17},{... | collective-permute-start | bytes 884744 | tf_op jit(solution)/shard_map/ppermute | solution.py:187
  23.0 1.7 %collective-permute-start.7 = (bf16[32,3072]{1,0:T(8,128)(2,1)S(1)}, bf16[32,3072]{1,0:T(8,128)(2,1)S(1)}, u32[]{:S(2)}, u32[]{:S(2)}) collective-permute-start(bf16[32,3072]{1,0:T(8,128)(2,1)S(1)} %pad_maximum_fusion.3), channel_id=1, source_target_pairs={{0,2},{1,3},{2,0},{3,1},{4,6},{5,7},{6,4},{7,5},{8,10},{9,11},{10,... | collective-permute-start | bytes 589832 | tf_op jit(solution)/shard_map/ppermute | solution.py:233
  24.7 9.3 %collective-permute-done.7 = bf16[32,3072]{1,0:T(8,128)(2,1)S(1)} collective-permute-done((bf16[32,3072]{1,0:T(8,128)(2,1)S(1)}, bf16[32,3072]{1,0:T(8,128)(2,1)S(1)}, u32[]{:S(2)}, u32[]{:S(2)}) %collective-permute-start.7) | collective-permute-done | bytes 196640 | tf_op jit(solution)/shard_map/ppermute | solution.py:233
  34.5 2.3 %collective-permute-done.3.refs_3_.refs_11_.refs_16_ = bf16[48,3584]{1,0:T(8,128)(2,1)S(1)} collective-permute-done((bf16[48,3584]{1,0:T(8,128)(2,1)S(1)}, bf16[48,3584]{1,0:T(8,128)(2,1)S(1)}, u32[]{:S(2)}, u32[]{:S(2)}) %collective-permute-start.3) | collective-permute-done | bytes 344096 | tf_op jit(solution)/shard_map/ppermute | solution.py:187
  37.5 1.6 %collective-permute-start.17 = (bf16[48,3072]{1,0:T(8,128)(2,1)S(1)}, bf16[48,3072]{1,0:T(8,128)(2,1)S(1)}, u32[]{:S(2)}, u32[]{:S(2)}) collective-permute-start(bf16[48,3072]{1,0:T(8,128)(2,1)S(1)} %pad_maximum_fusion.2.refs_9_), channel_id=1, source_target_pairs={{0,8},{4,12},{8,0},{12,4},{16,24},{20,28},{24,16},{28,20},{1,9},{5... | collective-permute-start | bytes 884744 | tf_op jit(solution)/shard_map/ppermute | solution.py:187
  41.9 3.8 %encode_kernel.1 = (bf16[256,512]{1,0:T(8,128)(2,1)S(1)}, bf16[512,512]{1,0:T(8,128)(2,1)S(1)}, bf16[512,512]{1,0:T(8,128)(2,1)S(1)}, f32[512,128]{1,0:T(8,128)S...) custom-call(bf16[512,512]{1,0:T(8,128)(2,1)S(1)} %get-tuple-element., ...), custom_call_target="tpu_custom_call" | custom-call | flops 3000000000 | bytes 5488640 | tf_op jit(solution)/shard_map/encode_kernel/pallas_call | solution.py:98
  47.9 6.3 %collective-permute-done.18.refs_12_ = bf16[48,3072]{1,0:T(8,128)(2,1)S(1)} collective-permute-done((bf16[48,3072]{1,0:T(8,128)(2,1)S(1)}, bf16[48,3072]{1,0:T(8,128)(2,1)S(1)}, u32[]{:S(2)}, u32[]{:S(2)}) %collective-permute-start.18) | collective-permute-done | bytes 294944 | tf_op jit(solution)/shard_map/ppermute | solution.py:187
  56.5 2.8 %collective-permute-start.15 = (bf16[16,512]{1,0:T(8,128)(2,1)S(1)}, bf16[16,512]{1,0:T(8,128)(2,1)S(1)}, u32[]{:S(2)}, u32[]{:S(2)}) collective-permute-start(bf16[16,512]{1,0:T(8,128)(2,1)S(1)} %get-tuple-element.97), channel_id=1, source_target_pairs={{0,3},{1,0},{2,1},{3,2},{4,7},{5,4},{6,5},{7,6},{8,11},{9,8},{10,9... | collective-permute-start | bytes 49160 | tf_op jit(solution)/shard_map/ppermute | solution.py:565
  59.3 1.7 %collective-permute-done.13.refs_3_ = bf16[16,512]{1,0:T(8,128)(2,1)S(1)} collective-permute-done((bf16[16,512]{1,0:T(8,128)(2,1)S(1)}, bf16[16,512]{1,0:T(8,128)(2,1)S(1)}, u32[]{:S(2)}, u32[]{:S(2)}) %collective-permute-start.13) | collective-permute-done | bytes 16416 | tf_op jit(solution)/shard_map/ppermute | solution.py:565
  61.6 5.3 %process_kernel.1 = (bf16[256,512]{1,0:T(8,128)(2,1)}, f32[256,512]{1,0:T(8,128)S(1)}, bf16[32,512]{1,0:T(8,128)(2,1)S(1)}, bf16[32,512]{1,0:T(8,128)(2,1)S(1)}) custom-call(bf16[256,512]{1,0:T(8,128)(2,1)} %refs_0_.7, bf16[256,512]{1,0:T(8,128)(2,1)S(1)} %get-tuple-element.89.refs_1_, bf16[16,512]{1,0:T(8,128)(2,1)S(1)} %get-tuple-element.94.refs_2_, ...), custom_call_target="tpu_custom_call" | custom-call | flops 5000000000 | bytes 4915200 | tf_op jit(solution)/shard_map/process_kernel/pallas_call | solution.py:98
  69.9 2.5 %collective-permute-done.22.refs_1_ = bf16[32,512]{1,0:T(8,128)(2,1)S(1)} collective-permute-done((bf16[32,512]{1,0:T(8,128)(2,1)S(1)}, bf16[32,512]{1,0:T(8,128)(2,1)S(1)}, u32[]{:S(2)}, u32[]{:S(2)}) %collective-permute-start.22) | collective-permute-done | bytes 32800 | tf_op jit(solution)/shard_map/ppermute | solution.py:569
  72.5 2.1 %collective-permute-start.23 = (bf16[16,512]{1,0:T(8,128)(2,1)S(1)}, bf16[16,512]{1,0:T(8,128)(2,1)S(1)}, u32[]{:S(2)}, u32[]{:S(2)}) collective-permute-start(bf16[16,512]{1,0:T(8,128)(2,1)S(1)} %get-tuple-element.111), channel_id=1, source_target_pairs={{0,1},{1,2},{2,3},{3,0},{4,5},{5,6},{6,7},{7,4},{8,9},{9,10},{10,1... | collective-permute-start | bytes 49160 | tf_op jit(solution)/shard_map/ppermute | solution.py:565
  74.6 1.8 %collective-permute-start.24 = (bf16[16,512]{1,0:T(8,128)(2,1)S(1)}, bf16[16,512]{1,0:T(8,128)(2,1)S(1)}, u32[]{:S(2)}, u32[]{:S(2)}) collective-permute-start(bf16[16,512]{1,0:T(8,128)(2,1)S(1)} %get-tuple-element.112), channel_id=1, source_target_pairs={{0,2},{1,3},{2,0},{3,1},{4,6},{5,7},{6,4},{7,5},{8,10},{9,11},{10,... | collective-permute-start | bytes 49160 | tf_op jit(solution)/shard_map/ppermute | solution.py:565
  80.2 3.2 %decode_kernel.1 = (f32[256,512]{1,0:T(8,128)}, bf16[32,512]{1,0:T(8,128)(2,1)S(1)}, bf16[32,512]{1,0:T(8,128)(2,1)S(1)}) custom-call(bf16[16,512]{1,0:T(8,128)(2,1)S(1)} %get-tuple-element.110.refs_0_, bf16[16,512]{1,0:T(8,128)(2,1)S(1)} %collective-permute-done.23.refs_1_, bf16[16,512]{1,0:T(8,128)(2,1)S(1)} %collective-permute-done.24.refs_2_, ...), custom_call_target="tpu_custom_call" | custom-call | flops 3000000000 | bytes 6471680 | tf_op jit(solution)/shard_map/decode_kernel/pallas_call | solution.py:98
  84.8 1.5 %collective-permute-start.27 = (bf16[32,512]{1,0:T(8,128)(2,1)S(1)}, bf16[32,512]{1,0:T(8,128)(2,1)S(1)}, u32[]{:S(2)}, u32[]{:S(2)}) collective-permute-start(bf16[32,512]{1,0:T(8,128)(2,1)S(1)} %get-tuple-element.126), channel_id=1, source_target_pairs={{0,8},{4,12},{8,0},{12,4},{1,9},{5,13},{9,1},{13,5},{2,10},{6,14},... | collective-permute-start | bytes 98312 | tf_op jit(solution)/shard_map/ppermute | solution.py:569
  86.3 2.5 %collective-permute-done.27.refs_1_ = bf16[32,512]{1,0:T(8,128)(2,1)S(1)} collective-permute-done((bf16[32,512]{1,0:T(8,128)(2,1)S(1)}, bf16[32,512]{1,0:T(8,128)(2,1)S(1)}, u32[]{:S(2)}, u32[]{:S(2)}) %collective-permute-start.27) | collective-permute-done | bytes 32800 | tf_op jit(solution)/shard_map/ppermute | solution.py:569
  89.6 2.4 %collective-permute-start.29 = (bf16[16,512]{1,0:T(8,128)(2,1)S(1)}, bf16[16,512]{1,0:T(8,128)(2,1)S(1)}, u32[]{:S(2)}, u32[]{:S(2)}) collective-permute-start(bf16[16,512]{1,0:T(8,128)(2,1)S(1)} %get-tuple-element.129), channel_id=1, source_target_pairs={{0,2},{1,3},{2,0},{3,1},{4,6},{5,7},{6,4},{7,5},{8,10},{9,11},{10,... | collective-permute-start | bytes 49160 | tf_op jit(solution)/shard_map/ppermute | solution.py:565
  (56 shorter events, 26.5 us)
Async XLA Ops:
  3.1 11.1 %collective-permute-start = (bf16[16,3584]{1,0:T(8,128)(2,1)S(1)}, bf16[16,3584]{1,0:T(8,128)(2,1)S(1)}, u32[]{:S(2)}, u32[]{:S(2)}) collective-permute-start(bf16[16,3584]{1,0:T(8,128)(2,1)S(1)} %get-tuple-element.73), channel_id=1, source_target_pairs={{0,1},{1,2},{2,3},{3,0},{4,5},{5,6},{6,7},{7,4},{8,9},{9,10},{10,1... | collective-permute-start | bytes 344072 | tf_op jit(solution)/shard_map/ppermute | solution.py:565
  6.2 10.2 %collective-permute-start.1 = (bf16[16,3584]{1,0:T(8,128)(2,1)S(1)}, bf16[16,3584]{1,0:T(8,128)(2,1)S(1)}, u32[]{:S(2)}, u32[]{:S(2)}) collective-permute-start(bf16[16,3584]{1,0:T(8,128)(2,1)S(1)} %get-tuple-element.74), channel_id=1, source_target_pairs={{0,2},{1,3},{2,0},{3,1},{4,6},{5,7},{6,4},{7,5},{8,10},{9,11},{10,... | collective-permute-start | bytes 344072 | tf_op jit(solution)/shard_map/ppermute | solution.py:565
  8.8 7.6 %collective-permute-start.2 = (bf16[16,3584]{1,0:T(8,128)(2,1)S(1)}, bf16[16,3584]{1,0:T(8,128)(2,1)S(1)}, u32[]{:S(2)}, u32[]{:S(2)}) collective-permute-start(bf16[16,3584]{1,0:T(8,128)(2,1)S(1)} %get-tuple-element.75), channel_id=1, source_target_pairs={{0,3},{1,0},{2,1},{3,2},{4,7},{5,4},{6,5},{7,6},{8,11},{9,8},{10,9... | collective-permute-start | bytes 344072 | tf_op jit(solution)/shard_map/ppermute | solution.py:565
  16.5 6.5 %collective-permute-start.6 = (bf16[16,3072]{1,0:T(8,128)(2,1)S(1)}, bf16[16,3072]{1,0:T(8,128)(2,1)S(1)}, u32[]{:S(2)}, u32[]{:S(2)}) collective-permute-start(bf16[16,3072]{1,0:T(8,128)(2,1)S(1)} %get-tuple-element.80), channel_id=1, source_target_pairs={{0,1},{1,0},{2,3},{3,2},{4,5},{5,4},{6,7},{7,6},{8,9},{9,8},{10,11... | collective-permute-start | bytes 294920 | tf_op jit(solution)/shard_map/ppermute | solution.py:231
  19.5 15.0 %collective-permute-start.4 = (bf16[48,3072]{1,0:T(8,128)(2,1)S(1)}, bf16[48,3072]{1,0:T(8,128)(2,1)S(1)}, u32[]{:S(2)}, u32[]{:S(2)}) collective-permute-start(bf16[48,3072]{1,0:T(8,128)(2,1)S(1)} %get-tuple-element.78.refs_9_.refs_14_), channel_id=1, source_target_pairs={{0,16},{4,20},{8,24},{12,28},{16,0},{20,4},{24,8},{28,12},{1,17},{... | collective-permute-start | bytes 884744 | tf_op jit(solution)/shard_map/ppermute | solution.py:187
  21.1 13.4 %collective-permute-start.5 = (bf16[48,3072]{1,0:T(8,128)(2,1)S(1)}, bf16[48,3072]{1,0:T(8,128)(2,1)S(1)}, u32[]{:S(2)}, u32[]{:S(2)}) collective-permute-start(bf16[48,3072]{1,0:T(8,128)(2,1)S(1)} %get-tuple-element.78.refs_9_.refs_14_), channel_id=1, source_target_pairs={{0,24},{4,28},{8,16},{12,20},{16,8},{20,12},{24,0},{28,4},{1,25},{... | collective-permute-start | bytes 884744 | tf_op jit(solution)/shard_map/ppermute | solution.py:187
  22.5 14.3 %collective-permute-start.3 = (bf16[48,3584]{1,0:T(8,128)(2,1)S(1)}, bf16[48,3584]{1,0:T(8,128)(2,1)S(1)}, u32[]{:S(2)}, u32[]{:S(2)}) collective-permute-start(bf16[48,3584]{1,0:T(8,128)(2,1)S(1)} %get-tuple-element.81), channel_id=1, source_target_pairs={{0,8},{4,12},{8,0},{12,4},{16,24},{20,28},{24,16},{28,20},{1,9},{5... | collective-permute-start | bytes 1032200 | tf_op jit(solution)/shard_map/ppermute | solution.py:187
  23.0 11.0 %collective-permute-start.7 = (bf16[32,3072]{1,0:T(8,128)(2,1)S(1)}, bf16[32,3072]{1,0:T(8,128)(2,1)S(1)}, u32[]{:S(2)}, u32[]{:S(2)}) collective-permute-start(bf16[32,3072]{1,0:T(8,128)(2,1)S(1)} %pad_maximum_fusion.3), channel_id=1, source_target_pairs={{0,2},{1,3},{2,0},{3,1},{4,6},{5,7},{6,4},{7,5},{8,10},{9,11},{10,... | collective-permute-start | bytes 589832 | tf_op jit(solution)/shard_map/ppermute | solution.py:233
  36.8 5.1 %collective-permute-start.10 = (bf16[96,3072]{1,0:T(8,128)(2,1)S(1)}, bf16[96,3072]{1,0:T(8,128)(2,1)S(1)}, u32[]{:S(2)}, u32[]{:S(2)}) collective-permute-start(bf16[96,3072]{1,0:T(8,128)(2,1)S(1)} %pad_maximum_fusion.1), channel_id=1, source_target_pairs={{0,4},{4,0},{8,12},{12,8},{16,20},{20,16},{24,28},{28,24},{1,5},{5... | collective-permute-start | bytes 1769480 | tf_op jit(solution)/shard_map/ppermute | solution.py:187
  37.4 4.5 %collective-permute-start.9 = (bf16[48,3584]{1,0:T(8,128)(2,1)S(1)}, bf16[48,3584]{1,0:T(8,128)(2,1)S(1)}, u32[]{:S(2)}, u32[]{:S(2)}) collective-permute-start(bf16[48,3584]{1,0:T(8,128)(2,1)S(1)} %collective-permute-done.3.refs_3_.refs_11_.refs_16_), channel_id=1, source_target_pairs={{0,4},{4,0},{8,12},{12,8},{16,20},{20,16},{24,28},{28,24},{1,5},{5... | collective-permute-start | bytes 1032200 | tf_op jit(solution)/shard_map/ppermute | solution.py:187
  37.5 10.4 %collective-permute-start.17 = (bf16[48,3072]{1,0:T(8,128)(2,1)S(1)}, bf16[48,3072]{1,0:T(8,128)(2,1)S(1)}, u32[]{:S(2)}, u32[]{:S(2)}) collective-permute-start(bf16[48,3072]{1,0:T(8,128)(2,1)S(1)} %pad_maximum_fusion.2.refs_9_), channel_id=1, source_target_pairs={{0,8},{4,12},{8,0},{12,4},{16,24},{20,28},{24,16},{28,20},{1,9},{5... | collective-permute-start | bytes 884744 | tf_op jit(solution)/shard_map/ppermute | solution.py:187
  39.1 15.2 %collective-permute-start.18 = (bf16[48,3072]{1,0:T(8,128)(2,1)S(1)}, bf16[48,3072]{1,0:T(8,128)(2,1)S(1)}, u32[]{:S(2)}, u32[]{:S(2)}) collective-permute-start(bf16[48,3072]{1,0:T(8,128)(2,1)S(1)} %pad_maximum_fusion.2.refs_9_), channel_id=1, source_target_pairs={{0,16},{4,20},{8,24},{12,28},{16,0},{20,4},{24,8},{28,12},{1,17},{... | collective-permute-start | bytes 884744 | tf_op jit(solution)/shard_map/ppermute | solution.py:187
  40.6 14.0 %collective-permute-start.19 = (bf16[48,3072]{1,0:T(8,128)(2,1)S(1)}, bf16[48,3072]{1,0:T(8,128)(2,1)S(1)}, u32[]{:S(2)}, u32[]{:S(2)}) collective-permute-start(bf16[48,3072]{1,0:T(8,128)(2,1)S(1)} %pad_maximum_fusion.2.refs_9_), channel_id=1, source_target_pairs={{0,24},{4,28},{8,16},{12,20},{16,8},{20,12},{24,0},{28,4},{1,25},{... | collective-permute-start | bytes 884744 | tf_op jit(solution)/shard_map/ppermute | solution.py:187
  47.2 7.6 %collective-permute-start.12 = (bf16[32,512]{1,0:T(8,128)(2,1)S(1)}, bf16[32,512]{1,0:T(8,128)(2,1)S(1)}, u32[]{:S(2)}, u32[]{:S(2)}) collective-permute-start(bf16[32,512]{1,0:T(8,128)(2,1)S(1)} %get-tuple-element.93), channel_id=1, source_target_pairs={{0,8},{4,12},{8,0},{12,4},{1,9},{5,13},{9,1},{13,5},{2,10},{6,14},... | collective-permute-start | bytes 98312 | tf_op jit(solution)/shard_map/ppermute | solution.py:569
  54.9 6.7 %collective-permute-start.20 = (bf16[144,3072]{1,0:T(8,128)(2,1)S(1)}, bf16[144,3072]{1,0:T(8,128)(2,1)S(1)}, u32[]{:S(2)}, u32[]{:S(2)}) collective-permute-start(bf16[144,3072]{1,0:T(8,128)(2,1)S(1)} %pad_maximum_fusion), channel_id=1, source_target_pairs={{0,4},{4,0},{8,12},{12,8},{16,20},{20,16},{24,28},{28,24},{1,5},{5... | collective-permute-start | bytes 2654216 | tf_op jit(solution)/shard_map/ppermute | solution.py:187
  55.0 4.3 %collective-permute-start.16 = (bf16[48,3072]{1,0:T(8,128)(2,1)S(1)}, bf16[48,3072]{1,0:T(8,128)(2,1)S(1)}, u32[]{:S(2)}, u32[]{:S(2)}) collective-permute-start(bf16[48,3072]{1,0:T(8,128)(2,1)S(1)} %pad_maximum_fusion.2.refs_9_), channel_id=1, source_target_pairs={{0,4},{4,0},{8,12},{12,8},{16,20},{20,16},{24,28},{28,24},{1,5},{5... | collective-permute-start | bytes 884744 | tf_op jit(solution)/shard_map/ppermute | solution.py:187
  55.5 5.5 %collective-permute-start.13 = (bf16[16,512]{1,0:T(8,128)(2,1)S(1)}, bf16[16,512]{1,0:T(8,128)(2,1)S(1)}, u32[]{:S(2)}, u32[]{:S(2)}) collective-permute-start(bf16[16,512]{1,0:T(8,128)(2,1)S(1)} %get-tuple-element.95), channel_id=1, source_target_pairs={{0,1},{1,2},{2,3},{3,0},{4,5},{5,6},{6,7},{7,4},{8,9},{9,10},{10,1... | collective-permute-start | bytes 49160 | tf_op jit(solution)/shard_map/ppermute | solution.py:565
  55.8 5.2 %collective-permute-start.14 = (bf16[16,512]{1,0:T(8,128)(2,1)S(1)}, bf16[16,512]{1,0:T(8,128)(2,1)S(1)}, u32[]{:S(2)}, u32[]{:S(2)}) collective-permute-start(bf16[16,512]{1,0:T(8,128)(2,1)S(1)} %get-tuple-element.96), channel_id=1, source_target_pairs={{0,2},{1,3},{2,0},{3,1},{4,6},{5,7},{6,4},{7,5},{8,10},{9,11},{10,... | collective-permute-start | bytes 49160 | tf_op jit(solution)/shard_map/ppermute | solution.py:565
  56.5 5.1 %collective-permute-start.15 = (bf16[16,512]{1,0:T(8,128)(2,1)S(1)}, bf16[16,512]{1,0:T(8,128)(2,1)S(1)}, u32[]{:S(2)}, u32[]{:S(2)}) collective-permute-start(bf16[16,512]{1,0:T(8,128)(2,1)S(1)} %get-tuple-element.97), channel_id=1, source_target_pairs={{0,3},{1,0},{2,1},{3,2},{4,7},{5,4},{6,5},{7,6},{8,11},{9,8},{10,9... | collective-permute-start | bytes 49160 | tf_op jit(solution)/shard_map/ppermute | solution.py:565
  68.4 4.0 %collective-permute-start.22 = (bf16[32,512]{1,0:T(8,128)(2,1)S(1)}, bf16[32,512]{1,0:T(8,128)(2,1)S(1)}, u32[]{:S(2)}, u32[]{:S(2)}) collective-permute-start(bf16[32,512]{1,0:T(8,128)(2,1)S(1)} %get-tuple-element.109), channel_id=1, source_target_pairs={{0,8},{4,12},{8,0},{12,4},{1,9},{5,13},{9,1},{13,5},{2,10},{6,14},... | collective-permute-start | bytes 98312 | tf_op jit(solution)/shard_map/ppermute | solution.py:569
  72.5 5.7 %collective-permute-start.23 = (bf16[16,512]{1,0:T(8,128)(2,1)S(1)}, bf16[16,512]{1,0:T(8,128)(2,1)S(1)}, u32[]{:S(2)}, u32[]{:S(2)}) collective-permute-start(bf16[16,512]{1,0:T(8,128)(2,1)S(1)} %get-tuple-element.111), channel_id=1, source_target_pairs={{0,1},{1,2},{2,3},{3,0},{4,5},{5,6},{6,7},{7,4},{8,9},{9,10},{10,1... | collective-permute-start | bytes 49160 | tf_op jit(solution)/shard_map/ppermute | solution.py:565
  74.6 4.6 %collective-permute-start.24 = (bf16[16,512]{1,0:T(8,128)(2,1)S(1)}, bf16[16,512]{1,0:T(8,128)(2,1)S(1)}, u32[]{:S(2)}, u32[]{:S(2)}) collective-permute-start(bf16[16,512]{1,0:T(8,128)(2,1)S(1)} %get-tuple-element.112), channel_id=1, source_target_pairs={{0,2},{1,3},{2,0},{3,1},{4,6},{5,7},{6,4},{7,5},{8,10},{9,11},{10,... | collective-permute-start | bytes 49160 | tf_op jit(solution)/shard_map/ppermute | solution.py:565
  89.0 5.6 %collective-permute-start.28 = (bf16[16,512]{1,0:T(8,128)(2,1)S(1)}, bf16[16,512]{1,0:T(8,128)(2,1)S(1)}, u32[]{:S(2)}, u32[]{:S(2)}) collective-permute-start(bf16[16,512]{1,0:T(8,128)(2,1)S(1)} %get-tuple-element.128), channel_id=1, source_target_pairs={{0,1},{1,2},{2,3},{3,0},{4,5},{5,6},{6,7},{7,4},{8,9},{9,10},{10,1... | collective-permute-start | bytes 49160 | tf_op jit(solution)/shard_map/ppermute | solution.py:565
  89.6 5.0 %collective-permute-start.29 = (bf16[16,512]{1,0:T(8,128)(2,1)S(1)}, bf16[16,512]{1,0:T(8,128)(2,1)S(1)}, u32[]{:S(2)}, u32[]{:S(2)}) collective-permute-start(bf16[16,512]{1,0:T(8,128)(2,1)S(1)} %get-tuple-element.129), channel_id=1, source_target_pairs={{0,2},{1,3},{2,0},{3,1},{4,6},{5,7},{6,4},{7,5},{8,10},{9,11},{10,... | collective-permute-start | bytes 49160 | tf_op jit(solution)/shard_map/ppermute | solution.py:565
  (7 other events, 19.0 us)

commit v11 on v6

--- a/solution.py
+++ b/solution.py
@@ -200,7 +200,7 @@
             rows.append(lax.all_gather(shards[2 * i + 1], "mp", axis=0, tiled=True))
         enc, proc = jnp.concatenate(rows[:4], axis=1), jnp.concatenate(rows[4:], axis=1)
         arrived = exchange(outgoing, step)
-        return [enc], lambda one, moved: [proc], arrived, grid_t, tables
+        return [enc], lambda moved, arrive: ([proc], arrive(moved)), arrived, grid_t, tables
     far = [Far(s) for s in shards]
     piece = hidden // planes
     width = 6 * features
@@ -213,7 +213,9 @@
     )
     enc_own, proc_own = call(own_kernel, [shape(hidden, width, BF16)] * 2, far)
     messages = [along(m, i + 1) for i, m in enumerate(messages)]
-    kept, enc_own, *tables = lax.optimization_barrier((kept, enc_own, *tables))
+    proc_piece, enc_own = lax.optimization_barrier((proc_piece, enc_own))
+    beside_me = lax.ppermute(proc_piece, "mp", [(m, m ^ 1) for m in range(mp)])
+    kept, beside_me, *tables = lax.optimization_barrier((kept, beside_me, *tables))
     rows = mp * step
     near, first, both = call(
         join_kernel,
@@ -221,25 +223,28 @@
         kept,
         messages,
     )
-    core, x, y = across(both, 1), across(both, 2), across(first, 4)
-    proc_piece, _ = lax.optimization_barrier((proc_piece, core))
-    low, high = relay(x, y)
-    x_core, y_core = across(x, 1), across(y, 1)
-    parts = [along(proc_piece, s) for s in (1, 2, 3)]
-    *parts, _, _ = lax.optimization_barrier((*parts, low, high))
-    far_corner = jnp.concatenate([low, high], axis=1)
-    enc = [enc_own, first, core, x, y, x_core, y_core, far_corner, across(far_corner, 1)]
+    x, y = across(both, 2), across(first, 4)
+    pair = jnp.concatenate([proc_piece, beside_me])
+    pairs = lax.ppermute(pair, "mp", [(m, m ^ 2) for m in range(mp)])
+    proc_first = jnp.concatenate([beside_me, pairs])
+    late_x, late_y, both, _ = lax.optimization_barrier((x, y, both, pairs))
+    low, high = relay(late_x, late_y)
+    core, x_core = across(both, 1), across(late_x, 1)
+    corner = jnp.concatenate([low, high], axis=1)
+    others = across(jnp.concatenate([y, corner]), 1)
+    enc = [enc_own, first, core, x, y, corner, x_core, others]
     arrived = [near, core, x, x_core]
-    proc_first = jnp.concatenate(parts)
-    proc_core, proc_x, proc_y = [across(proc_first, flip) for flip in (1, 2, 4)]
-
-    def finish(one, moved):
-        x, y, _ = lax.optimization_barrier((proc_x, proc_y, one))
+    proc_first, *_ = lax.optimization_barrier((proc_first, low, high))
+    proc_x, proc_y = across(proc_first, 2), across(proc_first, 4)
+
+    def finish(moved, arrive):
+        x, y, *_ = lax.optimization_barrier((proc_x, proc_y, *moved))
         low, high = relay(x, y)
-        x, y, *_ = lax.optimization_barrier((x, y, *moved))
-        corner = jnp.concatenate([low, high], axis=1)
-        blocks = [proc_own, proc_first, proc_core, x, y, across(x, 1), across(y, 1)]
-        return blocks + [corner, across(corner, 1)]
+        came = arrive(moved)
+        corner, *_ = lax.optimization_barrier((jnp.concatenate([low, high], axis=1), *came))
+        sides = jnp.concatenate([x, y])
+        blocks = [proc_own, proc_first, across(proc_first, 1), sides, across(sides, 1)]
+        return blocks + [corner, across(corner, 1)], came
 
     return enc, finish, arrived, grid_t, tables
 
@@ -251,9 +256,10 @@
 
 def forward(inputs, first, second):
     before = dot_trans(inputs, first)
-    logistic = jax.nn.sigmoid(before)
-    hidden = (before * logistic).astype(BF16)
-    slope = logistic * (1.0 + before * (1.0 - logistic))
+    logistic = 0.5 + 0.5 * jnp.tanh(0.5 * before)
+    wide = before * logistic
+    hidden = wide.astype(BF16)
+    slope = logistic + wide * (1.0 - logistic)
     summed = dot(hidden, second)
     centered = summed - jnp.mean(summed, axis=-1, keepdims=True)
     rescale = lax.rsqrt(jnp.mean(centered * centered, axis=-1, keepdims=True) + 1e-05)
@@ -567,9 +573,7 @@
         halo_g,
         flops=3 * 10**9,
     )
-    moved = first_level(halo_out, halo_step)
-    proc = finish(mesh_one, moved)
-    halo_in = second_level(moved)
+    proc, halo_in = finish(first_level(halo_out, halo_step), second_level)
     mesh_two, grad_one, *grad_halo = call(
         process_kernel,
         [shape(mesh_rows, features, BF16), shape(mesh_rows, features, F32)]

time: 103 us -> 98.7 us (0.958)
  starting transfers between devices: 37.7 us -> 34.4 us
  waiting for transfers between devices: 44 us -> 42.6 us
    ppermute x0 -> x2, waiting for transfers between devices: none -> 14.1 us  [the longest x1 10.4 us: start(): pairs = lax.ppermute(pair, 'mp', [(m, m ^ 2) for m in range(mp)])]
    ppermute x15 -> x12, waiting for transfers between devices: 21.7 us -> 11 us  [along(): lax.ppermute(block, 'mp', [(m, (m + shift) % size) for m in range(size)])]
    ppermute x15 -> x12, starting transfers between devices: 21.5 us -> 17.8 us  [along(): lax.ppermute(block, 'mp', [(m, (m + shift) % size) for m in range(size)])]
    ppermute x16 -> x14, waiting for transfers between devices: 14.1 us -> 10.4 us  [across(): lax.ppermute(x, ('groups', 'graph'), [(p, p ^ flip) for p in range(planes)])]
    ppermute x0 -> x2, starting transfers between devices: none -> 1.28 us  [the longest x1 0.74 us: start(): beside_me = lax.ppermute(proc_piece, 'mp', [(m, m ^ 1) for m in range(mp)])]
    ppermute x9, waiting for transfers between devices: 8.15 us -> 7.02 us  [beside(): lax.ppermute(block, 'graph', [(g, g ^ flip) for g in range(lax.axis_size(...]
    ppermute x16 -> x14, starting transfers between devices: 10.9 us -> 10.1 us  [across(): lax.ppermute(x, ('groups', 'graph'), [(p, p ^ flip) for p in range(planes)])]
  transfers between devices with their start and end apart: 40 -> 37, of which waited for: 21 -> 21; matrix products, arithmetic and copies ran while one was open for 0% -> 0% of each run, Pallas kernels for 7% -> 8%
where the time goes in v11:
time: 98.7 us; the launch traced here: 98.5 us
  waiting for transfers between devices  42.6 us (43%)
  starting transfers between devices  34.4 us (35%)
  Pallas kernels  20.5 us (21%)
    pallas_call x11, Pallas kernels, call(): pl.pallas_call(body, out_shape=out_shape, in_specs=[hbm if away else vmem...  20.5 us
    ppermute x12, starting transfers between devices, along(): lax.ppermute(block, 'mp', [(m, (m + shift) % size) for m in range(size)])  17.8 us
    ppermute x12, waiting for transfers between devices, along(): lax.ppermute(block, 'mp', [(m, (m + shift) % size) for m in range(size)])  11 us
    ppermute x14, waiting for transfers between devices, across(): lax.ppermute(x, ('groups', 'graph'), [(p, p ^ flip) for p in range(planes)])  10.4 us
    ppermute x1, waiting for transfers between devices, start(): pairs = lax.ppermute(pair, 'mp', [(m, m ^ 2) for m in range(mp)])  10.4 us
    ppermute x14, starting transfers between devices, across(): lax.ppermute(x, ('groups', 'graph'), [(p, p ^ flip) for p in range(planes)])  10.1 us
    ppermute x9, waiting for transfers between devices, beside(): lax.ppermute(block, 'graph', [(g, g ^ flip) for g in range(lax.axis_size(...  7.02 us
    ppermute x9, starting transfers between devices, beside(): lax.ppermute(block, 'graph', [(g, g ^ flip) for g in range(lax.axis_size(...  5.24 us
  transfers between devices with their start and end apart: 37, of which 21 were waited for; matrix products, arithmetic and copies ran while one was open for 0% of the time, Pallas kernels for 8%

profile of v11, /device:TPU:0, one launch (start us, length us, event | category | flops | bytes accessed | tf_op | source)
XLA Modules:
  0.0 98.5 jit_solution(2252362134746725073)
XLA Ops:
  0.6 2.4 %prepare_kernel.1 = (bf16[16,3072]{1,0:T(8,128)(2,1)S(1)}, bf16[512,64]{1,0:T(8,128)(2,1)S(1)}, bf16[16,512]{1,0:T(8,128)(2,1)S(1)}, bf16[16,3584]{1,0:T(8,128)(...) custom-call(bf16[512,512]{1,0:T(8,128)(2,1)} %refs_0_.4, s32[4,16]{1,0:T(4,128)} %bitcast.6, ...), custom_call_target="tpu_custom_call" | custom-call | bytes 2097408 | tf_op jit(solution)/shard_map/prepare_kernel/pallas_call | solution.py:96
  3.1 3.1 %collective-permute-start.1 = (bf16[16,3584]{1,0:T(8,128)(2,1)S(1)}, bf16[16,3584]{1,0:T(8,128)(2,1)S(1)}, u32[]{:S(2)}, u32[]{:S(2)}) collective-permute-start(bf16[16,3584]{1,0:T(8,128)(2,1)S(1)} %get-tuple-element.98), channel_id=1, source_target_pairs={{0,1},{1,2},{2,3},{3,0},{4,5},{5,6},{6,7},{7,4},{8,9},{9,10},{10,1... | collective-permute-start | bytes 344072 | tf_op jit(solution)/shard_map/ppermute | solution.py:482
  6.1 2.6 %collective-permute-start.2 = (bf16[16,3584]{1,0:T(8,128)(2,1)S(1)}, bf16[16,3584]{1,0:T(8,128)(2,1)S(1)}, u32[]{:S(2)}, u32[]{:S(2)}) collective-permute-start(bf16[16,3584]{1,0:T(8,128)(2,1)S(1)} %get-tuple-element.99), channel_id=1, source_target_pairs={{0,2},{1,3},{2,0},{3,1},{4,6},{5,7},{6,4},{7,5},{8,10},{9,11},{10,... | collective-permute-start | bytes 344072 | tf_op jit(solution)/shard_map/ppermute | solution.py:482
  10.1 2.0 %own_kernel.1 = (bf16[128,3072]{1,0:T(8,128)(2,1)S(1)}, bf16[128,3072]{1,0:T(8,128)(2,1)S(1)}) custom-call(bf16[1024,128]{1,0:T(8,128)(2,1)} %refs_0_.5, bf16[128,512]{1,0:T(8,128)(2,1)} %refs_1_.1, bf16[1024,128]{1,0:T(8,128)(2,1)} %refs_2_.3, bf16[128,512]{1,0:T(8,128)(2,1)} %refs_3_.3, bf16[1024,128]{1,0:T(8,128)(2,1)} %refs_4_.3, ...), custom_call_target="tpu_custom_call" | custom-call | bytes 1572864 | tf_op jit(solution)/shard_map/own_kernel/pallas_call | solution.py:96
  12.9 1.7 %tables_kernel.1 = (bf16[64,512]{1,0:T(8,128)(2,1)S(1)}, bf16[512,64]{1,0:T(8,128)(2,1)S(1)}, bf16[256,512]{1,0:T(8,128)(2,1)S(1)}, bf16[512,256]{1,0:T(8,128)(2...) custom-call(bf16[256,512]{1,0:T(8,128)(2,1)} %refs_7_.5, ...), custom_call_target="tpu_custom_call" | custom-call | bytes 270464 | tf_op jit(solution)/shard_map/tables_kernel/pallas_call | solution.py:96
  14.6 3.8 %collective-permute-done = bf16[16,3072]{1,0:T(8,128)(2,1)S(1)} collective-permute-done((bf16[16,3072]{1,0:T(8,128)(2,1)S(1)}, bf16[16,3072]{1,0:T(8,128)(2,1)S(1)}, u32[]{:S(2)}, u32[]{:S(2)}) %collective-permute-start) | collective-permute-done | bytes 98336 | tf_op jit(solution)/shard_map/ppermute | solution.py:217
  18.6 1.7 %collective-permute-start.5 = (bf16[48,3072]{1,0:T(8,128)(2,1)S(1)}, bf16[48,3072]{1,0:T(8,128)(2,1)S(1)}, u32[]{:S(2)}, u32[]{:S(2)}) collective-permute-start(bf16[48,3072]{1,0:T(8,128)(2,1)S(1)} %get-tuple-element.103.refs_9_.refs_14_), channel_id=1, source_target_pairs={{0,16},{4,20},{8,24},{12,28},{16,0},{20,4},{24,8},{28,12},{1,17},{... | collective-permute-start | bytes 884744 | tf_op jit(solution)/shard_map/ppermute | solution.py:185
  22.3 10.4 %collective-permute-done.6 = bf16[32,3072]{1,0:T(8,128)(2,1)S(1)} collective-permute-done((bf16[32,3072]{1,0:T(8,128)(2,1)S(1)}, bf16[32,3072]{1,0:T(8,128)(2,1)S(1)}, u32[]{:S(2)}, u32[]{:S(2)}) %collective-permute-start.6) | collective-permute-done | bytes 196640 | tf_op jit(solution)/shard_map/ppermute | solution.py:228
  34.0 3.9 %collective-permute-done.9 = bf16[48,1536]{1,0:T(8,128)(2,1)S(1)} collective-permute-done((bf16[48,1536]{1,0:T(8,128)(2,1)S(1)}, bf16[48,1536]{1,0:T(8,128)(2,1)S(1)}, u32[]{:S(2)}, u32[]{:S(2)}) %collective-permute-start.9) | collective-permute-done | bytes 147488 | tf_op jit(solution)/shard_map/ppermute | solution.py:185
  39.2 1.6 %collective-permute-start.20 = (bf16[48,3072]{1,0:T(8,128)(2,1)S(1)}, bf16[48,3072]{1,0:T(8,128)(2,1)S(1)}, u32[]{:S(2)}, u32[]{:S(2)}) collective-permute-start(bf16[48,3072]{1,0:T(8,128)(2,1)S(1)} %pad_maximum_fusion.1.refs_9_), channel_id=1, source_target_pairs={{0,16},{4,20},{8,24},{12,28},{16,0},{20,4},{24,8},{28,12},{1,17},{... | collective-permute-start | bytes 884744 | tf_op jit(solution)/shard_map/ppermute | solution.py:185
  41.6 3.8 %encode_kernel.1 = (bf16[256,512]{1,0:T(8,128)(2,1)S(1)}, bf16[512,512]{1,0:T(8,128)(2,1)S(1)}, bf16[512,512]{1,0:T(8,128)(2,1)S(1)}, f32[512,128]{1,0:T(8,128)S...) custom-call(bf16[512,512]{1,0:T(8,128)(2,1)S(1)} %get-tuple-element., ...), custom_call_target="tpu_custom_call" | custom-call | flops 3000000000 | bytes 5488640 | tf_op jit(solution)/shard_map/encode_kernel/pallas_call | solution.py:96
  45.5 2.1 %collective-permute-start.13 = (bf16[16,512]{1,0:T(8,128)(2,1)S(1)}, bf16[16,512]{1,0:T(8,128)(2,1)S(1)}, u32[]{:S(2)}, u32[]{:S(2)}) collective-permute-start(bf16[16,512]{1,0:T(8,128)(2,1)S(1)} %get-tuple-element.115), channel_id=1, source_target_pairs={{0,2},{1,3},{2,0},{3,1},{4,6},{5,7},{6,4},{7,5},{8,10},{9,11},{10,... | collective-permute-start | bytes 49160 | tf_op jit(solution)/shard_map/ppermute | solution.py:482
  47.6 1.7 %collective-permute-start.14 = (bf16[16,512]{1,0:T(8,128)(2,1)S(1)}, bf16[16,512]{1,0:T(8,128)(2,1)S(1)}, u32[]{:S(2)}, u32[]{:S(2)}) collective-permute-start(bf16[16,512]{1,0:T(8,128)(2,1)S(1)} %get-tuple-element.116), channel_id=1, source_target_pairs={{0,3},{1,0},{2,1},{3,2},{4,7},{5,4},{6,5},{7,6},{8,11},{9,8},{10,9... | collective-permute-start | bytes 49160 | tf_op jit(solution)/shard_map/ppermute | solution.py:482
  49.3 1.7 %collective-permute-done.12.refs_1_ = bf16[16,512]{1,0:T(8,128)(2,1)S(1)} collective-permute-done((bf16[16,512]{1,0:T(8,128)(2,1)S(1)}, bf16[16,512]{1,0:T(8,128)(2,1)S(1)}, u32[]{:S(2)}, u32[]{:S(2)}) %collective-permute-start.12) | collective-permute-done | bytes 16416 | tf_op jit(solution)/shard_map/ppermute | solution.py:482
  55.6 3.6 %collective-permute-done.23 = bf16[48,1536]{1,0:T(8,128)(2,1)S(1)} collective-permute-done((bf16[48,1536]{1,0:T(8,128)(2,1)S(1)}, bf16[48,1536]{1,0:T(8,128)(2,1)S(1)}, u32[]{:S(2)}, u32[]{:S(2)}) %collective-permute-start.23) | collective-permute-done | bytes 147488 | tf_op jit(solution)/shard_map/ppermute | solution.py:185
  60.2 2.2 %collective-permute-done.17.refs_5_ = bf16[16,512]{1,0:T(8,128)(2,1)S(1)} collective-permute-done((bf16[16,512]{1,0:T(8,128)(2,1)S(1)}, bf16[16,512]{1,0:T(8,128)(2,1)S(1)}, u32[]{:S(2)}, u32[]{:S(2)}) %collective-permute-start.17) | collective-permute-done | bytes 16416 | tf_op jit(solution)/shard_map/ppermute | solution.py:488
  62.4 1.6 %collective-permute-done.24.refs_14_ = bf16[48,3072]{1,0:T(8,128)(2,1)S(1)} collective-permute-done((bf16[48,3072]{1,0:T(8,128)(2,1)S(1)}, bf16[48,3072]{1,0:T(8,128)(2,1)S(1)}, u32[]{:S(2)}, u32[]{:S(2)}) %collective-permute-start.24) | collective-permute-done | bytes 294944 | tf_op jit(solution)/shard_map/ppermute | solution.py:185
  64.0 5.3 %process_kernel.1 = (bf16[256,512]{1,0:T(8,128)(2,1)}, f32[256,512]{1,0:T(8,128)S(1)}, bf16[16,512]{1,0:T(8,128)(2,1)S(1)}, bf16[16,512]{1,0:T(8,128)(2,1)S(1)},...) custom-call(bf16[256,512]{1,0:T(8,128)(2,1)} %refs_0_.7, bf16[256,512]{1,0:T(8,128)(2,1)S(1)} %get-tuple-element.112.refs_1_, ...), custom_call_target="tpu_custom_call" | custom-call | flops 5000000000 | bytes 4915200 | tf_op jit(solution)/shard_map/process_kernel/pallas_call | solution.py:96
  71.3 2.0 %collective-permute-done.26.refs_2_ = bf16[16,512]{1,0:T(8,128)(2,1)S(1)} collective-permute-done((bf16[16,512]{1,0:T(8,128)(2,1)S(1)}, bf16[16,512]{1,0:T(8,128)(2,1)S(1)}, u32[]{:S(2)}, u32[]{:S(2)}) %collective-permute-start.26) | collective-permute-done | bytes 16416 | tf_op jit(solution)/shard_map/ppermute | solution.py:488
  73.7 3.3 %collective-permute-start.28 = (bf16[16,512]{1,0:T(8,128)(2,1)S(1)}, bf16[16,512]{1,0:T(8,128)(2,1)S(1)}, u32[]{:S(2)}, u32[]{:S(2)}) collective-permute-start(bf16[16,512]{1,0:T(8,128)(2,1)S(1)} %get-tuple-element.136), channel_id=1, source_target_pairs={{0,3},{1,0},{2,1},{3,2},{4,7},{5,4},{6,5},{7,6},{8,11},{9,8},{10,9... | collective-permute-start | bytes 49160 | tf_op jit(solution)/shard_map/ppermute | solution.py:482
  78.5 3.2 %collective-permute-done.29.refs_2_ = bf16[16,512]{1,0:T(8,128)(2,1)S(1)} collective-permute-done((bf16[16,512]{1,0:T(8,128)(2,1)S(1)}, bf16[16,512]{1,0:T(8,128)(2,1)S(1)}, u32[]{:S(2)}, u32[]{:S(2)}) %collective-permute-start.29) | collective-permute-done | bytes 16416 | tf_op jit(solution)/shard_map/ppermute | solution.py:482
  82.8 3.2 %decode_kernel.1 = (f32[256,512]{1,0:T(8,128)}, bf16[16,512]{1,0:T(8,128)(2,1)S(1)}, bf16[16,512]{1,0:T(8,128)(2,1)S(1)}, bf16[16,512]{1,0:T(8,128)(2,1)S(1)}, bf16[16,512]{1,0:T(8,128)(2,1)S(1)}) custom-call(bf16[16,512]{1,0:T(8,128)(2,1)S(1)} %get-tuple-element.135.refs_0_, bf16[16,512]{1,0:T(8,128)(2,1)S(1)} %collective-permute-done.28.refs_1_, ...), custom_call_target="tpu_custom_call" | custom-call | flops 3000000000 | bytes 6471680 | tf_op jit(solution)/shard_map/decode_kernel/pallas_call | solution.py:96
  87.9 1.9 %collective-permute-done.32.refs_2_ = bf16[16,512]{1,0:T(8,128)(2,1)S(1)} collective-permute-done((bf16[16,512]{1,0:T(8,128)(2,1)S(1)}, bf16[16,512]{1,0:T(8,128)(2,1)S(1)}, u32[]{:S(2)}, u32[]{:S(2)}) %collective-permute-start.32) | collective-permute-done | bytes 16416 | tf_op jit(solution)/shard_map/ppermute | solution.py:488
  91.7 1.9 %collective-permute-start.36 = (bf16[16,512]{1,0:T(8,128)(2,1)S(1)}, bf16[16,512]{1,0:T(8,128)(2,1)S(1)}, u32[]{:S(2)}, u32[]{:S(2)}) collective-permute-start(bf16[16,512]{1,0:T(8,128)(2,1)S(1)} %get-tuple-element.156), channel_id=1, source_target_pairs={{0,1},{1,2},{2,3},{3,0},{4,5},{5,6},{6,7},{7,4},{8,9},{9,10},{10,1... | collective-permute-start | bytes 49160 | tf_op jit(solution)/shard_map/ppermute | solution.py:482
  (73 shorter events, 26.9 us)
Async XLA Ops:
  3.1 15.3 %collective-permute-start.1 = (bf16[16,3584]{1,0:T(8,128)(2,1)S(1)}, bf16[16,3584]{1,0:T(8,128)(2,1)S(1)}, u32[]{:S(2)}, u32[]{:S(2)}) collective-permute-start(bf16[16,3584]{1,0:T(8,128)(2,1)S(1)} %get-tuple-element.98), channel_id=1, source_target_pairs={{0,1},{1,2},{2,3},{3,0},{4,5},{5,6},{6,7},{7,4},{8,9},{9,10},{10,1... | collective-permute-start | bytes 344072 | tf_op jit(solution)/shard_map/ppermute | solution.py:482
  6.1 12.2 %collective-permute-start.2 = (bf16[16,3584]{1,0:T(8,128)(2,1)S(1)}, bf16[16,3584]{1,0:T(8,128)(2,1)S(1)}, u32[]{:S(2)}, u32[]{:S(2)}) collective-permute-start(bf16[16,3584]{1,0:T(8,128)(2,1)S(1)} %get-tuple-element.99), channel_id=1, source_target_pairs={{0,2},{1,3},{2,0},{3,1},{4,6},{5,7},{6,4},{7,5},{8,10},{9,11},{10,... | collective-permute-start | bytes 344072 | tf_op jit(solution)/shard_map/ppermute | solution.py:482
  8.7 9.6 %collective-permute-start.3 = (bf16[16,3584]{1,0:T(8,128)(2,1)S(1)}, bf16[16,3584]{1,0:T(8,128)(2,1)S(1)}, u32[]{:S(2)}, u32[]{:S(2)}) collective-permute-start(bf16[16,3584]{1,0:T(8,128)(2,1)S(1)} %get-tuple-element.100), channel_id=1, source_target_pairs={{0,3},{1,0},{2,1},{3,2},{4,7},{5,4},{6,5},{7,6},{8,11},{9,8},{10,9... | collective-permute-start | bytes 344072 | tf_op jit(solution)/shard_map/ppermute | solution.py:482
  12.1 6.2 %collective-permute-start = (bf16[16,3072]{1,0:T(8,128)(2,1)S(1)}, bf16[16,3072]{1,0:T(8,128)(2,1)S(1)}, u32[]{:S(2)}, u32[]{:S(2)}) collective-permute-start(bf16[16,3072]{1,0:T(8,128)(2,1)S(1)} %get-tuple-element.84), channel_id=1, source_target_pairs={{0,1},{1,0},{2,3},{3,2},{4,5},{5,4},{6,7},{7,6},{8,9},{9,8},{10,11... | collective-permute-start | bytes 294920 | tf_op jit(solution)/shard_map/ppermute | solution.py:217
  18.6 14.1 %collective-permute-start.5 = (bf16[48,3072]{1,0:T(8,128)(2,1)S(1)}, bf16[48,3072]{1,0:T(8,128)(2,1)S(1)}, u32[]{:S(2)}, u32[]{:S(2)}) collective-permute-start(bf16[48,3072]{1,0:T(8,128)(2,1)S(1)} %get-tuple-element.103.refs_9_.refs_14_), channel_id=1, source_target_pairs={{0,16},{4,20},{8,24},{12,28},{16,0},{20,4},{24,8},{28,12},{1,17},{... | collective-permute-start | bytes 884744 | tf_op jit(solution)/shard_map/ppermute | solution.py:185
  20.3 12.4 %collective-permute-start.4 = (bf16[48,3584]{1,0:T(8,128)(2,1)S(1)}, bf16[48,3584]{1,0:T(8,128)(2,1)S(1)}, u32[]{:S(2)}, u32[]{:S(2)}) collective-permute-start(bf16[48,3584]{1,0:T(8,128)(2,1)S(1)} %get-tuple-element.105), channel_id=1, source_target_pairs={{0,8},{4,12},{8,0},{12,4},{16,24},{20,28},{24,16},{28,20},{1,9},{5... | collective-permute-start | bytes 1032200 | tf_op jit(solution)/shard_map/ppermute | solution.py:185
  21.8 10.9 %collective-permute-start.6 = (bf16[32,3072]{1,0:T(8,128)(2,1)S(1)}, bf16[32,3072]{1,0:T(8,128)(2,1)S(1)}, u32[]{:S(2)}, u32[]{:S(2)}) collective-permute-start(bf16[32,3072]{1,0:T(8,128)(2,1)S(1)} %pad_maximum_fusion.3), channel_id=1, source_target_pairs={{0,2},{1,3},{2,0},{3,1},{4,6},{5,7},{6,4},{7,5},{8,10},{9,11},{10,... | collective-permute-start | bytes 589832 | tf_op jit(solution)/shard_map/ppermute | solution.py:228
  32.7 5.2 %collective-permute-start.9 = (bf16[48,1536]{1,0:T(8,128)(2,1)S(1)}, bf16[48,1536]{1,0:T(8,128)(2,1)S(1)}, u32[]{:S(2)}, u32[]{:S(2)}) collective-permute-start(bf16[48,1536]{1,0:T(8,128)(2,1)S(1)} %slice.12), channel_id=1, source_target_pairs={{0,16},{4,20},{8,24},{12,28},{16,0},{20,4},{24,8},{28,12},{1,17},{... | collective-permute-start | bytes 442376 | tf_op jit(solution)/shard_map/ppermute | solution.py:185
  33.3 5.2 %collective-permute-start.10 = (bf16[48,1536]{1,0:T(8,128)(2,1)S(1)}, bf16[48,1536]{1,0:T(8,128)(2,1)S(1)}, u32[]{:S(2)}, u32[]{:S(2)}) collective-permute-start(bf16[48,1536]{1,0:T(8,128)(2,1)S(1)} %slice.13), channel_id=1, source_target_pairs={{0,8},{4,12},{8,0},{12,4},{16,24},{20,28},{24,16},{28,20},{1,9},{5... | collective-permute-start | bytes 442376 | tf_op jit(solution)/shard_map/ppermute | solution.py:185
  39.2 13.9 %collective-permute-start.20 = (bf16[48,3072]{1,0:T(8,128)(2,1)S(1)}, bf16[48,3072]{1,0:T(8,128)(2,1)S(1)}, u32[]{:S(2)}, u32[]{:S(2)}) collective-permute-start(bf16[48,3072]{1,0:T(8,128)(2,1)S(1)} %pad_maximum_fusion.1.refs_9_), channel_id=1, source_target_pairs={{0,16},{4,20},{8,24},{12,28},{16,0},{20,4},{24,8},{28,12},{1,17},{... | collective-permute-start | bytes 884744 | tf_op jit(solution)/shard_map/ppermute | solution.py:185
  40.8 12.4 %collective-permute-start.19 = (bf16[48,3072]{1,0:T(8,128)(2,1)S(1)}, bf16[48,3072]{1,0:T(8,128)(2,1)S(1)}, u32[]{:S(2)}, u32[]{:S(2)}) collective-permute-start(bf16[48,3072]{1,0:T(8,128)(2,1)S(1)} %pad_maximum_fusion.1.refs_9_), channel_id=1, source_target_pairs={{0,8},{4,12},{8,0},{12,4},{16,24},{20,28},{24,16},{28,20},{1,9},{5... | collective-permute-start | bytes 884744 | tf_op jit(solution)/shard_map/ppermute | solution.py:185
  45.4 5.6 %collective-permute-start.12 = (bf16[16,512]{1,0:T(8,128)(2,1)S(1)}, bf16[16,512]{1,0:T(8,128)(2,1)S(1)}, u32[]{:S(2)}, u32[]{:S(2)}) collective-permute-start(bf16[16,512]{1,0:T(8,128)(2,1)S(1)} %get-tuple-element.114), channel_id=1, source_target_pairs={{0,1},{1,2},{2,3},{3,0},{4,5},{5,6},{6,7},{7,4},{8,9},{9,10},{10,1... | collective-permute-start | bytes 49160 | tf_op jit(solution)/shard_map/ppermute | solution.py:482
  45.5 5.5 %collective-permute-start.13 = (bf16[16,512]{1,0:T(8,128)(2,1)S(1)}, bf16[16,512]{1,0:T(8,128)(2,1)S(1)}, u32[]{:S(2)}, u32[]{:S(2)}) collective-permute-start(bf16[16,512]{1,0:T(8,128)(2,1)S(1)} %get-tuple-element.115), channel_id=1, source_target_pairs={{0,2},{1,3},{2,0},{3,1},{4,6},{5,7},{6,4},{7,5},{8,10},{9,11},{10,... | collective-permute-start | bytes 49160 | tf_op jit(solution)/shard_map/ppermute | solution.py:482
  51.0 11.4 %collective-permute-start.18 = (bf16[48,3072]{1,0:T(8,128)(2,1)S(1)}, bf16[48,3072]{1,0:T(8,128)(2,1)S(1)}, u32[]{:S(2)}, u32[]{:S(2)}) collective-permute-start(bf16[48,3072]{1,0:T(8,128)(2,1)S(1)} %pad_maximum_fusion.1.refs_9_), channel_id=1, source_target_pairs={{0,4},{4,0},{8,12},{12,8},{16,20},{20,16},{24,28},{28,24},{1,5},{5... | collective-permute-start | bytes 884744 | tf_op jit(solution)/shard_map/ppermute | solution.py:185
  51.8 8.4 %collective-permute-start.15 = (bf16[16,512]{1,0:T(8,128)(2,1)S(1)}, bf16[16,512]{1,0:T(8,128)(2,1)S(1)}, u32[]{:S(2)}, u32[]{:S(2)}) collective-permute-start(bf16[16,512]{1,0:T(8,128)(2,1)S(1)} %get-tuple-element.118), channel_id=1, source_target_pairs={{0,4},{4,0},{8,12},{12,8},{1,5},{5,1},{9,13},{13,9},{2,6},{6,2},{1... | collective-permute-start | bytes 49160 | tf_op jit(solution)/shard_map/ppermute | solution.py:488
  51.9 8.4 %collective-permute-start.16 = (bf16[16,512]{1,0:T(8,128)(2,1)S(1)}, bf16[16,512]{1,0:T(8,128)(2,1)S(1)}, u32[]{:S(2)}, u32[]{:S(2)}) collective-permute-start(bf16[16,512]{1,0:T(8,128)(2,1)S(1)} %get-tuple-element.119), channel_id=1, source_target_pairs={{0,8},{4,12},{8,0},{12,4},{1,9},{5,13},{9,1},{13,5},{2,10},{6,14},... | collective-permute-start | bytes 49160 | tf_op jit(solution)/shard_map/ppermute | solution.py:488
  53.3 6.0 %collective-permute-start.23 = (bf16[48,1536]{1,0:T(8,128)(2,1)S(1)}, bf16[48,1536]{1,0:T(8,128)(2,1)S(1)}, u32[]{:S(2)}, u32[]{:S(2)}) collective-permute-start(bf16[48,1536]{1,0:T(8,128)(2,1)S(1)} %slice.15), channel_id=1, source_target_pairs={{0,8},{4,12},{8,0},{12,4},{16,24},{20,28},{24,16},{28,20},{1,9},{5... | collective-permute-start | bytes 442376 | tf_op jit(solution)/shard_map/ppermute | solution.py:185
  54.1 5.6 %collective-permute-start.22 = (bf16[48,1536]{1,0:T(8,128)(2,1)S(1)}, bf16[48,1536]{1,0:T(8,128)(2,1)S(1)}, u32[]{:S(2)}, u32[]{:S(2)}) collective-permute-start(bf16[48,1536]{1,0:T(8,128)(2,1)S(1)} %slice.14), channel_id=1, source_target_pairs={{0,16},{4,20},{8,24},{12,28},{16,0},{20,4},{24,8},{28,12},{1,17},{... | collective-permute-start | bytes 442376 | tf_op jit(solution)/shard_map/ppermute | solution.py:185
  59.7 4.2 %collective-permute-start.21 = (bf16[96,3072]{1,0:T(8,128)(2,1)S(1)}, bf16[96,3072]{1,0:T(8,128)(2,1)S(1)}, u32[]{:S(2)}, u32[]{:S(2)}) collective-permute-start(bf16[96,3072]{1,0:T(8,128)(2,1)S(1)} %constant_dynamic-update-slice_fusion.2.refs_11_), channel_id=1, source_target_pairs={{0,4},{4,0},{8,12},{12,8},{16,20},{20,16},{24,28},{28,24},{1,5},{5... | collective-permute-start | bytes 1769480 | tf_op jit(solution)/shard_map/ppermute | solution.py:185
  73.7 4.8 %collective-permute-start.28 = (bf16[16,512]{1,0:T(8,128)(2,1)S(1)}, bf16[16,512]{1,0:T(8,128)(2,1)S(1)}, u32[]{:S(2)}, u32[]{:S(2)}) collective-permute-start(bf16[16,512]{1,0:T(8,128)(2,1)S(1)} %get-tuple-element.136), channel_id=1, source_target_pairs={{0,3},{1,0},{2,1},{3,2},{4,7},{5,4},{6,5},{7,6},{8,11},{9,8},{10,9... | collective-permute-start | bytes 49160 | tf_op jit(solution)/shard_map/ppermute | solution.py:482
  77.1 4.6 %collective-permute-start.29 = (bf16[16,512]{1,0:T(8,128)(2,1)S(1)}, bf16[16,512]{1,0:T(8,128)(2,1)S(1)}, u32[]{:S(2)}, u32[]{:S(2)}) collective-permute-start(bf16[16,512]{1,0:T(8,128)(2,1)S(1)} %get-tuple-element.137), channel_id=1, source_target_pairs={{0,2},{1,3},{2,0},{3,1},{4,6},{5,7},{6,4},{7,5},{8,10},{9,11},{10,... | collective-permute-start | bytes 49160 | tf_op jit(solution)/shard_map/ppermute | solution.py:482
  77.3 5.5 %collective-permute-start.30 = (bf16[16,512]{1,0:T(8,128)(2,1)S(1)}, bf16[16,512]{1,0:T(8,128)(2,1)S(1)}, u32[]{:S(2)}, u32[]{:S(2)}) collective-permute-start(bf16[16,512]{1,0:T(8,128)(2,1)S(1)} %get-tuple-element.138), channel_id=1, source_target_pairs={{0,1},{1,2},{2,3},{3,0},{4,5},{5,6},{6,7},{7,4},{8,9},{9,10},{10,1... | collective-permute-start | bytes 49160 | tf_op jit(solution)/shard_map/ppermute | solution.py:482
  91.1 4.8 %collective-permute-start.35 = (bf16[16,512]{1,0:T(8,128)(2,1)S(1)}, bf16[16,512]{1,0:T(8,128)(2,1)S(1)}, u32[]{:S(2)}, u32[]{:S(2)}) collective-permute-start(bf16[16,512]{1,0:T(8,128)(2,1)S(1)} %get-tuple-element.155), channel_id=1, source_target_pairs={{0,2},{1,3},{2,0},{3,1},{4,6},{5,7},{6,4},{7,5},{8,10},{9,11},{10,... | collective-permute-start | bytes 49160 | tf_op jit(solution)/shard_map/ppermute | solution.py:482
  91.7 5.5 %collective-permute-start.36 = (bf16[16,512]{1,0:T(8,128)(2,1)S(1)}, bf16[16,512]{1,0:T(8,128)(2,1)S(1)}, u32[]{:S(2)}, u32[]{:S(2)}) collective-permute-start(bf16[16,512]{1,0:T(8,128)(2,1)S(1)} %get-tuple-element.156), channel_id=1, source_target_pairs={{0,1},{1,2},{2,3},{3,0},{4,5},{5,6},{6,7},{7,4},{8,9},{9,10},{10,1... | collective-permute-start | bytes 49160 | tf_op jit(solution)/shard_map/ppermute | solution.py:482
  (13 other events, 38.5 us)

commit v12 on v7

--- a/solution.py
+++ b/solution.py
@@ -124,9 +124,11 @@
 def prepare_kernel(grid, send, shards, proc_piece, table_out, kept, *messages):
     plane = lax.axis_index("groups") * lax.axis_size("graph") + lax.axis_index("graph")
     width = 3 * FEATURES
-    rows = proc_piece.ref.shape[0]
-    base = plane * rows
-    for i in range(4):
+    graph = lax.axis_index("graph")
+    core_and_y = lax.axis_index("groups") * 2 + graph % 2
+    for i, part in enumerate((plane, plane, graph, core_and_y)):
+        rows = proc_piece.ref.shape[0] if i // 2 else messages[0].ref.shape[0]
+        base = part * rows
         one, two = shards[2 * i](), shards[2 * i + 1]()
         hidden = one.shape[1]
         select = jnp.where(
@@ -175,7 +177,7 @@
             1.0,
             0.0,
         ).astype(BF16)
-        out, low = outs[i // 2], i % 2 * width
+        out, low = outs[max(i - 1, 0)], i % 2 * width if i < 2 else 0
         out.ref[:, low : low + 2 * FEATURES] = turned(one[...], select)
         out.ref[:, low + 2 * FEATURES : low + width] = two[...]
 
@@ -198,20 +200,23 @@
         for i in range(4):
             rows.append(lax.all_gather(shards[2 * i], "mp", axis=1, tiled=True).T)
             rows.append(lax.all_gather(shards[2 * i + 1], "mp", axis=0, tiled=True))
-        enc, proc = jnp.concatenate(rows[:4], axis=1), jnp.concatenate(rows[4:], axis=1)
+        enc = jnp.concatenate(rows[:4], axis=1)
+        edge, node = jnp.concatenate(rows[4:6], axis=1), jnp.concatenate(rows[6:], axis=1)
         arrived = exchange(outgoing, step)
-        return [enc], lambda moved: [proc], arrived, grid_t, tables
+        return [enc], lambda one, early, moved, arrive: ([edge], [node], arrive(moved)), arrived, grid_t, tables
     far = [Far(s) for s in shards]
     piece = hidden // planes
     width = 6 * features
     proc_piece, grid_t, kept, *messages = call(
         prepare_kernel,
-        [shape(piece, width, BF16)] + sent[:2] + [shape(piece, width + features, BF16)] * 3,
+        [shape(2 * piece, width, BF16)] + sent[:2] + [shape(piece, width + features, BF16)] * 3,
         Far(grid_lat),
         Far(grid_send.T),
         far,
     )
-    enc_own, proc_own = call(own_kernel, [shape(hidden, width, BF16)] * 2, far)
+    enc_own, edge_own, node_own = call(
+        own_kernel, [shape(hidden, w, BF16) for w in (width, width // 2, width // 2)], far
+    )
     messages = [along(m, i + 1) for i, m in enumerate(messages)]
     kept, enc_own, *tables = lax.optimization_barrier((kept, enc_own, *tables))
     rows = mp * step
@@ -221,31 +226,45 @@
         kept,
         messages,
     )
-    x, y, corner, core = across(both, 2), across(first, 4), across(first, 6), across(both, 1)
-    proc_piece, _ = lax.optimization_barrier((proc_piece, core))
-    x_core = across(x, 1)
-    enc = [enc_own, first, core, x, y, corner, x_core, across(y, 1), across(corner, 1)]
+    x, y, corner = across(both, 2), across(first, 4), across(first, 6)
+    proc_piece, _ = lax.optimization_barrier((proc_piece, near))
+    beside_me = lax.ppermute(proc_piece, "mp", [(m, m ^ 1) for m in range(mp)])
+    half = width // 2
+    edge_pair, node_pair = [
+        jnp.concatenate([proc_piece[:, a : a + half], beside_me[:, a : a + half]]) for a in (0, half)
+    ]
+    over_two = [(m, m ^ 2) for m in range(mp)]
+    edge_pairs = lax.ppermute(edge_pair, "mp", over_two)
+    node_pair, _ = lax.optimization_barrier((node_pair, edge_pairs))
+    node_pairs = lax.ppermute(node_pair, "mp", over_two)
+    both, x, y, corner, _ = lax.optimization_barrier((both, x, y, corner, edge_pairs))
+    core, x_core = across(both, 1), across(x, 1)
+    enc = [enc_own, first, core, x, y, corner, x_core, across(jnp.concatenate([y, corner]), 1)]
     arrived = [near, core, x, x_core]
-    beside_me = lax.ppermute(proc_piece, "mp", [(m, m ^ 1) for m in range(mp)])
-    pair = jnp.concatenate([proc_piece, beside_me])
-    others = lax.ppermute(pair, "mp", [(m, m ^ 2) for m in range(mp)])
-    proc_first = jnp.concatenate([beside_me, others])
-    proc_first, *_ = lax.optimization_barrier((proc_first, x, y, corner))
-    plane = [across(proc_first, flip) for flip in (2, 4, 6)]
-    proc = [proc_own, proc_first, across(proc_first, 1)] + plane
-
-    def finish(moved):
-        tied, *_ = lax.optimization_barrier((jnp.concatenate(plane), *moved))
-        return proc + [across(tied, 1)]
+
+    def finish(one, early, moved, arrive):
+        near_edge, far_edge, _ = lax.optimization_barrier((beside_me, edge_pairs, one))
+        edge = jnp.concatenate([near_edge[:, :half], far_edge])
+        edge_x = across(edge, 2)
+        near_node, far_node, *_ = lax.optimization_barrier((beside_me, node_pairs, early))
+        node = jnp.concatenate([near_node[:, half:], far_node])
+        node_y = across(node, 4)
+        edge, edge_x, *_ = lax.optimization_barrier((edge, edge_x, *moved))
+        edge = jnp.concatenate([edge, edge_x])
+        came = arrive(moved)
+        node, node_y, *_ = lax.optimization_barrier((node, node_y, *came))
+        node = jnp.concatenate([node, node_y])
+        return [edge_own, edge, across(edge, 1)], [node_own, node, across(node, 1)], came
 
     return enc, finish, arrived, grid_t, tables
 
 
 def forward(inputs, first, second):
     before = dot_trans(inputs, first)
-    logistic = jax.nn.sigmoid(before)
-    hidden = (before * logistic).astype(BF16)
-    slope = logistic * (1.0 + before * (1.0 - logistic))
+    logistic = 0.5 + 0.5 * jnp.tanh(0.5 * before)
+    wide = before * logistic
+    hidden = wide.astype(BF16)
+    slope = logistic + wide * (1.0 - logistic)
     summed = dot(hidden, second)
     centered = summed - jnp.mean(summed, axis=-1, keepdims=True)
     rescale = lax.rsqrt(jnp.mean(centered * centered, axis=-1, keepdims=True) + 1e-05)
@@ -391,7 +410,7 @@
 
 
 def process_kernel(
-    cotangent_in, one_in, halo, sender_g, proc_g, weights, proc_t, sender_t, two, grad_one, *refs
+    cotangent_in, one_in, halo, sender_g, proc_g, edge, node, proc_t, sender_t, two, grad_one, *refs
 ):
     grad_halo, (slope_p, normed_p, scale_p, ga_p) = refs[:-4], refs[-4:]
     features = FEATURES
@@ -399,7 +418,7 @@
     mesh_rows = one.shape[0]
     lookup = jnp.concatenate([one, stacked(halo)], axis=0)
     edges = sender_g().shape[0]
-    first, second = layers(weights, 0)
+    first, second = layers(edge, 0)
     for low in range(0, edges, ROWS):
         rows = pl.ds(low, ROWS)
         sent = dot(sender_g()[rows, :], lookup).astype(BF16)
@@ -409,7 +428,7 @@
         normed_p[rows, :] = normed
         scale_p[rows, :] = jnp.broadcast_to(rescale, (ROWS, LANES))
     aggregate = dot(proc_t()[...], normed_p[...]).astype(BF16)
-    first_n, second_n = layers(weights, 1)
+    first_n, second_n = layers(node, 0)
     normed, slope, rounded, rescale = forward(
         jnp.concatenate([one, aggregate], axis=1), first_n, second_n
     )
@@ -559,9 +578,9 @@
         halo_g,
         flops=3 * 10**9,
     )
-    moved = first_level(halo_out, halo_step)
-    proc = finish(moved)
-    halo_in = second_level(moved)
+    shifted = [along(b, s) for s, b in enumerate(halo_out)]
+    moved = turn(shifted, graph, halo_step)
+    edge, node, halo_in = finish(mesh_one, shifted[1], moved, second_level)
     mesh_two, grad_one, *grad_halo = call(
         process_kernel,
         [shape(mesh_rows, features, BF16), shape(mesh_rows, features, F32)]
@@ -571,7 +590,8 @@
         halo_in,
         sender_g,
         proc_g,
-        proc,
+        edge,
+        node,
         proc_t,
         sender_t,
         last=(0,),

time: 94.8 us -> 99.7 us (1.052)
  waiting for transfers between devices: 39.3 us -> 43.2 us
    ppermute x12 -> x10, waiting for transfers between devices: 13.8 us -> 22 us  [across(): lax.ppermute(x, ('groups', 'graph'), [(p, p ^ flip) for p in range(planes)])]
    ppermute x12, waiting for transfers between devices: 17.7 us -> 12.5 us  [along(): lax.ppermute(block, 'mp', [(m, (m + shift) % size) for m in range(size)])]
    ppermute x12, starting transfers between devices: 15.3 us -> 17.5 us  [along(): lax.ppermute(block, 'mp', [(m, (m + shift) % size) for m in range(size)])]
    ppermute x9, waiting for transfers between devices: 7.76 us -> 6.16 us  [beside(): lax.ppermute(block, 'graph', [(g, g ^ flip) for g in range(lax.axis_size(...]
    ppermute x1, waiting for transfers between devices: 0.01 us -> 1.51 us  [start(): beside_me = lax.ppermute(proc_piece, 'mp', [(m, m ^ 1) for m in range(mp)])]
    ppermute x12 -> x10, starting transfers between devices: 8.19 us -> 7.03 us  [across(): lax.ppermute(x, ('groups', 'graph'), [(p, p ^ flip) for p in range(planes)])]
  transfers between devices with their start and end apart: 35 -> 34, of which waited for: 18 -> 24; matrix products, arithmetic and copies ran while one was open for 0% -> 0% of each run, Pallas kernels for 8% -> 8%
where the time goes in v12:
time: 99.7 us; the launch traced here: 99.5 us
  waiting for transfers between devices  43.2 us (43%)
  starting transfers between devices  34.7 us (35%)
  Pallas kernels  20.5 us (21%)
    ppermute x10, waiting for transfers between devices, across(): lax.ppermute(x, ('groups', 'graph'), [(p, p ^ flip) for p in range(planes)])  22 us
    pallas_call x11, Pallas kernels, call(): pl.pallas_call(body, out_shape=out_shape, in_specs=[hbm if away else vmem...  20.5 us
    ppermute x12, starting transfers between devices, along(): lax.ppermute(block, 'mp', [(m, (m + shift) % size) for m in range(size)])  17.5 us
    ppermute x12, waiting for transfers between devices, along(): lax.ppermute(block, 'mp', [(m, (m + shift) % size) for m in range(size)])  12.5 us
    ppermute x10, starting transfers between devices, across(): lax.ppermute(x, ('groups', 'graph'), [(p, p ^ flip) for p in range(planes)])  7.03 us
    ppermute x9, waiting for transfers between devices, beside(): lax.ppermute(block, 'graph', [(g, g ^ flip) for g in range(lax.axis_size(...  6.16 us
    ppermute x9, starting transfers between devices, beside(): lax.ppermute(block, 'graph', [(g, g ^ flip) for g in range(lax.axis_size(...  5.79 us
    ppermute x1, starting transfers between devices, start(): beside_me = lax.ppermute(proc_piece, 'mp', [(m, m ^ 1) for m in range(mp)])  2.99 us
  transfers between devices with their start and end apart: 34, of which 24 were waited for; matrix products, arithmetic and copies ran while one was open for 0% of the time, Pallas kernels for 8%

profile of v12, /device:TPU:0, one launch (start us, length us, event | category | flops | bytes accessed | tf_op | source)
XLA Modules:
  0.0 99.5 jit_solution(3057383454284693704)
XLA Ops:
  0.6 2.5 %prepare_kernel.1 = (bf16[32,3072]{1,0:T(8,128)(2,1)S(1)}, bf16[512,64]{1,0:T(8,128)(2,1)S(1)}, bf16[16,512]{1,0:T(8,128)(2,1)S(1)}, bf16[16,3584]{1,0:T(8,128)(...) custom-call(bf16[512,512]{1,0:T(8,128)(2,1)} %refs_0_.4, s32[4,16]{1,0:T(4,128)} %bitcast.6, ...), custom_call_target="tpu_custom_call" | custom-call | bytes 2097408 | tf_op jit(solution)/shard_map/prepare_kernel/pallas_call | solution.py:96
  3.1 3.1 %collective-permute-start = (bf16[16,3584]{1,0:T(8,128)(2,1)S(1)}, bf16[16,3584]{1,0:T(8,128)(2,1)S(1)}, u32[]{:S(2)}, u32[]{:S(2)}) collective-permute-start(bf16[16,3584]{1,0:T(8,128)(2,1)S(1)} %get-tuple-element.102), channel_id=1, source_target_pairs={{0,1},{1,2},{2,3},{3,0},{4,5},{5,6},{6,7},{7,4},{8,9},{9,10},{10,1... | collective-permute-start | bytes 344072 | tf_op jit(solution)/shard_map/ppermute | solution.py:487
  6.2 2.6 %collective-permute-start.1 = (bf16[16,3584]{1,0:T(8,128)(2,1)S(1)}, bf16[16,3584]{1,0:T(8,128)(2,1)S(1)}, u32[]{:S(2)}, u32[]{:S(2)}) collective-permute-start(bf16[16,3584]{1,0:T(8,128)(2,1)S(1)} %get-tuple-element.103), channel_id=1, source_target_pairs={{0,2},{1,3},{2,0},{3,1},{4,6},{5,7},{6,4},{7,5},{8,10},{9,11},{10,... | collective-permute-start | bytes 344072 | tf_op jit(solution)/shard_map/ppermute | solution.py:487
  10.1 2.0 %own_kernel.1 = (bf16[128,3072]{1,0:T(8,128)(2,1)S(1)}, bf16[128,1536]{1,0:T(8,128)(2,1)S(1)}, bf16[128,1536]{1,0:T(8,128)(2,1)S(1)}) custom-call(bf16[1024,128]{1,0:T(8,128)(2,1)} %refs_0_.5, bf16[128,512]{1,0:T(8,128)(2,1)} %refs_1_.1, bf16[1024,128]{1,0:T(8,128)(2,1)} %refs_2_.3, bf16[128,512]{1,0:T(8,128)(2,1)} %refs_3_.3, bf16[1024,128]{1,0:T(8,128)(2,1)} %refs_4_.3, ...), custom_call_target="tpu_custom_call" | custom-call | bytes 1572864 | tf_op jit(solution)/shard_map/own_kernel/pallas_call | solution.py:96
  12.1 1.7 %tables_kernel.1 = (bf16[64,512]{1,0:T(8,128)(2,1)S(1)}, bf16[512,64]{1,0:T(8,128)(2,1)S(1)}, bf16[256,512]{1,0:T(8,128)(2,1)S(1)}, bf16[512,256]{1,0:T(8,128)(2...) custom-call(bf16[256,512]{1,0:T(8,128)(2,1)} %refs_7_.5, ...), custom_call_target="tpu_custom_call" | custom-call | bytes 270464 | tf_op jit(solution)/shard_map/tables_kernel/pallas_call | solution.py:96
  13.9 2.5 %collective-permute-done.1.refs_2_ = bf16[16,3584]{1,0:T(8,128)(2,1)S(1)} collective-permute-done((bf16[16,3584]{1,0:T(8,128)(2,1)S(1)}, bf16[16,3584]{1,0:T(8,128)(2,1)S(1)}, u32[]{:S(2)}, u32[]{:S(2)}) %collective-permute-start.1) | collective-permute-done | bytes 114720 | tf_op jit(solution)/shard_map/ppermute | solution.py:487
  16.6 3.0 %collective-permute-start.6 = (bf16[32,3072]{1,0:T(8,128)(2,1)S(1)}, bf16[32,3072]{1,0:T(8,128)(2,1)S(1)}, u32[]{:S(2)}, u32[]{:S(2)}) collective-permute-start(bf16[32,3072]{1,0:T(8,128)(2,1)S(1)} %get-tuple-element.109), channel_id=1, source_target_pairs={{0,1},{1,0},{2,3},{3,2},{4,5},{5,4},{6,7},{7,6},{8,9},{9,8},{10,11... | collective-permute-start | bytes 589832 | tf_op jit(solution)/shard_map/ppermute | solution.py:231
  19.6 2.6 %collective-permute-start.5 = (bf16[48,3072]{1,0:T(8,128)(2,1)S(1)}, bf16[48,3072]{1,0:T(8,128)(2,1)S(1)}, u32[]{:S(2)}, u32[]{:S(2)}) collective-permute-start(bf16[48,3072]{1,0:T(8,128)(2,1)S(1)} %get-tuple-element.107.refs_9_.refs_14_), channel_id=1, source_target_pairs={{0,24},{4,28},{8,16},{12,20},{16,8},{20,12},{24,0},{28,4},{1,25},{... | collective-permute-start | bytes 884744 | tf_op jit(solution)/shard_map/ppermute | solution.py:187
  23.1 1.5 %collective-permute-done.6 = bf16[32,3072]{1,0:T(8,128)(2,1)S(1)} collective-permute-done((bf16[32,3072]{1,0:T(8,128)(2,1)S(1)}, bf16[32,3072]{1,0:T(8,128)(2,1)S(1)}, u32[]{:S(2)}, u32[]{:S(2)}) %collective-permute-start.6) | collective-permute-done | bytes 196640 | tf_op jit(solution)/shard_map/ppermute | solution.py:231
  25.5 5.0 %collective-permute-done.5.refs_13_.refs_18_ = bf16[48,3072]{1,0:T(8,128)(2,1)S(1)} collective-permute-done((bf16[48,3072]{1,0:T(8,128)(2,1)S(1)}, bf16[48,3072]{1,0:T(8,128)(2,1)S(1)}, u32[]{:S(2)}, u32[]{:S(2)}) %collective-permute-start.5) | collective-permute-done | bytes 294944 | tf_op jit(solution)/shard_map/ppermute | solution.py:187
  30.5 5.0 %collective-permute-done.4.refs_12_.refs_17_ = bf16[48,3072]{1,0:T(8,128)(2,1)S(1)} collective-permute-done((bf16[48,3072]{1,0:T(8,128)(2,1)S(1)}, bf16[48,3072]{1,0:T(8,128)(2,1)S(1)}, u32[]{:S(2)}, u32[]{:S(2)}) %collective-permute-start.4) | collective-permute-done | bytes 294944 | tf_op jit(solution)/shard_map/ppermute | solution.py:187
  39.8 3.8 %encode_kernel.1 = (bf16[256,512]{1,0:T(8,128)(2,1)S(1)}, bf16[512,512]{1,0:T(8,128)(2,1)S(1)}, bf16[512,512]{1,0:T(8,128)(2,1)S(1)}, f32[512,128]{1,0:T(8,128)S...) custom-call(bf16[512,512]{1,0:T(8,128)(2,1)S(1)} %get-tuple-element., ...), custom_call_target="tpu_custom_call" | custom-call | flops 3000000000 | bytes 5488640 | tf_op jit(solution)/shard_map/encode_kernel/pallas_call | solution.py:96
  43.7 1.6 %collective-permute-start.17 = (bf16[96,1536]{1,0:T(8,128)(2,1)S(1)}, bf16[96,1536]{1,0:T(8,128)(2,1)S(1)}, u32[]{:S(2)}, u32[]{:S(2)}) collective-permute-start(bf16[96,1536]{1,0:T(8,128)(2,1)S(1)} %pad_maximum_fusion.1), channel_id=1, source_target_pairs={{0,8},{4,12},{8,0},{12,4},{16,24},{20,28},{24,16},{28,20},{1,9},{5... | collective-permute-start | bytes 884744 | tf_op jit(solution)/shard_map/ppermute | solution.py:187
  46.4 2.6 %collective-permute-start.13 = (bf16[16,512]{1,0:T(8,128)(2,1)S(1)}, bf16[16,512]{1,0:T(8,128)(2,1)S(1)}, u32[]{:S(2)}, u32[]{:S(2)}) collective-permute-start(bf16[16,512]{1,0:T(8,128)(2,1)S(1)} %get-tuple-element.122), channel_id=1, source_target_pairs={{0,3},{1,0},{2,1},{3,2},{4,7},{5,4},{6,5},{7,6},{8,11},{9,8},{10,9... | collective-permute-start | bytes 49160 | tf_op jit(solution)/shard_map/ppermute | solution.py:487
  55.8 7.0 %collective-permute-done.20 = bf16[96,1536]{1,0:T(8,128)(2,1)S(1)} collective-permute-done((bf16[96,1536]{1,0:T(8,128)(2,1)S(1)}, bf16[96,1536]{1,0:T(8,128)(2,1)S(1)}, u32[]{:S(2)}, u32[]{:S(2)}) %collective-permute-start.20) | collective-permute-done | bytes 294944 | tf_op jit(solution)/shard_map/ppermute | solution.py:187
  63.0 2.0 %collective-permute-done.21.refs_13_ = bf16[192,1536]{1,0:T(8,128)(2,1)S(1)} collective-permute-done((bf16[192,1536]{1,0:T(8,128)(2,1)S(1)}, bf16[192,1536]{1,0:T(8,128)(2,1)S(1)}, u32[]{:S(2)}, u32[]{:S(2)}) %collective-permute-start.21) | collective-permute-done | bytes 589856 | tf_op jit(solution)/shard_map/ppermute | solution.py:187
  64.9 5.3 %process_kernel.1 = (bf16[256,512]{1,0:T(8,128)(2,1)}, f32[256,512]{1,0:T(8,128)S(1)}, bf16[16,512]{1,0:T(8,128)(2,1)S(1)}, bf16[16,512]{1,0:T(8,128)(2,1)S(1)},...) custom-call(bf16[256,512]{1,0:T(8,128)(2,1)} %refs_0_.7, bf16[256,512]{1,0:T(8,128)(2,1)S(1)} %get-tuple-element.118.refs_1_, ...), custom_call_target="tpu_custom_call" | custom-call | flops 5000000000 | bytes 4915200 | tf_op jit(solution)/shard_map/process_kernel/pallas_call | solution.py:96
  72.2 2.0 %collective-permute-done.23.refs_2_ = bf16[16,512]{1,0:T(8,128)(2,1)S(1)} collective-permute-done((bf16[16,512]{1,0:T(8,128)(2,1)S(1)}, bf16[16,512]{1,0:T(8,128)(2,1)S(1)}, u32[]{:S(2)}, u32[]{:S(2)}) %collective-permute-start.23) | collective-permute-done | bytes 16416 | tf_op jit(solution)/shard_map/ppermute | solution.py:493
  74.8 3.1 %collective-permute-start.25 = (bf16[16,512]{1,0:T(8,128)(2,1)S(1)}, bf16[16,512]{1,0:T(8,128)(2,1)S(1)}, u32[]{:S(2)}, u32[]{:S(2)}) collective-permute-start(bf16[16,512]{1,0:T(8,128)(2,1)S(1)} %get-tuple-element.148), channel_id=1, source_target_pairs={{0,3},{1,0},{2,1},{3,2},{4,7},{5,4},{6,5},{7,6},{8,11},{9,8},{10,9... | collective-permute-start | bytes 49160 | tf_op jit(solution)/shard_map/ppermute | solution.py:487
  79.3 3.2 %collective-permute-done.26.refs_2_ = bf16[16,512]{1,0:T(8,128)(2,1)S(1)} collective-permute-done((bf16[16,512]{1,0:T(8,128)(2,1)S(1)}, bf16[16,512]{1,0:T(8,128)(2,1)S(1)}, u32[]{:S(2)}, u32[]{:S(2)}) %collective-permute-start.26) | collective-permute-done | bytes 16416 | tf_op jit(solution)/shard_map/ppermute | solution.py:487
  83.6 3.2 %decode_kernel.1 = (f32[256,512]{1,0:T(8,128)}, bf16[16,512]{1,0:T(8,128)(2,1)S(1)}, bf16[16,512]{1,0:T(8,128)(2,1)S(1)}, bf16[16,512]{1,0:T(8,128)(2,1)S(1)}, bf16[16,512]{1,0:T(8,128)(2,1)S(1)}) custom-call(bf16[16,512]{1,0:T(8,128)(2,1)S(1)} %get-tuple-element.147.refs_0_, bf16[16,512]{1,0:T(8,128)(2,1)S(1)} %collective-permute-done.25.refs_1_, ...), custom_call_target="tpu_custom_call" | custom-call | flops 3000000000 | bytes 6471680 | tf_op jit(solution)/shard_map/decode_kernel/pallas_call | solution.py:96
  88.8 1.9 %collective-permute-done.29.refs_2_ = bf16[16,512]{1,0:T(8,128)(2,1)S(1)} collective-permute-done((bf16[16,512]{1,0:T(8,128)(2,1)S(1)}, bf16[16,512]{1,0:T(8,128)(2,1)S(1)}, u32[]{:S(2)}, u32[]{:S(2)}) %collective-permute-start.29) | collective-permute-done | bytes 16416 | tf_op jit(solution)/shard_map/ppermute | solution.py:493
  92.7 1.9 %collective-permute-start.33 = (bf16[16,512]{1,0:T(8,128)(2,1)S(1)}, bf16[16,512]{1,0:T(8,128)(2,1)S(1)}, u32[]{:S(2)}, u32[]{:S(2)}) collective-permute-start(bf16[16,512]{1,0:T(8,128)(2,1)S(1)} %get-tuple-element.168), channel_id=1, source_target_pairs={{0,1},{1,2},{2,3},{3,0},{4,5},{5,6},{6,7},{7,4},{8,9},{9,10},{10,1... | collective-permute-start | bytes 49160 | tf_op jit(solution)/shard_map/ppermute | solution.py:487
  95.4 1.4 %collective-permute-done.32.refs_2_ = bf16[16,512]{1,0:T(8,128)(2,1)S(1)} collective-permute-done((bf16[16,512]{1,0:T(8,128)(2,1)S(1)}, bf16[16,512]{1,0:T(8,128)(2,1)S(1)}, u32[]{:S(2)}, u32[]{:S(2)}) %collective-permute-start.32) | collective-permute-done | bytes 16416 | tf_op jit(solution)/shard_map/ppermute | solution.py:487
  (68 shorter events, 28.1 us)
Async XLA Ops:
  3.1 10.8 %collective-permute-start = (bf16[16,3584]{1,0:T(8,128)(2,1)S(1)}, bf16[16,3584]{1,0:T(8,128)(2,1)S(1)}, u32[]{:S(2)}, u32[]{:S(2)}) collective-permute-start(bf16[16,3584]{1,0:T(8,128)(2,1)S(1)} %get-tuple-element.102), channel_id=1, source_target_pairs={{0,1},{1,2},{2,3},{3,0},{4,5},{5,6},{6,7},{7,4},{8,9},{9,10},{10,1... | collective-permute-start | bytes 344072 | tf_op jit(solution)/shard_map/ppermute | solution.py:487
  6.2 10.2 %collective-permute-start.1 = (bf16[16,3584]{1,0:T(8,128)(2,1)S(1)}, bf16[16,3584]{1,0:T(8,128)(2,1)S(1)}, u32[]{:S(2)}, u32[]{:S(2)}) collective-permute-start(bf16[16,3584]{1,0:T(8,128)(2,1)S(1)} %get-tuple-element.103), channel_id=1, source_target_pairs={{0,2},{1,3},{2,0},{3,1},{4,6},{5,7},{6,4},{7,5},{8,10},{9,11},{10,... | collective-permute-start | bytes 344072 | tf_op jit(solution)/shard_map/ppermute | solution.py:487
  8.8 7.6 %collective-permute-start.2 = (bf16[16,3584]{1,0:T(8,128)(2,1)S(1)}, bf16[16,3584]{1,0:T(8,128)(2,1)S(1)}, u32[]{:S(2)}, u32[]{:S(2)}) collective-permute-start(bf16[16,3584]{1,0:T(8,128)(2,1)S(1)} %get-tuple-element.104), channel_id=1, source_target_pairs={{0,3},{1,0},{2,1},{3,2},{4,7},{5,4},{6,5},{7,6},{8,11},{9,8},{10,9... | collective-permute-start | bytes 344072 | tf_op jit(solution)/shard_map/ppermute | solution.py:487
  16.6 8.1 %collective-permute-start.6 = (bf16[32,3072]{1,0:T(8,128)(2,1)S(1)}, bf16[32,3072]{1,0:T(8,128)(2,1)S(1)}, u32[]{:S(2)}, u32[]{:S(2)}) collective-permute-start(bf16[32,3072]{1,0:T(8,128)(2,1)S(1)} %get-tuple-element.109), channel_id=1, source_target_pairs={{0,1},{1,0},{2,3},{3,2},{4,5},{5,4},{6,7},{7,6},{8,9},{9,8},{10,11... | collective-permute-start | bytes 589832 | tf_op jit(solution)/shard_map/ppermute | solution.py:231
  19.6 10.9 %collective-permute-start.5 = (bf16[48,3072]{1,0:T(8,128)(2,1)S(1)}, bf16[48,3072]{1,0:T(8,128)(2,1)S(1)}, u32[]{:S(2)}, u32[]{:S(2)}) collective-permute-start(bf16[48,3072]{1,0:T(8,128)(2,1)S(1)} %get-tuple-element.107.refs_9_.refs_14_), channel_id=1, source_target_pairs={{0,24},{4,28},{8,16},{12,20},{16,8},{20,12},{24,0},{28,4},{1,25},{... | collective-permute-start | bytes 884744 | tf_op jit(solution)/shard_map/ppermute | solution.py:187
  22.1 13.4 %collective-permute-start.4 = (bf16[48,3072]{1,0:T(8,128)(2,1)S(1)}, bf16[48,3072]{1,0:T(8,128)(2,1)S(1)}, u32[]{:S(2)}, u32[]{:S(2)}) collective-permute-start(bf16[48,3072]{1,0:T(8,128)(2,1)S(1)} %get-tuple-element.107.refs_9_.refs_14_), channel_id=1, source_target_pairs={{0,16},{4,20},{8,24},{12,28},{16,0},{20,4},{24,8},{28,12},{1,17},{... | collective-permute-start | bytes 884744 | tf_op jit(solution)/shard_map/ppermute | solution.py:187
  22.6 14.1 %collective-permute-start.3 = (bf16[48,3584]{1,0:T(8,128)(2,1)S(1)}, bf16[48,3584]{1,0:T(8,128)(2,1)S(1)}, u32[]{:S(2)}, u32[]{:S(2)}) collective-permute-start(bf16[48,3584]{1,0:T(8,128)(2,1)S(1)} %get-tuple-element.110), channel_id=1, source_target_pairs={{0,8},{4,12},{8,0},{12,4},{16,24},{20,28},{24,16},{28,20},{1,9},{5... | collective-permute-start | bytes 1032200 | tf_op jit(solution)/shard_map/ppermute | solution.py:187
  24.7 12.0 %collective-permute-start.7 = (bf16[64,1536]{1,0:T(8,128)(2,1)S(1)}, bf16[64,1536]{1,0:T(8,128)(2,1)S(1)}, u32[]{:S(2)}, u32[]{:S(2)}) collective-permute-start(bf16[64,1536]{1,0:T(8,128)(2,1)S(1)} %pad_maximum_fusion.3), channel_id=1, source_target_pairs={{0,2},{1,3},{2,0},{3,1},{4,6},{5,7},{6,4},{7,5},{8,10},{9,11},{10,... | collective-permute-start | bytes 589832 | tf_op jit(solution)/shard_map/ppermute | solution.py:237
  37.4 12.6 %collective-permute-start.19 = (bf16[64,1536]{1,0:T(8,128)(2,1)S(1)}, bf16[64,1536]{1,0:T(8,128)(2,1)S(1)}, u32[]{:S(2)}, u32[]{:S(2)}) collective-permute-start(bf16[64,1536]{1,0:T(8,128)(2,1)S(1)} %pad_maximum_fusion.4), channel_id=1, source_target_pairs={{0,2},{1,3},{2,0},{3,1},{4,6},{5,7},{6,4},{7,5},{8,10},{9,11},{10,... | collective-permute-start | bytes 589832 | tf_op jit(solution)/shard_map/ppermute | solution.py:239
  43.7 10.9 %collective-permute-start.17 = (bf16[96,1536]{1,0:T(8,128)(2,1)S(1)}, bf16[96,1536]{1,0:T(8,128)(2,1)S(1)}, u32[]{:S(2)}, u32[]{:S(2)}) collective-permute-start(bf16[96,1536]{1,0:T(8,128)(2,1)S(1)} %pad_maximum_fusion.1), channel_id=1, source_target_pairs={{0,8},{4,12},{8,0},{12,4},{16,24},{20,28},{24,16},{28,20},{1,9},{5... | collective-permute-start | bytes 884744 | tf_op jit(solution)/shard_map/ppermute | solution.py:187
  45.2 5.5 %collective-permute-start.11 = (bf16[16,512]{1,0:T(8,128)(2,1)S(1)}, bf16[16,512]{1,0:T(8,128)(2,1)S(1)}, u32[]{:S(2)}, u32[]{:S(2)}) collective-permute-start(bf16[16,512]{1,0:T(8,128)(2,1)S(1)} %get-tuple-element.120), channel_id=1, source_target_pairs={{0,1},{1,2},{2,3},{3,0},{4,5},{5,6},{6,7},{7,4},{8,9},{9,10},{10,1... | collective-permute-start | bytes 49160 | tf_op jit(solution)/shard_map/ppermute | solution.py:487
  45.5 5.2 %collective-permute-start.12 = (bf16[16,512]{1,0:T(8,128)(2,1)S(1)}, bf16[16,512]{1,0:T(8,128)(2,1)S(1)}, u32[]{:S(2)}, u32[]{:S(2)}) collective-permute-start(bf16[16,512]{1,0:T(8,128)(2,1)S(1)} %get-tuple-element.121), channel_id=1, source_target_pairs={{0,2},{1,3},{2,0},{3,1},{4,6},{5,7},{6,4},{7,5},{8,10},{9,11},{10,... | collective-permute-start | bytes 49160 | tf_op jit(solution)/shard_map/ppermute | solution.py:487
  46.4 4.9 %collective-permute-start.13 = (bf16[16,512]{1,0:T(8,128)(2,1)S(1)}, bf16[16,512]{1,0:T(8,128)(2,1)S(1)}, u32[]{:S(2)}, u32[]{:S(2)}) collective-permute-start(bf16[16,512]{1,0:T(8,128)(2,1)S(1)} %get-tuple-element.122), channel_id=1, source_target_pairs={{0,3},{1,0},{2,1},{3,2},{4,7},{5,4},{6,5},{7,6},{8,11},{9,8},{10,9... | collective-permute-start | bytes 49160 | tf_op jit(solution)/shard_map/ppermute | solution.py:487
  51.6 3.8 %collective-permute-start.15 = (bf16[16,512]{1,0:T(8,128)(2,1)S(1)}, bf16[16,512]{1,0:T(8,128)(2,1)S(1)}, u32[]{:S(2)}, u32[]{:S(2)}) collective-permute-start(bf16[16,512]{1,0:T(8,128)(2,1)S(1)} %get-tuple-element.125), channel_id=1, source_target_pairs={{0,8},{4,12},{8,0},{12,4},{1,9},{5,13},{9,1},{13,5},{2,10},{6,14},... | collective-permute-start | bytes 49160 | tf_op jit(solution)/shard_map/ppermute | solution.py:493
  53.5 9.3 %collective-permute-start.20 = (bf16[96,1536]{1,0:T(8,128)(2,1)S(1)}, bf16[96,1536]{1,0:T(8,128)(2,1)S(1)}, u32[]{:S(2)}, u32[]{:S(2)}) collective-permute-start(bf16[96,1536]{1,0:T(8,128)(2,1)S(1)} %pad_maximum_fusion.2), channel_id=1, source_target_pairs={{0,16},{4,20},{8,24},{12,28},{16,0},{20,4},{24,8},{28,12},{1,17},{... | collective-permute-start | bytes 884744 | tf_op jit(solution)/shard_map/ppermute | solution.py:187
  54.6 8.3 %collective-permute-start.18 = (bf16[192,1536]{1,0:T(8,128)(2,1)S(1)}, bf16[192,1536]{1,0:T(8,128)(2,1)S(1)}, u32[]{:S(2)}, u32[]{:S(2)}) collective-permute-start(bf16[192,1536]{1,0:T(8,128)(2,1)S(1)} %constant_dynamic-update-slice_fusion.refs_9_), channel_id=1, source_target_pairs={{0,4},{4,0},{8,12},{12,8},{16,20},{20,16},{24,28},{28,24},{1,5},{5... | collective-permute-start | bytes 1769480 | tf_op jit(solution)/shard_map/ppermute | solution.py:187
  70.5 3.8 %collective-permute-start.23 = (bf16[16,512]{1,0:T(8,128)(2,1)S(1)}, bf16[16,512]{1,0:T(8,128)(2,1)S(1)}, u32[]{:S(2)}, u32[]{:S(2)}) collective-permute-start(bf16[16,512]{1,0:T(8,128)(2,1)S(1)} %get-tuple-element.145), channel_id=1, source_target_pairs={{0,8},{4,12},{8,0},{12,4},{1,9},{5,13},{9,1},{13,5},{2,10},{6,14},... | collective-permute-start | bytes 49160 | tf_op jit(solution)/shard_map/ppermute | solution.py:493
  74.8 4.5 %collective-permute-start.25 = (bf16[16,512]{1,0:T(8,128)(2,1)S(1)}, bf16[16,512]{1,0:T(8,128)(2,1)S(1)}, u32[]{:S(2)}, u32[]{:S(2)}) collective-permute-start(bf16[16,512]{1,0:T(8,128)(2,1)S(1)} %get-tuple-element.148), channel_id=1, source_target_pairs={{0,3},{1,0},{2,1},{3,2},{4,7},{5,4},{6,5},{7,6},{8,11},{9,8},{10,9... | collective-permute-start | bytes 49160 | tf_op jit(solution)/shard_map/ppermute | solution.py:487
  77.9 4.6 %collective-permute-start.26 = (bf16[16,512]{1,0:T(8,128)(2,1)S(1)}, bf16[16,512]{1,0:T(8,128)(2,1)S(1)}, u32[]{:S(2)}, u32[]{:S(2)}) collective-permute-start(bf16[16,512]{1,0:T(8,128)(2,1)S(1)} %get-tuple-element.149), channel_id=1, source_target_pairs={{0,2},{1,3},{2,0},{3,1},{4,6},{5,7},{6,4},{7,5},{8,10},{9,11},{10,... | collective-permute-start | bytes 49160 | tf_op jit(solution)/shard_map/ppermute | solution.py:487
  78.1 5.5 %collective-permute-start.27 = (bf16[16,512]{1,0:T(8,128)(2,1)S(1)}, bf16[16,512]{1,0:T(8,128)(2,1)S(1)}, u32[]{:S(2)}, u32[]{:S(2)}) collective-permute-start(bf16[16,512]{1,0:T(8,128)(2,1)S(1)} %get-tuple-element.150), channel_id=1, source_target_pairs={{0,1},{1,2},{2,3},{3,0},{4,5},{5,6},{6,7},{7,4},{8,9},{9,10},{10,1... | collective-permute-start | bytes 49160 | tf_op jit(solution)/shard_map/ppermute | solution.py:487
  86.9 3.8 %collective-permute-start.29 = (bf16[16,512]{1,0:T(8,128)(2,1)S(1)}, bf16[16,512]{1,0:T(8,128)(2,1)S(1)}, u32[]{:S(2)}, u32[]{:S(2)}) collective-permute-start(bf16[16,512]{1,0:T(8,128)(2,1)S(1)} %get-tuple-element.163), channel_id=1, source_target_pairs={{0,8},{4,12},{8,0},{12,4},{1,9},{5,13},{9,1},{13,5},{2,10},{6,14},... | collective-permute-start | bytes 49160 | tf_op jit(solution)/shard_map/ppermute | solution.py:493
  91.6 3.8 %collective-permute-start.31 = (bf16[16,512]{1,0:T(8,128)(2,1)S(1)}, bf16[16,512]{1,0:T(8,128)(2,1)S(1)}, u32[]{:S(2)}, u32[]{:S(2)}) collective-permute-start(bf16[16,512]{1,0:T(8,128)(2,1)S(1)} %get-tuple-element.166), channel_id=1, source_target_pairs={{0,3},{1,0},{2,1},{3,2},{4,7},{5,4},{6,5},{7,6},{8,11},{9,8},{10,9... | collective-permute-start | bytes 49160 | tf_op jit(solution)/shard_map/ppermute | solution.py:487
  92.0 4.8 %collective-permute-start.32 = (bf16[16,512]{1,0:T(8,128)(2,1)S(1)}, bf16[16,512]{1,0:T(8,128)(2,1)S(1)}, u32[]{:S(2)}, u32[]{:S(2)}) collective-permute-start(bf16[16,512]{1,0:T(8,128)(2,1)S(1)} %get-tuple-element.167), channel_id=1, source_target_pairs={{0,2},{1,3},{2,0},{3,1},{4,6},{5,7},{6,4},{7,5},{8,10},{9,11},{10,... | collective-permute-start | bytes 49160 | tf_op jit(solution)/shard_map/ppermute | solution.py:487
  92.7 5.5 %collective-permute-start.33 = (bf16[16,512]{1,0:T(8,128)(2,1)S(1)}, bf16[16,512]{1,0:T(8,128)(2,1)S(1)}, u32[]{:S(2)}, u32[]{:S(2)}) collective-permute-start(bf16[16,512]{1,0:T(8,128)(2,1)S(1)} %get-tuple-element.168), channel_id=1, source_target_pairs={{0,1},{1,2},{2,3},{3,0},{4,5},{5,6},{6,7},{7,4},{8,9},{9,10},{10,1... | collective-permute-start | bytes 49160 | tf_op jit(solution)/shard_map/ppermute | solution.py:487
  (10 other events, 26.7 us)

commit v13 on v7

--- a/solution.py
+++ b/solution.py
@@ -121,31 +121,32 @@
     return dot_trans(select, first).astype(BF16)
 
 
-def prepare_kernel(grid, send, shards, proc_piece, table_out, kept, *messages):
-    plane = lax.axis_index("groups") * lax.axis_size("graph") + lax.axis_index("graph")
+def prepare_kernel(grid, send, shards, table_out, kept, *messages):
     width = 3 * FEATURES
-    rows = proc_piece.ref.shape[0]
-    base = plane * rows
-    for i in range(4):
-        one, two = shards[2 * i](), shards[2 * i + 1]()
-        hidden = one.shape[1]
-        select = jnp.where(
-            lax.broadcasted_iota(jnp.int32, (rows, hidden), 0) + base
-            == lax.broadcasted_iota(jnp.int32, (rows, hidden), 1),
-            1.0,
-            0.0,
-        ).astype(BF16)
-        low = i % 2 * width
-        first = turned(one[...], select)
-        second = two[pl.ds(pl.multiple_of(base, rows), rows), :]
-        for out in (proc_piece,) if i // 2 else messages:
-            out.ref[:, low : low + 2 * FEATURES] = first
-            out.ref[:, low + 2 * FEATURES : low + width] = second
     outgoing = send_rows(grid, send, table_out)
     size = kept.ref.shape[0]
     kept.ref[...] = outgoing[:size, :].astype(BF16)
     for i, out in enumerate(messages):
         out.ref[:, 2 * width :] = outgoing[(i + 1) * size : (i + 2) * size, :].astype(BF16)
+    for i in range(2):
+        first, second = piece_of(shards[2 * i], shards[2 * i + 1], messages[0].ref.shape[0])
+        low = i * width
+        for out in messages:
+            out.ref[:, low : low + 2 * FEATURES] = first
+            out.ref[:, low + 2 * FEATURES : low + width] = second
+
+
+def piece_of(one, two, rows):
+    plane = lax.axis_index("groups") * lax.axis_size("graph") + lax.axis_index("graph")
+    base = plane * rows
+    hidden = two().shape[0]
+    select = jnp.where(
+        lax.broadcasted_iota(jnp.int32, (rows, hidden), 0) + base
+        == lax.broadcasted_iota(jnp.int32, (rows, hidden), 1),
+        1.0,
+        0.0,
+    ).astype(BF16)
+    return turned(one()[...], select), two()[pl.ds(pl.multiple_of(base, rows), rows), :]
 
 
 def join_kernel(kept, messages, near, block, both):
@@ -164,7 +165,7 @@
             both.ref[(j - 1) * size : j * size, width:] = moved
 
 
-def own_kernel(shards, *outs):
+def own_kernel(shards, enc_own, proc_own, proc_piece):
     width = 3 * FEATURES
     for i in range(4):
         one, two = shards[2 * i](), shards[2 * i + 1]()
@@ -175,9 +176,14 @@
             1.0,
             0.0,
         ).astype(BF16)
-        out, low = outs[i // 2], i % 2 * width
+        out, low = (enc_own, proc_own)[i // 2], i % 2 * width
         out.ref[:, low : low + 2 * FEATURES] = turned(one[...], select)
         out.ref[:, low + 2 * FEATURES : low + width] = two[...]
+    for i in (2, 3):
+        first, second = piece_of(shards[2 * i], shards[2 * i + 1], proc_piece.ref.shape[0])
+        low = i % 2 * width
+        proc_piece.ref[:, low : low + 2 * FEATURES] = first
+        proc_piece.ref[:, low + 2 * FEATURES : low + width] = second
 
 
 def across(x, flip):
@@ -200,18 +206,20 @@
             rows.append(lax.all_gather(shards[2 * i + 1], "mp", axis=0, tiled=True))
         enc, proc = jnp.concatenate(rows[:4], axis=1), jnp.concatenate(rows[4:], axis=1)
         arrived = exchange(outgoing, step)
-        return [enc], lambda moved: [proc], arrived, grid_t, tables
+        return [enc], lambda after: [proc], arrived, grid_t, tables
     far = [Far(s) for s in shards]
     piece = hidden // planes
     width = 6 * features
-    proc_piece, grid_t, kept, *messages = call(
+    grid_t, kept, *messages = call(
         prepare_kernel,
-        [shape(piece, width, BF16)] + sent[:2] + [shape(piece, width + features, BF16)] * 3,
+        sent[:2] + [shape(piece, width + features, BF16)] * 3,
         Far(grid_lat),
         Far(grid_send.T),
-        far,
-    )
-    enc_own, proc_own = call(own_kernel, [shape(hidden, width, BF16)] * 2, far)
+        far[:4],
+    )
+    enc_own, proc_own, proc_piece = call(
+        own_kernel, [shape(hidden, width, BF16)] * 2 + [shape(piece, width, BF16)], far
+    )
     messages = [along(m, i + 1) for i, m in enumerate(messages)]
     kept, enc_own, *tables = lax.optimization_barrier((kept, enc_own, *tables))
     rows = mp * step
@@ -221,31 +229,33 @@
         kept,
         messages,
     )
-    x, y, corner, core = across(both, 2), across(first, 4), across(first, 6), across(both, 1)
-    proc_piece, _ = lax.optimization_barrier((proc_piece, core))
-    x_core = across(x, 1)
-    enc = [enc_own, first, core, x, y, corner, x_core, across(y, 1), across(corner, 1)]
-    arrived = [near, core, x, x_core]
+    x, y, corner = across(both, 2), across(first, 4), across(first, 6)
+    proc_piece, _ = lax.optimization_barrier((proc_piece, near))
     beside_me = lax.ppermute(proc_piece, "mp", [(m, m ^ 1) for m in range(mp)])
     pair = jnp.concatenate([proc_piece, beside_me])
-    others = lax.ppermute(pair, "mp", [(m, m ^ 2) for m in range(mp)])
-    proc_first = jnp.concatenate([beside_me, others])
+    pairs = lax.ppermute(pair, "mp", [(m, m ^ 2) for m in range(mp)])
+    proc_first = jnp.concatenate([beside_me, pairs])
+    both, x, y, corner, _ = lax.optimization_barrier((both, x, y, corner, pairs))
+    core, x_core, others = across(both, 1), across(x, 1), across(jnp.concatenate([y, corner]), 1)
+    enc = [enc_own, first, core, x, y, corner, x_core, others]
+    arrived = [near, core, x, x_core]
     proc_first, *_ = lax.optimization_barrier((proc_first, x, y, corner))
     plane = [across(proc_first, flip) for flip in (2, 4, 6)]
     proc = [proc_own, proc_first, across(proc_first, 1)] + plane
 
-    def finish(moved):
-        tied, *_ = lax.optimization_barrier((jnp.concatenate(plane), *moved))
-        return proc + [across(tied, 1)]
+    def finish(after):
+        tied = [lax.optimization_barrier((block, *after))[0] for block in plane]
+        return proc + [across(jnp.concatenate(tied), 1)]
 
     return enc, finish, arrived, grid_t, tables
 
 
 def forward(inputs, first, second):
     before = dot_trans(inputs, first)
-    logistic = jax.nn.sigmoid(before)
-    hidden = (before * logistic).astype(BF16)
-    slope = logistic * (1.0 + before * (1.0 - logistic))
+    logistic = 0.5 + 0.5 * jnp.tanh(0.5 * before)
+    wide = before * logistic
+    hidden = wide.astype(BF16)
+    slope = logistic + wide * (1.0 - logistic)
     summed = dot(hidden, second)
     centered = summed - jnp.mean(summed, axis=-1, keepdims=True)
     rescale = lax.rsqrt(jnp.mean(centered * centered, axis=-1, keepdims=True) + 1e-05)
@@ -391,9 +401,10 @@
 
 
 def process_kernel(
-    cotangent_in, one_in, halo, sender_g, proc_g, weights, proc_t, sender_t, two, grad_one, *refs
+    cotangent_in, one_in, halo, sender_g, proc_g, weights, proc_t, sender_t, two, part, ga, *refs
 ):
-    grad_halo, (slope_p, normed_p, scale_p, ga_p) = refs[:-4], refs[-4:]
+    grad_halo, (slope_p, normed_p, scale_p) = refs[:-3], refs[-3:]
+    ga_p = ga.ref
     features = FEATURES
     one = one_in()[...]
     mesh_rows = one.shape[0]
@@ -415,8 +426,7 @@
     )
     two.send((one.astype(F32) + normed).astype(BF16))
     cotangent = cotangent_in()[...].astype(F32)
-    ga = backward_hidden(cotangent, slope, rounded, rescale, second_n)
-    g_q = dot(ga, first_n)
+    g_q = dot(backward_hidden(cotangent, slope, rounded, rescale, second_n), first_n)
     g_msg = g_q[:, features:].astype(BF16)
     for low in range(0, edges, ROWS):
         rows = pl.ds(low, ROWS)
@@ -427,22 +437,27 @@
     by_send = dot(sender_t()[...], ga_p[...]).astype(BF16)
     g_send = dot(by_send, first[:, :features])
     split(g_send[mesh_rows:, :], grad_halo)
-    by_recv = dot(proc_t()[...], ga_p[...]).astype(BF16)
-    g_recv = dot(by_recv, first[:, features:])
-    grad_one.ref[...] = cotangent + g_q[:, :features] + g_recv + g_send[:mesh_rows, :]
+    part.ref[...] = cotangent + g_q[:, :features] + g_send[:mesh_rows, :]
+
+
+def receive_kernel(part, ga, scatter, weights, out):
+    by_recv = dot(scatter()[...], ga()[...]).astype(BF16)
+    first, _ = layers(weights, 0)
+    out.send(part()[...] + dot(by_recv, first[:, FEATURES:]))
 
 
 def decode_kernel(
     back, halo_t, grad_in, slope_n, normed_n, scale_n, enc_g, slope_e, normed_e, scale_e,
-    weights, slot_t, enc_t, mesh_grad, *refs
+    weights, slot_t, part, ga, *grad_slots
 ):
-    grad_slots, ga_e = refs[:-1], refs[-1]
+    ga_e = ga.ref
     features = FEATURES
     edges = enc_g().shape[0]
     grad_one = grad_in()[...] + dot(halo_t()[...], stacked(back))
     first_n, second_n = layers(weights, 1)
-    ga = backward_hidden(grad_one, slope_n()[...], normed_n()[...], scale_n()[:, 0:1], second_n)
-    g_n = dot(ga, first_n)
+    ga_n = backward_hidden(grad_one, slope_n()[...], normed_n()[...], scale_n()[:, 0:1], second_n)
+    g_n = dot(ga_n, first_n)
+    part.ref[...] = grad_one + g_n[:, :features]
     g_edge = g_n[:, features:].astype(BF16)
     first, second = layers(weights, 0)
     for low in range(0, edges, ROWS):
@@ -451,8 +466,6 @@
         ga_e[rows, :] = backward_hidden(
             incoming, slope_e()[rows, :], normed_e()[rows, :], scale_e()[rows, 0:1], second
         )
-    by_recv = dot(enc_t()[...], ga_e[...]).astype(BF16)
-    mesh_grad.send(grad_one + g_n[:, :features] + dot(by_recv, first[:, features:]))
     by_slot = dot(slot_t()[...], ga_e[...]).astype(BF16)
     split(dot(by_slot, first[:, :features]), grad_slots)
 
@@ -493,7 +506,7 @@
 
 def exchange_back(blocks, step):
     blocks = turn([beside(b, t) for t, b in enumerate(blocks)], lax.axis_size("mp"), step)
-    return [along(b, -s) for s, b in enumerate(blocks)]
+    return [along(b, -s) for s, b in enumerate(blocks)], blocks[0]
 
 
 def local(
@@ -559,12 +572,15 @@
         halo_g,
         flops=3 * 10**9,
     )
-    moved = first_level(halo_out, halo_step)
-    proc = finish(moved)
-    halo_in = second_level(moved)
-    mesh_two, grad_one, *grad_halo = call(
+    halo_in = second_level(first_level(halo_out, halo_step))
+    proc = finish(halo_in[1:])
+    mesh_two, part, ga, *grad_halo = call(
         process_kernel,
-        [shape(mesh_rows, features, BF16), shape(mesh_rows, features, F32)]
+        [
+            shape(mesh_rows, features, BF16),
+            shape(mesh_rows, features, F32),
+            shape(mesh_edges, features, BF16),
+        ]
         + [shape(mp * halo_step, features, BF16)] * graph,
         Far(cotangent),
         mesh_one,
@@ -580,13 +596,17 @@
             pltpu.VMEM((mesh_edges, features), BF16),
             pltpu.VMEM((mesh_edges, features), BF16),
             pltpu.VMEM((mesh_edges, LANES), F32),
-            pltpu.VMEM((mesh_edges, features), BF16),
         ],
     )
-    halo_back = exchange_back(grad_halo, halo_step)
-    mesh_grad, *grad_slots = call(
+    halo_back, half_way = exchange_back(grad_halo, halo_step)
+    part, _ = lax.optimization_barrier((part, half_way))
+    (grad_one,) = call(
+        receive_kernel, [shape(mesh_rows, features, F32)], part, ga, proc_t, proc, flops=3 * 10**8
+    )
+    part, ga, *grad_slots = call(
         decode_kernel,
-        [shape(mesh_rows, features, F32)] + [shape(mp * step, features, BF16)] * graph,
+        [shape(mesh_rows, features, F32), shape(edges, features, BF16)]
+        + [shape(mp * step, features, BF16)] * graph,
         halo_back,
         halo_t,
         grad_one,
@@ -599,12 +619,13 @@
         scale_e,
         enc,
         slot_t,
-        enc_t,
-        last=(0,),
         flops=3 * 10**9,
-        scratch=[pltpu.VMEM((edges, features), BF16)],
-    )
-    returned = exchange_back(grad_slots, step)
+    )
+    returned, half_way = exchange_back(grad_slots, step)
+    part, _ = lax.optimization_barrier((part, half_way))
+    (mesh_grad,) = call(
+        receive_kernel, [shape(mesh_rows, features, F32)], part, ga, enc_t, enc, last=(0,), flops=3 * 10**8
+    )
     (grid_grad,) = call(
         grid_kernel, [shape(grid_rows, features, F32)], returned, grid_t, last=(0,)
     )

time: 94.8 us -> 93.7 us (0.988)
  starting transfers between devices: 33.8 us -> 32.5 us
    ppermute x1, waiting for transfers between devices: 0.01 us -> 9.26 us  [start(): pairs = lax.ppermute(pair, 'mp', [(m, m ^ 2) for m in range(mp)])]
    ppermute x12 -> x11, waiting for transfers between devices: 13.8 us -> 4.95 us  [across(): lax.ppermute(x, ('groups', 'graph'), [(p, p ^ flip) for p in range(planes)])]
    ppermute x12, starting transfers between devices: 15.3 us -> 13.8 us  [along(): lax.ppermute(block, 'mp', [(m, (m + shift) % size) for m in range(size)])]
    pallas_call x11 -> x13, Pallas kernels: 20.3 us -> 20.7 us  [call(): pl.pallas_call(body, out_shape=out_shape, in_specs=[hbm if away else vmem...]
    ppermute x12 -> x11, starting transfers between devices: 8.19 us -> 8.26 us  [across(): lax.ppermute(x, ('groups', 'graph'), [(p, p ^ flip) for p in range(planes)])]
  transfers between devices with their start and end apart: 35 -> 34, of which waited for: 18 -> 18; matrix products, arithmetic and copies ran while one was open for 0% -> 0% of each run, Pallas kernels for 8% -> 10%
where the time goes in v13:
time: 93.7 us; the launch traced here: 93.5 us
  waiting for transfers between devices  39.2 us (42%)
  starting transfers between devices  32.5 us (35%)
  Pallas kernels  20.7 us (22%)
  between operations  0.98 us (1%)
    pallas_call x13, Pallas kernels, call(): pl.pallas_call(body, out_shape=out_shape, in_specs=[hbm if away else vmem...  20.7 us
    ppermute x12, waiting for transfers between devices, along(): lax.ppermute(block, 'mp', [(m, (m + shift) % size) for m in range(size)])  17.2 us
    ppermute x12, starting transfers between devices, along(): lax.ppermute(block, 'mp', [(m, (m + shift) % size) for m in range(size)])  13.8 us
    ppermute x1, waiting for transfers between devices, start(): pairs = lax.ppermute(pair, 'mp', [(m, m ^ 2) for m in range(mp)])  9.26 us
    ppermute x11, starting transfers between devices, across(): lax.ppermute(x, ('groups', 'graph'), [(p, p ^ flip) for p in range(planes)])  8.26 us
    ppermute x9, waiting for transfers between devices, beside(): lax.ppermute(block, 'graph', [(g, g ^ flip) for g in range(lax.axis_size(...  7.72 us
    ppermute x9, starting transfers between devices, beside(): lax.ppermute(block, 'graph', [(g, g ^ flip) for g in range(lax.axis_size(...  5.79 us
    ppermute x11, waiting for transfers between devices, across(): lax.ppermute(x, ('groups', 'graph'), [(p, p ^ flip) for p in range(planes)])  4.95 us
  transfers between devices with their start and end apart: 34, of which 18 were waited for; matrix products, arithmetic and copies ran while one was open for 0% of the time, Pallas kernels for 10%

profile of v13, /device:TPU:0, one launch (start us, length us, event | category | flops | bytes accessed | tf_op | source)
XLA Modules:
  0.0 93.5 jit_solution(17714705187725197086)
XLA Ops:
  0.6 1.7 %prepare_kernel.1 = (bf16[512,64]{1,0:T(8,128)(2,1)S(1)}, bf16[16,512]{1,0:T(8,128)(2,1)S(1)}, bf16[16,3584]{1,0:T(8,128)(2,1)S(1)}, bf16[16,3584]{1,0:T(8,128)(2,1)S(1)}, bf16[16,3584]{1,0:T(8,128)(2,1)S(1)}) custom-call(bf16[512,512]{1,0:T(8,128)(2,1)} %refs_0_.4, s32[4,16]{1,0:T(4,128)} %bitcast.6, bf16[1024,128]{1,0:T(8,128)(2,1)} %refs_0_.5, ...), custom_call_target="tpu_custom_call" | custom-call | bytes 1310976 | tf_op jit(solution)/shard_map/prepare_kernel/pallas_call | solution.py:96
  2.4 3.1 %collective-permute-start = (bf16[16,3584]{1,0:T(8,128)(2,1)S(1)}, bf16[16,3584]{1,0:T(8,128)(2,1)S(1)}, u32[]{:S(2)}, u32[]{:S(2)}) collective-permute-start(bf16[16,3584]{1,0:T(8,128)(2,1)S(1)} %get-tuple-element.100), channel_id=1, source_target_pairs={{0,1},{1,2},{2,3},{3,0},{4,5},{5,6},{6,7},{7,4},{8,9},{9,10},{10,1... | collective-permute-start | bytes 344072 | tf_op jit(solution)/shard_map/ppermute | solution.py:481
  5.5 2.6 %collective-permute-start.1 = (bf16[16,3584]{1,0:T(8,128)(2,1)S(1)}, bf16[16,3584]{1,0:T(8,128)(2,1)S(1)}, u32[]{:S(2)}, u32[]{:S(2)}) collective-permute-start(bf16[16,3584]{1,0:T(8,128)(2,1)S(1)} %get-tuple-element.101), channel_id=1, source_target_pairs={{0,2},{1,3},{2,0},{3,1},{4,6},{5,7},{6,4},{7,5},{8,10},{9,11},{10,... | collective-permute-start | bytes 344072 | tf_op jit(solution)/shard_map/ppermute | solution.py:481
  9.4 2.1 %own_kernel.1 = (bf16[128,3072]{1,0:T(8,128)(2,1)S(1)}, bf16[128,3072]{1,0:T(8,128)(2,1)S(1)}, bf16[16,3072]{1,0:T(8,128)(2,1)S(1)}) custom-call(bf16[1024,128]{1,0:T(8,128)(2,1)} %refs_0_.5, bf16[128,512]{1,0:T(8,128)(2,1)} %refs_1_.1, bf16[1024,128]{1,0:T(8,128)(2,1)} %refs_2_.3, bf16[128,512]{1,0:T(8,128)(2,1)} %refs_3_.3, bf16[1024,128]{1,0:T(8,128)(2,1)} %refs_4_.3, ...), custom_call_target="tpu_custom_call" | custom-call | bytes 1572864 | tf_op jit(solution)/shard_map/own_kernel/pallas_call | solution.py:96
  11.5 1.7 %tables_kernel.1 = (bf16[64,512]{1,0:T(8,128)(2,1)S(1)}, bf16[512,64]{1,0:T(8,128)(2,1)S(1)}, bf16[256,512]{1,0:T(8,128)(2,1)S(1)}, bf16[512,256]{1,0:T(8,128)(2...) custom-call(bf16[256,512]{1,0:T(8,128)(2,1)} %refs_7_.3, ...), custom_call_target="tpu_custom_call" | custom-call | bytes 270464 | tf_op jit(solution)/shard_map/tables_kernel/pallas_call | solution.py:96
  13.3 2.4 %collective-permute-done.1.refs_2_ = bf16[16,3584]{1,0:T(8,128)(2,1)S(1)} collective-permute-done((bf16[16,3584]{1,0:T(8,128)(2,1)S(1)}, bf16[16,3584]{1,0:T(8,128)(2,1)S(1)}, u32[]{:S(2)}, u32[]{:S(2)}) %collective-permute-start.1) | collective-permute-done | bytes 114720 | tf_op jit(solution)/shard_map/ppermute | solution.py:481
  15.8 3.0 %collective-permute-start.6 = (bf16[16,3072]{1,0:T(8,128)(2,1)S(1)}, bf16[16,3072]{1,0:T(8,128)(2,1)S(1)}, u32[]{:S(2)}, u32[]{:S(2)}) collective-permute-start(bf16[16,3072]{1,0:T(8,128)(2,1)S(1)} %get-tuple-element.107), channel_id=1, source_target_pairs={{0,1},{1,0},{2,3},{3,2},{4,5},{5,4},{6,7},{7,6},{8,9},{9,8},{10,11... | collective-permute-start | bytes 294920 | tf_op jit(solution)/shard_map/ppermute | solution.py:234
  18.8 2.5 %collective-permute-start.5 = (bf16[48,3072]{1,0:T(8,128)(2,1)S(1)}, bf16[48,3072]{1,0:T(8,128)(2,1)S(1)}, u32[]{:S(2)}, u32[]{:S(2)}) collective-permute-start(bf16[48,3072]{1,0:T(8,128)(2,1)S(1)} %get-tuple-element.105.refs_9_.refs_14_.refs_4_), channel_id=1, source_target_pairs={{0,24},{4,28},{8,16},{12,20},{16,8},{20,12},{24,0},{28,4},{1,25},{... | collective-permute-start | bytes 884744 | tf_op jit(solution)/shard_map/ppermute | solution.py:191
  22.3 1.7 %collective-permute-start.7 = (bf16[32,3072]{1,0:T(8,128)(2,1)S(1)}, bf16[32,3072]{1,0:T(8,128)(2,1)S(1)}, u32[]{:S(2)}, u32[]{:S(2)}) collective-permute-start(bf16[32,3072]{1,0:T(8,128)(2,1)S(1)} %pad_maximum_fusion.3), channel_id=1, source_target_pairs={{0,2},{1,3},{2,0},{3,1},{4,6},{5,7},{6,4},{7,5},{8,10},{9,11},{10,... | collective-permute-start | bytes 589832 | tf_op jit(solution)/shard_map/ppermute | solution.py:236
  24.0 9.3 %collective-permute-done.7 = bf16[32,3072]{1,0:T(8,128)(2,1)S(1)} collective-permute-done((bf16[32,3072]{1,0:T(8,128)(2,1)S(1)}, bf16[32,3072]{1,0:T(8,128)(2,1)S(1)}, u32[]{:S(2)}, u32[]{:S(2)}) %collective-permute-start.7) | collective-permute-done | bytes 196640 | tf_op jit(solution)/shard_map/ppermute | solution.py:236
  38.1 1.5 %collective-permute-start.19 = (bf16[48,3072]{1,0:T(8,128)(2,1)S(1)}, bf16[48,3072]{1,0:T(8,128)(2,1)S(1)}, u32[]{:S(2)}, u32[]{:S(2)}) collective-permute-start(bf16[48,3072]{1,0:T(8,128)(2,1)S(1)} %pad_maximum_fusion.2.refs_9_.refs_4_), channel_id=1, source_target_pairs={{0,16},{4,20},{8,24},{12,28},{16,0},{20,4},{24,8},{28,12},{1,17},{... | collective-permute-start | bytes 884744 | tf_op jit(solution)/shard_map/ppermute | solution.py:191
  40.2 3.8 %encode_kernel.1 = (bf16[256,512]{1,0:T(8,128)(2,1)S(1)}, bf16[512,512]{1,0:T(8,128)(2,1)S(1)}, bf16[512,512]{1,0:T(8,128)(2,1)S(1)}, f32[512,128]{1,0:T(8,128)S...) custom-call(bf16[512,512]{1,0:T(8,128)(2,1)S(1)} %get-tuple-element., ...), custom_call_target="tpu_custom_call" | custom-call | flops 3000000000 | bytes 5488640 | tf_op jit(solution)/shard_map/encode_kernel/pallas_call | solution.py:96
  45.1 4.5 %collective-permute-done.11.refs_1_ = bf16[16,512]{1,0:T(8,128)(2,1)S(1)} collective-permute-done((bf16[16,512]{1,0:T(8,128)(2,1)S(1)}, bf16[16,512]{1,0:T(8,128)(2,1)S(1)}, u32[]{:S(2)}, u32[]{:S(2)}) %collective-permute-start.11) | collective-permute-done | bytes 16416 | tf_op jit(solution)/shard_map/ppermute | solution.py:481
  49.6 3.7 %collective-permute-done.13.refs_3_ = bf16[16,512]{1,0:T(8,128)(2,1)S(1)} collective-permute-done((bf16[16,512]{1,0:T(8,128)(2,1)S(1)}, bf16[16,512]{1,0:T(8,128)(2,1)S(1)}, u32[]{:S(2)}, u32[]{:S(2)}) %collective-permute-start.13) | collective-permute-done | bytes 16416 | tf_op jit(solution)/shard_map/ppermute | solution.py:481
  53.6 1.6 %collective-permute-start.15 = (bf16[16,512]{1,0:T(8,128)(2,1)S(1)}, bf16[16,512]{1,0:T(8,128)(2,1)S(1)}, u32[]{:S(2)}, u32[]{:S(2)}) collective-permute-start(bf16[16,512]{1,0:T(8,128)(2,1)S(1)} %get-tuple-element.123), channel_id=1, source_target_pairs={{0,8},{4,12},{8,0},{12,4},{1,9},{5,13},{9,1},{13,5},{2,10},{6,14},... | collective-permute-start | bytes 49160 | tf_op jit(solution)/shard_map/ppermute | solution.py:487
  55.5 1.9 %collective-permute-done.15.refs_4_ = bf16[16,512]{1,0:T(8,128)(2,1)S(1)} collective-permute-done((bf16[16,512]{1,0:T(8,128)(2,1)S(1)}, bf16[16,512]{1,0:T(8,128)(2,1)S(1)}, u32[]{:S(2)}, u32[]{:S(2)}) %collective-permute-start.15) | collective-permute-done | bytes 16416 | tf_op jit(solution)/shard_map/ppermute | solution.py:487
  59.0 2.3 %collective-permute-done.17.refs_10_.refs_5_ = bf16[48,3072]{1,0:T(8,128)(2,1)S(1)} collective-permute-done((bf16[48,3072]{1,0:T(8,128)(2,1)S(1)}, bf16[48,3072]{1,0:T(8,128)(2,1)S(1)}, u32[]{:S(2)}, u32[]{:S(2)}) %collective-permute-start.17) | collective-permute-done | bytes 294944 | tf_op jit(solution)/shard_map/ppermute | solution.py:191
  61.3 5.2 %process_kernel.1 = (bf16[256,512]{1,0:T(8,128)(2,1)}, f32[256,512]{1,0:T(8,128)S(1)}, bf16[512,512]{1,0:T(8,128)(2,1)S(1)}, bf16[16,512]{1,0:T(8,128)(2,1)S(1)}...) custom-call(bf16[256,512]{1,0:T(8,128)(2,1)} %refs_0_.7, ...), custom_call_target="tpu_custom_call" | custom-call | flops 5000000000 | bytes 4915200 | tf_op jit(solution)/shard_map/process_kernel/pallas_call | solution.py:96
  68.5 2.1 %collective-permute-done.23.refs_2_ = bf16[16,512]{1,0:T(8,128)(2,1)S(1)} collective-permute-done((bf16[16,512]{1,0:T(8,128)(2,1)S(1)}, bf16[16,512]{1,0:T(8,128)(2,1)S(1)}, u32[]{:S(2)}, u32[]{:S(2)}) %collective-permute-start.23) | collective-permute-done | bytes 16416 | tf_op jit(solution)/shard_map/ppermute | solution.py:487
  70.9 1.9 %collective-permute-start.25 = (bf16[16,512]{1,0:T(8,128)(2,1)S(1)}, bf16[16,512]{1,0:T(8,128)(2,1)S(1)}, u32[]{:S(2)}, u32[]{:S(2)}) collective-permute-start(bf16[16,512]{1,0:T(8,128)(2,1)S(1)} %get-tuple-element.140), channel_id=1, source_target_pairs={{0,3},{1,0},{2,1},{3,2},{4,7},{5,4},{6,5},{7,6},{8,11},{9,8},{10,9... | collective-permute-start | bytes 49160 | tf_op jit(solution)/shard_map/ppermute | solution.py:481
  74.7 2.7 %collective-permute-done.26.refs_2_ = bf16[16,512]{1,0:T(8,128)(2,1)S(1)} collective-permute-done((bf16[16,512]{1,0:T(8,128)(2,1)S(1)}, bf16[16,512]{1,0:T(8,128)(2,1)S(1)}, u32[]{:S(2)}, u32[]{:S(2)}) %collective-permute-start.26) | collective-permute-done | bytes 16416 | tf_op jit(solution)/shard_map/ppermute | solution.py:481
  78.3 2.2 %decode_kernel.1 = (f32[256,512]{1,0:T(8,128)S(1)}, bf16[512,512]{1,0:T(8,128)(2,1)S(1)}, bf16[16,512]{1,0:T(8,128)(2,1)S(1)}, bf16[16,512]{1,0:T(8,128)(2,1)S(1...) custom-call(bf16[16,512]{1,0:T(8,128)(2,1)S(1)} %get-tuple-element.139.refs_0_, ...), custom_call_target="tpu_custom_call" | custom-call | flops 3000000000 | bytes 6209536 | tf_op jit(solution)/shard_map/decode_kernel/pallas_call | solution.py:96
  82.5 1.9 %collective-permute-done.29.refs_2_ = bf16[16,512]{1,0:T(8,128)(2,1)S(1)} collective-permute-done((bf16[16,512]{1,0:T(8,128)(2,1)S(1)}, bf16[16,512]{1,0:T(8,128)(2,1)S(1)}, u32[]{:S(2)}, u32[]{:S(2)}) %collective-permute-start.29) | collective-permute-done | bytes 16416 | tf_op jit(solution)/shard_map/ppermute | solution.py:487
  86.5 1.9 %collective-permute-start.33 = (bf16[16,512]{1,0:T(8,128)(2,1)S(1)}, bf16[16,512]{1,0:T(8,128)(2,1)S(1)}, u32[]{:S(2)}, u32[]{:S(2)}) collective-permute-start(bf16[16,512]{1,0:T(8,128)(2,1)S(1)} %get-tuple-element.162), channel_id=1, source_target_pairs={{0,1},{1,2},{2,3},{3,0},{4,5},{5,6},{6,7},{7,4},{8,9},{9,10},{10,1... | collective-permute-start | bytes 49160 | tf_op jit(solution)/shard_map/ppermute | solution.py:481
  (61 shorter events, 25.0 us)
Async XLA Ops:
  2.4 10.9 %collective-permute-start = (bf16[16,3584]{1,0:T(8,128)(2,1)S(1)}, bf16[16,3584]{1,0:T(8,128)(2,1)S(1)}, u32[]{:S(2)}, u32[]{:S(2)}) collective-permute-start(bf16[16,3584]{1,0:T(8,128)(2,1)S(1)} %get-tuple-element.100), channel_id=1, source_target_pairs={{0,1},{1,2},{2,3},{3,0},{4,5},{5,6},{6,7},{7,4},{8,9},{9,10},{10,1... | collective-permute-start | bytes 344072 | tf_op jit(solution)/shard_map/ppermute | solution.py:481
  5.5 10.2 %collective-permute-start.1 = (bf16[16,3584]{1,0:T(8,128)(2,1)S(1)}, bf16[16,3584]{1,0:T(8,128)(2,1)S(1)}, u32[]{:S(2)}, u32[]{:S(2)}) collective-permute-start(bf16[16,3584]{1,0:T(8,128)(2,1)S(1)} %get-tuple-element.101), channel_id=1, source_target_pairs={{0,2},{1,3},{2,0},{3,1},{4,6},{5,7},{6,4},{7,5},{8,10},{9,11},{10,... | collective-permute-start | bytes 344072 | tf_op jit(solution)/shard_map/ppermute | solution.py:481
  8.0 7.6 %collective-permute-start.2 = (bf16[16,3584]{1,0:T(8,128)(2,1)S(1)}, bf16[16,3584]{1,0:T(8,128)(2,1)S(1)}, u32[]{:S(2)}, u32[]{:S(2)}) collective-permute-start(bf16[16,3584]{1,0:T(8,128)(2,1)S(1)} %get-tuple-element.102), channel_id=1, source_target_pairs={{0,3},{1,0},{2,1},{3,2},{4,7},{5,4},{6,5},{7,6},{8,11},{9,8},{10,9... | collective-permute-start | bytes 344072 | tf_op jit(solution)/shard_map/ppermute | solution.py:481
  15.8 6.5 %collective-permute-start.6 = (bf16[16,3072]{1,0:T(8,128)(2,1)S(1)}, bf16[16,3072]{1,0:T(8,128)(2,1)S(1)}, u32[]{:S(2)}, u32[]{:S(2)}) collective-permute-start(bf16[16,3072]{1,0:T(8,128)(2,1)S(1)} %get-tuple-element.107), channel_id=1, source_target_pairs={{0,1},{1,0},{2,3},{3,2},{4,5},{5,4},{6,7},{7,6},{8,9},{9,8},{10,11... | collective-permute-start | bytes 294920 | tf_op jit(solution)/shard_map/ppermute | solution.py:234
  18.8 14.5 %collective-permute-start.5 = (bf16[48,3072]{1,0:T(8,128)(2,1)S(1)}, bf16[48,3072]{1,0:T(8,128)(2,1)S(1)}, u32[]{:S(2)}, u32[]{:S(2)}) collective-permute-start(bf16[48,3072]{1,0:T(8,128)(2,1)S(1)} %get-tuple-element.105.refs_9_.refs_14_.refs_4_), channel_id=1, source_target_pairs={{0,24},{4,28},{8,16},{12,20},{16,8},{20,12},{24,0},{28,4},{1,25},{... | collective-permute-start | bytes 884744 | tf_op jit(solution)/shard_map/ppermute | solution.py:191
  21.3 13.4 %collective-permute-start.4 = (bf16[48,3072]{1,0:T(8,128)(2,1)S(1)}, bf16[48,3072]{1,0:T(8,128)(2,1)S(1)}, u32[]{:S(2)}, u32[]{:S(2)}) collective-permute-start(bf16[48,3072]{1,0:T(8,128)(2,1)S(1)} %get-tuple-element.105.refs_9_.refs_14_.refs_4_), channel_id=1, source_target_pairs={{0,16},{4,20},{8,24},{12,28},{16,0},{20,4},{24,8},{28,12},{1,17},{... | collective-permute-start | bytes 884744 | tf_op jit(solution)/shard_map/ppermute | solution.py:191
  21.8 14.1 %collective-permute-start.3 = (bf16[48,3584]{1,0:T(8,128)(2,1)S(1)}, bf16[48,3584]{1,0:T(8,128)(2,1)S(1)}, u32[]{:S(2)}, u32[]{:S(2)}) collective-permute-start(bf16[48,3584]{1,0:T(8,128)(2,1)S(1)} %get-tuple-element.108), channel_id=1, source_target_pairs={{0,8},{4,12},{8,0},{12,4},{16,24},{20,28},{24,16},{28,20},{1,9},{5... | collective-permute-start | bytes 1032200 | tf_op jit(solution)/shard_map/ppermute | solution.py:191
  22.3 11.0 %collective-permute-start.7 = (bf16[32,3072]{1,0:T(8,128)(2,1)S(1)}, bf16[32,3072]{1,0:T(8,128)(2,1)S(1)}, u32[]{:S(2)}, u32[]{:S(2)}) collective-permute-start(bf16[32,3072]{1,0:T(8,128)(2,1)S(1)} %pad_maximum_fusion.3), channel_id=1, source_target_pairs={{0,2},{1,3},{2,0},{3,1},{4,6},{5,7},{6,4},{7,5},{8,10},{9,11},{10,... | collective-permute-start | bytes 589832 | tf_op jit(solution)/shard_map/ppermute | solution.py:236
  35.9 4.2 %collective-permute-start.10 = (bf16[96,3072]{1,0:T(8,128)(2,1)S(1)}, bf16[96,3072]{1,0:T(8,128)(2,1)S(1)}, u32[]{:S(2)}, u32[]{:S(2)}) collective-permute-start(bf16[96,3072]{1,0:T(8,128)(2,1)S(1)} %pad_maximum_fusion.1), channel_id=1, source_target_pairs={{0,4},{4,0},{8,12},{12,8},{16,20},{20,16},{24,28},{28,24},{1,5},{5... | collective-permute-start | bytes 1769480 | tf_op jit(solution)/shard_map/ppermute | solution.py:191
  36.6 18.5 %collective-permute-start.20 = (bf16[48,3072]{1,0:T(8,128)(2,1)S(1)}, bf16[48,3072]{1,0:T(8,128)(2,1)S(1)}, u32[]{:S(2)}, u32[]{:S(2)}) collective-permute-start(bf16[48,3072]{1,0:T(8,128)(2,1)S(1)} %pad_maximum_fusion.2.refs_9_.refs_4_), channel_id=1, source_target_pairs={{0,24},{4,28},{8,16},{12,20},{16,8},{20,12},{24,0},{28,4},{1,25},{... | collective-permute-start | bytes 884744 | tf_op jit(solution)/shard_map/ppermute | solution.py:191
  38.1 20.2 %collective-permute-start.19 = (bf16[48,3072]{1,0:T(8,128)(2,1)S(1)}, bf16[48,3072]{1,0:T(8,128)(2,1)S(1)}, u32[]{:S(2)}, u32[]{:S(2)}) collective-permute-start(bf16[48,3072]{1,0:T(8,128)(2,1)S(1)} %pad_maximum_fusion.2.refs_9_.refs_4_), channel_id=1, source_target_pairs={{0,16},{4,20},{8,24},{12,28},{16,0},{20,4},{24,8},{28,12},{1,17},{... | collective-permute-start | bytes 884744 | tf_op jit(solution)/shard_map/ppermute | solution.py:191
  39.6 18.7 %collective-permute-start.18 = (bf16[48,3072]{1,0:T(8,128)(2,1)S(1)}, bf16[48,3072]{1,0:T(8,128)(2,1)S(1)}, u32[]{:S(2)}, u32[]{:S(2)}) collective-permute-start(bf16[48,3072]{1,0:T(8,128)(2,1)S(1)} %pad_maximum_fusion.2.refs_9_.refs_4_), channel_id=1, source_target_pairs={{0,8},{4,12},{8,0},{12,4},{16,24},{20,28},{24,16},{28,20},{1,9},{5... | collective-permute-start | bytes 884744 | tf_op jit(solution)/shard_map/ppermute | solution.py:191
  44.0 5.6 %collective-permute-start.11 = (bf16[16,512]{1,0:T(8,128)(2,1)S(1)}, bf16[16,512]{1,0:T(8,128)(2,1)S(1)}, u32[]{:S(2)}, u32[]{:S(2)}) collective-permute-start(bf16[16,512]{1,0:T(8,128)(2,1)S(1)} %get-tuple-element.118), channel_id=1, source_target_pairs={{0,1},{1,2},{2,3},{3,0},{4,5},{5,6},{6,7},{7,4},{8,9},{9,10},{10,1... | collective-permute-start | bytes 49160 | tf_op jit(solution)/shard_map/ppermute | solution.py:481
  44.4 5.2 %collective-permute-start.12 = (bf16[16,512]{1,0:T(8,128)(2,1)S(1)}, bf16[16,512]{1,0:T(8,128)(2,1)S(1)}, u32[]{:S(2)}, u32[]{:S(2)}) collective-permute-start(bf16[16,512]{1,0:T(8,128)(2,1)S(1)} %get-tuple-element.119), channel_id=1, source_target_pairs={{0,2},{1,3},{2,0},{3,1},{4,6},{5,7},{6,4},{7,5},{8,10},{9,11},{10,... | collective-permute-start | bytes 49160 | tf_op jit(solution)/shard_map/ppermute | solution.py:481
  49.6 3.7 %collective-permute-start.13 = (bf16[16,512]{1,0:T(8,128)(2,1)S(1)}, bf16[16,512]{1,0:T(8,128)(2,1)S(1)}, u32[]{:S(2)}, u32[]{:S(2)}) collective-permute-start(bf16[16,512]{1,0:T(8,128)(2,1)S(1)} %get-tuple-element.120), channel_id=1, source_target_pairs={{0,3},{1,0},{2,1},{3,2},{4,7},{5,4},{6,5},{7,6},{8,11},{9,8},{10,9... | collective-permute-start | bytes 49160 | tf_op jit(solution)/shard_map/ppermute | solution.py:481
  53.6 3.8 %collective-permute-start.15 = (bf16[16,512]{1,0:T(8,128)(2,1)S(1)}, bf16[16,512]{1,0:T(8,128)(2,1)S(1)}, u32[]{:S(2)}, u32[]{:S(2)}) collective-permute-start(bf16[16,512]{1,0:T(8,128)(2,1)S(1)} %get-tuple-element.123), channel_id=1, source_target_pairs={{0,8},{4,12},{8,0},{12,4},{1,9},{5,13},{9,1},{13,5},{2,10},{6,14},... | collective-permute-start | bytes 49160 | tf_op jit(solution)/shard_map/ppermute | solution.py:487
  66.8 3.8 %collective-permute-start.23 = (bf16[16,512]{1,0:T(8,128)(2,1)S(1)}, bf16[16,512]{1,0:T(8,128)(2,1)S(1)}, u32[]{:S(2)}, u32[]{:S(2)}) collective-permute-start(bf16[16,512]{1,0:T(8,128)(2,1)S(1)} %get-tuple-element.137), channel_id=1, source_target_pairs={{0,8},{4,12},{8,0},{12,4},{1,9},{5,13},{9,1},{13,5},{2,10},{6,14},... | collective-permute-start | bytes 49160 | tf_op jit(solution)/shard_map/ppermute | solution.py:487
  70.9 3.8 %collective-permute-start.25 = (bf16[16,512]{1,0:T(8,128)(2,1)S(1)}, bf16[16,512]{1,0:T(8,128)(2,1)S(1)}, u32[]{:S(2)}, u32[]{:S(2)}) collective-permute-start(bf16[16,512]{1,0:T(8,128)(2,1)S(1)} %get-tuple-element.140), channel_id=1, source_target_pairs={{0,3},{1,0},{2,1},{3,2},{4,7},{5,4},{6,5},{7,6},{8,11},{9,8},{10,9... | collective-permute-start | bytes 49160 | tf_op jit(solution)/shard_map/ppermute | solution.py:481
  72.8 4.7 %collective-permute-start.26 = (bf16[16,512]{1,0:T(8,128)(2,1)S(1)}, bf16[16,512]{1,0:T(8,128)(2,1)S(1)}, u32[]{:S(2)}, u32[]{:S(2)}) collective-permute-start(bf16[16,512]{1,0:T(8,128)(2,1)S(1)} %get-tuple-element.141), channel_id=1, source_target_pairs={{0,2},{1,3},{2,0},{3,1},{4,6},{5,7},{6,4},{7,5},{8,10},{9,11},{10,... | collective-permute-start | bytes 49160 | tf_op jit(solution)/shard_map/ppermute | solution.py:481
  72.8 5.5 %collective-permute-start.27 = (bf16[16,512]{1,0:T(8,128)(2,1)S(1)}, bf16[16,512]{1,0:T(8,128)(2,1)S(1)}, u32[]{:S(2)}, u32[]{:S(2)}) collective-permute-start(bf16[16,512]{1,0:T(8,128)(2,1)S(1)} %get-tuple-element.142), channel_id=1, source_target_pairs={{0,1},{1,2},{2,3},{3,0},{4,5},{5,6},{6,7},{7,4},{8,9},{9,10},{10,1... | collective-permute-start | bytes 49160 | tf_op jit(solution)/shard_map/ppermute | solution.py:481
  80.6 3.8 %collective-permute-start.29 = (bf16[16,512]{1,0:T(8,128)(2,1)S(1)}, bf16[16,512]{1,0:T(8,128)(2,1)S(1)}, u32[]{:S(2)}, u32[]{:S(2)}) collective-permute-start(bf16[16,512]{1,0:T(8,128)(2,1)S(1)} %get-tuple-element.157), channel_id=1, source_target_pairs={{0,8},{4,12},{8,0},{12,4},{1,9},{5,13},{9,1},{13,5},{2,10},{6,14},... | collective-permute-start | bytes 49160 | tf_op jit(solution)/shard_map/ppermute | solution.py:487
  85.3 4.5 %collective-permute-start.31 = (bf16[16,512]{1,0:T(8,128)(2,1)S(1)}, bf16[16,512]{1,0:T(8,128)(2,1)S(1)}, u32[]{:S(2)}, u32[]{:S(2)}) collective-permute-start(bf16[16,512]{1,0:T(8,128)(2,1)S(1)} %get-tuple-element.160), channel_id=1, source_target_pairs={{0,3},{1,0},{2,1},{3,2},{4,7},{5,4},{6,5},{7,6},{8,11},{9,8},{10,9... | collective-permute-start | bytes 49160 | tf_op jit(solution)/shard_map/ppermute | solution.py:481
  86.1 4.6 %collective-permute-start.32 = (bf16[16,512]{1,0:T(8,128)(2,1)S(1)}, bf16[16,512]{1,0:T(8,128)(2,1)S(1)}, u32[]{:S(2)}, u32[]{:S(2)}) collective-permute-start(bf16[16,512]{1,0:T(8,128)(2,1)S(1)} %get-tuple-element.161), channel_id=1, source_target_pairs={{0,2},{1,3},{2,0},{3,1},{4,6},{5,7},{6,4},{7,5},{8,10},{9,11},{10,... | collective-permute-start | bytes 49160 | tf_op jit(solution)/shard_map/ppermute | solution.py:481
  86.5 5.5 %collective-permute-start.33 = (bf16[16,512]{1,0:T(8,128)(2,1)S(1)}, bf16[16,512]{1,0:T(8,128)(2,1)S(1)}, u32[]{:S(2)}, u32[]{:S(2)}) collective-permute-start(bf16[16,512]{1,0:T(8,128)(2,1)S(1)} %get-tuple-element.162), channel_id=1, source_target_pairs={{0,1},{1,2},{2,3},{3,0},{4,5},{5,6},{6,7},{7,4},{8,9},{9,10},{10,1... | collective-permute-start | bytes 49160 | tf_op jit(solution)/shard_map/ppermute | solution.py:481
  (10 other events, 28.3 us)

commit v14 on v13

--- a/solution.py
+++ b/solution.py
@@ -8,7 +8,7 @@
 F32 = jnp.float32
 BF16 = jnp.bfloat16
 LANES = 128
-ROWS = 256
+ROWS = 512
 FEATURES = 512
 AXES = ("groups", "graph", "mp")
 

time: 93.7 us -> 93.3 us (level)
  no operation moved by 1% of the time
where the time goes in v14:
time: 93.3 us; the launch traced here: 93.1 us
  waiting for transfers between devices  39.2 us (42%)
  starting transfers between devices  32.6 us (35%)
  Pallas kernels  20.4 us (22%)
    pallas_call x13, Pallas kernels, call(): pl.pallas_call(body, out_shape=out_shape, in_specs=[hbm if away else vmem...  20.4 us
    ppermute x12, waiting for transfers between devices, along(): lax.ppermute(block, 'mp', [(m, (m + shift) % size) for m in range(size)])  17.2 us
    ppermute x12, starting transfers between devices, along(): lax.ppermute(block, 'mp', [(m, (m + shift) % size) for m in range(size)])  13.8 us
    ppermute x1, waiting for transfers between devices, start(): pairs = lax.ppermute(pair, 'mp', [(m, m ^ 2) for m in range(mp)])  9.26 us
    ppermute x11, starting transfers between devices, across(): lax.ppermute(x, ('groups', 'graph'), [(p, p ^ flip) for p in range(planes)])  8.26 us
    ppermute x9, waiting for transfers between devices, beside(): lax.ppermute(block, 'graph', [(g, g ^ flip) for g in range(lax.axis_size(...  7.71 us
    ppermute x9, starting transfers between devices, beside(): lax.ppermute(block, 'graph', [(g, g ^ flip) for g in range(lax.axis_size(...  5.79 us
    ppermute x11, waiting for transfers between devices, across(): lax.ppermute(x, ('groups', 'graph'), [(p, p ^ flip) for p in range(planes)])  4.95 us
  transfers between devices with their start and end apart: 34, of which 18 were waited for; matrix products, arithmetic and copies ran while one was open for 0% of the time, Pallas kernels for 10%

profile of v14, /device:TPU:0, one launch (start us, length us, event | category | flops | bytes accessed | tf_op | source)
XLA Modules:
  0.0 93.1 jit_solution(11259102804612372283)
XLA Ops:
  0.6 1.7 %prepare_kernel.1 = (bf16[512,64]{1,0:T(8,128)(2,1)S(1)}, bf16[16,512]{1,0:T(8,128)(2,1)S(1)}, bf16[16,3584]{1,0:T(8,128)(2,1)S(1)}, bf16[16,3584]{1,0:T(8,128)(2,1)S(1)}, bf16[16,3584]{1,0:T(8,128)(2,1)S(1)}) custom-call(bf16[512,512]{1,0:T(8,128)(2,1)} %refs_0_.4, s32[4,16]{1,0:T(4,128)} %bitcast.6, bf16[1024,128]{1,0:T(8,128)(2,1)} %refs_0_.5, ...), custom_call_target="tpu_custom_call" | custom-call | bytes 1310976 | tf_op jit(solution)/shard_map/prepare_kernel/pallas_call | solution.py:96
  2.4 3.1 %collective-permute-start = (bf16[16,3584]{1,0:T(8,128)(2,1)S(1)}, bf16[16,3584]{1,0:T(8,128)(2,1)S(1)}, u32[]{:S(2)}, u32[]{:S(2)}) collective-permute-start(bf16[16,3584]{1,0:T(8,128)(2,1)S(1)} %get-tuple-element.100), channel_id=1, source_target_pairs={{0,1},{1,2},{2,3},{3,0},{4,5},{5,6},{6,7},{7,4},{8,9},{9,10},{10,1... | collective-permute-start | bytes 344072 | tf_op jit(solution)/shard_map/ppermute | solution.py:481
  5.5 2.6 %collective-permute-start.1 = (bf16[16,3584]{1,0:T(8,128)(2,1)S(1)}, bf16[16,3584]{1,0:T(8,128)(2,1)S(1)}, u32[]{:S(2)}, u32[]{:S(2)}) collective-permute-start(bf16[16,3584]{1,0:T(8,128)(2,1)S(1)} %get-tuple-element.101), channel_id=1, source_target_pairs={{0,2},{1,3},{2,0},{3,1},{4,6},{5,7},{6,4},{7,5},{8,10},{9,11},{10,... | collective-permute-start | bytes 344072 | tf_op jit(solution)/shard_map/ppermute | solution.py:481
  9.4 2.1 %own_kernel.1 = (bf16[128,3072]{1,0:T(8,128)(2,1)S(1)}, bf16[128,3072]{1,0:T(8,128)(2,1)S(1)}, bf16[16,3072]{1,0:T(8,128)(2,1)S(1)}) custom-call(bf16[1024,128]{1,0:T(8,128)(2,1)} %refs_0_.5, bf16[128,512]{1,0:T(8,128)(2,1)} %refs_1_.1, bf16[1024,128]{1,0:T(8,128)(2,1)} %refs_2_.3, bf16[128,512]{1,0:T(8,128)(2,1)} %refs_3_.3, bf16[1024,128]{1,0:T(8,128)(2,1)} %refs_4_.3, ...), custom_call_target="tpu_custom_call" | custom-call | bytes 1572864 | tf_op jit(solution)/shard_map/own_kernel/pallas_call | solution.py:96
  11.5 1.7 %tables_kernel.1 = (bf16[64,512]{1,0:T(8,128)(2,1)S(1)}, bf16[512,64]{1,0:T(8,128)(2,1)S(1)}, bf16[256,512]{1,0:T(8,128)(2,1)S(1)}, bf16[512,256]{1,0:T(8,128)(2...) custom-call(bf16[256,512]{1,0:T(8,128)(2,1)} %refs_7_.3, ...), custom_call_target="tpu_custom_call" | custom-call | bytes 270464 | tf_op jit(solution)/shard_map/tables_kernel/pallas_call | solution.py:96
  13.3 2.4 %collective-permute-done.1.refs_2_ = bf16[16,3584]{1,0:T(8,128)(2,1)S(1)} collective-permute-done((bf16[16,3584]{1,0:T(8,128)(2,1)S(1)}, bf16[16,3584]{1,0:T(8,128)(2,1)S(1)}, u32[]{:S(2)}, u32[]{:S(2)}) %collective-permute-start.1) | collective-permute-done | bytes 114720 | tf_op jit(solution)/shard_map/ppermute | solution.py:481
  15.8 3.0 %collective-permute-start.6 = (bf16[16,3072]{1,0:T(8,128)(2,1)S(1)}, bf16[16,3072]{1,0:T(8,128)(2,1)S(1)}, u32[]{:S(2)}, u32[]{:S(2)}) collective-permute-start(bf16[16,3072]{1,0:T(8,128)(2,1)S(1)} %get-tuple-element.107), channel_id=1, source_target_pairs={{0,1},{1,0},{2,3},{3,2},{4,5},{5,4},{6,7},{7,6},{8,9},{9,8},{10,11... | collective-permute-start | bytes 294920 | tf_op jit(solution)/shard_map/ppermute | solution.py:234
  18.8 2.5 %collective-permute-start.5 = (bf16[48,3072]{1,0:T(8,128)(2,1)S(1)}, bf16[48,3072]{1,0:T(8,128)(2,1)S(1)}, u32[]{:S(2)}, u32[]{:S(2)}) collective-permute-start(bf16[48,3072]{1,0:T(8,128)(2,1)S(1)} %get-tuple-element.105.refs_9_.refs_14_.refs_4_), channel_id=1, source_target_pairs={{0,24},{4,28},{8,16},{12,20},{16,8},{20,12},{24,0},{28,4},{1,25},{... | collective-permute-start | bytes 884744 | tf_op jit(solution)/shard_map/ppermute | solution.py:191
  22.3 1.7 %collective-permute-start.7 = (bf16[32,3072]{1,0:T(8,128)(2,1)S(1)}, bf16[32,3072]{1,0:T(8,128)(2,1)S(1)}, u32[]{:S(2)}, u32[]{:S(2)}) collective-permute-start(bf16[32,3072]{1,0:T(8,128)(2,1)S(1)} %pad_maximum_fusion.3), channel_id=1, source_target_pairs={{0,2},{1,3},{2,0},{3,1},{4,6},{5,7},{6,4},{7,5},{8,10},{9,11},{10,... | collective-permute-start | bytes 589832 | tf_op jit(solution)/shard_map/ppermute | solution.py:236
  24.0 9.3 %collective-permute-done.7 = bf16[32,3072]{1,0:T(8,128)(2,1)S(1)} collective-permute-done((bf16[32,3072]{1,0:T(8,128)(2,1)S(1)}, bf16[32,3072]{1,0:T(8,128)(2,1)S(1)}, u32[]{:S(2)}, u32[]{:S(2)}) %collective-permute-start.7) | collective-permute-done | bytes 196640 | tf_op jit(solution)/shard_map/ppermute | solution.py:236
  38.1 1.5 %collective-permute-start.19 = (bf16[48,3072]{1,0:T(8,128)(2,1)S(1)}, bf16[48,3072]{1,0:T(8,128)(2,1)S(1)}, u32[]{:S(2)}, u32[]{:S(2)}) collective-permute-start(bf16[48,3072]{1,0:T(8,128)(2,1)S(1)} %pad_maximum_fusion.2.refs_9_.refs_4_), channel_id=1, source_target_pairs={{0,16},{4,20},{8,24},{12,28},{16,0},{20,4},{24,8},{28,12},{1,17},{... | collective-permute-start | bytes 884744 | tf_op jit(solution)/shard_map/ppermute | solution.py:191
  40.2 3.6 %encode_kernel.1 = (bf16[256,512]{1,0:T(8,128)(2,1)S(1)}, bf16[512,512]{1,0:T(8,128)(2,1)S(1)}, bf16[512,512]{1,0:T(8,128)(2,1)S(1)}, f32[512,128]{1,0:T(8,128)S...) custom-call(bf16[512,512]{1,0:T(8,128)(2,1)S(1)} %get-tuple-element., ...), custom_call_target="tpu_custom_call" | custom-call | flops 3000000000 | bytes 5488640 | tf_op jit(solution)/shard_map/encode_kernel/pallas_call | solution.py:96
  44.8 4.5 %collective-permute-done.11.refs_1_ = bf16[16,512]{1,0:T(8,128)(2,1)S(1)} collective-permute-done((bf16[16,512]{1,0:T(8,128)(2,1)S(1)}, bf16[16,512]{1,0:T(8,128)(2,1)S(1)}, u32[]{:S(2)}, u32[]{:S(2)}) %collective-permute-start.11) | collective-permute-done | bytes 16416 | tf_op jit(solution)/shard_map/ppermute | solution.py:481
  49.4 3.7 %collective-permute-done.13.refs_3_ = bf16[16,512]{1,0:T(8,128)(2,1)S(1)} collective-permute-done((bf16[16,512]{1,0:T(8,128)(2,1)S(1)}, bf16[16,512]{1,0:T(8,128)(2,1)S(1)}, u32[]{:S(2)}, u32[]{:S(2)}) %collective-permute-start.13) | collective-permute-done | bytes 16416 | tf_op jit(solution)/shard_map/ppermute | solution.py:481
  53.4 1.6 %collective-permute-start.15 = (bf16[16,512]{1,0:T(8,128)(2,1)S(1)}, bf16[16,512]{1,0:T(8,128)(2,1)S(1)}, u32[]{:S(2)}, u32[]{:S(2)}) collective-permute-start(bf16[16,512]{1,0:T(8,128)(2,1)S(1)} %get-tuple-element.123), channel_id=1, source_target_pairs={{0,8},{4,12},{8,0},{12,4},{1,9},{5,13},{9,1},{13,5},{2,10},{6,14},... | collective-permute-start | bytes 49160 | tf_op jit(solution)/shard_map/ppermute | solution.py:487
  55.2 1.9 %collective-permute-done.15.refs_4_ = bf16[16,512]{1,0:T(8,128)(2,1)S(1)} collective-permute-done((bf16[16,512]{1,0:T(8,128)(2,1)S(1)}, bf16[16,512]{1,0:T(8,128)(2,1)S(1)}, u32[]{:S(2)}, u32[]{:S(2)}) %collective-permute-start.15) | collective-permute-done | bytes 16416 | tf_op jit(solution)/shard_map/ppermute | solution.py:487
  58.8 2.3 %collective-permute-done.17.refs_10_.refs_5_ = bf16[48,3072]{1,0:T(8,128)(2,1)S(1)} collective-permute-done((bf16[48,3072]{1,0:T(8,128)(2,1)S(1)}, bf16[48,3072]{1,0:T(8,128)(2,1)S(1)}, u32[]{:S(2)}, u32[]{:S(2)}) %collective-permute-start.17) | collective-permute-done | bytes 294944 | tf_op jit(solution)/shard_map/ppermute | solution.py:191
  61.1 5.3 %process_kernel.1 = (bf16[256,512]{1,0:T(8,128)(2,1)}, f32[256,512]{1,0:T(8,128)S(1)}, bf16[512,512]{1,0:T(8,128)(2,1)S(1)}, bf16[16,512]{1,0:T(8,128)(2,1)S(1)}...) custom-call(bf16[256,512]{1,0:T(8,128)(2,1)} %refs_0_.7, ...), custom_call_target="tpu_custom_call" | custom-call | flops 5000000000 | bytes 4915200 | tf_op jit(solution)/shard_map/process_kernel/pallas_call | solution.py:96
  68.3 2.1 %collective-permute-done.23.refs_2_ = bf16[16,512]{1,0:T(8,128)(2,1)S(1)} collective-permute-done((bf16[16,512]{1,0:T(8,128)(2,1)S(1)}, bf16[16,512]{1,0:T(8,128)(2,1)S(1)}, u32[]{:S(2)}, u32[]{:S(2)}) %collective-permute-start.23) | collective-permute-done | bytes 16416 | tf_op jit(solution)/shard_map/ppermute | solution.py:487
  70.7 1.9 %collective-permute-start.25 = (bf16[16,512]{1,0:T(8,128)(2,1)S(1)}, bf16[16,512]{1,0:T(8,128)(2,1)S(1)}, u32[]{:S(2)}, u32[]{:S(2)}) collective-permute-start(bf16[16,512]{1,0:T(8,128)(2,1)S(1)} %get-tuple-element.140), channel_id=1, source_target_pairs={{0,3},{1,0},{2,1},{3,2},{4,7},{5,4},{6,5},{7,6},{8,11},{9,8},{10,9... | collective-permute-start | bytes 49160 | tf_op jit(solution)/shard_map/ppermute | solution.py:481
  74.5 2.7 %collective-permute-done.26.refs_2_ = bf16[16,512]{1,0:T(8,128)(2,1)S(1)} collective-permute-done((bf16[16,512]{1,0:T(8,128)(2,1)S(1)}, bf16[16,512]{1,0:T(8,128)(2,1)S(1)}, u32[]{:S(2)}, u32[]{:S(2)}) %collective-permute-start.26) | collective-permute-done | bytes 16416 | tf_op jit(solution)/shard_map/ppermute | solution.py:481
  78.2 2.1 %decode_kernel.1 = (f32[256,512]{1,0:T(8,128)S(1)}, bf16[512,512]{1,0:T(8,128)(2,1)S(1)}, bf16[16,512]{1,0:T(8,128)(2,1)S(1)}, bf16[16,512]{1,0:T(8,128)(2,1)S(1...) custom-call(bf16[16,512]{1,0:T(8,128)(2,1)S(1)} %get-tuple-element.139.refs_0_, ...), custom_call_target="tpu_custom_call" | custom-call | flops 3000000000 | bytes 6209536 | tf_op jit(solution)/shard_map/decode_kernel/pallas_call | solution.py:96
  82.2 1.9 %collective-permute-done.29.refs_2_ = bf16[16,512]{1,0:T(8,128)(2,1)S(1)} collective-permute-done((bf16[16,512]{1,0:T(8,128)(2,1)S(1)}, bf16[16,512]{1,0:T(8,128)(2,1)S(1)}, u32[]{:S(2)}, u32[]{:S(2)}) %collective-permute-start.29) | collective-permute-done | bytes 16416 | tf_op jit(solution)/shard_map/ppermute | solution.py:487
  86.3 1.9 %collective-permute-start.33 = (bf16[16,512]{1,0:T(8,128)(2,1)S(1)}, bf16[16,512]{1,0:T(8,128)(2,1)S(1)}, u32[]{:S(2)}, u32[]{:S(2)}) collective-permute-start(bf16[16,512]{1,0:T(8,128)(2,1)S(1)} %get-tuple-element.162), channel_id=1, source_target_pairs={{0,1},{1,2},{2,3},{3,0},{4,5},{5,6},{6,7},{7,4},{8,9},{9,10},{10,1... | collective-permute-start | bytes 49160 | tf_op jit(solution)/shard_map/ppermute | solution.py:481
  (61 shorter events, 25.0 us)
Async XLA Ops:
  2.4 10.9 %collective-permute-start = (bf16[16,3584]{1,0:T(8,128)(2,1)S(1)}, bf16[16,3584]{1,0:T(8,128)(2,1)S(1)}, u32[]{:S(2)}, u32[]{:S(2)}) collective-permute-start(bf16[16,3584]{1,0:T(8,128)(2,1)S(1)} %get-tuple-element.100), channel_id=1, source_target_pairs={{0,1},{1,2},{2,3},{3,0},{4,5},{5,6},{6,7},{7,4},{8,9},{9,10},{10,1... | collective-permute-start | bytes 344072 | tf_op jit(solution)/shard_map/ppermute | solution.py:481
  5.5 10.2 %collective-permute-start.1 = (bf16[16,3584]{1,0:T(8,128)(2,1)S(1)}, bf16[16,3584]{1,0:T(8,128)(2,1)S(1)}, u32[]{:S(2)}, u32[]{:S(2)}) collective-permute-start(bf16[16,3584]{1,0:T(8,128)(2,1)S(1)} %get-tuple-element.101), channel_id=1, source_target_pairs={{0,2},{1,3},{2,0},{3,1},{4,6},{5,7},{6,4},{7,5},{8,10},{9,11},{10,... | collective-permute-start | bytes 344072 | tf_op jit(solution)/shard_map/ppermute | solution.py:481
  8.0 7.6 %collective-permute-start.2 = (bf16[16,3584]{1,0:T(8,128)(2,1)S(1)}, bf16[16,3584]{1,0:T(8,128)(2,1)S(1)}, u32[]{:S(2)}, u32[]{:S(2)}) collective-permute-start(bf16[16,3584]{1,0:T(8,128)(2,1)S(1)} %get-tuple-element.102), channel_id=1, source_target_pairs={{0,3},{1,0},{2,1},{3,2},{4,7},{5,4},{6,5},{7,6},{8,11},{9,8},{10,9... | collective-permute-start | bytes 344072 | tf_op jit(solution)/shard_map/ppermute | solution.py:481
  15.8 6.5 %collective-permute-start.6 = (bf16[16,3072]{1,0:T(8,128)(2,1)S(1)}, bf16[16,3072]{1,0:T(8,128)(2,1)S(1)}, u32[]{:S(2)}, u32[]{:S(2)}) collective-permute-start(bf16[16,3072]{1,0:T(8,128)(2,1)S(1)} %get-tuple-element.107), channel_id=1, source_target_pairs={{0,1},{1,0},{2,3},{3,2},{4,5},{5,4},{6,7},{7,6},{8,9},{9,8},{10,11... | collective-permute-start | bytes 294920 | tf_op jit(solution)/shard_map/ppermute | solution.py:234
  18.8 14.5 %collective-permute-start.5 = (bf16[48,3072]{1,0:T(8,128)(2,1)S(1)}, bf16[48,3072]{1,0:T(8,128)(2,1)S(1)}, u32[]{:S(2)}, u32[]{:S(2)}) collective-permute-start(bf16[48,3072]{1,0:T(8,128)(2,1)S(1)} %get-tuple-element.105.refs_9_.refs_14_.refs_4_), channel_id=1, source_target_pairs={{0,24},{4,28},{8,16},{12,20},{16,8},{20,12},{24,0},{28,4},{1,25},{... | collective-permute-start | bytes 884744 | tf_op jit(solution)/shard_map/ppermute | solution.py:191
  21.3 13.4 %collective-permute-start.4 = (bf16[48,3072]{1,0:T(8,128)(2,1)S(1)}, bf16[48,3072]{1,0:T(8,128)(2,1)S(1)}, u32[]{:S(2)}, u32[]{:S(2)}) collective-permute-start(bf16[48,3072]{1,0:T(8,128)(2,1)S(1)} %get-tuple-element.105.refs_9_.refs_14_.refs_4_), channel_id=1, source_target_pairs={{0,16},{4,20},{8,24},{12,28},{16,0},{20,4},{24,8},{28,12},{1,17},{... | collective-permute-start | bytes 884744 | tf_op jit(solution)/shard_map/ppermute | solution.py:191
  21.8 14.1 %collective-permute-start.3 = (bf16[48,3584]{1,0:T(8,128)(2,1)S(1)}, bf16[48,3584]{1,0:T(8,128)(2,1)S(1)}, u32[]{:S(2)}, u32[]{:S(2)}) collective-permute-start(bf16[48,3584]{1,0:T(8,128)(2,1)S(1)} %get-tuple-element.108), channel_id=1, source_target_pairs={{0,8},{4,12},{8,0},{12,4},{16,24},{20,28},{24,16},{28,20},{1,9},{5... | collective-permute-start | bytes 1032200 | tf_op jit(solution)/shard_map/ppermute | solution.py:191
  22.3 11.0 %collective-permute-start.7 = (bf16[32,3072]{1,0:T(8,128)(2,1)S(1)}, bf16[32,3072]{1,0:T(8,128)(2,1)S(1)}, u32[]{:S(2)}, u32[]{:S(2)}) collective-permute-start(bf16[32,3072]{1,0:T(8,128)(2,1)S(1)} %pad_maximum_fusion.3), channel_id=1, source_target_pairs={{0,2},{1,3},{2,0},{3,1},{4,6},{5,7},{6,4},{7,5},{8,10},{9,11},{10,... | collective-permute-start | bytes 589832 | tf_op jit(solution)/shard_map/ppermute | solution.py:236
  35.9 4.2 %collective-permute-start.10 = (bf16[96,3072]{1,0:T(8,128)(2,1)S(1)}, bf16[96,3072]{1,0:T(8,128)(2,1)S(1)}, u32[]{:S(2)}, u32[]{:S(2)}) collective-permute-start(bf16[96,3072]{1,0:T(8,128)(2,1)S(1)} %pad_maximum_fusion.1), channel_id=1, source_target_pairs={{0,4},{4,0},{8,12},{12,8},{16,20},{20,16},{24,28},{28,24},{1,5},{5... | collective-permute-start | bytes 1769480 | tf_op jit(solution)/shard_map/ppermute | solution.py:191
  36.6 18.3 %collective-permute-start.20 = (bf16[48,3072]{1,0:T(8,128)(2,1)S(1)}, bf16[48,3072]{1,0:T(8,128)(2,1)S(1)}, u32[]{:S(2)}, u32[]{:S(2)}) collective-permute-start(bf16[48,3072]{1,0:T(8,128)(2,1)S(1)} %pad_maximum_fusion.2.refs_9_.refs_4_), channel_id=1, source_target_pairs={{0,24},{4,28},{8,16},{12,20},{16,8},{20,12},{24,0},{28,4},{1,25},{... | collective-permute-start | bytes 884744 | tf_op jit(solution)/shard_map/ppermute | solution.py:191
  38.1 20.0 %collective-permute-start.19 = (bf16[48,3072]{1,0:T(8,128)(2,1)S(1)}, bf16[48,3072]{1,0:T(8,128)(2,1)S(1)}, u32[]{:S(2)}, u32[]{:S(2)}) collective-permute-start(bf16[48,3072]{1,0:T(8,128)(2,1)S(1)} %pad_maximum_fusion.2.refs_9_.refs_4_), channel_id=1, source_target_pairs={{0,16},{4,20},{8,24},{12,28},{16,0},{20,4},{24,8},{28,12},{1,17},{... | collective-permute-start | bytes 884744 | tf_op jit(solution)/shard_map/ppermute | solution.py:191
  39.6 18.5 %collective-permute-start.18 = (bf16[48,3072]{1,0:T(8,128)(2,1)S(1)}, bf16[48,3072]{1,0:T(8,128)(2,1)S(1)}, u32[]{:S(2)}, u32[]{:S(2)}) collective-permute-start(bf16[48,3072]{1,0:T(8,128)(2,1)S(1)} %pad_maximum_fusion.2.refs_9_.refs_4_), channel_id=1, source_target_pairs={{0,8},{4,12},{8,0},{12,4},{16,24},{20,28},{24,16},{28,20},{1,9},{5... | collective-permute-start | bytes 884744 | tf_op jit(solution)/shard_map/ppermute | solution.py:191
  43.8 5.6 %collective-permute-start.11 = (bf16[16,512]{1,0:T(8,128)(2,1)S(1)}, bf16[16,512]{1,0:T(8,128)(2,1)S(1)}, u32[]{:S(2)}, u32[]{:S(2)}) collective-permute-start(bf16[16,512]{1,0:T(8,128)(2,1)S(1)} %get-tuple-element.118), channel_id=1, source_target_pairs={{0,1},{1,2},{2,3},{3,0},{4,5},{5,6},{6,7},{7,4},{8,9},{9,10},{10,1... | collective-permute-start | bytes 49160 | tf_op jit(solution)/shard_map/ppermute | solution.py:481
  44.2 5.2 %collective-permute-start.12 = (bf16[16,512]{1,0:T(8,128)(2,1)S(1)}, bf16[16,512]{1,0:T(8,128)(2,1)S(1)}, u32[]{:S(2)}, u32[]{:S(2)}) collective-permute-start(bf16[16,512]{1,0:T(8,128)(2,1)S(1)} %get-tuple-element.119), channel_id=1, source_target_pairs={{0,2},{1,3},{2,0},{3,1},{4,6},{5,7},{6,4},{7,5},{8,10},{9,11},{10,... | collective-permute-start | bytes 49160 | tf_op jit(solution)/shard_map/ppermute | solution.py:481
  49.4 3.7 %collective-permute-start.13 = (bf16[16,512]{1,0:T(8,128)(2,1)S(1)}, bf16[16,512]{1,0:T(8,128)(2,1)S(1)}, u32[]{:S(2)}, u32[]{:S(2)}) collective-permute-start(bf16[16,512]{1,0:T(8,128)(2,1)S(1)} %get-tuple-element.120), channel_id=1, source_target_pairs={{0,3},{1,0},{2,1},{3,2},{4,7},{5,4},{6,5},{7,6},{8,11},{9,8},{10,9... | collective-permute-start | bytes 49160 | tf_op jit(solution)/shard_map/ppermute | solution.py:481
  53.4 3.8 %collective-permute-start.15 = (bf16[16,512]{1,0:T(8,128)(2,1)S(1)}, bf16[16,512]{1,0:T(8,128)(2,1)S(1)}, u32[]{:S(2)}, u32[]{:S(2)}) collective-permute-start(bf16[16,512]{1,0:T(8,128)(2,1)S(1)} %get-tuple-element.123), channel_id=1, source_target_pairs={{0,8},{4,12},{8,0},{12,4},{1,9},{5,13},{9,1},{13,5},{2,10},{6,14},... | collective-permute-start | bytes 49160 | tf_op jit(solution)/shard_map/ppermute | solution.py:487
  66.6 3.8 %collective-permute-start.23 = (bf16[16,512]{1,0:T(8,128)(2,1)S(1)}, bf16[16,512]{1,0:T(8,128)(2,1)S(1)}, u32[]{:S(2)}, u32[]{:S(2)}) collective-permute-start(bf16[16,512]{1,0:T(8,128)(2,1)S(1)} %get-tuple-element.137), channel_id=1, source_target_pairs={{0,8},{4,12},{8,0},{12,4},{1,9},{5,13},{9,1},{13,5},{2,10},{6,14},... | collective-permute-start | bytes 49160 | tf_op jit(solution)/shard_map/ppermute | solution.py:487
  70.7 3.8 %collective-permute-start.25 = (bf16[16,512]{1,0:T(8,128)(2,1)S(1)}, bf16[16,512]{1,0:T(8,128)(2,1)S(1)}, u32[]{:S(2)}, u32[]{:S(2)}) collective-permute-start(bf16[16,512]{1,0:T(8,128)(2,1)S(1)} %get-tuple-element.140), channel_id=1, source_target_pairs={{0,3},{1,0},{2,1},{3,2},{4,7},{5,4},{6,5},{7,6},{8,11},{9,8},{10,9... | collective-permute-start | bytes 49160 | tf_op jit(solution)/shard_map/ppermute | solution.py:481
  72.6 4.6 %collective-permute-start.26 = (bf16[16,512]{1,0:T(8,128)(2,1)S(1)}, bf16[16,512]{1,0:T(8,128)(2,1)S(1)}, u32[]{:S(2)}, u32[]{:S(2)}) collective-permute-start(bf16[16,512]{1,0:T(8,128)(2,1)S(1)} %get-tuple-element.141), channel_id=1, source_target_pairs={{0,2},{1,3},{2,0},{3,1},{4,6},{5,7},{6,4},{7,5},{8,10},{9,11},{10,... | collective-permute-start | bytes 49160 | tf_op jit(solution)/shard_map/ppermute | solution.py:481
  72.6 5.5 %collective-permute-start.27 = (bf16[16,512]{1,0:T(8,128)(2,1)S(1)}, bf16[16,512]{1,0:T(8,128)(2,1)S(1)}, u32[]{:S(2)}, u32[]{:S(2)}) collective-permute-start(bf16[16,512]{1,0:T(8,128)(2,1)S(1)} %get-tuple-element.142), channel_id=1, source_target_pairs={{0,1},{1,2},{2,3},{3,0},{4,5},{5,6},{6,7},{7,4},{8,9},{9,10},{10,1... | collective-permute-start | bytes 49160 | tf_op jit(solution)/shard_map/ppermute | solution.py:481
  80.3 3.8 %collective-permute-start.29 = (bf16[16,512]{1,0:T(8,128)(2,1)S(1)}, bf16[16,512]{1,0:T(8,128)(2,1)S(1)}, u32[]{:S(2)}, u32[]{:S(2)}) collective-permute-start(bf16[16,512]{1,0:T(8,128)(2,1)S(1)} %get-tuple-element.157), channel_id=1, source_target_pairs={{0,8},{4,12},{8,0},{12,4},{1,9},{5,13},{9,1},{13,5},{2,10},{6,14},... | collective-permute-start | bytes 49160 | tf_op jit(solution)/shard_map/ppermute | solution.py:487
  85.0 4.6 %collective-permute-start.31 = (bf16[16,512]{1,0:T(8,128)(2,1)S(1)}, bf16[16,512]{1,0:T(8,128)(2,1)S(1)}, u32[]{:S(2)}, u32[]{:S(2)}) collective-permute-start(bf16[16,512]{1,0:T(8,128)(2,1)S(1)} %get-tuple-element.160), channel_id=1, source_target_pairs={{0,3},{1,0},{2,1},{3,2},{4,7},{5,4},{6,5},{7,6},{8,11},{9,8},{10,9... | collective-permute-start | bytes 49160 | tf_op jit(solution)/shard_map/ppermute | solution.py:481
  85.8 4.6 %collective-permute-start.32 = (bf16[16,512]{1,0:T(8,128)(2,1)S(1)}, bf16[16,512]{1,0:T(8,128)(2,1)S(1)}, u32[]{:S(2)}, u32[]{:S(2)}) collective-permute-start(bf16[16,512]{1,0:T(8,128)(2,1)S(1)} %get-tuple-element.161), channel_id=1, source_target_pairs={{0,2},{1,3},{2,0},{3,1},{4,6},{5,7},{6,4},{7,5},{8,10},{9,11},{10,... | collective-permute-start | bytes 49160 | tf_op jit(solution)/shard_map/ppermute | solution.py:481
  86.3 5.5 %collective-permute-start.33 = (bf16[16,512]{1,0:T(8,128)(2,1)S(1)}, bf16[16,512]{1,0:T(8,128)(2,1)S(1)}, u32[]{:S(2)}, u32[]{:S(2)}) collective-permute-start(bf16[16,512]{1,0:T(8,128)(2,1)S(1)} %get-tuple-element.162), channel_id=1, source_target_pairs={{0,1},{1,2},{2,3},{3,0},{4,5},{5,6},{6,7},{7,4},{8,9},{9,10},{10,1... | collective-permute-start | bytes 49160 | tf_op jit(solution)/shard_map/ppermute | solution.py:481
  (10 other events, 28.3 us)

commit v15 on v14

--- a/solution.py
+++ b/solution.py
@@ -206,7 +206,7 @@
             rows.append(lax.all_gather(shards[2 * i + 1], "mp", axis=0, tiled=True))
         enc, proc = jnp.concatenate(rows[:4], axis=1), jnp.concatenate(rows[4:], axis=1)
         arrived = exchange(outgoing, step)
-        return [enc], lambda after: [proc], arrived, grid_t, tables
+        return [enc], lambda one, moved, came: [proc], arrived, grid_t, tables
     far = [Far(s) for s in shards]
     piece = hidden // planes
     width = 6 * features
@@ -240,12 +240,15 @@
     enc = [enc_own, first, core, x, y, corner, x_core, others]
     arrived = [near, core, x, x_core]
     proc_first, *_ = lax.optimization_barrier((proc_first, x, y, corner))
-    plane = [across(proc_first, flip) for flip in (2, 4, 6)]
-    proc = [proc_own, proc_first, across(proc_first, 1)] + plane
-
-    def finish(after):
-        tied = [lax.optimization_barrier((block, *after))[0] for block in plane]
-        return proc + [across(jnp.concatenate(tied), 1)]
+    proc_x, proc_y = across(proc_first, 2), across(proc_first, 4)
+
+    def finish(one, moved, came):
+        late, _ = lax.optimization_barrier((proc_first, one))
+        corner = across(late, 6)
+        x, y, *_ = lax.optimization_barrier((proc_x, proc_y, *moved))
+        sides = across(jnp.concatenate([x, y]), 1)
+        corner, *_ = lax.optimization_barrier((corner, *came))
+        return [proc_own, proc_first, across(proc_first, 1), x, y, sides, corner, across(corner, 1)]
 
     return enc, finish, arrived, grid_t, tables
 
@@ -572,8 +575,9 @@
         halo_g,
         flops=3 * 10**9,
     )
-    halo_in = second_level(first_level(halo_out, halo_step))
-    proc = finish(halo_in[1:])
+    moved = first_level(halo_out, halo_step)
+    halo_in = second_level(moved)
+    proc = finish(mesh_one, moved, halo_in[1:])
     mesh_two, part, ga, *grad_halo = call(
         process_kernel,
         [

time: 93.3 us -> 90.9 us (0.974)
  waiting for transfers between devices: 39.2 us -> 34.6 us
  starting transfers between devices: 32.6 us -> 34.8 us
    ppermute x12, waiting for transfers between devices: 17.2 us -> 10.9 us  [along(): lax.ppermute(block, 'mp', [(m, (m + shift) % size) for m in range(size)])]
    ppermute x12, starting transfers between devices: 13.8 us -> 16 us  [along(): lax.ppermute(block, 'mp', [(m, (m + shift) % size) for m in range(size)])]
    ppermute x9, waiting for transfers between devices: 7.71 us -> 9.57 us  [beside(): lax.ppermute(block, 'graph', [(g, g ^ flip) for g in range(lax.axis_size(...]
    ppermute x11 -> x12, waiting for transfers between devices: 4.95 us -> 4.8 us  [across(): lax.ppermute(x, ('groups', 'graph'), [(p, p ^ flip) for p in range(planes)])]
    ppermute x11 -> x12, starting transfers between devices: 8.26 us -> 8.33 us  [across(): lax.ppermute(x, ('groups', 'graph'), [(p, p ^ flip) for p in range(planes)])]
  transfers between devices with their start and end apart: 34 -> 35, of which waited for: 18 -> 20; matrix products, arithmetic and copies ran while one was open for 0% -> 0% of each run, Pallas kernels for 10% -> 10%
where the time goes in v15:
time: 90.9 us; the launch traced here: 90.7 us
  starting transfers between devices  34.8 us (38%)
  waiting for transfers between devices  34.6 us (38%)
  Pallas kernels  20.4 us (22%)
    pallas_call x13, Pallas kernels, call(): pl.pallas_call(body, out_shape=out_shape, in_specs=[hbm if away else vmem...  20.4 us
    ppermute x12, starting transfers between devices, along(): lax.ppermute(block, 'mp', [(m, (m + shift) % size) for m in range(size)])  16 us
    ppermute x12, waiting for transfers between devices, along(): lax.ppermute(block, 'mp', [(m, (m + shift) % size) for m in range(size)])  10.9 us
    ppermute x9, waiting for transfers between devices, beside(): lax.ppermute(block, 'graph', [(g, g ^ flip) for g in range(lax.axis_size(...  9.57 us
    ppermute x1, waiting for transfers between devices, start(): pairs = lax.ppermute(pair, 'mp', [(m, m ^ 2) for m in range(mp)])  9.26 us
    ppermute x12, starting transfers between devices, across(): lax.ppermute(x, ('groups', 'graph'), [(p, p ^ flip) for p in range(planes)])  8.33 us
    ppermute x9, starting transfers between devices, beside(): lax.ppermute(block, 'graph', [(g, g ^ flip) for g in range(lax.axis_size(...  5.78 us
    ppermute x12, waiting for transfers between devices, across(): lax.ppermute(x, ('groups', 'graph'), [(p, p ^ flip) for p in range(planes)])  4.8 us
  transfers between devices with their start and end apart: 35, of which 20 were waited for; matrix products, arithmetic and copies ran while one was open for 0% of the time, Pallas kernels for 10%

profile of v15, /device:TPU:0, one launch (start us, length us, event | category | flops | bytes accessed | tf_op | source)
XLA Modules:
  0.0 90.7 jit_solution(8219312867820054871)
XLA Ops:
  0.6 1.7 %prepare_kernel.1 = (bf16[512,64]{1,0:T(8,128)(2,1)S(1)}, bf16[16,512]{1,0:T(8,128)(2,1)S(1)}, bf16[16,3584]{1,0:T(8,128)(2,1)S(1)}, bf16[16,3584]{1,0:T(8,128)(2,1)S(1)}, bf16[16,3584]{1,0:T(8,128)(2,1)S(1)}) custom-call(bf16[512,512]{1,0:T(8,128)(2,1)} %refs_0_.4, s32[4,16]{1,0:T(4,128)} %bitcast.6, bf16[1024,128]{1,0:T(8,128)(2,1)} %refs_0_.5, ...), custom_call_target="tpu_custom_call" | custom-call | bytes 1310976 | tf_op jit(solution)/shard_map/prepare_kernel/pallas_call | solution.py:96
  2.4 3.1 %collective-permute-start = (bf16[16,3584]{1,0:T(8,128)(2,1)S(1)}, bf16[16,3584]{1,0:T(8,128)(2,1)S(1)}, u32[]{:S(2)}, u32[]{:S(2)}) collective-permute-start(bf16[16,3584]{1,0:T(8,128)(2,1)S(1)} %get-tuple-element.101), channel_id=1, source_target_pairs={{0,1},{1,2},{2,3},{3,0},{4,5},{5,6},{6,7},{7,4},{8,9},{9,10},{10,1... | collective-permute-start | bytes 344072 | tf_op jit(solution)/shard_map/ppermute | solution.py:484
  5.5 2.6 %collective-permute-start.1 = (bf16[16,3584]{1,0:T(8,128)(2,1)S(1)}, bf16[16,3584]{1,0:T(8,128)(2,1)S(1)}, u32[]{:S(2)}, u32[]{:S(2)}) collective-permute-start(bf16[16,3584]{1,0:T(8,128)(2,1)S(1)} %get-tuple-element.102), channel_id=1, source_target_pairs={{0,2},{1,3},{2,0},{3,1},{4,6},{5,7},{6,4},{7,5},{8,10},{9,11},{10,... | collective-permute-start | bytes 344072 | tf_op jit(solution)/shard_map/ppermute | solution.py:484
  9.4 2.1 %own_kernel.1 = (bf16[128,3072]{1,0:T(8,128)(2,1)S(1)}, bf16[128,3072]{1,0:T(8,128)(2,1)S(1)}, bf16[16,3072]{1,0:T(8,128)(2,1)S(1)}) custom-call(bf16[1024,128]{1,0:T(8,128)(2,1)} %refs_0_.5, bf16[128,512]{1,0:T(8,128)(2,1)} %refs_1_.1, bf16[1024,128]{1,0:T(8,128)(2,1)} %refs_2_.3, bf16[128,512]{1,0:T(8,128)(2,1)} %refs_3_.3, bf16[1024,128]{1,0:T(8,128)(2,1)} %refs_4_.3, ...), custom_call_target="tpu_custom_call" | custom-call | bytes 1572864 | tf_op jit(solution)/shard_map/own_kernel/pallas_call | solution.py:96
  11.5 1.7 %tables_kernel.1 = (bf16[64,512]{1,0:T(8,128)(2,1)S(1)}, bf16[512,64]{1,0:T(8,128)(2,1)S(1)}, bf16[256,512]{1,0:T(8,128)(2,1)S(1)}, bf16[512,256]{1,0:T(8,128)(2...) custom-call(bf16[256,512]{1,0:T(8,128)(2,1)} %refs_7_.3, ...), custom_call_target="tpu_custom_call" | custom-call | bytes 270464 | tf_op jit(solution)/shard_map/tables_kernel/pallas_call | solution.py:96
  13.3 2.4 %collective-permute-done.1.refs_2_ = bf16[16,3584]{1,0:T(8,128)(2,1)S(1)} collective-permute-done((bf16[16,3584]{1,0:T(8,128)(2,1)S(1)}, bf16[16,3584]{1,0:T(8,128)(2,1)S(1)}, u32[]{:S(2)}, u32[]{:S(2)}) %collective-permute-start.1) | collective-permute-done | bytes 114720 | tf_op jit(solution)/shard_map/ppermute | solution.py:484
  15.8 3.0 %collective-permute-start.6 = (bf16[16,3072]{1,0:T(8,128)(2,1)S(1)}, bf16[16,3072]{1,0:T(8,128)(2,1)S(1)}, u32[]{:S(2)}, u32[]{:S(2)}) collective-permute-start(bf16[16,3072]{1,0:T(8,128)(2,1)S(1)} %get-tuple-element.108), channel_id=1, source_target_pairs={{0,1},{1,0},{2,3},{3,2},{4,5},{5,4},{6,7},{7,6},{8,9},{9,8},{10,11... | collective-permute-start | bytes 294920 | tf_op jit(solution)/shard_map/ppermute | solution.py:234
  18.8 2.5 %collective-permute-start.5 = (bf16[48,3072]{1,0:T(8,128)(2,1)S(1)}, bf16[48,3072]{1,0:T(8,128)(2,1)S(1)}, u32[]{:S(2)}, u32[]{:S(2)}) collective-permute-start(bf16[48,3072]{1,0:T(8,128)(2,1)S(1)} %get-tuple-element.106.refs_9_.refs_14_.refs_4_), channel_id=1, source_target_pairs={{0,24},{4,28},{8,16},{12,20},{16,8},{20,12},{24,0},{28,4},{1,25},{... | collective-permute-start | bytes 884744 | tf_op jit(solution)/shard_map/ppermute | solution.py:191
  22.3 1.7 %collective-permute-start.7 = (bf16[32,3072]{1,0:T(8,128)(2,1)S(1)}, bf16[32,3072]{1,0:T(8,128)(2,1)S(1)}, u32[]{:S(2)}, u32[]{:S(2)}) collective-permute-start(bf16[32,3072]{1,0:T(8,128)(2,1)S(1)} %pad_maximum_fusion.3), channel_id=1, source_target_pairs={{0,2},{1,3},{2,0},{3,1},{4,6},{5,7},{6,4},{7,5},{8,10},{9,11},{10,... | collective-permute-start | bytes 589832 | tf_op jit(solution)/shard_map/ppermute | solution.py:236
  24.0 9.3 %collective-permute-done.7 = bf16[32,3072]{1,0:T(8,128)(2,1)S(1)} collective-permute-done((bf16[32,3072]{1,0:T(8,128)(2,1)S(1)}, bf16[32,3072]{1,0:T(8,128)(2,1)S(1)}, u32[]{:S(2)}, u32[]{:S(2)}) %collective-permute-start.7) | collective-permute-done | bytes 196640 | tf_op jit(solution)/shard_map/ppermute | solution.py:236
  37.1 1.5 %collective-permute-start.18 = (bf16[48,3072]{1,0:T(8,128)(2,1)S(1)}, bf16[48,3072]{1,0:T(8,128)(2,1)S(1)}, u32[]{:S(2)}, u32[]{:S(2)}) collective-permute-start(bf16[48,3072]{1,0:T(8,128)(2,1)S(1)} %pad_maximum_fusion.2.refs_9_.refs_4_), channel_id=1, source_target_pairs={{0,8},{4,12},{8,0},{12,4},{16,24},{20,28},{24,16},{28,20},{1,9},{5... | collective-permute-start | bytes 884744 | tf_op jit(solution)/shard_map/ppermute | solution.py:191
  39.0 3.6 %encode_kernel.1 = (bf16[256,512]{1,0:T(8,128)(2,1)S(1)}, bf16[512,512]{1,0:T(8,128)(2,1)S(1)}, bf16[512,512]{1,0:T(8,128)(2,1)S(1)}, f32[512,128]{1,0:T(8,128)S...) custom-call(bf16[512,512]{1,0:T(8,128)(2,1)S(1)} %get-tuple-element., ...), custom_call_target="tpu_custom_call" | custom-call | flops 3000000000 | bytes 5488640 | tf_op jit(solution)/shard_map/encode_kernel/pallas_call | solution.py:96
  43.7 2.8 %collective-permute-start.13 = (bf16[16,512]{1,0:T(8,128)(2,1)S(1)}, bf16[16,512]{1,0:T(8,128)(2,1)S(1)}, u32[]{:S(2)}, u32[]{:S(2)}) collective-permute-start(bf16[16,512]{1,0:T(8,128)(2,1)S(1)} %get-tuple-element.121), channel_id=1, source_target_pairs={{0,3},{1,0},{2,1},{3,2},{4,7},{5,4},{6,5},{7,6},{8,11},{9,8},{10,9... | collective-permute-start | bytes 49160 | tf_op jit(solution)/shard_map/ppermute | solution.py:484
  46.5 1.7 %collective-permute-done.11.refs_1_ = bf16[16,512]{1,0:T(8,128)(2,1)S(1)} collective-permute-done((bf16[16,512]{1,0:T(8,128)(2,1)S(1)}, bf16[16,512]{1,0:T(8,128)(2,1)S(1)}, u32[]{:S(2)}, u32[]{:S(2)}) %collective-permute-start.11) | collective-permute-done | bytes 16416 | tf_op jit(solution)/shard_map/ppermute | solution.py:484
  52.6 4.4 %collective-permute-done.15.refs_4_ = bf16[16,512]{1,0:T(8,128)(2,1)S(1)} collective-permute-done((bf16[16,512]{1,0:T(8,128)(2,1)S(1)}, bf16[16,512]{1,0:T(8,128)(2,1)S(1)}, u32[]{:S(2)}, u32[]{:S(2)}) %collective-permute-start.15) | collective-permute-done | bytes 16416 | tf_op jit(solution)/shard_map/ppermute | solution.py:490
  57.3 1.6 %collective-permute-done.22.refs_15_.refs_10_ = bf16[48,3072]{1,0:T(8,128)(2,1)S(1)} collective-permute-done((bf16[48,3072]{1,0:T(8,128)(2,1)S(1)}, bf16[48,3072]{1,0:T(8,128)(2,1)S(1)}, u32[]{:S(2)}, u32[]{:S(2)}) %collective-permute-start.22) | collective-permute-done | bytes 294944 | tf_op jit(solution)/shard_map/ppermute | solution.py:191
  58.9 5.3 %process_kernel.1 = (bf16[256,512]{1,0:T(8,128)(2,1)}, f32[256,512]{1,0:T(8,128)S(1)}, bf16[512,512]{1,0:T(8,128)(2,1)S(1)}, bf16[16,512]{1,0:T(8,128)(2,1)S(1)}...) custom-call(bf16[256,512]{1,0:T(8,128)(2,1)} %refs_0_.7, ...), custom_call_target="tpu_custom_call" | custom-call | flops 5000000000 | bytes 4915200 | tf_op jit(solution)/shard_map/process_kernel/pallas_call | solution.py:96
  66.2 2.0 %collective-permute-done.24.refs_2_ = bf16[16,512]{1,0:T(8,128)(2,1)S(1)} collective-permute-done((bf16[16,512]{1,0:T(8,128)(2,1)S(1)}, bf16[16,512]{1,0:T(8,128)(2,1)S(1)}, u32[]{:S(2)}, u32[]{:S(2)}) %collective-permute-start.24) | collective-permute-done | bytes 16416 | tf_op jit(solution)/shard_map/ppermute | solution.py:490
  70.3 1.7 %collective-permute-start.28 = (bf16[16,512]{1,0:T(8,128)(2,1)S(1)}, bf16[16,512]{1,0:T(8,128)(2,1)S(1)}, u32[]{:S(2)}, u32[]{:S(2)}) collective-permute-start(bf16[16,512]{1,0:T(8,128)(2,1)S(1)} %get-tuple-element.144), channel_id=1, source_target_pairs={{0,1},{1,2},{2,3},{3,0},{4,5},{5,6},{6,7},{7,4},{8,9},{9,10},{10,1... | collective-permute-start | bytes 49160 | tf_op jit(solution)/shard_map/ppermute | solution.py:484
  74.1 1.8 %collective-permute-done.28.refs_3_ = bf16[16,512]{1,0:T(8,128)(2,1)S(1)} collective-permute-done((bf16[16,512]{1,0:T(8,128)(2,1)S(1)}, bf16[16,512]{1,0:T(8,128)(2,1)S(1)}, u32[]{:S(2)}, u32[]{:S(2)}) %collective-permute-start.28) | collective-permute-done | bytes 16416 | tf_op jit(solution)/shard_map/ppermute | solution.py:484
  75.8 2.1 %decode_kernel.1 = (f32[256,512]{1,0:T(8,128)S(1)}, bf16[512,512]{1,0:T(8,128)(2,1)S(1)}, bf16[16,512]{1,0:T(8,128)(2,1)S(1)}, bf16[16,512]{1,0:T(8,128)(2,1)S(1...) custom-call(bf16[16,512]{1,0:T(8,128)(2,1)S(1)} %get-tuple-element.141.refs_0_, ...), custom_call_target="tpu_custom_call" | custom-call | flops 3000000000 | bytes 6209536 | tf_op jit(solution)/shard_map/decode_kernel/pallas_call | solution.py:96
  79.9 2.0 %collective-permute-done.30.refs_2_ = bf16[16,512]{1,0:T(8,128)(2,1)S(1)} collective-permute-done((bf16[16,512]{1,0:T(8,128)(2,1)S(1)}, bf16[16,512]{1,0:T(8,128)(2,1)S(1)}, u32[]{:S(2)}, u32[]{:S(2)}) %collective-permute-start.30) | collective-permute-done | bytes 16416 | tf_op jit(solution)/shard_map/ppermute | solution.py:490
  82.2 1.7 %collective-permute-start.32 = (bf16[16,512]{1,0:T(8,128)(2,1)S(1)}, bf16[16,512]{1,0:T(8,128)(2,1)S(1)}, u32[]{:S(2)}, u32[]{:S(2)}) collective-permute-start(bf16[16,512]{1,0:T(8,128)(2,1)S(1)} %get-tuple-element.162), channel_id=1, source_target_pairs={{0,3},{1,0},{2,1},{3,2},{4,7},{5,4},{6,5},{7,6},{8,11},{9,8},{10,9... | collective-permute-start | bytes 49160 | tf_op jit(solution)/shard_map/ppermute | solution.py:484
  86.0 2.7 %collective-permute-done.33.refs_2_ = bf16[16,512]{1,0:T(8,128)(2,1)S(1)} collective-permute-done((bf16[16,512]{1,0:T(8,128)(2,1)S(1)}, bf16[16,512]{1,0:T(8,128)(2,1)S(1)}, u32[]{:S(2)}, u32[]{:S(2)}) %collective-permute-start.33) | collective-permute-done | bytes 16416 | tf_op jit(solution)/shard_map/ppermute | solution.py:484
  (63 shorter events, 24.9 us)
Async XLA Ops:
  2.4 10.9 %collective-permute-start = (bf16[16,3584]{1,0:T(8,128)(2,1)S(1)}, bf16[16,3584]{1,0:T(8,128)(2,1)S(1)}, u32[]{:S(2)}, u32[]{:S(2)}) collective-permute-start(bf16[16,3584]{1,0:T(8,128)(2,1)S(1)} %get-tuple-element.101), channel_id=1, source_target_pairs={{0,1},{1,2},{2,3},{3,0},{4,5},{5,6},{6,7},{7,4},{8,9},{9,10},{10,1... | collective-permute-start | bytes 344072 | tf_op jit(solution)/shard_map/ppermute | solution.py:484
  5.5 10.2 %collective-permute-start.1 = (bf16[16,3584]{1,0:T(8,128)(2,1)S(1)}, bf16[16,3584]{1,0:T(8,128)(2,1)S(1)}, u32[]{:S(2)}, u32[]{:S(2)}) collective-permute-start(bf16[16,3584]{1,0:T(8,128)(2,1)S(1)} %get-tuple-element.102), channel_id=1, source_target_pairs={{0,2},{1,3},{2,0},{3,1},{4,6},{5,7},{6,4},{7,5},{8,10},{9,11},{10,... | collective-permute-start | bytes 344072 | tf_op jit(solution)/shard_map/ppermute | solution.py:484
  8.0 7.6 %collective-permute-start.2 = (bf16[16,3584]{1,0:T(8,128)(2,1)S(1)}, bf16[16,3584]{1,0:T(8,128)(2,1)S(1)}, u32[]{:S(2)}, u32[]{:S(2)}) collective-permute-start(bf16[16,3584]{1,0:T(8,128)(2,1)S(1)} %get-tuple-element.103), channel_id=1, source_target_pairs={{0,3},{1,0},{2,1},{3,2},{4,7},{5,4},{6,5},{7,6},{8,11},{9,8},{10,9... | collective-permute-start | bytes 344072 | tf_op jit(solution)/shard_map/ppermute | solution.py:484
  15.8 6.5 %collective-permute-start.6 = (bf16[16,3072]{1,0:T(8,128)(2,1)S(1)}, bf16[16,3072]{1,0:T(8,128)(2,1)S(1)}, u32[]{:S(2)}, u32[]{:S(2)}) collective-permute-start(bf16[16,3072]{1,0:T(8,128)(2,1)S(1)} %get-tuple-element.108), channel_id=1, source_target_pairs={{0,1},{1,0},{2,3},{3,2},{4,5},{5,4},{6,7},{7,6},{8,9},{9,8},{10,11... | collective-permute-start | bytes 294920 | tf_op jit(solution)/shard_map/ppermute | solution.py:234
  18.8 14.5 %collective-permute-start.5 = (bf16[48,3072]{1,0:T(8,128)(2,1)S(1)}, bf16[48,3072]{1,0:T(8,128)(2,1)S(1)}, u32[]{:S(2)}, u32[]{:S(2)}) collective-permute-start(bf16[48,3072]{1,0:T(8,128)(2,1)S(1)} %get-tuple-element.106.refs_9_.refs_14_.refs_4_), channel_id=1, source_target_pairs={{0,24},{4,28},{8,16},{12,20},{16,8},{20,12},{24,0},{28,4},{1,25},{... | collective-permute-start | bytes 884744 | tf_op jit(solution)/shard_map/ppermute | solution.py:191
  21.3 13.4 %collective-permute-start.4 = (bf16[48,3072]{1,0:T(8,128)(2,1)S(1)}, bf16[48,3072]{1,0:T(8,128)(2,1)S(1)}, u32[]{:S(2)}, u32[]{:S(2)}) collective-permute-start(bf16[48,3072]{1,0:T(8,128)(2,1)S(1)} %get-tuple-element.106.refs_9_.refs_14_.refs_4_), channel_id=1, source_target_pairs={{0,16},{4,20},{8,24},{12,28},{16,0},{20,4},{24,8},{28,12},{1,17},{... | collective-permute-start | bytes 884744 | tf_op jit(solution)/shard_map/ppermute | solution.py:191
  21.8 14.1 %collective-permute-start.3 = (bf16[48,3584]{1,0:T(8,128)(2,1)S(1)}, bf16[48,3584]{1,0:T(8,128)(2,1)S(1)}, u32[]{:S(2)}, u32[]{:S(2)}) collective-permute-start(bf16[48,3584]{1,0:T(8,128)(2,1)S(1)} %get-tuple-element.109), channel_id=1, source_target_pairs={{0,8},{4,12},{8,0},{12,4},{16,24},{20,28},{24,16},{28,20},{1,9},{5... | collective-permute-start | bytes 1032200 | tf_op jit(solution)/shard_map/ppermute | solution.py:191
  22.3 11.0 %collective-permute-start.7 = (bf16[32,3072]{1,0:T(8,128)(2,1)S(1)}, bf16[32,3072]{1,0:T(8,128)(2,1)S(1)}, u32[]{:S(2)}, u32[]{:S(2)}) collective-permute-start(bf16[32,3072]{1,0:T(8,128)(2,1)S(1)} %pad_maximum_fusion.3), channel_id=1, source_target_pairs={{0,2},{1,3},{2,0},{3,1},{4,6},{5,7},{6,4},{7,5},{8,10},{9,11},{10,... | collective-permute-start | bytes 589832 | tf_op jit(solution)/shard_map/ppermute | solution.py:236
  36.6 13.2 %collective-permute-start.19 = (bf16[48,3072]{1,0:T(8,128)(2,1)S(1)}, bf16[48,3072]{1,0:T(8,128)(2,1)S(1)}, u32[]{:S(2)}, u32[]{:S(2)}) collective-permute-start(bf16[48,3072]{1,0:T(8,128)(2,1)S(1)} %pad_maximum_fusion.2.refs_9_.refs_4_), channel_id=1, source_target_pairs={{0,16},{4,20},{8,24},{12,28},{16,0},{20,4},{24,8},{28,12},{1,17},{... | collective-permute-start | bytes 884744 | tf_op jit(solution)/shard_map/ppermute | solution.py:191
  37.1 12.7 %collective-permute-start.18 = (bf16[48,3072]{1,0:T(8,128)(2,1)S(1)}, bf16[48,3072]{1,0:T(8,128)(2,1)S(1)}, u32[]{:S(2)}, u32[]{:S(2)}) collective-permute-start(bf16[48,3072]{1,0:T(8,128)(2,1)S(1)} %pad_maximum_fusion.2.refs_9_.refs_4_), channel_id=1, source_target_pairs={{0,8},{4,12},{8,0},{12,4},{16,24},{20,28},{24,16},{28,20},{1,9},{5... | collective-permute-start | bytes 884744 | tf_op jit(solution)/shard_map/ppermute | solution.py:191
  42.6 5.6 %collective-permute-start.11 = (bf16[16,512]{1,0:T(8,128)(2,1)S(1)}, bf16[16,512]{1,0:T(8,128)(2,1)S(1)}, u32[]{:S(2)}, u32[]{:S(2)}) collective-permute-start(bf16[16,512]{1,0:T(8,128)(2,1)S(1)} %get-tuple-element.119), channel_id=1, source_target_pairs={{0,1},{1,2},{2,3},{3,0},{4,5},{5,6},{6,7},{7,4},{8,9},{9,10},{10,1... | collective-permute-start | bytes 49160 | tf_op jit(solution)/shard_map/ppermute | solution.py:484
  43.0 6.6 %collective-permute-start.12 = (bf16[16,512]{1,0:T(8,128)(2,1)S(1)}, bf16[16,512]{1,0:T(8,128)(2,1)S(1)}, u32[]{:S(2)}, u32[]{:S(2)}) collective-permute-start(bf16[16,512]{1,0:T(8,128)(2,1)S(1)} %get-tuple-element.120), channel_id=1, source_target_pairs={{0,2},{1,3},{2,0},{3,1},{4,6},{5,7},{6,4},{7,5},{8,10},{9,11},{10,... | collective-permute-start | bytes 49160 | tf_op jit(solution)/shard_map/ppermute | solution.py:484
  43.7 6.0 %collective-permute-start.13 = (bf16[16,512]{1,0:T(8,128)(2,1)S(1)}, bf16[16,512]{1,0:T(8,128)(2,1)S(1)}, u32[]{:S(2)}, u32[]{:S(2)}) collective-permute-start(bf16[16,512]{1,0:T(8,128)(2,1)S(1)} %get-tuple-element.121), channel_id=1, source_target_pairs={{0,3},{1,0},{2,1},{3,2},{4,7},{5,4},{6,5},{7,6},{8,11},{9,8},{10,9... | collective-permute-start | bytes 49160 | tf_op jit(solution)/shard_map/ppermute | solution.py:484
  48.2 9.2 %collective-permute-start.21 = (bf16[48,3072]{1,0:T(8,128)(2,1)S(1)}, bf16[48,3072]{1,0:T(8,128)(2,1)S(1)}, u32[]{:S(2)}, u32[]{:S(2)}) collective-permute-start(bf16[48,3072]{1,0:T(8,128)(2,1)S(1)} %pad_maximum_fusion.2.refs_9_.refs_4_), channel_id=1, source_target_pairs={{0,24},{4,28},{8,16},{12,20},{16,8},{20,12},{24,0},{28,4},{1,25},{... | collective-permute-start | bytes 884744 | tf_op jit(solution)/shard_map/ppermute | solution.py:191
  49.9 9.0 %collective-permute-start.20 = (bf16[96,3072]{1,0:T(8,128)(2,1)S(1)}, bf16[96,3072]{1,0:T(8,128)(2,1)S(1)}, u32[]{:S(2)}, u32[]{:S(2)}) collective-permute-start(bf16[96,3072]{1,0:T(8,128)(2,1)S(1)} %pad_maximum_fusion.1), channel_id=1, source_target_pairs={{0,4},{4,0},{8,12},{12,8},{16,20},{20,16},{24,28},{28,24},{1,5},{5... | collective-permute-start | bytes 1769480 | tf_op jit(solution)/shard_map/ppermute | solution.py:191
  50.4 6.6 %collective-permute-start.15 = (bf16[16,512]{1,0:T(8,128)(2,1)S(1)}, bf16[16,512]{1,0:T(8,128)(2,1)S(1)}, u32[]{:S(2)}, u32[]{:S(2)}) collective-permute-start(bf16[16,512]{1,0:T(8,128)(2,1)S(1)} %get-tuple-element.124), channel_id=1, source_target_pairs={{0,8},{4,12},{8,0},{12,4},{1,9},{5,13},{9,1},{13,5},{2,10},{6,14},... | collective-permute-start | bytes 49160 | tf_op jit(solution)/shard_map/ppermute | solution.py:490
  51.7 5.3 %collective-permute-start.16 = (bf16[16,512]{1,0:T(8,128)(2,1)S(1)}, bf16[16,512]{1,0:T(8,128)(2,1)S(1)}, u32[]{:S(2)}, u32[]{:S(2)}) collective-permute-start(bf16[16,512]{1,0:T(8,128)(2,1)S(1)} %get-tuple-element.125), channel_id=1, source_target_pairs={{0,12},{4,8},{8,4},{12,0},{1,13},{5,9},{9,5},{13,1},{2,14},{6,10},... | collective-permute-start | bytes 49160 | tf_op jit(solution)/shard_map/ppermute | solution.py:490
  52.0 5.4 %collective-permute-start.17 = (bf16[48,3072]{1,0:T(8,128)(2,1)S(1)}, bf16[48,3072]{1,0:T(8,128)(2,1)S(1)}, u32[]{:S(2)}, u32[]{:S(2)}) collective-permute-start(bf16[48,3072]{1,0:T(8,128)(2,1)S(1)} %pad_maximum_fusion.2.refs_9_.refs_4_), channel_id=1, source_target_pairs={{0,4},{4,0},{8,12},{12,8},{16,20},{20,16},{24,28},{28,24},{1,5},{5... | collective-permute-start | bytes 884744 | tf_op jit(solution)/shard_map/ppermute | solution.py:191
  69.3 3.8 %collective-permute-start.26 = (bf16[16,512]{1,0:T(8,128)(2,1)S(1)}, bf16[16,512]{1,0:T(8,128)(2,1)S(1)}, u32[]{:S(2)}, u32[]{:S(2)}) collective-permute-start(bf16[16,512]{1,0:T(8,128)(2,1)S(1)} %get-tuple-element.142), channel_id=1, source_target_pairs={{0,3},{1,0},{2,1},{3,2},{4,7},{5,4},{6,5},{7,6},{8,11},{9,8},{10,9... | collective-permute-start | bytes 49160 | tf_op jit(solution)/shard_map/ppermute | solution.py:484
  69.4 4.7 %collective-permute-start.27 = (bf16[16,512]{1,0:T(8,128)(2,1)S(1)}, bf16[16,512]{1,0:T(8,128)(2,1)S(1)}, u32[]{:S(2)}, u32[]{:S(2)}) collective-permute-start(bf16[16,512]{1,0:T(8,128)(2,1)S(1)} %get-tuple-element.143), channel_id=1, source_target_pairs={{0,2},{1,3},{2,0},{3,1},{4,6},{5,7},{6,4},{7,5},{8,10},{9,11},{10,... | collective-permute-start | bytes 49160 | tf_op jit(solution)/shard_map/ppermute | solution.py:484
  70.3 5.5 %collective-permute-start.28 = (bf16[16,512]{1,0:T(8,128)(2,1)S(1)}, bf16[16,512]{1,0:T(8,128)(2,1)S(1)}, u32[]{:S(2)}, u32[]{:S(2)}) collective-permute-start(bf16[16,512]{1,0:T(8,128)(2,1)S(1)} %get-tuple-element.144), channel_id=1, source_target_pairs={{0,1},{1,2},{2,3},{3,0},{4,5},{5,6},{6,7},{7,4},{8,9},{9,10},{10,1... | collective-permute-start | bytes 49160 | tf_op jit(solution)/shard_map/ppermute | solution.py:484
  78.0 3.9 %collective-permute-start.30 = (bf16[16,512]{1,0:T(8,128)(2,1)S(1)}, bf16[16,512]{1,0:T(8,128)(2,1)S(1)}, u32[]{:S(2)}, u32[]{:S(2)}) collective-permute-start(bf16[16,512]{1,0:T(8,128)(2,1)S(1)} %get-tuple-element.159), channel_id=1, source_target_pairs={{0,8},{4,12},{8,0},{12,4},{1,9},{5,13},{9,1},{13,5},{2,10},{6,14},... | collective-permute-start | bytes 49160 | tf_op jit(solution)/shard_map/ppermute | solution.py:490
  83.9 4.8 %collective-permute-start.33 = (bf16[16,512]{1,0:T(8,128)(2,1)S(1)}, bf16[16,512]{1,0:T(8,128)(2,1)S(1)}, u32[]{:S(2)}, u32[]{:S(2)}) collective-permute-start(bf16[16,512]{1,0:T(8,128)(2,1)S(1)} %get-tuple-element.163), channel_id=1, source_target_pairs={{0,2},{1,3},{2,0},{3,1},{4,6},{5,7},{6,4},{7,5},{8,10},{9,11},{10,... | collective-permute-start | bytes 49160 | tf_op jit(solution)/shard_map/ppermute | solution.py:484
  83.9 5.5 %collective-permute-start.34 = (bf16[16,512]{1,0:T(8,128)(2,1)S(1)}, bf16[16,512]{1,0:T(8,128)(2,1)S(1)}, u32[]{:S(2)}, u32[]{:S(2)}) collective-permute-start(bf16[16,512]{1,0:T(8,128)(2,1)S(1)} %get-tuple-element.164), channel_id=1, source_target_pairs={{0,1},{1,2},{2,3},{3,0},{4,5},{5,6},{6,7},{7,4},{8,9},{9,10},{10,1... | collective-permute-start | bytes 49160 | tf_op jit(solution)/shard_map/ppermute | solution.py:484
  (11 other events, 29.6 us)

commit v16 on v15

--- a/solution.py
+++ b/solution.py
@@ -285,16 +285,19 @@
     return max(capacity, 16 // min(lax.axis_size("mp"), lax.axis_size("graph")))
 
 
+def apart_at(peer, slot, step, mp_first):
+    mp, graph = lax.axis_size("mp"), lax.axis_size("graph")
+    along_mp, along_graph = peer % mp ^ lax.axis_index("mp"), peer // mp ^ lax.axis_index("graph")
+    block = along_mp * graph + along_graph if mp_first else along_graph * mp + along_mp
+    return block * step + slot
+
+
 def sent_at(peer, slot, step):
-    mp, graph = lax.axis_size("mp"), lax.axis_size("graph")
-    shift = (peer % mp + mp - lax.axis_index("mp")) % mp
-    return (shift * graph + (peer // mp ^ lax.axis_index("graph"))) * step + slot
+    return apart_at(peer, slot, step, True)
 
 
 def arrived_at(peer, slot, step):
-    mp = lax.axis_size("mp")
-    shift = (lax.axis_index("mp") + mp - peer % mp) % mp
-    return ((peer // mp ^ lax.axis_index("graph")) * mp + shift) * step + slot
+    return apart_at(peer, slot, step, False)
 
 
 def sent_row(index, step):
@@ -477,11 +480,11 @@
     out.send(dot(table_in()[...], stacked(back)))
 
 
-def along(block, shift):
+def along(block, flip):
     size = lax.axis_size("mp")
-    if shift % size == 0:
+    if flip == 0:
         return block
-    return lax.ppermute(block, "mp", [(m, (m + shift) % size) for m in range(size)])
+    return lax.ppermute(block, "mp", [(m, m ^ flip) for m in range(size)])
 
 
 def beside(block, flip):
@@ -509,7 +512,7 @@
 
 def exchange_back(blocks, step):
     blocks = turn([beside(b, t) for t, b in enumerate(blocks)], lax.axis_size("mp"), step)
-    return [along(b, -s) for s, b in enumerate(blocks)], blocks[0]
+    return [along(b, s) for s, b in enumerate(blocks)], blocks[0]
 
 
 def local(

time: 90.9 us -> 91.5 us (level)
  starting transfers between devices: 34.8 us -> 37.4 us
  waiting for transfers between devices: 34.6 us -> 32.5 us
    ppermute x12, starting transfers between devices: 16 us -> 19 us  [along(): return lax.ppermute(block, 'mp', [(m, m ^ flip) for m in range(size)])]
    ppermute x12, waiting for transfers between devices: 10.9 us -> 13.7 us  [along(): return lax.ppermute(block, 'mp', [(m, m ^ flip) for m in range(size)])]
    ppermute x9, waiting for transfers between devices: 9.57 us -> 7.21 us  [beside(): lax.ppermute(block, 'graph', [(g, g ^ flip) for g in range(lax.axis_size(...]
    ppermute x1, waiting for transfers between devices: 9.26 us -> 7.12 us  [start(): pairs = lax.ppermute(pair, 'mp', [(m, m ^ 2) for m in range(mp)])]
    ppermute x1, starting transfers between devices: 2.99 us -> 1.85 us  [start(): beside_me = lax.ppermute(proc_piece, 'mp', [(m, m ^ 1) for m in range(mp)])]
  transfers between devices with their start and end apart: 35 -> 35, of which waited for: 20 -> 16; matrix products, arithmetic and copies ran while one was open for 0% -> 0% of each run, Pallas kernels for 10% -> 10%
where the time goes in v16:
time: 91.5 us; the launch traced here: 91.3 us
  starting transfers between devices  37.4 us (41%)
  waiting for transfers between devices  32.5 us (36%)
  Pallas kernels  20.4 us (22%)
    pallas_call x13, Pallas kernels, call(): pl.pallas_call(body, out_shape=out_shape, in_specs=[hbm if away else vmem...  20.4 us
    ppermute x12, starting transfers between devices, along(): return lax.ppermute(block, 'mp', [(m, m ^ flip) for m in range(size)])  19 us
    ppermute x12, waiting for transfers between devices, along(): return lax.ppermute(block, 'mp', [(m, m ^ flip) for m in range(size)])  13.7 us
    ppermute x12, starting transfers between devices, across(): lax.ppermute(x, ('groups', 'graph'), [(p, p ^ flip) for p in range(planes)])  8.42 us
    ppermute x9, waiting for transfers between devices, beside(): lax.ppermute(block, 'graph', [(g, g ^ flip) for g in range(lax.axis_size(...  7.21 us
    ppermute x1, waiting for transfers between devices, start(): pairs = lax.ppermute(pair, 'mp', [(m, m ^ 2) for m in range(mp)])  7.12 us
    ppermute x9, starting transfers between devices, beside(): lax.ppermute(block, 'graph', [(g, g ^ flip) for g in range(lax.axis_size(...  5.85 us
    ppermute x12, waiting for transfers between devices, across(): lax.ppermute(x, ('groups', 'graph'), [(p, p ^ flip) for p in range(planes)])  4.46 us
  transfers between devices with their start and end apart: 35, of which 16 were waited for; matrix products, arithmetic and copies ran while one was open for 0% of the time, Pallas kernels for 10%

profile of v16, /device:TPU:0, one launch (start us, length us, event | category | flops | bytes accessed | tf_op | source)
XLA Modules:
  0.0 91.3 jit_solution(3610483309289965867)
XLA Ops:
  0.6 1.7 %prepare_kernel.1 = (bf16[512,64]{1,0:T(8,128)(2,1)S(1)}, bf16[16,512]{1,0:T(8,128)(2,1)S(1)}, bf16[16,3584]{1,0:T(8,128)(2,1)S(1)}, bf16[16,3584]{1,0:T(8,128)(2,1)S(1)}, bf16[16,3584]{1,0:T(8,128)(2,1)S(1)}) custom-call(bf16[512,512]{1,0:T(8,128)(2,1)} %refs_0_.4, s32[4,16]{1,0:T(4,128)} %bitcast.6, bf16[1024,128]{1,0:T(8,128)(2,1)} %refs_0_.5, ...), custom_call_target="tpu_custom_call" | custom-call | bytes 1310976 | tf_op jit(solution)/shard_map/prepare_kernel/pallas_call | solution.py:96
  2.4 3.1 %collective-permute-start = (bf16[16,3584]{1,0:T(8,128)(2,1)S(1)}, bf16[16,3584]{1,0:T(8,128)(2,1)S(1)}, u32[]{:S(2)}, u32[]{:S(2)}) collective-permute-start(bf16[16,3584]{1,0:T(8,128)(2,1)S(1)} %get-tuple-element.101), channel_id=1, source_target_pairs={{0,1},{1,0},{2,3},{3,2},{4,5},{5,4},{6,7},{7,6},{8,9},{9,8},{10,11... | collective-permute-start | bytes 344072 | tf_op jit(solution)/shard_map/ppermute | solution.py:487
  5.5 2.6 %collective-permute-start.1 = (bf16[16,3584]{1,0:T(8,128)(2,1)S(1)}, bf16[16,3584]{1,0:T(8,128)(2,1)S(1)}, u32[]{:S(2)}, u32[]{:S(2)}) collective-permute-start(bf16[16,3584]{1,0:T(8,128)(2,1)S(1)} %get-tuple-element.102), channel_id=1, source_target_pairs={{0,2},{1,3},{2,0},{3,1},{4,6},{5,7},{6,4},{7,5},{8,10},{9,11},{10,... | collective-permute-start | bytes 344072 | tf_op jit(solution)/shard_map/ppermute | solution.py:487
  8.1 2.1 %own_kernel.1 = (bf16[128,3072]{1,0:T(8,128)(2,1)S(1)}, bf16[128,3072]{1,0:T(8,128)(2,1)S(1)}, bf16[16,3072]{1,0:T(8,128)(2,1)S(1)}) custom-call(bf16[1024,128]{1,0:T(8,128)(2,1)} %refs_0_.5, bf16[128,512]{1,0:T(8,128)(2,1)} %refs_1_.1, bf16[1024,128]{1,0:T(8,128)(2,1)} %refs_2_.3, bf16[128,512]{1,0:T(8,128)(2,1)} %refs_3_.3, bf16[1024,128]{1,0:T(8,128)(2,1)} %refs_4_.3, ...), custom_call_target="tpu_custom_call" | custom-call | bytes 1572864 | tf_op jit(solution)/shard_map/own_kernel/pallas_call | solution.py:96
  10.2 1.7 %tables_kernel.1 = (bf16[64,512]{1,0:T(8,128)(2,1)S(1)}, bf16[512,64]{1,0:T(8,128)(2,1)S(1)}, bf16[256,512]{1,0:T(8,128)(2,1)S(1)}, bf16[512,256]{1,0:T(8,128)(2...) custom-call(bf16[256,512]{1,0:T(8,128)(2,1)} %refs_7_.3, ...), custom_call_target="tpu_custom_call" | custom-call | bytes 270464 | tf_op jit(solution)/shard_map/tables_kernel/pallas_call | solution.py:96
  11.9 5.2 %collective-permute-done.1.refs_2_ = bf16[16,3584]{1,0:T(8,128)(2,1)S(1)} collective-permute-done((bf16[16,3584]{1,0:T(8,128)(2,1)S(1)}, bf16[16,3584]{1,0:T(8,128)(2,1)S(1)}, u32[]{:S(2)}, u32[]{:S(2)}) %collective-permute-start.1) | collective-permute-done | bytes 114720 | tf_op jit(solution)/shard_map/ppermute | solution.py:487
  17.4 1.9 %collective-permute-start.6 = (bf16[16,3072]{1,0:T(8,128)(2,1)S(1)}, bf16[16,3072]{1,0:T(8,128)(2,1)S(1)}, u32[]{:S(2)}, u32[]{:S(2)}) collective-permute-start(bf16[16,3072]{1,0:T(8,128)(2,1)S(1)} %get-tuple-element.108), channel_id=1, source_target_pairs={{0,1},{1,0},{2,3},{3,2},{4,5},{5,4},{6,7},{7,6},{8,9},{9,8},{10,11... | collective-permute-start | bytes 294920 | tf_op jit(solution)/shard_map/ppermute | solution.py:234
  19.2 2.5 %collective-permute-start.5 = (bf16[48,3072]{1,0:T(8,128)(2,1)S(1)}, bf16[48,3072]{1,0:T(8,128)(2,1)S(1)}, u32[]{:S(2)}, u32[]{:S(2)}) collective-permute-start(bf16[48,3072]{1,0:T(8,128)(2,1)S(1)} %get-tuple-element.106.refs_9_.refs_14_.refs_4_), channel_id=1, source_target_pairs={{0,24},{4,28},{8,16},{12,20},{16,8},{20,12},{24,0},{28,4},{1,25},{... | collective-permute-start | bytes 884744 | tf_op jit(solution)/shard_map/ppermute | solution.py:191
  22.7 2.3 %collective-permute-start.7 = (bf16[32,3072]{1,0:T(8,128)(2,1)S(1)}, bf16[32,3072]{1,0:T(8,128)(2,1)S(1)}, u32[]{:S(2)}, u32[]{:S(2)}) collective-permute-start(bf16[32,3072]{1,0:T(8,128)(2,1)S(1)} %pad_maximum_fusion.3), channel_id=1, source_target_pairs={{0,2},{1,3},{2,0},{3,1},{4,6},{5,7},{6,4},{7,5},{8,10},{9,11},{10,... | collective-permute-start | bytes 589832 | tf_op jit(solution)/shard_map/ppermute | solution.py:236
  25.0 7.1 %collective-permute-done.7 = bf16[32,3072]{1,0:T(8,128)(2,1)S(1)} collective-permute-done((bf16[32,3072]{1,0:T(8,128)(2,1)S(1)}, bf16[32,3072]{1,0:T(8,128)(2,1)S(1)}, u32[]{:S(2)}, u32[]{:S(2)}) %collective-permute-start.7) | collective-permute-done | bytes 196640 | tf_op jit(solution)/shard_map/ppermute | solution.py:236
  36.0 1.5 %collective-permute-start.18 = (bf16[48,3072]{1,0:T(8,128)(2,1)S(1)}, bf16[48,3072]{1,0:T(8,128)(2,1)S(1)}, u32[]{:S(2)}, u32[]{:S(2)}) collective-permute-start(bf16[48,3072]{1,0:T(8,128)(2,1)S(1)} %pad_maximum_fusion.2.refs_9_.refs_4_), channel_id=1, source_target_pairs={{0,8},{4,12},{8,0},{12,4},{16,24},{20,28},{24,16},{28,20},{1,9},{5... | collective-permute-start | bytes 884744 | tf_op jit(solution)/shard_map/ppermute | solution.py:191
  37.9 3.6 %encode_kernel.1 = (bf16[256,512]{1,0:T(8,128)(2,1)S(1)}, bf16[512,512]{1,0:T(8,128)(2,1)S(1)}, bf16[512,512]{1,0:T(8,128)(2,1)S(1)}, f32[512,128]{1,0:T(8,128)S...) custom-call(bf16[512,512]{1,0:T(8,128)(2,1)S(1)} %get-tuple-element., ...), custom_call_target="tpu_custom_call" | custom-call | flops 3000000000 | bytes 5488640 | tf_op jit(solution)/shard_map/encode_kernel/pallas_call | solution.py:96
  41.9 2.7 %collective-permute-start.12 = (bf16[16,512]{1,0:T(8,128)(2,1)S(1)}, bf16[16,512]{1,0:T(8,128)(2,1)S(1)}, u32[]{:S(2)}, u32[]{:S(2)}) collective-permute-start(bf16[16,512]{1,0:T(8,128)(2,1)S(1)} %get-tuple-element.120), channel_id=1, source_target_pairs={{0,2},{1,3},{2,0},{3,1},{4,6},{5,7},{6,4},{7,5},{8,10},{9,11},{10,... | collective-permute-start | bytes 49160 | tf_op jit(solution)/shard_map/ppermute | solution.py:487
  47.4 2.8 %collective-permute-done.13.refs_3_ = bf16[16,512]{1,0:T(8,128)(2,1)S(1)} collective-permute-done((bf16[16,512]{1,0:T(8,128)(2,1)S(1)}, bf16[16,512]{1,0:T(8,128)(2,1)S(1)}, u32[]{:S(2)}, u32[]{:S(2)}) %collective-permute-start.13) | collective-permute-done | bytes 16416 | tf_op jit(solution)/shard_map/ppermute | solution.py:487
  53.1 1.8 %collective-permute-done.15.refs_4_ = bf16[16,512]{1,0:T(8,128)(2,1)S(1)} collective-permute-done((bf16[16,512]{1,0:T(8,128)(2,1)S(1)}, bf16[16,512]{1,0:T(8,128)(2,1)S(1)}, u32[]{:S(2)}, u32[]{:S(2)}) %collective-permute-start.15) | collective-permute-done | bytes 16416 | tf_op jit(solution)/shard_map/ppermute | solution.py:493
  57.3 5.3 %process_kernel.1 = (bf16[256,512]{1,0:T(8,128)(2,1)}, f32[256,512]{1,0:T(8,128)S(1)}, bf16[512,512]{1,0:T(8,128)(2,1)S(1)}, bf16[16,512]{1,0:T(8,128)(2,1)S(1)}...) custom-call(bf16[256,512]{1,0:T(8,128)(2,1)} %refs_0_.7, ...), custom_call_target="tpu_custom_call" | custom-call | flops 5000000000 | bytes 4915200 | tf_op jit(solution)/shard_map/process_kernel/pallas_call | solution.py:96
  64.6 2.0 %collective-permute-done.24.refs_2_ = bf16[16,512]{1,0:T(8,128)(2,1)S(1)} collective-permute-done((bf16[16,512]{1,0:T(8,128)(2,1)S(1)}, bf16[16,512]{1,0:T(8,128)(2,1)S(1)}, u32[]{:S(2)}, u32[]{:S(2)}) %collective-permute-start.24) | collective-permute-done | bytes 16416 | tf_op jit(solution)/shard_map/ppermute | solution.py:493
  67.3 3.2 %collective-permute-start.27 = (bf16[16,512]{1,0:T(8,128)(2,1)S(1)}, bf16[16,512]{1,0:T(8,128)(2,1)S(1)}, u32[]{:S(2)}, u32[]{:S(2)}) collective-permute-start(bf16[16,512]{1,0:T(8,128)(2,1)S(1)} %get-tuple-element.143), channel_id=1, source_target_pairs={{0,2},{1,3},{2,0},{3,1},{4,6},{5,7},{6,4},{7,5},{8,10},{9,11},{10,... | collective-permute-start | bytes 49160 | tf_op jit(solution)/shard_map/ppermute | solution.py:487
  72.4 3.6 %collective-permute-done.28.refs_3_ = bf16[16,512]{1,0:T(8,128)(2,1)S(1)} collective-permute-done((bf16[16,512]{1,0:T(8,128)(2,1)S(1)}, bf16[16,512]{1,0:T(8,128)(2,1)S(1)}, u32[]{:S(2)}, u32[]{:S(2)}) %collective-permute-start.28) | collective-permute-done | bytes 16416 | tf_op jit(solution)/shard_map/ppermute | solution.py:487
  76.0 2.1 %decode_kernel.1 = (f32[256,512]{1,0:T(8,128)S(1)}, bf16[512,512]{1,0:T(8,128)(2,1)S(1)}, bf16[16,512]{1,0:T(8,128)(2,1)S(1)}, bf16[16,512]{1,0:T(8,128)(2,1)S(1...) custom-call(bf16[16,512]{1,0:T(8,128)(2,1)S(1)} %get-tuple-element.141.refs_0_, ...), custom_call_target="tpu_custom_call" | custom-call | flops 3000000000 | bytes 6209536 | tf_op jit(solution)/shard_map/decode_kernel/pallas_call | solution.py:96
  80.0 2.0 %collective-permute-done.30.refs_2_ = bf16[16,512]{1,0:T(8,128)(2,1)S(1)} collective-permute-done((bf16[16,512]{1,0:T(8,128)(2,1)S(1)}, bf16[16,512]{1,0:T(8,128)(2,1)S(1)}, u32[]{:S(2)}, u32[]{:S(2)}) %collective-permute-start.30) | collective-permute-done | bytes 16416 | tf_op jit(solution)/shard_map/ppermute | solution.py:493
  82.4 2.1 %collective-permute-start.33 = (bf16[16,512]{1,0:T(8,128)(2,1)S(1)}, bf16[16,512]{1,0:T(8,128)(2,1)S(1)}, u32[]{:S(2)}, u32[]{:S(2)}) collective-permute-start(bf16[16,512]{1,0:T(8,128)(2,1)S(1)} %get-tuple-element.163), channel_id=1, source_target_pairs={{0,2},{1,3},{2,0},{3,1},{4,6},{5,7},{6,4},{7,5},{8,10},{9,11},{10,... | collective-permute-start | bytes 49160 | tf_op jit(solution)/shard_map/ppermute | solution.py:487
  84.5 2.3 %collective-permute-start.34 = (bf16[16,512]{1,0:T(8,128)(2,1)S(1)}, bf16[16,512]{1,0:T(8,128)(2,1)S(1)}, u32[]{:S(2)}, u32[]{:S(2)}) collective-permute-start(bf16[16,512]{1,0:T(8,128)(2,1)S(1)} %get-tuple-element.164), channel_id=1, source_target_pairs={{0,3},{1,2},{2,1},{3,0},{4,7},{5,6},{6,5},{7,4},{8,11},{9,10},{10,... | collective-permute-start | bytes 49160 | tf_op jit(solution)/shard_map/ppermute | solution.py:487
  88.1 1.9 %collective-permute-done.34.refs_3_ = bf16[16,512]{1,0:T(8,128)(2,1)S(1)} collective-permute-done((bf16[16,512]{1,0:T(8,128)(2,1)S(1)}, bf16[16,512]{1,0:T(8,128)(2,1)S(1)}, u32[]{:S(2)}, u32[]{:S(2)}) %collective-permute-start.34) | collective-permute-done | bytes 16416 | tf_op jit(solution)/shard_map/ppermute | solution.py:487
  (63 shorter events, 23.4 us)
Async XLA Ops:
  2.4 9.5 %collective-permute-start = (bf16[16,3584]{1,0:T(8,128)(2,1)S(1)}, bf16[16,3584]{1,0:T(8,128)(2,1)S(1)}, u32[]{:S(2)}, u32[]{:S(2)}) collective-permute-start(bf16[16,3584]{1,0:T(8,128)(2,1)S(1)} %get-tuple-element.101), channel_id=1, source_target_pairs={{0,1},{1,0},{2,3},{3,2},{4,5},{5,4},{6,7},{7,6},{8,9},{9,8},{10,11... | collective-permute-start | bytes 344072 | tf_op jit(solution)/shard_map/ppermute | solution.py:487
  5.5 11.7 %collective-permute-start.1 = (bf16[16,3584]{1,0:T(8,128)(2,1)S(1)}, bf16[16,3584]{1,0:T(8,128)(2,1)S(1)}, u32[]{:S(2)}, u32[]{:S(2)}) collective-permute-start(bf16[16,3584]{1,0:T(8,128)(2,1)S(1)} %get-tuple-element.102), channel_id=1, source_target_pairs={{0,2},{1,3},{2,0},{3,1},{4,6},{5,7},{6,4},{7,5},{8,10},{9,11},{10,... | collective-permute-start | bytes 344072 | tf_op jit(solution)/shard_map/ppermute | solution.py:487
  8.1 9.1 %collective-permute-start.2 = (bf16[16,3584]{1,0:T(8,128)(2,1)S(1)}, bf16[16,3584]{1,0:T(8,128)(2,1)S(1)}, u32[]{:S(2)}, u32[]{:S(2)}) collective-permute-start(bf16[16,3584]{1,0:T(8,128)(2,1)S(1)} %get-tuple-element.103), channel_id=1, source_target_pairs={{0,3},{1,2},{2,1},{3,0},{4,7},{5,6},{6,5},{7,4},{8,11},{9,10},{10,... | collective-permute-start | bytes 344072 | tf_op jit(solution)/shard_map/ppermute | solution.py:487
  17.4 5.3 %collective-permute-start.6 = (bf16[16,3072]{1,0:T(8,128)(2,1)S(1)}, bf16[16,3072]{1,0:T(8,128)(2,1)S(1)}, u32[]{:S(2)}, u32[]{:S(2)}) collective-permute-start(bf16[16,3072]{1,0:T(8,128)(2,1)S(1)} %get-tuple-element.108), channel_id=1, source_target_pairs={{0,1},{1,0},{2,3},{3,2},{4,5},{5,4},{6,7},{7,6},{8,9},{9,8},{10,11... | collective-permute-start | bytes 294920 | tf_op jit(solution)/shard_map/ppermute | solution.py:234
  19.2 12.9 %collective-permute-start.5 = (bf16[48,3072]{1,0:T(8,128)(2,1)S(1)}, bf16[48,3072]{1,0:T(8,128)(2,1)S(1)}, u32[]{:S(2)}, u32[]{:S(2)}) collective-permute-start(bf16[48,3072]{1,0:T(8,128)(2,1)S(1)} %get-tuple-element.106.refs_9_.refs_14_.refs_4_), channel_id=1, source_target_pairs={{0,24},{4,28},{8,16},{12,20},{16,8},{20,12},{24,0},{28,4},{1,25},{... | collective-permute-start | bytes 884744 | tf_op jit(solution)/shard_map/ppermute | solution.py:191
  21.7 11.9 %collective-permute-start.4 = (bf16[48,3072]{1,0:T(8,128)(2,1)S(1)}, bf16[48,3072]{1,0:T(8,128)(2,1)S(1)}, u32[]{:S(2)}, u32[]{:S(2)}) collective-permute-start(bf16[48,3072]{1,0:T(8,128)(2,1)S(1)} %get-tuple-element.106.refs_9_.refs_14_.refs_4_), channel_id=1, source_target_pairs={{0,16},{4,20},{8,24},{12,28},{16,0},{20,4},{24,8},{28,12},{1,17},{... | collective-permute-start | bytes 884744 | tf_op jit(solution)/shard_map/ppermute | solution.py:191
  22.2 12.6 %collective-permute-start.3 = (bf16[48,3584]{1,0:T(8,128)(2,1)S(1)}, bf16[48,3584]{1,0:T(8,128)(2,1)S(1)}, u32[]{:S(2)}, u32[]{:S(2)}) collective-permute-start(bf16[48,3584]{1,0:T(8,128)(2,1)S(1)} %get-tuple-element.109), channel_id=1, source_target_pairs={{0,8},{4,12},{8,0},{12,4},{16,24},{20,28},{24,16},{28,20},{1,9},{5... | collective-permute-start | bytes 1032200 | tf_op jit(solution)/shard_map/ppermute | solution.py:191
  22.7 9.4 %collective-permute-start.7 = (bf16[32,3072]{1,0:T(8,128)(2,1)S(1)}, bf16[32,3072]{1,0:T(8,128)(2,1)S(1)}, u32[]{:S(2)}, u32[]{:S(2)}) collective-permute-start(bf16[32,3072]{1,0:T(8,128)(2,1)S(1)} %pad_maximum_fusion.3), channel_id=1, source_target_pairs={{0,2},{1,3},{2,0},{3,1},{4,6},{5,7},{6,4},{7,5},{8,10},{9,11},{10,... | collective-permute-start | bytes 589832 | tf_op jit(solution)/shard_map/ppermute | solution.py:236
  35.5 14.8 %collective-permute-start.19 = (bf16[48,3072]{1,0:T(8,128)(2,1)S(1)}, bf16[48,3072]{1,0:T(8,128)(2,1)S(1)}, u32[]{:S(2)}, u32[]{:S(2)}) collective-permute-start(bf16[48,3072]{1,0:T(8,128)(2,1)S(1)} %pad_maximum_fusion.2.refs_9_.refs_4_), channel_id=1, source_target_pairs={{0,16},{4,20},{8,24},{12,28},{16,0},{20,4},{24,8},{28,12},{1,17},{... | collective-permute-start | bytes 884744 | tf_op jit(solution)/shard_map/ppermute | solution.py:191
  36.0 14.3 %collective-permute-start.18 = (bf16[48,3072]{1,0:T(8,128)(2,1)S(1)}, bf16[48,3072]{1,0:T(8,128)(2,1)S(1)}, u32[]{:S(2)}, u32[]{:S(2)}) collective-permute-start(bf16[48,3072]{1,0:T(8,128)(2,1)S(1)} %pad_maximum_fusion.2.refs_9_.refs_4_), channel_id=1, source_target_pairs={{0,8},{4,12},{8,0},{12,4},{16,24},{20,28},{24,16},{28,20},{1,9},{5... | collective-permute-start | bytes 884744 | tf_op jit(solution)/shard_map/ppermute | solution.py:191
  41.5 4.5 %collective-permute-start.11 = (bf16[16,512]{1,0:T(8,128)(2,1)S(1)}, bf16[16,512]{1,0:T(8,128)(2,1)S(1)}, u32[]{:S(2)}, u32[]{:S(2)}) collective-permute-start(bf16[16,512]{1,0:T(8,128)(2,1)S(1)} %get-tuple-element.119), channel_id=1, source_target_pairs={{0,1},{1,0},{2,3},{3,2},{4,5},{5,4},{6,7},{7,6},{8,9},{9,8},{10,11... | collective-permute-start | bytes 49160 | tf_op jit(solution)/shard_map/ppermute | solution.py:487
  41.9 5.5 %collective-permute-start.12 = (bf16[16,512]{1,0:T(8,128)(2,1)S(1)}, bf16[16,512]{1,0:T(8,128)(2,1)S(1)}, u32[]{:S(2)}, u32[]{:S(2)}) collective-permute-start(bf16[16,512]{1,0:T(8,128)(2,1)S(1)} %get-tuple-element.120), channel_id=1, source_target_pairs={{0,2},{1,3},{2,0},{3,1},{4,6},{5,7},{6,4},{7,5},{8,10},{9,11},{10,... | collective-permute-start | bytes 49160 | tf_op jit(solution)/shard_map/ppermute | solution.py:487
  44.6 5.5 %collective-permute-start.13 = (bf16[16,512]{1,0:T(8,128)(2,1)S(1)}, bf16[16,512]{1,0:T(8,128)(2,1)S(1)}, u32[]{:S(2)}, u32[]{:S(2)}) collective-permute-start(bf16[16,512]{1,0:T(8,128)(2,1)S(1)} %get-tuple-element.121), channel_id=1, source_target_pairs={{0,3},{1,2},{2,1},{3,0},{4,7},{5,6},{6,5},{7,4},{8,11},{9,10},{10,... | collective-permute-start | bytes 49160 | tf_op jit(solution)/shard_map/ppermute | solution.py:487
  45.9 9.8 %collective-permute-start.21 = (bf16[48,3072]{1,0:T(8,128)(2,1)S(1)}, bf16[48,3072]{1,0:T(8,128)(2,1)S(1)}, u32[]{:S(2)}, u32[]{:S(2)}) collective-permute-start(bf16[48,3072]{1,0:T(8,128)(2,1)S(1)} %pad_maximum_fusion.2.refs_9_.refs_4_), channel_id=1, source_target_pairs={{0,24},{4,28},{8,16},{12,20},{16,8},{20,12},{24,0},{28,4},{1,25},{... | collective-permute-start | bytes 884744 | tf_op jit(solution)/shard_map/ppermute | solution.py:191
  50.4 7.0 %collective-permute-start.20 = (bf16[96,3072]{1,0:T(8,128)(2,1)S(1)}, bf16[96,3072]{1,0:T(8,128)(2,1)S(1)}, u32[]{:S(2)}, u32[]{:S(2)}) collective-permute-start(bf16[96,3072]{1,0:T(8,128)(2,1)S(1)} %pad_maximum_fusion.1), channel_id=1, source_target_pairs={{0,4},{4,0},{8,12},{12,8},{16,20},{20,16},{24,28},{28,24},{1,5},{5... | collective-permute-start | bytes 1769480 | tf_op jit(solution)/shard_map/ppermute | solution.py:191
  50.9 3.9 %collective-permute-start.15 = (bf16[16,512]{1,0:T(8,128)(2,1)S(1)}, bf16[16,512]{1,0:T(8,128)(2,1)S(1)}, u32[]{:S(2)}, u32[]{:S(2)}) collective-permute-start(bf16[16,512]{1,0:T(8,128)(2,1)S(1)} %get-tuple-element.124), channel_id=1, source_target_pairs={{0,8},{4,12},{8,0},{12,4},{1,9},{5,13},{9,1},{13,5},{2,10},{6,14},... | collective-permute-start | bytes 49160 | tf_op jit(solution)/shard_map/ppermute | solution.py:493
  62.9 3.8 %collective-permute-start.24 = (bf16[16,512]{1,0:T(8,128)(2,1)S(1)}, bf16[16,512]{1,0:T(8,128)(2,1)S(1)}, u32[]{:S(2)}, u32[]{:S(2)}) collective-permute-start(bf16[16,512]{1,0:T(8,128)(2,1)S(1)} %get-tuple-element.139), channel_id=1, source_target_pairs={{0,8},{4,12},{8,0},{12,4},{1,9},{5,13},{9,1},{13,5},{2,10},{6,14},... | collective-permute-start | bytes 49160 | tf_op jit(solution)/shard_map/ppermute | solution.py:493
  67.2 5.0 %collective-permute-start.26 = (bf16[16,512]{1,0:T(8,128)(2,1)S(1)}, bf16[16,512]{1,0:T(8,128)(2,1)S(1)}, u32[]{:S(2)}, u32[]{:S(2)}) collective-permute-start(bf16[16,512]{1,0:T(8,128)(2,1)S(1)} %get-tuple-element.142), channel_id=1, source_target_pairs={{0,1},{1,0},{2,3},{3,2},{4,5},{5,4},{6,7},{7,6},{8,9},{9,8},{10,11... | collective-permute-start | bytes 49160 | tf_op jit(solution)/shard_map/ppermute | solution.py:487
  67.3 5.1 %collective-permute-start.27 = (bf16[16,512]{1,0:T(8,128)(2,1)S(1)}, bf16[16,512]{1,0:T(8,128)(2,1)S(1)}, u32[]{:S(2)}, u32[]{:S(2)}) collective-permute-start(bf16[16,512]{1,0:T(8,128)(2,1)S(1)} %get-tuple-element.143), channel_id=1, source_target_pairs={{0,2},{1,3},{2,0},{3,1},{4,6},{5,7},{6,4},{7,5},{8,10},{9,11},{10,... | collective-permute-start | bytes 49160 | tf_op jit(solution)/shard_map/ppermute | solution.py:487
  70.5 5.5 %collective-permute-start.28 = (bf16[16,512]{1,0:T(8,128)(2,1)S(1)}, bf16[16,512]{1,0:T(8,128)(2,1)S(1)}, u32[]{:S(2)}, u32[]{:S(2)}) collective-permute-start(bf16[16,512]{1,0:T(8,128)(2,1)S(1)} %get-tuple-element.144), channel_id=1, source_target_pairs={{0,3},{1,2},{2,1},{3,0},{4,7},{5,6},{6,5},{7,4},{8,11},{9,10},{10,... | collective-permute-start | bytes 49160 | tf_op jit(solution)/shard_map/ppermute | solution.py:487
  78.2 3.8 %collective-permute-start.30 = (bf16[16,512]{1,0:T(8,128)(2,1)S(1)}, bf16[16,512]{1,0:T(8,128)(2,1)S(1)}, u32[]{:S(2)}, u32[]{:S(2)}) collective-permute-start(bf16[16,512]{1,0:T(8,128)(2,1)S(1)} %get-tuple-element.159), channel_id=1, source_target_pairs={{0,8},{4,12},{8,0},{12,4},{1,9},{5,13},{9,1},{13,5},{2,10},{6,14},... | collective-permute-start | bytes 49160 | tf_op jit(solution)/shard_map/ppermute | solution.py:493
  82.3 5.8 %collective-permute-start.32 = (bf16[16,512]{1,0:T(8,128)(2,1)S(1)}, bf16[16,512]{1,0:T(8,128)(2,1)S(1)}, u32[]{:S(2)}, u32[]{:S(2)}) collective-permute-start(bf16[16,512]{1,0:T(8,128)(2,1)S(1)} %get-tuple-element.162), channel_id=1, source_target_pairs={{0,1},{1,0},{2,3},{3,2},{4,5},{5,4},{6,7},{7,6},{8,9},{9,8},{10,11... | collective-permute-start | bytes 49160 | tf_op jit(solution)/shard_map/ppermute | solution.py:487
  82.4 5.7 %collective-permute-start.33 = (bf16[16,512]{1,0:T(8,128)(2,1)S(1)}, bf16[16,512]{1,0:T(8,128)(2,1)S(1)}, u32[]{:S(2)}, u32[]{:S(2)}) collective-permute-start(bf16[16,512]{1,0:T(8,128)(2,1)S(1)} %get-tuple-element.163), channel_id=1, source_target_pairs={{0,2},{1,3},{2,0},{3,1},{4,6},{5,7},{6,4},{7,5},{8,10},{9,11},{10,... | collective-permute-start | bytes 49160 | tf_op jit(solution)/shard_map/ppermute | solution.py:487
  84.5 5.5 %collective-permute-start.34 = (bf16[16,512]{1,0:T(8,128)(2,1)S(1)}, bf16[16,512]{1,0:T(8,128)(2,1)S(1)}, u32[]{:S(2)}, u32[]{:S(2)}) collective-permute-start(bf16[16,512]{1,0:T(8,128)(2,1)S(1)} %get-tuple-element.164), channel_id=1, source_target_pairs={{0,3},{1,2},{2,1},{3,0},{4,7},{5,6},{6,5},{7,4},{8,11},{9,10},{10,... | collective-permute-start | bytes 49160 | tf_op jit(solution)/shard_map/ppermute | solution.py:487
  (11 other events, 28.7 us)

commit v17 on v15

--- a/solution.py
+++ b/solution.py
@@ -121,9 +121,9 @@
     return dot_trans(select, first).astype(BF16)
 
 
-def prepare_kernel(grid, send, shards, table_out, kept, *messages):
+def prepare_kernel(grid, send, shards, kept, *messages):
     width = 3 * FEATURES
-    outgoing = send_rows(grid, send, table_out)
+    outgoing = send_rows(grid, send)
     size = kept.ref.shape[0]
     kept.ref[...] = outgoing[:size, :].astype(BF16)
     for i, out in enumerate(messages):
@@ -195,24 +195,24 @@
     grid_rows, features = grid_lat.shape
     mp, graph = lax.axis_size("mp"), lax.axis_size("graph")
     step = stride(grid_send.shape[1])
-    sent = [shape(grid_rows, mp * graph * step, BF16)] + [shape(graph * step, features, BF16)] * mp
+    sent = [shape(graph * step, features, BF16)] * mp
     planes = lax.axis_size("groups") * graph
     hidden = shards[1].shape[0]
     if planes != 8 or mp != 4 or hidden != 128 or features != FEATURES:
-        grid_t, *outgoing = call(send_kernel, sent, Far(grid_lat), Far(grid_send.T))
+        outgoing = call(send_kernel, sent, Far(grid_lat), Far(grid_send.T))
         rows = []
         for i in range(4):
             rows.append(lax.all_gather(shards[2 * i], "mp", axis=1, tiled=True).T)
             rows.append(lax.all_gather(shards[2 * i + 1], "mp", axis=0, tiled=True))
         enc, proc = jnp.concatenate(rows[:4], axis=1), jnp.concatenate(rows[4:], axis=1)
         arrived = exchange(outgoing, step)
-        return [enc], lambda one, moved, came: [proc], arrived, grid_t, tables
+        return [enc], lambda one, moved, came: [proc], arrived, tables
     far = [Far(s) for s in shards]
     piece = hidden // planes
     width = 6 * features
-    grid_t, kept, *messages = call(
+    kept, *messages = call(
         prepare_kernel,
-        sent[:2] + [shape(piece, width + features, BF16)] * 3,
+        sent[:1] + [shape(piece, width + features, BF16)] * 3,
         Far(grid_lat),
         Far(grid_send.T),
         far[:4],
@@ -220,7 +220,7 @@
     enc_own, proc_own, proc_piece = call(
         own_kernel, [shape(hidden, width, BF16)] * 2 + [shape(piece, width, BF16)], far
     )
-    messages = [along(m, i + 1) for i, m in enumerate(messages)]
+    messages = [along(m, i + 1, True) for i, m in enumerate(messages)]
     kept, enc_own, *tables = lax.optimization_barrier((kept, enc_own, *tables))
     rows = mp * step
     near, first, both = call(
@@ -250,7 +250,7 @@
         corner, *_ = lax.optimization_barrier((corner, *came))
         return [proc_own, proc_first, across(proc_first, 1), x, y, sides, corner, across(corner, 1)]
 
-    return enc, finish, arrived, grid_t, tables
+    return enc, finish, arrived, tables
 
 
 def forward(inputs, first, second):
@@ -285,26 +285,29 @@
     return max(capacity, 16 // min(lax.axis_size("mp"), lax.axis_size("graph")))
 
 
-def sent_at(peer, slot, step):
+def sent_at(peer, slot, step, paired=False):
     mp, graph = lax.axis_size("mp"), lax.axis_size("graph")
-    shift = (peer % mp + mp - lax.axis_index("mp")) % mp
+    me, other = lax.axis_index("mp"), peer % mp
+    shift = other ^ me if paired else (other + mp - me) % mp
     return (shift * graph + (peer // mp ^ lax.axis_index("graph"))) * step + slot
 
 
-def arrived_at(peer, slot, step):
+def arrived_at(peer, slot, step, paired=False):
     mp = lax.axis_size("mp")
-    shift = (lax.axis_index("mp") + mp - peer % mp) % mp
+    me, other = lax.axis_index("mp"), peer % mp
+    shift = other ^ me if paired else (me + mp - other) % mp
     return ((peer // mp ^ lax.axis_index("graph")) * mp + shift) * step + slot
 
 
-def sent_row(index, step):
+def sent_row(index, step, paired=False):
     width, count = index.shape
     index = index.astype(F32).T
     at = lax.broadcasted_iota(jnp.int32, (count, count * step), 1)
     peer = lax.broadcasted_iota(jnp.int32, (count, count * step), 0)
     row = jnp.zeros(at.shape, F32)
     for slot in range(width):
-        row = jnp.where(sent_at(peer, slot, step) == at, index[:, slot : slot + 1] + 1.0, row)
+        hit = sent_at(peer, slot, step, paired) == at
+        row = jnp.where(hit, index[:, slot : slot + 1] + 1.0, row)
     return jnp.sum(row, axis=0, keepdims=True).astype(jnp.int32) - 1
 
 
@@ -318,15 +321,14 @@
         out.ref[...] = rows[i * size : (i + 1) * size, :].astype(BF16)
 
 
-def send_rows(grid, send, table_out):
-    count = table_out.ref.shape[1]
-    one = table(sent_row(send()[...], count // send().shape[1]), grid().shape[0])
-    table_out.ref[...] = one.astype(BF16)
+def send_rows(grid, send):
+    index = send()[...]
+    one = table(sent_row(index, stride(index.shape[0]), True), grid().shape[0])
     return dot(one.T.astype(BF16), grid()[...])
 
 
-def send_kernel(grid, send, table_out, *outgoing):
-    split(send_rows(grid, send, table_out), outgoing)
+def send_kernel(grid, send, *outgoing):
+    split(send_rows(grid, send), outgoing)
 
 
 def turn_table(sources, targets, step, j):
@@ -343,12 +345,13 @@
         out.ref[...] = dot(turn_table(len(blocks), len(outs), step, j), rows).astype(BF16)
 
 
-def tables_kernel(mesh, slot, recv_e, halo, sender, recv_p, *outs):
+def tables_kernel(mesh, slot, recv_e, halo, sender, recv_p, send, *outs):
     mesh_rows = mesh().shape[0]
     peers = halo().shape[1]
     slot_step, halo_step = outs[0].ref.shape[0] // peers, outs[4].ref.shape[1] // peers
     capacity, halo_capacity = slot_step, halo().shape[0]
     slots = slot()[...]
+    coming = arrived_at(slots // capacity, slots % capacity, slot_step, True)
     slots = arrived_at(slots // capacity, slots % capacity, slot_step)
     senders = sender()[...]
     remote = jnp.maximum(senders - mesh_rows, 0)
@@ -359,8 +362,9 @@
         scatter, gather = outs[2 * i : 2 * i + 2]
         one = table(row, scatter.ref.shape[0])
         scatter.ref[...] = one.astype(BF16)
-        gather.ref[...] = one.T.astype(BF16)
+        gather.ref[...] = (table(coming, slot_step * peers) if i == 0 else one).T.astype(BF16)
     outs[10].ref[...] = dot(outs[3].ref[...], mesh()[...]).astype(BF16)
+    outs[11].ref[...] = table(sent_row(send()[...], slot_step), outs[11].ref.shape[0]).astype(BF16)
 
 
 def arrived_rows(blocks):
@@ -477,11 +481,12 @@
     out.send(dot(table_in()[...], stacked(back)))
 
 
-def along(block, shift):
+def along(block, shift, paired=False):
     size = lax.axis_size("mp")
     if shift % size == 0:
         return block
-    return lax.ppermute(block, "mp", [(m, (m + shift) % size) for m in range(size)])
+    to = [m ^ shift if paired else (m + shift) % size for m in range(size)]
+    return lax.ppermute(block, "mp", list(enumerate(to)))
 
 
 def beside(block, flip):
@@ -496,11 +501,11 @@
 
 
 def exchange(blocks, step):
-    return second_level(first_level(blocks, step))
-
-
-def first_level(blocks, step):
-    return turn([along(b, s) for s, b in enumerate(blocks)], lax.axis_size("graph"), step)
+    return second_level(first_level(blocks, step, True))
+
+
+def first_level(blocks, step, paired=False):
+    return turn([along(b, s, paired) for s, b in enumerate(blocks)], lax.axis_size("graph"), step)
 
 
 def second_level(blocks):
@@ -545,6 +550,7 @@
             shape(mesh_rows, mesh_edges, BF16),
             shape(mesh_edges, mesh_rows, BF16),
             shape(edges, features, BF16),
+            shape(grid_rows, slots, BF16),
         ],
         Far(mesh_lat),
         Far(g2m_slot.reshape(1, edges)),
@@ -552,9 +558,11 @@
         Far(halo_send.T),
         Far(mesh_sender.reshape(1, mesh_edges)),
         Far(mesh_receiver.reshape(1, mesh_edges)),
-    )
-    enc, finish, arrived, grid_t, tables = start(grid_lat, grid_send, shards, tables)
-    slot_t, slot_g, enc_t, enc_g, halo_t, halo_g, sender_t, sender_g, proc_t, proc_g, recv_rows = tables
+        Far(grid_send.T),
+    )
+    enc, finish, arrived, tables = start(grid_lat, grid_send, shards, tables)
+    slot_t, slot_g, enc_t, enc_g, halo_t, halo_g, sender_t, sender_g, proc_t, proc_g = tables[:10]
+    recv_rows, grid_t = tables[10:]
     saved = [
         shape(edges, features, BF16),
         shape(edges, features, BF16),

time: 90.9 us -> 89.8 us (0.988)
  starting transfers between devices: 34.8 us -> 33.8 us
    ppermute x1, waiting for transfers between devices: 9.26 us -> 7.12 us  [start(): pairs = lax.ppermute(pair, 'mp', [(m, m ^ 2) for m in range(mp)])]
    ppermute x12, waiting for transfers between devices: 10.9 us -> 12.6 us  [along(): return lax.ppermute(block, 'mp', list(enumerate(to)))]
    ppermute x1, starting transfers between devices: 2.99 us -> 1.85 us  [start(): beside_me = lax.ppermute(proc_piece, 'mp', [(m, m ^ 1) for m in range(mp)])]
  transfers between devices with their start and end apart: 35 -> 35, of which waited for: 20 -> 19; matrix products, arithmetic and copies ran while one was open for 0% -> 0% of each run, Pallas kernels for 10% -> 11%
where the time goes in v17:
time: 89.8 us; the launch traced here: 89.5 us
  waiting for transfers between devices  34.1 us (38%)
  starting transfers between devices  33.8 us (38%)
  Pallas kernels  20.7 us (23%)
    pallas_call x13, Pallas kernels, call(): pl.pallas_call(body, out_shape=out_shape, in_specs=[hbm if away else vmem...  20.7 us
    ppermute x12, starting transfers between devices, along(): return lax.ppermute(block, 'mp', list(enumerate(to)))  15.6 us
    ppermute x12, waiting for transfers between devices, along(): return lax.ppermute(block, 'mp', list(enumerate(to)))  12.6 us
    ppermute x9, waiting for transfers between devices, beside(): lax.ppermute(block, 'graph', [(g, g ^ flip) for g in range(lax.axis_size(...  9.54 us
    ppermute x12, starting transfers between devices, across(): lax.ppermute(x, ('groups', 'graph'), [(p, p ^ flip) for p in range(planes)])  8.33 us
    ppermute x1, waiting for transfers between devices, start(): pairs = lax.ppermute(pair, 'mp', [(m, m ^ 2) for m in range(mp)])  7.12 us
    ppermute x9, starting transfers between devices, beside(): lax.ppermute(block, 'graph', [(g, g ^ flip) for g in range(lax.axis_size(...  5.78 us
    ppermute x12, waiting for transfers between devices, across(): lax.ppermute(x, ('groups', 'graph'), [(p, p ^ flip) for p in range(planes)])  4.84 us
  transfers between devices with their start and end apart: 35, of which 19 were waited for; matrix products, arithmetic and copies ran while one was open for 0% of the time, Pallas kernels for 11%

profile of v17, /device:TPU:0, one launch (start us, length us, event | category | flops | bytes accessed | tf_op | source)
XLA Modules:
  0.0 89.5 jit_solution(1708759060880524286)
XLA Ops:
  0.6 1.7 %prepare_kernel.1 = (bf16[16,512]{1,0:T(8,128)(2,1)S(1)}, bf16[16,3584]{1,0:T(8,128)(2,1)S(1)}, bf16[16,3584]{1,0:T(8,128)(2,1)S(1)}, bf16[16,3584]{1,0:T(8,128)(2,1)S(1)}) custom-call(bf16[512,512]{1,0:T(8,128)(2,1)} %refs_0_.4, s32[4,16]{1,0:T(4,128)} %bitcast.6, bf16[1024,128]{1,0:T(8,128)(2,1)} %refs_0_.5, bf16[128,512]{1,0:T(8,128)(2,1)} %refs_1_.1, ...), custom_call_target="tpu_custom_call" | custom-call | bytes 1310976 | tf_op jit(solution)/shard_map/prepare_kernel/pallas_call | solution.py:96
  2.4 3.1 %collective-permute-start = (bf16[16,3584]{1,0:T(8,128)(2,1)S(1)}, bf16[16,3584]{1,0:T(8,128)(2,1)S(1)}, u32[]{:S(2)}, u32[]{:S(2)}) collective-permute-start(bf16[16,3584]{1,0:T(8,128)(2,1)S(1)} %get-tuple-element.103), channel_id=1, source_target_pairs={{0,1},{1,0},{2,3},{3,2},{4,5},{5,4},{6,7},{7,6},{8,9},{9,8},{10,11... | collective-permute-start | bytes 344072 | tf_op jit(solution)/shard_map/ppermute | solution.py:489
  5.5 2.6 %collective-permute-start.1 = (bf16[16,3584]{1,0:T(8,128)(2,1)S(1)}, bf16[16,3584]{1,0:T(8,128)(2,1)S(1)}, u32[]{:S(2)}, u32[]{:S(2)}) collective-permute-start(bf16[16,3584]{1,0:T(8,128)(2,1)S(1)} %get-tuple-element.104), channel_id=1, source_target_pairs={{0,2},{1,3},{2,0},{3,1},{4,6},{5,7},{6,4},{7,5},{8,10},{9,11},{10,... | collective-permute-start | bytes 344072 | tf_op jit(solution)/shard_map/ppermute | solution.py:489
  8.1 2.1 %own_kernel.1 = (bf16[128,3072]{1,0:T(8,128)(2,1)S(1)}, bf16[128,3072]{1,0:T(8,128)(2,1)S(1)}, bf16[16,3072]{1,0:T(8,128)(2,1)S(1)}) custom-call(bf16[1024,128]{1,0:T(8,128)(2,1)} %refs_0_.5, bf16[128,512]{1,0:T(8,128)(2,1)} %refs_1_.1, bf16[1024,128]{1,0:T(8,128)(2,1)} %refs_2_.3, bf16[128,512]{1,0:T(8,128)(2,1)} %refs_3_.3, bf16[1024,128]{1,0:T(8,128)(2,1)} %refs_4_.3, ...), custom_call_target="tpu_custom_call" | custom-call | bytes 1572864 | tf_op jit(solution)/shard_map/own_kernel/pallas_call | solution.py:96
  10.2 2.0 %tables_kernel.1 = (bf16[64,512]{1,0:T(8,128)(2,1)S(1)}, bf16[512,64]{1,0:T(8,128)(2,1)S(1)}, bf16[256,512]{1,0:T(8,128)(2,1)S(1)}, bf16[512,256]{1,0:T(8,128)(2...) custom-call(bf16[256,512]{1,0:T(8,128)(2,1)} %refs_7_.3, ...), custom_call_target="tpu_custom_call" | custom-call | bytes 270720 | tf_op jit(solution)/shard_map/tables_kernel/pallas_call | solution.py:96
  12.2 5.0 %collective-permute-done.1.refs_2_ = bf16[16,3584]{1,0:T(8,128)(2,1)S(1)} collective-permute-done((bf16[16,3584]{1,0:T(8,128)(2,1)S(1)}, bf16[16,3584]{1,0:T(8,128)(2,1)S(1)}, u32[]{:S(2)}, u32[]{:S(2)}) %collective-permute-start.1) | collective-permute-done | bytes 114720 | tf_op jit(solution)/shard_map/ppermute | solution.py:489
  17.4 1.9 %collective-permute-start.6 = (bf16[16,3072]{1,0:T(8,128)(2,1)S(1)}, bf16[16,3072]{1,0:T(8,128)(2,1)S(1)}, u32[]{:S(2)}, u32[]{:S(2)}) collective-permute-start(bf16[16,3072]{1,0:T(8,128)(2,1)S(1)} %get-tuple-element.110), channel_id=1, source_target_pairs={{0,1},{1,0},{2,3},{3,2},{4,5},{5,4},{6,7},{7,6},{8,9},{9,8},{10,11... | collective-permute-start | bytes 294920 | tf_op jit(solution)/shard_map/ppermute | solution.py:234
  19.2 2.5 %collective-permute-start.5 = (bf16[48,3072]{1,0:T(8,128)(2,1)S(1)}, bf16[48,3072]{1,0:T(8,128)(2,1)S(1)}, u32[]{:S(2)}, u32[]{:S(2)}) collective-permute-start(bf16[48,3072]{1,0:T(8,128)(2,1)S(1)} %get-tuple-element.108.refs_9_.refs_14_.refs_4_), channel_id=1, source_target_pairs={{0,24},{4,28},{8,16},{12,20},{16,8},{20,12},{24,0},{28,4},{1,25},{... | collective-permute-start | bytes 884744 | tf_op jit(solution)/shard_map/ppermute | solution.py:191
  22.7 2.3 %collective-permute-start.7 = (bf16[32,3072]{1,0:T(8,128)(2,1)S(1)}, bf16[32,3072]{1,0:T(8,128)(2,1)S(1)}, u32[]{:S(2)}, u32[]{:S(2)}) collective-permute-start(bf16[32,3072]{1,0:T(8,128)(2,1)S(1)} %pad_maximum_fusion.3), channel_id=1, source_target_pairs={{0,2},{1,3},{2,0},{3,1},{4,6},{5,7},{6,4},{7,5},{8,10},{9,11},{10,... | collective-permute-start | bytes 589832 | tf_op jit(solution)/shard_map/ppermute | solution.py:236
  25.0 7.1 %collective-permute-done.7 = bf16[32,3072]{1,0:T(8,128)(2,1)S(1)} collective-permute-done((bf16[32,3072]{1,0:T(8,128)(2,1)S(1)}, bf16[32,3072]{1,0:T(8,128)(2,1)S(1)}, u32[]{:S(2)}, u32[]{:S(2)}) %collective-permute-start.7) | collective-permute-done | bytes 196640 | tf_op jit(solution)/shard_map/ppermute | solution.py:236
  32.1 1.5 %collective-permute-done.4.refs_12_.refs_17_.refs_7_ = bf16[48,3072]{1,0:T(8,128)(2,1)S(1)} collective-permute-done((bf16[48,3072]{1,0:T(8,128)(2,1)S(1)}, bf16[48,3072]{1,0:T(8,128)(2,1)S(1)}, u32[]{:S(2)}, u32[]{:S(2)}) %collective-permute-start.4) | collective-permute-done | bytes 294944 | tf_op jit(solution)/shard_map/ppermute | solution.py:191
  36.0 1.5 %collective-permute-start.18 = (bf16[48,3072]{1,0:T(8,128)(2,1)S(1)}, bf16[48,3072]{1,0:T(8,128)(2,1)S(1)}, u32[]{:S(2)}, u32[]{:S(2)}) collective-permute-start(bf16[48,3072]{1,0:T(8,128)(2,1)S(1)} %pad_maximum_fusion.2.refs_9_.refs_4_), channel_id=1, source_target_pairs={{0,8},{4,12},{8,0},{12,4},{16,24},{20,28},{24,16},{28,20},{1,9},{5... | collective-permute-start | bytes 884744 | tf_op jit(solution)/shard_map/ppermute | solution.py:191
  37.9 3.6 %encode_kernel.1 = (bf16[256,512]{1,0:T(8,128)(2,1)S(1)}, bf16[512,512]{1,0:T(8,128)(2,1)S(1)}, bf16[512,512]{1,0:T(8,128)(2,1)S(1)}, f32[512,128]{1,0:T(8,128)S...) custom-call(bf16[512,512]{1,0:T(8,128)(2,1)S(1)} %get-tuple-element., ...), custom_call_target="tpu_custom_call" | custom-call | flops 3000000000 | bytes 5488640 | tf_op jit(solution)/shard_map/encode_kernel/pallas_call | solution.py:96
  41.9 2.7 %collective-permute-start.12 = (bf16[16,512]{1,0:T(8,128)(2,1)S(1)}, bf16[16,512]{1,0:T(8,128)(2,1)S(1)}, u32[]{:S(2)}, u32[]{:S(2)}) collective-permute-start(bf16[16,512]{1,0:T(8,128)(2,1)S(1)} %get-tuple-element.122), channel_id=1, source_target_pairs={{0,2},{1,3},{2,0},{3,1},{4,6},{5,7},{6,4},{7,5},{8,10},{9,11},{10,... | collective-permute-start | bytes 49160 | tf_op jit(solution)/shard_map/ppermute | solution.py:489
  51.5 4.4 %collective-permute-done.15.refs_4_ = bf16[16,512]{1,0:T(8,128)(2,1)S(1)} collective-permute-done((bf16[16,512]{1,0:T(8,128)(2,1)S(1)}, bf16[16,512]{1,0:T(8,128)(2,1)S(1)}, u32[]{:S(2)}, u32[]{:S(2)}) %collective-permute-start.15) | collective-permute-done | bytes 16416 | tf_op jit(solution)/shard_map/ppermute | solution.py:495
  56.2 1.6 %collective-permute-done.22.refs_15_.refs_10_ = bf16[48,3072]{1,0:T(8,128)(2,1)S(1)} collective-permute-done((bf16[48,3072]{1,0:T(8,128)(2,1)S(1)}, bf16[48,3072]{1,0:T(8,128)(2,1)S(1)}, u32[]{:S(2)}, u32[]{:S(2)}) %collective-permute-start.22) | collective-permute-done | bytes 294944 | tf_op jit(solution)/shard_map/ppermute | solution.py:191
  57.8 5.3 %process_kernel.1 = (bf16[256,512]{1,0:T(8,128)(2,1)}, f32[256,512]{1,0:T(8,128)S(1)}, bf16[512,512]{1,0:T(8,128)(2,1)S(1)}, bf16[16,512]{1,0:T(8,128)(2,1)S(1)}...) custom-call(bf16[256,512]{1,0:T(8,128)(2,1)} %refs_0_.7, ...), custom_call_target="tpu_custom_call" | custom-call | flops 5000000000 | bytes 4915200 | tf_op jit(solution)/shard_map/process_kernel/pallas_call | solution.py:96
  63.3 1.5 %collective-permute-start.24 = (bf16[16,512]{1,0:T(8,128)(2,1)S(1)}, bf16[16,512]{1,0:T(8,128)(2,1)S(1)}, u32[]{:S(2)}, u32[]{:S(2)}) collective-permute-start(bf16[16,512]{1,0:T(8,128)(2,1)S(1)} %get-tuple-element.141), channel_id=1, source_target_pairs={{0,8},{4,12},{8,0},{12,4},{1,9},{5,13},{9,1},{13,5},{2,10},{6,14},... | collective-permute-start | bytes 49160 | tf_op jit(solution)/shard_map/ppermute | solution.py:495
  65.0 2.0 %collective-permute-done.24.refs_2_ = bf16[16,512]{1,0:T(8,128)(2,1)S(1)} collective-permute-done((bf16[16,512]{1,0:T(8,128)(2,1)S(1)}, bf16[16,512]{1,0:T(8,128)(2,1)S(1)}, u32[]{:S(2)}, u32[]{:S(2)}) %collective-permute-start.24) | collective-permute-done | bytes 16416 | tf_op jit(solution)/shard_map/ppermute | solution.py:495
  72.0 1.9 %collective-permute-done.27.refs_2_ = bf16[16,512]{1,0:T(8,128)(2,1)S(1)} collective-permute-done((bf16[16,512]{1,0:T(8,128)(2,1)S(1)}, bf16[16,512]{1,0:T(8,128)(2,1)S(1)}, u32[]{:S(2)}, u32[]{:S(2)}) %collective-permute-start.27) | collective-permute-done | bytes 16416 | tf_op jit(solution)/shard_map/ppermute | solution.py:489
  75.1 2.1 %decode_kernel.1 = (f32[256,512]{1,0:T(8,128)S(1)}, bf16[512,512]{1,0:T(8,128)(2,1)S(1)}, bf16[16,512]{1,0:T(8,128)(2,1)S(1)}, bf16[16,512]{1,0:T(8,128)(2,1)S(1...) custom-call(bf16[16,512]{1,0:T(8,128)(2,1)S(1)} %get-tuple-element.143.refs_0_, ...), custom_call_target="tpu_custom_call" | custom-call | flops 3000000000 | bytes 6209536 | tf_op jit(solution)/shard_map/decode_kernel/pallas_call | solution.py:96
  79.1 2.0 %collective-permute-done.30.refs_2_ = bf16[16,512]{1,0:T(8,128)(2,1)S(1)} collective-permute-done((bf16[16,512]{1,0:T(8,128)(2,1)S(1)}, bf16[16,512]{1,0:T(8,128)(2,1)S(1)}, u32[]{:S(2)}, u32[]{:S(2)}) %collective-permute-start.30) | collective-permute-done | bytes 16416 | tf_op jit(solution)/shard_map/ppermute | solution.py:495
  82.7 1.5 %collective-permute-start.34 = (bf16[16,512]{1,0:T(8,128)(2,1)S(1)}, bf16[16,512]{1,0:T(8,128)(2,1)S(1)}, u32[]{:S(2)}, u32[]{:S(2)}) collective-permute-start(bf16[16,512]{1,0:T(8,128)(2,1)S(1)} %get-tuple-element.166), channel_id=1, source_target_pairs={{0,1},{1,2},{2,3},{3,0},{4,5},{5,6},{6,7},{7,4},{8,9},{9,10},{10,1... | collective-permute-start | bytes 49160 | tf_op jit(solution)/shard_map/ppermute | solution.py:489
  85.6 1.8 %collective-permute-done.33.refs_2_ = bf16[16,512]{1,0:T(8,128)(2,1)S(1)} collective-permute-done((bf16[16,512]{1,0:T(8,128)(2,1)S(1)}, bf16[16,512]{1,0:T(8,128)(2,1)S(1)}, u32[]{:S(2)}, u32[]{:S(2)}) %collective-permute-start.33) | collective-permute-done | bytes 16416 | tf_op jit(solution)/shard_map/ppermute | solution.py:489
  (63 shorter events, 25.2 us)
Async XLA Ops:
  2.4 9.8 %collective-permute-start = (bf16[16,3584]{1,0:T(8,128)(2,1)S(1)}, bf16[16,3584]{1,0:T(8,128)(2,1)S(1)}, u32[]{:S(2)}, u32[]{:S(2)}) collective-permute-start(bf16[16,3584]{1,0:T(8,128)(2,1)S(1)} %get-tuple-element.103), channel_id=1, source_target_pairs={{0,1},{1,0},{2,3},{3,2},{4,5},{5,4},{6,7},{7,6},{8,9},{9,8},{10,11... | collective-permute-start | bytes 344072 | tf_op jit(solution)/shard_map/ppermute | solution.py:489
  5.5 11.7 %collective-permute-start.1 = (bf16[16,3584]{1,0:T(8,128)(2,1)S(1)}, bf16[16,3584]{1,0:T(8,128)(2,1)S(1)}, u32[]{:S(2)}, u32[]{:S(2)}) collective-permute-start(bf16[16,3584]{1,0:T(8,128)(2,1)S(1)} %get-tuple-element.104), channel_id=1, source_target_pairs={{0,2},{1,3},{2,0},{3,1},{4,6},{5,7},{6,4},{7,5},{8,10},{9,11},{10,... | collective-permute-start | bytes 344072 | tf_op jit(solution)/shard_map/ppermute | solution.py:489
  8.1 9.1 %collective-permute-start.2 = (bf16[16,3584]{1,0:T(8,128)(2,1)S(1)}, bf16[16,3584]{1,0:T(8,128)(2,1)S(1)}, u32[]{:S(2)}, u32[]{:S(2)}) collective-permute-start(bf16[16,3584]{1,0:T(8,128)(2,1)S(1)} %get-tuple-element.105), channel_id=1, source_target_pairs={{0,3},{1,2},{2,1},{3,0},{4,7},{5,6},{6,5},{7,4},{8,11},{9,10},{10,... | collective-permute-start | bytes 344072 | tf_op jit(solution)/shard_map/ppermute | solution.py:489
  17.4 5.3 %collective-permute-start.6 = (bf16[16,3072]{1,0:T(8,128)(2,1)S(1)}, bf16[16,3072]{1,0:T(8,128)(2,1)S(1)}, u32[]{:S(2)}, u32[]{:S(2)}) collective-permute-start(bf16[16,3072]{1,0:T(8,128)(2,1)S(1)} %get-tuple-element.110), channel_id=1, source_target_pairs={{0,1},{1,0},{2,3},{3,2},{4,5},{5,4},{6,7},{7,6},{8,9},{9,8},{10,11... | collective-permute-start | bytes 294920 | tf_op jit(solution)/shard_map/ppermute | solution.py:234
  19.2 12.9 %collective-permute-start.5 = (bf16[48,3072]{1,0:T(8,128)(2,1)S(1)}, bf16[48,3072]{1,0:T(8,128)(2,1)S(1)}, u32[]{:S(2)}, u32[]{:S(2)}) collective-permute-start(bf16[48,3072]{1,0:T(8,128)(2,1)S(1)} %get-tuple-element.108.refs_9_.refs_14_.refs_4_), channel_id=1, source_target_pairs={{0,24},{4,28},{8,16},{12,20},{16,8},{20,12},{24,0},{28,4},{1,25},{... | collective-permute-start | bytes 884744 | tf_op jit(solution)/shard_map/ppermute | solution.py:191
  21.7 11.9 %collective-permute-start.4 = (bf16[48,3072]{1,0:T(8,128)(2,1)S(1)}, bf16[48,3072]{1,0:T(8,128)(2,1)S(1)}, u32[]{:S(2)}, u32[]{:S(2)}) collective-permute-start(bf16[48,3072]{1,0:T(8,128)(2,1)S(1)} %get-tuple-element.108.refs_9_.refs_14_.refs_4_), channel_id=1, source_target_pairs={{0,16},{4,20},{8,24},{12,28},{16,0},{20,4},{24,8},{28,12},{1,17},{... | collective-permute-start | bytes 884744 | tf_op jit(solution)/shard_map/ppermute | solution.py:191
  22.2 12.6 %collective-permute-start.3 = (bf16[48,3584]{1,0:T(8,128)(2,1)S(1)}, bf16[48,3584]{1,0:T(8,128)(2,1)S(1)}, u32[]{:S(2)}, u32[]{:S(2)}) collective-permute-start(bf16[48,3584]{1,0:T(8,128)(2,1)S(1)} %get-tuple-element.111), channel_id=1, source_target_pairs={{0,8},{4,12},{8,0},{12,4},{16,24},{20,28},{24,16},{28,20},{1,9},{5... | collective-permute-start | bytes 1032200 | tf_op jit(solution)/shard_map/ppermute | solution.py:191
  22.7 9.4 %collective-permute-start.7 = (bf16[32,3072]{1,0:T(8,128)(2,1)S(1)}, bf16[32,3072]{1,0:T(8,128)(2,1)S(1)}, u32[]{:S(2)}, u32[]{:S(2)}) collective-permute-start(bf16[32,3072]{1,0:T(8,128)(2,1)S(1)} %pad_maximum_fusion.3), channel_id=1, source_target_pairs={{0,2},{1,3},{2,0},{3,1},{4,6},{5,7},{6,4},{7,5},{8,10},{9,11},{10,... | collective-permute-start | bytes 589832 | tf_op jit(solution)/shard_map/ppermute | solution.py:236
  35.5 13.2 %collective-permute-start.19 = (bf16[48,3072]{1,0:T(8,128)(2,1)S(1)}, bf16[48,3072]{1,0:T(8,128)(2,1)S(1)}, u32[]{:S(2)}, u32[]{:S(2)}) collective-permute-start(bf16[48,3072]{1,0:T(8,128)(2,1)S(1)} %pad_maximum_fusion.2.refs_9_.refs_4_), channel_id=1, source_target_pairs={{0,16},{4,20},{8,24},{12,28},{16,0},{20,4},{24,8},{28,12},{1,17},{... | collective-permute-start | bytes 884744 | tf_op jit(solution)/shard_map/ppermute | solution.py:191
  36.0 12.7 %collective-permute-start.18 = (bf16[48,3072]{1,0:T(8,128)(2,1)S(1)}, bf16[48,3072]{1,0:T(8,128)(2,1)S(1)}, u32[]{:S(2)}, u32[]{:S(2)}) collective-permute-start(bf16[48,3072]{1,0:T(8,128)(2,1)S(1)} %pad_maximum_fusion.2.refs_9_.refs_4_), channel_id=1, source_target_pairs={{0,8},{4,12},{8,0},{12,4},{16,24},{20,28},{24,16},{28,20},{1,9},{5... | collective-permute-start | bytes 884744 | tf_op jit(solution)/shard_map/ppermute | solution.py:191
  41.4 5.6 %collective-permute-start.11 = (bf16[16,512]{1,0:T(8,128)(2,1)S(1)}, bf16[16,512]{1,0:T(8,128)(2,1)S(1)}, u32[]{:S(2)}, u32[]{:S(2)}) collective-permute-start(bf16[16,512]{1,0:T(8,128)(2,1)S(1)} %get-tuple-element.121), channel_id=1, source_target_pairs={{0,1},{1,2},{2,3},{3,0},{4,5},{5,6},{6,7},{7,4},{8,9},{9,10},{10,1... | collective-permute-start | bytes 49160 | tf_op jit(solution)/shard_map/ppermute | solution.py:489
  41.9 6.7 %collective-permute-start.12 = (bf16[16,512]{1,0:T(8,128)(2,1)S(1)}, bf16[16,512]{1,0:T(8,128)(2,1)S(1)}, u32[]{:S(2)}, u32[]{:S(2)}) collective-permute-start(bf16[16,512]{1,0:T(8,128)(2,1)S(1)} %get-tuple-element.122), channel_id=1, source_target_pairs={{0,2},{1,3},{2,0},{3,1},{4,6},{5,7},{6,4},{7,5},{8,10},{9,11},{10,... | collective-permute-start | bytes 49160 | tf_op jit(solution)/shard_map/ppermute | solution.py:489
  44.6 4.0 %collective-permute-start.13 = (bf16[16,512]{1,0:T(8,128)(2,1)S(1)}, bf16[16,512]{1,0:T(8,128)(2,1)S(1)}, u32[]{:S(2)}, u32[]{:S(2)}) collective-permute-start(bf16[16,512]{1,0:T(8,128)(2,1)S(1)} %get-tuple-element.123), channel_id=1, source_target_pairs={{0,3},{1,0},{2,1},{3,2},{4,7},{5,4},{6,5},{7,6},{8,11},{9,8},{10,9... | collective-permute-start | bytes 49160 | tf_op jit(solution)/shard_map/ppermute | solution.py:489
  47.1 9.1 %collective-permute-start.21 = (bf16[48,3072]{1,0:T(8,128)(2,1)S(1)}, bf16[48,3072]{1,0:T(8,128)(2,1)S(1)}, u32[]{:S(2)}, u32[]{:S(2)}) collective-permute-start(bf16[48,3072]{1,0:T(8,128)(2,1)S(1)} %pad_maximum_fusion.2.refs_9_.refs_4_), channel_id=1, source_target_pairs={{0,24},{4,28},{8,16},{12,20},{16,8},{20,12},{24,0},{28,4},{1,25},{... | collective-permute-start | bytes 884744 | tf_op jit(solution)/shard_map/ppermute | solution.py:191
  48.8 9.0 %collective-permute-start.20 = (bf16[96,3072]{1,0:T(8,128)(2,1)S(1)}, bf16[96,3072]{1,0:T(8,128)(2,1)S(1)}, u32[]{:S(2)}, u32[]{:S(2)}) collective-permute-start(bf16[96,3072]{1,0:T(8,128)(2,1)S(1)} %pad_maximum_fusion.1), channel_id=1, source_target_pairs={{0,4},{4,0},{8,12},{12,8},{16,20},{20,16},{24,28},{28,24},{1,5},{5... | collective-permute-start | bytes 1769480 | tf_op jit(solution)/shard_map/ppermute | solution.py:191
  49.3 6.5 %collective-permute-start.15 = (bf16[16,512]{1,0:T(8,128)(2,1)S(1)}, bf16[16,512]{1,0:T(8,128)(2,1)S(1)}, u32[]{:S(2)}, u32[]{:S(2)}) collective-permute-start(bf16[16,512]{1,0:T(8,128)(2,1)S(1)} %get-tuple-element.126), channel_id=1, source_target_pairs={{0,8},{4,12},{8,0},{12,4},{1,9},{5,13},{9,1},{13,5},{2,10},{6,14},... | collective-permute-start | bytes 49160 | tf_op jit(solution)/shard_map/ppermute | solution.py:495
  50.6 5.3 %collective-permute-start.16 = (bf16[16,512]{1,0:T(8,128)(2,1)S(1)}, bf16[16,512]{1,0:T(8,128)(2,1)S(1)}, u32[]{:S(2)}, u32[]{:S(2)}) collective-permute-start(bf16[16,512]{1,0:T(8,128)(2,1)S(1)} %get-tuple-element.127), channel_id=1, source_target_pairs={{0,12},{4,8},{8,4},{12,0},{1,13},{5,9},{9,5},{13,1},{2,14},{6,10},... | collective-permute-start | bytes 49160 | tf_op jit(solution)/shard_map/ppermute | solution.py:495
  50.9 5.3 %collective-permute-start.17 = (bf16[48,3072]{1,0:T(8,128)(2,1)S(1)}, bf16[48,3072]{1,0:T(8,128)(2,1)S(1)}, u32[]{:S(2)}, u32[]{:S(2)}) collective-permute-start(bf16[48,3072]{1,0:T(8,128)(2,1)S(1)} %pad_maximum_fusion.2.refs_9_.refs_4_), channel_id=1, source_target_pairs={{0,4},{4,0},{8,12},{12,8},{16,20},{20,16},{24,28},{28,24},{1,5},{5... | collective-permute-start | bytes 884744 | tf_op jit(solution)/shard_map/ppermute | solution.py:191
  69.2 4.6 %collective-permute-start.27 = (bf16[16,512]{1,0:T(8,128)(2,1)S(1)}, bf16[16,512]{1,0:T(8,128)(2,1)S(1)}, u32[]{:S(2)}, u32[]{:S(2)}) collective-permute-start(bf16[16,512]{1,0:T(8,128)(2,1)S(1)} %get-tuple-element.145), channel_id=1, source_target_pairs={{0,2},{1,3},{2,0},{3,1},{4,6},{5,7},{6,4},{7,5},{8,10},{9,11},{10,... | collective-permute-start | bytes 49160 | tf_op jit(solution)/shard_map/ppermute | solution.py:489
  69.5 5.5 %collective-permute-start.28 = (bf16[16,512]{1,0:T(8,128)(2,1)S(1)}, bf16[16,512]{1,0:T(8,128)(2,1)S(1)}, u32[]{:S(2)}, u32[]{:S(2)}) collective-permute-start(bf16[16,512]{1,0:T(8,128)(2,1)S(1)} %get-tuple-element.146), channel_id=1, source_target_pairs={{0,1},{1,2},{2,3},{3,0},{4,5},{5,6},{6,7},{7,4},{8,9},{9,10},{10,1... | collective-permute-start | bytes 49160 | tf_op jit(solution)/shard_map/ppermute | solution.py:489
  77.3 3.9 %collective-permute-start.30 = (bf16[16,512]{1,0:T(8,128)(2,1)S(1)}, bf16[16,512]{1,0:T(8,128)(2,1)S(1)}, u32[]{:S(2)}, u32[]{:S(2)}) collective-permute-start(bf16[16,512]{1,0:T(8,128)(2,1)S(1)} %get-tuple-element.161), channel_id=1, source_target_pairs={{0,8},{4,12},{8,0},{12,4},{1,9},{5,13},{9,1},{13,5},{2,10},{6,14},... | collective-permute-start | bytes 49160 | tf_op jit(solution)/shard_map/ppermute | solution.py:495
  81.4 4.2 %collective-permute-start.32 = (bf16[16,512]{1,0:T(8,128)(2,1)S(1)}, bf16[16,512]{1,0:T(8,128)(2,1)S(1)}, u32[]{:S(2)}, u32[]{:S(2)}) collective-permute-start(bf16[16,512]{1,0:T(8,128)(2,1)S(1)} %get-tuple-element.164), channel_id=1, source_target_pairs={{0,3},{1,0},{2,1},{3,2},{4,7},{5,4},{6,5},{7,6},{8,11},{9,8},{10,9... | collective-permute-start | bytes 49160 | tf_op jit(solution)/shard_map/ppermute | solution.py:489
  82.7 4.6 %collective-permute-start.33 = (bf16[16,512]{1,0:T(8,128)(2,1)S(1)}, bf16[16,512]{1,0:T(8,128)(2,1)S(1)}, u32[]{:S(2)}, u32[]{:S(2)}) collective-permute-start(bf16[16,512]{1,0:T(8,128)(2,1)S(1)} %get-tuple-element.165), channel_id=1, source_target_pairs={{0,2},{1,3},{2,0},{3,1},{4,6},{5,7},{6,4},{7,5},{8,10},{9,11},{10,... | collective-permute-start | bytes 49160 | tf_op jit(solution)/shard_map/ppermute | solution.py:489
  82.7 5.5 %collective-permute-start.34 = (bf16[16,512]{1,0:T(8,128)(2,1)S(1)}, bf16[16,512]{1,0:T(8,128)(2,1)S(1)}, u32[]{:S(2)}, u32[]{:S(2)}) collective-permute-start(bf16[16,512]{1,0:T(8,128)(2,1)S(1)} %get-tuple-element.166), channel_id=1, source_target_pairs={{0,1},{1,2},{2,3},{3,0},{4,5},{5,6},{6,7},{7,4},{8,9},{9,10},{10,1... | collective-permute-start | bytes 49160 | tf_op jit(solution)/shard_map/ppermute | solution.py:489
  (11 other events, 29.6 us)

commit v18 on v17

--- a/solution.py
+++ b/solution.py
@@ -243,8 +243,8 @@
     proc_x, proc_y = across(proc_first, 2), across(proc_first, 4)
 
     def finish(one, moved, came):
-        late, _ = lax.optimization_barrier((proc_first, one))
-        corner = across(late, 6)
+        late, _ = lax.optimization_barrier((proc_x, one))
+        corner = across(late, 4)
         x, y, *_ = lax.optimization_barrier((proc_x, proc_y, *moved))
         sides = across(jnp.concatenate([x, y]), 1)
         corner, *_ = lax.optimization_barrier((corner, *came))

time: 89.8 us -> 88.9 us (0.990)
  waiting for transfers between devices: 34.1 us -> 32.2 us
  starting transfers between devices: 33.8 us -> 35 us
    ppermute x9, waiting for transfers between devices: 9.54 us -> 8.26 us  [beside(): lax.ppermute(block, 'graph', [(g, g ^ flip) for g in range(lax.axis_size(...]
    ppermute x12, starting transfers between devices: 15.6 us -> 16.9 us  [along(): return lax.ppermute(block, 'mp', list(enumerate(to)))]
  transfers between devices with their start and end apart: 35 -> 35, of which waited for: 19 -> 18; matrix products, arithmetic and copies ran while one was open for 0% -> 0% of each run, Pallas kernels for 11% -> 11%
where the time goes in v18:
time: 88.9 us; the launch traced here: 88.7 us
  starting transfers between devices  35 us (39%)
  waiting for transfers between devices  32.2 us (36%)
  Pallas kernels  20.6 us (23%)
    pallas_call x13, Pallas kernels, call(): pl.pallas_call(body, out_shape=out_shape, in_specs=[hbm if away else vmem...  20.6 us
    ppermute x12, starting transfers between devices, along(): return lax.ppermute(block, 'mp', list(enumerate(to)))  16.9 us
    ppermute x12, waiting for transfers between devices, along(): return lax.ppermute(block, 'mp', list(enumerate(to)))  12.1 us
    ppermute x9, waiting for transfers between devices, beside(): lax.ppermute(block, 'graph', [(g, g ^ flip) for g in range(lax.axis_size(...  8.26 us
    ppermute x12, starting transfers between devices, across(): lax.ppermute(x, ('groups', 'graph'), [(p, p ^ flip) for p in range(planes)])  8.12 us
    ppermute x1, waiting for transfers between devices, start(): pairs = lax.ppermute(pair, 'mp', [(m, m ^ 2) for m in range(mp)])  7.12 us
    ppermute x9, starting transfers between devices, beside(): lax.ppermute(block, 'graph', [(g, g ^ flip) for g in range(lax.axis_size(...  5.85 us
    ppermute x12, waiting for transfers between devices, across(): lax.ppermute(x, ('groups', 'graph'), [(p, p ^ flip) for p in range(planes)])  4.64 us
  transfers between devices with their start and end apart: 35, of which 18 were waited for; matrix products, arithmetic and copies ran while one was open for 0% of the time, Pallas kernels for 11%

profile of v18, /device:TPU:0, one launch (start us, length us, event | category | flops | bytes accessed | tf_op | source)
XLA Modules:
  0.0 88.7 jit_solution(3224098497991509870)
XLA Ops:
  0.6 1.7 %prepare_kernel.1 = (bf16[16,512]{1,0:T(8,128)(2,1)S(1)}, bf16[16,3584]{1,0:T(8,128)(2,1)S(1)}, bf16[16,3584]{1,0:T(8,128)(2,1)S(1)}, bf16[16,3584]{1,0:T(8,128)(2,1)S(1)}) custom-call(bf16[512,512]{1,0:T(8,128)(2,1)} %refs_0_.4, s32[4,16]{1,0:T(4,128)} %bitcast.6, bf16[1024,128]{1,0:T(8,128)(2,1)} %refs_0_.5, bf16[128,512]{1,0:T(8,128)(2,1)} %refs_1_.1, ...), custom_call_target="tpu_custom_call" | custom-call | bytes 1310976 | tf_op jit(solution)/shard_map/prepare_kernel/pallas_call | solution.py:96
  2.4 3.1 %collective-permute-start = (bf16[16,3584]{1,0:T(8,128)(2,1)S(1)}, bf16[16,3584]{1,0:T(8,128)(2,1)S(1)}, u32[]{:S(2)}, u32[]{:S(2)}) collective-permute-start(bf16[16,3584]{1,0:T(8,128)(2,1)S(1)} %get-tuple-element.103), channel_id=1, source_target_pairs={{0,1},{1,0},{2,3},{3,2},{4,5},{5,4},{6,7},{7,6},{8,9},{9,8},{10,11... | collective-permute-start | bytes 344072 | tf_op jit(solution)/shard_map/ppermute | solution.py:489
  5.5 2.6 %collective-permute-start.1 = (bf16[16,3584]{1,0:T(8,128)(2,1)S(1)}, bf16[16,3584]{1,0:T(8,128)(2,1)S(1)}, u32[]{:S(2)}, u32[]{:S(2)}) collective-permute-start(bf16[16,3584]{1,0:T(8,128)(2,1)S(1)} %get-tuple-element.104), channel_id=1, source_target_pairs={{0,2},{1,3},{2,0},{3,1},{4,6},{5,7},{6,4},{7,5},{8,10},{9,11},{10,... | collective-permute-start | bytes 344072 | tf_op jit(solution)/shard_map/ppermute | solution.py:489
  8.1 2.1 %own_kernel.1 = (bf16[128,3072]{1,0:T(8,128)(2,1)S(1)}, bf16[128,3072]{1,0:T(8,128)(2,1)S(1)}, bf16[16,3072]{1,0:T(8,128)(2,1)S(1)}) custom-call(bf16[1024,128]{1,0:T(8,128)(2,1)} %refs_0_.5, bf16[128,512]{1,0:T(8,128)(2,1)} %refs_1_.1, bf16[1024,128]{1,0:T(8,128)(2,1)} %refs_2_.3, bf16[128,512]{1,0:T(8,128)(2,1)} %refs_3_.3, bf16[1024,128]{1,0:T(8,128)(2,1)} %refs_4_.3, ...), custom_call_target="tpu_custom_call" | custom-call | bytes 1572864 | tf_op jit(solution)/shard_map/own_kernel/pallas_call | solution.py:96
  10.2 2.0 %tables_kernel.1 = (bf16[64,512]{1,0:T(8,128)(2,1)S(1)}, bf16[512,64]{1,0:T(8,128)(2,1)S(1)}, bf16[256,512]{1,0:T(8,128)(2,1)S(1)}, bf16[512,256]{1,0:T(8,128)(2...) custom-call(bf16[256,512]{1,0:T(8,128)(2,1)} %refs_7_.3, ...), custom_call_target="tpu_custom_call" | custom-call | bytes 270720 | tf_op jit(solution)/shard_map/tables_kernel/pallas_call | solution.py:96
  12.2 5.0 %collective-permute-done.1.refs_2_ = bf16[16,3584]{1,0:T(8,128)(2,1)S(1)} collective-permute-done((bf16[16,3584]{1,0:T(8,128)(2,1)S(1)}, bf16[16,3584]{1,0:T(8,128)(2,1)S(1)}, u32[]{:S(2)}, u32[]{:S(2)}) %collective-permute-start.1) | collective-permute-done | bytes 114720 | tf_op jit(solution)/shard_map/ppermute | solution.py:489
  17.4 1.9 %collective-permute-start.6 = (bf16[16,3072]{1,0:T(8,128)(2,1)S(1)}, bf16[16,3072]{1,0:T(8,128)(2,1)S(1)}, u32[]{:S(2)}, u32[]{:S(2)}) collective-permute-start(bf16[16,3072]{1,0:T(8,128)(2,1)S(1)} %get-tuple-element.110), channel_id=1, source_target_pairs={{0,1},{1,0},{2,3},{3,2},{4,5},{5,4},{6,7},{7,6},{8,9},{9,8},{10,11... | collective-permute-start | bytes 294920 | tf_op jit(solution)/shard_map/ppermute | solution.py:234
  19.2 2.5 %collective-permute-start.5 = (bf16[48,3072]{1,0:T(8,128)(2,1)S(1)}, bf16[48,3072]{1,0:T(8,128)(2,1)S(1)}, u32[]{:S(2)}, u32[]{:S(2)}) collective-permute-start(bf16[48,3072]{1,0:T(8,128)(2,1)S(1)} %get-tuple-element.108.refs_9_.refs_14_.refs_4_), channel_id=1, source_target_pairs={{0,24},{4,28},{8,16},{12,20},{16,8},{20,12},{24,0},{28,4},{1,25},{... | collective-permute-start | bytes 884744 | tf_op jit(solution)/shard_map/ppermute | solution.py:191
  22.7 2.3 %collective-permute-start.7 = (bf16[32,3072]{1,0:T(8,128)(2,1)S(1)}, bf16[32,3072]{1,0:T(8,128)(2,1)S(1)}, u32[]{:S(2)}, u32[]{:S(2)}) collective-permute-start(bf16[32,3072]{1,0:T(8,128)(2,1)S(1)} %pad_maximum_fusion.3), channel_id=1, source_target_pairs={{0,2},{1,3},{2,0},{3,1},{4,6},{5,7},{6,4},{7,5},{8,10},{9,11},{10,... | collective-permute-start | bytes 589832 | tf_op jit(solution)/shard_map/ppermute | solution.py:236
  25.0 7.1 %collective-permute-done.7 = bf16[32,3072]{1,0:T(8,128)(2,1)S(1)} collective-permute-done((bf16[32,3072]{1,0:T(8,128)(2,1)S(1)}, bf16[32,3072]{1,0:T(8,128)(2,1)S(1)}, u32[]{:S(2)}, u32[]{:S(2)}) %collective-permute-start.7) | collective-permute-done | bytes 196640 | tf_op jit(solution)/shard_map/ppermute | solution.py:236
  36.0 1.5 %collective-permute-start.18 = (bf16[48,3072]{1,0:T(8,128)(2,1)S(1)}, bf16[48,3072]{1,0:T(8,128)(2,1)S(1)}, u32[]{:S(2)}, u32[]{:S(2)}) collective-permute-start(bf16[48,3072]{1,0:T(8,128)(2,1)S(1)} %pad_maximum_fusion.2.refs_9_.refs_4_), channel_id=1, source_target_pairs={{0,8},{4,12},{8,0},{12,4},{16,24},{20,28},{24,16},{28,20},{1,9},{5... | collective-permute-start | bytes 884744 | tf_op jit(solution)/shard_map/ppermute | solution.py:191
  37.9 3.6 %encode_kernel.1 = (bf16[256,512]{1,0:T(8,128)(2,1)S(1)}, bf16[512,512]{1,0:T(8,128)(2,1)S(1)}, bf16[512,512]{1,0:T(8,128)(2,1)S(1)}, f32[512,128]{1,0:T(8,128)S...) custom-call(bf16[512,512]{1,0:T(8,128)(2,1)S(1)} %get-tuple-element., ...), custom_call_target="tpu_custom_call" | custom-call | flops 3000000000 | bytes 5488640 | tf_op jit(solution)/shard_map/encode_kernel/pallas_call | solution.py:96
  41.9 2.7 %collective-permute-start.12 = (bf16[16,512]{1,0:T(8,128)(2,1)S(1)}, bf16[16,512]{1,0:T(8,128)(2,1)S(1)}, u32[]{:S(2)}, u32[]{:S(2)}) collective-permute-start(bf16[16,512]{1,0:T(8,128)(2,1)S(1)} %get-tuple-element.122), channel_id=1, source_target_pairs={{0,2},{1,3},{2,0},{3,1},{4,6},{5,7},{6,4},{7,5},{8,10},{9,11},{10,... | collective-permute-start | bytes 49160 | tf_op jit(solution)/shard_map/ppermute | solution.py:489
  51.3 1.6 %collective-permute-done.15.refs_4_ = bf16[16,512]{1,0:T(8,128)(2,1)S(1)} collective-permute-done((bf16[16,512]{1,0:T(8,128)(2,1)S(1)}, bf16[16,512]{1,0:T(8,128)(2,1)S(1)}, u32[]{:S(2)}, u32[]{:S(2)}) %collective-permute-start.15) | collective-permute-done | bytes 16416 | tf_op jit(solution)/shard_map/ppermute | solution.py:495
  54.0 1.6 %collective-permute-done.22.refs_15_.refs_10_ = bf16[48,3072]{1,0:T(8,128)(2,1)S(1)} collective-permute-done((bf16[48,3072]{1,0:T(8,128)(2,1)S(1)}, bf16[48,3072]{1,0:T(8,128)(2,1)S(1)}, u32[]{:S(2)}, u32[]{:S(2)}) %collective-permute-start.22) | collective-permute-done | bytes 294944 | tf_op jit(solution)/shard_map/ppermute | solution.py:191
  55.6 5.3 %process_kernel.1 = (bf16[256,512]{1,0:T(8,128)(2,1)}, f32[256,512]{1,0:T(8,128)S(1)}, bf16[512,512]{1,0:T(8,128)(2,1)S(1)}, bf16[16,512]{1,0:T(8,128)(2,1)S(1)}...) custom-call(bf16[256,512]{1,0:T(8,128)(2,1)} %refs_0_.7, ...), custom_call_target="tpu_custom_call" | custom-call | flops 5000000000 | bytes 4915200 | tf_op jit(solution)/shard_map/process_kernel/pallas_call | solution.py:96
  61.1 1.5 %collective-permute-start.24 = (bf16[16,512]{1,0:T(8,128)(2,1)S(1)}, bf16[16,512]{1,0:T(8,128)(2,1)S(1)}, u32[]{:S(2)}, u32[]{:S(2)}) collective-permute-start(bf16[16,512]{1,0:T(8,128)(2,1)S(1)} %get-tuple-element.141), channel_id=1, source_target_pairs={{0,8},{4,12},{8,0},{12,4},{1,9},{5,13},{9,1},{13,5},{2,10},{6,14},... | collective-permute-start | bytes 49160 | tf_op jit(solution)/shard_map/ppermute | solution.py:495
  62.9 2.0 %collective-permute-done.24.refs_2_ = bf16[16,512]{1,0:T(8,128)(2,1)S(1)} collective-permute-done((bf16[16,512]{1,0:T(8,128)(2,1)S(1)}, bf16[16,512]{1,0:T(8,128)(2,1)S(1)}, u32[]{:S(2)}, u32[]{:S(2)}) %collective-permute-start.24) | collective-permute-done | bytes 16416 | tf_op jit(solution)/shard_map/ppermute | solution.py:495
  66.0 2.3 %collective-permute-start.26 = (bf16[16,512]{1,0:T(8,128)(2,1)S(1)}, bf16[16,512]{1,0:T(8,128)(2,1)S(1)}, u32[]{:S(2)}, u32[]{:S(2)}) collective-permute-start(bf16[16,512]{1,0:T(8,128)(2,1)S(1)} %get-tuple-element.144), channel_id=1, source_target_pairs={{0,3},{1,0},{2,1},{3,2},{4,7},{5,4},{6,5},{7,6},{8,11},{9,8},{10,9... | collective-permute-start | bytes 49160 | tf_op jit(solution)/shard_map/ppermute | solution.py:489
  70.2 2.7 %collective-permute-done.27.refs_2_ = bf16[16,512]{1,0:T(8,128)(2,1)S(1)} collective-permute-done((bf16[16,512]{1,0:T(8,128)(2,1)S(1)}, bf16[16,512]{1,0:T(8,128)(2,1)S(1)}, u32[]{:S(2)}, u32[]{:S(2)}) %collective-permute-start.27) | collective-permute-done | bytes 16416 | tf_op jit(solution)/shard_map/ppermute | solution.py:489
  73.8 2.1 %decode_kernel.1 = (f32[256,512]{1,0:T(8,128)S(1)}, bf16[512,512]{1,0:T(8,128)(2,1)S(1)}, bf16[16,512]{1,0:T(8,128)(2,1)S(1)}, bf16[16,512]{1,0:T(8,128)(2,1)S(1...) custom-call(bf16[16,512]{1,0:T(8,128)(2,1)S(1)} %get-tuple-element.143.refs_0_, ...), custom_call_target="tpu_custom_call" | custom-call | flops 3000000000 | bytes 6209536 | tf_op jit(solution)/shard_map/decode_kernel/pallas_call | solution.py:96
  77.9 1.9 %collective-permute-done.30.refs_2_ = bf16[16,512]{1,0:T(8,128)(2,1)S(1)} collective-permute-done((bf16[16,512]{1,0:T(8,128)(2,1)S(1)}, bf16[16,512]{1,0:T(8,128)(2,1)S(1)}, u32[]{:S(2)}, u32[]{:S(2)}) %collective-permute-start.30) | collective-permute-done | bytes 16416 | tf_op jit(solution)/shard_map/ppermute | solution.py:495
  81.9 1.9 %collective-permute-start.34 = (bf16[16,512]{1,0:T(8,128)(2,1)S(1)}, bf16[16,512]{1,0:T(8,128)(2,1)S(1)}, u32[]{:S(2)}, u32[]{:S(2)}) collective-permute-start(bf16[16,512]{1,0:T(8,128)(2,1)S(1)} %get-tuple-element.166), channel_id=1, source_target_pairs={{0,1},{1,2},{2,3},{3,0},{4,5},{5,6},{6,7},{7,4},{8,9},{9,10},{10,1... | collective-permute-start | bytes 49160 | tf_op jit(solution)/shard_map/ppermute | solution.py:489
  85.9 1.5 %collective-permute-done.34.refs_3_ = bf16[16,512]{1,0:T(8,128)(2,1)S(1)} collective-permute-done((bf16[16,512]{1,0:T(8,128)(2,1)S(1)}, bf16[16,512]{1,0:T(8,128)(2,1)S(1)}, u32[]{:S(2)}, u32[]{:S(2)}) %collective-permute-start.34) | collective-permute-done | bytes 16416 | tf_op jit(solution)/shard_map/ppermute | solution.py:489
  (63 shorter events, 25.4 us)
Async XLA Ops:
  2.4 9.8 %collective-permute-start = (bf16[16,3584]{1,0:T(8,128)(2,1)S(1)}, bf16[16,3584]{1,0:T(8,128)(2,1)S(1)}, u32[]{:S(2)}, u32[]{:S(2)}) collective-permute-start(bf16[16,3584]{1,0:T(8,128)(2,1)S(1)} %get-tuple-element.103), channel_id=1, source_target_pairs={{0,1},{1,0},{2,3},{3,2},{4,5},{5,4},{6,7},{7,6},{8,9},{9,8},{10,11... | collective-permute-start | bytes 344072 | tf_op jit(solution)/shard_map/ppermute | solution.py:489
  5.5 11.7 %collective-permute-start.1 = (bf16[16,3584]{1,0:T(8,128)(2,1)S(1)}, bf16[16,3584]{1,0:T(8,128)(2,1)S(1)}, u32[]{:S(2)}, u32[]{:S(2)}) collective-permute-start(bf16[16,3584]{1,0:T(8,128)(2,1)S(1)} %get-tuple-element.104), channel_id=1, source_target_pairs={{0,2},{1,3},{2,0},{3,1},{4,6},{5,7},{6,4},{7,5},{8,10},{9,11},{10,... | collective-permute-start | bytes 344072 | tf_op jit(solution)/shard_map/ppermute | solution.py:489
  8.1 9.1 %collective-permute-start.2 = (bf16[16,3584]{1,0:T(8,128)(2,1)S(1)}, bf16[16,3584]{1,0:T(8,128)(2,1)S(1)}, u32[]{:S(2)}, u32[]{:S(2)}) collective-permute-start(bf16[16,3584]{1,0:T(8,128)(2,1)S(1)} %get-tuple-element.105), channel_id=1, source_target_pairs={{0,3},{1,2},{2,1},{3,0},{4,7},{5,6},{6,5},{7,4},{8,11},{9,10},{10,... | collective-permute-start | bytes 344072 | tf_op jit(solution)/shard_map/ppermute | solution.py:489
  17.4 5.3 %collective-permute-start.6 = (bf16[16,3072]{1,0:T(8,128)(2,1)S(1)}, bf16[16,3072]{1,0:T(8,128)(2,1)S(1)}, u32[]{:S(2)}, u32[]{:S(2)}) collective-permute-start(bf16[16,3072]{1,0:T(8,128)(2,1)S(1)} %get-tuple-element.110), channel_id=1, source_target_pairs={{0,1},{1,0},{2,3},{3,2},{4,5},{5,4},{6,7},{7,6},{8,9},{9,8},{10,11... | collective-permute-start | bytes 294920 | tf_op jit(solution)/shard_map/ppermute | solution.py:234
  19.2 12.9 %collective-permute-start.5 = (bf16[48,3072]{1,0:T(8,128)(2,1)S(1)}, bf16[48,3072]{1,0:T(8,128)(2,1)S(1)}, u32[]{:S(2)}, u32[]{:S(2)}) collective-permute-start(bf16[48,3072]{1,0:T(8,128)(2,1)S(1)} %get-tuple-element.108.refs_9_.refs_14_.refs_4_), channel_id=1, source_target_pairs={{0,24},{4,28},{8,16},{12,20},{16,8},{20,12},{24,0},{28,4},{1,25},{... | collective-permute-start | bytes 884744 | tf_op jit(solution)/shard_map/ppermute | solution.py:191
  21.7 11.9 %collective-permute-start.4 = (bf16[48,3072]{1,0:T(8,128)(2,1)S(1)}, bf16[48,3072]{1,0:T(8,128)(2,1)S(1)}, u32[]{:S(2)}, u32[]{:S(2)}) collective-permute-start(bf16[48,3072]{1,0:T(8,128)(2,1)S(1)} %get-tuple-element.108.refs_9_.refs_14_.refs_4_), channel_id=1, source_target_pairs={{0,16},{4,20},{8,24},{12,28},{16,0},{20,4},{24,8},{28,12},{1,17},{... | collective-permute-start | bytes 884744 | tf_op jit(solution)/shard_map/ppermute | solution.py:191
  22.2 12.6 %collective-permute-start.3 = (bf16[48,3584]{1,0:T(8,128)(2,1)S(1)}, bf16[48,3584]{1,0:T(8,128)(2,1)S(1)}, u32[]{:S(2)}, u32[]{:S(2)}) collective-permute-start(bf16[48,3584]{1,0:T(8,128)(2,1)S(1)} %get-tuple-element.111), channel_id=1, source_target_pairs={{0,8},{4,12},{8,0},{12,4},{16,24},{20,28},{24,16},{28,20},{1,9},{5... | collective-permute-start | bytes 1032200 | tf_op jit(solution)/shard_map/ppermute | solution.py:191
  22.7 9.4 %collective-permute-start.7 = (bf16[32,3072]{1,0:T(8,128)(2,1)S(1)}, bf16[32,3072]{1,0:T(8,128)(2,1)S(1)}, u32[]{:S(2)}, u32[]{:S(2)}) collective-permute-start(bf16[32,3072]{1,0:T(8,128)(2,1)S(1)} %pad_maximum_fusion.3), channel_id=1, source_target_pairs={{0,2},{1,3},{2,0},{3,1},{4,6},{5,7},{6,4},{7,5},{8,10},{9,11},{10,... | collective-permute-start | bytes 589832 | tf_op jit(solution)/shard_map/ppermute | solution.py:236
  35.5 13.0 %collective-permute-start.19 = (bf16[48,3072]{1,0:T(8,128)(2,1)S(1)}, bf16[48,3072]{1,0:T(8,128)(2,1)S(1)}, u32[]{:S(2)}, u32[]{:S(2)}) collective-permute-start(bf16[48,3072]{1,0:T(8,128)(2,1)S(1)} %pad_maximum_fusion.2.refs_9_.refs_4_), channel_id=1, source_target_pairs={{0,16},{4,20},{8,24},{12,28},{16,0},{20,4},{24,8},{28,12},{1,17},{... | collective-permute-start | bytes 884744 | tf_op jit(solution)/shard_map/ppermute | solution.py:191
  36.0 9.8 %collective-permute-start.18 = (bf16[48,3072]{1,0:T(8,128)(2,1)S(1)}, bf16[48,3072]{1,0:T(8,128)(2,1)S(1)}, u32[]{:S(2)}, u32[]{:S(2)}) collective-permute-start(bf16[48,3072]{1,0:T(8,128)(2,1)S(1)} %pad_maximum_fusion.2.refs_9_.refs_4_), channel_id=1, source_target_pairs={{0,8},{4,12},{8,0},{12,4},{16,24},{20,28},{24,16},{28,20},{1,9},{5... | collective-permute-start | bytes 884744 | tf_op jit(solution)/shard_map/ppermute | solution.py:191
  41.4 5.6 %collective-permute-start.11 = (bf16[16,512]{1,0:T(8,128)(2,1)S(1)}, bf16[16,512]{1,0:T(8,128)(2,1)S(1)}, u32[]{:S(2)}, u32[]{:S(2)}) collective-permute-start(bf16[16,512]{1,0:T(8,128)(2,1)S(1)} %get-tuple-element.121), channel_id=1, source_target_pairs={{0,1},{1,2},{2,3},{3,0},{4,5},{5,6},{6,7},{7,4},{8,9},{9,10},{10,1... | collective-permute-start | bytes 49160 | tf_op jit(solution)/shard_map/ppermute | solution.py:489
  41.9 5.2 %collective-permute-start.12 = (bf16[16,512]{1,0:T(8,128)(2,1)S(1)}, bf16[16,512]{1,0:T(8,128)(2,1)S(1)}, u32[]{:S(2)}, u32[]{:S(2)}) collective-permute-start(bf16[16,512]{1,0:T(8,128)(2,1)S(1)} %get-tuple-element.122), channel_id=1, source_target_pairs={{0,2},{1,3},{2,0},{3,1},{4,6},{5,7},{6,4},{7,5},{8,10},{9,11},{10,... | collective-permute-start | bytes 49160 | tf_op jit(solution)/shard_map/ppermute | solution.py:489
  44.6 3.7 %collective-permute-start.13 = (bf16[16,512]{1,0:T(8,128)(2,1)S(1)}, bf16[16,512]{1,0:T(8,128)(2,1)S(1)}, u32[]{:S(2)}, u32[]{:S(2)}) collective-permute-start(bf16[16,512]{1,0:T(8,128)(2,1)S(1)} %get-tuple-element.123), channel_id=1, source_target_pairs={{0,3},{1,0},{2,1},{3,2},{4,7},{5,4},{6,5},{7,6},{8,11},{9,8},{10,9... | collective-permute-start | bytes 49160 | tf_op jit(solution)/shard_map/ppermute | solution.py:489
  45.8 8.2 %collective-permute-start.21 = (bf16[48,3072]{1,0:T(8,128)(2,1)S(1)}, bf16[48,3072]{1,0:T(8,128)(2,1)S(1)}, u32[]{:S(2)}, u32[]{:S(2)}) collective-permute-start(bf16[48,3072]{1,0:T(8,128)(2,1)S(1)} %collective-permute-done.18.refs_11_.refs_6_), channel_id=1, source_target_pairs={{0,16},{4,20},{8,24},{12,28},{16,0},{20,4},{24,8},{28,12},{1,17},{... | collective-permute-start | bytes 884744 | tf_op jit(solution)/shard_map/ppermute | solution.py:191
  48.5 7.1 %collective-permute-start.20 = (bf16[96,3072]{1,0:T(8,128)(2,1)S(1)}, bf16[96,3072]{1,0:T(8,128)(2,1)S(1)}, u32[]{:S(2)}, u32[]{:S(2)}) collective-permute-start(bf16[96,3072]{1,0:T(8,128)(2,1)S(1)} %pad_maximum_fusion.1), channel_id=1, source_target_pairs={{0,4},{4,0},{8,12},{12,8},{16,20},{20,16},{24,28},{28,24},{1,5},{5... | collective-permute-start | bytes 1769480 | tf_op jit(solution)/shard_map/ppermute | solution.py:191
  49.1 3.7 %collective-permute-start.15 = (bf16[16,512]{1,0:T(8,128)(2,1)S(1)}, bf16[16,512]{1,0:T(8,128)(2,1)S(1)}, u32[]{:S(2)}, u32[]{:S(2)}) collective-permute-start(bf16[16,512]{1,0:T(8,128)(2,1)S(1)} %get-tuple-element.126), channel_id=1, source_target_pairs={{0,8},{4,12},{8,0},{12,4},{1,9},{5,13},{9,1},{13,5},{2,10},{6,14},... | collective-permute-start | bytes 49160 | tf_op jit(solution)/shard_map/ppermute | solution.py:495
  61.1 3.8 %collective-permute-start.24 = (bf16[16,512]{1,0:T(8,128)(2,1)S(1)}, bf16[16,512]{1,0:T(8,128)(2,1)S(1)}, u32[]{:S(2)}, u32[]{:S(2)}) collective-permute-start(bf16[16,512]{1,0:T(8,128)(2,1)S(1)} %get-tuple-element.141), channel_id=1, source_target_pairs={{0,8},{4,12},{8,0},{12,4},{1,9},{5,13},{9,1},{13,5},{2,10},{6,14},... | collective-permute-start | bytes 49160 | tf_op jit(solution)/shard_map/ppermute | solution.py:495
  66.0 4.2 %collective-permute-start.26 = (bf16[16,512]{1,0:T(8,128)(2,1)S(1)}, bf16[16,512]{1,0:T(8,128)(2,1)S(1)}, u32[]{:S(2)}, u32[]{:S(2)}) collective-permute-start(bf16[16,512]{1,0:T(8,128)(2,1)S(1)} %get-tuple-element.144), channel_id=1, source_target_pairs={{0,3},{1,0},{2,1},{3,2},{4,7},{5,4},{6,5},{7,6},{8,11},{9,8},{10,9... | collective-permute-start | bytes 49160 | tf_op jit(solution)/shard_map/ppermute | solution.py:489
  68.3 4.6 %collective-permute-start.27 = (bf16[16,512]{1,0:T(8,128)(2,1)S(1)}, bf16[16,512]{1,0:T(8,128)(2,1)S(1)}, u32[]{:S(2)}, u32[]{:S(2)}) collective-permute-start(bf16[16,512]{1,0:T(8,128)(2,1)S(1)} %get-tuple-element.145), channel_id=1, source_target_pairs={{0,2},{1,3},{2,0},{3,1},{4,6},{5,7},{6,4},{7,5},{8,10},{9,11},{10,... | collective-permute-start | bytes 49160 | tf_op jit(solution)/shard_map/ppermute | solution.py:489
  68.3 5.5 %collective-permute-start.28 = (bf16[16,512]{1,0:T(8,128)(2,1)S(1)}, bf16[16,512]{1,0:T(8,128)(2,1)S(1)}, u32[]{:S(2)}, u32[]{:S(2)}) collective-permute-start(bf16[16,512]{1,0:T(8,128)(2,1)S(1)} %get-tuple-element.146), channel_id=1, source_target_pairs={{0,1},{1,2},{2,3},{3,0},{4,5},{5,6},{6,7},{7,4},{8,9},{9,10},{10,1... | collective-permute-start | bytes 49160 | tf_op jit(solution)/shard_map/ppermute | solution.py:489
  76.0 3.8 %collective-permute-start.30 = (bf16[16,512]{1,0:T(8,128)(2,1)S(1)}, bf16[16,512]{1,0:T(8,128)(2,1)S(1)}, u32[]{:S(2)}, u32[]{:S(2)}) collective-permute-start(bf16[16,512]{1,0:T(8,128)(2,1)S(1)} %get-tuple-element.161), channel_id=1, source_target_pairs={{0,8},{4,12},{8,0},{12,4},{1,9},{5,13},{9,1},{13,5},{2,10},{6,14},... | collective-permute-start | bytes 49160 | tf_op jit(solution)/shard_map/ppermute | solution.py:495
  80.7 4.5 %collective-permute-start.32 = (bf16[16,512]{1,0:T(8,128)(2,1)S(1)}, bf16[16,512]{1,0:T(8,128)(2,1)S(1)}, u32[]{:S(2)}, u32[]{:S(2)}) collective-permute-start(bf16[16,512]{1,0:T(8,128)(2,1)S(1)} %get-tuple-element.164), channel_id=1, source_target_pairs={{0,3},{1,0},{2,1},{3,2},{4,7},{5,4},{6,5},{7,6},{8,11},{9,8},{10,9... | collective-permute-start | bytes 49160 | tf_op jit(solution)/shard_map/ppermute | solution.py:489
  81.3 4.6 %collective-permute-start.33 = (bf16[16,512]{1,0:T(8,128)(2,1)S(1)}, bf16[16,512]{1,0:T(8,128)(2,1)S(1)}, u32[]{:S(2)}, u32[]{:S(2)}) collective-permute-start(bf16[16,512]{1,0:T(8,128)(2,1)S(1)} %get-tuple-element.165), channel_id=1, source_target_pairs={{0,2},{1,3},{2,0},{3,1},{4,6},{5,7},{6,4},{7,5},{8,10},{9,11},{10,... | collective-permute-start | bytes 49160 | tf_op jit(solution)/shard_map/ppermute | solution.py:489
  81.9 5.5 %collective-permute-start.34 = (bf16[16,512]{1,0:T(8,128)(2,1)S(1)}, bf16[16,512]{1,0:T(8,128)(2,1)S(1)}, u32[]{:S(2)}, u32[]{:S(2)}) collective-permute-start(bf16[16,512]{1,0:T(8,128)(2,1)S(1)} %get-tuple-element.166), channel_id=1, source_target_pairs={{0,1},{1,2},{2,3},{3,0},{4,5},{5,6},{6,7},{7,4},{8,9},{9,10},{10,1... | collective-permute-start | bytes 49160 | tf_op jit(solution)/shard_map/ppermute | solution.py:489
  (11 other events, 28.7 us)

commit v19 on v18

--- a/solution.py
+++ b/solution.py
@@ -299,14 +299,14 @@
     return ((peer // mp ^ lax.axis_index("graph")) * mp + shift) * step + slot
 
 
-def sent_row(index, step, paired=False):
+def sent_row(index, step, paired=False, order=sent_at):
     width, count = index.shape
     index = index.astype(F32).T
     at = lax.broadcasted_iota(jnp.int32, (count, count * step), 1)
     peer = lax.broadcasted_iota(jnp.int32, (count, count * step), 0)
     row = jnp.zeros(at.shape, F32)
     for slot in range(width):
-        hit = sent_at(peer, slot, step, paired) == at
+        hit = order(peer, slot, step, paired) == at
         row = jnp.where(hit, index[:, slot : slot + 1] + 1.0, row)
     return jnp.sum(row, axis=0, keepdims=True).astype(jnp.int32) - 1
 
@@ -352,19 +352,26 @@
     capacity, halo_capacity = slot_step, halo().shape[0]
     slots = slot()[...]
     coming = arrived_at(slots // capacity, slots % capacity, slot_step, True)
-    slots = arrived_at(slots // capacity, slots % capacity, slot_step)
+    slots = sent_at(slots // capacity, slots % capacity, slot_step)
     senders = sender()[...]
     remote = jnp.maximum(senders - mesh_rows, 0)
-    remote = arrived_at(remote // halo_capacity, remote % halo_capacity, halo_step)
-    senders = jnp.where(senders < mesh_rows, senders, mesh_rows + remote)
-    rows = (slots, recv_e()[...], sent_row(halo()[...], halo_step), senders, recv_p()[...])
+    own, peer, place = senders < mesh_rows, remote // halo_capacity, remote % halo_capacity
+    back = jnp.where(own, senders, mesh_rows + sent_at(peer, place, halo_step))
+    senders = jnp.where(own, senders, mesh_rows + arrived_at(peer, place, halo_step))
+    halo_back = sent_row(halo()[...], halo_step, order=arrived_at)
+    halo_rows = sent_row(halo()[...], halo_step)
+    rows = (slots, recv_e()[...], halo_back, back, recv_p()[...])
+    gathered = (coming, rows[1], halo_rows, senders, rows[4])
     for i, row in enumerate(rows):
         scatter, gather = outs[2 * i : 2 * i + 2]
-        one = table(row, scatter.ref.shape[0])
+        count = scatter.ref.shape[0]
+        one = table(row, count)
         scatter.ref[...] = one.astype(BF16)
-        gather.ref[...] = (table(coming, slot_step * peers) if i == 0 else one).T.astype(BF16)
+        other = one if gathered[i] is row else table(gathered[i], count)
+        gather.ref[...] = other.T.astype(BF16)
     outs[10].ref[...] = dot(outs[3].ref[...], mesh()[...]).astype(BF16)
-    outs[11].ref[...] = table(sent_row(send()[...], slot_step), outs[11].ref.shape[0]).astype(BF16)
+    returned = sent_row(send()[...], slot_step, order=arrived_at)
+    outs[11].ref[...] = table(returned, outs[11].ref.shape[0]).astype(BF16)
 
 
 def arrived_rows(blocks):
@@ -513,8 +520,8 @@
 
 
 def exchange_back(blocks, step):
-    blocks = turn([beside(b, t) for t, b in enumerate(blocks)], lax.axis_size("mp"), step)
-    return [along(b, -s) for s, b in enumerate(blocks)], blocks[0]
+    moved = first_level(blocks, step)
+    return second_level(moved), moved[0]
 
 
 def local(
@@ -593,7 +600,7 @@
             shape(mesh_rows, features, F32),
             shape(mesh_edges, features, BF16),
         ]
-        + [shape(mp * halo_step, features, BF16)] * graph,
+        + [shape(graph * halo_step, features, BF16)] * mp,
         Far(cotangent),
         mesh_one,
         halo_in,
@@ -618,7 +625,7 @@
     part, ga, *grad_slots = call(
         decode_kernel,
         [shape(mesh_rows, features, F32), shape(edges, features, BF16)]
-        + [shape(mp * step, features, BF16)] * graph,
+        + [shape(graph * step, features, BF16)] * mp,
         halo_back,
         halo_t,
         grad_one,

time: 88.9 us -> 88.2 us (level)
  waiting for transfers between devices: 32.2 us -> 29.5 us
  starting transfers between devices: 35 us -> 36.8 us
    ppermute x9, waiting for transfers between devices: 8.26 us -> 5.03 us  [beside(): lax.ppermute(block, 'graph', [(g, g ^ flip) for g in range(lax.axis_size(...]
    ppermute x12, starting transfers between devices: 16.9 us -> 18.7 us  [along(): return lax.ppermute(block, 'mp', list(enumerate(to)))]
  transfers between devices with their start and end apart: 35 -> 35, of which waited for: 18 -> 19; matrix products, arithmetic and copies ran while one was open for 0% -> 0% of each run, Pallas kernels for 11% -> 11%
where the time goes in v19:
time: 88.2 us; the launch traced here: 87.9 us
  starting transfers between devices  36.8 us (42%)
  waiting for transfers between devices  29.5 us (33%)
  Pallas kernels  20.7 us (23%)
    pallas_call x13, Pallas kernels, call(): pl.pallas_call(body, out_shape=out_shape, in_specs=[hbm if away else vmem...  20.7 us
    ppermute x12, starting transfers between devices, along(): return lax.ppermute(block, 'mp', list(enumerate(to)))  18.7 us
    ppermute x12, waiting for transfers between devices, along(): return lax.ppermute(block, 'mp', list(enumerate(to)))  12.7 us
    ppermute x12, starting transfers between devices, across(): lax.ppermute(x, ('groups', 'graph'), [(p, p ^ flip) for p in range(planes)])  8.12 us
    ppermute x1, waiting for transfers between devices, start(): pairs = lax.ppermute(pair, 'mp', [(m, m ^ 2) for m in range(mp)])  7.12 us
    ppermute x9, starting transfers between devices, beside(): lax.ppermute(block, 'graph', [(g, g ^ flip) for g in range(lax.axis_size(...  5.85 us
    ppermute x9, waiting for transfers between devices, beside(): lax.ppermute(block, 'graph', [(g, g ^ flip) for g in range(lax.axis_size(...  5.03 us
    ppermute x12, waiting for transfers between devices, across(): lax.ppermute(x, ('groups', 'graph'), [(p, p ^ flip) for p in range(planes)])  4.64 us
  transfers between devices with their start and end apart: 35, of which 19 were waited for; matrix products, arithmetic and copies ran while one was open for 0% of the time, Pallas kernels for 11%

profile of v19, /device:TPU:0, one launch (start us, length us, event | category | flops | bytes accessed | tf_op | source)
XLA Modules:
  0.0 87.9 jit_solution(13619889647182299108)
XLA Ops:
  0.6 1.7 %prepare_kernel.1 = (bf16[16,512]{1,0:T(8,128)(2,1)S(1)}, bf16[16,3584]{1,0:T(8,128)(2,1)S(1)}, bf16[16,3584]{1,0:T(8,128)(2,1)S(1)}, bf16[16,3584]{1,0:T(8,128)(2,1)S(1)}) custom-call(bf16[512,512]{1,0:T(8,128)(2,1)} %refs_0_.4, s32[4,16]{1,0:T(4,128)} %bitcast.6, bf16[1024,128]{1,0:T(8,128)(2,1)} %refs_0_.5, bf16[128,512]{1,0:T(8,128)(2,1)} %refs_1_.1, ...), custom_call_target="tpu_custom_call" | custom-call | bytes 1310976 | tf_op jit(solution)/shard_map/prepare_kernel/pallas_call | solution.py:96
  2.4 3.1 %collective-permute-start = (bf16[16,3584]{1,0:T(8,128)(2,1)S(1)}, bf16[16,3584]{1,0:T(8,128)(2,1)S(1)}, u32[]{:S(2)}, u32[]{:S(2)}) collective-permute-start(bf16[16,3584]{1,0:T(8,128)(2,1)S(1)} %get-tuple-element.103), channel_id=1, source_target_pairs={{0,1},{1,0},{2,3},{3,2},{4,5},{5,4},{6,7},{7,6},{8,9},{9,8},{10,11... | collective-permute-start | bytes 344072 | tf_op jit(solution)/shard_map/ppermute | solution.py:496
  5.5 2.6 %collective-permute-start.1 = (bf16[16,3584]{1,0:T(8,128)(2,1)S(1)}, bf16[16,3584]{1,0:T(8,128)(2,1)S(1)}, u32[]{:S(2)}, u32[]{:S(2)}) collective-permute-start(bf16[16,3584]{1,0:T(8,128)(2,1)S(1)} %get-tuple-element.104), channel_id=1, source_target_pairs={{0,2},{1,3},{2,0},{3,1},{4,6},{5,7},{6,4},{7,5},{8,10},{9,11},{10,... | collective-permute-start | bytes 344072 | tf_op jit(solution)/shard_map/ppermute | solution.py:496
  8.1 2.1 %own_kernel.1 = (bf16[128,3072]{1,0:T(8,128)(2,1)S(1)}, bf16[128,3072]{1,0:T(8,128)(2,1)S(1)}, bf16[16,3072]{1,0:T(8,128)(2,1)S(1)}) custom-call(bf16[1024,128]{1,0:T(8,128)(2,1)} %refs_0_.5, bf16[128,512]{1,0:T(8,128)(2,1)} %refs_1_.1, bf16[1024,128]{1,0:T(8,128)(2,1)} %refs_2_.3, bf16[128,512]{1,0:T(8,128)(2,1)} %refs_3_.3, bf16[1024,128]{1,0:T(8,128)(2,1)} %refs_4_.3, ...), custom_call_target="tpu_custom_call" | custom-call | bytes 1572864 | tf_op jit(solution)/shard_map/own_kernel/pallas_call | solution.py:96
  10.2 2.0 %tables_kernel.1 = (bf16[64,512]{1,0:T(8,128)(2,1)S(1)}, bf16[512,64]{1,0:T(8,128)(2,1)S(1)}, bf16[256,512]{1,0:T(8,128)(2,1)S(1)}, bf16[512,256]{1,0:T(8,128)(2...) custom-call(bf16[256,512]{1,0:T(8,128)(2,1)} %refs_7_.3, ...), custom_call_target="tpu_custom_call" | custom-call | bytes 270720 | tf_op jit(solution)/shard_map/tables_kernel/pallas_call | solution.py:96
  12.2 4.9 %collective-permute-done.1.refs_2_ = bf16[16,3584]{1,0:T(8,128)(2,1)S(1)} collective-permute-done((bf16[16,3584]{1,0:T(8,128)(2,1)S(1)}, bf16[16,3584]{1,0:T(8,128)(2,1)S(1)}, u32[]{:S(2)}, u32[]{:S(2)}) %collective-permute-start.1) | collective-permute-done | bytes 114720 | tf_op jit(solution)/shard_map/ppermute | solution.py:496
  17.4 1.9 %collective-permute-start.6 = (bf16[16,3072]{1,0:T(8,128)(2,1)S(1)}, bf16[16,3072]{1,0:T(8,128)(2,1)S(1)}, u32[]{:S(2)}, u32[]{:S(2)}) collective-permute-start(bf16[16,3072]{1,0:T(8,128)(2,1)S(1)} %get-tuple-element.110), channel_id=1, source_target_pairs={{0,1},{1,0},{2,3},{3,2},{4,5},{5,4},{6,7},{7,6},{8,9},{9,8},{10,11... | collective-permute-start | bytes 294920 | tf_op jit(solution)/shard_map/ppermute | solution.py:234
  19.2 2.5 %collective-permute-start.5 = (bf16[48,3072]{1,0:T(8,128)(2,1)S(1)}, bf16[48,3072]{1,0:T(8,128)(2,1)S(1)}, u32[]{:S(2)}, u32[]{:S(2)}) collective-permute-start(bf16[48,3072]{1,0:T(8,128)(2,1)S(1)} %get-tuple-element.108.refs_9_.refs_14_.refs_4_), channel_id=1, source_target_pairs={{0,24},{4,28},{8,16},{12,20},{16,8},{20,12},{24,0},{28,4},{1,25},{... | collective-permute-start | bytes 884744 | tf_op jit(solution)/shard_map/ppermute | solution.py:191
  22.7 2.3 %collective-permute-start.7 = (bf16[32,3072]{1,0:T(8,128)(2,1)S(1)}, bf16[32,3072]{1,0:T(8,128)(2,1)S(1)}, u32[]{:S(2)}, u32[]{:S(2)}) collective-permute-start(bf16[32,3072]{1,0:T(8,128)(2,1)S(1)} %pad_maximum_fusion.3), channel_id=1, source_target_pairs={{0,2},{1,3},{2,0},{3,1},{4,6},{5,7},{6,4},{7,5},{8,10},{9,11},{10,... | collective-permute-start | bytes 589832 | tf_op jit(solution)/shard_map/ppermute | solution.py:236
  25.0 7.1 %collective-permute-done.7 = bf16[32,3072]{1,0:T(8,128)(2,1)S(1)} collective-permute-done((bf16[32,3072]{1,0:T(8,128)(2,1)S(1)}, bf16[32,3072]{1,0:T(8,128)(2,1)S(1)}, u32[]{:S(2)}, u32[]{:S(2)}) %collective-permute-start.7) | collective-permute-done | bytes 196640 | tf_op jit(solution)/shard_map/ppermute | solution.py:236
  32.1 1.5 %collective-permute-done.4.refs_12_.refs_17_.refs_7_ = bf16[48,3072]{1,0:T(8,128)(2,1)S(1)} collective-permute-done((bf16[48,3072]{1,0:T(8,128)(2,1)S(1)}, bf16[48,3072]{1,0:T(8,128)(2,1)S(1)}, u32[]{:S(2)}, u32[]{:S(2)}) %collective-permute-start.4) | collective-permute-done | bytes 294944 | tf_op jit(solution)/shard_map/ppermute | solution.py:191
  36.0 1.5 %collective-permute-start.18 = (bf16[48,3072]{1,0:T(8,128)(2,1)S(1)}, bf16[48,3072]{1,0:T(8,128)(2,1)S(1)}, u32[]{:S(2)}, u32[]{:S(2)}) collective-permute-start(bf16[48,3072]{1,0:T(8,128)(2,1)S(1)} %pad_maximum_fusion.2.refs_9_.refs_4_), channel_id=1, source_target_pairs={{0,8},{4,12},{8,0},{12,4},{16,24},{20,28},{24,16},{28,20},{1,9},{5... | collective-permute-start | bytes 884744 | tf_op jit(solution)/shard_map/ppermute | solution.py:191
  37.9 3.6 %encode_kernel.1 = (bf16[256,512]{1,0:T(8,128)(2,1)S(1)}, bf16[512,512]{1,0:T(8,128)(2,1)S(1)}, bf16[512,512]{1,0:T(8,128)(2,1)S(1)}, f32[512,128]{1,0:T(8,128)S...) custom-call(bf16[512,512]{1,0:T(8,128)(2,1)S(1)} %get-tuple-element., ...), custom_call_target="tpu_custom_call" | custom-call | flops 3000000000 | bytes 5488640 | tf_op jit(solution)/shard_map/encode_kernel/pallas_call | solution.py:96
  41.9 2.7 %collective-permute-start.12 = (bf16[16,512]{1,0:T(8,128)(2,1)S(1)}, bf16[16,512]{1,0:T(8,128)(2,1)S(1)}, u32[]{:S(2)}, u32[]{:S(2)}) collective-permute-start(bf16[16,512]{1,0:T(8,128)(2,1)S(1)} %get-tuple-element.122), channel_id=1, source_target_pairs={{0,2},{1,3},{2,0},{3,1},{4,6},{5,7},{6,4},{7,5},{8,10},{9,11},{10,... | collective-permute-start | bytes 49160 | tf_op jit(solution)/shard_map/ppermute | solution.py:496
  49.1 1.5 %collective-permute-start.15 = (bf16[16,512]{1,0:T(8,128)(2,1)S(1)}, bf16[16,512]{1,0:T(8,128)(2,1)S(1)}, u32[]{:S(2)}, u32[]{:S(2)}) collective-permute-start(bf16[16,512]{1,0:T(8,128)(2,1)S(1)} %get-tuple-element.126), channel_id=1, source_target_pairs={{0,8},{4,12},{8,0},{12,4},{1,9},{5,13},{9,1},{13,5},{2,10},{6,14},... | collective-permute-start | bytes 49160 | tf_op jit(solution)/shard_map/ppermute | solution.py:502
  51.3 1.6 %collective-permute-done.15.refs_4_ = bf16[16,512]{1,0:T(8,128)(2,1)S(1)} collective-permute-done((bf16[16,512]{1,0:T(8,128)(2,1)S(1)}, bf16[16,512]{1,0:T(8,128)(2,1)S(1)}, u32[]{:S(2)}, u32[]{:S(2)}) %collective-permute-start.15) | collective-permute-done | bytes 16416 | tf_op jit(solution)/shard_map/ppermute | solution.py:502
  54.0 1.6 %collective-permute-done.22.refs_15_.refs_10_ = bf16[48,3072]{1,0:T(8,128)(2,1)S(1)} collective-permute-done((bf16[48,3072]{1,0:T(8,128)(2,1)S(1)}, bf16[48,3072]{1,0:T(8,128)(2,1)S(1)}, u32[]{:S(2)}, u32[]{:S(2)}) %collective-permute-start.22) | collective-permute-done | bytes 294944 | tf_op jit(solution)/shard_map/ppermute | solution.py:191
  55.6 5.3 %process_kernel.1 = (bf16[256,512]{1,0:T(8,128)(2,1)}, f32[256,512]{1,0:T(8,128)S(1)}, bf16[512,512]{1,0:T(8,128)(2,1)S(1)}, bf16[16,512]{1,0:T(8,128)(2,1)S(1)}...) custom-call(bf16[256,512]{1,0:T(8,128)(2,1)} %refs_0_.7, ...), custom_call_target="tpu_custom_call" | custom-call | flops 5000000000 | bytes 4915200 | tf_op jit(solution)/shard_map/process_kernel/pallas_call | solution.py:96
  62.2 2.3 %collective-permute-start.24 = (bf16[16,512]{1,0:T(8,128)(2,1)S(1)}, bf16[16,512]{1,0:T(8,128)(2,1)S(1)}, u32[]{:S(2)}, u32[]{:S(2)}) collective-permute-start(bf16[16,512]{1,0:T(8,128)(2,1)S(1)} %get-tuple-element.141), channel_id=1, source_target_pairs={{0,2},{1,3},{2,0},{3,1},{4,6},{5,7},{6,4},{7,5},{8,10},{9,11},{10,... | collective-permute-start | bytes 49160 | tf_op jit(solution)/shard_map/ppermute | solution.py:496
  70.9 1.6 %collective-permute-done.27.refs_2_ = bf16[16,512]{1,0:T(8,128)(2,1)S(1)} collective-permute-done((bf16[16,512]{1,0:T(8,128)(2,1)S(1)}, bf16[16,512]{1,0:T(8,128)(2,1)S(1)}, u32[]{:S(2)}, u32[]{:S(2)}) %collective-permute-start.27) | collective-permute-done | bytes 16416 | tf_op jit(solution)/shard_map/ppermute | solution.py:502
  72.5 2.1 %decode_kernel.1 = (f32[256,512]{1,0:T(8,128)S(1)}, bf16[512,512]{1,0:T(8,128)(2,1)S(1)}, bf16[16,512]{1,0:T(8,128)(2,1)S(1)}, bf16[16,512]{1,0:T(8,128)(2,1)S(1...) custom-call(bf16[16,512]{1,0:T(8,128)(2,1)S(1)} %get-tuple-element.143.refs_0_, ...), custom_call_target="tpu_custom_call" | custom-call | flops 3000000000 | bytes 6209536 | tf_op jit(solution)/shard_map/decode_kernel/pallas_call | solution.py:96
  74.6 1.7 %collective-permute-start.29 = (bf16[16,512]{1,0:T(8,128)(2,1)S(1)}, bf16[16,512]{1,0:T(8,128)(2,1)S(1)}, u32[]{:S(2)}, u32[]{:S(2)}) collective-permute-start(bf16[16,512]{1,0:T(8,128)(2,1)S(1)} %get-tuple-element.160), channel_id=1, source_target_pairs={{0,1},{1,2},{2,3},{3,0},{4,5},{5,6},{6,7},{7,4},{8,9},{9,10},{10,1... | collective-permute-start | bytes 49160 | tf_op jit(solution)/shard_map/ppermute | solution.py:496
  76.2 2.5 %collective-permute-start.30 = (bf16[16,512]{1,0:T(8,128)(2,1)S(1)}, bf16[16,512]{1,0:T(8,128)(2,1)S(1)}, u32[]{:S(2)}, u32[]{:S(2)}) collective-permute-start(bf16[16,512]{1,0:T(8,128)(2,1)S(1)} %get-tuple-element.161), channel_id=1, source_target_pairs={{0,2},{1,3},{2,0},{3,1},{4,6},{5,7},{6,4},{7,5},{8,10},{9,11},{10,... | collective-permute-start | bytes 49160 | tf_op jit(solution)/shard_map/ppermute | solution.py:496
  78.7 1.5 %collective-permute-done.29.refs_1_ = bf16[16,512]{1,0:T(8,128)(2,1)S(1)} collective-permute-done((bf16[16,512]{1,0:T(8,128)(2,1)S(1)}, bf16[16,512]{1,0:T(8,128)(2,1)S(1)}, u32[]{:S(2)}, u32[]{:S(2)}) %collective-permute-start.29) | collective-permute-done | bytes 16416 | tf_op jit(solution)/shard_map/ppermute | solution.py:496
  (63 shorter events, 26.2 us)
Async XLA Ops:
  2.4 9.8 %collective-permute-start = (bf16[16,3584]{1,0:T(8,128)(2,1)S(1)}, bf16[16,3584]{1,0:T(8,128)(2,1)S(1)}, u32[]{:S(2)}, u32[]{:S(2)}) collective-permute-start(bf16[16,3584]{1,0:T(8,128)(2,1)S(1)} %get-tuple-element.103), channel_id=1, source_target_pairs={{0,1},{1,0},{2,3},{3,2},{4,5},{5,4},{6,7},{7,6},{8,9},{9,8},{10,11... | collective-permute-start | bytes 344072 | tf_op jit(solution)/shard_map/ppermute | solution.py:496
  5.5 11.7 %collective-permute-start.1 = (bf16[16,3584]{1,0:T(8,128)(2,1)S(1)}, bf16[16,3584]{1,0:T(8,128)(2,1)S(1)}, u32[]{:S(2)}, u32[]{:S(2)}) collective-permute-start(bf16[16,3584]{1,0:T(8,128)(2,1)S(1)} %get-tuple-element.104), channel_id=1, source_target_pairs={{0,2},{1,3},{2,0},{3,1},{4,6},{5,7},{6,4},{7,5},{8,10},{9,11},{10,... | collective-permute-start | bytes 344072 | tf_op jit(solution)/shard_map/ppermute | solution.py:496
  8.1 9.1 %collective-permute-start.2 = (bf16[16,3584]{1,0:T(8,128)(2,1)S(1)}, bf16[16,3584]{1,0:T(8,128)(2,1)S(1)}, u32[]{:S(2)}, u32[]{:S(2)}) collective-permute-start(bf16[16,3584]{1,0:T(8,128)(2,1)S(1)} %get-tuple-element.105), channel_id=1, source_target_pairs={{0,3},{1,2},{2,1},{3,0},{4,7},{5,6},{6,5},{7,4},{8,11},{9,10},{10,... | collective-permute-start | bytes 344072 | tf_op jit(solution)/shard_map/ppermute | solution.py:496
  17.4 5.3 %collective-permute-start.6 = (bf16[16,3072]{1,0:T(8,128)(2,1)S(1)}, bf16[16,3072]{1,0:T(8,128)(2,1)S(1)}, u32[]{:S(2)}, u32[]{:S(2)}) collective-permute-start(bf16[16,3072]{1,0:T(8,128)(2,1)S(1)} %get-tuple-element.110), channel_id=1, source_target_pairs={{0,1},{1,0},{2,3},{3,2},{4,5},{5,4},{6,7},{7,6},{8,9},{9,8},{10,11... | collective-permute-start | bytes 294920 | tf_op jit(solution)/shard_map/ppermute | solution.py:234
  19.2 12.9 %collective-permute-start.5 = (bf16[48,3072]{1,0:T(8,128)(2,1)S(1)}, bf16[48,3072]{1,0:T(8,128)(2,1)S(1)}, u32[]{:S(2)}, u32[]{:S(2)}) collective-permute-start(bf16[48,3072]{1,0:T(8,128)(2,1)S(1)} %get-tuple-element.108.refs_9_.refs_14_.refs_4_), channel_id=1, source_target_pairs={{0,24},{4,28},{8,16},{12,20},{16,8},{20,12},{24,0},{28,4},{1,25},{... | collective-permute-start | bytes 884744 | tf_op jit(solution)/shard_map/ppermute | solution.py:191
  21.7 11.9 %collective-permute-start.4 = (bf16[48,3072]{1,0:T(8,128)(2,1)S(1)}, bf16[48,3072]{1,0:T(8,128)(2,1)S(1)}, u32[]{:S(2)}, u32[]{:S(2)}) collective-permute-start(bf16[48,3072]{1,0:T(8,128)(2,1)S(1)} %get-tuple-element.108.refs_9_.refs_14_.refs_4_), channel_id=1, source_target_pairs={{0,16},{4,20},{8,24},{12,28},{16,0},{20,4},{24,8},{28,12},{1,17},{... | collective-permute-start | bytes 884744 | tf_op jit(solution)/shard_map/ppermute | solution.py:191
  22.2 12.6 %collective-permute-start.3 = (bf16[48,3584]{1,0:T(8,128)(2,1)S(1)}, bf16[48,3584]{1,0:T(8,128)(2,1)S(1)}, u32[]{:S(2)}, u32[]{:S(2)}) collective-permute-start(bf16[48,3584]{1,0:T(8,128)(2,1)S(1)} %get-tuple-element.111), channel_id=1, source_target_pairs={{0,8},{4,12},{8,0},{12,4},{16,24},{20,28},{24,16},{28,20},{1,9},{5... | collective-permute-start | bytes 1032200 | tf_op jit(solution)/shard_map/ppermute | solution.py:191
  22.7 9.4 %collective-permute-start.7 = (bf16[32,3072]{1,0:T(8,128)(2,1)S(1)}, bf16[32,3072]{1,0:T(8,128)(2,1)S(1)}, u32[]{:S(2)}, u32[]{:S(2)}) collective-permute-start(bf16[32,3072]{1,0:T(8,128)(2,1)S(1)} %pad_maximum_fusion.3), channel_id=1, source_target_pairs={{0,2},{1,3},{2,0},{3,1},{4,6},{5,7},{6,4},{7,5},{8,10},{9,11},{10,... | collective-permute-start | bytes 589832 | tf_op jit(solution)/shard_map/ppermute | solution.py:236
  35.5 13.0 %collective-permute-start.19 = (bf16[48,3072]{1,0:T(8,128)(2,1)S(1)}, bf16[48,3072]{1,0:T(8,128)(2,1)S(1)}, u32[]{:S(2)}, u32[]{:S(2)}) collective-permute-start(bf16[48,3072]{1,0:T(8,128)(2,1)S(1)} %pad_maximum_fusion.2.refs_9_.refs_4_), channel_id=1, source_target_pairs={{0,16},{4,20},{8,24},{12,28},{16,0},{20,4},{24,8},{28,12},{1,17},{... | collective-permute-start | bytes 884744 | tf_op jit(solution)/shard_map/ppermute | solution.py:191
  36.0 9.8 %collective-permute-start.18 = (bf16[48,3072]{1,0:T(8,128)(2,1)S(1)}, bf16[48,3072]{1,0:T(8,128)(2,1)S(1)}, u32[]{:S(2)}, u32[]{:S(2)}) collective-permute-start(bf16[48,3072]{1,0:T(8,128)(2,1)S(1)} %pad_maximum_fusion.2.refs_9_.refs_4_), channel_id=1, source_target_pairs={{0,8},{4,12},{8,0},{12,4},{16,24},{20,28},{24,16},{28,20},{1,9},{5... | collective-permute-start | bytes 884744 | tf_op jit(solution)/shard_map/ppermute | solution.py:191
  41.4 5.6 %collective-permute-start.11 = (bf16[16,512]{1,0:T(8,128)(2,1)S(1)}, bf16[16,512]{1,0:T(8,128)(2,1)S(1)}, u32[]{:S(2)}, u32[]{:S(2)}) collective-permute-start(bf16[16,512]{1,0:T(8,128)(2,1)S(1)} %get-tuple-element.121), channel_id=1, source_target_pairs={{0,1},{1,2},{2,3},{3,0},{4,5},{5,6},{6,7},{7,4},{8,9},{9,10},{10,1... | collective-permute-start | bytes 49160 | tf_op jit(solution)/shard_map/ppermute | solution.py:496
  41.9 5.2 %collective-permute-start.12 = (bf16[16,512]{1,0:T(8,128)(2,1)S(1)}, bf16[16,512]{1,0:T(8,128)(2,1)S(1)}, u32[]{:S(2)}, u32[]{:S(2)}) collective-permute-start(bf16[16,512]{1,0:T(8,128)(2,1)S(1)} %get-tuple-element.122), channel_id=1, source_target_pairs={{0,2},{1,3},{2,0},{3,1},{4,6},{5,7},{6,4},{7,5},{8,10},{9,11},{10,... | collective-permute-start | bytes 49160 | tf_op jit(solution)/shard_map/ppermute | solution.py:496
  44.6 3.7 %collective-permute-start.13 = (bf16[16,512]{1,0:T(8,128)(2,1)S(1)}, bf16[16,512]{1,0:T(8,128)(2,1)S(1)}, u32[]{:S(2)}, u32[]{:S(2)}) collective-permute-start(bf16[16,512]{1,0:T(8,128)(2,1)S(1)} %get-tuple-element.123), channel_id=1, source_target_pairs={{0,3},{1,0},{2,1},{3,2},{4,7},{5,4},{6,5},{7,6},{8,11},{9,8},{10,9... | collective-permute-start | bytes 49160 | tf_op jit(solution)/shard_map/ppermute | solution.py:496
  45.8 8.2 %collective-permute-start.21 = (bf16[48,3072]{1,0:T(8,128)(2,1)S(1)}, bf16[48,3072]{1,0:T(8,128)(2,1)S(1)}, u32[]{:S(2)}, u32[]{:S(2)}) collective-permute-start(bf16[48,3072]{1,0:T(8,128)(2,1)S(1)} %collective-permute-done.18.refs_11_.refs_6_), channel_id=1, source_target_pairs={{0,16},{4,20},{8,24},{12,28},{16,0},{20,4},{24,8},{28,12},{1,17},{... | collective-permute-start | bytes 884744 | tf_op jit(solution)/shard_map/ppermute | solution.py:191
  48.5 7.1 %collective-permute-start.20 = (bf16[96,3072]{1,0:T(8,128)(2,1)S(1)}, bf16[96,3072]{1,0:T(8,128)(2,1)S(1)}, u32[]{:S(2)}, u32[]{:S(2)}) collective-permute-start(bf16[96,3072]{1,0:T(8,128)(2,1)S(1)} %pad_maximum_fusion.1), channel_id=1, source_target_pairs={{0,4},{4,0},{8,12},{12,8},{16,20},{20,16},{24,28},{28,24},{1,5},{5... | collective-permute-start | bytes 1769480 | tf_op jit(solution)/shard_map/ppermute | solution.py:191
  49.1 3.7 %collective-permute-start.15 = (bf16[16,512]{1,0:T(8,128)(2,1)S(1)}, bf16[16,512]{1,0:T(8,128)(2,1)S(1)}, u32[]{:S(2)}, u32[]{:S(2)}) collective-permute-start(bf16[16,512]{1,0:T(8,128)(2,1)S(1)} %get-tuple-element.126), channel_id=1, source_target_pairs={{0,8},{4,12},{8,0},{12,4},{1,9},{5,13},{9,1},{13,5},{2,10},{6,14},... | collective-permute-start | bytes 49160 | tf_op jit(solution)/shard_map/ppermute | solution.py:502
  60.9 5.6 %collective-permute-start.23 = (bf16[16,512]{1,0:T(8,128)(2,1)S(1)}, bf16[16,512]{1,0:T(8,128)(2,1)S(1)}, u32[]{:S(2)}, u32[]{:S(2)}) collective-permute-start(bf16[16,512]{1,0:T(8,128)(2,1)S(1)} %get-tuple-element.140), channel_id=1, source_target_pairs={{0,1},{1,2},{2,3},{3,0},{4,5},{5,6},{6,7},{7,4},{8,9},{9,10},{10,1... | collective-permute-start | bytes 49160 | tf_op jit(solution)/shard_map/ppermute | solution.py:496
  62.2 4.7 %collective-permute-start.24 = (bf16[16,512]{1,0:T(8,128)(2,1)S(1)}, bf16[16,512]{1,0:T(8,128)(2,1)S(1)}, u32[]{:S(2)}, u32[]{:S(2)}) collective-permute-start(bf16[16,512]{1,0:T(8,128)(2,1)S(1)} %get-tuple-element.141), channel_id=1, source_target_pairs={{0,2},{1,3},{2,0},{3,1},{4,6},{5,7},{6,4},{7,5},{8,10},{9,11},{10,... | collective-permute-start | bytes 49160 | tf_op jit(solution)/shard_map/ppermute | solution.py:496
  64.5 3.7 %collective-permute-start.25 = (bf16[16,512]{1,0:T(8,128)(2,1)S(1)}, bf16[16,512]{1,0:T(8,128)(2,1)S(1)}, u32[]{:S(2)}, u32[]{:S(2)}) collective-permute-start(bf16[16,512]{1,0:T(8,128)(2,1)S(1)} %get-tuple-element.142), channel_id=1, source_target_pairs={{0,3},{1,0},{2,1},{3,2},{4,7},{5,4},{6,5},{7,6},{8,11},{9,8},{10,9... | collective-permute-start | bytes 49160 | tf_op jit(solution)/shard_map/ppermute | solution.py:496
  68.5 4.0 %collective-permute-start.27 = (bf16[16,512]{1,0:T(8,128)(2,1)S(1)}, bf16[16,512]{1,0:T(8,128)(2,1)S(1)}, u32[]{:S(2)}, u32[]{:S(2)}) collective-permute-start(bf16[16,512]{1,0:T(8,128)(2,1)S(1)} %get-tuple-element.145), channel_id=1, source_target_pairs={{0,8},{4,12},{8,0},{12,4},{1,9},{5,13},{9,1},{13,5},{2,10},{6,14},... | collective-permute-start | bytes 49160 | tf_op jit(solution)/shard_map/ppermute | solution.py:502
  74.6 5.6 %collective-permute-start.29 = (bf16[16,512]{1,0:T(8,128)(2,1)S(1)}, bf16[16,512]{1,0:T(8,128)(2,1)S(1)}, u32[]{:S(2)}, u32[]{:S(2)}) collective-permute-start(bf16[16,512]{1,0:T(8,128)(2,1)S(1)} %get-tuple-element.160), channel_id=1, source_target_pairs={{0,1},{1,2},{2,3},{3,0},{4,5},{5,6},{6,7},{7,4},{8,9},{9,10},{10,1... | collective-permute-start | bytes 49160 | tf_op jit(solution)/shard_map/ppermute | solution.py:496
  76.2 4.9 %collective-permute-start.30 = (bf16[16,512]{1,0:T(8,128)(2,1)S(1)}, bf16[16,512]{1,0:T(8,128)(2,1)S(1)}, u32[]{:S(2)}, u32[]{:S(2)}) collective-permute-start(bf16[16,512]{1,0:T(8,128)(2,1)S(1)} %get-tuple-element.161), channel_id=1, source_target_pairs={{0,2},{1,3},{2,0},{3,1},{4,6},{5,7},{6,4},{7,5},{8,10},{9,11},{10,... | collective-permute-start | bytes 49160 | tf_op jit(solution)/shard_map/ppermute | solution.py:496
  78.7 3.7 %collective-permute-start.31 = (bf16[16,512]{1,0:T(8,128)(2,1)S(1)}, bf16[16,512]{1,0:T(8,128)(2,1)S(1)}, u32[]{:S(2)}, u32[]{:S(2)}) collective-permute-start(bf16[16,512]{1,0:T(8,128)(2,1)S(1)} %get-tuple-element.162), channel_id=1, source_target_pairs={{0,3},{1,0},{2,1},{3,2},{4,7},{5,4},{6,5},{7,6},{8,11},{9,8},{10,9... | collective-permute-start | bytes 49160 | tf_op jit(solution)/shard_map/ppermute | solution.py:496
  82.7 3.9 %collective-permute-start.33 = (bf16[16,512]{1,0:T(8,128)(2,1)S(1)}, bf16[16,512]{1,0:T(8,128)(2,1)S(1)}, u32[]{:S(2)}, u32[]{:S(2)}) collective-permute-start(bf16[16,512]{1,0:T(8,128)(2,1)S(1)} %get-tuple-element.165), channel_id=1, source_target_pairs={{0,8},{4,12},{8,0},{12,4},{1,9},{5,13},{9,1},{13,5},{2,10},{6,14},... | collective-permute-start | bytes 49160 | tf_op jit(solution)/shard_map/ppermute | solution.py:502
  (11 other events, 30.8 us)

commit v20 on v19

--- a/solution.py
+++ b/solution.py
@@ -42,8 +42,13 @@
 
 
 class Output:
-    def __init__(self, ref, copy):
-        self.ref, self.copy = ref, copy
+    def __init__(self, ref, copy, part=None):
+        self.ref, self.copy, self.part = ref, copy, part
+
+    def send_part(self, low, value):
+        rows = value.shape[0]
+        self.ref[pl.ds(low, rows), :] = value
+        self.part(low, rows).start()
 
     def send(self, value=None):
         if value is not None:
@@ -76,12 +81,18 @@
             inputs.append(Input(copy, ref))
         outputs = []
         for i, ref in enumerate(out_refs):
-            copy = None
+            copy = part = None
             if i in last:
                 place = results.pop(0)
-                copy = pltpu.make_async_copy(place, ref, sem_out.at[len(results)])
+                sem = sem_out.at[len(results)]
+                copy = pltpu.make_async_copy(place, ref, sem)
+
+                def part(low, rows, place=place, ref=ref, sem=sem):
+                    at = pl.ds(low, rows)
+                    return pltpu.make_async_copy(place.at[at, :], ref.at[at, :], sem)
+
                 ref = place
-            outputs.append(Output(ref, copy))
+            outputs.append(Output(ref, copy, part))
         given = []
         for arg, group in zip(args, groups):
             part, inputs = inputs[: len(group)], inputs[len(group) :]
@@ -485,7 +496,10 @@
 
 
 def grid_kernel(back, table_in, out):
-    out.send(dot(table_in()[...], stacked(back)))
+    rows = stacked(back)
+    size = out.ref.shape[0] // 4
+    for low in range(0, 4 * size, size):
+        out.send_part(low, dot(table_in()[pl.ds(low, size), :], rows))
 
 
 def along(block, shift, paired=False):

time: 88.2 us -> 88.1 us (level)
  no operation moved by 1% of the time
where the time goes in v20:
time: 88.1 us; the launch traced here: 87.8 us
  starting transfers between devices  36.8 us (42%)
  waiting for transfers between devices  29.5 us (33%)
  Pallas kernels  20.6 us (23%)
    pallas_call x13, Pallas kernels, call(): pl.pallas_call(body, out_shape=out_shape, in_specs=[hbm if away else vmem...  20.6 us
    ppermute x12, starting transfers between devices, along(): return lax.ppermute(block, 'mp', list(enumerate(to)))  18.7 us
    ppermute x12, waiting for transfers between devices, along(): return lax.ppermute(block, 'mp', list(enumerate(to)))  12.7 us
    ppermute x12, starting transfers between devices, across(): lax.ppermute(x, ('groups', 'graph'), [(p, p ^ flip) for p in range(planes)])  8.12 us
    ppermute x1, waiting for transfers between devices, start(): pairs = lax.ppermute(pair, 'mp', [(m, m ^ 2) for m in range(mp)])  7.12 us
    ppermute x9, starting transfers between devices, beside(): lax.ppermute(block, 'graph', [(g, g ^ flip) for g in range(lax.axis_size(...  5.85 us
    ppermute x9, waiting for transfers between devices, beside(): lax.ppermute(block, 'graph', [(g, g ^ flip) for g in range(lax.axis_size(...  5.03 us
    ppermute x12, waiting for transfers between devices, across(): lax.ppermute(x, ('groups', 'graph'), [(p, p ^ flip) for p in range(planes)])  4.64 us
  transfers between devices with their start and end apart: 35, of which 19 were waited for; matrix products, arithmetic and copies ran while one was open for 0% of the time, Pallas kernels for 11%

profile of v20, /device:TPU:0, one launch (start us, length us, event | category | flops | bytes accessed | tf_op | source)
XLA Modules:
  0.0 87.8 jit_solution(7856276276278020706)
XLA Ops:
  0.6 1.7 %prepare_kernel.1 = (bf16[16,512]{1,0:T(8,128)(2,1)S(1)}, bf16[16,3584]{1,0:T(8,128)(2,1)S(1)}, bf16[16,3584]{1,0:T(8,128)(2,1)S(1)}, bf16[16,3584]{1,0:T(8,128)(2,1)S(1)}) custom-call(bf16[512,512]{1,0:T(8,128)(2,1)} %refs_0_.4, s32[4,16]{1,0:T(4,128)} %bitcast.6, bf16[1024,128]{1,0:T(8,128)(2,1)} %refs_0_.5, bf16[128,512]{1,0:T(8,128)(2,1)} %refs_1_.1, ...), custom_call_target="tpu_custom_call" | custom-call | bytes 1310976 | tf_op jit(solution)/shard_map/prepare_kernel/pallas_call | solution.py:107
  2.4 3.1 %collective-permute-start = (bf16[16,3584]{1,0:T(8,128)(2,1)S(1)}, bf16[16,3584]{1,0:T(8,128)(2,1)S(1)}, u32[]{:S(2)}, u32[]{:S(2)}) collective-permute-start(bf16[16,3584]{1,0:T(8,128)(2,1)S(1)} %get-tuple-element.103), channel_id=1, source_target_pairs={{0,1},{1,0},{2,3},{3,2},{4,5},{5,4},{6,7},{7,6},{8,9},{9,8},{10,11... | collective-permute-start | bytes 344072 | tf_op jit(solution)/shard_map/ppermute | solution.py:510
  5.5 2.6 %collective-permute-start.1 = (bf16[16,3584]{1,0:T(8,128)(2,1)S(1)}, bf16[16,3584]{1,0:T(8,128)(2,1)S(1)}, u32[]{:S(2)}, u32[]{:S(2)}) collective-permute-start(bf16[16,3584]{1,0:T(8,128)(2,1)S(1)} %get-tuple-element.104), channel_id=1, source_target_pairs={{0,2},{1,3},{2,0},{3,1},{4,6},{5,7},{6,4},{7,5},{8,10},{9,11},{10,... | collective-permute-start | bytes 344072 | tf_op jit(solution)/shard_map/ppermute | solution.py:510
  8.1 2.1 %own_kernel.1 = (bf16[128,3072]{1,0:T(8,128)(2,1)S(1)}, bf16[128,3072]{1,0:T(8,128)(2,1)S(1)}, bf16[16,3072]{1,0:T(8,128)(2,1)S(1)}) custom-call(bf16[1024,128]{1,0:T(8,128)(2,1)} %refs_0_.5, bf16[128,512]{1,0:T(8,128)(2,1)} %refs_1_.1, bf16[1024,128]{1,0:T(8,128)(2,1)} %refs_2_.3, bf16[128,512]{1,0:T(8,128)(2,1)} %refs_3_.3, bf16[1024,128]{1,0:T(8,128)(2,1)} %refs_4_.3, ...), custom_call_target="tpu_custom_call" | custom-call | bytes 1572864 | tf_op jit(solution)/shard_map/own_kernel/pallas_call | solution.py:107
  10.2 2.0 %tables_kernel.1 = (bf16[64,512]{1,0:T(8,128)(2,1)S(1)}, bf16[512,64]{1,0:T(8,128)(2,1)S(1)}, bf16[256,512]{1,0:T(8,128)(2,1)S(1)}, bf16[512,256]{1,0:T(8,128)(2...) custom-call(bf16[256,512]{1,0:T(8,128)(2,1)} %refs_7_.3, ...), custom_call_target="tpu_custom_call" | custom-call | bytes 270720 | tf_op jit(solution)/shard_map/tables_kernel/pallas_call | solution.py:107
  12.2 4.9 %collective-permute-done.1.refs_2_ = bf16[16,3584]{1,0:T(8,128)(2,1)S(1)} collective-permute-done((bf16[16,3584]{1,0:T(8,128)(2,1)S(1)}, bf16[16,3584]{1,0:T(8,128)(2,1)S(1)}, u32[]{:S(2)}, u32[]{:S(2)}) %collective-permute-start.1) | collective-permute-done | bytes 114720 | tf_op jit(solution)/shard_map/ppermute | solution.py:510
  17.4 1.9 %collective-permute-start.6 = (bf16[16,3072]{1,0:T(8,128)(2,1)S(1)}, bf16[16,3072]{1,0:T(8,128)(2,1)S(1)}, u32[]{:S(2)}, u32[]{:S(2)}) collective-permute-start(bf16[16,3072]{1,0:T(8,128)(2,1)S(1)} %get-tuple-element.110), channel_id=1, source_target_pairs={{0,1},{1,0},{2,3},{3,2},{4,5},{5,4},{6,7},{7,6},{8,9},{9,8},{10,11... | collective-permute-start | bytes 294920 | tf_op jit(solution)/shard_map/ppermute | solution.py:245
  19.2 2.5 %collective-permute-start.5 = (bf16[48,3072]{1,0:T(8,128)(2,1)S(1)}, bf16[48,3072]{1,0:T(8,128)(2,1)S(1)}, u32[]{:S(2)}, u32[]{:S(2)}) collective-permute-start(bf16[48,3072]{1,0:T(8,128)(2,1)S(1)} %get-tuple-element.108.refs_9_.refs_14_.refs_4_), channel_id=1, source_target_pairs={{0,24},{4,28},{8,16},{12,20},{16,8},{20,12},{24,0},{28,4},{1,25},{... | collective-permute-start | bytes 884744 | tf_op jit(solution)/shard_map/ppermute | solution.py:202
  22.7 2.3 %collective-permute-start.7 = (bf16[32,3072]{1,0:T(8,128)(2,1)S(1)}, bf16[32,3072]{1,0:T(8,128)(2,1)S(1)}, u32[]{:S(2)}, u32[]{:S(2)}) collective-permute-start(bf16[32,3072]{1,0:T(8,128)(2,1)S(1)} %pad_maximum_fusion.3), channel_id=1, source_target_pairs={{0,2},{1,3},{2,0},{3,1},{4,6},{5,7},{6,4},{7,5},{8,10},{9,11},{10,... | collective-permute-start | bytes 589832 | tf_op jit(solution)/shard_map/ppermute | solution.py:247
  25.0 7.1 %collective-permute-done.7 = bf16[32,3072]{1,0:T(8,128)(2,1)S(1)} collective-permute-done((bf16[32,3072]{1,0:T(8,128)(2,1)S(1)}, bf16[32,3072]{1,0:T(8,128)(2,1)S(1)}, u32[]{:S(2)}, u32[]{:S(2)}) %collective-permute-start.7) | collective-permute-done | bytes 196640 | tf_op jit(solution)/shard_map/ppermute | solution.py:247
  32.1 1.5 %collective-permute-done.4.refs_12_.refs_17_.refs_7_ = bf16[48,3072]{1,0:T(8,128)(2,1)S(1)} collective-permute-done((bf16[48,3072]{1,0:T(8,128)(2,1)S(1)}, bf16[48,3072]{1,0:T(8,128)(2,1)S(1)}, u32[]{:S(2)}, u32[]{:S(2)}) %collective-permute-start.4) | collective-permute-done | bytes 294944 | tf_op jit(solution)/shard_map/ppermute | solution.py:202
  36.0 1.5 %collective-permute-start.18 = (bf16[48,3072]{1,0:T(8,128)(2,1)S(1)}, bf16[48,3072]{1,0:T(8,128)(2,1)S(1)}, u32[]{:S(2)}, u32[]{:S(2)}) collective-permute-start(bf16[48,3072]{1,0:T(8,128)(2,1)S(1)} %pad_maximum_fusion.2.refs_9_.refs_4_), channel_id=1, source_target_pairs={{0,8},{4,12},{8,0},{12,4},{16,24},{20,28},{24,16},{28,20},{1,9},{5... | collective-permute-start | bytes 884744 | tf_op jit(solution)/shard_map/ppermute | solution.py:202
  37.9 3.6 %encode_kernel.1 = (bf16[256,512]{1,0:T(8,128)(2,1)S(1)}, bf16[512,512]{1,0:T(8,128)(2,1)S(1)}, bf16[512,512]{1,0:T(8,128)(2,1)S(1)}, f32[512,128]{1,0:T(8,128)S...) custom-call(bf16[512,512]{1,0:T(8,128)(2,1)S(1)} %get-tuple-element., ...), custom_call_target="tpu_custom_call" | custom-call | flops 3000000000 | bytes 5488640 | tf_op jit(solution)/shard_map/encode_kernel/pallas_call | solution.py:107
  41.9 2.7 %collective-permute-start.12 = (bf16[16,512]{1,0:T(8,128)(2,1)S(1)}, bf16[16,512]{1,0:T(8,128)(2,1)S(1)}, u32[]{:S(2)}, u32[]{:S(2)}) collective-permute-start(bf16[16,512]{1,0:T(8,128)(2,1)S(1)} %get-tuple-element.122), channel_id=1, source_target_pairs={{0,2},{1,3},{2,0},{3,1},{4,6},{5,7},{6,4},{7,5},{8,10},{9,11},{10,... | collective-permute-start | bytes 49160 | tf_op jit(solution)/shard_map/ppermute | solution.py:510
  49.1 1.5 %collective-permute-start.15 = (bf16[16,512]{1,0:T(8,128)(2,1)S(1)}, bf16[16,512]{1,0:T(8,128)(2,1)S(1)}, u32[]{:S(2)}, u32[]{:S(2)}) collective-permute-start(bf16[16,512]{1,0:T(8,128)(2,1)S(1)} %get-tuple-element.126), channel_id=1, source_target_pairs={{0,8},{4,12},{8,0},{12,4},{1,9},{5,13},{9,1},{13,5},{2,10},{6,14},... | collective-permute-start | bytes 49160 | tf_op jit(solution)/shard_map/ppermute | solution.py:516
  51.3 1.6 %collective-permute-done.15.refs_4_ = bf16[16,512]{1,0:T(8,128)(2,1)S(1)} collective-permute-done((bf16[16,512]{1,0:T(8,128)(2,1)S(1)}, bf16[16,512]{1,0:T(8,128)(2,1)S(1)}, u32[]{:S(2)}, u32[]{:S(2)}) %collective-permute-start.15) | collective-permute-done | bytes 16416 | tf_op jit(solution)/shard_map/ppermute | solution.py:516
  54.0 1.6 %collective-permute-done.22.refs_15_.refs_10_ = bf16[48,3072]{1,0:T(8,128)(2,1)S(1)} collective-permute-done((bf16[48,3072]{1,0:T(8,128)(2,1)S(1)}, bf16[48,3072]{1,0:T(8,128)(2,1)S(1)}, u32[]{:S(2)}, u32[]{:S(2)}) %collective-permute-start.22) | collective-permute-done | bytes 294944 | tf_op jit(solution)/shard_map/ppermute | solution.py:202
  55.6 5.3 %process_kernel.1 = (bf16[256,512]{1,0:T(8,128)(2,1)}, f32[256,512]{1,0:T(8,128)S(1)}, bf16[512,512]{1,0:T(8,128)(2,1)S(1)}, bf16[16,512]{1,0:T(8,128)(2,1)S(1)}...) custom-call(bf16[256,512]{1,0:T(8,128)(2,1)} %refs_0_.7, ...), custom_call_target="tpu_custom_call" | custom-call | flops 5000000000 | bytes 4915200 | tf_op jit(solution)/shard_map/process_kernel/pallas_call | solution.py:107
  62.2 2.3 %collective-permute-start.24 = (bf16[16,512]{1,0:T(8,128)(2,1)S(1)}, bf16[16,512]{1,0:T(8,128)(2,1)S(1)}, u32[]{:S(2)}, u32[]{:S(2)}) collective-permute-start(bf16[16,512]{1,0:T(8,128)(2,1)S(1)} %get-tuple-element.141), channel_id=1, source_target_pairs={{0,2},{1,3},{2,0},{3,1},{4,6},{5,7},{6,4},{7,5},{8,10},{9,11},{10,... | collective-permute-start | bytes 49160 | tf_op jit(solution)/shard_map/ppermute | solution.py:510
  70.9 1.6 %collective-permute-done.27.refs_2_ = bf16[16,512]{1,0:T(8,128)(2,1)S(1)} collective-permute-done((bf16[16,512]{1,0:T(8,128)(2,1)S(1)}, bf16[16,512]{1,0:T(8,128)(2,1)S(1)}, u32[]{:S(2)}, u32[]{:S(2)}) %collective-permute-start.27) | collective-permute-done | bytes 16416 | tf_op jit(solution)/shard_map/ppermute | solution.py:516
  72.5 2.1 %decode_kernel.1 = (f32[256,512]{1,0:T(8,128)S(1)}, bf16[512,512]{1,0:T(8,128)(2,1)S(1)}, bf16[16,512]{1,0:T(8,128)(2,1)S(1)}, bf16[16,512]{1,0:T(8,128)(2,1)S(1...) custom-call(bf16[16,512]{1,0:T(8,128)(2,1)S(1)} %get-tuple-element.143.refs_0_, ...), custom_call_target="tpu_custom_call" | custom-call | flops 3000000000 | bytes 6209536 | tf_op jit(solution)/shard_map/decode_kernel/pallas_call | solution.py:107
  74.6 1.7 %collective-permute-start.29 = (bf16[16,512]{1,0:T(8,128)(2,1)S(1)}, bf16[16,512]{1,0:T(8,128)(2,1)S(1)}, u32[]{:S(2)}, u32[]{:S(2)}) collective-permute-start(bf16[16,512]{1,0:T(8,128)(2,1)S(1)} %get-tuple-element.160), channel_id=1, source_target_pairs={{0,1},{1,2},{2,3},{3,0},{4,5},{5,6},{6,7},{7,4},{8,9},{9,10},{10,1... | collective-permute-start | bytes 49160 | tf_op jit(solution)/shard_map/ppermute | solution.py:510
  76.2 2.5 %collective-permute-start.30 = (bf16[16,512]{1,0:T(8,128)(2,1)S(1)}, bf16[16,512]{1,0:T(8,128)(2,1)S(1)}, u32[]{:S(2)}, u32[]{:S(2)}) collective-permute-start(bf16[16,512]{1,0:T(8,128)(2,1)S(1)} %get-tuple-element.161), channel_id=1, source_target_pairs={{0,2},{1,3},{2,0},{3,1},{4,6},{5,7},{6,4},{7,5},{8,10},{9,11},{10,... | collective-permute-start | bytes 49160 | tf_op jit(solution)/shard_map/ppermute | solution.py:510
  78.7 1.5 %collective-permute-done.29.refs_1_ = bf16[16,512]{1,0:T(8,128)(2,1)S(1)} collective-permute-done((bf16[16,512]{1,0:T(8,128)(2,1)S(1)}, bf16[16,512]{1,0:T(8,128)(2,1)S(1)}, u32[]{:S(2)}, u32[]{:S(2)}) %collective-permute-start.29) | collective-permute-done | bytes 16416 | tf_op jit(solution)/shard_map/ppermute | solution.py:510
  (63 shorter events, 26.1 us)
Async XLA Ops:
  2.4 9.8 %collective-permute-start = (bf16[16,3584]{1,0:T(8,128)(2,1)S(1)}, bf16[16,3584]{1,0:T(8,128)(2,1)S(1)}, u32[]{:S(2)}, u32[]{:S(2)}) collective-permute-start(bf16[16,3584]{1,0:T(8,128)(2,1)S(1)} %get-tuple-element.103), channel_id=1, source_target_pairs={{0,1},{1,0},{2,3},{3,2},{4,5},{5,4},{6,7},{7,6},{8,9},{9,8},{10,11... | collective-permute-start | bytes 344072 | tf_op jit(solution)/shard_map/ppermute | solution.py:510
  5.5 11.7 %collective-permute-start.1 = (bf16[16,3584]{1,0:T(8,128)(2,1)S(1)}, bf16[16,3584]{1,0:T(8,128)(2,1)S(1)}, u32[]{:S(2)}, u32[]{:S(2)}) collective-permute-start(bf16[16,3584]{1,0:T(8,128)(2,1)S(1)} %get-tuple-element.104), channel_id=1, source_target_pairs={{0,2},{1,3},{2,0},{3,1},{4,6},{5,7},{6,4},{7,5},{8,10},{9,11},{10,... | collective-permute-start | bytes 344072 | tf_op jit(solution)/shard_map/ppermute | solution.py:510
  8.1 9.1 %collective-permute-start.2 = (bf16[16,3584]{1,0:T(8,128)(2,1)S(1)}, bf16[16,3584]{1,0:T(8,128)(2,1)S(1)}, u32[]{:S(2)}, u32[]{:S(2)}) collective-permute-start(bf16[16,3584]{1,0:T(8,128)(2,1)S(1)} %get-tuple-element.105), channel_id=1, source_target_pairs={{0,3},{1,2},{2,1},{3,0},{4,7},{5,6},{6,5},{7,4},{8,11},{9,10},{10,... | collective-permute-start | bytes 344072 | tf_op jit(solution)/shard_map/ppermute | solution.py:510
  17.4 5.3 %collective-permute-start.6 = (bf16[16,3072]{1,0:T(8,128)(2,1)S(1)}, bf16[16,3072]{1,0:T(8,128)(2,1)S(1)}, u32[]{:S(2)}, u32[]{:S(2)}) collective-permute-start(bf16[16,3072]{1,0:T(8,128)(2,1)S(1)} %get-tuple-element.110), channel_id=1, source_target_pairs={{0,1},{1,0},{2,3},{3,2},{4,5},{5,4},{6,7},{7,6},{8,9},{9,8},{10,11... | collective-permute-start | bytes 294920 | tf_op jit(solution)/shard_map/ppermute | solution.py:245
  19.2 12.9 %collective-permute-start.5 = (bf16[48,3072]{1,0:T(8,128)(2,1)S(1)}, bf16[48,3072]{1,0:T(8,128)(2,1)S(1)}, u32[]{:S(2)}, u32[]{:S(2)}) collective-permute-start(bf16[48,3072]{1,0:T(8,128)(2,1)S(1)} %get-tuple-element.108.refs_9_.refs_14_.refs_4_), channel_id=1, source_target_pairs={{0,24},{4,28},{8,16},{12,20},{16,8},{20,12},{24,0},{28,4},{1,25},{... | collective-permute-start | bytes 884744 | tf_op jit(solution)/shard_map/ppermute | solution.py:202
  21.7 11.9 %collective-permute-start.4 = (bf16[48,3072]{1,0:T(8,128)(2,1)S(1)}, bf16[48,3072]{1,0:T(8,128)(2,1)S(1)}, u32[]{:S(2)}, u32[]{:S(2)}) collective-permute-start(bf16[48,3072]{1,0:T(8,128)(2,1)S(1)} %get-tuple-element.108.refs_9_.refs_14_.refs_4_), channel_id=1, source_target_pairs={{0,16},{4,20},{8,24},{12,28},{16,0},{20,4},{24,8},{28,12},{1,17},{... | collective-permute-start | bytes 884744 | tf_op jit(solution)/shard_map/ppermute | solution.py:202
  22.2 12.6 %collective-permute-start.3 = (bf16[48,3584]{1,0:T(8,128)(2,1)S(1)}, bf16[48,3584]{1,0:T(8,128)(2,1)S(1)}, u32[]{:S(2)}, u32[]{:S(2)}) collective-permute-start(bf16[48,3584]{1,0:T(8,128)(2,1)S(1)} %get-tuple-element.111), channel_id=1, source_target_pairs={{0,8},{4,12},{8,0},{12,4},{16,24},{20,28},{24,16},{28,20},{1,9},{5... | collective-permute-start | bytes 1032200 | tf_op jit(solution)/shard_map/ppermute | solution.py:202
  22.7 9.4 %collective-permute-start.7 = (bf16[32,3072]{1,0:T(8,128)(2,1)S(1)}, bf16[32,3072]{1,0:T(8,128)(2,1)S(1)}, u32[]{:S(2)}, u32[]{:S(2)}) collective-permute-start(bf16[32,3072]{1,0:T(8,128)(2,1)S(1)} %pad_maximum_fusion.3), channel_id=1, source_target_pairs={{0,2},{1,3},{2,0},{3,1},{4,6},{5,7},{6,4},{7,5},{8,10},{9,11},{10,... | collective-permute-start | bytes 589832 | tf_op jit(solution)/shard_map/ppermute | solution.py:247
  35.5 13.0 %collective-permute-start.19 = (bf16[48,3072]{1,0:T(8,128)(2,1)S(1)}, bf16[48,3072]{1,0:T(8,128)(2,1)S(1)}, u32[]{:S(2)}, u32[]{:S(2)}) collective-permute-start(bf16[48,3072]{1,0:T(8,128)(2,1)S(1)} %pad_maximum_fusion.2.refs_9_.refs_4_), channel_id=1, source_target_pairs={{0,16},{4,20},{8,24},{12,28},{16,0},{20,4},{24,8},{28,12},{1,17},{... | collective-permute-start | bytes 884744 | tf_op jit(solution)/shard_map/ppermute | solution.py:202
  36.0 9.8 %collective-permute-start.18 = (bf16[48,3072]{1,0:T(8,128)(2,1)S(1)}, bf16[48,3072]{1,0:T(8,128)(2,1)S(1)}, u32[]{:S(2)}, u32[]{:S(2)}) collective-permute-start(bf16[48,3072]{1,0:T(8,128)(2,1)S(1)} %pad_maximum_fusion.2.refs_9_.refs_4_), channel_id=1, source_target_pairs={{0,8},{4,12},{8,0},{12,4},{16,24},{20,28},{24,16},{28,20},{1,9},{5... | collective-permute-start | bytes 884744 | tf_op jit(solution)/shard_map/ppermute | solution.py:202
  41.4 5.6 %collective-permute-start.11 = (bf16[16,512]{1,0:T(8,128)(2,1)S(1)}, bf16[16,512]{1,0:T(8,128)(2,1)S(1)}, u32[]{:S(2)}, u32[]{:S(2)}) collective-permute-start(bf16[16,512]{1,0:T(8,128)(2,1)S(1)} %get-tuple-element.121), channel_id=1, source_target_pairs={{0,1},{1,2},{2,3},{3,0},{4,5},{5,6},{6,7},{7,4},{8,9},{9,10},{10,1... | collective-permute-start | bytes 49160 | tf_op jit(solution)/shard_map/ppermute | solution.py:510
  41.9 5.2 %collective-permute-start.12 = (bf16[16,512]{1,0:T(8,128)(2,1)S(1)}, bf16[16,512]{1,0:T(8,128)(2,1)S(1)}, u32[]{:S(2)}, u32[]{:S(2)}) collective-permute-start(bf16[16,512]{1,0:T(8,128)(2,1)S(1)} %get-tuple-element.122), channel_id=1, source_target_pairs={{0,2},{1,3},{2,0},{3,1},{4,6},{5,7},{6,4},{7,5},{8,10},{9,11},{10,... | collective-permute-start | bytes 49160 | tf_op jit(solution)/shard_map/ppermute | solution.py:510
  44.6 3.7 %collective-permute-start.13 = (bf16[16,512]{1,0:T(8,128)(2,1)S(1)}, bf16[16,512]{1,0:T(8,128)(2,1)S(1)}, u32[]{:S(2)}, u32[]{:S(2)}) collective-permute-start(bf16[16,512]{1,0:T(8,128)(2,1)S(1)} %get-tuple-element.123), channel_id=1, source_target_pairs={{0,3},{1,0},{2,1},{3,2},{4,7},{5,4},{6,5},{7,6},{8,11},{9,8},{10,9... | collective-permute-start | bytes 49160 | tf_op jit(solution)/shard_map/ppermute | solution.py:510
  45.8 8.2 %collective-permute-start.21 = (bf16[48,3072]{1,0:T(8,128)(2,1)S(1)}, bf16[48,3072]{1,0:T(8,128)(2,1)S(1)}, u32[]{:S(2)}, u32[]{:S(2)}) collective-permute-start(bf16[48,3072]{1,0:T(8,128)(2,1)S(1)} %collective-permute-done.18.refs_11_.refs_6_), channel_id=1, source_target_pairs={{0,16},{4,20},{8,24},{12,28},{16,0},{20,4},{24,8},{28,12},{1,17},{... | collective-permute-start | bytes 884744 | tf_op jit(solution)/shard_map/ppermute | solution.py:202
  48.5 7.1 %collective-permute-start.20 = (bf16[96,3072]{1,0:T(8,128)(2,1)S(1)}, bf16[96,3072]{1,0:T(8,128)(2,1)S(1)}, u32[]{:S(2)}, u32[]{:S(2)}) collective-permute-start(bf16[96,3072]{1,0:T(8,128)(2,1)S(1)} %pad_maximum_fusion.1), channel_id=1, source_target_pairs={{0,4},{4,0},{8,12},{12,8},{16,20},{20,16},{24,28},{28,24},{1,5},{5... | collective-permute-start | bytes 1769480 | tf_op jit(solution)/shard_map/ppermute | solution.py:202
  49.1 3.7 %collective-permute-start.15 = (bf16[16,512]{1,0:T(8,128)(2,1)S(1)}, bf16[16,512]{1,0:T(8,128)(2,1)S(1)}, u32[]{:S(2)}, u32[]{:S(2)}) collective-permute-start(bf16[16,512]{1,0:T(8,128)(2,1)S(1)} %get-tuple-element.126), channel_id=1, source_target_pairs={{0,8},{4,12},{8,0},{12,4},{1,9},{5,13},{9,1},{13,5},{2,10},{6,14},... | collective-permute-start | bytes 49160 | tf_op jit(solution)/shard_map/ppermute | solution.py:516
  60.9 5.6 %collective-permute-start.23 = (bf16[16,512]{1,0:T(8,128)(2,1)S(1)}, bf16[16,512]{1,0:T(8,128)(2,1)S(1)}, u32[]{:S(2)}, u32[]{:S(2)}) collective-permute-start(bf16[16,512]{1,0:T(8,128)(2,1)S(1)} %get-tuple-element.140), channel_id=1, source_target_pairs={{0,1},{1,2},{2,3},{3,0},{4,5},{5,6},{6,7},{7,4},{8,9},{9,10},{10,1... | collective-permute-start | bytes 49160 | tf_op jit(solution)/shard_map/ppermute | solution.py:510
  62.2 4.7 %collective-permute-start.24 = (bf16[16,512]{1,0:T(8,128)(2,1)S(1)}, bf16[16,512]{1,0:T(8,128)(2,1)S(1)}, u32[]{:S(2)}, u32[]{:S(2)}) collective-permute-start(bf16[16,512]{1,0:T(8,128)(2,1)S(1)} %get-tuple-element.141), channel_id=1, source_target_pairs={{0,2},{1,3},{2,0},{3,1},{4,6},{5,7},{6,4},{7,5},{8,10},{9,11},{10,... | collective-permute-start | bytes 49160 | tf_op jit(solution)/shard_map/ppermute | solution.py:510
  64.5 3.7 %collective-permute-start.25 = (bf16[16,512]{1,0:T(8,128)(2,1)S(1)}, bf16[16,512]{1,0:T(8,128)(2,1)S(1)}, u32[]{:S(2)}, u32[]{:S(2)}) collective-permute-start(bf16[16,512]{1,0:T(8,128)(2,1)S(1)} %get-tuple-element.142), channel_id=1, source_target_pairs={{0,3},{1,0},{2,1},{3,2},{4,7},{5,4},{6,5},{7,6},{8,11},{9,8},{10,9... | collective-permute-start | bytes 49160 | tf_op jit(solution)/shard_map/ppermute | solution.py:510
  68.5 4.0 %collective-permute-start.27 = (bf16[16,512]{1,0:T(8,128)(2,1)S(1)}, bf16[16,512]{1,0:T(8,128)(2,1)S(1)}, u32[]{:S(2)}, u32[]{:S(2)}) collective-permute-start(bf16[16,512]{1,0:T(8,128)(2,1)S(1)} %get-tuple-element.145), channel_id=1, source_target_pairs={{0,8},{4,12},{8,0},{12,4},{1,9},{5,13},{9,1},{13,5},{2,10},{6,14},... | collective-permute-start | bytes 49160 | tf_op jit(solution)/shard_map/ppermute | solution.py:516
  74.6 5.6 %collective-permute-start.29 = (bf16[16,512]{1,0:T(8,128)(2,1)S(1)}, bf16[16,512]{1,0:T(8,128)(2,1)S(1)}, u32[]{:S(2)}, u32[]{:S(2)}) collective-permute-start(bf16[16,512]{1,0:T(8,128)(2,1)S(1)} %get-tuple-element.160), channel_id=1, source_target_pairs={{0,1},{1,2},{2,3},{3,0},{4,5},{5,6},{6,7},{7,4},{8,9},{9,10},{10,1... | collective-permute-start | bytes 49160 | tf_op jit(solution)/shard_map/ppermute | solution.py:510
  76.2 4.9 %collective-permute-start.30 = (bf16[16,512]{1,0:T(8,128)(2,1)S(1)}, bf16[16,512]{1,0:T(8,128)(2,1)S(1)}, u32[]{:S(2)}, u32[]{:S(2)}) collective-permute-start(bf16[16,512]{1,0:T(8,128)(2,1)S(1)} %get-tuple-element.161), channel_id=1, source_target_pairs={{0,2},{1,3},{2,0},{3,1},{4,6},{5,7},{6,4},{7,5},{8,10},{9,11},{10,... | collective-permute-start | bytes 49160 | tf_op jit(solution)/shard_map/ppermute | solution.py:510
  78.7 3.7 %collective-permute-start.31 = (bf16[16,512]{1,0:T(8,128)(2,1)S(1)}, bf16[16,512]{1,0:T(8,128)(2,1)S(1)}, u32[]{:S(2)}, u32[]{:S(2)}) collective-permute-start(bf16[16,512]{1,0:T(8,128)(2,1)S(1)} %get-tuple-element.162), channel_id=1, source_target_pairs={{0,3},{1,0},{2,1},{3,2},{4,7},{5,4},{6,5},{7,6},{8,11},{9,8},{10,9... | collective-permute-start | bytes 49160 | tf_op jit(solution)/shard_map/ppermute | solution.py:510
  82.7 3.9 %collective-permute-start.33 = (bf16[16,512]{1,0:T(8,128)(2,1)S(1)}, bf16[16,512]{1,0:T(8,128)(2,1)S(1)}, u32[]{:S(2)}, u32[]{:S(2)}) collective-permute-start(bf16[16,512]{1,0:T(8,128)(2,1)S(1)} %get-tuple-element.165), channel_id=1, source_target_pairs={{0,8},{4,12},{8,0},{12,4},{1,9},{5,13},{9,1},{13,5},{2,10},{6,14},... | collective-permute-start | bytes 49160 | tf_op jit(solution)/shard_map/ppermute | solution.py:516
  (11 other events, 30.8 us)

commit v21 on v20

--- a/solution.py
+++ b/solution.py
@@ -350,7 +350,7 @@
 
 
 def turn_kernel(blocks, *outs):
-    rows = stacked(blocks)
+    rows = stacked(blocks[::-1])
     step = rows.shape[0] // (len(blocks) * len(outs))
     for j, out in enumerate(outs):
         out.ref[...] = dot(turn_table(len(blocks), len(outs), step, j), rows).astype(BF16)
@@ -518,7 +518,7 @@
 
 def turn(blocks, count, step):
     out = shape(len(blocks) * step, blocks[0].shape[1], BF16)
-    return call(turn_kernel, [out] * count, list(blocks))
+    return call(turn_kernel, [out] * count, list(blocks)[::-1])
 
 
 def exchange(blocks, step):

time: 88.1 us -> 88.7 us (level)
  waiting for transfers between devices: 29.5 us -> 33.7 us
  starting transfers between devices: 36.8 us -> 33.2 us
    ppermute x12, starting transfers between devices: 18.7 us -> 14.7 us  [along(): return lax.ppermute(block, 'mp', list(enumerate(to)))]
    ppermute x12, waiting for transfers between devices: 12.7 us -> 16.2 us  [along(): return lax.ppermute(block, 'mp', list(enumerate(to)))]
  transfers between devices with their start and end apart: 35 -> 35, of which waited for: 19 -> 21; matrix products, arithmetic and copies ran while one was open for 0% -> 0% of each run, Pallas kernels for 11% -> 11%
where the time goes in v21:
time: 88.7 us; the launch traced here: 88.5 us
  waiting for transfers between devices  33.7 us (38%)
  starting transfers between devices  33.2 us (37%)
  Pallas kernels  20.6 us (23%)
    pallas_call x13, Pallas kernels, call(): pl.pallas_call(body, out_shape=out_shape, in_specs=[hbm if away else vmem...  20.6 us
    ppermute x12, waiting for transfers between devices, along(): return lax.ppermute(block, 'mp', list(enumerate(to)))  16.2 us
    ppermute x12, starting transfers between devices, along(): return lax.ppermute(block, 'mp', list(enumerate(to)))  14.7 us
    ppermute x12, starting transfers between devices, across(): lax.ppermute(x, ('groups', 'graph'), [(p, p ^ flip) for p in range(planes)])  8.51 us
    ppermute x1, waiting for transfers between devices, start(): pairs = lax.ppermute(pair, 'mp', [(m, m ^ 2) for m in range(mp)])  7.12 us
    ppermute x9, starting transfers between devices, beside(): lax.ppermute(block, 'graph', [(g, g ^ flip) for g in range(lax.axis_size(...  5.85 us
    ppermute x9, waiting for transfers between devices, beside(): lax.ppermute(block, 'graph', [(g, g ^ flip) for g in range(lax.axis_size(...  5.78 us
    ppermute x12, waiting for transfers between devices, across(): lax.ppermute(x, ('groups', 'graph'), [(p, p ^ flip) for p in range(planes)])  4.66 us
  transfers between devices with their start and end apart: 35, of which 21 were waited for; matrix products, arithmetic and copies ran while one was open for 0% of the time, Pallas kernels for 11%

profile of v21, /device:TPU:0, one launch (start us, length us, event | category | flops | bytes accessed | tf_op | source)
XLA Modules:
  0.0 88.5 jit_solution(11981678596317971506)
XLA Ops:
  0.6 1.7 %prepare_kernel.1 = (bf16[16,512]{1,0:T(8,128)(2,1)S(1)}, bf16[16,3584]{1,0:T(8,128)(2,1)S(1)}, bf16[16,3584]{1,0:T(8,128)(2,1)S(1)}, bf16[16,3584]{1,0:T(8,128)(2,1)S(1)}) custom-call(bf16[512,512]{1,0:T(8,128)(2,1)} %refs_0_.4, s32[4,16]{1,0:T(4,128)} %bitcast.6, bf16[1024,128]{1,0:T(8,128)(2,1)} %refs_0_.5, bf16[128,512]{1,0:T(8,128)(2,1)} %refs_1_.1, ...), custom_call_target="tpu_custom_call" | custom-call | bytes 1310976 | tf_op jit(solution)/shard_map/prepare_kernel/pallas_call | solution.py:107
  2.4 3.1 %collective-permute-start = (bf16[16,3584]{1,0:T(8,128)(2,1)S(1)}, bf16[16,3584]{1,0:T(8,128)(2,1)S(1)}, u32[]{:S(2)}, u32[]{:S(2)}) collective-permute-start(bf16[16,3584]{1,0:T(8,128)(2,1)S(1)} %get-tuple-element.103), channel_id=1, source_target_pairs={{0,1},{1,0},{2,3},{3,2},{4,5},{5,4},{6,7},{7,6},{8,9},{9,8},{10,11... | collective-permute-start | bytes 344072 | tf_op jit(solution)/shard_map/ppermute | solution.py:510
  5.5 2.6 %collective-permute-start.1 = (bf16[16,3584]{1,0:T(8,128)(2,1)S(1)}, bf16[16,3584]{1,0:T(8,128)(2,1)S(1)}, u32[]{:S(2)}, u32[]{:S(2)}) collective-permute-start(bf16[16,3584]{1,0:T(8,128)(2,1)S(1)} %get-tuple-element.104), channel_id=1, source_target_pairs={{0,2},{1,3},{2,0},{3,1},{4,6},{5,7},{6,4},{7,5},{8,10},{9,11},{10,... | collective-permute-start | bytes 344072 | tf_op jit(solution)/shard_map/ppermute | solution.py:510
  8.1 2.1 %own_kernel.1 = (bf16[128,3072]{1,0:T(8,128)(2,1)S(1)}, bf16[128,3072]{1,0:T(8,128)(2,1)S(1)}, bf16[16,3072]{1,0:T(8,128)(2,1)S(1)}) custom-call(bf16[1024,128]{1,0:T(8,128)(2,1)} %refs_0_.5, bf16[128,512]{1,0:T(8,128)(2,1)} %refs_1_.1, bf16[1024,128]{1,0:T(8,128)(2,1)} %refs_2_.3, bf16[128,512]{1,0:T(8,128)(2,1)} %refs_3_.3, bf16[1024,128]{1,0:T(8,128)(2,1)} %refs_4_.3, ...), custom_call_target="tpu_custom_call" | custom-call | bytes 1572864 | tf_op jit(solution)/shard_map/own_kernel/pallas_call | solution.py:107
  10.2 2.0 %tables_kernel.1 = (bf16[64,512]{1,0:T(8,128)(2,1)S(1)}, bf16[512,64]{1,0:T(8,128)(2,1)S(1)}, bf16[256,512]{1,0:T(8,128)(2,1)S(1)}, bf16[512,256]{1,0:T(8,128)(2...) custom-call(bf16[256,512]{1,0:T(8,128)(2,1)} %refs_7_.3, ...), custom_call_target="tpu_custom_call" | custom-call | bytes 270720 | tf_op jit(solution)/shard_map/tables_kernel/pallas_call | solution.py:107
  12.2 4.9 %collective-permute-done.1.refs_2_ = bf16[16,3584]{1,0:T(8,128)(2,1)S(1)} collective-permute-done((bf16[16,3584]{1,0:T(8,128)(2,1)S(1)}, bf16[16,3584]{1,0:T(8,128)(2,1)S(1)}, u32[]{:S(2)}, u32[]{:S(2)}) %collective-permute-start.1) | collective-permute-done | bytes 114720 | tf_op jit(solution)/shard_map/ppermute | solution.py:510
  17.4 1.9 %collective-permute-start.6 = (bf16[16,3072]{1,0:T(8,128)(2,1)S(1)}, bf16[16,3072]{1,0:T(8,128)(2,1)S(1)}, u32[]{:S(2)}, u32[]{:S(2)}) collective-permute-start(bf16[16,3072]{1,0:T(8,128)(2,1)S(1)} %get-tuple-element.110), channel_id=1, source_target_pairs={{0,1},{1,0},{2,3},{3,2},{4,5},{5,4},{6,7},{7,6},{8,9},{9,8},{10,11... | collective-permute-start | bytes 294920 | tf_op jit(solution)/shard_map/ppermute | solution.py:245
  19.2 2.5 %collective-permute-start.5 = (bf16[48,3072]{1,0:T(8,128)(2,1)S(1)}, bf16[48,3072]{1,0:T(8,128)(2,1)S(1)}, u32[]{:S(2)}, u32[]{:S(2)}) collective-permute-start(bf16[48,3072]{1,0:T(8,128)(2,1)S(1)} %get-tuple-element.108.refs_9_.refs_14_.refs_4_), channel_id=1, source_target_pairs={{0,24},{4,28},{8,16},{12,20},{16,8},{20,12},{24,0},{28,4},{1,25},{... | collective-permute-start | bytes 884744 | tf_op jit(solution)/shard_map/ppermute | solution.py:202
  22.7 2.3 %collective-permute-start.7 = (bf16[32,3072]{1,0:T(8,128)(2,1)S(1)}, bf16[32,3072]{1,0:T(8,128)(2,1)S(1)}, u32[]{:S(2)}, u32[]{:S(2)}) collective-permute-start(bf16[32,3072]{1,0:T(8,128)(2,1)S(1)} %pad_maximum_fusion.3), channel_id=1, source_target_pairs={{0,2},{1,3},{2,0},{3,1},{4,6},{5,7},{6,4},{7,5},{8,10},{9,11},{10,... | collective-permute-start | bytes 589832 | tf_op jit(solution)/shard_map/ppermute | solution.py:247
  25.0 7.1 %collective-permute-done.7 = bf16[32,3072]{1,0:T(8,128)(2,1)S(1)} collective-permute-done((bf16[32,3072]{1,0:T(8,128)(2,1)S(1)}, bf16[32,3072]{1,0:T(8,128)(2,1)S(1)}, u32[]{:S(2)}, u32[]{:S(2)}) %collective-permute-start.7) | collective-permute-done | bytes 196640 | tf_op jit(solution)/shard_map/ppermute | solution.py:247
  36.0 1.5 %collective-permute-start.18 = (bf16[48,3072]{1,0:T(8,128)(2,1)S(1)}, bf16[48,3072]{1,0:T(8,128)(2,1)S(1)}, u32[]{:S(2)}, u32[]{:S(2)}) collective-permute-start(bf16[48,3072]{1,0:T(8,128)(2,1)S(1)} %pad_maximum_fusion.2.refs_9_.refs_4_), channel_id=1, source_target_pairs={{0,8},{4,12},{8,0},{12,4},{16,24},{20,28},{24,16},{28,20},{1,9},{5... | collective-permute-start | bytes 884744 | tf_op jit(solution)/shard_map/ppermute | solution.py:202
  37.9 3.6 %encode_kernel.1 = (bf16[256,512]{1,0:T(8,128)(2,1)S(1)}, bf16[512,512]{1,0:T(8,128)(2,1)S(1)}, bf16[512,512]{1,0:T(8,128)(2,1)S(1)}, f32[512,128]{1,0:T(8,128)S...) custom-call(bf16[512,512]{1,0:T(8,128)(2,1)S(1)} %get-tuple-element., ...), custom_call_target="tpu_custom_call" | custom-call | flops 3000000000 | bytes 5488640 | tf_op jit(solution)/shard_map/encode_kernel/pallas_call | solution.py:107
  41.4 2.5 %collective-permute-start.11 = (bf16[16,512]{1,0:T(8,128)(2,1)S(1)}, bf16[16,512]{1,0:T(8,128)(2,1)S(1)}, u32[]{:S(2)}, u32[]{:S(2)}) collective-permute-start(bf16[16,512]{1,0:T(8,128)(2,1)S(1)} %get-tuple-element.120), channel_id=1, source_target_pairs={{0,3},{1,0},{2,1},{3,2},{4,7},{5,4},{6,5},{7,6},{8,11},{9,8},{10,9... | collective-permute-start | bytes 49160 | tf_op jit(solution)/shard_map/ppermute | solution.py:510
  45.1 1.5 %collective-permute-start.21 = (bf16[48,3072]{1,0:T(8,128)(2,1)S(1)}, bf16[48,3072]{1,0:T(8,128)(2,1)S(1)}, u32[]{:S(2)}, u32[]{:S(2)}) collective-permute-start(bf16[48,3072]{1,0:T(8,128)(2,1)S(1)} %collective-permute-done.18.refs_11_.refs_6_), channel_id=1, source_target_pairs={{0,16},{4,20},{8,24},{12,28},{16,0},{20,4},{24,8},{28,12},{1,17},{... | collective-permute-start | bytes 884744 | tf_op jit(solution)/shard_map/ppermute | solution.py:202
  46.7 2.0 %collective-permute-done.12.refs_1_ = bf16[16,512]{1,0:T(8,128)(2,1)S(1)} collective-permute-done((bf16[16,512]{1,0:T(8,128)(2,1)S(1)}, bf16[16,512]{1,0:T(8,128)(2,1)S(1)}, u32[]{:S(2)}, u32[]{:S(2)}) %collective-permute-start.12) | collective-permute-done | bytes 16416 | tf_op jit(solution)/shard_map/ppermute | solution.py:510
  52.5 1.6 %collective-permute-done.15.refs_4_ = bf16[16,512]{1,0:T(8,128)(2,1)S(1)} collective-permute-done((bf16[16,512]{1,0:T(8,128)(2,1)S(1)}, bf16[16,512]{1,0:T(8,128)(2,1)S(1)}, u32[]{:S(2)}, u32[]{:S(2)}) %collective-permute-start.15) | collective-permute-done | bytes 16416 | tf_op jit(solution)/shard_map/ppermute | solution.py:516
  55.3 1.5 %collective-permute-done.22.refs_15_.refs_10_ = bf16[48,3072]{1,0:T(8,128)(2,1)S(1)} collective-permute-done((bf16[48,3072]{1,0:T(8,128)(2,1)S(1)}, bf16[48,3072]{1,0:T(8,128)(2,1)S(1)}, u32[]{:S(2)}, u32[]{:S(2)}) %collective-permute-start.22) | collective-permute-done | bytes 294944 | tf_op jit(solution)/shard_map/ppermute | solution.py:202
  56.8 5.3 %process_kernel.1 = (bf16[256,512]{1,0:T(8,128)(2,1)}, f32[256,512]{1,0:T(8,128)S(1)}, bf16[512,512]{1,0:T(8,128)(2,1)S(1)}, bf16[16,512]{1,0:T(8,128)(2,1)S(1)}...) custom-call(bf16[256,512]{1,0:T(8,128)(2,1)} %refs_0_.7, ...), custom_call_target="tpu_custom_call" | custom-call | flops 5000000000 | bytes 4915200 | tf_op jit(solution)/shard_map/process_kernel/pallas_call | solution.py:107
  65.9 2.0 %collective-permute-done.24.refs_1_ = bf16[16,512]{1,0:T(8,128)(2,1)S(1)} collective-permute-done((bf16[16,512]{1,0:T(8,128)(2,1)S(1)}, bf16[16,512]{1,0:T(8,128)(2,1)S(1)}, u32[]{:S(2)}, u32[]{:S(2)}) %collective-permute-start.24) | collective-permute-done | bytes 16416 | tf_op jit(solution)/shard_map/ppermute | solution.py:510
  67.9 1.7 %collective-permute-done.25.refs_2_ = bf16[16,512]{1,0:T(8,128)(2,1)S(1)} collective-permute-done((bf16[16,512]{1,0:T(8,128)(2,1)S(1)}, bf16[16,512]{1,0:T(8,128)(2,1)S(1)}, u32[]{:S(2)}, u32[]{:S(2)}) %collective-permute-start.25) | collective-permute-done | bytes 16416 | tf_op jit(solution)/shard_map/ppermute | solution.py:510
  69.9 1.6 %collective-permute-start.27 = (bf16[16,512]{1,0:T(8,128)(2,1)S(1)}, bf16[16,512]{1,0:T(8,128)(2,1)S(1)}, u32[]{:S(2)}, u32[]{:S(2)}) collective-permute-start(bf16[16,512]{1,0:T(8,128)(2,1)S(1)} %get-tuple-element.145), channel_id=1, source_target_pairs={{0,8},{4,12},{8,0},{12,4},{1,9},{5,13},{9,1},{13,5},{2,10},{6,14},... | collective-permute-start | bytes 49160 | tf_op jit(solution)/shard_map/ppermute | solution.py:516
  74.6 2.1 %decode_kernel.1 = (f32[256,512]{1,0:T(8,128)S(1)}, bf16[512,512]{1,0:T(8,128)(2,1)S(1)}, bf16[16,512]{1,0:T(8,128)(2,1)S(1)}, bf16[16,512]{1,0:T(8,128)(2,1)S(1...) custom-call(bf16[16,512]{1,0:T(8,128)(2,1)S(1)} %get-tuple-element.143.refs_0_, ...), custom_call_target="tpu_custom_call" | custom-call | flops 3000000000 | bytes 6209536 | tf_op jit(solution)/shard_map/decode_kernel/pallas_call | solution.py:107
  77.1 1.9 %collective-permute-start.31 = (bf16[16,512]{1,0:T(8,128)(2,1)S(1)}, bf16[16,512]{1,0:T(8,128)(2,1)S(1)}, u32[]{:S(2)}, u32[]{:S(2)}) collective-permute-start(bf16[16,512]{1,0:T(8,128)(2,1)S(1)} %get-tuple-element.161), channel_id=1, source_target_pairs={{0,1},{1,2},{2,3},{3,0},{4,5},{5,6},{6,7},{7,4},{8,9},{9,10},{10,1... | collective-permute-start | bytes 49160 | tf_op jit(solution)/shard_map/ppermute | solution.py:510
  81.5 1.6 %collective-permute-done.31.refs_2_ = bf16[16,512]{1,0:T(8,128)(2,1)S(1)} collective-permute-done((bf16[16,512]{1,0:T(8,128)(2,1)S(1)}, bf16[16,512]{1,0:T(8,128)(2,1)S(1)}, u32[]{:S(2)}, u32[]{:S(2)}) %collective-permute-start.31) | collective-permute-done | bytes 16416 | tf_op jit(solution)/shard_map/ppermute | solution.py:510
  (63 shorter events, 26.9 us)
Async XLA Ops:
  2.4 9.8 %collective-permute-start = (bf16[16,3584]{1,0:T(8,128)(2,1)S(1)}, bf16[16,3584]{1,0:T(8,128)(2,1)S(1)}, u32[]{:S(2)}, u32[]{:S(2)}) collective-permute-start(bf16[16,3584]{1,0:T(8,128)(2,1)S(1)} %get-tuple-element.103), channel_id=1, source_target_pairs={{0,1},{1,0},{2,3},{3,2},{4,5},{5,4},{6,7},{7,6},{8,9},{9,8},{10,11... | collective-permute-start | bytes 344072 | tf_op jit(solution)/shard_map/ppermute | solution.py:510
  5.5 11.7 %collective-permute-start.1 = (bf16[16,3584]{1,0:T(8,128)(2,1)S(1)}, bf16[16,3584]{1,0:T(8,128)(2,1)S(1)}, u32[]{:S(2)}, u32[]{:S(2)}) collective-permute-start(bf16[16,3584]{1,0:T(8,128)(2,1)S(1)} %get-tuple-element.104), channel_id=1, source_target_pairs={{0,2},{1,3},{2,0},{3,1},{4,6},{5,7},{6,4},{7,5},{8,10},{9,11},{10,... | collective-permute-start | bytes 344072 | tf_op jit(solution)/shard_map/ppermute | solution.py:510
  8.1 9.1 %collective-permute-start.2 = (bf16[16,3584]{1,0:T(8,128)(2,1)S(1)}, bf16[16,3584]{1,0:T(8,128)(2,1)S(1)}, u32[]{:S(2)}, u32[]{:S(2)}) collective-permute-start(bf16[16,3584]{1,0:T(8,128)(2,1)S(1)} %get-tuple-element.105), channel_id=1, source_target_pairs={{0,3},{1,2},{2,1},{3,0},{4,7},{5,6},{6,5},{7,4},{8,11},{9,10},{10,... | collective-permute-start | bytes 344072 | tf_op jit(solution)/shard_map/ppermute | solution.py:510
  17.4 5.3 %collective-permute-start.6 = (bf16[16,3072]{1,0:T(8,128)(2,1)S(1)}, bf16[16,3072]{1,0:T(8,128)(2,1)S(1)}, u32[]{:S(2)}, u32[]{:S(2)}) collective-permute-start(bf16[16,3072]{1,0:T(8,128)(2,1)S(1)} %get-tuple-element.110), channel_id=1, source_target_pairs={{0,1},{1,0},{2,3},{3,2},{4,5},{5,4},{6,7},{7,6},{8,9},{9,8},{10,11... | collective-permute-start | bytes 294920 | tf_op jit(solution)/shard_map/ppermute | solution.py:245
  19.2 12.9 %collective-permute-start.5 = (bf16[48,3072]{1,0:T(8,128)(2,1)S(1)}, bf16[48,3072]{1,0:T(8,128)(2,1)S(1)}, u32[]{:S(2)}, u32[]{:S(2)}) collective-permute-start(bf16[48,3072]{1,0:T(8,128)(2,1)S(1)} %get-tuple-element.108.refs_9_.refs_14_.refs_4_), channel_id=1, source_target_pairs={{0,24},{4,28},{8,16},{12,20},{16,8},{20,12},{24,0},{28,4},{1,25},{... | collective-permute-start | bytes 884744 | tf_op jit(solution)/shard_map/ppermute | solution.py:202
  21.7 11.9 %collective-permute-start.4 = (bf16[48,3072]{1,0:T(8,128)(2,1)S(1)}, bf16[48,3072]{1,0:T(8,128)(2,1)S(1)}, u32[]{:S(2)}, u32[]{:S(2)}) collective-permute-start(bf16[48,3072]{1,0:T(8,128)(2,1)S(1)} %get-tuple-element.108.refs_9_.refs_14_.refs_4_), channel_id=1, source_target_pairs={{0,16},{4,20},{8,24},{12,28},{16,0},{20,4},{24,8},{28,12},{1,17},{... | collective-permute-start | bytes 884744 | tf_op jit(solution)/shard_map/ppermute | solution.py:202
  22.2 12.6 %collective-permute-start.3 = (bf16[48,3584]{1,0:T(8,128)(2,1)S(1)}, bf16[48,3584]{1,0:T(8,128)(2,1)S(1)}, u32[]{:S(2)}, u32[]{:S(2)}) collective-permute-start(bf16[48,3584]{1,0:T(8,128)(2,1)S(1)} %get-tuple-element.111), channel_id=1, source_target_pairs={{0,8},{4,12},{8,0},{12,4},{16,24},{20,28},{24,16},{28,20},{1,9},{5... | collective-permute-start | bytes 1032200 | tf_op jit(solution)/shard_map/ppermute | solution.py:202
  22.7 9.4 %collective-permute-start.7 = (bf16[32,3072]{1,0:T(8,128)(2,1)S(1)}, bf16[32,3072]{1,0:T(8,128)(2,1)S(1)}, u32[]{:S(2)}, u32[]{:S(2)}) collective-permute-start(bf16[32,3072]{1,0:T(8,128)(2,1)S(1)} %pad_maximum_fusion.3), channel_id=1, source_target_pairs={{0,2},{1,3},{2,0},{3,1},{4,6},{5,7},{6,4},{7,5},{8,10},{9,11},{10,... | collective-permute-start | bytes 589832 | tf_op jit(solution)/shard_map/ppermute | solution.py:247
  35.5 14.2 %collective-permute-start.19 = (bf16[48,3072]{1,0:T(8,128)(2,1)S(1)}, bf16[48,3072]{1,0:T(8,128)(2,1)S(1)}, u32[]{:S(2)}, u32[]{:S(2)}) collective-permute-start(bf16[48,3072]{1,0:T(8,128)(2,1)S(1)} %pad_maximum_fusion.2.refs_9_.refs_4_), channel_id=1, source_target_pairs={{0,16},{4,20},{8,24},{12,28},{16,0},{20,4},{24,8},{28,12},{1,17},{... | collective-permute-start | bytes 884744 | tf_op jit(solution)/shard_map/ppermute | solution.py:202
  36.0 9.1 %collective-permute-start.18 = (bf16[48,3072]{1,0:T(8,128)(2,1)S(1)}, bf16[48,3072]{1,0:T(8,128)(2,1)S(1)}, u32[]{:S(2)}, u32[]{:S(2)}) collective-permute-start(bf16[48,3072]{1,0:T(8,128)(2,1)S(1)} %pad_maximum_fusion.2.refs_9_.refs_4_), channel_id=1, source_target_pairs={{0,8},{4,12},{8,0},{12,4},{16,24},{20,28},{24,16},{28,20},{1,9},{5... | collective-permute-start | bytes 884744 | tf_op jit(solution)/shard_map/ppermute | solution.py:202
  41.4 5.2 %collective-permute-start.11 = (bf16[16,512]{1,0:T(8,128)(2,1)S(1)}, bf16[16,512]{1,0:T(8,128)(2,1)S(1)}, u32[]{:S(2)}, u32[]{:S(2)}) collective-permute-start(bf16[16,512]{1,0:T(8,128)(2,1)S(1)} %get-tuple-element.120), channel_id=1, source_target_pairs={{0,3},{1,0},{2,1},{3,2},{4,7},{5,4},{6,5},{7,6},{8,11},{9,8},{10,9... | collective-permute-start | bytes 49160 | tf_op jit(solution)/shard_map/ppermute | solution.py:510
  44.0 4.6 %collective-permute-start.12 = (bf16[16,512]{1,0:T(8,128)(2,1)S(1)}, bf16[16,512]{1,0:T(8,128)(2,1)S(1)}, u32[]{:S(2)}, u32[]{:S(2)}) collective-permute-start(bf16[16,512]{1,0:T(8,128)(2,1)S(1)} %get-tuple-element.121), channel_id=1, source_target_pairs={{0,2},{1,3},{2,0},{3,1},{4,6},{5,7},{6,4},{7,5},{8,10},{9,11},{10,... | collective-permute-start | bytes 49160 | tf_op jit(solution)/shard_map/ppermute | solution.py:510
  44.0 5.5 %collective-permute-start.13 = (bf16[16,512]{1,0:T(8,128)(2,1)S(1)}, bf16[16,512]{1,0:T(8,128)(2,1)S(1)}, u32[]{:S(2)}, u32[]{:S(2)}) collective-permute-start(bf16[16,512]{1,0:T(8,128)(2,1)S(1)} %get-tuple-element.122), channel_id=1, source_target_pairs={{0,1},{1,2},{2,3},{3,0},{4,5},{5,6},{6,7},{7,4},{8,9},{9,10},{10,1... | collective-permute-start | bytes 49160 | tf_op jit(solution)/shard_map/ppermute | solution.py:510
  45.1 10.0 %collective-permute-start.21 = (bf16[48,3072]{1,0:T(8,128)(2,1)S(1)}, bf16[48,3072]{1,0:T(8,128)(2,1)S(1)}, u32[]{:S(2)}, u32[]{:S(2)}) collective-permute-start(bf16[48,3072]{1,0:T(8,128)(2,1)S(1)} %collective-permute-done.18.refs_11_.refs_6_), channel_id=1, source_target_pairs={{0,16},{4,20},{8,24},{12,28},{16,0},{20,4},{24,8},{28,12},{1,17},{... | collective-permute-start | bytes 884744 | tf_op jit(solution)/shard_map/ppermute | solution.py:202
  49.8 7.0 %collective-permute-start.20 = (bf16[96,3072]{1,0:T(8,128)(2,1)S(1)}, bf16[96,3072]{1,0:T(8,128)(2,1)S(1)}, u32[]{:S(2)}, u32[]{:S(2)}) collective-permute-start(bf16[96,3072]{1,0:T(8,128)(2,1)S(1)} %pad_maximum_fusion.1), channel_id=1, source_target_pairs={{0,4},{4,0},{8,12},{12,8},{16,20},{20,16},{24,28},{28,24},{1,5},{5... | collective-permute-start | bytes 1769480 | tf_op jit(solution)/shard_map/ppermute | solution.py:202
  50.4 3.7 %collective-permute-start.15 = (bf16[16,512]{1,0:T(8,128)(2,1)S(1)}, bf16[16,512]{1,0:T(8,128)(2,1)S(1)}, u32[]{:S(2)}, u32[]{:S(2)}) collective-permute-start(bf16[16,512]{1,0:T(8,128)(2,1)S(1)} %get-tuple-element.126), channel_id=1, source_target_pairs={{0,8},{4,12},{8,0},{12,4},{1,9},{5,13},{9,1},{13,5},{2,10},{6,14},... | collective-permute-start | bytes 49160 | tf_op jit(solution)/shard_map/ppermute | solution.py:516
  62.1 3.8 %collective-permute-start.23 = (bf16[16,512]{1,0:T(8,128)(2,1)S(1)}, bf16[16,512]{1,0:T(8,128)(2,1)S(1)}, u32[]{:S(2)}, u32[]{:S(2)}) collective-permute-start(bf16[16,512]{1,0:T(8,128)(2,1)S(1)} %get-tuple-element.139), channel_id=1, source_target_pairs={{0,3},{1,0},{2,1},{3,2},{4,7},{5,4},{6,5},{7,6},{8,11},{9,8},{10,9... | collective-permute-start | bytes 49160 | tf_op jit(solution)/shard_map/ppermute | solution.py:510
  63.3 4.6 %collective-permute-start.24 = (bf16[16,512]{1,0:T(8,128)(2,1)S(1)}, bf16[16,512]{1,0:T(8,128)(2,1)S(1)}, u32[]{:S(2)}, u32[]{:S(2)}) collective-permute-start(bf16[16,512]{1,0:T(8,128)(2,1)S(1)} %get-tuple-element.140), channel_id=1, source_target_pairs={{0,2},{1,3},{2,0},{3,1},{4,6},{5,7},{6,4},{7,5},{8,10},{9,11},{10,... | collective-permute-start | bytes 49160 | tf_op jit(solution)/shard_map/ppermute | solution.py:510
  64.1 5.5 %collective-permute-start.25 = (bf16[16,512]{1,0:T(8,128)(2,1)S(1)}, bf16[16,512]{1,0:T(8,128)(2,1)S(1)}, u32[]{:S(2)}, u32[]{:S(2)}) collective-permute-start(bf16[16,512]{1,0:T(8,128)(2,1)S(1)} %get-tuple-element.141), channel_id=1, source_target_pairs={{0,1},{1,2},{2,3},{3,0},{4,5},{5,6},{6,7},{7,4},{8,9},{9,10},{10,1... | collective-permute-start | bytes 49160 | tf_op jit(solution)/shard_map/ppermute | solution.py:510
  69.9 3.8 %collective-permute-start.27 = (bf16[16,512]{1,0:T(8,128)(2,1)S(1)}, bf16[16,512]{1,0:T(8,128)(2,1)S(1)}, u32[]{:S(2)}, u32[]{:S(2)}) collective-permute-start(bf16[16,512]{1,0:T(8,128)(2,1)S(1)} %get-tuple-element.145), channel_id=1, source_target_pairs={{0,8},{4,12},{8,0},{12,4},{1,9},{5,13},{9,1},{13,5},{2,10},{6,14},... | collective-permute-start | bytes 49160 | tf_op jit(solution)/shard_map/ppermute | solution.py:516
  76.7 3.8 %collective-permute-start.29 = (bf16[16,512]{1,0:T(8,128)(2,1)S(1)}, bf16[16,512]{1,0:T(8,128)(2,1)S(1)}, u32[]{:S(2)}, u32[]{:S(2)}) collective-permute-start(bf16[16,512]{1,0:T(8,128)(2,1)S(1)} %get-tuple-element.159), channel_id=1, source_target_pairs={{0,3},{1,0},{2,1},{3,2},{4,7},{5,4},{6,5},{7,6},{8,11},{9,8},{10,9... | collective-permute-start | bytes 49160 | tf_op jit(solution)/shard_map/ppermute | solution.py:510
  76.8 4.7 %collective-permute-start.30 = (bf16[16,512]{1,0:T(8,128)(2,1)S(1)}, bf16[16,512]{1,0:T(8,128)(2,1)S(1)}, u32[]{:S(2)}, u32[]{:S(2)}) collective-permute-start(bf16[16,512]{1,0:T(8,128)(2,1)S(1)} %get-tuple-element.160), channel_id=1, source_target_pairs={{0,2},{1,3},{2,0},{3,1},{4,6},{5,7},{6,4},{7,5},{8,10},{9,11},{10,... | collective-permute-start | bytes 49160 | tf_op jit(solution)/shard_map/ppermute | solution.py:510
  77.1 5.9 %collective-permute-start.31 = (bf16[16,512]{1,0:T(8,128)(2,1)S(1)}, bf16[16,512]{1,0:T(8,128)(2,1)S(1)}, u32[]{:S(2)}, u32[]{:S(2)}) collective-permute-start(bf16[16,512]{1,0:T(8,128)(2,1)S(1)} %get-tuple-element.161), channel_id=1, source_target_pairs={{0,1},{1,2},{2,3},{3,0},{4,5},{5,6},{6,7},{7,4},{8,9},{9,10},{10,1... | collective-permute-start | bytes 49160 | tf_op jit(solution)/shard_map/ppermute | solution.py:510
  83.3 3.9 %collective-permute-start.33 = (bf16[16,512]{1,0:T(8,128)(2,1)S(1)}, bf16[16,512]{1,0:T(8,128)(2,1)S(1)}, u32[]{:S(2)}, u32[]{:S(2)}) collective-permute-start(bf16[16,512]{1,0:T(8,128)(2,1)S(1)} %get-tuple-element.165), channel_id=1, source_target_pairs={{0,8},{4,12},{8,0},{12,4},{1,9},{5,13},{9,1},{13,5},{2,10},{6,14},... | collective-permute-start | bytes 49160 | tf_op jit(solution)/shard_map/ppermute | solution.py:516
  (11 other events, 30.7 us)
